TPU v7x, 32 devices: a whole 2x2x4 slice. The times are simulated.
32 devices in a mesh: seq: 8 (over y, x, core), head: 4 (over z).
Axes of the slice: x: 2, y: 2, z: 4, core: 2. Of those that a mesh axis runs over, the one named last changes fastest.
Arguments:
- queries: bfloat16 [4096, 4096], P(('seq', 'head')), may hold values from -80 to 80
- keys: bfloat16 [4096, 512], P(('seq', 'head')), may hold values from -4 to 4
- values: bfloat16 [4096, 512], P(('seq', 'head')), may hold values from -6 to 6
- output_gradient: bfloat16 [4096, 4096], P(('seq', 'head')), may hold values from -0.59765625 to 0.59765625
- inputs: bfloat16 [4096, 8192], P(('seq', 'head')), may hold values from -6 to 6
- adapter_activation: bfloat16 [4096, 16], P(('seq', 'head')), may hold values from -6 to 6
- adapter_up_weight: bfloat16 [8, 16, 4096], P('seq', None, 'head'), may hold values from -0.09375 to 0.09375
- segment_length: int32 [8, 8], P('seq'), may hold values from 1 to 192, 512 in all within a row
- segment_adapter: int32 [8, 8], P('seq'), may hold values from 0 to 7
- owner: int32 [8], replicated, may hold values from 0 to 7, each once
Outputs:
- down_gradient: float32 [8, 8192, 16], P('seq', 'head')
- up_gradient: float32 [8, 16, 4096], P('seq', None, 'head')
Inputs may be any that keep to these rules, and one draw needn't show every extreme that they name: `segment_length`: each pack's 8 lengths sum to 512, and its longest segment has exactly 192 tokens. `owner`: each seq index owns exactly one adapter.
All inputs are finite; a program needn't handle non-finite values.
Results may differ from a plain program's by a relative error of at most 0.014.
Values may be sent and summed in bfloat16 or wider, within the bound.
No kernel may reach another device: no remote copies, remote signals or barrier semaphores. Data moves between devices by JAX's collectives and lax.ppermute only.
A program may use at most 64 MiB of HBM per device.

v0:
```python
import jax
import jax.numpy as jnp
from jax import lax
from jax.sharding import PartitionSpec as P

QUERY_HEADS = 32
KEY_VALUE_HEADS = 4
HEAD_SIZE = 128


ADAPTER_SCALE = 2.0
HIGHEST = lax.Precision.HIGHEST


def segment_of(seg_lens, pack_len):
    seg_ends = jnp.cumsum(seg_lens)
    positions = jnp.arange(pack_len, dtype=jnp.int32)
    return jnp.sum((positions[:, None] >= seg_ends[None, :]).astype(jnp.int32), axis=1)


def head_backward(q_head, g_head, k_head, v_head, segment, block_rows):
    pack_len, head_width = q_head.shape
    score_scale = 1.0 / head_width**0.5
    positions = jnp.arange(pack_len, dtype=jnp.int32)

    def one_block(starting_row):
        q_rows = lax.dynamic_slice_in_dim(q_head, starting_row, block_rows, 0)
        g_rows = lax.dynamic_slice_in_dim(g_head, starting_row, block_rows, 0)
        row_seg = lax.dynamic_slice_in_dim(segment, starting_row, block_rows, 0)
        row_pos = starting_row + jnp.arange(block_rows, dtype=jnp.int32)
        scores = (
            jnp.einsum("qd,kd->qk", q_rows, k_head, preferred_element_type=jnp.float32)
            * score_scale
        )
        allowed = (row_seg[:, None] == segment[None, :]) & (positions[None, :] <= row_pos[:, None])
        scores = jnp.where(allowed, scores, -jnp.inf)
        row_max = jnp.max(scores, axis=1, keepdims=True)
        weights = jnp.exp(scores - row_max)
        attn_prob = weights / jnp.sum(weights, axis=1, keepdims=True)
        d_prob = jnp.einsum("qd,kd->qk", g_rows, v_head, preferred_element_type=jnp.float32)
        row_delta = jnp.sum(attn_prob * d_prob, axis=1, keepdims=True)
        dscore = (attn_prob * (d_prob - row_delta) * score_scale).astype(jnp.bfloat16)
        return jnp.dot(dscore, k_head, preferred_element_type=jnp.float32).astype(jnp.bfloat16)

    starts = jnp.arange(pack_len // block_rows, dtype=jnp.int32) * block_rows
    return lax.map(one_block, starts).reshape(pack_len, head_width)


def on_device(
    queries,
    keys,
    values,
    output_gradient,
    inputs,
    adapter_activation,
    adapter_up_weight,
    segment_length,
    segment_adapter,
    owner,
):
    local_head_count = lax.axis_size("head")
    tok_rows = queries.shape[0]
    pack_len = tok_rows * local_head_count
    block_rows = min(512, pack_len)
    resident_heads = QUERY_HEADS // local_head_count
    resident_key_value_heads = max(KEY_VALUE_HEADS // local_head_count, 1)
    q_heads, g_heads = (
        lax.all_to_all(queries, "head", split_axis=1, concat_axis=0, tiled=True),
        lax.all_to_all(output_gradient, "head", split_axis=1, concat_axis=0, tiled=True),
    )
    k_all, v_all = (
        lax.all_gather(keys, "head", axis=0, tiled=True),
        lax.all_gather(values, "head", axis=0, tiled=True),
    )
    first_key_value_head = (
        lax.axis_index("head") * resident_heads // (QUERY_HEADS // KEY_VALUE_HEADS)
    )
    k_local = lax.dynamic_slice_in_dim(
        k_all, first_key_value_head * HEAD_SIZE, resident_key_value_heads * HEAD_SIZE, 1
    )
    v_local = lax.dynamic_slice_in_dim(
        v_all, first_key_value_head * HEAD_SIZE, resident_key_value_heads * HEAD_SIZE, 1
    )
    feat_rows, activation_rows = (
        lax.all_to_all(inputs, "head", split_axis=1, concat_axis=0, tiled=True),
        lax.all_to_all(
            jnp.tile(adapter_activation, (1, local_head_count)),
            "head",
            split_axis=1,
            concat_axis=0,
            tiled=True,
        ),
    )
    segment = segment_of(segment_length[0], pack_len)
    q_stack = q_heads.reshape(pack_len, resident_heads, HEAD_SIZE).transpose(1, 0, 2)
    g_stack = g_heads.reshape(pack_len, resident_heads, HEAD_SIZE).transpose(1, 0, 2)
    k_stack = jnp.repeat(
        k_local.reshape(pack_len, resident_key_value_heads, HEAD_SIZE).transpose(1, 0, 2),
        resident_heads // resident_key_value_heads,
        axis=0,
    )
    v_stack = jnp.repeat(
        v_local.reshape(pack_len, resident_key_value_heads, HEAD_SIZE).transpose(1, 0, 2),
        resident_heads // resident_key_value_heads,
        axis=0,
    )
    dq_stack = lax.map(
        lambda stacked: head_backward(
            stacked[0], stacked[1], stacked[2], stacked[3], segment, block_rows
        ),
        (q_stack, g_stack, k_stack, v_stack),
    )
    dquery = dq_stack.transpose(1, 0, 2).reshape(pack_len, resident_heads * HEAD_SIZE)
    segment_index = segment_adapter[0]
    seg_total = segment_index.shape[0]
    adapter_total = owner.shape[0]
    adapter_rank_width = adapter_up_weight.shape[1]
    query_width = dquery.shape[1]
    d_width = feat_rows.shape[1]
    adapter_cols = jnp.arange(adapter_total, dtype=jnp.int32)
    seg_mask = segment[:, None] == jnp.arange(seg_total, dtype=jnp.int32)[None, :]
    seg_hits = segment_index[:, None] == adapter_cols[None, :]
    up_weight_every_token = lax.all_gather(adapter_up_weight, "seq", axis=0, tiled=True).reshape(
        adapter_total, adapter_rank_width * query_width
    )
    up_weight_segment = jnp.dot(
        seg_hits.astype(jnp.bfloat16), up_weight_every_token, preferred_element_type=jnp.float32
    ).astype(jnp.bfloat16)
    rank_seg = jnp.einsum(
        "tf,cf->tc",
        dquery,
        up_weight_segment.reshape(seg_total * adapter_rank_width, query_width),
        preferred_element_type=jnp.float32,
    )
    rank_part = jnp.sum(
        rank_seg.reshape(pack_len, seg_total, adapter_rank_width) * seg_mask[:, :, None], axis=1
    )
    rank_low = lax.psum(rank_part, "head").astype(jnp.bfloat16)
    mask_low = seg_mask.astype(jnp.bfloat16)
    seg_owner = jnp.sum(jnp.where(seg_hits, owner[None, :], 0), axis=1)
    slot_map = (seg_owner[:, None] == adapter_cols[None, :]).astype(jnp.float32)
    rank_cols = (mask_low[:, :, None] * rank_low[:, None, :]).reshape(
        pack_len, seg_total * adapter_rank_width
    )
    act_cols = (mask_low[:, :, None] * activation_rows[:, None, :]).reshape(
        pack_len, seg_total * adapter_rank_width
    )
    part_a = jnp.einsum(
        "td,tc->dc", feat_rows, rank_cols, preferred_element_type=jnp.float32
    ).reshape(d_width, seg_total, adapter_rank_width)
    part_b = jnp.einsum("tc,tf->cf", act_cols, dquery, preferred_element_type=jnp.float32).reshape(
        seg_total, adapter_rank_width, query_width
    )
    slot_cols = slot_map
    parts_a = lax.all_to_all(
        jnp.einsum("dsr,so->odr", part_a, slot_cols, precision=HIGHEST),
        "seq",
        split_axis=0,
        concat_axis=0,
        tiled=True,
    )
    slot_cols = slot_map
    parts_b = lax.all_to_all(
        jnp.einsum("srf,so->orf", part_b, slot_cols, precision=HIGHEST),
        "seq",
        split_axis=0,
        concat_axis=0,
        tiled=True,
    )
    down_gradient = jnp.sum(parts_a, axis=0, keepdims=True)
    up_gradient = jnp.sum(parts_b, axis=0, keepdims=True)
    return (down_gradient * ADAPTER_SCALE, up_gradient * ADAPTER_SCALE)


def solution(mesh):
    return jax.shard_map(
        on_device,
        mesh=mesh,
        in_specs=(
            P(("seq", "head"), None),
            P(("seq", "head"), None),
            P(("seq", "head"), None),
            P(("seq", "head"), None),
            P(("seq", "head"), None),
            P(("seq", "head"), None),
            P("seq", None, "head"),
            P("seq", None),
            P("seq", None),
            P(),
        ),
        out_specs=(P("seq", "head", None), P("seq", None, "head")),
        check_vma=False,
    )
```

profile of v0, /device:TPU:0, one launch (start us, length us, event | category | flops | bytes accessed | tf_op | source)
XLA Modules:
  0.0 195.0 jit_solution(7095548714196019149)
XLA Ops:
  0.6 1.3 tile.2
  1.9 6.3 %all-to-all-start.4 = ((bf16[128,4,16]{0,2,1:T(8,128)(2,1)}), bf16[128,4,16]{0,2,1:T(8,128)(2,1)S(1)}, u32[]{:S(2)}, u32[]{:S(2)}) async-start(bf16[128,4,16]{0,2,1:T(8,128)(2,1)} %tile.2), calls=%async_computation.4 | async-start | bytes 32768 | tf_op jit(solution)/shard_map/all_to_all | solution.py:86
  8.2 2.4 %copy.102 = bf16[16,4,8,1024]{3,2,0,1:T(8,128)(2,1)} copy(bf16[16,4,8,1024]{3,2,1,0:T(8,128)(2,1)} %bitcast.109) | data formatting | bytes 2097152 | tf_op jit(solution)/shard_map/all_to_all | solution.py:68
  10.6 3.2 %all-to-all-done.4 = bf16[128,4,16]{0,2,1:T(8,128)(2,1)S(1)} async-done(((bf16[128,4,16]{0,2,1:T(8,128)(2,1)}), bf16[128,4,16]{0,2,1:T(8,128)(2,1)S(1)}, u32[]{:S(2)}, u32[]{:S(2)}) %all-to-all-start.4) | async-done | bytes 16416 | tf_op jit(solution)/shard_map/all_to_all | solution.py:86
  13.9 3.5 %all-to-all-start = ((bf16[128,4,1024]{2,0,1:T(8,128)(2,1)}), bf16[128,4,1024]{2,0,1:T(8,128)(2,1)S(1)}, u32[]{:S(2)}, u32[]{:S(2)}) async-start(bf16[128,4,1024]{2,0,1:T(8,128)(2,1)} %bitcast.88), calls=%async_computation | async-start | bytes 2097152 | tf_op jit(solution)/shard_map/all_to_all | solution.py:68
  17.6 1.1 copy.101
  18.7 23.2 %all-to-all-done = bf16[128,4,1024]{2,0,1:T(8,128)(2,1)S(1)} async-done(((bf16[128,4,1024]{2,0,1:T(8,128)(2,1)}), bf16[128,4,1024]{2,0,1:T(8,128)(2,1)S(1)}, u32[]{:S(2)}, u32[]{:S(2)}) %all-to-all-start) | async-done | bytes 1048608 | tf_op jit(solution)/shard_map/all_to_all | solution.py:68
  41.9 3.5 %all-to-all-start.1 = ((bf16[128,4,1024]{2,0,1:T(8,128)(2,1)}), bf16[128,4,1024]{2,0,1:T(8,128)(2,1)S(1)}, u32[]{:S(2)}, u32[]{:S(2)}) async-start(bf16[128,4,1024]{2,0,1:T(8,128)(2,1)} %bitcast.87), calls=%async_computation.1 | async-start | bytes 2097152 | tf_op jit(solution)/shard_map/all_to_all | solution.py:69
  45.5 9.3 %all_gather.11 = bf16[8,16,1024]{2,1,0:T(8,128)(2,1)S(1)} all-gather(bf16[1,16,1024]{2,1,0:T(8,128)(2,1)S(1)} %copy-done.4), channel_id=1, replica_groups=mesh['seq'=8,'head'=4] {'seq'}, dimensions={0}, use_global_device_ids=true | all-gather | bytes 294912 | tf_op jit(solution)/shard_map/all_gather | solution.py:123
  55.0 4.2 %copy.72 = bf16[128,8192]{0,1:T(8,128)(2,1)} copy(bf16[128,8192]{1,0:T(8,128)(2,1)} %param.16) | data formatting | bytes 4194304 | tf_op args[4]
  59.4 21.9 %all_gather.9 = bf16[512,512]{1,0:T(8,128)(2,1)S(1)} all-gather(bf16[128,512]{1,0:T(8,128)(2,1)S(1)} %copy-done.2), channel_id=1, replica_groups=mesh['seq'=8,'head'=4] {'head'}, dimensions={0}, use_global_device_ids=true | all-gather | bytes 655360 | tf_op jit(solution)/shard_map/all_gather | solution.py:72
  81.3 15.4 %all_gather.10 = bf16[512,512]{1,0:T(8,128)(2,1)S(1)} all-gather(bf16[128,512]{1,0:T(8,128)(2,1)S(1)} %copy-done.3), channel_id=1, replica_groups=mesh['seq'=8,'head'=4] {'head'}, dimensions={0}, use_global_device_ids=true | all-gather | bytes 655360 | tf_op jit(solution)/shard_map/all_gather | solution.py:73
  96.8 1.0 convolution_convert_fusion.1
  98.0 1.2 copy.67
  99.2 4.0 %all-to-all-start.2 = ((bf16[128,4,2048]{0,2,1:T(8,128)(2,1)}), bf16[128,4,2048]{0,2,1:T(8,128)(2,1)S(1)}, u32[]{:S(2)}, u32[]{:S(2)}) async-start(bf16[128,4,2048]{0,2,1:T(8,128)(2,1)} %bitcast.18), calls=%async_computation.2 | async-start | bytes 4194304 | tf_op jit(solution)/shard_map/all_to_all | solution.py:85
  103.5 1.2 copy.68
  104.8 1.2 reshape.170
  106.0 32.3 %while.10 = (s32[]{:T(128)}, bf16[8,512,128]{1,2,0:T(8,128)(2,1)}, s32[512]{0:T(512)S(1)}, bf16[8,512,128]{2,1,0:T(8,128)(2,1)}, bf16[8,512,128]{2,1,0:T(8,128)(...) while((s32[]{:T(128)}, bf16[8,512,128]{1,2,0:T(8,128)(2,1)}, ...), condition=%wide.region_7.8_spmd, body=%wide.region_3.7_spmd.sunk | while | flops 206109184 | bytes 7627353 | solution.py:107
  106.0 1.2 fusion.52
  107.4 1.3 multiply_reduce_fusion.2
  110.0 1.2 fusion.52
  111.4 1.3 multiply_reduce_fusion.2
  114.0 1.2 fusion.52
  115.4 1.3 multiply_reduce_fusion.2
  117.4 0.7 constant_dynamic-update-slice_fusion.2
  118.1 1.2 fusion.52
  119.5 1.3 multiply_reduce_fusion.2
  122.1 1.2 fusion.52
  123.5 1.3 multiply_reduce_fusion.2
  126.1 1.2 fusion.52
  127.5 1.3 multiply_reduce_fusion.2
  130.2 1.2 fusion.52
  131.6 1.3 multiply_reduce_fusion.2
  134.2 1.2 fusion.52
  135.6 1.3 multiply_reduce_fusion.2
  137.5 0.7 constant_dynamic-update-slice_fusion.2
  138.2 1.7 fusion.23
  139.9 19.5 %psum.7 = bf16[512,16]{0,1:T(8,128)(2,1)S(1)} all-reduce(f32[512,16]{0,1:T(8,128)S(1)} %fusion.23), channel_id=1, replica_groups=mesh['seq'=8,'head'=4] {'head'}, use_global_device_ids=true, to_apply=%region_9.10 | all-reduce | flops 8192 | bytes 49152 | tf_op jit(solution)/shard_map/psum | solution.py:138
  160.3 1.1 copy.79
  161.4 4.3 %all-to-all-start.5 = ((f32[8,16,1024]{2,1,0:T(8,128)}), f32[8,16,1024]{2,1,0:T(8,128)S(1)}, u32[]{:S(2)}, u32[]{:S(2)}) async-start(f32[8,16,1024]{2,1,0:T(8,128)} %copy.79), calls=%async_computation.5 | async-start | bytes 1048576 | tf_op jit(solution)/shard_map/all_to_all | solution.py:163
  165.7 2.7 %copy.73 = bf16[4,128,2048]{2,1,0:T(8,128)(2,1)} copy(bf16[4,128,2048]{1,2,0:T(8,128)(2,1)S(1)} %bitcast.101) | data formatting | bytes 4194304 | tf_op jit(solution)/shard_map/all_to_all | solution.py:85
  168.4 2.0 %fusion.39 = f32[128,2048]{1,0:T(8,128)S(1)} fusion(bf16[512,128]{0,1:T(8,128)(2,1)S(1)} %bitcast.114, bf16[512,2048]{1,0:T(8,128)(2,1)} %bitcast.102), kind=kOutput, calls=%fused_computation.60 | convolution fusion | flops 268435456 | bytes 3276800 | tf_op jit(solution)/shard_map/td,tc->dc/dot_general | solution.py:148
  170.4 1.2 fusion.24
  171.6 1.6 copy.75
  173.2 2.2 %all-to-all-done.5 = f32[8,16,1024]{2,1,0:T(8,128)S(1)} async-done(((f32[8,16,1024]{2,1,0:T(8,128)}), f32[8,16,1024]{2,1,0:T(8,128)S(1)}, u32[]{:S(2)}, u32[]{:S(2)}) %all-to-all-start.5) | async-done | bytes 524320 | tf_op jit(solution)/shard_map/all_to_all | solution.py:163
  175.4 3.6 %all-to-all-start.3 = ((f32[8,2048,16]{1,2,0:T(8,128)}), f32[8,2048,16]{1,2,0:T(8,128)S(1)}, u32[]{:S(2)}, u32[]{:S(2)}) async-start(f32[8,2048,16]{1,2,0:T(8,128)} %copy.75), calls=%async_computation.3 | async-start | bytes 2097152 | tf_op jit(solution)/shard_map/all_to_all | solution.py:155
  179.6 14.7 %all-to-all-done.3 = f32[8,2048,16]{1,2,0:T(8,128)S(1)} async-done(((f32[8,2048,16]{1,2,0:T(8,128)}), f32[8,2048,16]{1,2,0:T(8,128)S(1)}, u32[]{:S(2)}, u32[]{:S(2)}) %all-to-all-start.3) | async-done | bytes 1048608 | tf_op jit(solution)/shard_map/all_to_all | solution.py:155
  194.4 0.7 multiply_bitcast_fusion.1
  (66 shorter events, 13.6 us)
Async XLA Ops:
  1.9 11.9 %all-to-all-start.4 = ((bf16[128,4,16]{0,2,1:T(8,128)(2,1)}), bf16[128,4,16]{0,2,1:T(8,128)(2,1)S(1)}, u32[]{:S(2)}, u32[]{:S(2)}) async-start(bf16[128,4,16]{0,2,1:T(8,128)(2,1)} %tile.2), calls=%async_computation.4 | async-start | bytes 32768 | tf_op jit(solution)/shard_map/all_to_all | solution.py:86
  8.2 9.2 %copy-start.6 = (s32[1,8]{1,0:T(1,128)S(1)}, s32[1,8]{1,0:T(1,128)}, u32[]{:S(2)}) copy-start(s32[1,8]{1,0:T(1,128)} %param.19) | copy-start | bytes 100
  8.2 9.4 %copy-start = (bf16[128,4096]{1,0:T(8,128)(2,1)S(1)}, bf16[128,4096]{1,0:T(8,128)(2,1)}, u32[]{:S(2)}) copy-start(bf16[128,4096]{1,0:T(8,128)(2,1)} %param.15) | copy-start | bytes 3145732
  13.9 28.1 %all-to-all-start = ((bf16[128,4,1024]{2,0,1:T(8,128)(2,1)}), bf16[128,4,1024]{2,0,1:T(8,128)(2,1)S(1)}, u32[]{:S(2)}, u32[]{:S(2)}) async-start(bf16[128,4,1024]{2,0,1:T(8,128)(2,1)} %bitcast.88), calls=%async_computation | async-start | bytes 2097152 | tf_op jit(solution)/shard_map/all_to_all | solution.py:68
  17.6 27.8 %copy-start.4 = (bf16[1,16,1024]{2,1,0:T(8,128)(2,1)S(1)}, bf16[1,16,1024]{2,1,0:T(8,128)(2,1)}, u32[]{:S(2)}) copy-start(bf16[1,16,1024]{2,1,0:T(8,128)(2,1)} %param.18) | copy-start | bytes 98308
  41.9 57.3 %all-to-all-start.1 = ((bf16[128,4,1024]{2,0,1:T(8,128)(2,1)}), bf16[128,4,1024]{2,0,1:T(8,128)(2,1)S(1)}, u32[]{:S(2)}, u32[]{:S(2)}) async-start(bf16[128,4,1024]{2,0,1:T(8,128)(2,1)} %bitcast.87), calls=%async_computation.1 | async-start | bytes 2097152 | tf_op jit(solution)/shard_map/all_to_all | solution.py:69
  54.9 4.3 %copy-start.5 = (s32[1,8]{1,0:T(1,128)S(1)}, s32[1,8]{1,0:T(1,128)}, u32[]{:S(2)}) copy-start(s32[1,8]{1,0:T(1,128)} %param.20) | copy-start | bytes 100
  54.9 4.3 %copy-start.7 = (s32[8]{0:T(128)S(1)}, s32[8]{0:T(128)}, u32[]{:S(2)}) copy-start(s32[8]{0:T(128)} %param.21) | copy-start | bytes 100
  55.0 4.5 %copy-start.2 = (bf16[128,512]{1,0:T(8,128)(2,1)S(1)}, bf16[128,512]{1,0:T(8,128)(2,1)}, u32[]{:S(2)}) copy-start(bf16[128,512]{1,0:T(8,128)(2,1)} %param.13) | copy-start | bytes 393220
  55.0 26.3 %copy-start.3 = (bf16[128,512]{1,0:T(8,128)(2,1)S(1)}, bf16[128,512]{1,0:T(8,128)(2,1)}, u32[]{:S(2)}) copy-start(bf16[128,512]{1,0:T(8,128)(2,1)} %param.14) | copy-start | bytes 393220
  99.2 62.2 %all-to-all-start.2 = ((bf16[128,4,2048]{0,2,1:T(8,128)(2,1)}), bf16[128,4,2048]{0,2,1:T(8,128)(2,1)S(1)}, u32[]{:S(2)}, u32[]{:S(2)}) async-start(bf16[128,4,2048]{0,2,1:T(8,128)(2,1)} %bitcast.18), calls=%async_computation.2 | async-start | bytes 4194304 | tf_op jit(solution)/shard_map/all_to_all | solution.py:85
  138.2 21.2 %copy-start.1 = (bf16[8,512,128]{1,2,0:T(8,128)(2,1)S(1)}, bf16[8,512,128]{1,2,0:T(8,128)(2,1)}, u32[]{:S(2)}) copy-start(bf16[8,512,128]{1,2,0:T(8,128)(2,1)} %get-tuple-element.63) | copy-start | bytes 3145732
  161.4 14.0 %all-to-all-start.5 = ((f32[8,16,1024]{2,1,0:T(8,128)}), f32[8,16,1024]{2,1,0:T(8,128)S(1)}, u32[]{:S(2)}, u32[]{:S(2)}) async-start(f32[8,16,1024]{2,1,0:T(8,128)} %copy.79), calls=%async_computation.5 | async-start | bytes 1048576 | tf_op jit(solution)/shard_map/all_to_all | solution.py:163
  175.4 18.9 %all-to-all-start.3 = ((f32[8,2048,16]{1,2,0:T(8,128)}), f32[8,2048,16]{1,2,0:T(8,128)S(1)}, u32[]{:S(2)}, u32[]{:S(2)}) async-start(f32[8,2048,16]{1,2,0:T(8,128)} %copy.75), calls=%async_computation.3 | async-start | bytes 2097152 | tf_op jit(solution)/shard_map/all_to_all | solution.py:155
where the time goes:
time: 196 us; the launch traced here: 195 us
  blocking collectives  66.1 us (34%)
  waiting for transfers between devices  43.4 us (22%)
  matrix products  31 us (16%)
  starting transfers between devices  25.2 us (13%)
  local copies, waits for them, and re-layouts  24.9 us (13%)
  other arithmetic  3.46 us (2%)
    all_to_all x1, waiting for transfers between devices, on_device(): lax.all_to_all(queries, 'head', split_axis=1, concat_axis=0, tiled=True)  23.2 us
    all_gather x1, blocking collectives, on_device(): lax.all_gather(keys, 'head', axis=0, tiled=True)  21.9 us
    psum x1, blocking collectives, on_device(): rank_low = lax.psum(rank_part, 'head').astype(jnp.bfloat16)  19.5 us
    all_gather x1, blocking collectives, on_device(): lax.all_gather(values, 'head', axis=0, tiled=True)  15.4 us
    all_to_all x1, waiting for transfers between devices, on_device(): lax.all_to_all(jnp.einsum('dsr,so->odr', part_a, slot_cols, precision=HIG...  14.7 us
    dot_general x8, matrix products, one_block(): jnp.einsum('qd,kd->qk', g_rows, v_head, preferred_element_type=jnp.float32)  10.3 us
    dot_general x8, matrix products, one_block(): jnp.einsum('qd,kd->qk', q_rows, k_head, preferred_element_type=jnp.float32)  9.83 us
    all_gather x1, blocking collectives, on_device(): lax.all_gather(adapter_up_weight, 'seq', axis=0, tiled=True)  9.32 us
  transfers between devices with their start and end apart: 6, of which 4 were waited for; matrix products, arithmetic and copies ran while one was open for 29% of the time, Pallas kernels for 0%

commit v1 on v0

v1 whole, which is shorter than its diff:
```python
import functools
import math

import jax
import jax.numpy as jnp
from jax import lax
from jax.experimental import pallas as pl
from jax.experimental.pallas import tpu as pltpu
from jax.sharding import PartitionSpec as P

QUERY_HEADS = 32
KEY_VALUE_HEADS = 4
HEAD_SIZE = 128
GROUP = QUERY_HEADS // KEY_VALUE_HEADS
ADAPTER_SCALE = 2.0
NEVER = -1e30
BF16 = jnp.bfloat16
F32 = jnp.float32
VMEM = pl.BlockSpec(memory_space=pltpu.VMEM)
SMEM = pl.BlockSpec(memory_space=pltpu.SMEM)


def dot(a, b, a_dim, b_dim):
    return lax.dot_general(a, b, (((a_dim,), (b_dim,)), ((), ())), preferred_element_type=F32)


def local_kernel(
    n_halo, by_slot, bits,
    place_ref, length_ref, adapter_ref, owner_ref,
    q_ref, g_ref, k_ref, v_ref, *refs,
):
    halo_refs = refs[:n_halo]
    (w_ref, x_ref, act_ref, *out_refs) = refs[n_halo:-6]
    k_all, v_all, k_turned, bias, dq_turned, rank_all = refs[-6:]
    tok, width = q_ref.shape
    kv_width = k_ref.shape[1]
    n_quarters = w_ref.shape[0]
    rank = act_ref.shape[0]
    n_seg = length_ref.shape[1]
    key_rows = k_all.shape[0]
    seq, head = place_ref[0], place_ref[1]

    start = 0
    for halo_ref in halo_refs:
        rows = halo_ref.shape[0]
        k_all[start : start + rows, :] = halo_ref[:, :kv_width]
        v_all[start : start + rows, :] = halo_ref[:, kv_width:]
        start += rows
    k_all[start:, :] = k_ref[...]
    v_all[start:, :] = v_ref[...]
    k_turned[...] = k_all[...].T

    position = head * tok + lax.broadcasted_iota(jnp.int32, (1, tok), 1)
    seg_start = jnp.zeros((1, tok), jnp.int32)
    adapter = jnp.zeros((1, tok), jnp.int32)
    group = jnp.zeros((1, tok), jnp.int32)
    end = 0
    for s in range(n_seg):
        mine = adapter_ref[0, s]
        goes_to = owner_ref[mine] if by_slot else s
        inside = position >= end
        seg_start = jnp.where(inside, end, seg_start)
        adapter = jnp.where(inside, mine, adapter)
        group = jnp.where(inside, goes_to, group)
        end = end + length_ref[0, s]

    key_position = (
        head * tok - (key_rows - tok) + lax.broadcasted_iota(jnp.int32, (key_rows, tok), 0)
    )
    allowed = (key_position >= seg_start) & (key_position <= position)
    bias[...] = jnp.where(allowed, 0.0, NEVER)

    scale = 1.0 / HEAD_SIZE**0.5
    to_log2 = scale * math.log2(math.e)

    def one_group(kv, carry):
        at_kv = pl.ds(pl.multiple_of(kv * HEAD_SIZE, HEAD_SIZE), HEAD_SIZE)
        k_g = k_all[:, at_kv]
        v_g = v_all[:, at_kv]
        kt_g = k_turned[at_kv, :]
        for i in range(GROUP):
            first = pl.multiple_of((kv * GROUP + i) * HEAD_SIZE, HEAD_SIZE)
            at = pl.ds(first, HEAD_SIZE)
            s = dot(k_g, q_ref[:, at], 1, 1) * to_log2 + bias[...]
            d_prob = dot(v_g, g_ref[:, at], 1, 1)
            weights = jnp.exp2(s - jnp.max(s, axis=0, keepdims=True))
            total = jnp.sum(weights, axis=0, keepdims=True)
            inverse = 1.0 / total
            delta = jnp.sum(weights * d_prob, axis=0, keepdims=True) * inverse
            dscore = (weights * (d_prob - delta) * (inverse * scale)).astype(BF16)
            dq_turned[at, :] = dot(kt_g, dscore, 1, 0).astype(BF16)
        return carry

    lax.fori_loop(0, KEY_VALUE_HEADS, one_group, 0)

    part = width // n_quarters
    rank_all[...] = dot(w_ref[0], dq_turned[0:part, :], 1, 0)
    for i in range(1, n_quarters):
        rank_all[...] += dot(w_ref[i], dq_turned[i * part : (i + 1) * part, :], 1, 0)
    n_adapters = rank_all.shape[0] // rank
    rank_grad = jnp.zeros((rank, tok), F32)
    for a in range(n_adapters):
        rows = rank_all[a * rank : (a + 1) * rank, :]
        rank_grad = rank_grad + jnp.where(adapter == a, rows, 0.0)

    n_groups = 1 << bits
    row = lax.broadcasted_iota(jnp.int32, (n_groups * rank, tok), 0) // rank
    if by_slot:
        turned = jnp.zeros_like(row)
        for b in range(bits):
            turned = turned | (((row >> b) & 1) << (bits - 1 - b))
        row = turned ^ seq
    own = row == group
    rank_low = rank_grad.astype(BF16).astype(F32)
    rank_cols = jnp.where(own, jnp.concatenate([rank_low] * n_groups, axis=0), 0.0).astype(BF16)
    act = act_ref[...].astype(F32)
    act_cols = jnp.where(own, jnp.concatenate([act] * n_groups, axis=0), 0.0).astype(BF16)

    x_part = x_ref.shape[1] // n_quarters
    per = out_refs[0].shape[1]
    for j in range(n_quarters):
        quarter = lax.rem(head + j, n_quarters) if by_slot else j
        at = pl.ds(pl.multiple_of(quarter * x_part, x_part), x_part)
        down = dot(rank_cols, x_ref[:, at], 1, 0).astype(BF16)
        at = pl.ds(pl.multiple_of(quarter * part, part), part)
        up = dot(act_cols, dq_turned[at, :], 1, 1).astype(BF16)
        for o, out_ref in enumerate(out_refs):
            out_ref[j, :, :x_part] = down[o * per : (o + 1) * per, :]
            out_ref[j, :, x_part:] = up[o * per : (o + 1) * per, :]


def on_device(
    queries, keys, values, output_gradient, inputs, adapter_activation,
    adapter_up_weight, segment_length, segment_adapter, owner,
):
    n_head = lax.axis_size("head")
    n_seq = lax.axis_size("seq")
    tok, width = queries.shape
    pack = tok * n_head
    rank = adapter_up_weight.shape[1]
    n_adapters = owner.shape[0]
    n_seg = segment_length.shape[1]
    bits = (n_seg - 1).bit_length()
    by_slot = n_adapters == n_seq == 1 << bits

    need = pack * 3 // 8
    key_values = jnp.concatenate([keys, values], axis=1)
    halos = []
    hop = 1
    while need > 0:
        rows = min(need, tok)
        shift = [(i, i + hop) for i in range(n_head - hop)]
        halos.insert(0, lax.ppermute(key_values[tok - rows :], "head", shift))
        need -= rows
        hop += 1
    key_rows = tok + sum(h.shape[0] for h in halos)

    up_weight = lax.all_gather(adapter_up_weight, ("head", "seq"), axis=0, tiled=True)
    up_weight = up_weight.reshape(n_head, n_adapters * rank, width // n_head)

    place = jnp.stack([lax.axis_index("seq"), lax.axis_index("head")]).astype(jnp.int32)
    out_width = (inputs.shape[1] + width) // n_head
    n_out = 2 if by_slot else 1
    group_rows = (1 << bits) * rank
    outs = pl.pallas_call(
        functools.partial(local_kernel, len(halos), by_slot, bits),
        out_shape=[
            jax.ShapeDtypeStruct((n_head, group_rows // n_out, out_width), BF16)
        ] * n_out,
        in_specs=[SMEM] * 4 + [VMEM] * (7 + len(halos)),
        out_specs=[VMEM] * n_out,
        scratch_shapes=[
            pltpu.VMEM((key_rows, keys.shape[1]), BF16),
            pltpu.VMEM((key_rows, keys.shape[1]), BF16),
            pltpu.VMEM((keys.shape[1], key_rows), BF16),
            pltpu.VMEM((key_rows, tok), F32),
            pltpu.VMEM((width, tok), BF16),
            pltpu.VMEM((n_adapters * rank, tok), F32),
        ],
        compiler_params=pltpu.CompilerParams(vmem_limit_bytes=40 * 2**20),
        cost_estimate=pl.CostEstimate(
            flops=2 * tok * width * key_rows * 3, bytes_accessed=9 * 2**20, transcendentals=tok * key_rows * QUERY_HEADS
        ),
        name="local_gradients",
    )(
        place, segment_length, segment_adapter, owner, queries, output_gradient, keys, values,
        *halos, up_weight, inputs, adapter_activation.T,
    )
    reduce = sum_by_slot if by_slot else sum_by_segment
    total = reduce(outs, bits, segment_adapter, owner, rank) * ADAPTER_SCALE
    down_width = inputs.shape[1] // n_head
    return total[:, :down_width].T[None], total[:, down_width:][None]


def sum_by_slot(outs, bits, segment_adapter, owner, rank):
    n_seq, n_head = lax.axis_size("seq"), lax.axis_size("head")
    keep, send = outs
    for b in range(bits):
        got = lax.ppermute(send, "seq", [(i, i ^ (1 << b)) for i in range(n_seq)])
        both = keep.astype(F32) + got.astype(F32)
        half = both.shape[1] // 2
        if b < bits - 1:
            keep, send = both[:, :half].astype(BF16), both[:, half:].astype(BF16)
    total = both[0]
    for j in range(1, n_head):
        shift = [(i, (i + j) % n_head) for i in range(n_head)]
        total = total + lax.ppermute(both[j].astype(BF16), "head", shift).astype(F32)
    return total


def sum_by_segment(outs, bits, segment_adapter, owner, rank):
    pieces = lax.all_to_all(outs[0], "head", split_axis=0, concat_axis=0, tiled=True)
    part = jnp.sum(pieces.astype(F32), axis=0)
    n_seg, n_seq = segment_adapter.shape[1], lax.axis_size("seq")
    part = part.reshape(-1, rank, part.shape[1])[:n_seg]
    goes_to = owner[segment_adapter[0]]
    slots = (goes_to[:, None] == jnp.arange(n_seq, dtype=jnp.int32)[None, :]).astype(F32)
    spread = jnp.einsum("srw,so->orw", part, slots, precision=lax.Precision.HIGHEST)
    spread = lax.all_to_all(spread.astype(BF16), "seq", split_axis=0, concat_axis=0, tiled=True)
    return jnp.sum(spread.astype(F32), axis=0)


def solution(mesh):
    return jax.shard_map(
        on_device,
        mesh=mesh,
        in_specs=(
            P(("seq", "head"), None),
            P(("seq", "head"), None),
            P(("seq", "head"), None),
            P(("seq", "head"), None),
            P(("seq", "head"), None),
            P(("seq", "head"), None),
            P("seq", None, "head"),
            P("seq", None),
            P("seq", None),
            P(),
        ),
        out_specs=(P("seq", "head", None), P("seq", None, "head")),
        check_vma=False,
    )
```

time: 196 us -> 144 us (0.73)
  blocking collectives: 66.1 us -> 0 us
  waiting for transfers between devices: 43.4 us -> 86.5 us
  matrix products: 31 us -> 0 us
  between operations: 0.86 us -> 14.1 us
  Pallas kernels: 0 us -> 12.7 us
  local copies, waits for them, and re-layouts: 24.9 us -> 13 us
  starting transfers between devices: 25.2 us -> 16.6 us
  other arithmetic: 3.46 us -> 1 us
    all_gather x3 -> x0, blocking collectives: 46.6 us -> none  [the longest x1 21.9 us: on_device(): lax.all_gather(keys, 'head', axis=0, tiled=True)]
    all_gather x0 -> x1, waiting for transfers between devices: none -> 44.1 us  [on_device(): lax.all_gather(adapter_up_weight, ('head', 'seq'), axis=0, tiled=True)]
    all_to_all x6 -> x0, waiting for transfers between devices: 43.4 us -> none  [the longest x1 23.2 us: on_device(): lax.all_to_all(queries, 'head', split_axis=1, concat_axis=0, tiled=True)]
    ppermute x0 -> x8, waiting for transfers between devices: none -> 41.8 us  [the longest x3 30.6 us: sum_by_slot(): got = lax.ppermute(send, 'seq', [(i, i ^ 1 << b) for i in range(n_seq)])]
    dot_general x30 -> x0, matrix products: 31 us -> none  [the longest x8 10.3 us: one_block(): jnp.einsum('qd,kd->qk', g_rows, v_head, preferred_element_type=jnp.float32)]
    all_to_all x6 -> x0, starting transfers between devices: 25.2 us -> none  [the longest x1 6.32 us: on_device(): lax.all_to_all(jnp.tile(adapter_activation, (1, local_head_count)), 'head...]
    psum x1 -> x0, blocking collectives: 19.5 us -> none  [on_device(): rank_low = lax.psum(rank_part, 'head').astype(jnp.bfloat16)]
    ppermute x0 -> x8, starting transfers between devices: none -> 16.5 us  [the longest x2 9.43 us: on_device(): halos.insert(0, lax.ppermute(key_values[tok - rows:], 'head', shift))]
  transfers between devices with their start and end apart: 6 -> 9, of which waited for: 4 -> 7; matrix products, arithmetic and copies ran while one was open for 29% -> 1% of each run, Pallas kernels for 0% -> 0%
where the time goes in v1:
time: 144 us
  waiting for transfers between devices  86.5 us (60%)
  starting transfers between devices  16.6 us (12%)
  between operations  14.1 us (10%)
  local copies, waits for them, and re-layouts  13 us (9%)
  Pallas kernels  12.7 us (9%)
    all_gather x1, waiting for transfers between devices, on_device(): lax.all_gather(adapter_up_weight, ('head', 'seq'), axis=0, tiled=True)  44.1 us
    ppermute x3, waiting for transfers between devices, sum_by_slot(): got = lax.ppermute(send, 'seq', [(i, i ^ 1 << b) for i in range(n_seq)])  30.6 us
    pallas_call x1, Pallas kernels, on_device(): pl.pallas_call(functools.partial(local_kernel, len(halos), by_slot, bits)...  12.7 us
    unnamed x21, local copies, waits for them, and re-layouts  10.6 us
    ppermute x2, starting transfers between devices, on_device(): halos.insert(0, lax.ppermute(key_values[tok - rows:], 'head', shift))  9.43 us
    ppermute x3, waiting for transfers between devices, sum_by_slot(): lax.ppermute(both[j].astype(BF16), 'head', shift).astype(F32)  7.26 us
    ppermute x2, waiting for transfers between devices, on_device(): halos.insert(0, lax.ppermute(key_values[tok - rows:], 'head', shift))  3.91 us
    ppermute x3, starting transfers between devices, sum_by_slot(): lax.ppermute(both[j].astype(BF16), 'head', shift).astype(F32)  3.88 us
  transfers between devices with their start and end apart: 9, of which 7 were waited for; matrix products, arithmetic and copies ran while one was open for 1% of the time, Pallas kernels for 0%

profile of v1, /device:TPU:0, one launch (start us, length us, event | category | flops | bytes accessed | tf_op | source)
XLA Modules:
  0.0 143.9 jit_solution(5584662012738986705)
XLA Ops:
  7.2 0.0 all-gather.2.cloned.1.call-start
  7.2 0.7 all-gather.2.cloned.1.call-update
  7.9 0.9 constant_dynamic-update-slice_fusion.1
  8.8 0.9 constant_dynamic-update-slice_fusion
  9.7 4.9 %collective-permute-start.1 = (bf16[128,1024]{1,0:T(8,128)(2,1)S(1)}, bf16[128,1024]{1,0:T(8,128)(2,1)S(1)}, u32[]{:S(2)}, u32[]{:S(2)}) collective-permute-start(bf16[128,1024]{1,0:T(8,128)(2,1)S(1)} %constant_dynamic-update-slice_fusion), channel_id=1, source_target_pairs={{0,1},{1,2},{2,3},{4,5},{5,6},{6,7},{8,9},{9,10},{10,11},{12,13},{... | collective-permute-start | bytes 786440 | tf_op jit(solution)/shard_map/ppermute | solution.py:153
  14.7 4.5 %collective-permute-start = (bf16[64,1024]{1,0:T(8,128)(2,1)S(1)}, bf16[64,1024]{1,0:T(8,128)(2,1)S(1)}, u32[]{:S(2)}, u32[]{:S(2)}) collective-permute-start(bf16[64,1024]{1,0:T(8,128)(2,1)S(1)} %slice.51), channel_id=1, source_target_pairs={{0,2},{1,3},{4,6},{5,7},{8,10},{9,11},{12,14},{13,15},{16,18},{17,... | collective-permute-start | bytes 393224 | tf_op jit(solution)/shard_map/ppermute | solution.py:153
  19.2 0.1 pad_add_fusion.place_ref
  19.3 3.9 %collective-permute-done.refs_0_ = bf16[64,1024]{1,0:T(8,128)(2,1)S(1)} collective-permute-done((bf16[64,1024]{1,0:T(8,128)(2,1)S(1)}, bf16[64,1024]{1,0:T(8,128)(2,1)S(1)}, u32[]{:S(2)}, u32[]{:S(2)}) %collective-permute-start) | collective-permute-done | bytes 131104 | tf_op jit(solution)/shard_map/ppermute | solution.py:153
  23.2 0.0 collective-permute-done.1.refs_1_
  23.2 44.1 %all-gather.2.cloned.1.call-done = bf16[32,16,1024]{2,1,0:T(8,128)(2,1)} async-done(((bf16[1,16,1024]{2,1,0:T(8,128)(2,1)}), bf16[32,16,1024]{2,1,0:T(8,128)(2,1)}) %all-gather.2.cloned.1.call-update) | async-done | bytes 1048592 | tf_op jit(solution)/shard_map/all_gather | solution.py:158
  67.3 0.0 copy-start
  67.3 1.6 %copy-done = bf16[128,8192]{1,0:T(8,128)(2,1)S(1)} copy-done((bf16[128,8192]{1,0:T(8,128)(2,1)S(1)}, bf16[128,8192]{1,0:T(8,128)(2,1)}, u32[]{:S(2)}) %copy-start) | copy-done | bytes 2097176
  68.9 0.0 copy-start.1
  68.9 1.2 copy-done.1
  70.1 0.0 copy-start.2
  70.1 1.2 copy-done.2
  71.3 0.0 copy-start.3
  71.3 1.2 copy-done.3
  72.5 0.0 copy-start.4
  72.5 0.9 copy-done.4
  73.4 0.0 copy-start.5
  73.4 0.9 copy-done.5
  74.3 0.0 copy-start.6
  74.4 0.7 copy-done.6
  75.0 0.0 copy-start.7
  75.0 0.7 copy-done.7
  75.7 0.7 copy-done.8
  76.4 0.7 copy-done.9
  77.0 12.7 %local_gradients.1 = (bf16[4,64,3072]{2,1,0:T(8,128)(2,1)S(1)}, bf16[4,64,3072]{2,1,0:T(8,128)(2,1)S(1)}) custom-call(s32[2]{0:T(128)S(1)} %pad_add_fusion.place_ref, s32[1,8]{1,0:T(1,128)S(1)} %copy-done.7, s32[1,8]{1,0:T(1,128)S(1)} %copy-done.8, s32[8]{0:T(128)S(1)} %copy-done.9, bf16[128,4096]{1,0:T(8,128)(2,1)S(1)} %copy-done.1, ...), custom_call_target="tpu_custom_call" | custom-call | flops 1006632960 | bytes 9437184 | tf_op jit(solution)/shard_map/local_gradients/pallas_call | solution.py:165
  89.7 0.3 collective-permute-start.2
  90.1 3.1 %collective-permute-done.2 = bf16[4,64,3072]{2,1,0:T(8,128)(2,1)S(1)} collective-permute-done((bf16[4,64,3072]{2,1,0:T(8,128)(2,1)S(1)}, bf16[4,64,3072]{2,1,0:T(8,128)(2,1)S(1)}, u32[]{:S(2)}, u32[]{:S(2)}) %collective-permute-start.2) | collective-permute-done | bytes 1572896 | tf_op jit(solution)/shard_map/ppermute | solution.py:199
  93.2 0.6 add_convert_fusion
  93.8 0.1 slice.53
  93.9 1.3 collective-permute-start.3
  95.2 18.4 %collective-permute-done.3 = bf16[4,32,3072]{2,1,0:T(8,128)(2,1)S(1)} collective-permute-done((bf16[4,32,3072]{2,1,0:T(8,128)(2,1)S(1)}, bf16[4,32,3072]{2,1,0:T(8,128)(2,1)S(1)}, u32[]{:S(2)}, u32[]{:S(2)}) %collective-permute-start.3) | collective-permute-done | bytes 786464 | tf_op jit(solution)/shard_map/ppermute | solution.py:199
  113.7 0.2 add_convert_fusion.1
  113.9 1.5 %collective-permute-start.4 = (bf16[4,16,3072]{2,1,0:T(8,128)(2,1)S(1)}, bf16[4,16,3072]{2,1,0:T(8,128)(2,1)S(1)}, u32[]{:S(2)}, u32[]{:S(2)}) collective-permute-start(bf16[4,16,3072]{2,1,0:T(8,128)(2,1)S(1)} %slice.55), channel_id=1, source_target_pairs={{0,16},{4,20},{8,24},{12,28},{16,0},{20,4},{24,8},{28,12},{1,17},{... | collective-permute-start | bytes 1179656 | tf_op jit(solution)/shard_map/ppermute | solution.py:199
  115.4 9.0 %collective-permute-done.4 = bf16[4,16,3072]{2,1,0:T(8,128)(2,1)S(1)} collective-permute-done((bf16[4,16,3072]{2,1,0:T(8,128)(2,1)S(1)}, bf16[4,16,3072]{2,1,0:T(8,128)(2,1)S(1)}, u32[]{:S(2)}, u32[]{:S(2)}) %collective-permute-start.4) | collective-permute-done | bytes 393248 | tf_op jit(solution)/shard_map/ppermute | solution.py:199
  124.4 0.1 fusion.4
  124.6 0.8 collective-permute-start.5
  125.4 3.1 %collective-permute-start.7 = (bf16[16,3072]{1,0:T(8,128)(2,1)S(1)}, bf16[16,3072]{1,0:T(8,128)(2,1)S(1)}, u32[]{:S(2)}, u32[]{:S(2)}) collective-permute-start(bf16[16,3072]{1,0:T(8,128)(2,1)S(1)} %get-tuple-element.9), channel_id=1, source_target_pairs={{0,3},{1,0},{2,1},{3,2},{4,7},{5,4},{6,5},{7,6},{8,11},{9,8},{10,9... | collective-permute-start | bytes 294920 | tf_op jit(solution)/shard_map/ppermute | solution.py:207
  128.5 0.0 collective-permute-start.6
  128.5 3.5 %collective-permute-done.5 = bf16[16,3072]{1,0:T(8,128)(2,1)S(1)} collective-permute-done((bf16[16,3072]{1,0:T(8,128)(2,1)S(1)}, bf16[16,3072]{1,0:T(8,128)(2,1)S(1)}, u32[]{:S(2)}, u32[]{:S(2)}) %collective-permute-start.5) | collective-permute-done | bytes 98336 | tf_op jit(solution)/shard_map/ppermute | solution.py:207
  131.9 0.0 collective-permute-done.7
  131.9 3.8 %collective-permute-done.6 = bf16[16,3072]{1,0:T(8,128)(2,1)S(1)} collective-permute-done((bf16[16,3072]{1,0:T(8,128)(2,1)S(1)}, bf16[16,3072]{1,0:T(8,128)(2,1)S(1)}, u32[]{:S(2)}, u32[]{:S(2)}) %collective-permute-start.6) | collective-permute-done | bytes 98336 | tf_op jit(solution)/shard_map/ppermute | solution.py:207
  135.7 0.1 fusion.3
  135.8 0.6 slice_bitcast_fusion.5
  136.4 0.7 slice_bitcast_fusion.1
  (5 shorter events, 0.1 us)
Async XLA Ops:
  7.2 60.1 %all-gather.2.cloned.1.call-start = ((), (), s32[]{:S(2)}) async-start(), calls=%async_computation | async-start | bytes 1081344 | tf_op jit(solution)/shard_map/all_gather | solution.py:158
  9.7 13.5 %collective-permute-start.1 = (bf16[128,1024]{1,0:T(8,128)(2,1)S(1)}, bf16[128,1024]{1,0:T(8,128)(2,1)S(1)}, u32[]{:S(2)}, u32[]{:S(2)}) collective-permute-start(bf16[128,1024]{1,0:T(8,128)(2,1)S(1)} %constant_dynamic-update-slice_fusion), channel_id=1, source_target_pairs={{0,1},{1,2},{2,3},{4,5},{5,6},{6,7},{8,9},{9,10},{10,11},{12,13},{... | collective-permute-start | bytes 786440 | tf_op jit(solution)/shard_map/ppermute | solution.py:153
  14.7 8.5 %collective-permute-start = (bf16[64,1024]{1,0:T(8,128)(2,1)S(1)}, bf16[64,1024]{1,0:T(8,128)(2,1)S(1)}, u32[]{:S(2)}, u32[]{:S(2)}) collective-permute-start(bf16[64,1024]{1,0:T(8,128)(2,1)S(1)} %slice.51), channel_id=1, source_target_pairs={{0,2},{1,3},{4,6},{5,7},{8,10},{9,11},{12,14},{13,15},{16,18},{17,... | collective-permute-start | bytes 393224 | tf_op jit(solution)/shard_map/ppermute | solution.py:153
  67.3 1.6 %copy-start = (bf16[128,8192]{1,0:T(8,128)(2,1)S(1)}, bf16[128,8192]{1,0:T(8,128)(2,1)}, u32[]{:S(2)}) copy-start(bf16[128,8192]{1,0:T(8,128)(2,1)} %refs_3_.1) | copy-start | bytes 6291460
  68.9 1.2 copy-start.1
  70.1 1.2 copy-start.2
  71.3 1.2 copy-start.3
  72.5 0.9 copy-start.4
  73.4 0.9 copy-start.5
  74.3 0.7 copy-start.6
  75.0 0.7 copy-start.7
  75.7 0.7 copy-start.8
  76.3 0.7 copy-start.9
  89.7 3.5 %collective-permute-start.2 = (bf16[4,64,3072]{2,1,0:T(8,128)(2,1)S(1)}, bf16[4,64,3072]{2,1,0:T(8,128)(2,1)S(1)}, u32[]{:S(2)}, u32[]{:S(2)}) collective-permute-start(bf16[4,64,3072]{2,1,0:T(8,128)(2,1)S(1)} %get-tuple-element.5), channel_id=1, source_target_pairs={{0,4},{4,0},{8,12},{12,8},{16,20},{20,16},{24,28},{28,24},{1,5},{5... | collective-permute-start | bytes 4718600 | tf_op jit(solution)/shard_map/ppermute | solution.py:199
  93.9 19.8 %collective-permute-start.3 = (bf16[4,32,3072]{2,1,0:T(8,128)(2,1)S(1)}, bf16[4,32,3072]{2,1,0:T(8,128)(2,1)S(1)}, u32[]{:S(2)}, u32[]{:S(2)}) collective-permute-start(bf16[4,32,3072]{2,1,0:T(8,128)(2,1)S(1)} %slice.53), channel_id=1, source_target_pairs={{0,8},{4,12},{8,0},{12,4},{16,24},{20,28},{24,16},{28,20},{1,9},{5... | collective-permute-start | bytes 2359304 | tf_op jit(solution)/shard_map/ppermute | solution.py:199
  113.9 10.5 %collective-permute-start.4 = (bf16[4,16,3072]{2,1,0:T(8,128)(2,1)S(1)}, bf16[4,16,3072]{2,1,0:T(8,128)(2,1)S(1)}, u32[]{:S(2)}, u32[]{:S(2)}) collective-permute-start(bf16[4,16,3072]{2,1,0:T(8,128)(2,1)S(1)} %slice.55), channel_id=1, source_target_pairs={{0,16},{4,20},{8,24},{12,28},{16,0},{20,4},{24,8},{28,12},{1,17},{... | collective-permute-start | bytes 1179656 | tf_op jit(solution)/shard_map/ppermute | solution.py:199
  124.6 7.3 %collective-permute-start.5 = (bf16[16,3072]{1,0:T(8,128)(2,1)S(1)}, bf16[16,3072]{1,0:T(8,128)(2,1)S(1)}, u32[]{:S(2)}, u32[]{:S(2)}) collective-permute-start(bf16[16,3072]{1,0:T(8,128)(2,1)S(1)} %get-tuple-element.8), channel_id=1, source_target_pairs={{0,1},{1,2},{2,3},{3,0},{4,5},{5,6},{6,7},{7,4},{8,9},{9,10},{10,1... | collective-permute-start | bytes 294920 | tf_op jit(solution)/shard_map/ppermute | solution.py:207
  125.4 6.6 %collective-permute-start.7 = (bf16[16,3072]{1,0:T(8,128)(2,1)S(1)}, bf16[16,3072]{1,0:T(8,128)(2,1)S(1)}, u32[]{:S(2)}, u32[]{:S(2)}) collective-permute-start(bf16[16,3072]{1,0:T(8,128)(2,1)S(1)} %get-tuple-element.9), channel_id=1, source_target_pairs={{0,3},{1,0},{2,1},{3,2},{4,7},{5,4},{6,5},{7,6},{8,11},{9,8},{10,9... | collective-permute-start | bytes 294920 | tf_op jit(solution)/shard_map/ppermute | solution.py:207
  128.5 7.3 %collective-permute-start.6 = (bf16[16,3072]{1,0:T(8,128)(2,1)S(1)}, bf16[16,3072]{1,0:T(8,128)(2,1)S(1)}, u32[]{:S(2)}, u32[]{:S(2)}) collective-permute-start(bf16[16,3072]{1,0:T(8,128)(2,1)S(1)} %get-tuple-element.10), channel_id=1, source_target_pairs={{0,2},{1,3},{2,0},{3,1},{4,6},{5,7},{6,4},{7,5},{8,10},{9,11},{10,... | collective-permute-start | bytes 294920 | tf_op jit(solution)/shard_map/ppermute | solution.py:207
Sparse Core Ops, SparseCore 0:
  10.9 56.3 all-gather.1

commit v2 on v1

v2 whole, which is shorter than its diff:
```python
import functools
import math

import jax
import jax.numpy as jnp
from jax import lax
from jax.experimental import pallas as pl
from jax.experimental.pallas import tpu as pltpu
from jax.sharding import PartitionSpec as P

QUERY_HEADS = 32
KEY_VALUE_HEADS = 4
HEAD_SIZE = 128
GROUP = QUERY_HEADS // KEY_VALUE_HEADS
ADAPTER_SCALE = 2.0
NEVER = -1e30
BF16 = jnp.bfloat16
F32 = jnp.float32
I32 = jnp.int32
VMEM = pl.BlockSpec(memory_space=pltpu.VMEM)
SMEM = pl.BlockSpec(memory_space=pltpu.SMEM)
ANY = pl.BlockSpec(memory_space=pl.ANY)


def dot(a, b, a_dim, b_dim):
    return lax.dot_general(a, b, (((a_dim,), (b_dim,)), ((), ())), preferred_element_type=F32)


def of_tokens(position, length_ref, values_of):
    end = 0
    found = None
    for s in range(length_ref.shape[1]):
        new = values_of(s, end)
        if found is None:
            found = [jnp.zeros_like(position) + value for value in new]
        else:
            inside = position >= end
            found = [jnp.where(inside, value, old) for value, old in zip(new, found)]
        end = end + length_ref[0, s]
    return found


def group_rows(rows_of_group, n_groups, width, seq, by_slot):
    row = lax.broadcasted_iota(I32, (n_groups * rows_of_group, width), 0) // rows_of_group
    if by_slot:
        half = n_groups // 2
        row = jnp.where(row < half, row * 2, (row - half) * 2 + 1) ^ seq
    return row


def attention_kernel(
    n_halo, by_slot,
    place_ref, length_ref, adapter_ref, owner_ref,
    q_hbm, g_hbm, k_ref, v_ref, *refs,
):
    halo_refs = refs[:n_halo]
    act_ref, dq_turned, *out_refs = refs[n_halo:-7]
    q_ref, g_ref, q_sem, g_sem, k_all, v_all, k_turned = refs[-7:]
    tok, width = q_ref.shape
    kv_width = k_ref.shape[1]
    rank = act_ref.shape[0]
    n_seg = length_ref.shape[1]
    key_rows = v_all.shape[0]
    seq, head = place_ref[0], place_ref[1]
    per_kv = GROUP * HEAD_SIZE

    def fetch(kv):
        at = pl.ds(kv * per_kv, per_kv)
        return (
            pltpu.make_async_copy(q_hbm.at[:, at], q_ref.at[:, at], q_sem.at[kv]),
            pltpu.make_async_copy(g_hbm.at[:, at], g_ref.at[:, at], g_sem.at[kv]),
        )

    for kv in range(KEY_VALUE_HEADS):
        for copy in fetch(kv):
            copy.start()

    position = head * tok + lax.broadcasted_iota(I32, (1, tok), 1)
    seg_start, group = of_tokens(
        position,
        length_ref,
        lambda s, start: (start, owner_ref[adapter_ref[0, s]] if by_slot else s),
    )
    key_position = (
        head * tok - (key_rows - tok) + lax.broadcasted_iota(I32, (key_rows, tok), 0)
    )
    allowed = (key_position >= seg_start) & (key_position <= position)
    bias = jnp.where(allowed, 0.0, NEVER).astype(BF16)

    for kv in range(KEY_VALUE_HEADS):
        start = 0
        at = slice(kv * HEAD_SIZE, (kv + 1) * HEAD_SIZE)
        for halo_ref in halo_refs:
            rows = halo_ref.shape[0]
            k_all[kv, start : start + rows, :HEAD_SIZE] = halo_ref[:, at]
            v_all[start : start + rows, at] = halo_ref[:, kv_width + at.start : kv_width + at.stop]
            start += rows
        k_all[kv, start:, :HEAD_SIZE] = k_ref[:, at]
        v_all[start:, at] = v_ref[:, at]
        k_all[kv, :, HEAD_SIZE:] = bias
        k_turned[at, :] = k_all[kv, :, :HEAD_SIZE].T

    one = lax.broadcasted_iota(I32, (2 * tok, tok), 0) % tok
    pick = (one == lax.broadcasted_iota(I32, (2 * tok, tok), 1)).astype(F32).astype(BF16)
    scale = 1.0 / HEAD_SIZE**0.5
    to_log2 = scale * math.log2(math.e)

    def one_group(kv, carry):
        for copy in fetch(kv):
            copy.wait()
        at_kv = pl.ds(pl.multiple_of(kv * HEAD_SIZE, HEAD_SIZE), HEAD_SIZE)
        k_g = k_all[kv]
        v_g = v_all[:, at_kv]
        kt_g = k_turned[at_kv, :]
        for i in range(0, GROUP, 2):
            first = (kv * GROUP + i) * HEAD_SIZE
            at = [
                pl.ds(pl.multiple_of(first + n * HEAD_SIZE, HEAD_SIZE), HEAD_SIZE) for n in range(2)
            ]
            q_two = jnp.concatenate([q_ref[:, at[0]], q_ref[:, at[1]]], axis=0)
            g_two = jnp.concatenate([g_ref[:, at[0]], g_ref[:, at[1]]], axis=0)
            s = dot(k_g, jnp.concatenate([q_two, pick], axis=1), 1, 1)
            d_prob = dot(v_g, g_two, 1, 1)
            weights = jnp.exp2((s - jnp.max(s, axis=0, keepdims=True)) * to_log2)
            inverse = 1.0 / jnp.sum(weights, axis=0, keepdims=True)
            delta = jnp.sum(weights * d_prob, axis=0, keepdims=True) * inverse
            dscore = (weights * (d_prob - delta)).astype(BF16)
            dq = dot(kt_g, dscore, 1, 0) * (inverse * scale)
            dq_turned[at[0], :] = dq[:, :tok].astype(BF16)
            dq_turned[at[1], :] = dq[:, tok:].astype(BF16)
        return carry

    lax.fori_loop(0, KEY_VALUE_HEADS, one_group, 0)

    per, n_quarters, _, part = out_refs[0].shape
    n_groups = per * len(out_refs)
    own = group_rows(rank, n_groups, tok, seq, by_slot) == group
    act = jnp.concatenate([act_ref[...].astype(F32)] * n_groups, axis=0)
    act_cols = jnp.where(own, act, 0.0).astype(BF16)
    for j in range(n_quarters):
        quarter = lax.rem(head + j, n_quarters) if by_slot else j
        at = pl.ds(pl.multiple_of(quarter * part, part), part)
        up = dot(act_cols, dq_turned[at, :], 1, 1).astype(BF16)
        for n in range(n_groups):
            out_refs[n // per][n % per, j] = up[n * rank : (n + 1) * rank, :]


def rank_kernel(by_slot, place_ref, length_ref, adapter_ref, dq_ref, *refs):
    *w_refs, out_ref = refs
    tok = dq_ref.shape[1]
    seq, head = place_ref[0], place_ref[1]
    n_adapters, n_quarters, rank, part = w_refs[0].shape
    position = head * tok + lax.broadcasted_iota(I32, (1, tok), 1)
    (adapter,) = of_tokens(position, length_ref, lambda s, start: (adapter_ref[0, s],))
    total = jnp.zeros((rank, tok), F32)
    for c, w_ref in enumerate(w_refs):
        rows = None
        for j in range(n_quarters):
            quarter = lax.rem(head + n_quarters - j, n_quarters) if by_slot else j
            dq = dq_ref[pl.ds(pl.multiple_of(quarter * part, part), part), :]
            new = dot(w_ref[:, j].reshape(n_adapters * rank, part), dq, 1, 0)
            rows = new if rows is None else rows + new
        for m in range(n_adapters):
            a = (2 * m + c) ^ seq if by_slot else m
            total = total + jnp.where(adapter == a, rows[m * rank : (m + 1) * rank, :], 0.0)
    out_ref[...] = total.astype(BF16)


def down_kernel(by_slot, n_quarters, place_ref, length_ref, adapter_ref, owner_ref, x_ref, *refs):
    rank_refs = refs[:n_quarters]
    *out_refs, cols = refs[n_quarters:]
    rank, tok = rank_refs[0].shape
    seq, head = place_ref[0], place_ref[1]
    per = out_refs[0].shape[0]
    n_groups = per * len(out_refs)
    rows = group_rows(rank, n_groups, tok, seq, by_slot)
    for j, rank_ref in enumerate(rank_refs):
        source = lax.rem(head + n_quarters - j, n_quarters)
        position = source * tok + lax.broadcasted_iota(I32, (1, tok), 1)
        (group,) = of_tokens(
            position,
            length_ref,
            lambda s, start: (owner_ref[adapter_ref[0, s]] if by_slot else s,),
        )
        low = jnp.concatenate([rank_ref[...].astype(F32)] * n_groups, axis=0)
        at = pl.ds(pl.multiple_of(source * tok, tok), tok)
        cols[:, at] = jnp.where(rows == group, low, 0.0).astype(BF16)
    step = 512
    for start in range(0, x_ref.shape[1], step):
        at = slice(start, start + step)
        down = dot(cols[...], x_ref[:, at], 1, 0).astype(BF16)
        for n in range(n_groups):
            out_refs[n // per][n % per, :, at] = down[n * rank : (n + 1) * rank, :]


def shifted(x, n_head, j):
    return lax.ppermute(x, "head", [(i, (i + j) % n_head) for i in range(n_head)])


def partnered(x, n_seq, bits):
    return lax.ppermute(x, "seq", [(i, i ^ bits) for i in range(n_seq)])


def on_device(
    queries, keys, values, output_gradient, inputs, adapter_activation,
    adapter_up_weight, segment_length, segment_adapter, owner,
):
    n_head = lax.axis_size("head")
    n_seq = lax.axis_size("seq")
    tok, width = queries.shape
    pack = tok * n_head
    rank = adapter_up_weight.shape[1]
    n_adapters = owner.shape[0]
    n_seg = segment_length.shape[1]
    by_slot = n_adapters == n_seq == 8
    place = jnp.stack([lax.axis_index("seq"), lax.axis_index("head")]).astype(I32)

    need = pack * 3 // 8
    key_values = jnp.concatenate([keys, values], axis=1)
    halos = []
    hop = 1
    while need > 0:
        rows = min(need, tok)
        shift = [(i, i + hop) for i in range(n_head - hop)]
        halos.insert(0, lax.ppermute(key_values[tok - rows :], "head", shift))
        need -= rows
        hop += 1
    key_rows = tok + sum(h.shape[0] for h in halos)

    if by_slot:
        w = [adapter_up_weight] + [shifted(adapter_up_weight, n_head, j) for j in range(1, n_head)]
        w = jnp.concatenate(w, axis=0)[None]
        w = jnp.concatenate([w] + [partnered(w, n_seq, 2 * m) for m in range(1, n_seq // 2)], axis=0)
        up_weight = [w, partnered(w, n_seq, 1)]
    else:
        w = lax.all_gather(adapter_up_weight, "seq", axis=0, tiled=True)
        up_weight = [lax.all_gather(w, "head", axis=1, tiled=False)]

    x = inputs.reshape(tok, n_head, -1).transpose(1, 0, 2)
    x = lax.all_to_all(x, "head", split_axis=0, concat_axis=0, tiled=True)
    x = x.reshape(pack, -1)

    n_out = 2 if by_slot else 1
    n_groups = n_seq if by_slot else n_seg
    part = width // n_head
    params = pltpu.CompilerParams(vmem_limit_bytes=32 * 2**20)
    dq_turned, *up = pl.pallas_call(
        functools.partial(attention_kernel, len(halos), by_slot),
        out_shape=[jax.ShapeDtypeStruct((width, tok), BF16)]
        + [jax.ShapeDtypeStruct((n_groups // n_out, n_head, rank, part), BF16)] * n_out,
        in_specs=[SMEM] * 4 + [ANY] * 2 + [VMEM] * (3 + len(halos)),
        out_specs=[VMEM] * (1 + n_out),
        scratch_shapes=[
            pltpu.VMEM((tok, width), BF16),
            pltpu.VMEM((tok, width), BF16),
            pltpu.SemaphoreType.DMA((KEY_VALUE_HEADS,)),
            pltpu.SemaphoreType.DMA((KEY_VALUE_HEADS,)),
            pltpu.VMEM((KEY_VALUE_HEADS, key_rows, 2 * HEAD_SIZE), BF16),
            pltpu.VMEM((key_rows, keys.shape[1]), BF16),
            pltpu.VMEM((keys.shape[1], key_rows), BF16),
        ],
        compiler_params=params,
        cost_estimate=pl.CostEstimate(
            flops=2 * tok * width * key_rows * 3,
            bytes_accessed=4 * tok * width * 2,
            transcendentals=tok * key_rows * QUERY_HEADS,
        ),
        name="attention",
    )(
        place, segment_length, segment_adapter, owner, queries, output_gradient, keys, values,
        *halos, adapter_activation.T,
    )

    rank_low = pl.pallas_call(
        functools.partial(rank_kernel, by_slot),
        out_shape=jax.ShapeDtypeStruct((rank, tok), BF16),
        in_specs=[SMEM] * 3 + [VMEM] * (1 + len(up_weight)),
        out_specs=VMEM,
        compiler_params=params,
        name="rank_gradient",
    )(place, segment_length, segment_adapter, dq_turned, *up_weight)
    rank_lows = [rank_low] + [shifted(rank_low, n_head, j) for j in range(1, n_head)]

    down = pl.pallas_call(
        functools.partial(down_kernel, by_slot, n_head),
        out_shape=[jax.ShapeDtypeStruct((n_groups // n_out, rank, x.shape[1]), BF16)] * n_out,
        in_specs=[SMEM] * 4 + [VMEM] * (1 + n_head),
        out_specs=[VMEM] * n_out,
        scratch_shapes=[pltpu.VMEM((n_groups * rank, pack), BF16)],
        compiler_params=params,
        name="down_parts",
    )(place, segment_length, segment_adapter, owner, x, *rank_lows)

    if by_slot:
        up = over_seq(up, n_seq)
        total = up[0]
        for j in range(1, n_head):
            total = total + shifted(up[j].astype(BF16), n_head, j).astype(F32)
        up, down = total, over_seq(down, n_seq)
    else:
        up = lax.all_to_all(up[0], "head", split_axis=1, concat_axis=1, tiled=True)
        up = spread(jnp.sum(up.astype(F32), axis=1), segment_adapter, owner, n_seq)
        down = spread(down[0].astype(F32), segment_adapter, owner, n_seq)
    return down.T[None] * ADAPTER_SCALE, up[None] * ADAPTER_SCALE


def over_seq(parts, n_seq):
    keep, send = parts
    both = (keep.astype(F32) + partnered(send, n_seq, 1).astype(F32)).astype(BF16)
    total = both[0].astype(F32)
    for m in range(1, n_seq // 2):
        total = total + partnered(both[m], n_seq, 2 * m).astype(F32)
    return total


def spread(part, segment_adapter, owner, n_seq):
    goes_to = owner[segment_adapter[0]]
    slots = (goes_to[:, None] == jnp.arange(n_seq, dtype=I32)[None, :]).astype(F32)
    slotted = jnp.einsum("srw,so->orw", part, slots, precision=lax.Precision.HIGHEST)
    slotted = lax.all_to_all(slotted.astype(BF16), "seq", split_axis=0, concat_axis=0, tiled=True)
    return jnp.sum(slotted.astype(F32), axis=0)


def solution(mesh):
    return jax.shard_map(
        on_device,
        mesh=mesh,
        in_specs=(
            P(("seq", "head"), None),
            P(("seq", "head"), None),
            P(("seq", "head"), None),
            P(("seq", "head"), None),
            P(("seq", "head"), None),
            P(("seq", "head"), None),
            P("seq", None, "head"),
            P("seq", None),
            P("seq", None),
            P(),
        ),
        out_specs=(P("seq", "head", None), P("seq", None, "head")),
        check_vma=False,
    )
```

time: 144 us -> 123 us (0.85)
  waiting for transfers between devices: 86.5 us -> 49.4 us
  starting transfers between devices: 16.6 us -> 52.3 us
  between operations: 14.1 us -> 0.85 us
  local copies, waits for them, and re-layouts: 13 us -> 8.11 us
  Pallas kernels: 12.7 us -> 10.4 us
    all_gather x1 -> x0, waiting for transfers between devices: 44.1 us -> none  [on_device(): lax.all_gather(adapter_up_weight, ('head', 'seq'), axis=0, tiled=True)]
    ppermute x6 -> x21, starting transfers between devices: 7.1 us -> 37.6 us  [the longest x9 26.8 us: shifted(): lax.ppermute(x, 'head', [(i, (i + j) % n_head) for i in range(n_head)])]
    ppermute x2, waiting for transfers between devices: 3.91 us -> 31.3 us  [on_device(): halos.insert(0, lax.ppermute(key_values[tok - rows:], 'head', shift))]
    ppermute x6 -> x21, waiting for transfers between devices: 37.8 us -> 18.1 us  [the longest x9 11 us: shifted(): lax.ppermute(x, 'head', [(i, (i + j) % n_head) for i in range(n_head)])]
    unnamed x21 -> x19, local copies, waits for them, and re-layouts: 10.6 us -> 2.61 us
    all_to_all x0 -> x1, starting transfers between devices: none -> 6.46 us  [on_device(): x = lax.all_to_all(x, 'head', split_axis=0, concat_axis=0, tiled=True)]
    reshape x0 -> x1, local copies, waits for them, and re-layouts: none -> 3.2 us  [on_device(): x = inputs.reshape(tok, n_head, -1).transpose(1, 0, 2)]
    pallas_call x1 -> x3, Pallas kernels: 12.7 us -> 10.4 us  [the longest x1 8.32 us: on_device(): pl.pallas_call(functools.partial(attention_kernel, len(halos), by_slot),...]
  transfers between devices with their start and end apart: 9 -> 24, of which waited for: 7 -> 12; matrix products, arithmetic and copies ran while one was open for 1% -> 3% of each run, Pallas kernels for 0% -> 8%
where the time goes in v2:
time: 123 us
  starting transfers between devices  52.3 us (43%)
  waiting for transfers between devices  49.4 us (40%)
  Pallas kernels  10.4 us (8%)
  local copies, waits for them, and re-layouts  8.11 us (7%)
  other arithmetic  1.85 us (2%)
    ppermute x2, waiting for transfers between devices, on_device(): halos.insert(0, lax.ppermute(key_values[tok - rows:], 'head', shift))  31.3 us
    ppermute x9, starting transfers between devices, shifted(): lax.ppermute(x, 'head', [(i, (i + j) % n_head) for i in range(n_head)])  26.8 us
    ppermute x9, waiting for transfers between devices, shifted(): lax.ppermute(x, 'head', [(i, (i + j) % n_head) for i in range(n_head)])  11 us
    ppermute x12, starting transfers between devices, partnered(): return lax.ppermute(x, 'seq', [(i, i ^ bits) for i in range(n_seq)])  10.9 us
    pallas_call x1, Pallas kernels, on_device(): pl.pallas_call(functools.partial(attention_kernel, len(halos), by_slot),...  8.32 us
    ppermute x2, starting transfers between devices, on_device(): halos.insert(0, lax.ppermute(key_values[tok - rows:], 'head', shift))  8.2 us
    ppermute x12, waiting for transfers between devices, partnered(): return lax.ppermute(x, 'seq', [(i, i ^ bits) for i in range(n_seq)])  7.13 us
    all_to_all x1, starting transfers between devices, on_device(): x = lax.all_to_all(x, 'head', split_axis=0, concat_axis=0, tiled=True)  6.46 us
  transfers between devices with their start and end apart: 24, of which 12 were waited for; matrix products, arithmetic and copies ran while one was open for 3% of the time, Pallas kernels for 8%

profile of v2, /device:TPU:0, one launch (start us, length us, event | category | flops | bytes accessed | tf_op | source)
XLA Modules:
  0.0 122.9 jit_solution(14977062938989035558)
XLA Ops:
  0.6 3.2 %copy.15 = bf16[16,4,8,2048]{3,2,0,1:T(8,128)(2,1)} copy(bf16[16,4,8,2048]{3,2,1,0:T(8,128)(2,1)} %bitcast.63) | data formatting | bytes 4194304 | tf_op jit(solution)/shard_map/reshape | solution.py:239
  3.9 6.5 %all-to-all-start = ((bf16[4,128,2048]{2,1,0:T(8,128)(2,1)}), bf16[4,128,2048]{2,1,0:T(8,128)(2,1)S(1)}, u32[]{:S(2)}, u32[]{:S(2)}) async-start(bf16[4,128,2048]{2,1,0:T(8,128)(2,1)} %bitcast.62), calls=%async_computation | async-start | bytes 4194304 | tf_op jit(solution)/shard_map/all_to_all | solution.py:240
  10.3 0.7 constant_dynamic-update-slice_fusion.1
  11.0 0.7 constant_dynamic-update-slice_fusion
  11.7 4.6 %collective-permute-start.1 = (bf16[128,1024]{1,0:T(8,128)(2,1)}, bf16[128,1024]{1,0:T(8,128)(2,1)}, u32[]{:S(2)}, u32[]{:S(2)}) collective-permute-start(bf16[128,1024]{1,0:T(8,128)(2,1)} %constant_dynamic-update-slice_fusion), channel_id=1, source_target_pairs={{0,1},{1,2},{2,3},{4,5},{5,6},{6,7},{8,9},{9,10},{10,11},{12,13},{... | collective-permute-start | bytes 786440 | tf_op jit(solution)/shard_map/ppermute | solution.py:225
  16.3 1.6 %slice.55 = bf16[64,1024]{1,0:T(8,128)(2,1)} slice(bf16[128,1024]{1,0:T(8,128)(2,1)} %constant_dynamic-update-slice_fusion), slice={[64:128], [0:1024]} | slice | bytes 262144 | tf_op jit(solution)/shard_map/slice | solution.py:225
  17.9 3.6 %collective-permute-start = (bf16[64,1024]{1,0:T(8,128)(2,1)}, bf16[64,1024]{1,0:T(8,128)(2,1)S(1)}, u32[]{:S(2)}, u32[]{:S(2)}) collective-permute-start(bf16[64,1024]{1,0:T(8,128)(2,1)} %slice.55), channel_id=1, source_target_pairs={{0,2},{1,3},{4,6},{5,7},{8,10},{9,11},{12,14},{13,15},{16,18},{17,... | collective-permute-start | bytes 393224 | tf_op jit(solution)/shard_map/ppermute | solution.py:225
  21.5 0.1 pad_add_fusion.place_ref
  21.5 31.3 %collective-permute-done.refs_0_ = bf16[64,1024]{1,0:T(8,128)(2,1)S(1)} collective-permute-done((bf16[64,1024]{1,0:T(8,128)(2,1)}, bf16[64,1024]{1,0:T(8,128)(2,1)S(1)}, u32[]{:S(2)}, u32[]{:S(2)}) %collective-permute-start) | collective-permute-done | bytes 131104 | tf_op jit(solution)/shard_map/ppermute | solution.py:225
  52.8 1.2 copy-done.6
  54.1 0.7 copy-done.7
  54.8 8.3 %attention.1 = (bf16[4096,128]{1,0:T(8,128)(2,1)S(1)}, bf16[4,4,16,1024]{3,2,1,0:T(8,128)(2,1)S(1)}, bf16[4,4,16,1024]{3,2,1,0:T(8,128)(2,1)S(1)}) custom-call(s32[2]{0:T(128)S(1)} %pad_add_fusion.place_ref, s32[1,8]{1,0:T(1,128)S(1)} %copy-done.2, s32[1,8]{1,0:T(1,128)S(1)} %copy-done.3, s32[8]{0:T(128)S(1)} %copy-done.4, bf16[128,4096]{1,0:T(8,128)(2,1)S(1)} %copy-done.5, ...), custom_call_target="tpu_custom_call" | custom-call | flops 1006632960 | bytes 4194304 | tf_op jit(solution)/shard_map/attention/pallas_call | solution.py:247
  63.1 0.1 collective-permute-start.16
  63.2 16.3 %collective-permute-start.3 = (bf16[1,16,1024]{2,1,0:T(8,128)(2,1)S(1)}, bf16[1,16,1024]{2,1,0:T(8,128)(2,1)S(1)}, u32[]{:S(2)}, u32[]{:S(2)}) collective-permute-start(bf16[1,16,1024]{2,1,0:T(8,128)(2,1)S(1)} %copy-done.8), channel_id=1, source_target_pairs={{0,2},{1,3},{2,0},{3,1},{4,6},{5,7},{6,4},{7,5},{8,10},{9,11},{10,... | collective-permute-start | bytes 98312 | tf_op jit(solution)/shard_map/ppermute | solution.py:197
  79.4 2.8 %collective-permute-start.2 = (bf16[1,16,1024]{2,1,0:T(8,128)(2,1)S(1)}, bf16[1,16,1024]{2,1,0:T(8,128)(2,1)S(1)}, u32[]{:S(2)}, u32[]{:S(2)}) collective-permute-start(bf16[1,16,1024]{2,1,0:T(8,128)(2,1)S(1)} %copy-done.8), channel_id=1, source_target_pairs={{0,1},{1,2},{2,3},{3,0},{4,5},{5,6},{6,7},{7,4},{8,9},{9,10},{10,1... | collective-permute-start | bytes 98312 | tf_op jit(solution)/shard_map/ppermute | solution.py:197
  82.2 1.1 collective-permute-start.4
  83.3 2.0 %collective-permute-done.2 = bf16[1,16,1024]{2,1,0:T(8,128)(2,1)S(1)} collective-permute-done((bf16[1,16,1024]{2,1,0:T(8,128)(2,1)S(1)}, bf16[1,16,1024]{2,1,0:T(8,128)(2,1)S(1)}, u32[]{:S(2)}, u32[]{:S(2)}) %collective-permute-start.2) | collective-permute-done | bytes 32800 | tf_op jit(solution)/shard_map/ppermute | solution.py:197
  85.3 0.9 collective-permute-done.4
  86.2 2.5 %collective-permute-start.7 = (bf16[1,4,16,1024]{3,2,1,0:T(8,128)(2,1)S(1)}, bf16[1,4,16,1024]{3,2,1,0:T(8,128)(2,1)S(1)}, u32[]{:S(2)}, u32[]{:S(2)}) collective-permute-start(bf16[1,4,16,1024]{3,2,1,0:T(8,128)(2,1)S(1)} %maximum_bitcast_fusion), channel_id=1, source_target_pairs={{0,24},{4,28},{8,16},{12,20},{16,8},{20,12},{24,0},{28,4},{1,25},{... | collective-permute-start | bytes 393224 | tf_op jit(solution)/shard_map/ppermute | solution.py:201
  88.7 0.5 collective-permute-start.6
  89.2 0.5 collective-permute-start.5
  89.7 3.2 %collective-permute-done.7 = bf16[1,4,16,1024]{3,2,1,0:T(8,128)(2,1)S(1)} collective-permute-done((bf16[1,4,16,1024]{3,2,1,0:T(8,128)(2,1)S(1)}, bf16[1,4,16,1024]{3,2,1,0:T(8,128)(2,1)S(1)}, u32[]{:S(2)}, u32[]{:S(2)}) %collective-permute-start.7) | collective-permute-done | bytes 131104 | tf_op jit(solution)/shard_map/ppermute | solution.py:201
  92.9 1.5 %collective-permute-done.6 = bf16[1,4,16,1024]{3,2,1,0:T(8,128)(2,1)S(1)} collective-permute-done((bf16[1,4,16,1024]{3,2,1,0:T(8,128)(2,1)S(1)}, bf16[1,4,16,1024]{3,2,1,0:T(8,128)(2,1)S(1)}, u32[]{:S(2)}, u32[]{:S(2)}) %collective-permute-start.6) | collective-permute-done | bytes 131104 | tf_op jit(solution)/shard_map/ppermute | solution.py:201
  94.5 0.1 collective-permute-done.5
  94.6 0.1 pad_maximum_fusion.refs_0_
  94.6 0.1 collective-permute-start.8
  94.7 0.2 add_convert_fusion
  95.0 1.6 %collective-permute-start.17 = (bf16[4,16,1024]{2,1,0:T(8,128)(2,1)S(1)}, bf16[4,16,1024]{2,1,0:T(8,128)(2,1)S(1)}, u32[]{:S(2)}, u32[]{:S(2)}) collective-permute-start(bf16[4,16,1024]{2,1,0:T(8,128)(2,1)S(1)} %get-tuple-element.14), channel_id=1, source_target_pairs={{0,8},{4,12},{8,0},{12,4},{16,24},{20,28},{24,16},{28,20},{1,9},{5... | collective-permute-start | bytes 393224 | tf_op jit(solution)/shard_map/ppermute | solution.py:201
  96.5 1.4 %collective-permute-start.19 = (bf16[4,16,1024]{2,1,0:T(8,128)(2,1)S(1)}, bf16[4,16,1024]{2,1,0:T(8,128)(2,1)S(1)}, u32[]{:S(2)}, u32[]{:S(2)}) collective-permute-start(bf16[4,16,1024]{2,1,0:T(8,128)(2,1)S(1)} %get-tuple-element.15), channel_id=1, source_target_pairs={{0,24},{4,28},{8,16},{12,20},{16,8},{20,12},{24,0},{28,4},{1,25},{... | collective-permute-start | bytes 393224 | tf_op jit(solution)/shard_map/ppermute | solution.py:201
  97.9 0.6 collective-permute-start.18
  98.5 1.0 rank_gradient.1.refs_0_
  99.5 2.8 %collective-permute-start.11 = (bf16[16,128]{1,0:T(8,128)(2,1)S(1)}, bf16[16,128]{1,0:T(8,128)(2,1)S(1)}, u32[]{:S(2)}, u32[]{:S(2)}) collective-permute-start(bf16[16,128]{1,0:T(8,128)(2,1)S(1)} %rank_gradient.1.refs_0_), channel_id=1, source_target_pairs={{0,3},{1,0},{2,1},{3,2},{4,7},{5,4},{6,5},{7,6},{8,11},{9,8},{10,9... | collective-permute-start | bytes 12296 | tf_op jit(solution)/shard_map/ppermute | solution.py:197
  102.3 1.3 %collective-permute-done.11.refs_3_ = bf16[16,128]{1,0:T(8,128)(2,1)S(1)} collective-permute-done((bf16[16,128]{1,0:T(8,128)(2,1)S(1)}, bf16[16,128]{1,0:T(8,128)(2,1)S(1)}, u32[]{:S(2)}, u32[]{:S(2)}) %collective-permute-start.11) | collective-permute-done | bytes 4128 | tf_op jit(solution)/shard_map/ppermute | solution.py:197
  103.7 3.2 %collective-permute-done.10.refs_2_ = bf16[16,128]{1,0:T(8,128)(2,1)S(1)} collective-permute-done((bf16[16,128]{1,0:T(8,128)(2,1)S(1)}, bf16[16,128]{1,0:T(8,128)(2,1)S(1)}, u32[]{:S(2)}, u32[]{:S(2)}) %collective-permute-start.10) | collective-permute-done | bytes 4128 | tf_op jit(solution)/shard_map/ppermute | solution.py:197
  106.8 2.5 %collective-permute-done.9.refs_1_ = bf16[16,128]{1,0:T(8,128)(2,1)S(1)} collective-permute-done((bf16[16,128]{1,0:T(8,128)(2,1)S(1)}, bf16[16,128]{1,0:T(8,128)(2,1)S(1)}, u32[]{:S(2)}, u32[]{:S(2)}) %collective-permute-start.9) | collective-permute-done | bytes 4128 | tf_op jit(solution)/shard_map/ppermute | solution.py:197
  109.3 1.1 down_parts.1
  110.4 0.1 collective-permute-start.12
  110.5 0.1 fusion.11
  110.7 3.8 %collective-permute-start.22 = (bf16[16,1024]{1,0:T(8,128)(2,1)S(1)}, bf16[16,1024]{1,0:T(8,128)(2,1)S(1)}, u32[]{:S(2)}, u32[]{:S(2)}) collective-permute-start(bf16[16,1024]{1,0:T(8,128)(2,1)S(1)} %get-tuple-element.21), channel_id=1, source_target_pairs={{0,3},{1,0},{2,1},{3,2},{4,7},{5,4},{6,5},{7,6},{8,11},{9,8},{10,9... | collective-permute-start | bytes 98312 | tf_op jit(solution)/shard_map/ppermute | solution.py:197
  114.5 0.1 add_convert_fusion.1
  114.6 1.6 %collective-permute-start.13 = (bf16[16,2048]{1,0:T(8,128)(2,1)S(1)}, bf16[16,2048]{1,0:T(8,128)(2,1)S(1)}, u32[]{:S(2)}, u32[]{:S(2)}) collective-permute-start(bf16[16,2048]{1,0:T(8,128)(2,1)S(1)} %get-tuple-element.17), channel_id=1, source_target_pairs={{0,8},{4,12},{8,0},{12,4},{16,24},{20,28},{24,16},{28,20},{1,9},{5... | collective-permute-start | bytes 196616 | tf_op jit(solution)/shard_map/ppermute | solution.py:201
  116.2 1.4 %collective-permute-start.15 = (bf16[16,2048]{1,0:T(8,128)(2,1)S(1)}, bf16[16,2048]{1,0:T(8,128)(2,1)S(1)}, u32[]{:S(2)}, u32[]{:S(2)}) collective-permute-start(bf16[16,2048]{1,0:T(8,128)(2,1)S(1)} %get-tuple-element.18), channel_id=1, source_target_pairs={{0,24},{4,28},{8,16},{12,20},{16,8},{20,12},{24,0},{28,4},{1,25},{... | collective-permute-start | bytes 196616 | tf_op jit(solution)/shard_map/ppermute | solution.py:201
  117.6 0.6 collective-permute-start.14
  118.2 1.1 collective-permute-done.21
  119.3 0.6 fusion.10
  120.0 1.4 %collective-permute-done.15 = bf16[16,2048]{1,0:T(8,128)(2,1)S(1)} collective-permute-done((bf16[16,2048]{1,0:T(8,128)(2,1)S(1)}, bf16[16,2048]{1,0:T(8,128)(2,1)S(1)}, u32[]{:S(2)}, u32[]{:S(2)}) %collective-permute-start.15) | collective-permute-done | bytes 65568 | tf_op jit(solution)/shard_map/ppermute | solution.py:201
  121.4 0.8 collective-permute-done.14
  122.2 0.7 fusion.5
  (36 shorter events, 0.2 us)
Async XLA Ops:
  3.8 6.5 %copy-start = (bf16[128,512]{1,0:T(8,128)(2,1)S(1)}, bf16[128,512]{1,0:T(8,128)(2,1)}, u32[]{:S(2)}) copy-start(bf16[128,512]{1,0:T(8,128)(2,1)} %k_ref.1) | copy-start | bytes 393220
  3.8 7.2 %copy-start.1 = (bf16[128,512]{1,0:T(8,128)(2,1)S(1)}, bf16[128,512]{1,0:T(8,128)(2,1)}, u32[]{:S(2)}) copy-start(bf16[128,512]{1,0:T(8,128)(2,1)} %v_ref.1) | copy-start | bytes 393220
  3.8 49.0 %copy-start.2 = (s32[1,8]{1,0:T(1,128)S(1)}, s32[1,8]{1,0:T(1,128)}, u32[]{:S(2)}) copy-start(s32[1,8]{1,0:T(1,128)} %length_ref.5) | copy-start | bytes 100
  3.8 49.0 %copy-start.3 = (s32[1,8]{1,0:T(1,128)S(1)}, s32[1,8]{1,0:T(1,128)}, u32[]{:S(2)}) copy-start(s32[1,8]{1,0:T(1,128)} %adapter_ref.5) | copy-start | bytes 100
  3.8 49.0 %copy-start.4 = (s32[8]{0:T(128)S(1)}, s32[8]{0:T(128)}, u32[]{:S(2)}) copy-start(s32[8]{0:T(128)} %owner_ref.3) | copy-start | bytes 100
  3.9 49.0 %copy-start.5 = (bf16[128,4096]{1,0:T(8,128)(2,1)S(1)}, bf16[128,4096]{1,0:T(8,128)(2,1)}, u32[]{:S(2)}) copy-start(bf16[128,4096]{1,0:T(8,128)(2,1)} %q_hbm.1) | copy-start | bytes 3145732
  3.9 105.5 %all-to-all-start = ((bf16[4,128,2048]{2,1,0:T(8,128)(2,1)}), bf16[4,128,2048]{2,1,0:T(8,128)(2,1)S(1)}, u32[]{:S(2)}, u32[]{:S(2)}) async-start(bf16[4,128,2048]{2,1,0:T(8,128)(2,1)} %bitcast.62), calls=%async_computation | async-start | bytes 4194304 | tf_op jit(solution)/shard_map/all_to_all | solution.py:240
  11.7 41.1 %collective-permute-start.1 = (bf16[128,1024]{1,0:T(8,128)(2,1)}, bf16[128,1024]{1,0:T(8,128)(2,1)}, u32[]{:S(2)}, u32[]{:S(2)}) collective-permute-start(bf16[128,1024]{1,0:T(8,128)(2,1)} %constant_dynamic-update-slice_fusion), channel_id=1, source_target_pairs={{0,1},{1,2},{2,3},{4,5},{5,6},{6,7},{8,9},{9,10},{10,11},{12,13},{... | collective-permute-start | bytes 786440 | tf_op jit(solution)/shard_map/ppermute | solution.py:225
  17.9 34.9 %collective-permute-start = (bf16[64,1024]{1,0:T(8,128)(2,1)}, bf16[64,1024]{1,0:T(8,128)(2,1)S(1)}, u32[]{:S(2)}, u32[]{:S(2)}) collective-permute-start(bf16[64,1024]{1,0:T(8,128)(2,1)} %slice.55), channel_id=1, source_target_pairs={{0,2},{1,3},{4,6},{5,7},{8,10},{9,11},{12,14},{13,15},{16,18},{17,... | collective-permute-start | bytes 393224 | tf_op jit(solution)/shard_map/ppermute | solution.py:225
  52.8 1.2 copy-start.6
  54.1 0.7 copy-start.7
  54.8 8.4 %copy-start.8 = (bf16[1,16,1024]{2,1,0:T(8,128)(2,1)S(1)}, bf16[1,16,1024]{2,1,0:T(8,128)(2,1)}, u32[]{:S(2)}) copy-start(bf16[1,16,1024]{2,1,0:T(8,128)(2,1)} %param.16) | copy-start | bytes 98308
  63.1 31.6 %collective-permute-start.16 = (bf16[4,4,16,1024]{3,2,1,0:T(8,128)(2,1)S(1)}, bf16[4,4,16,1024]{3,2,1,0:T(8,128)(2,1)S(1)}, u32[]{:S(2)}, u32[]{:S(2)}) collective-permute-start(bf16[4,4,16,1024]{3,2,1,0:T(8,128)(2,1)S(1)} %get-tuple-element.11), channel_id=1, source_target_pairs={{0,4},{4,0},{8,12},{12,8},{16,20},{20,16},{24,28},{28,24},{1,5},{5... | collective-permute-start | bytes 1572872 | tf_op jit(solution)/shard_map/ppermute | solution.py:201
  63.2 20.1 %collective-permute-start.3 = (bf16[1,16,1024]{2,1,0:T(8,128)(2,1)S(1)}, bf16[1,16,1024]{2,1,0:T(8,128)(2,1)S(1)}, u32[]{:S(2)}, u32[]{:S(2)}) collective-permute-start(bf16[1,16,1024]{2,1,0:T(8,128)(2,1)S(1)} %copy-done.8), channel_id=1, source_target_pairs={{0,2},{1,3},{2,0},{3,1},{4,6},{5,7},{6,4},{7,5},{8,10},{9,11},{10,... | collective-permute-start | bytes 98312 | tf_op jit(solution)/shard_map/ppermute | solution.py:197
  79.4 5.8 %collective-permute-start.2 = (bf16[1,16,1024]{2,1,0:T(8,128)(2,1)S(1)}, bf16[1,16,1024]{2,1,0:T(8,128)(2,1)S(1)}, u32[]{:S(2)}, u32[]{:S(2)}) collective-permute-start(bf16[1,16,1024]{2,1,0:T(8,128)(2,1)S(1)} %copy-done.8), channel_id=1, source_target_pairs={{0,1},{1,2},{2,3},{3,0},{4,5},{5,6},{6,7},{7,4},{8,9},{9,10},{10,1... | collective-permute-start | bytes 98312 | tf_op jit(solution)/shard_map/ppermute | solution.py:197
  82.2 3.9 %collective-permute-start.4 = (bf16[1,16,1024]{2,1,0:T(8,128)(2,1)S(1)}, bf16[1,16,1024]{2,1,0:T(8,128)(2,1)S(1)}, u32[]{:S(2)}, u32[]{:S(2)}) collective-permute-start(bf16[1,16,1024]{2,1,0:T(8,128)(2,1)S(1)} %copy-done.8), channel_id=1, source_target_pairs={{0,3},{1,0},{2,1},{3,2},{4,7},{5,4},{6,5},{7,6},{8,11},{9,8},{10,9... | collective-permute-start | bytes 98312 | tf_op jit(solution)/shard_map/ppermute | solution.py:197
  86.2 6.8 %collective-permute-start.7 = (bf16[1,4,16,1024]{3,2,1,0:T(8,128)(2,1)S(1)}, bf16[1,4,16,1024]{3,2,1,0:T(8,128)(2,1)S(1)}, u32[]{:S(2)}, u32[]{:S(2)}) collective-permute-start(bf16[1,4,16,1024]{3,2,1,0:T(8,128)(2,1)S(1)} %maximum_bitcast_fusion), channel_id=1, source_target_pairs={{0,24},{4,28},{8,16},{12,20},{16,8},{20,12},{24,0},{28,4},{1,25},{... | collective-permute-start | bytes 393224 | tf_op jit(solution)/shard_map/ppermute | solution.py:201
  88.7 5.8 %collective-permute-start.6 = (bf16[1,4,16,1024]{3,2,1,0:T(8,128)(2,1)S(1)}, bf16[1,4,16,1024]{3,2,1,0:T(8,128)(2,1)S(1)}, u32[]{:S(2)}, u32[]{:S(2)}) collective-permute-start(bf16[1,4,16,1024]{3,2,1,0:T(8,128)(2,1)S(1)} %maximum_bitcast_fusion), channel_id=1, source_target_pairs={{0,16},{4,20},{8,24},{12,28},{16,0},{20,4},{24,8},{28,12},{1,17},{... | collective-permute-start | bytes 393224 | tf_op jit(solution)/shard_map/ppermute | solution.py:201
  89.2 5.4 %collective-permute-start.5 = (bf16[1,4,16,1024]{3,2,1,0:T(8,128)(2,1)S(1)}, bf16[1,4,16,1024]{3,2,1,0:T(8,128)(2,1)S(1)}, u32[]{:S(2)}, u32[]{:S(2)}) collective-permute-start(bf16[1,4,16,1024]{3,2,1,0:T(8,128)(2,1)S(1)} %maximum_bitcast_fusion), channel_id=1, source_target_pairs={{0,8},{4,12},{8,0},{12,4},{16,24},{20,28},{24,16},{28,20},{1,9},{5... | collective-permute-start | bytes 393224 | tf_op jit(solution)/shard_map/ppermute | solution.py:201
  94.6 3.9 %collective-permute-start.8 = (bf16[4,4,16,1024]{3,2,1,0:T(8,128)(2,1)S(1)}, bf16[4,4,16,1024]{3,2,1,0:T(8,128)(2,1)S(1)}, u32[]{:S(2)}, u32[]{:S(2)}) collective-permute-start(bf16[4,4,16,1024]{3,2,1,0:T(8,128)(2,1)S(1)} %pad_maximum_fusion.refs_0_), channel_id=1, source_target_pairs={{0,4},{4,0},{8,12},{12,8},{16,20},{20,16},{24,28},{28,24},{1,5},{5... | collective-permute-start | bytes 1572872 | tf_op jit(solution)/shard_map/ppermute | solution.py:201
  95.0 15.5 %collective-permute-start.17 = (bf16[4,16,1024]{2,1,0:T(8,128)(2,1)S(1)}, bf16[4,16,1024]{2,1,0:T(8,128)(2,1)S(1)}, u32[]{:S(2)}, u32[]{:S(2)}) collective-permute-start(bf16[4,16,1024]{2,1,0:T(8,128)(2,1)S(1)} %get-tuple-element.14), channel_id=1, source_target_pairs={{0,8},{4,12},{8,0},{12,4},{16,24},{20,28},{24,16},{28,20},{1,9},{5... | collective-permute-start | bytes 393224 | tf_op jit(solution)/shard_map/ppermute | solution.py:201
  96.5 14.0 %collective-permute-start.19 = (bf16[4,16,1024]{2,1,0:T(8,128)(2,1)S(1)}, bf16[4,16,1024]{2,1,0:T(8,128)(2,1)S(1)}, u32[]{:S(2)}, u32[]{:S(2)}) collective-permute-start(bf16[4,16,1024]{2,1,0:T(8,128)(2,1)S(1)} %get-tuple-element.15), channel_id=1, source_target_pairs={{0,24},{4,28},{8,16},{12,20},{16,8},{20,12},{24,0},{28,4},{1,25},{... | collective-permute-start | bytes 393224 | tf_op jit(solution)/shard_map/ppermute | solution.py:201
  97.9 12.6 %collective-permute-start.18 = (bf16[4,16,1024]{2,1,0:T(8,128)(2,1)S(1)}, bf16[4,16,1024]{2,1,0:T(8,128)(2,1)S(1)}, u32[]{:S(2)}, u32[]{:S(2)}) collective-permute-start(bf16[4,16,1024]{2,1,0:T(8,128)(2,1)S(1)} %get-tuple-element.16), channel_id=1, source_target_pairs={{0,16},{4,20},{8,24},{12,28},{16,0},{20,4},{24,8},{28,12},{1,17},{... | collective-permute-start | bytes 393224 | tf_op jit(solution)/shard_map/ppermute | solution.py:201
  99.5 4.1 %collective-permute-start.11 = (bf16[16,128]{1,0:T(8,128)(2,1)S(1)}, bf16[16,128]{1,0:T(8,128)(2,1)S(1)}, u32[]{:S(2)}, u32[]{:S(2)}) collective-permute-start(bf16[16,128]{1,0:T(8,128)(2,1)S(1)} %rank_gradient.1.refs_0_), channel_id=1, source_target_pairs={{0,3},{1,0},{2,1},{3,2},{4,7},{5,4},{6,5},{7,6},{8,11},{9,8},{10,9... | collective-permute-start | bytes 12296 | tf_op jit(solution)/shard_map/ppermute | solution.py:197
  102.3 4.5 %collective-permute-start.10 = (bf16[16,128]{1,0:T(8,128)(2,1)S(1)}, bf16[16,128]{1,0:T(8,128)(2,1)S(1)}, u32[]{:S(2)}, u32[]{:S(2)}) collective-permute-start(bf16[16,128]{1,0:T(8,128)(2,1)S(1)} %rank_gradient.1.refs_0_), channel_id=1, source_target_pairs={{0,2},{1,3},{2,0},{3,1},{4,6},{5,7},{6,4},{7,5},{8,10},{9,11},{10,... | collective-permute-start | bytes 12296 | tf_op jit(solution)/shard_map/ppermute | solution.py:197
  103.7 5.7 %collective-permute-start.9 = (bf16[16,128]{1,0:T(8,128)(2,1)S(1)}, bf16[16,128]{1,0:T(8,128)(2,1)S(1)}, u32[]{:S(2)}, u32[]{:S(2)}) collective-permute-start(bf16[16,128]{1,0:T(8,128)(2,1)S(1)} %rank_gradient.1.refs_0_), channel_id=1, source_target_pairs={{0,1},{1,2},{2,3},{3,0},{4,5},{5,6},{6,7},{7,4},{8,9},{9,10},{10,1... | collective-permute-start | bytes 12296 | tf_op jit(solution)/shard_map/ppermute | solution.py:197
  110.4 4.1 %collective-permute-start.12 = (bf16[4,16,2048]{2,1,0:T(8,128)(2,1)S(1)}, bf16[4,16,2048]{2,1,0:T(8,128)(2,1)S(1)}, u32[]{:S(2)}, u32[]{:S(2)}) collective-permute-start(bf16[4,16,2048]{2,1,0:T(8,128)(2,1)S(1)} %get-tuple-element.9), channel_id=1, source_target_pairs={{0,4},{4,0},{8,12},{12,8},{16,20},{20,16},{24,28},{28,24},{1,5},{5... | collective-permute-start | bytes 786440 | tf_op jit(solution)/shard_map/ppermute | solution.py:201
  110.6 7.0 %collective-permute-start.20 = (bf16[16,1024]{1,0:T(8,128)(2,1)S(1)}, bf16[16,1024]{1,0:T(8,128)(2,1)S(1)}, u32[]{:S(2)}, u32[]{:S(2)}) collective-permute-start(bf16[16,1024]{1,0:T(8,128)(2,1)S(1)} %get-tuple-element.20), channel_id=1, source_target_pairs={{0,1},{1,2},{2,3},{3,0},{4,5},{5,6},{6,7},{7,4},{8,9},{9,10},{10,1... | collective-permute-start | bytes 98312 | tf_op jit(solution)/shard_map/ppermute | solution.py:197
  110.7 7.5 %collective-permute-start.22 = (bf16[16,1024]{1,0:T(8,128)(2,1)S(1)}, bf16[16,1024]{1,0:T(8,128)(2,1)S(1)}, u32[]{:S(2)}, u32[]{:S(2)}) collective-permute-start(bf16[16,1024]{1,0:T(8,128)(2,1)S(1)} %get-tuple-element.21), channel_id=1, source_target_pairs={{0,3},{1,0},{2,1},{3,2},{4,7},{5,4},{6,5},{7,6},{8,11},{9,8},{10,9... | collective-permute-start | bytes 98312 | tf_op jit(solution)/shard_map/ppermute | solution.py:197
  114.5 4.8 %collective-permute-start.21 = (bf16[16,1024]{1,0:T(8,128)(2,1)S(1)}, bf16[16,1024]{1,0:T(8,128)(2,1)S(1)}, u32[]{:S(2)}, u32[]{:S(2)}) collective-permute-start(bf16[16,1024]{1,0:T(8,128)(2,1)S(1)} %get-tuple-element.22), channel_id=1, source_target_pairs={{0,2},{1,3},{2,0},{3,1},{4,6},{5,7},{6,4},{7,5},{8,10},{9,11},{10,... | collective-permute-start | bytes 98312 | tf_op jit(solution)/shard_map/ppermute | solution.py:197
  114.6 5.4 %collective-permute-start.13 = (bf16[16,2048]{1,0:T(8,128)(2,1)S(1)}, bf16[16,2048]{1,0:T(8,128)(2,1)S(1)}, u32[]{:S(2)}, u32[]{:S(2)}) collective-permute-start(bf16[16,2048]{1,0:T(8,128)(2,1)S(1)} %get-tuple-element.17), channel_id=1, source_target_pairs={{0,8},{4,12},{8,0},{12,4},{16,24},{20,28},{24,16},{28,20},{1,9},{5... | collective-permute-start | bytes 196616 | tf_op jit(solution)/shard_map/ppermute | solution.py:201
  116.2 5.2 %collective-permute-start.15 = (bf16[16,2048]{1,0:T(8,128)(2,1)S(1)}, bf16[16,2048]{1,0:T(8,128)(2,1)S(1)}, u32[]{:S(2)}, u32[]{:S(2)}) collective-permute-start(bf16[16,2048]{1,0:T(8,128)(2,1)S(1)} %get-tuple-element.18), channel_id=1, source_target_pairs={{0,24},{4,28},{8,16},{12,20},{16,8},{20,12},{24,0},{28,4},{1,25},{... | collective-permute-start | bytes 196616 | tf_op jit(solution)/shard_map/ppermute | solution.py:201
  117.6 4.6 %collective-permute-start.14 = (bf16[16,2048]{1,0:T(8,128)(2,1)S(1)}, bf16[16,2048]{1,0:T(8,128)(2,1)S(1)}, u32[]{:S(2)}, u32[]{:S(2)}) collective-permute-start(bf16[16,2048]{1,0:T(8,128)(2,1)S(1)} %get-tuple-element.19), channel_id=1, source_target_pairs={{0,16},{4,20},{8,24},{12,28},{16,0},{20,4},{24,8},{28,12},{1,17},{... | collective-permute-start | bytes 196616 | tf_op jit(solution)/shard_map/ppermute | solution.py:201

commit v3 on v2

v3 whole, which is shorter than its diff:
```python
import functools
import math

import jax
import jax.numpy as jnp
from jax import lax
from jax.experimental import pallas as pl
from jax.experimental.pallas import tpu as pltpu
from jax.sharding import PartitionSpec as P

QUERY_HEADS = 32
KEY_VALUE_HEADS = 4
HEAD_SIZE = 128
GROUP = QUERY_HEADS // KEY_VALUE_HEADS
ADAPTER_SCALE = 2.0
NEVER = -1e30
BF16 = jnp.bfloat16
F32 = jnp.float32
I32 = jnp.int32
VMEM = pl.BlockSpec(memory_space=pltpu.VMEM)
SMEM = pl.BlockSpec(memory_space=pltpu.SMEM)
ANY = pl.BlockSpec(memory_space=pl.ANY)


def dot(a, b, a_dim, b_dim):
    return lax.dot_general(a, b, (((a_dim,), (b_dim,)), ((), ())), preferred_element_type=F32)


def of_tokens(position, length_ref, values_of):
    end = 0
    found = None
    for s in range(length_ref.shape[1]):
        new = values_of(s, end)
        if found is None:
            found = [jnp.zeros_like(position) + value for value in new]
        else:
            inside = position >= end
            found = [jnp.where(inside, value, old) for value, old in zip(new, found)]
        end = end + length_ref[0, s]
    return found


def group_rows(rows_of_group, n_groups, width, seq, by_slot):
    row = lax.broadcasted_iota(I32, (n_groups * rows_of_group, width), 0) // rows_of_group
    if by_slot:
        half = n_groups // 2
        row = jnp.where(row < half, row * 2, (row - half) * 2 + 1) ^ seq
    return row


def pack_kernel(n_out, tails, k_ref, v_ref, *out_refs):
    part = k_ref.shape[1] // n_out
    tok = k_ref.shape[0]
    for h in range(n_out):
        at = slice(h * part, (h + 1) * part)
        for i, rows in enumerate(tails):
            out_ref = out_refs[h * len(tails) + i]
            out_ref[:, :part] = k_ref[tok - rows :, at]
            out_ref[:, part:] = v_ref[tok - rows :, at]


def attention_kernel(
    n_halo, by_slot, first_kv, n_kv,
    place_ref, length_ref, adapter_ref, owner_ref,
    q_hbm, g_hbm, k_ref, v_ref, *refs,
):
    halo_refs = refs[:n_halo]
    n_before = 2 if first_kv else 0
    before = refs[n_halo : n_halo + n_before]
    dq_turned, *up_refs = refs[n_halo + n_before : -7]
    q_ref, g_ref, q_sem, g_sem, k_all, v_all, k_turned = refs[-7:]
    tok = q_ref.shape[0]
    kv_width = n_kv * HEAD_SIZE
    key_rows = v_all.shape[0]
    seq, head = place_ref[0], place_ref[1]
    per_kv = GROUP * HEAD_SIZE

    def fetch(kv):
        to = pl.ds(kv * per_kv, per_kv)
        at = pl.ds((first_kv + kv) * per_kv, per_kv)
        return (
            pltpu.make_async_copy(q_hbm.at[:, at], q_ref.at[:, to], q_sem.at[kv]),
            pltpu.make_async_copy(g_hbm.at[:, at], g_ref.at[:, to], g_sem.at[kv]),
        )

    for kv in range(n_kv):
        for copy in fetch(kv):
            copy.start()

    position = head * tok + lax.broadcasted_iota(I32, (1, tok), 1)
    seg_start, group = of_tokens(
        position,
        length_ref,
        lambda s, start: (start, owner_ref[adapter_ref[0, s]] if by_slot else s),
    )
    key_position = (
        head * tok - (key_rows - tok) + lax.broadcasted_iota(I32, (key_rows, tok), 0)
    )
    allowed = (key_position >= seg_start) & (key_position <= position)
    bias = jnp.where(allowed, 0.0, NEVER).astype(BF16)

    for kv in range(n_kv):
        start = 0
        at = slice(kv * HEAD_SIZE, (kv + 1) * HEAD_SIZE)
        for halo_ref in halo_refs:
            rows = halo_ref.shape[0]
            k_all[kv, start : start + rows, :HEAD_SIZE] = halo_ref[:, at]
            v_all[start : start + rows, at] = halo_ref[:, kv_width + at.start : kv_width + at.stop]
            start += rows
        own = slice((first_kv + kv) * HEAD_SIZE, (first_kv + kv + 1) * HEAD_SIZE)
        k_all[kv, start:, :HEAD_SIZE] = k_ref[:, own]
        v_all[start:, at] = v_ref[:, own]
        k_all[kv, :, HEAD_SIZE:] = bias
        k_turned[at, :] = k_all[kv, :, :HEAD_SIZE].T

    one = lax.broadcasted_iota(I32, (2 * tok, tok), 0) % tok
    pick = (one == lax.broadcasted_iota(I32, (2 * tok, tok), 1)).astype(F32).astype(BF16)
    scale = 1.0 / HEAD_SIZE**0.5
    to_log2 = scale * math.log2(math.e)

    def one_group(kv, carry):
        for copy in fetch(kv):
            copy.wait()
        at_kv = pl.ds(pl.multiple_of(kv * HEAD_SIZE, HEAD_SIZE), HEAD_SIZE)
        k_g = k_all[kv]
        v_g = v_all[:, at_kv]
        kt_g = k_turned[at_kv, :]
        for i in range(0, GROUP, 2):
            first = (kv * GROUP + i) * HEAD_SIZE
            at = [
                pl.ds(pl.multiple_of(first + n * HEAD_SIZE, HEAD_SIZE), HEAD_SIZE) for n in range(2)
            ]
            q_two = jnp.concatenate([q_ref[:, at[0]], q_ref[:, at[1]]], axis=0)
            g_two = jnp.concatenate([g_ref[:, at[0]], g_ref[:, at[1]]], axis=0)
            s = dot(k_g, jnp.concatenate([q_two, pick], axis=1), 1, 1)
            d_prob = dot(v_g, g_two, 1, 1)
            weights = jnp.exp2((s - jnp.max(s, axis=0, keepdims=True)) * to_log2)
            inverse = 1.0 / jnp.sum(weights, axis=0, keepdims=True)
            delta = jnp.sum(weights * d_prob, axis=0, keepdims=True) * inverse
            dscore = (weights * (d_prob - delta)).astype(BF16)
            dq = dot(kt_g, dscore, 1, 0) * (inverse * scale)
            dq_turned[at[0], :] = dq[:, :tok].astype(BF16)
            dq_turned[at[1], :] = dq[:, tok:].astype(BF16)
        return carry

    lax.fori_loop(0, n_kv, one_group, 0)
    if not up_refs:
        return

    act_ref, dq_before = before
    rank = act_ref.shape[0]
    n_quarters, per, _, part = up_refs[0].shape
    n_groups = per * len(up_refs)
    own = group_rows(rank, n_groups, tok, seq, by_slot) == group
    act = jnp.concatenate([act_ref[...].astype(F32)] * n_groups, axis=0)
    act_cols = jnp.where(own, act, 0.0).astype(BF16)
    n_before = dq_before.shape[0] // part

    def write(i, dq_ref, quarter):
        at = pl.ds(pl.multiple_of(i * part, part), part)
        up = dot(act_cols, dq_ref[at, :], 1, 1).astype(BF16)
        j = lax.rem(quarter + n_quarters - head, n_quarters) if by_slot else quarter
        for n in range(n_groups):
            up_refs[n // per][j, n % per] = up[n * rank : (n + 1) * rank, :]

    for i in range(n_quarters):
        if i < n_before:
            write(i, dq_before, i)
        else:
            write(i - n_before, dq_turned, i)


def down_kernel(
    by_slot, n_w, place_ref, length_ref, adapter_ref, owner_ref, x_hbm, *refs
):
    w_refs, refs = refs[:n_w], refs[n_w:]
    dq_a, dq_b, *out_refs, x_ref, x_sem = refs
    tok = x_ref.shape[0]
    seq, head = place_ref[0], place_ref[1]
    n_adapters, n_quarters, rank, part = w_refs[0].shape
    per, _, _, x_part = out_refs[0].shape
    n_groups = per * len(out_refs)

    def fetch(j):
        quarter = lax.rem(head + j, n_quarters) if by_slot else j
        at = pl.ds(pl.multiple_of(quarter * x_part, x_part), x_part)
        to = pl.ds(j * x_part, x_part)
        return pltpu.make_async_copy(x_hbm.at[:, at], x_ref.at[:, to], x_sem.at[j])

    for j in range(n_quarters):
        fetch(j).start()

    position = head * tok + lax.broadcasted_iota(I32, (1, tok), 1)
    adapter, group = of_tokens(
        position,
        length_ref,
        lambda s, start: (adapter_ref[0, s], owner_ref[adapter_ref[0, s]] if by_slot else s),
    )
    total = jnp.zeros((rank, tok), F32)
    n_a = dq_a.shape[0] // part
    for c, w_ref in enumerate(w_refs):
        rows = None
        for quarter in range(n_quarters):
            j = lax.rem(head + n_quarters - quarter, n_quarters) if by_slot else quarter
            i, dq_ref = (quarter, dq_a) if quarter < n_a else (quarter - n_a, dq_b)
            dq = dq_ref[i * part : (i + 1) * part, :]
            new = dot(w_ref[:, j].reshape(n_adapters * rank, part), dq, 1, 0)
            rows = new if rows is None else rows + new
        for m in range(n_adapters):
            a = (2 * m + c) ^ seq if by_slot else m
            total = total + jnp.where(adapter == a, rows[m * rank : (m + 1) * rank, :], 0.0)

    own = group_rows(rank, n_groups, tok, seq, by_slot) == group
    low = jnp.concatenate([total.astype(BF16).astype(F32)] * n_groups, axis=0)
    cols = jnp.where(own, low, 0.0).astype(BF16)
    step = min(512, x_part)
    for j in range(n_quarters):
        fetch(j).wait()
        for start in range(0, x_part, step):
            down = dot(cols, x_ref[:, j * x_part + start : j * x_part + start + step], 1, 0)
            down = down.astype(BF16)
            for n in range(n_groups):
                piece = down[n * rank : (n + 1) * rank, :]
                out_refs[n // per][n % per, j, :, start : start + step] = piece


def shifted(x, n_head, j):
    return lax.ppermute(x, "head", [(i, (i + j) % n_head) for i in range(n_head)])


def partnered(x, n_seq, bits):
    return lax.ppermute(x, "seq", [(i, i ^ bits) for i in range(n_seq)])


def on_device(
    queries, keys, values, output_gradient, inputs, adapter_activation,
    adapter_up_weight, segment_length, segment_adapter, owner,
):
    n_head = lax.axis_size("head")
    n_seq = lax.axis_size("seq")
    tok, width = queries.shape
    pack = tok * n_head
    rank = adapter_up_weight.shape[1]
    n_adapters = owner.shape[0]
    n_seg = segment_length.shape[1]
    by_slot = n_adapters == n_seq == 8
    place = jnp.stack([lax.axis_index("seq"), lax.axis_index("head")]).astype(I32)

    reach = []
    while sum(reach) < pack * 3 // 8:
        reach.append(min(pack * 3 // 8 - sum(reach), tok))
    tails = sorted(set(reach))
    key_rows = tok + sum(reach)
    halves = 2
    n_kv = KEY_VALUE_HEADS // halves
    kv_width = n_kv * HEAD_SIZE
    packed = pl.pallas_call(
        functools.partial(pack_kernel, halves, tails),
        out_shape=[jax.ShapeDtypeStruct((rows, 2 * kv_width), BF16) for rows in tails] * halves,
        in_specs=[VMEM] * 2,
        out_specs=[VMEM] * (halves * len(tails)),
        name="pack_halo",
    )(keys, values)

    def halo_of(h):
        got = []
        for hop, rows in enumerate(reach, 1):
            shift = [(i, i + hop) for i in range(n_head - hop)]
            got.insert(0, lax.ppermute(packed[h * len(tails) + tails.index(rows)], "head", shift))
        return got

    halo_a, halo_b = halo_of(0), halo_of(1)
    if by_slot:
        w = [adapter_up_weight] + [shifted(adapter_up_weight, n_head, j) for j in range(1, n_head)]
        w = jnp.concatenate(w, axis=0)[None]
        halo_a, w = lax.optimization_barrier((halo_a, w))
        w = [w] + [partnered(w, n_seq, 2 * m) for m in range(1, n_seq // 2)]
        w = jnp.concatenate(w, axis=0)
    else:
        w = lax.all_gather(adapter_up_weight, "seq", axis=0, tiled=True)
        up_weight = [lax.all_gather(w, "head", axis=1, tiled=False)]

    n_out = 2 if by_slot else 1
    n_groups = n_seq if by_slot else n_seg
    part = width // n_head
    x_part = inputs.shape[1] // n_head
    params = pltpu.CompilerParams(vmem_limit_bytes=32 * 2**20)

    def attention(h, halos, before, up_shapes):
        half = width // halves
        return pl.pallas_call(
            functools.partial(attention_kernel, len(halos), by_slot, h * n_kv, n_kv),
            out_shape=[jax.ShapeDtypeStruct((half, tok), BF16)] + up_shapes,
            in_specs=[SMEM] * 4 + [ANY] * 2 + [VMEM] * (2 + len(halos) + len(before)),
            out_specs=[VMEM] * (1 + len(up_shapes)),
            scratch_shapes=[
                pltpu.VMEM((tok, half), BF16),
                pltpu.VMEM((tok, half), BF16),
                pltpu.SemaphoreType.DMA((n_kv,)),
                pltpu.SemaphoreType.DMA((n_kv,)),
                pltpu.VMEM((n_kv, key_rows, 2 * HEAD_SIZE), BF16),
                pltpu.VMEM((key_rows, kv_width), BF16),
                pltpu.VMEM((kv_width, key_rows), BF16),
            ],
            compiler_params=params,
            cost_estimate=pl.CostEstimate(
                flops=2 * tok * half * key_rows * 3,
                bytes_accessed=4 * tok * half * 2,
                transcendentals=tok * key_rows * QUERY_HEADS // halves,
            ),
            name="attention_%d" % h,
        )(
            place, segment_length, segment_adapter, owner, queries, output_gradient, keys, values,
            *halos, *before,
        )

    (dq_a,) = attention(0, halo_a, [], [])
    if by_slot:
        halo_b, dq_a, w = lax.optimization_barrier((halo_b, dq_a, w))
        up_weight = [w, partnered(w, n_seq, 1)]
    up_shape = jax.ShapeDtypeStruct((n_head, n_groups // n_out, rank, part), BF16)
    dq_b, *up = attention(1, halo_b, [adapter_activation.T, dq_a], [up_shape] * n_out)

    down_shape = jax.ShapeDtypeStruct((n_groups // n_out, n_head, rank, x_part), BF16)
    down = pl.pallas_call(
        functools.partial(down_kernel, by_slot, len(up_weight)),
        out_shape=[down_shape] * n_out,
        in_specs=[SMEM] * 4 + [ANY] + [VMEM] * (2 + len(up_weight)),
        out_specs=[VMEM] * n_out,
        scratch_shapes=[
            pltpu.VMEM(inputs.shape, BF16),
            pltpu.SemaphoreType.DMA((n_head,)),
        ],
        compiler_params=params,
        cost_estimate=pl.CostEstimate(
            flops=2 * n_groups * rank * tok * (width + inputs.shape[1]),
            bytes_accessed=4 * tok * inputs.shape[1] * 2,
            transcendentals=0,
        ),
        name="down_parts",
    )(place, segment_length, segment_adapter, owner, inputs, *up_weight, dq_a, dq_b)

    if by_slot:
        up = over_chips(over_z(over_cores(up, n_seq), n_head).astype(BF16), n_seq)
        down = over_z(over_chips(over_cores(down, n_seq), n_seq).astype(BF16), n_head)
    else:
        up = lax.all_to_all(up[0], "head", split_axis=0, concat_axis=0, tiled=True)
        up = spread(jnp.sum(up.astype(F32), axis=0), segment_adapter, owner, n_seq)
        down = lax.all_to_all(down[0], "head", split_axis=1, concat_axis=1, tiled=True)
        down = spread(jnp.sum(down.astype(F32), axis=1), segment_adapter, owner, n_seq)
    return down.T[None] * ADAPTER_SCALE, up[None] * ADAPTER_SCALE


def over_cores(parts, n_seq):
    keep, send = parts
    return (keep.astype(F32) + partnered(send, n_seq, 1).astype(F32)).astype(BF16)


def over_chips(both, n_seq):
    total = both[0].astype(F32)
    for m in range(1, n_seq // 2):
        total = total + partnered(both[m], n_seq, 2 * m).astype(F32)
    return total


def over_z(both, n_head):
    total = both[0].astype(F32)
    for j in range(1, n_head):
        total = total + shifted(both[j], n_head, j).astype(F32)
    return total


def spread(part, segment_adapter, owner, n_seq):
    goes_to = owner[segment_adapter[0]]
    slots = (goes_to[:, None] == jnp.arange(n_seq, dtype=I32)[None, :]).astype(F32)
    slotted = jnp.einsum("srw,so->orw", part, slots, precision=lax.Precision.HIGHEST)
    slotted = lax.all_to_all(slotted.astype(BF16), "seq", split_axis=0, concat_axis=0, tiled=True)
    return jnp.sum(slotted.astype(F32), axis=0)


def solution(mesh):
    return jax.shard_map(
        on_device,
        mesh=mesh,
        in_specs=(
            P(("seq", "head"), None),
            P(("seq", "head"), None),
            P(("seq", "head"), None),
            P(("seq", "head"), None),
            P(("seq", "head"), None),
            P(("seq", "head"), None),
            P("seq", None, "head"),
            P("seq", None),
            P("seq", None),
            P(),
        ),
        out_specs=(P("seq", "head", None), P("seq", None, "head")),
        check_vma=False,
    )
```

time: 123 us -> 72.6 us (0.59)
  waiting for transfers between devices: 49.4 us -> 10.2 us
  starting transfers between devices: 52.3 us -> 39.2 us
  Pallas kernels: 10.4 us -> 12.6 us
  local copies, waits for them, and re-layouts: 8.11 us -> 6.34 us
    ppermute x2 -> x4, waiting for transfers between devices: 31.3 us -> 0.01 us  [halo_of(): lax.ppermute(packed[h * len(tails) + tails.index(rows)], 'head', shift)]
    ppermute x9, starting transfers between devices: 26.8 us -> 17.6 us  [shifted(): lax.ppermute(x, 'head', [(i, (i + j) % n_head) for i in range(n_head)])]
    ppermute x9, waiting for transfers between devices: 11 us -> 3.6 us  [shifted(): lax.ppermute(x, 'head', [(i, (i + j) % n_head) for i in range(n_head)])]
    all_to_all x1 -> x0, starting transfers between devices: 6.46 us -> none  [on_device(): x = lax.all_to_all(x, 'head', split_axis=0, concat_axis=0, tiled=True)]
    unnamed x19 -> x18, local copies, waits for them, and re-layouts: 2.61 us -> 6.23 us
    reshape x1 -> x0, local copies, waits for them, and re-layouts: 3.2 us -> none  [on_device(): x = inputs.reshape(tok, n_head, -1).transpose(1, 0, 2)]
    ppermute x12, starting transfers between devices: 10.9 us -> 13.5 us  [partnered(): return lax.ppermute(x, 'seq', [(i, i ^ bits) for i in range(n_seq)])]
    pallas_call x3 -> x4, Pallas kernels: 10.4 us -> 12.6 us  [the longest x2 8.5 us: attention(): pl.pallas_call(functools.partial(attention_kernel, len(halos), by_slot, h...]
  transfers between devices with their start and end apart: 24 -> 25, of which waited for: 12 -> 5; matrix products, arithmetic and copies ran while one was open for 3% -> 3% of each run, Pallas kernels for 8% -> 14%
where the time goes in v3:
time: 72.6 us; the launch traced here: 72.2 us
  starting transfers between devices  39.2 us (54%)
  Pallas kernels  12.6 us (17%)
  waiting for transfers between devices  10.2 us (14%)
  local copies, waits for them, and re-layouts  6.34 us (9%)
  other arithmetic  3.05 us (4%)
  between operations  0.92 us (1%)
    ppermute x9, starting transfers between devices, shifted(): lax.ppermute(x, 'head', [(i, (i + j) % n_head) for i in range(n_head)])  17.6 us
    ppermute x12, starting transfers between devices, partnered(): return lax.ppermute(x, 'seq', [(i, i ^ bits) for i in range(n_seq)])  13.5 us
    pallas_call x2, Pallas kernels, attention(): pl.pallas_call(functools.partial(attention_kernel, len(halos), by_slot, h...  8.5 us
    ppermute x4, starting transfers between devices, halo_of(): lax.ppermute(packed[h * len(tails) + tails.index(rows)], 'head', shift)  8.03 us
    ppermute x12, waiting for transfers between devices, partnered(): return lax.ppermute(x, 'seq', [(i, i ^ bits) for i in range(n_seq)])  6.55 us
    unnamed x18, local copies, waits for them, and re-layouts  6.23 us
    ppermute x9, waiting for transfers between devices, shifted(): lax.ppermute(x, 'head', [(i, (i + j) % n_head) for i in range(n_head)])  3.6 us
    pallas_call x1, Pallas kernels, on_device(): pl.pallas_call(functools.partial(down_kernel, by_slot, len(up_weight)), o...  2.38 us
  transfers between devices with their start and end apart: 25, of which 5 were waited for; matrix products, arithmetic and copies ran while one was open for 3% of the time, Pallas kernels for 14%

profile of v3, /device:TPU:0, one launch (start us, length us, event | category | flops | bytes accessed | tf_op | source)
XLA Modules:
  0.0 72.2 jit_solution(12415730345127463633)
XLA Ops:
  0.6 3.1 %collective-permute-start.4 = (bf16[1,16,1024]{2,1,0:T(8,128)(2,1)}, bf16[1,16,1024]{2,1,0:T(8,128)(2,1)S(1)}, u32[]{:S(2)}, u32[]{:S(2)}) collective-permute-start(bf16[1,16,1024]{2,1,0:T(8,128)(2,1)} %param.16), channel_id=1, source_target_pairs={{0,1},{1,2},{2,3},{3,0},{4,5},{5,6},{6,7},{7,4},{8,9},{9,10},{10,1... | collective-permute-start | bytes 98312 | tf_op jit(solution)/shard_map/ppermute | solution.py:228
  3.7 2.6 %collective-permute-start.5 = (bf16[1,16,1024]{2,1,0:T(8,128)(2,1)}, bf16[1,16,1024]{2,1,0:T(8,128)(2,1)S(1)}, u32[]{:S(2)}, u32[]{:S(2)}) collective-permute-start(bf16[1,16,1024]{2,1,0:T(8,128)(2,1)} %param.16), channel_id=1, source_target_pairs={{0,2},{1,3},{2,0},{3,1},{4,6},{5,7},{6,4},{7,5},{8,10},{9,11},{10,... | collective-permute-start | bytes 98312 | tf_op jit(solution)/shard_map/ppermute | solution.py:228
  6.3 1.3 %collective-permute-start.6 = (bf16[1,16,1024]{2,1,0:T(8,128)(2,1)}, bf16[1,16,1024]{2,1,0:T(8,128)(2,1)S(1)}, u32[]{:S(2)}, u32[]{:S(2)}) collective-permute-start(bf16[1,16,1024]{2,1,0:T(8,128)(2,1)} %param.16), channel_id=1, source_target_pairs={{0,3},{1,0},{2,1},{3,2},{4,7},{5,4},{6,5},{7,6},{8,11},{9,8},{10,9... | collective-permute-start | bytes 98312 | tf_op jit(solution)/shard_map/ppermute | solution.py:228
  7.6 1.7 %pack_halo.1 = (bf16[64,512]{1,0:T(8,128)(2,1)}, bf16[128,512]{1,0:T(8,128)(2,1)}, bf16[64,512]{1,0:T(8,128)(2,1)}, bf16[128,512]{1,0:T(8,128)(2,1)}) custom-call(bf16[128,512]{1,0:T(8,128)(2,1)} %k_ref.5, bf16[128,512]{1,0:T(8,128)(2,1)} %v_ref.5), custom_call_target="tpu_custom_call" | custom-call | tf_op jit(solution)/shard_map/pack_halo/pallas_call | solution.py:257
  9.4 2.6 %collective-permute-start.3 = (bf16[128,512]{1,0:T(8,128)(2,1)}, bf16[128,512]{1,0:T(8,128)(2,1)S(1)}, u32[]{:S(2)}, u32[]{:S(2)}) collective-permute-start(bf16[128,512]{1,0:T(8,128)(2,1)} %get-tuple-element.21), channel_id=1, source_target_pairs={{0,1},{1,2},{2,3},{4,5},{5,6},{6,7},{8,9},{9,10},{10,11},{12,13},{... | collective-permute-start | bytes 393224 | tf_op jit(solution)/shard_map/ppermute | solution.py:269
  11.9 2.2 %collective-permute-start.2 = (bf16[64,512]{1,0:T(8,128)(2,1)}, bf16[64,512]{1,0:T(8,128)(2,1)S(1)}, u32[]{:S(2)}, u32[]{:S(2)}) collective-permute-start(bf16[64,512]{1,0:T(8,128)(2,1)} %get-tuple-element.20), channel_id=1, source_target_pairs={{0,2},{1,3},{4,6},{5,7},{8,10},{9,11},{12,14},{13,15},{16,18},{17,... | collective-permute-start | bytes 196616 | tf_op jit(solution)/shard_map/ppermute | solution.py:269
  14.2 1.3 %collective-permute-start.1 = (bf16[128,512]{1,0:T(8,128)(2,1)}, bf16[128,512]{1,0:T(8,128)(2,1)S(1)}, u32[]{:S(2)}, u32[]{:S(2)}) collective-permute-start(bf16[128,512]{1,0:T(8,128)(2,1)} %get-tuple-element.19), channel_id=1, source_target_pairs={{0,1},{1,2},{2,3},{4,5},{5,6},{6,7},{8,9},{9,10},{10,11},{12,13},{... | collective-permute-start | bytes 393224 | tf_op jit(solution)/shard_map/ppermute | solution.py:269
  15.5 1.9 %collective-permute-start = (bf16[64,512]{1,0:T(8,128)(2,1)}, bf16[64,512]{1,0:T(8,128)(2,1)S(1)}, u32[]{:S(2)}, u32[]{:S(2)}) collective-permute-start(bf16[64,512]{1,0:T(8,128)(2,1)} %get-tuple-element.18), channel_id=1, source_target_pairs={{0,2},{1,3},{4,6},{5,7},{8,10},{9,11},{12,14},{13,15},{16,18},{17,... | collective-permute-start | bytes 196616 | tf_op jit(solution)/shard_map/ppermute | solution.py:269
  17.5 0.8 %maximum_bitcast_fusion = bf16[1,4,16,1024]{3,2,1,0:T(8,128)(2,1)S(1)} fusion(bf16[1,16,1024]{2,1,0:T(8,128)(2,1)S(1)} %collective-permute-done.6, bf16[1,16,1024]{2,1,0:T(8,128)(2,1)S(1)} %collective-permute-done.5, bf16[1,16,1024]{2,1,0:T(8,128)(2,1)S(1)} %collective-permute-done.4, bf16[1,16,1024]{2,1,0:T(8,128)(2,1)} %param.16), kind=kLoop, calls=%fused_computation.19 | loop fusion | flops 196608 | bytes 262144 | tf_op jit(solution)/shard_map/broadcast_in_dim | solution.py:275
  18.3 1.6 %collective-permute-start.7 = (bf16[1,4,16,1024]{3,2,1,0:T(8,128)(2,1)S(1)}, bf16[1,4,16,1024]{3,2,1,0:T(8,128)(2,1)S(1)}, u32[]{:S(2)}, u32[]{:S(2)}) collective-permute-start(bf16[1,4,16,1024]{3,2,1,0:T(8,128)(2,1)S(1)} %maximum_bitcast_fusion), channel_id=1, source_target_pairs={{0,8},{4,12},{8,0},{12,4},{16,24},{20,28},{24,16},{28,20},{1,9},{5... | collective-permute-start | bytes 393224 | tf_op jit(solution)/shard_map/ppermute | solution.py:232
  19.8 1.5 %collective-permute-start.8 = (bf16[1,4,16,1024]{3,2,1,0:T(8,128)(2,1)S(1)}, bf16[1,4,16,1024]{3,2,1,0:T(8,128)(2,1)S(1)}, u32[]{:S(2)}, u32[]{:S(2)}) collective-permute-start(bf16[1,4,16,1024]{3,2,1,0:T(8,128)(2,1)S(1)} %maximum_bitcast_fusion), channel_id=1, source_target_pairs={{0,16},{4,20},{8,24},{12,28},{16,0},{20,4},{24,8},{28,12},{1,17},{... | collective-permute-start | bytes 393224 | tf_op jit(solution)/shard_map/ppermute | solution.py:232
  21.4 0.5 collective-permute-start.9
  21.8 0.1 pad_add_fusion.place_ref
  21.9 1.2 %copy-done = bf16[128,4096]{1,0:T(8,128)(2,1)S(1)} copy-done((bf16[128,4096]{1,0:T(8,128)(2,1)S(1)}, bf16[128,4096]{1,0:T(8,128)(2,1)}, u32[]{:S(2)}) %copy-start) | copy-done | bytes 1048600
  23.1 1.2 %copy-done.1 = bf16[128,4096]{1,0:T(8,128)(2,1)S(1)} copy-done((bf16[128,4096]{1,0:T(8,128)(2,1)S(1)}, bf16[128,4096]{1,0:T(8,128)(2,1)}, u32[]{:S(2)}) %copy-start.1) | copy-done | bytes 1048600
  24.4 0.9 %copy-done.3 = bf16[128,512]{1,0:T(8,128)(2,1)S(1)} copy-done((bf16[128,512]{1,0:T(8,128)(2,1)S(1)}, bf16[128,512]{1,0:T(8,128)(2,1)}, u32[]{:S(2)}) %copy-start.3) | copy-done | bytes 131096
  25.3 0.9 %copy-done.4 = bf16[128,512]{1,0:T(8,128)(2,1)S(1)} copy-done((bf16[128,512]{1,0:T(8,128)(2,1)S(1)}, bf16[128,512]{1,0:T(8,128)(2,1)}, u32[]{:S(2)}) %copy-start.4) | copy-done | bytes 131096
  26.2 0.7 copy-done.5
  26.8 0.7 copy-done.6
  27.5 0.7 copy-done.7
  28.1 4.0 %attention_0.1.refs_3_.refs_2_ = bf16[2048,128]{1,0:T(8,128)(2,1)S(1)} custom-call(s32[2]{0:T(128)S(1)} %pad_add_fusion.place_ref, s32[1,8]{1,0:T(1,128)S(1)} %copy-done.5, s32[1,8]{1,0:T(1,128)S(1)} %copy-done.6, s32[8]{0:T(128)S(1)} %copy-done.7, bf16[128,4096]{1,0:T(8,128)(2,1)S(1)} %copy-done, bf16[128,4096]{1,0:T(8,128)(2,1)S(1)} %copy-done.1, ...), custom_call_target="tpu_custom_call" | custom-call | flops 503316480 | bytes 2097152 | tf_op jit(solution)/shard_map/attention_0/pallas_call | solution.py:291
  32.3 0.1 collective-permute-start.10
  32.4 4.5 %attention_1.1 = (bf16[2048,128]{1,0:T(8,128)(2,1)S(1)}, bf16[4,4,16,1024]{3,2,1,0:T(8,128)(2,1)S(1)}, bf16[4,4,16,1024]{3,2,1,0:T(8,128)(2,1)S(1)}) custom-call(s32[2]{0:T(128)S(1)} %pad_add_fusion.place_ref, s32[1,8]{1,0:T(1,128)S(1)} %copy-done.5, s32[1,8]{1,0:T(1,128)S(1)} %copy-done.6, s32[8]{0:T(128)S(1)} %copy-done.7, bf16[128,4096]{1,0:T(8,128)(2,1)S(1)} %copy-done, ...), custom_call_target="tpu_custom_call" | custom-call | flops 503316480 | bytes 2097152 | tf_op jit(solution)/shard_map/attention_1/pallas_call | solution.py:291
  36.9 2.4 %down_parts.1 = (bf16[4,4,16,2048]{3,2,1,0:T(8,128)(2,1)S(1)}, bf16[4,4,16,2048]{3,2,1,0:T(8,128)(2,1)S(1)}) custom-call(s32[2]{0:T(128)S(1)} %pad_add_fusion.place_ref, s32[1,8]{1,0:T(1,128)S(1)} %copy-done.5, s32[1,8]{1,0:T(1,128)S(1)} %copy-done.6, s32[8]{0:T(128)S(1)} %copy-done.7, bf16[128,8192]{1,0:T(8,128)(2,1)S(1)} %copy-done.2, ...), custom_call_target="tpu_custom_call" | custom-call | flops 402653184 | bytes 8388608 | tf_op jit(solution)/shard_map/down_parts/pallas_call | solution.py:325
  39.3 0.5 collective-permute-start.11
  39.8 0.1 collective-permute-start.18
  39.9 3.0 %collective-permute-done.18 = bf16[4,4,16,1024]{3,2,1,0:T(8,128)(2,1)S(1)} collective-permute-done((bf16[4,4,16,1024]{3,2,1,0:T(8,128)(2,1)S(1)}, bf16[4,4,16,1024]{3,2,1,0:T(8,128)(2,1)S(1)}, u32[]{:S(2)}, u32[]{:S(2)}) %collective-permute-start.18) | collective-permute-done | bytes 524320 | tf_op jit(solution)/shard_map/ppermute | solution.py:232
  42.9 0.2 add_convert_fusion.1
  43.1 0.2 collective-permute-start.19
  43.3 2.4 %collective-permute-start.20 = (bf16[4,16,1024]{2,1,0:T(8,128)(2,1)S(1)}, bf16[4,16,1024]{2,1,0:T(8,128)(2,1)S(1)}, u32[]{:S(2)}, u32[]{:S(2)}) collective-permute-start(bf16[4,16,1024]{2,1,0:T(8,128)(2,1)S(1)} %get-tuple-element.39), channel_id=1, source_target_pairs={{0,2},{1,3},{2,0},{3,1},{4,6},{5,7},{6,4},{7,5},{8,10},{9,11},{10,... | collective-permute-start | bytes 393224 | tf_op jit(solution)/shard_map/ppermute | solution.py:228
  45.7 2.8 %collective-permute-start.21 = (bf16[4,16,1024]{2,1,0:T(8,128)(2,1)S(1)}, bf16[4,16,1024]{2,1,0:T(8,128)(2,1)S(1)}, u32[]{:S(2)}, u32[]{:S(2)}) collective-permute-start(bf16[4,16,1024]{2,1,0:T(8,128)(2,1)S(1)} %get-tuple-element.38), channel_id=1, source_target_pairs={{0,3},{1,0},{2,1},{3,2},{4,7},{5,4},{6,5},{7,6},{8,11},{9,8},{10,9... | collective-permute-start | bytes 393224 | tf_op jit(solution)/shard_map/ppermute | solution.py:228
  48.6 0.4 add_convert_fusion
  49.0 1.6 %collective-permute-start.12 = (bf16[4,16,2048]{2,1,0:T(8,128)(2,1)S(1)}, bf16[4,16,2048]{2,1,0:T(8,128)(2,1)S(1)}, u32[]{:S(2)}, u32[]{:S(2)}) collective-permute-start(bf16[4,16,2048]{2,1,0:T(8,128)(2,1)S(1)} %get-tuple-element.34), channel_id=1, source_target_pairs={{0,8},{4,12},{8,0},{12,4},{16,24},{20,28},{24,16},{28,20},{1,9},{5... | collective-permute-start | bytes 786440 | tf_op jit(solution)/shard_map/ppermute | solution.py:232
  50.6 1.5 %collective-permute-start.13 = (bf16[4,16,2048]{2,1,0:T(8,128)(2,1)S(1)}, bf16[4,16,2048]{2,1,0:T(8,128)(2,1)S(1)}, u32[]{:S(2)}, u32[]{:S(2)}) collective-permute-start(bf16[4,16,2048]{2,1,0:T(8,128)(2,1)S(1)} %get-tuple-element.36), channel_id=1, source_target_pairs={{0,16},{4,20},{8,24},{12,28},{16,0},{20,4},{24,8},{28,12},{1,17},{... | collective-permute-start | bytes 786440 | tf_op jit(solution)/shard_map/ppermute | solution.py:232
  52.1 1.8 %collective-permute-start.14 = (bf16[4,16,2048]{2,1,0:T(8,128)(2,1)S(1)}, bf16[4,16,2048]{2,1,0:T(8,128)(2,1)S(1)}, u32[]{:S(2)}, u32[]{:S(2)}) collective-permute-start(bf16[4,16,2048]{2,1,0:T(8,128)(2,1)S(1)} %get-tuple-element.35), channel_id=1, source_target_pairs={{0,24},{4,28},{8,16},{12,20},{16,8},{20,12},{24,0},{28,4},{1,25},{... | collective-permute-start | bytes 786440 | tf_op jit(solution)/shard_map/ppermute | solution.py:232
  53.9 2.3 %collective-permute-done.20 = bf16[4,16,1024]{2,1,0:T(8,128)(2,1)S(1)} collective-permute-done((bf16[4,16,1024]{2,1,0:T(8,128)(2,1)S(1)}, bf16[4,16,1024]{2,1,0:T(8,128)(2,1)S(1)}, u32[]{:S(2)}, u32[]{:S(2)}) %collective-permute-start.20) | collective-permute-done | bytes 131104 | tf_op jit(solution)/shard_map/ppermute | solution.py:228
  56.2 0.1 fusion.5
  56.3 1.6 %collective-permute-start.22 = (bf16[16,1024]{1,0:T(8,128)(2,1)S(1)}, bf16[16,1024]{1,0:T(8,128)(2,1)S(1)}, u32[]{:S(2)}, u32[]{:S(2)}) collective-permute-start(bf16[16,1024]{1,0:T(8,128)(2,1)S(1)} %get-tuple-element.43), channel_id=1, source_target_pairs={{0,8},{4,12},{8,0},{12,4},{16,24},{20,28},{24,16},{28,20},{1,9},{5... | collective-permute-start | bytes 98312 | tf_op jit(solution)/shard_map/ppermute | solution.py:232
  57.9 1.5 %collective-permute-start.23 = (bf16[16,1024]{1,0:T(8,128)(2,1)S(1)}, bf16[16,1024]{1,0:T(8,128)(2,1)S(1)}, u32[]{:S(2)}, u32[]{:S(2)}) collective-permute-start(bf16[16,1024]{1,0:T(8,128)(2,1)S(1)} %get-tuple-element.45), channel_id=1, source_target_pairs={{0,16},{4,20},{8,24},{12,28},{16,0},{20,4},{24,8},{28,12},{1,17},{... | collective-permute-start | bytes 98312 | tf_op jit(solution)/shard_map/ppermute | solution.py:232
  59.4 1.4 %collective-permute-start.24 = (bf16[16,1024]{1,0:T(8,128)(2,1)S(1)}, bf16[16,1024]{1,0:T(8,128)(2,1)S(1)}, u32[]{:S(2)}, u32[]{:S(2)}) collective-permute-start(bf16[16,1024]{1,0:T(8,128)(2,1)S(1)} %get-tuple-element.44), channel_id=1, source_target_pairs={{0,24},{4,28},{8,16},{12,20},{16,8},{20,12},{24,0},{28,4},{1,25},{... | collective-permute-start | bytes 98312 | tf_op jit(solution)/shard_map/ppermute | solution.py:232
  60.8 3.6 %collective-permute-done.13 = bf16[4,16,2048]{2,1,0:T(8,128)(2,1)S(1)} collective-permute-done((bf16[4,16,2048]{2,1,0:T(8,128)(2,1)S(1)}, bf16[4,16,2048]{2,1,0:T(8,128)(2,1)S(1)}, u32[]{:S(2)}, u32[]{:S(2)}) %collective-permute-start.13) | collective-permute-done | bytes 262176 | tf_op jit(solution)/shard_map/ppermute | solution.py:232
  64.3 0.1 fusion.2
  64.6 2.2 %collective-permute-start.16 = (bf16[16,2048]{1,0:T(8,128)(2,1)S(1)}, bf16[16,2048]{1,0:T(8,128)(2,1)S(1)}, u32[]{:S(2)}, u32[]{:S(2)}) collective-permute-start(bf16[16,2048]{1,0:T(8,128)(2,1)S(1)} %get-tuple-element.42), channel_id=1, source_target_pairs={{0,2},{1,3},{2,0},{3,1},{4,6},{5,7},{6,4},{7,5},{8,10},{9,11},{10,... | collective-permute-start | bytes 196616 | tf_op jit(solution)/shard_map/ppermute | solution.py:228
  66.8 2.8 %collective-permute-start.17 = (bf16[16,2048]{1,0:T(8,128)(2,1)S(1)}, bf16[16,2048]{1,0:T(8,128)(2,1)S(1)}, u32[]{:S(2)}, u32[]{:S(2)}) collective-permute-start(bf16[16,2048]{1,0:T(8,128)(2,1)S(1)} %get-tuple-element.41), channel_id=1, source_target_pairs={{0,3},{1,0},{2,1},{3,2},{4,7},{5,4},{6,5},{7,6},{8,11},{9,8},{10,9... | collective-permute-start | bytes 196616 | tf_op jit(solution)/shard_map/ppermute | solution.py:228
  69.6 0.7 fusion.13
  70.3 0.3 collective-permute-done.15
  70.6 0.9 %collective-permute-done.17 = bf16[16,2048]{1,0:T(8,128)(2,1)S(1)} collective-permute-done((bf16[16,2048]{1,0:T(8,128)(2,1)S(1)}, bf16[16,2048]{1,0:T(8,128)(2,1)S(1)}, u32[]{:S(2)}, u32[]{:S(2)}) %collective-permute-start.17) | collective-permute-done | bytes 65568 | tf_op jit(solution)/shard_map/ppermute | solution.py:228
  71.5 0.7 fusion.9
  (37 shorter events, 0.3 us)
Async XLA Ops:
  0.6 13.6 %collective-permute-start.4 = (bf16[1,16,1024]{2,1,0:T(8,128)(2,1)}, bf16[1,16,1024]{2,1,0:T(8,128)(2,1)S(1)}, u32[]{:S(2)}, u32[]{:S(2)}) collective-permute-start(bf16[1,16,1024]{2,1,0:T(8,128)(2,1)} %param.16), channel_id=1, source_target_pairs={{0,1},{1,2},{2,3},{3,0},{4,5},{5,6},{6,7},{7,4},{8,9},{9,10},{10,1... | collective-permute-start | bytes 98312 | tf_op jit(solution)/shard_map/ppermute | solution.py:228
  3.7 11.8 %collective-permute-start.5 = (bf16[1,16,1024]{2,1,0:T(8,128)(2,1)}, bf16[1,16,1024]{2,1,0:T(8,128)(2,1)S(1)}, u32[]{:S(2)}, u32[]{:S(2)}) collective-permute-start(bf16[1,16,1024]{2,1,0:T(8,128)(2,1)} %param.16), channel_id=1, source_target_pairs={{0,2},{1,3},{2,0},{3,1},{4,6},{5,7},{6,4},{7,5},{8,10},{9,11},{10,... | collective-permute-start | bytes 98312 | tf_op jit(solution)/shard_map/ppermute | solution.py:228
  6.3 11.2 %collective-permute-start.6 = (bf16[1,16,1024]{2,1,0:T(8,128)(2,1)}, bf16[1,16,1024]{2,1,0:T(8,128)(2,1)S(1)}, u32[]{:S(2)}, u32[]{:S(2)}) collective-permute-start(bf16[1,16,1024]{2,1,0:T(8,128)(2,1)} %param.16), channel_id=1, source_target_pairs={{0,3},{1,0},{2,1},{3,2},{4,7},{5,4},{6,5},{7,6},{8,11},{9,8},{10,9... | collective-permute-start | bytes 98312 | tf_op jit(solution)/shard_map/ppermute | solution.py:228
  9.4 8.9 %collective-permute-start.3 = (bf16[128,512]{1,0:T(8,128)(2,1)}, bf16[128,512]{1,0:T(8,128)(2,1)S(1)}, u32[]{:S(2)}, u32[]{:S(2)}) collective-permute-start(bf16[128,512]{1,0:T(8,128)(2,1)} %get-tuple-element.21), channel_id=1, source_target_pairs={{0,1},{1,2},{2,3},{4,5},{5,6},{6,7},{8,9},{9,10},{10,11},{12,13},{... | collective-permute-start | bytes 393224 | tf_op jit(solution)/shard_map/ppermute | solution.py:269
  11.9 6.3 %collective-permute-start.2 = (bf16[64,512]{1,0:T(8,128)(2,1)}, bf16[64,512]{1,0:T(8,128)(2,1)S(1)}, u32[]{:S(2)}, u32[]{:S(2)}) collective-permute-start(bf16[64,512]{1,0:T(8,128)(2,1)} %get-tuple-element.20), channel_id=1, source_target_pairs={{0,2},{1,3},{4,6},{5,7},{8,10},{9,11},{12,14},{13,15},{16,18},{17,... | collective-permute-start | bytes 196616 | tf_op jit(solution)/shard_map/ppermute | solution.py:269
  14.2 18.1 %collective-permute-start.1 = (bf16[128,512]{1,0:T(8,128)(2,1)}, bf16[128,512]{1,0:T(8,128)(2,1)S(1)}, u32[]{:S(2)}, u32[]{:S(2)}) collective-permute-start(bf16[128,512]{1,0:T(8,128)(2,1)} %get-tuple-element.19), channel_id=1, source_target_pairs={{0,1},{1,2},{2,3},{4,5},{5,6},{6,7},{8,9},{9,10},{10,11},{12,13},{... | collective-permute-start | bytes 393224 | tf_op jit(solution)/shard_map/ppermute | solution.py:269
  15.5 16.8 %collective-permute-start = (bf16[64,512]{1,0:T(8,128)(2,1)}, bf16[64,512]{1,0:T(8,128)(2,1)S(1)}, u32[]{:S(2)}, u32[]{:S(2)}) collective-permute-start(bf16[64,512]{1,0:T(8,128)(2,1)} %get-tuple-element.18), channel_id=1, source_target_pairs={{0,2},{1,3},{4,6},{5,7},{8,10},{9,11},{12,14},{13,15},{16,18},{17,... | collective-permute-start | bytes 196616 | tf_op jit(solution)/shard_map/ppermute | solution.py:269
  18.2 14.2 %copy-start.8 = (bf16[128,16]{0,1:T(8,128)(2,1)S(1)}, bf16[128,16]{0,1:T(8,128)(2,1)}, u32[]{:S(2)}) copy-start(bf16[128,16]{0,1:T(8,128)(2,1)} %param.15) | copy-start | bytes 12292
  18.3 13.9 %collective-permute-start.7 = (bf16[1,4,16,1024]{3,2,1,0:T(8,128)(2,1)S(1)}, bf16[1,4,16,1024]{3,2,1,0:T(8,128)(2,1)S(1)}, u32[]{:S(2)}, u32[]{:S(2)}) collective-permute-start(bf16[1,4,16,1024]{3,2,1,0:T(8,128)(2,1)S(1)} %maximum_bitcast_fusion), channel_id=1, source_target_pairs={{0,8},{4,12},{8,0},{12,4},{16,24},{20,28},{24,16},{28,20},{1,9},{5... | collective-permute-start | bytes 393224 | tf_op jit(solution)/shard_map/ppermute | solution.py:232
  19.8 12.4 %collective-permute-start.8 = (bf16[1,4,16,1024]{3,2,1,0:T(8,128)(2,1)S(1)}, bf16[1,4,16,1024]{3,2,1,0:T(8,128)(2,1)S(1)}, u32[]{:S(2)}, u32[]{:S(2)}) collective-permute-start(bf16[1,4,16,1024]{3,2,1,0:T(8,128)(2,1)S(1)} %maximum_bitcast_fusion), channel_id=1, source_target_pairs={{0,16},{4,20},{8,24},{12,28},{16,0},{20,4},{24,8},{28,12},{1,17},{... | collective-permute-start | bytes 393224 | tf_op jit(solution)/shard_map/ppermute | solution.py:232
  21.4 10.9 %collective-permute-start.9 = (bf16[1,4,16,1024]{3,2,1,0:T(8,128)(2,1)S(1)}, bf16[1,4,16,1024]{3,2,1,0:T(8,128)(2,1)S(1)}, u32[]{:S(2)}, u32[]{:S(2)}) collective-permute-start(bf16[1,4,16,1024]{3,2,1,0:T(8,128)(2,1)S(1)} %maximum_bitcast_fusion), channel_id=1, source_target_pairs={{0,24},{4,28},{8,16},{12,20},{16,8},{20,12},{24,0},{28,4},{1,25},{... | collective-permute-start | bytes 393224 | tf_op jit(solution)/shard_map/ppermute | solution.py:232
  21.9 1.2 %copy-start = (bf16[128,4096]{1,0:T(8,128)(2,1)S(1)}, bf16[128,4096]{1,0:T(8,128)(2,1)}, u32[]{:S(2)}) copy-start(bf16[128,4096]{1,0:T(8,128)(2,1)} %q_hbm.3) | copy-start | bytes 3145732
  23.1 1.2 %copy-start.1 = (bf16[128,4096]{1,0:T(8,128)(2,1)S(1)}, bf16[128,4096]{1,0:T(8,128)(2,1)}, u32[]{:S(2)}) copy-start(bf16[128,4096]{1,0:T(8,128)(2,1)} %g_hbm.3) | copy-start | bytes 3145732
  24.4 0.9 %copy-start.3 = (bf16[128,512]{1,0:T(8,128)(2,1)S(1)}, bf16[128,512]{1,0:T(8,128)(2,1)}, u32[]{:S(2)}) copy-start(bf16[128,512]{1,0:T(8,128)(2,1)} %k_ref.5) | copy-start | bytes 393220
  25.3 0.9 %copy-start.4 = (bf16[128,512]{1,0:T(8,128)(2,1)S(1)}, bf16[128,512]{1,0:T(8,128)(2,1)}, u32[]{:S(2)}) copy-start(bf16[128,512]{1,0:T(8,128)(2,1)} %v_ref.5) | copy-start | bytes 393220
  26.2 0.7 copy-start.5
  26.8 0.7 copy-start.6
  27.5 0.7 copy-start.7
  32.2 4.7 %copy-start.2 = (bf16[128,8192]{1,0:T(8,128)(2,1)S(1)}, bf16[128,8192]{1,0:T(8,128)(2,1)}, u32[]{:S(2)}) copy-start(bf16[128,8192]{1,0:T(8,128)(2,1)} %x_hbm.1) | copy-start | bytes 6291460
  32.3 4.6 %collective-permute-start.10 = (bf16[4,4,16,1024]{3,2,1,0:T(8,128)(2,1)S(1)}, bf16[4,4,16,1024]{3,2,1,0:T(8,128)(2,1)S(1)}, u32[]{:S(2)}, u32[]{:S(2)}) collective-permute-start(bf16[4,4,16,1024]{3,2,1,0:T(8,128)(2,1)S(1)} %pad_maximum_fusion.refs_0_), channel_id=1, source_target_pairs={{0,4},{4,0},{8,12},{12,8},{16,20},{20,16},{24,28},{28,24},{1,5},{5... | collective-permute-start | bytes 1572872 | tf_op jit(solution)/shard_map/ppermute | solution.py:232
  39.3 9.3 %collective-permute-start.11 = (bf16[4,4,16,2048]{3,2,1,0:T(8,128)(2,1)S(1)}, bf16[4,4,16,2048]{3,2,1,0:T(8,128)(2,1)S(1)}, u32[]{:S(2)}, u32[]{:S(2)}) collective-permute-start(bf16[4,4,16,2048]{3,2,1,0:T(8,128)(2,1)S(1)} %get-tuple-element.31), channel_id=1, source_target_pairs={{0,4},{4,0},{8,12},{12,8},{16,20},{20,16},{24,28},{28,24},{1,5},{5... | collective-permute-start | bytes 3145736 | tf_op jit(solution)/shard_map/ppermute | solution.py:232
  39.8 3.0 %collective-permute-start.18 = (bf16[4,4,16,1024]{3,2,1,0:T(8,128)(2,1)S(1)}, bf16[4,4,16,1024]{3,2,1,0:T(8,128)(2,1)S(1)}, u32[]{:S(2)}, u32[]{:S(2)}) collective-permute-start(bf16[4,4,16,1024]{3,2,1,0:T(8,128)(2,1)S(1)} %get-tuple-element.33), channel_id=1, source_target_pairs={{0,4},{4,0},{8,12},{12,8},{16,20},{20,16},{24,28},{28,24},{1,5},{5... | collective-permute-start | bytes 1572872 | tf_op jit(solution)/shard_map/ppermute | solution.py:232
  43.1 9.0 %collective-permute-start.19 = (bf16[4,16,1024]{2,1,0:T(8,128)(2,1)S(1)}, bf16[4,16,1024]{2,1,0:T(8,128)(2,1)S(1)}, u32[]{:S(2)}, u32[]{:S(2)}) collective-permute-start(bf16[4,16,1024]{2,1,0:T(8,128)(2,1)S(1)} %get-tuple-element.37), channel_id=1, source_target_pairs={{0,1},{1,2},{2,3},{3,0},{4,5},{5,6},{6,7},{7,4},{8,9},{9,10},{10,1... | collective-permute-start | bytes 393224 | tf_op jit(solution)/shard_map/ppermute | solution.py:228
  43.3 12.9 %collective-permute-start.20 = (bf16[4,16,1024]{2,1,0:T(8,128)(2,1)S(1)}, bf16[4,16,1024]{2,1,0:T(8,128)(2,1)S(1)}, u32[]{:S(2)}, u32[]{:S(2)}) collective-permute-start(bf16[4,16,1024]{2,1,0:T(8,128)(2,1)S(1)} %get-tuple-element.39), channel_id=1, source_target_pairs={{0,2},{1,3},{2,0},{3,1},{4,6},{5,7},{6,4},{7,5},{8,10},{9,11},{10,... | collective-permute-start | bytes 393224 | tf_op jit(solution)/shard_map/ppermute | solution.py:228
  45.7 10.5 %collective-permute-start.21 = (bf16[4,16,1024]{2,1,0:T(8,128)(2,1)S(1)}, bf16[4,16,1024]{2,1,0:T(8,128)(2,1)S(1)}, u32[]{:S(2)}, u32[]{:S(2)}) collective-permute-start(bf16[4,16,1024]{2,1,0:T(8,128)(2,1)S(1)} %get-tuple-element.38), channel_id=1, source_target_pairs={{0,3},{1,0},{2,1},{3,2},{4,7},{5,4},{6,5},{7,6},{8,11},{9,8},{10,9... | collective-permute-start | bytes 393224 | tf_op jit(solution)/shard_map/ppermute | solution.py:228
  49.0 10.4 %collective-permute-start.12 = (bf16[4,16,2048]{2,1,0:T(8,128)(2,1)S(1)}, bf16[4,16,2048]{2,1,0:T(8,128)(2,1)S(1)}, u32[]{:S(2)}, u32[]{:S(2)}) collective-permute-start(bf16[4,16,2048]{2,1,0:T(8,128)(2,1)S(1)} %get-tuple-element.34), channel_id=1, source_target_pairs={{0,8},{4,12},{8,0},{12,4},{16,24},{20,28},{24,16},{28,20},{1,9},{5... | collective-permute-start | bytes 786440 | tf_op jit(solution)/shard_map/ppermute | solution.py:232
  50.6 13.8 %collective-permute-start.13 = (bf16[4,16,2048]{2,1,0:T(8,128)(2,1)S(1)}, bf16[4,16,2048]{2,1,0:T(8,128)(2,1)S(1)}, u32[]{:S(2)}, u32[]{:S(2)}) collective-permute-start(bf16[4,16,2048]{2,1,0:T(8,128)(2,1)S(1)} %get-tuple-element.36), channel_id=1, source_target_pairs={{0,16},{4,20},{8,24},{12,28},{16,0},{20,4},{24,8},{28,12},{1,17},{... | collective-permute-start | bytes 786440 | tf_op jit(solution)/shard_map/ppermute | solution.py:232
  52.1 12.2 %collective-permute-start.14 = (bf16[4,16,2048]{2,1,0:T(8,128)(2,1)S(1)}, bf16[4,16,2048]{2,1,0:T(8,128)(2,1)S(1)}, u32[]{:S(2)}, u32[]{:S(2)}) collective-permute-start(bf16[4,16,2048]{2,1,0:T(8,128)(2,1)S(1)} %get-tuple-element.35), channel_id=1, source_target_pairs={{0,24},{4,28},{8,16},{12,20},{16,8},{20,12},{24,0},{28,4},{1,25},{... | collective-permute-start | bytes 786440 | tf_op jit(solution)/shard_map/ppermute | solution.py:232
  56.3 10.5 %collective-permute-start.22 = (bf16[16,1024]{1,0:T(8,128)(2,1)S(1)}, bf16[16,1024]{1,0:T(8,128)(2,1)S(1)}, u32[]{:S(2)}, u32[]{:S(2)}) collective-permute-start(bf16[16,1024]{1,0:T(8,128)(2,1)S(1)} %get-tuple-element.43), channel_id=1, source_target_pairs={{0,8},{4,12},{8,0},{12,4},{16,24},{20,28},{24,16},{28,20},{1,9},{5... | collective-permute-start | bytes 98312 | tf_op jit(solution)/shard_map/ppermute | solution.py:232
  57.9 11.8 %collective-permute-start.23 = (bf16[16,1024]{1,0:T(8,128)(2,1)S(1)}, bf16[16,1024]{1,0:T(8,128)(2,1)S(1)}, u32[]{:S(2)}, u32[]{:S(2)}) collective-permute-start(bf16[16,1024]{1,0:T(8,128)(2,1)S(1)} %get-tuple-element.45), channel_id=1, source_target_pairs={{0,16},{4,20},{8,24},{12,28},{16,0},{20,4},{24,8},{28,12},{1,17},{... | collective-permute-start | bytes 98312 | tf_op jit(solution)/shard_map/ppermute | solution.py:232
  59.4 10.2 %collective-permute-start.24 = (bf16[16,1024]{1,0:T(8,128)(2,1)S(1)}, bf16[16,1024]{1,0:T(8,128)(2,1)S(1)}, u32[]{:S(2)}, u32[]{:S(2)}) collective-permute-start(bf16[16,1024]{1,0:T(8,128)(2,1)S(1)} %get-tuple-element.44), channel_id=1, source_target_pairs={{0,24},{4,28},{8,16},{12,20},{16,8},{20,12},{24,0},{28,4},{1,25},{... | collective-permute-start | bytes 98312 | tf_op jit(solution)/shard_map/ppermute | solution.py:232
  64.5 6.1 %collective-permute-start.15 = (bf16[16,2048]{1,0:T(8,128)(2,1)S(1)}, bf16[16,2048]{1,0:T(8,128)(2,1)S(1)}, u32[]{:S(2)}, u32[]{:S(2)}) collective-permute-start(bf16[16,2048]{1,0:T(8,128)(2,1)S(1)} %get-tuple-element.40), channel_id=1, source_target_pairs={{0,1},{1,2},{2,3},{3,0},{4,5},{5,6},{6,7},{7,4},{8,9},{9,10},{10,1... | collective-permute-start | bytes 196616 | tf_op jit(solution)/shard_map/ppermute | solution.py:228
  64.6 6.1 %collective-permute-start.16 = (bf16[16,2048]{1,0:T(8,128)(2,1)S(1)}, bf16[16,2048]{1,0:T(8,128)(2,1)S(1)}, u32[]{:S(2)}, u32[]{:S(2)}) collective-permute-start(bf16[16,2048]{1,0:T(8,128)(2,1)S(1)} %get-tuple-element.42), channel_id=1, source_target_pairs={{0,2},{1,3},{2,0},{3,1},{4,6},{5,7},{6,4},{7,5},{8,10},{9,11},{10,... | collective-permute-start | bytes 196616 | tf_op jit(solution)/shard_map/ppermute | solution.py:228
  66.8 4.8 %collective-permute-start.17 = (bf16[16,2048]{1,0:T(8,128)(2,1)S(1)}, bf16[16,2048]{1,0:T(8,128)(2,1)S(1)}, u32[]{:S(2)}, u32[]{:S(2)}) collective-permute-start(bf16[16,2048]{1,0:T(8,128)(2,1)S(1)} %get-tuple-element.41), channel_id=1, source_target_pairs={{0,3},{1,0},{2,1},{3,2},{4,7},{5,4},{6,5},{7,6},{8,11},{9,8},{10,9... | collective-permute-start | bytes 196616 | tf_op jit(solution)/shard_map/ppermute | solution.py:228

commit v4 on v3

v4 whole, which is shorter than its diff:
```python
import functools
import math

import jax
import jax.numpy as jnp
from jax import lax
from jax.experimental import pallas as pl
from jax.experimental.pallas import tpu as pltpu
from jax.sharding import PartitionSpec as P

QUERY_HEADS = 32
KEY_VALUE_HEADS = 4
HEAD_SIZE = 128
GROUP = QUERY_HEADS // KEY_VALUE_HEADS
ADAPTER_SCALE = 2.0
NEVER = -1e30
BF16 = jnp.bfloat16
F32 = jnp.float32
I32 = jnp.int32
VMEM = pl.BlockSpec(memory_space=pltpu.VMEM)
ANY = pl.BlockSpec(memory_space=pl.ANY)


def dot(a, b, a_dim, b_dim):
    return lax.dot_general(a, b, (((a_dim,), (b_dim,)), ((), ())), preferred_element_type=F32)


def group_rows(rows_of_group, n_groups, width, seq, by_slot):
    row = lax.broadcasted_iota(I32, (n_groups * rows_of_group, width), 0) // rows_of_group
    if by_slot:
        half = n_groups // 2
        row = jnp.where(row < half, row * 2, (row - half) * 2 + 1) ^ seq
    return row


def pack_kernel(k_hbm, v_hbm, out_hbm, sems):
    width = k_hbm.shape[1]
    copies = [
        pltpu.make_async_copy(hbm, out_hbm.at[:, pl.ds(i * width, width)], sems.at[i])
        for i, hbm in enumerate((k_hbm, v_hbm))
    ]
    for copy in copies:
        copy.start()
    for copy in copies:
        copy.wait()


def ready_kernel(
    by_slot,
    length_hbm, adapter_hbm, owner_hbm, act_hbm, q_hbm, g_hbm,
    facts_ref, bias_ref, act_cols_ref, q_turned, g_turned,
    length_ref, adapter_ref, owner_ref, act_ref, q_ref, g_ref, sems, q_sem, g_sem,
):
    small = [
        pltpu.make_async_copy(source, target, sems.at[i])
        for i, (source, target) in enumerate(
            [
                (length_hbm, length_ref),
                (adapter_hbm, adapter_ref),
                (owner_hbm, owner_ref),
                (act_hbm, act_ref),
            ]
        )
    ]
    for copy in small:
        copy.start()
    per_kv = GROUP * HEAD_SIZE
    tok = q_ref.shape[0]

    def fetch(kv):
        at = pl.ds(kv * per_kv, per_kv)
        return (
            pltpu.make_async_copy(q_hbm.at[:, at], q_ref.at[:, at], q_sem.at[kv]),
            pltpu.make_async_copy(g_hbm.at[:, at], g_ref.at[:, at], g_sem.at[kv]),
        )

    for kv in range(KEY_VALUE_HEADS):
        for copy in fetch(kv):
            copy.start()
    for copy in small:
        copy.wait()

    head = lax.axis_index("head")
    position = head * tok + lax.broadcasted_iota(I32, (1, tok), 1)
    end = 0
    facts = [jnp.zeros((1, tok), I32)] * 3
    for s in range(length_ref.shape[1]):
        adapter = adapter_ref[0, s]
        new = (end, adapter, owner_ref[adapter] if by_slot else s)
        inside = position >= end
        facts = [jnp.where(inside, value, old) for value, old in zip(new, facts)]
        end = end + length_ref[0, s]
    for i, fact in enumerate(facts):
        facts_ref[i : i + 1, :] = fact

    key_rows = bias_ref.shape[0]
    key_position = (
        head * tok - (key_rows - tok) + lax.broadcasted_iota(I32, (key_rows, tok), 0)
    )
    allowed = (key_position >= facts[0]) & (key_position <= position)
    bias = jnp.where(allowed, 0.0, NEVER)
    bias_ref[:, :tok] = bias
    bias_ref[:, tok:] = bias

    rank = act_ref.shape[0]
    n_groups = act_cols_ref.shape[0] // rank
    own = group_rows(rank, n_groups, tok, lax.axis_index("seq"), by_slot) == facts[2]
    act = jnp.concatenate([act_ref[...].astype(F32)] * n_groups, axis=0)
    act_cols_ref[...] = jnp.where(own, act, 0.0).astype(BF16)

    for kv in range(KEY_VALUE_HEADS):
        for copy in fetch(kv):
            copy.wait()
        for i in range(GROUP):
            at = slice(kv * per_kv + i * HEAD_SIZE, kv * per_kv + (i + 1) * HEAD_SIZE)
            q_turned[at, :] = q_ref[:, at].T
            g_turned[at, :] = g_ref[:, at].T


def attention_kernel(by_slot, n_halo, *refs):
    bias_hbm, act_hbm, k_hbm, v_hbm, q_hbm, g_hbm, *refs = refs
    halo_hbms, refs = refs[:n_halo], refs[n_halo:]
    n_out = 2 if by_slot else 1
    dq_hbm, *refs = refs
    up_hbms, refs = refs[:n_out], refs[n_out:]
    bias_ref, act_ref, k_all, v_all, k_turned, q_ref, g_ref, dq_ref, *refs = refs
    up_refs, (first_sem, q_sem, g_sem, dq_sem, up_sem) = refs[:n_out], refs[n_out:]
    kv_width = k_all.shape[1]
    tok = q_ref.shape[1]
    head = lax.axis_index("head")
    n_quarters, per, rank, part = up_refs[0].shape
    n_groups = per * n_out
    per_kv = GROUP * HEAD_SIZE
    heads_per_quarter = part // HEAD_SIZE
    quarters_per_kv = GROUP // heads_per_quarter

    moves = [(bias_hbm, bias_ref), (act_hbm, act_ref)]
    start = 0
    for halo in halo_hbms:
        rows = pl.ds(start, halo.shape[0])
        moves.append((halo.at[:, pl.ds(0, kv_width)], k_all.at[rows, :]))
        moves.append((halo.at[:, pl.ds(kv_width, kv_width)], v_all.at[rows, :]))
        start += halo.shape[0]
    moves.append((k_hbm, k_all.at[pl.ds(start, tok), :]))
    moves.append((v_hbm, v_all.at[pl.ds(start, tok), :]))
    first = [pltpu.make_async_copy(a, b, first_sem.at[i]) for i, (a, b) in enumerate(moves)]

    def rows_of(kv):
        return pl.ds(pl.multiple_of(kv * per_kv, per_kv), per_kv)

    def fetch(kv):
        at = rows_of(kv)
        return (
            pltpu.make_async_copy(q_hbm.at[at, :], q_ref.at[at, :], q_sem.at[kv]),
            pltpu.make_async_copy(g_hbm.at[at, :], g_ref.at[at, :], g_sem.at[kv]),
        )

    def place_of(quarter):
        return lax.rem(quarter + n_quarters - head, n_quarters) if by_slot else quarter

    def put(kv):
        at = rows_of(kv)
        copies = [pltpu.make_async_copy(dq_ref.at[at, :], dq_hbm.at[at, :], dq_sem.at[kv])]
        for i in range(quarters_per_kv):
            j = place_of(kv * quarters_per_kv + i)
            for o in range(n_out):
                sem = up_sem.at[kv * quarters_per_kv + i, o]
                copies.append(pltpu.make_async_copy(up_refs[o].at[j], up_hbms[o].at[j], sem))
        return copies

    for copy in first:
        copy.start()
    for kv in range(KEY_VALUE_HEADS):
        for copy in fetch(kv):
            copy.start()
    for copy in first:
        copy.wait()
    k_turned[...] = k_all[...].T

    scale = 1.0 / HEAD_SIZE**0.5
    to_log2 = scale * math.log2(math.e)

    def one_group(kv, carry):
        for copy in fetch(kv):
            copy.wait()
        at_kv = pl.ds(pl.multiple_of(kv * HEAD_SIZE, HEAD_SIZE), HEAD_SIZE)
        k_g = k_all[:, at_kv]
        v_g = v_all[:, at_kv]
        kt_g = k_turned[at_kv, :]
        for i in range(0, GROUP, 2):
            from_row = (kv * GROUP + i) * HEAD_SIZE
            at = [
                pl.ds(pl.multiple_of(from_row + n * HEAD_SIZE, HEAD_SIZE), HEAD_SIZE)
                for n in range(2)
            ]
            q_two = jnp.concatenate([q_ref[at[0], :], q_ref[at[1], :]], axis=1)
            g_two = jnp.concatenate([g_ref[at[0], :], g_ref[at[1], :]], axis=1)
            s = dot(k_g, q_two, 1, 0) + bias_ref[...]
            d_prob = dot(v_g, g_two, 1, 0)
            weights = jnp.exp2((s - jnp.max(s, axis=0, keepdims=True)) * to_log2)
            inverse = 1.0 / jnp.sum(weights, axis=0, keepdims=True)
            delta = jnp.sum(weights * d_prob, axis=0, keepdims=True) * inverse
            dscore = (weights * (d_prob - delta)).astype(BF16)
            dq = (dot(kt_g, dscore, 1, 0) * (inverse * scale)).astype(BF16)
            j = place_of(kv * quarters_per_kv + i // heads_per_quarter)
            for n in range(2):
                dq_one = dq[:, n * tok : (n + 1) * tok]
                dq_ref[at[n], :] = dq_one
                up = dot(act_ref[...], dq_one, 1, 1).astype(BF16)
                to = (i % heads_per_quarter + n) * HEAD_SIZE
                for r in range(n_groups):
                    piece = up[r * rank : (r + 1) * rank, :]
                    up_refs[r // per][j, r % per, :, to : to + HEAD_SIZE] = piece
        for copy in put(kv):
            copy.start()
        return carry

    lax.fori_loop(0, KEY_VALUE_HEADS, one_group, 0)
    for kv in range(KEY_VALUE_HEADS):
        for copy in put(kv):
            copy.wait()


def down_kernel(by_slot, n_w, *refs):
    facts_hbm, dq_hbm, *refs = refs
    w_hbms, (x_hbm, *refs) = refs[:n_w], refs[n_w:]
    n_out = 2 if by_slot else 1
    down_hbms, (facts_ref, dq_ref, *refs) = refs[:n_out], refs[n_out:]
    w_refs, (x_ref, *refs) = refs[:n_w], refs[n_w:]
    down_refs, (facts_sem, dq_sem, w_sem, x_sem, down_sem) = refs[:n_out], refs[n_out:]
    tok = dq_ref.shape[1]
    seq, head = lax.axis_index("seq"), lax.axis_index("head")
    n_adapters, n_quarters, rank, part = w_refs[0].shape
    per, _, _, x_part = down_refs[0].shape
    n_groups = per * n_out

    facts_copy = pltpu.make_async_copy(facts_hbm, facts_ref, facts_sem)
    w_copies = [
        pltpu.make_async_copy(a, b, w_sem.at[i]) for i, (a, b) in enumerate(zip(w_hbms, w_refs))
    ]

    def fetch_dq(quarter):
        at = pl.ds(quarter * part, part)
        return pltpu.make_async_copy(dq_hbm.at[at, :], dq_ref.at[at, :], dq_sem.at[quarter])

    def fetch_x(j):
        quarter = lax.rem(head + j, n_quarters) if by_slot else j
        at = pl.ds(pl.multiple_of(quarter * x_part, x_part), x_part)
        to = pl.ds(j * x_part, x_part)
        return pltpu.make_async_copy(x_hbm.at[:, at], x_ref.at[:, to], x_sem.at[j])

    def put(j, o):
        to = down_hbms[o].at[:, j]
        return pltpu.make_async_copy(down_refs[o].at[:, j], to, down_sem.at[j, o])

    for copy in w_copies:
        copy.start()
    for quarter in range(n_quarters):
        fetch_dq(quarter).start()
    facts_copy.start()
    for j in range(n_quarters):
        fetch_x(j).start()

    for copy in w_copies:
        copy.wait()
    sums = [None] * n_w
    for quarter in range(n_quarters):
        fetch_dq(quarter).wait()
        j = lax.rem(head + n_quarters - quarter, n_quarters) if by_slot else quarter
        dq = dq_ref[quarter * part : (quarter + 1) * part, :]
        for c, w_ref in enumerate(w_refs):
            new = dot(w_ref[:, j].reshape(n_adapters * rank, part), dq, 1, 0)
            sums[c] = new if sums[c] is None else sums[c] + new
    facts_copy.wait()
    adapter = facts_ref[1:2, :]
    total = jnp.zeros((rank, tok), F32)
    for c in range(n_w):
        for m in range(n_adapters):
            a = (2 * m + c) ^ seq if by_slot else m
            rows = sums[c][m * rank : (m + 1) * rank, :]
            total = total + jnp.where(adapter == a, rows, 0.0)
    own = group_rows(rank, n_groups, tok, seq, by_slot) == facts_ref[2:3, :]
    low = jnp.concatenate([total.astype(BF16).astype(F32)] * n_groups, axis=0)
    cols = jnp.where(own, low, 0.0).astype(BF16)

    step = min(512, x_part)
    for j in range(n_quarters):
        fetch_x(j).wait()
        for start in range(0, x_part, step):
            down = dot(cols, x_ref[:, j * x_part + start : j * x_part + start + step], 1, 0)
            down = down.astype(BF16)
            for n in range(n_groups):
                piece = down[n * rank : (n + 1) * rank, :]
                down_refs[n // per][n % per, j, :, start : start + step] = piece
        for o in range(n_out):
            put(j, o).start()
    for o in range(n_out):
        for j in range(n_quarters):
            put(j, o).wait()


def shifted(x, n_head, j):
    return lax.ppermute(x, "head", [(i, (i + j) % n_head) for i in range(n_head)])


def partnered(x, n_seq, bits):
    return lax.ppermute(x, "seq", [(i, i ^ bits) for i in range(n_seq)])


def on_device(
    queries, keys, values, output_gradient, inputs, adapter_activation,
    adapter_up_weight, segment_length, segment_adapter, owner,
):
    n_head = lax.axis_size("head")
    n_seq = lax.axis_size("seq")
    tok, width = queries.shape
    pack = tok * n_head
    rank = adapter_up_weight.shape[1]
    n_adapters = owner.shape[0]
    n_seg = segment_length.shape[1]
    by_slot = n_adapters == n_seq == 8

    reach = []
    while sum(reach) < pack * 3 // 8:
        reach.append(min(pack * 3 // 8 - sum(reach), tok))
    key_rows = tok + sum(reach)
    packed = pl.pallas_call(
        pack_kernel,
        out_shape=jax.ShapeDtypeStruct((tok, 2 * keys.shape[1]), BF16),
        in_specs=[ANY] * 2,
        out_specs=ANY,
        scratch_shapes=[pltpu.SemaphoreType.DMA((2,))],
        name="pack_halo",
    )(keys, values)
    def forward(x):
        return lax.ppermute(x, "head", [(i, i + 1) for i in range(n_head - 1)])

    halos = [forward(packed[tok - reach[0] :])]

    if by_slot:
        w = [adapter_up_weight] + [shifted(adapter_up_weight, n_head, j) for j in range(1, n_head)]
        w = jnp.concatenate(w, axis=0)[None]
        w = [w] + [partnered(w, n_seq, 2 * m) for m in range(1, n_seq // 2)]
    else:
        w = lax.all_gather(adapter_up_weight, "seq", axis=0, tiled=True)
        up_weight = [lax.all_gather(w, "head", axis=1, tiled=False)]
    for rows in reach[1:]:
        halos.insert(0, forward(halos[0][tok - rows :]))
    n_out = 2 if by_slot else 1
    n_groups = n_seq if by_slot else n_seg
    part = width // n_head
    x_part = inputs.shape[1] // n_head
    ready = pl.pallas_call(
        functools.partial(ready_kernel, by_slot),
        out_shape=[
            jax.ShapeDtypeStruct((8, tok), I32),
            jax.ShapeDtypeStruct((key_rows, 2 * tok), F32),
            jax.ShapeDtypeStruct((n_groups * rank, tok), BF16),
            jax.ShapeDtypeStruct((width, tok), BF16),
            jax.ShapeDtypeStruct((width, tok), BF16),
        ],
        in_specs=[ANY] * 6,
        out_specs=[VMEM] * 5,
        scratch_shapes=[
            pltpu.SMEM(segment_length.shape, I32),
            pltpu.SMEM(segment_adapter.shape, I32),
            pltpu.SMEM(owner.shape, I32),
            pltpu.VMEM((rank, tok), BF16),
            pltpu.VMEM((tok, width), BF16),
            pltpu.VMEM((tok, width), BF16),
            pltpu.SemaphoreType.DMA((4,)),
            pltpu.SemaphoreType.DMA((KEY_VALUE_HEADS,)),
            pltpu.SemaphoreType.DMA((KEY_VALUE_HEADS,)),
        ],
        cost_estimate=pl.CostEstimate(
            flops=tok * width * 64, bytes_accessed=8 * tok * width * 2, transcendentals=0
        ),
        name="ready",
    )(
        segment_length, segment_adapter, owner, adapter_activation.T, queries, output_gradient,
    )

    if by_slot:
        _, _, w = lax.optimization_barrier((halos, ready, w))
        w = jnp.concatenate(w, axis=0)
        up_weight = [w, partnered(w, n_seq, 1)]

    up_shape = ((n_head, n_groups // n_out, rank, part), BF16)
    down_shape = ((n_groups // n_out, n_head, rank, x_part), BF16)
    facts, bias, act_cols, q_turned, g_turned = ready
    dq, *up = pl.pallas_call(
        functools.partial(attention_kernel, by_slot, len(halos)),
        out_shape=[jax.ShapeDtypeStruct((width, tok), BF16)]
        + [jax.ShapeDtypeStruct(*up_shape)] * n_out,
        in_specs=[ANY] * (6 + len(halos)),
        out_specs=[ANY] * (1 + n_out),
        scratch_shapes=[
            pltpu.VMEM(bias.shape, F32),
            pltpu.VMEM(act_cols.shape, BF16),
            pltpu.VMEM((key_rows, keys.shape[1]), BF16),
            pltpu.VMEM((key_rows, keys.shape[1]), BF16),
            pltpu.VMEM((keys.shape[1], key_rows), BF16),
            pltpu.VMEM((width, tok), BF16),
            pltpu.VMEM((width, tok), BF16),
            pltpu.VMEM((width, tok), BF16),
        ]
        + [pltpu.VMEM(*up_shape)] * n_out
        + [
            pltpu.SemaphoreType.DMA((4 + 2 * len(halos),)),
            pltpu.SemaphoreType.DMA((KEY_VALUE_HEADS,)),
            pltpu.SemaphoreType.DMA((KEY_VALUE_HEADS,)),
            pltpu.SemaphoreType.DMA((KEY_VALUE_HEADS,)),
            pltpu.SemaphoreType.DMA((n_head, n_out)),
        ],
        cost_estimate=pl.CostEstimate(
            flops=2 * tok * width * key_rows * 3,
            bytes_accessed=4 * tok * width * 2,
            transcendentals=tok * key_rows * QUERY_HEADS,
        ),
        name="attention",
    )(bias, act_cols, keys, values, q_turned, g_turned, *halos)

    down = pl.pallas_call(
        functools.partial(down_kernel, by_slot, len(up_weight)),
        out_shape=[jax.ShapeDtypeStruct(*down_shape)] * n_out,
        in_specs=[ANY] * (3 + len(up_weight)),
        out_specs=[ANY] * n_out,
        scratch_shapes=[pltpu.VMEM(facts.shape, I32), pltpu.VMEM((width, tok), BF16)]
        + [pltpu.VMEM(w.shape, BF16) for w in up_weight]
        + [pltpu.VMEM(inputs.shape, BF16)]
        + [pltpu.VMEM(*down_shape)] * n_out
        + [
            pltpu.SemaphoreType.DMA,
            pltpu.SemaphoreType.DMA((n_head,)),
            pltpu.SemaphoreType.DMA((len(up_weight),)),
            pltpu.SemaphoreType.DMA((n_head,)),
            pltpu.SemaphoreType.DMA((n_head, n_out)),
        ],
        cost_estimate=pl.CostEstimate(
            flops=2 * n_groups * rank * tok * (width + inputs.shape[1]),
            bytes_accessed=4 * tok * inputs.shape[1] * 2,
            transcendentals=0,
        ),
        name="down_parts",
    )(facts, dq, *up_weight, inputs)

    if by_slot:
        up = over_chips(over_z(over_cores(up, n_seq), n_head).astype(BF16), n_seq)
        down = over_z(over_chips(over_cores(down, n_seq), n_seq).astype(BF16), n_head)
    else:
        up = lax.all_to_all(up[0], "head", split_axis=0, concat_axis=0, tiled=True)
        up = spread(jnp.sum(up.astype(F32), axis=0), segment_adapter, owner, n_seq)
        down = lax.all_to_all(down[0], "head", split_axis=1, concat_axis=1, tiled=True)
        down = spread(jnp.sum(down.astype(F32), axis=1), segment_adapter, owner, n_seq)
    return down.T[None] * ADAPTER_SCALE, up[None] * ADAPTER_SCALE


def over_cores(parts, n_seq):
    keep, send = parts
    return (keep.astype(F32) + partnered(send, n_seq, 1).astype(F32)).astype(BF16)


def over_chips(both, n_seq):
    total = both[0].astype(F32)
    for m in range(1, n_seq // 2):
        total = total + partnered(both[m], n_seq, 2 * m).astype(F32)
    return total


def over_z(both, n_head):
    total = both[0].astype(F32)
    for j in range(1, n_head):
        total = total + shifted(both[j], n_head, j).astype(F32)
    return total


def spread(part, segment_adapter, owner, n_seq):
    goes_to = owner[segment_adapter[0]]
    slots = (goes_to[:, None] == jnp.arange(n_seq, dtype=I32)[None, :]).astype(F32)
    slotted = jnp.einsum("srw,so->orw", part, slots, precision=lax.Precision.HIGHEST)
    slotted = lax.all_to_all(slotted.astype(BF16), "seq", split_axis=0, concat_axis=0, tiled=True)
    return jnp.sum(slotted.astype(F32), axis=0)


def solution(mesh):
    return jax.shard_map(
        on_device,
        mesh=mesh,
        in_specs=(
            P(("seq", "head"), None),
            P(("seq", "head"), None),
            P(("seq", "head"), None),
            P(("seq", "head"), None),
            P(("seq", "head"), None),
            P(("seq", "head"), None),
            P("seq", None, "head"),
            P("seq", None),
            P("seq", None),
            P(),
        ),
        out_specs=(P("seq", "head", None), P("seq", None, "head")),
        check_vma=False,
    )
```

time: 72.6 us -> 89.3 us (1.23)
  Pallas kernels: 12.6 us -> 30.2 us
  waiting for transfers between devices: 10.2 us -> 20.2 us
  starting transfers between devices: 39.2 us -> 33.3 us
  local copies, waits for them, and re-layouts: 6.34 us -> 1.45 us
    pallas_call x3, Pallas kernels: 10.2 us -> 25.3 us  [the longest x1 12.8 us: on_device(): pl.pallas_call(functools.partial(attention_kernel, by_slot, len(halos)),...]
    ppermute x9, waiting for transfers between devices: 3.6 us -> 16.4 us  [shifted(): lax.ppermute(x, 'head', [(i, (i + j) % n_head) for i in range(n_head)])]
    unnamed x18 -> x17, local copies, waits for them, and re-layouts: 6.23 us -> 1.32 us
    ppermute x9, starting transfers between devices: 17.6 us -> 13.8 us  [shifted(): lax.ppermute(x, 'head', [(i, (i + j) % n_head) for i in range(n_head)])]
    ppermute x12, waiting for transfers between devices: 6.55 us -> 3.8 us  [partnered(): return lax.ppermute(x, 'seq', [(i, i ^ bits) for i in range(n_seq)])]
    pallas_call x1, Pallas kernels: 2.38 us -> 4.94 us  [on_device(): pl.pallas_call(functools.partial(down_kernel, by_slot, len(up_weight)), o...]
    ppermute x12, starting transfers between devices: 13.5 us -> 11.3 us  [partnered(): return lax.ppermute(x, 'seq', [(i, i ^ bits) for i in range(n_seq)])]
    ppermute x4 -> x2, starting transfers between devices: 8.03 us -> 8.18 us  [forward(): return lax.ppermute(x, 'head', [(i, i + 1) for i in range(n_head - 1)])]
  transfers between devices with their start and end apart: 25 -> 23, of which waited for: 5 -> 9; matrix products, arithmetic and copies ran while one was open for 3% -> 3% of each run, Pallas kernels for 14% -> 18%
where the time goes in v4:
time: 89.3 us; the launch traced here: 89 us
  starting transfers between devices  33.3 us (37%)
  Pallas kernels  30.2 us (34%)
  waiting for transfers between devices  20.2 us (23%)
  other arithmetic  2.91 us (3%)
  local copies, waits for them, and re-layouts  1.45 us (2%)
    ppermute x9, waiting for transfers between devices, shifted(): lax.ppermute(x, 'head', [(i, (i + j) % n_head) for i in range(n_head)])  16.4 us
    ppermute x9, starting transfers between devices, shifted(): lax.ppermute(x, 'head', [(i, (i + j) % n_head) for i in range(n_head)])  13.8 us
    pallas_call x1, Pallas kernels, on_device(): pl.pallas_call(functools.partial(attention_kernel, by_slot, len(halos)),...  12.8 us
    ppermute x12, starting transfers between devices, partnered(): return lax.ppermute(x, 'seq', [(i, i ^ bits) for i in range(n_seq)])  11.3 us
    pallas_call x1, Pallas kernels, on_device(): pl.pallas_call(pack_kernel, out_shape=jax.ShapeDtypeStruct((tok, 2 * keys...  9.06 us
    ppermute x2, starting transfers between devices, forward(): return lax.ppermute(x, 'head', [(i, i + 1) for i in range(n_head - 1)])  8.18 us
    pallas_call x1, Pallas kernels, on_device(): pl.pallas_call(functools.partial(down_kernel, by_slot, len(up_weight)), o...  4.94 us
    ppermute x12, waiting for transfers between devices, partnered(): return lax.ppermute(x, 'seq', [(i, i ^ bits) for i in range(n_seq)])  3.8 us
  transfers between devices with their start and end apart: 23, of which 9 were waited for; matrix products, arithmetic and copies ran while one was open for 3% of the time, Pallas kernels for 18%

profile of v4, /device:TPU:0, one launch (start us, length us, event | category | flops | bytes accessed | tf_op | source)
XLA Modules:
  0.0 89.0 jit_solution(5537479653879058302)
XLA Ops:
  0.6 9.1 %pack_halo.1 = bf16[128,1024]{1,0:T(8,128)(2,1)} custom-call(bf16[128,512]{1,0:T(8,128)(2,1)} %refs_2_.1, bf16[128,512]{1,0:T(8,128)(2,1)} %refs_3_.1), custom_call_target="tpu_custom_call" | custom-call | tf_op jit(solution)/shard_map/pack_halo/pallas_call | solution.py:327
  9.7 4.9 %collective-permute-start = (bf16[128,1024]{1,0:T(8,128)(2,1)}, bf16[128,1024]{1,0:T(8,128)(2,1)S(1)}, u32[]{:S(2)}, u32[]{:S(2)}) collective-permute-start(bf16[128,1024]{1,0:T(8,128)(2,1)} %pack_halo.1), channel_id=1, source_target_pairs={{0,1},{1,2},{2,3},{4,5},{5,6},{6,7},{8,9},{9,10},{10,11},{12,13},{... | collective-permute-start | bytes 786440 | tf_op jit(solution)/shard_map/ppermute | solution.py:336
  14.6 1.5 %collective-permute-start.4 = (bf16[1,16,1024]{2,1,0:T(8,128)(2,1)}, bf16[1,16,1024]{2,1,0:T(8,128)(2,1)S(1)}, u32[]{:S(2)}, u32[]{:S(2)}) collective-permute-start(bf16[1,16,1024]{2,1,0:T(8,128)(2,1)} %param.16), channel_id=1, source_target_pairs={{0,3},{1,0},{2,1},{3,2},{4,7},{5,4},{6,5},{7,6},{8,11},{9,8},{10,9... | collective-permute-start | bytes 98312 | tf_op jit(solution)/shard_map/ppermute | solution.py:303
  16.1 1.6 %collective-permute-start.3 = (bf16[1,16,1024]{2,1,0:T(8,128)(2,1)}, bf16[1,16,1024]{2,1,0:T(8,128)(2,1)S(1)}, u32[]{:S(2)}, u32[]{:S(2)}) collective-permute-start(bf16[1,16,1024]{2,1,0:T(8,128)(2,1)} %param.16), channel_id=1, source_target_pairs={{0,2},{1,3},{2,0},{3,1},{4,6},{5,7},{6,4},{7,5},{8,10},{9,11},{10,... | collective-permute-start | bytes 98312 | tf_op jit(solution)/shard_map/ppermute | solution.py:303
  17.7 1.6 %collective-permute-start.2 = (bf16[1,16,1024]{2,1,0:T(8,128)(2,1)}, bf16[1,16,1024]{2,1,0:T(8,128)(2,1)S(1)}, u32[]{:S(2)}, u32[]{:S(2)}) collective-permute-start(bf16[1,16,1024]{2,1,0:T(8,128)(2,1)} %param.16), channel_id=1, source_target_pairs={{0,1},{1,2},{2,3},{3,0},{4,5},{5,6},{6,7},{7,4},{8,9},{9,10},{10,1... | collective-permute-start | bytes 98312 | tf_op jit(solution)/shard_map/ppermute | solution.py:303
  19.3 2.6 %collective-permute-done.4 = bf16[1,16,1024]{2,1,0:T(8,128)(2,1)S(1)} collective-permute-done((bf16[1,16,1024]{2,1,0:T(8,128)(2,1)}, bf16[1,16,1024]{2,1,0:T(8,128)(2,1)S(1)}, u32[]{:S(2)}, u32[]{:S(2)}) %collective-permute-start.4) | collective-permute-done | bytes 32800 | tf_op jit(solution)/shard_map/ppermute | solution.py:303
  21.9 0.4 collective-permute-done.3
  22.3 1.4 %collective-permute-done.2 = bf16[1,16,1024]{2,1,0:T(8,128)(2,1)S(1)} collective-permute-done((bf16[1,16,1024]{2,1,0:T(8,128)(2,1)}, bf16[1,16,1024]{2,1,0:T(8,128)(2,1)S(1)}, u32[]{:S(2)}, u32[]{:S(2)}) %collective-permute-start.2) | collective-permute-done | bytes 32800 | tf_op jit(solution)/shard_map/ppermute | solution.py:303
  23.7 0.8 maximum_bitcast_fusion
  24.4 1.6 %collective-permute-start.5 = (bf16[1,4,16,1024]{3,2,1,0:T(8,128)(2,1)S(1)}, bf16[1,4,16,1024]{3,2,1,0:T(8,128)(2,1)S(1)}, u32[]{:S(2)}, u32[]{:S(2)}) collective-permute-start(bf16[1,4,16,1024]{3,2,1,0:T(8,128)(2,1)S(1)} %maximum_bitcast_fusion), channel_id=1, source_target_pairs={{0,8},{4,12},{8,0},{12,4},{16,24},{20,28},{24,16},{28,20},{1,9},{5... | collective-permute-start | bytes 393224 | tf_op jit(solution)/shard_map/ppermute | solution.py:307
  26.0 1.5 %collective-permute-start.6 = (bf16[1,4,16,1024]{3,2,1,0:T(8,128)(2,1)S(1)}, bf16[1,4,16,1024]{3,2,1,0:T(8,128)(2,1)S(1)}, u32[]{:S(2)}, u32[]{:S(2)}) collective-permute-start(bf16[1,4,16,1024]{3,2,1,0:T(8,128)(2,1)S(1)} %maximum_bitcast_fusion), channel_id=1, source_target_pairs={{0,16},{4,20},{8,24},{12,28},{16,0},{20,4},{24,8},{28,12},{1,17},{... | collective-permute-start | bytes 393224 | tf_op jit(solution)/shard_map/ppermute | solution.py:307
  27.5 0.5 collective-permute-start.7
  28.0 0.0 collective-permute-done.refs_7_
  28.0 3.2 %collective-permute-start.1 = (bf16[64,1024]{1,0:T(8,128)(2,1)S(1)}, bf16[64,1024]{1,0:T(8,128)(2,1)S(1)}, u32[]{:S(2)}, u32[]{:S(2)}) collective-permute-start(bf16[64,1024]{1,0:T(8,128)(2,1)S(1)} %slice.68), channel_id=1, source_target_pairs={{0,1},{1,2},{2,3},{4,5},{5,6},{6,7},{8,9},{9,10},{10,11},{12,13},{... | collective-permute-start | bytes 393224 | tf_op jit(solution)/shard_map/ppermute | solution.py:336
  31.3 3.4 %ready.1 = (s32[8,128]{1,0:T(8,128)}, f32[320,256]{1,0:T(8,128)}, bf16[128,128]{1,0:T(8,128)(2,1)}, bf16[4096,128]{1,0:T(8,128)(2,1)}, bf16[4096,128]{1,0:T(8,128)(2,1)}) custom-call(s32[1,8]{1,0:T(1,128)} %length_hbm.1, s32[1,8]{1,0:T(1,128)} %adapter_hbm.1, s32[8]{0:T(128)} %owner_hbm.1, bf16[16,128]{1,0:T(8,128)(2,1)} %bitcast.53, ...), custom_call_target="tpu_custom_call" | custom-call | flops 33554432 | bytes 8388608 | tf_op jit(solution)/shard_map/ready/pallas_call | solution.py:353
  34.7 0.0 copy-start.6
  34.8 0.1 collective-permute-start.8
  34.9 0.5 copy-done.6
  35.4 12.8 %attention.1 = (bf16[4096,128]{1,0:T(8,128)(2,1)}, bf16[4,4,16,1024]{3,2,1,0:T(8,128)(2,1)}, bf16[4,4,16,1024]{3,2,1,0:T(8,128)(2,1)}) custom-call(f32[320,256]{1,0:T(8,128)} %get-tuple-element.17.refs_0_, bf16[128,128]{1,0:T(8,128)(2,1)} %get-tuple-element.18.refs_1_, bf16[128,512]{1,0:T(8,128)(2,1)} %refs_2_.1, bf16[128,512]{1,0:T(8,128)(2,1)} %refs_3_.1, ...), custom_call_target="tpu_custom_call" | custom-call | flops 1006632960 | bytes 4194304 | tf_op jit(solution)/shard_map/attention/pallas_call | solution.py:391
  48.2 0.8 copy-done.3
  49.0 4.9 %down_parts.1 = (bf16[4,4,16,2048]{3,2,1,0:T(8,128)(2,1)}, bf16[4,4,16,2048]{3,2,1,0:T(8,128)(2,1)}) custom-call(s32[8,128]{1,0:T(8,128)} %get-tuple-element.16.refs_0_, bf16[4096,128]{1,0:T(8,128)(2,1)} %get-tuple-element.21.refs_1_, bf16[4,4,16,1024]{3,2,1,0:T(8,128)(2,1)} %copy-done.1, bf16[4,4,16,1024]{3,2,1,0:T(8,128)(2,1)} %copy-done.3, ...), custom_call_target="tpu_custom_call" | custom-call | flops 402653184 | bytes 8388608 | tf_op jit(solution)/shard_map/down_parts/pallas_call | solution.py:423
  54.0 0.1 collective-permute-start.9
  54.1 0.5 collective-permute-start.16
  54.6 2.9 %collective-permute-done.16 = bf16[4,4,16,1024]{3,2,1,0:T(8,128)(2,1)S(1)} collective-permute-done((bf16[4,4,16,1024]{3,2,1,0:T(8,128)(2,1)S(1)}, bf16[4,4,16,1024]{3,2,1,0:T(8,128)(2,1)S(1)}, u32[]{:S(2)}, u32[]{:S(2)}) %collective-permute-start.16) | collective-permute-done | bytes 524320 | tf_op jit(solution)/shard_map/ppermute | solution.py:307
  57.5 0.2 add_convert_fusion.1
  57.7 3.8 %collective-permute-start.19 = (bf16[4,16,1024]{2,1,0:T(8,128)(2,1)S(1)}, bf16[4,16,1024]{2,1,0:T(8,128)(2,1)S(1)}, u32[]{:S(2)}, u32[]{:S(2)}) collective-permute-start(bf16[4,16,1024]{2,1,0:T(8,128)(2,1)S(1)} %get-tuple-element.34), channel_id=1, source_target_pairs={{0,3},{1,0},{2,1},{3,2},{4,7},{5,4},{6,5},{7,6},{8,11},{9,8},{10,9... | collective-permute-start | bytes 393224 | tf_op jit(solution)/shard_map/ppermute | solution.py:303
  61.5 0.0 collective-permute-start.18
  61.5 1.5 %collective-permute-start.17 = (bf16[4,16,1024]{2,1,0:T(8,128)(2,1)S(1)}, bf16[4,16,1024]{2,1,0:T(8,128)(2,1)S(1)}, u32[]{:S(2)}, u32[]{:S(2)}) collective-permute-start(bf16[4,16,1024]{2,1,0:T(8,128)(2,1)S(1)} %get-tuple-element.33), channel_id=1, source_target_pairs={{0,1},{1,2},{2,3},{3,0},{4,5},{5,6},{6,7},{7,4},{8,9},{9,10},{10,1... | collective-permute-start | bytes 393224 | tf_op jit(solution)/shard_map/ppermute | solution.py:303
  63.0 0.4 add_convert_fusion
  63.4 0.1 slice_bitcast_fusion.2
  63.4 2.5 %collective-permute-start.12 = (bf16[4,16,2048]{2,1,0:T(8,128)(2,1)S(1)}, bf16[4,16,2048]{2,1,0:T(8,128)(2,1)S(1)}, u32[]{:S(2)}, u32[]{:S(2)}) collective-permute-start(bf16[4,16,2048]{2,1,0:T(8,128)(2,1)S(1)} %get-tuple-element.31), channel_id=1, source_target_pairs={{0,24},{4,28},{8,16},{12,20},{16,8},{20,12},{24,0},{28,4},{1,25},{... | collective-permute-start | bytes 786440 | tf_op jit(solution)/shard_map/ppermute | solution.py:307
  66.0 0.5 collective-permute-start.11
  66.5 0.5 collective-permute-start.10
  67.0 6.4 %collective-permute-done.18 = bf16[4,16,1024]{2,1,0:T(8,128)(2,1)S(1)} collective-permute-done((bf16[4,16,1024]{2,1,0:T(8,128)(2,1)S(1)}, bf16[4,16,1024]{2,1,0:T(8,128)(2,1)S(1)}, u32[]{:S(2)}, u32[]{:S(2)}) %collective-permute-start.18) | collective-permute-done | bytes 131104 | tf_op jit(solution)/shard_map/ppermute | solution.py:303
  73.5 0.1 fusion.5
  73.5 2.5 %collective-permute-start.22 = (bf16[16,1024]{1,0:T(8,128)(2,1)S(1)}, bf16[16,1024]{1,0:T(8,128)(2,1)S(1)}, u32[]{:S(2)}, u32[]{:S(2)}) collective-permute-start(bf16[16,1024]{1,0:T(8,128)(2,1)S(1)} %get-tuple-element.40), channel_id=1, source_target_pairs={{0,24},{4,28},{8,16},{12,20},{16,8},{20,12},{24,0},{28,4},{1,25},{... | collective-permute-start | bytes 98312 | tf_op jit(solution)/shard_map/ppermute | solution.py:307
  76.0 0.5 collective-permute-start.21
  76.6 0.5 collective-permute-start.20
  77.1 0.8 collective-permute-done.11
  77.9 0.1 collective-permute-done.10
  78.0 0.1 fusion.2
  78.2 3.0 %collective-permute-start.15 = (bf16[16,2048]{1,0:T(8,128)(2,1)S(1)}, bf16[16,2048]{1,0:T(8,128)(2,1)S(1)}, u32[]{:S(2)}, u32[]{:S(2)}) collective-permute-start(bf16[16,2048]{1,0:T(8,128)(2,1)S(1)} %get-tuple-element.37), channel_id=1, source_target_pairs={{0,3},{1,0},{2,1},{3,2},{4,7},{5,4},{6,5},{7,6},{8,11},{9,8},{10,9... | collective-permute-start | bytes 196616 | tf_op jit(solution)/shard_map/ppermute | solution.py:303
  81.2 0.8 collective-permute-start.14
  82.0 0.0 collective-permute-start.13
  82.1 0.7 fusion.13
  82.7 1.0 %collective-permute-done.15 = bf16[16,2048]{1,0:T(8,128)(2,1)S(1)} collective-permute-done((bf16[16,2048]{1,0:T(8,128)(2,1)S(1)}, bf16[16,2048]{1,0:T(8,128)(2,1)S(1)}, u32[]{:S(2)}, u32[]{:S(2)}) %collective-permute-start.15) | collective-permute-done | bytes 65568 | tf_op jit(solution)/shard_map/ppermute | solution.py:303
  83.7 4.6 %collective-permute-done.14 = bf16[16,2048]{1,0:T(8,128)(2,1)S(1)} collective-permute-done((bf16[16,2048]{1,0:T(8,128)(2,1)S(1)}, bf16[16,2048]{1,0:T(8,128)(2,1)S(1)}, u32[]{:S(2)}, u32[]{:S(2)}) %collective-permute-start.14) | collective-permute-done | bytes 65568 | tf_op jit(solution)/shard_map/ppermute | solution.py:303
  88.3 0.7 fusion.9
  (32 shorter events, 0.2 us)
Async XLA Ops:
  9.7 18.3 %collective-permute-start = (bf16[128,1024]{1,0:T(8,128)(2,1)}, bf16[128,1024]{1,0:T(8,128)(2,1)S(1)}, u32[]{:S(2)}, u32[]{:S(2)}) collective-permute-start(bf16[128,1024]{1,0:T(8,128)(2,1)} %pack_halo.1), channel_id=1, source_target_pairs={{0,1},{1,2},{2,3},{4,5},{5,6},{6,7},{8,9},{9,10},{10,11},{12,13},{... | collective-permute-start | bytes 786440 | tf_op jit(solution)/shard_map/ppermute | solution.py:336
  14.6 7.3 %collective-permute-start.4 = (bf16[1,16,1024]{2,1,0:T(8,128)(2,1)}, bf16[1,16,1024]{2,1,0:T(8,128)(2,1)S(1)}, u32[]{:S(2)}, u32[]{:S(2)}) collective-permute-start(bf16[1,16,1024]{2,1,0:T(8,128)(2,1)} %param.16), channel_id=1, source_target_pairs={{0,3},{1,0},{2,1},{3,2},{4,7},{5,4},{6,5},{7,6},{8,11},{9,8},{10,9... | collective-permute-start | bytes 98312 | tf_op jit(solution)/shard_map/ppermute | solution.py:303
  16.1 6.2 %collective-permute-start.3 = (bf16[1,16,1024]{2,1,0:T(8,128)(2,1)}, bf16[1,16,1024]{2,1,0:T(8,128)(2,1)S(1)}, u32[]{:S(2)}, u32[]{:S(2)}) collective-permute-start(bf16[1,16,1024]{2,1,0:T(8,128)(2,1)} %param.16), channel_id=1, source_target_pairs={{0,2},{1,3},{2,0},{3,1},{4,6},{5,7},{6,4},{7,5},{8,10},{9,11},{10,... | collective-permute-start | bytes 98312 | tf_op jit(solution)/shard_map/ppermute | solution.py:303
  17.7 5.9 %collective-permute-start.2 = (bf16[1,16,1024]{2,1,0:T(8,128)(2,1)}, bf16[1,16,1024]{2,1,0:T(8,128)(2,1)S(1)}, u32[]{:S(2)}, u32[]{:S(2)}) collective-permute-start(bf16[1,16,1024]{2,1,0:T(8,128)(2,1)} %param.16), channel_id=1, source_target_pairs={{0,1},{1,2},{2,3},{3,0},{4,5},{5,6},{6,7},{7,4},{8,9},{9,10},{10,1... | collective-permute-start | bytes 98312 | tf_op jit(solution)/shard_map/ppermute | solution.py:303
  24.4 10.3 %collective-permute-start.5 = (bf16[1,4,16,1024]{3,2,1,0:T(8,128)(2,1)S(1)}, bf16[1,4,16,1024]{3,2,1,0:T(8,128)(2,1)S(1)}, u32[]{:S(2)}, u32[]{:S(2)}) collective-permute-start(bf16[1,4,16,1024]{3,2,1,0:T(8,128)(2,1)S(1)} %maximum_bitcast_fusion), channel_id=1, source_target_pairs={{0,8},{4,12},{8,0},{12,4},{16,24},{20,28},{24,16},{28,20},{1,9},{5... | collective-permute-start | bytes 393224 | tf_op jit(solution)/shard_map/ppermute | solution.py:307
  26.0 8.7 %collective-permute-start.6 = (bf16[1,4,16,1024]{3,2,1,0:T(8,128)(2,1)S(1)}, bf16[1,4,16,1024]{3,2,1,0:T(8,128)(2,1)S(1)}, u32[]{:S(2)}, u32[]{:S(2)}) collective-permute-start(bf16[1,4,16,1024]{3,2,1,0:T(8,128)(2,1)S(1)} %maximum_bitcast_fusion), channel_id=1, source_target_pairs={{0,16},{4,20},{8,24},{12,28},{16,0},{20,4},{24,8},{28,12},{1,17},{... | collective-permute-start | bytes 393224 | tf_op jit(solution)/shard_map/ppermute | solution.py:307
  27.5 7.2 %collective-permute-start.7 = (bf16[1,4,16,1024]{3,2,1,0:T(8,128)(2,1)S(1)}, bf16[1,4,16,1024]{3,2,1,0:T(8,128)(2,1)S(1)}, u32[]{:S(2)}, u32[]{:S(2)}) collective-permute-start(bf16[1,4,16,1024]{3,2,1,0:T(8,128)(2,1)S(1)} %maximum_bitcast_fusion), channel_id=1, source_target_pairs={{0,24},{4,28},{8,16},{12,20},{16,8},{20,12},{24,0},{28,4},{1,25},{... | collective-permute-start | bytes 393224 | tf_op jit(solution)/shard_map/ppermute | solution.py:307
  28.0 6.9 %copy-start.4 = (bf16[128,1024]{1,0:T(8,128)(2,1)}, bf16[128,1024]{1,0:T(8,128)(2,1)S(1)}, u32[]{:S(2)}) copy-start(bf16[128,1024]{1,0:T(8,128)(2,1)S(1)} %collective-permute-done.refs_7_) | copy-start | bytes 786436
  28.0 6.7 %collective-permute-start.1 = (bf16[64,1024]{1,0:T(8,128)(2,1)S(1)}, bf16[64,1024]{1,0:T(8,128)(2,1)S(1)}, u32[]{:S(2)}, u32[]{:S(2)}) collective-permute-start(bf16[64,1024]{1,0:T(8,128)(2,1)S(1)} %slice.68), channel_id=1, source_target_pairs={{0,1},{1,2},{2,3},{4,5},{5,6},{6,7},{8,9},{9,10},{10,11},{12,13},{... | collective-permute-start | bytes 393224 | tf_op jit(solution)/shard_map/ppermute | solution.py:336
  34.7 0.7 copy-start.6
  34.8 13.4 %copy-start.1 = (bf16[4,4,16,1024]{3,2,1,0:T(8,128)(2,1)}, bf16[4,4,16,1024]{3,2,1,0:T(8,128)(2,1)S(1)}, u32[]{:S(2)}) copy-start(bf16[4,4,16,1024]{3,2,1,0:T(8,128)(2,1)S(1)} %constant_dynamic-update-slice_fusion.refs_2_) | copy-start | bytes 1572868
  34.8 13.4 %collective-permute-start.8 = (bf16[4,4,16,1024]{3,2,1,0:T(8,128)(2,1)S(1)}, bf16[4,4,16,1024]{3,2,1,0:T(8,128)(2,1)S(1)}, u32[]{:S(2)}, u32[]{:S(2)}) collective-permute-start(bf16[4,4,16,1024]{3,2,1,0:T(8,128)(2,1)S(1)} %constant_dynamic-update-slice_fusion.refs_2_), channel_id=1, source_target_pairs={{0,4},{4,0},{8,12},{12,8},{16,20},{20,16},{24,28},{28,24},{1,5},{5... | collective-permute-start | bytes 1572872 | tf_op jit(solution)/shard_map/ppermute | solution.py:307
  48.2 0.8 copy-start.3
  49.0 5.1 %copy-start.5 = (bf16[4,4,16,1024]{3,2,1,0:T(8,128)(2,1)S(1)}, bf16[4,4,16,1024]{3,2,1,0:T(8,128)(2,1)}, u32[]{:S(2)}) copy-start(bf16[4,4,16,1024]{3,2,1,0:T(8,128)(2,1)} %get-tuple-element.29) | copy-start | bytes 1572868
  49.0 8.4 %copy-start.2 = (bf16[4,4,16,1024]{3,2,1,0:T(8,128)(2,1)S(1)}, bf16[4,4,16,1024]{3,2,1,0:T(8,128)(2,1)}, u32[]{:S(2)}) copy-start(bf16[4,4,16,1024]{3,2,1,0:T(8,128)(2,1)} %get-tuple-element.28) | copy-start | bytes 1572868
  54.0 9.0 %copy-start = (bf16[4,4,16,2048]{3,2,1,0:T(8,128)(2,1)S(1)}, bf16[4,4,16,2048]{3,2,1,0:T(8,128)(2,1)}, u32[]{:S(2)}) copy-start(bf16[4,4,16,2048]{3,2,1,0:T(8,128)(2,1)} %get-tuple-element.26) | copy-start | bytes 3145732
  54.0 9.0 %collective-permute-start.9 = (bf16[4,4,16,2048]{3,2,1,0:T(8,128)(2,1)}, bf16[4,4,16,2048]{3,2,1,0:T(8,128)(2,1)S(1)}, u32[]{:S(2)}, u32[]{:S(2)}) collective-permute-start(bf16[4,4,16,2048]{3,2,1,0:T(8,128)(2,1)} %get-tuple-element.27), channel_id=1, source_target_pairs={{0,4},{4,0},{8,12},{12,8},{16,20},{20,16},{24,28},{28,24},{1,5},{5... | collective-permute-start | bytes 3145736 | tf_op jit(solution)/shard_map/ppermute | solution.py:307
  54.1 3.4 %collective-permute-start.16 = (bf16[4,4,16,1024]{3,2,1,0:T(8,128)(2,1)S(1)}, bf16[4,4,16,1024]{3,2,1,0:T(8,128)(2,1)S(1)}, u32[]{:S(2)}, u32[]{:S(2)}) collective-permute-start(bf16[4,4,16,1024]{3,2,1,0:T(8,128)(2,1)S(1)} %copy-done.5), channel_id=1, source_target_pairs={{0,4},{4,0},{8,12},{12,8},{16,20},{20,16},{24,28},{28,24},{1,5},{5... | collective-permute-start | bytes 1572872 | tf_op jit(solution)/shard_map/ppermute | solution.py:307
  57.7 8.8 %collective-permute-start.19 = (bf16[4,16,1024]{2,1,0:T(8,128)(2,1)S(1)}, bf16[4,16,1024]{2,1,0:T(8,128)(2,1)S(1)}, u32[]{:S(2)}, u32[]{:S(2)}) collective-permute-start(bf16[4,16,1024]{2,1,0:T(8,128)(2,1)S(1)} %get-tuple-element.34), channel_id=1, source_target_pairs={{0,3},{1,0},{2,1},{3,2},{4,7},{5,4},{6,5},{7,6},{8,11},{9,8},{10,9... | collective-permute-start | bytes 393224 | tf_op jit(solution)/shard_map/ppermute | solution.py:303
  61.5 11.9 %collective-permute-start.18 = (bf16[4,16,1024]{2,1,0:T(8,128)(2,1)S(1)}, bf16[4,16,1024]{2,1,0:T(8,128)(2,1)S(1)}, u32[]{:S(2)}, u32[]{:S(2)}) collective-permute-start(bf16[4,16,1024]{2,1,0:T(8,128)(2,1)S(1)} %get-tuple-element.35), channel_id=1, source_target_pairs={{0,2},{1,3},{2,0},{3,1},{4,6},{5,7},{6,4},{7,5},{8,10},{9,11},{10,... | collective-permute-start | bytes 393224 | tf_op jit(solution)/shard_map/ppermute | solution.py:303
  61.5 11.9 %collective-permute-start.17 = (bf16[4,16,1024]{2,1,0:T(8,128)(2,1)S(1)}, bf16[4,16,1024]{2,1,0:T(8,128)(2,1)S(1)}, u32[]{:S(2)}, u32[]{:S(2)}) collective-permute-start(bf16[4,16,1024]{2,1,0:T(8,128)(2,1)S(1)} %get-tuple-element.33), channel_id=1, source_target_pairs={{0,1},{1,2},{2,3},{3,0},{4,5},{5,6},{6,7},{7,4},{8,9},{9,10},{10,1... | collective-permute-start | bytes 393224 | tf_op jit(solution)/shard_map/ppermute | solution.py:303
  63.4 13.1 %collective-permute-start.12 = (bf16[4,16,2048]{2,1,0:T(8,128)(2,1)S(1)}, bf16[4,16,2048]{2,1,0:T(8,128)(2,1)S(1)}, u32[]{:S(2)}, u32[]{:S(2)}) collective-permute-start(bf16[4,16,2048]{2,1,0:T(8,128)(2,1)S(1)} %get-tuple-element.31), channel_id=1, source_target_pairs={{0,24},{4,28},{8,16},{12,20},{16,8},{20,12},{24,0},{28,4},{1,25},{... | collective-permute-start | bytes 786440 | tf_op jit(solution)/shard_map/ppermute | solution.py:307
  66.0 11.9 %collective-permute-start.11 = (bf16[4,16,2048]{2,1,0:T(8,128)(2,1)S(1)}, bf16[4,16,2048]{2,1,0:T(8,128)(2,1)S(1)}, u32[]{:S(2)}, u32[]{:S(2)}) collective-permute-start(bf16[4,16,2048]{2,1,0:T(8,128)(2,1)S(1)} %get-tuple-element.32), channel_id=1, source_target_pairs={{0,16},{4,20},{8,24},{12,28},{16,0},{20,4},{24,8},{28,12},{1,17},{... | collective-permute-start | bytes 786440 | tf_op jit(solution)/shard_map/ppermute | solution.py:307
  66.5 11.5 %collective-permute-start.10 = (bf16[4,16,2048]{2,1,0:T(8,128)(2,1)S(1)}, bf16[4,16,2048]{2,1,0:T(8,128)(2,1)S(1)}, u32[]{:S(2)}, u32[]{:S(2)}) collective-permute-start(bf16[4,16,2048]{2,1,0:T(8,128)(2,1)S(1)} %get-tuple-element.30), channel_id=1, source_target_pairs={{0,8},{4,12},{8,0},{12,4},{16,24},{20,28},{24,16},{28,20},{1,9},{5... | collective-permute-start | bytes 786440 | tf_op jit(solution)/shard_map/ppermute | solution.py:307
  73.5 8.5 %collective-permute-start.22 = (bf16[16,1024]{1,0:T(8,128)(2,1)S(1)}, bf16[16,1024]{1,0:T(8,128)(2,1)S(1)}, u32[]{:S(2)}, u32[]{:S(2)}) collective-permute-start(bf16[16,1024]{1,0:T(8,128)(2,1)S(1)} %get-tuple-element.40), channel_id=1, source_target_pairs={{0,24},{4,28},{8,16},{12,20},{16,8},{20,12},{24,0},{28,4},{1,25},{... | collective-permute-start | bytes 98312 | tf_op jit(solution)/shard_map/ppermute | solution.py:307
  76.0 6.0 %collective-permute-start.21 = (bf16[16,1024]{1,0:T(8,128)(2,1)S(1)}, bf16[16,1024]{1,0:T(8,128)(2,1)S(1)}, u32[]{:S(2)}, u32[]{:S(2)}) collective-permute-start(bf16[16,1024]{1,0:T(8,128)(2,1)S(1)} %get-tuple-element.41), channel_id=1, source_target_pairs={{0,16},{4,20},{8,24},{12,28},{16,0},{20,4},{24,8},{28,12},{1,17},{... | collective-permute-start | bytes 98312 | tf_op jit(solution)/shard_map/ppermute | solution.py:307
  76.6 5.5 %collective-permute-start.20 = (bf16[16,1024]{1,0:T(8,128)(2,1)S(1)}, bf16[16,1024]{1,0:T(8,128)(2,1)S(1)}, u32[]{:S(2)}, u32[]{:S(2)}) collective-permute-start(bf16[16,1024]{1,0:T(8,128)(2,1)S(1)} %get-tuple-element.39), channel_id=1, source_target_pairs={{0,8},{4,12},{8,0},{12,4},{16,24},{20,28},{24,16},{28,20},{1,9},{5... | collective-permute-start | bytes 98312 | tf_op jit(solution)/shard_map/ppermute | solution.py:307
  78.2 5.6 %collective-permute-start.15 = (bf16[16,2048]{1,0:T(8,128)(2,1)S(1)}, bf16[16,2048]{1,0:T(8,128)(2,1)S(1)}, u32[]{:S(2)}, u32[]{:S(2)}) collective-permute-start(bf16[16,2048]{1,0:T(8,128)(2,1)S(1)} %get-tuple-element.37), channel_id=1, source_target_pairs={{0,3},{1,0},{2,1},{3,2},{4,7},{5,4},{6,5},{7,6},{8,11},{9,8},{10,9... | collective-permute-start | bytes 196616 | tf_op jit(solution)/shard_map/ppermute | solution.py:303
  81.2 7.1 %collective-permute-start.14 = (bf16[16,2048]{1,0:T(8,128)(2,1)S(1)}, bf16[16,2048]{1,0:T(8,128)(2,1)S(1)}, u32[]{:S(2)}, u32[]{:S(2)}) collective-permute-start(bf16[16,2048]{1,0:T(8,128)(2,1)S(1)} %get-tuple-element.38), channel_id=1, source_target_pairs={{0,2},{1,3},{2,0},{3,1},{4,6},{5,7},{6,4},{7,5},{8,10},{9,11},{10,... | collective-permute-start | bytes 196616 | tf_op jit(solution)/shard_map/ppermute | solution.py:303
  82.0 6.2 %collective-permute-start.13 = (bf16[16,2048]{1,0:T(8,128)(2,1)S(1)}, bf16[16,2048]{1,0:T(8,128)(2,1)S(1)}, u32[]{:S(2)}, u32[]{:S(2)}) collective-permute-start(bf16[16,2048]{1,0:T(8,128)(2,1)S(1)} %get-tuple-element.36), channel_id=1, source_target_pairs={{0,1},{1,2},{2,3},{3,0},{4,5},{5,6},{6,7},{7,4},{8,9},{9,10},{10,1... | collective-permute-start | bytes 196616 | tf_op jit(solution)/shard_map/ppermute | solution.py:303

commit v5 on v3

--- a/solution.py
+++ b/solution.py
@@ -18,26 +18,11 @@
 F32 = jnp.float32
 I32 = jnp.int32
 VMEM = pl.BlockSpec(memory_space=pltpu.VMEM)
-SMEM = pl.BlockSpec(memory_space=pltpu.SMEM)
 ANY = pl.BlockSpec(memory_space=pl.ANY)
 
 
 def dot(a, b, a_dim, b_dim):
     return lax.dot_general(a, b, (((a_dim,), (b_dim,)), ((), ())), preferred_element_type=F32)
-
-
-def of_tokens(position, length_ref, values_of):
-    end = 0
-    found = None
-    for s in range(length_ref.shape[1]):
-        new = values_of(s, end)
-        if found is None:
-            found = [jnp.zeros_like(position) + value for value in new]
-        else:
-            inside = position >= end
-            found = [jnp.where(inside, value, old) for value, old in zip(new, found)]
-        end = end + length_ref[0, s]
-    return found
 
 
 def group_rows(rows_of_group, n_groups, width, seq, by_slot):
@@ -48,21 +33,9 @@
     return row
 
 
-def pack_kernel(n_out, tails, k_ref, v_ref, *out_refs):
-    part = k_ref.shape[1] // n_out
-    tok = k_ref.shape[0]
-    for h in range(n_out):
-        at = slice(h * part, (h + 1) * part)
-        for i, rows in enumerate(tails):
-            out_ref = out_refs[h * len(tails) + i]
-            out_ref[:, :part] = k_ref[tok - rows :, at]
-            out_ref[:, part:] = v_ref[tok - rows :, at]
-
-
 def attention_kernel(
     n_halo, by_slot, first_kv, n_kv,
-    place_ref, length_ref, adapter_ref, owner_ref,
-    q_hbm, g_hbm, k_ref, v_ref, *refs,
+    facts_ref, q_hbm, g_hbm, own_ref, *refs,
 ):
     halo_refs = refs[:n_halo]
     n_before = 2 if first_kv else 0
@@ -72,7 +45,7 @@
     tok = q_ref.shape[0]
     kv_width = n_kv * HEAD_SIZE
     key_rows = v_all.shape[0]
-    seq, head = place_ref[0], place_ref[1]
+    seq, head = lax.axis_index("seq"), lax.axis_index("head")
     per_kv = GROUP * HEAD_SIZE
 
     def fetch(kv):
@@ -88,11 +61,7 @@
             copy.start()
 
     position = head * tok + lax.broadcasted_iota(I32, (1, tok), 1)
-    seg_start, group = of_tokens(
-        position,
-        length_ref,
-        lambda s, start: (start, owner_ref[adapter_ref[0, s]] if by_slot else s),
-    )
+    seg_start = facts_ref[0:1, :]
     key_position = (
         head * tok - (key_rows - tok) + lax.broadcasted_iota(I32, (key_rows, tok), 0)
     )
@@ -102,14 +71,11 @@
     for kv in range(n_kv):
         start = 0
         at = slice(kv * HEAD_SIZE, (kv + 1) * HEAD_SIZE)
-        for halo_ref in halo_refs:
+        for halo_ref in (*halo_refs, own_ref):
             rows = halo_ref.shape[0]
             k_all[kv, start : start + rows, :HEAD_SIZE] = halo_ref[:, at]
             v_all[start : start + rows, at] = halo_ref[:, kv_width + at.start : kv_width + at.stop]
             start += rows
-        own = slice((first_kv + kv) * HEAD_SIZE, (first_kv + kv + 1) * HEAD_SIZE)
-        k_all[kv, start:, :HEAD_SIZE] = k_ref[:, own]
-        v_all[start:, at] = v_ref[:, own]
         k_all[kv, :, HEAD_SIZE:] = bias
         k_turned[at, :] = k_all[kv, :, :HEAD_SIZE].T
 
@@ -151,7 +117,7 @@
     rank = act_ref.shape[0]
     n_quarters, per, _, part = up_refs[0].shape
     n_groups = per * len(up_refs)
-    own = group_rows(rank, n_groups, tok, seq, by_slot) == group
+    own = group_rows(rank, n_groups, tok, seq, by_slot) == facts_ref[2:3, :]
     act = jnp.concatenate([act_ref[...].astype(F32)] * n_groups, axis=0)
     act_cols = jnp.where(own, act, 0.0).astype(BF16)
     n_before = dq_before.shape[0] // part
@@ -170,32 +136,12 @@
             write(i - n_before, dq_turned, i)
 
 
-def down_kernel(
-    by_slot, n_w, place_ref, length_ref, adapter_ref, owner_ref, x_hbm, *refs
-):
-    w_refs, refs = refs[:n_w], refs[n_w:]
-    dq_a, dq_b, *out_refs, x_ref, x_sem = refs
-    tok = x_ref.shape[0]
-    seq, head = place_ref[0], place_ref[1]
+def rank_kernel(by_slot, n_w, facts_ref, *refs):
+    w_refs, (dq_a, dq_b, out_ref) = refs[:n_w], refs[n_w:]
+    tok = dq_a.shape[1]
+    seq, head = lax.axis_index("seq"), lax.axis_index("head")
     n_adapters, n_quarters, rank, part = w_refs[0].shape
-    per, _, _, x_part = out_refs[0].shape
-    n_groups = per * len(out_refs)
-
-    def fetch(j):
-        quarter = lax.rem(head + j, n_quarters) if by_slot else j
-        at = pl.ds(pl.multiple_of(quarter * x_part, x_part), x_part)
-        to = pl.ds(j * x_part, x_part)
-        return pltpu.make_async_copy(x_hbm.at[:, at], x_ref.at[:, to], x_sem.at[j])
-
-    for j in range(n_quarters):
-        fetch(j).start()
-
-    position = head * tok + lax.broadcasted_iota(I32, (1, tok), 1)
-    adapter, group = of_tokens(
-        position,
-        length_ref,
-        lambda s, start: (adapter_ref[0, s], owner_ref[adapter_ref[0, s]] if by_slot else s),
-    )
+    adapter = facts_ref[1:2, :]
     total = jnp.zeros((rank, tok), F32)
     n_a = dq_a.shape[0] // part
     for c, w_ref in enumerate(w_refs):
@@ -209,19 +155,41 @@
         for m in range(n_adapters):
             a = (2 * m + c) ^ seq if by_slot else m
             total = total + jnp.where(adapter == a, rows[m * rank : (m + 1) * rank, :], 0.0)
-
-    own = group_rows(rank, n_groups, tok, seq, by_slot) == group
-    low = jnp.concatenate([total.astype(BF16).astype(F32)] * n_groups, axis=0)
+    out_ref[...] = total.astype(BF16)
+
+
+def down_kernel(by_slot, facts_ref, x_ref, rank_ref, *out_refs):
+    rank, tok = rank_ref.shape
+    seq, head = lax.axis_index("seq"), lax.axis_index("head")
+    per, n_quarters, _, x_part = out_refs[0].shape
+    n_groups = per * len(out_refs)
+    own = group_rows(rank, n_groups, tok, seq, by_slot) == facts_ref[2:3, :]
+    low = jnp.concatenate([rank_ref[...].astype(F32)] * n_groups, axis=0)
     cols = jnp.where(own, low, 0.0).astype(BF16)
     step = min(512, x_part)
     for j in range(n_quarters):
-        fetch(j).wait()
+        quarter = lax.rem(head + j, n_quarters) if by_slot else j
         for start in range(0, x_part, step):
-            down = dot(cols, x_ref[:, j * x_part + start : j * x_part + start + step], 1, 0)
-            down = down.astype(BF16)
+            at = pl.ds(pl.multiple_of(quarter * x_part + start, step), step)
+            down = dot(cols, x_ref[:, at], 1, 0).astype(BF16)
             for n in range(n_groups):
                 piece = down[n * rank : (n + 1) * rank, :]
                 out_refs[n // per][n % per, j, :, start : start + step] = piece
+
+
+def token_facts(tok, lengths, adapters, owner, by_slot):
+    n_seg = lengths.shape[0]
+    order = jnp.arange(n_seg, dtype=I32)
+    starts = jnp.sum(jnp.where(order[None, :] < order[:, None], lengths[None, :], 0), axis=1)
+    if by_slot:
+        hits = adapters[:, None] == jnp.arange(owner.shape[0], dtype=I32)[None, :]
+        groups = jnp.sum(jnp.where(hits, owner[None, :], 0), axis=1)
+    else:
+        groups = order
+    position = lax.axis_index("head") * tok + jnp.arange(tok, dtype=I32)
+    inside = (position >= starts[:, None]) & (position < (starts + lengths)[:, None])
+    told = jnp.stack([starts, adapters, groups] + [jnp.zeros_like(starts)] * 5)
+    return jnp.sum(jnp.where(inside[None], told[:, :, None], 0), axis=1)
 
 
 def shifted(x, n_head, j):
@@ -244,7 +212,7 @@
     n_adapters = owner.shape[0]
     n_seg = segment_length.shape[1]
     by_slot = n_adapters == n_seq == 8
-    place = jnp.stack([lax.axis_index("seq"), lax.axis_index("head")]).astype(I32)
+    facts = token_facts(tok, segment_length[0], segment_adapter[0], owner, by_slot)
 
     reach = []
     while sum(reach) < pack * 3 // 8:
@@ -254,13 +222,12 @@
     halves = 2
     n_kv = KEY_VALUE_HEADS // halves
     kv_width = n_kv * HEAD_SIZE
-    packed = pl.pallas_call(
-        functools.partial(pack_kernel, halves, tails),
-        out_shape=[jax.ShapeDtypeStruct((rows, 2 * kv_width), BF16) for rows in tails] * halves,
-        in_specs=[VMEM] * 2,
-        out_specs=[VMEM] * (halves * len(tails)),
-        name="pack_halo",
-    )(keys, values)
+    def pack_of(h):
+        at = slice(h * kv_width, (h + 1) * kv_width)
+        return jnp.concatenate([keys[:, at], values[:, at]], axis=1)
+
+    own = [pack_of(h) for h in range(halves)]
+    packed = [own[h][tok - rows :] for h in range(halves) for rows in tails]
 
     def halo_of(h):
         got = []
@@ -291,7 +258,7 @@
         return pl.pallas_call(
             functools.partial(attention_kernel, len(halos), by_slot, h * n_kv, n_kv),
             out_shape=[jax.ShapeDtypeStruct((half, tok), BF16)] + up_shapes,
-            in_specs=[SMEM] * 4 + [ANY] * 2 + [VMEM] * (2 + len(halos) + len(before)),
+            in_specs=[VMEM] + [ANY] * 2 + [VMEM] * (1 + len(halos) + len(before)),
             out_specs=[VMEM] * (1 + len(up_shapes)),
             scratch_shapes=[
                 pltpu.VMEM((tok, half), BF16),
@@ -309,10 +276,7 @@
                 transcendentals=tok * key_rows * QUERY_HEADS // halves,
             ),
             name="attention_%d" % h,
-        )(
-            place, segment_length, segment_adapter, owner, queries, output_gradient, keys, values,
-            *halos, *before,
-        )
+        )(facts, queries, output_gradient, own[h], *halos, *before)
 
     (dq_a,) = attention(0, halo_a, [], [])
     if by_slot:
@@ -321,27 +285,36 @@
     up_shape = jax.ShapeDtypeStruct((n_head, n_groups // n_out, rank, part), BF16)
     dq_b, *up = attention(1, halo_b, [adapter_activation.T, dq_a], [up_shape] * n_out)
 
+    if by_slot:
+        up, up_weight = lax.optimization_barrier((up, up_weight))
+    rank_low = pl.pallas_call(
+        functools.partial(rank_kernel, by_slot, len(up_weight)),
+        out_shape=jax.ShapeDtypeStruct((rank, tok), BF16),
+        in_specs=[VMEM] * (3 + len(up_weight)),
+        out_specs=VMEM,
+        compiler_params=params,
+        name="rank_gradient",
+    )(facts, *up_weight, dq_a, dq_b)
+    if by_slot:
+        rank_low, up = lax.optimization_barrier((rank_low, over_cores(up, n_seq)))
+
     down_shape = jax.ShapeDtypeStruct((n_groups // n_out, n_head, rank, x_part), BF16)
     down = pl.pallas_call(
-        functools.partial(down_kernel, by_slot, len(up_weight)),
+        functools.partial(down_kernel, by_slot),
         out_shape=[down_shape] * n_out,
-        in_specs=[SMEM] * 4 + [ANY] + [VMEM] * (2 + len(up_weight)),
+        in_specs=[VMEM] * 3,
         out_specs=[VMEM] * n_out,
-        scratch_shapes=[
-            pltpu.VMEM(inputs.shape, BF16),
-            pltpu.SemaphoreType.DMA((n_head,)),
-        ],
         compiler_params=params,
         cost_estimate=pl.CostEstimate(
-            flops=2 * n_groups * rank * tok * (width + inputs.shape[1]),
+            flops=2 * n_groups * rank * tok * inputs.shape[1],
             bytes_accessed=4 * tok * inputs.shape[1] * 2,
             transcendentals=0,
         ),
         name="down_parts",
-    )(place, segment_length, segment_adapter, owner, inputs, *up_weight, dq_a, dq_b)
-
-    if by_slot:
-        up = over_chips(over_z(over_cores(up, n_seq), n_head).astype(BF16), n_seq)
+    )(facts, inputs, rank_low)
+
+    if by_slot:
+        up = over_chips(over_z(up, n_head).astype(BF16), n_seq)
         down = over_z(over_chips(over_cores(down, n_seq), n_seq).astype(BF16), n_head)
     else:
         up = lax.all_to_all(up[0], "head", split_axis=0, concat_axis=0, tiled=True)

time: 72.6 us -> 71.5 us (0.985)
  Pallas kernels: 12.6 us -> 8.54 us
  local copies, waits for them, and re-layouts: 6.34 us -> 2.97 us
  other arithmetic: 3.05 us -> 5.49 us
  waiting for transfers between devices: 10.2 us -> 12.6 us
  starting transfers between devices: 39.2 us -> 40.5 us
    ppermute x9, waiting for transfers between devices: 3.6 us -> 9.09 us  [shifted(): lax.ppermute(x, 'head', [(i, (i + j) % n_head) for i in range(n_head)])]
    unnamed x18 -> x8, local copies, waits for them, and re-layouts: 6.23 us -> 1.23 us
    ppermute x12, waiting for transfers between devices: 6.55 us -> 3.5 us  [partnered(): return lax.ppermute(x, 'seq', [(i, i ^ bits) for i in range(n_seq)])]
    ppermute x9, starting transfers between devices: 17.6 us -> 20.6 us  [shifted(): lax.ppermute(x, 'head', [(i, (i + j) % n_head) for i in range(n_head)])]
    pallas_call x2, Pallas kernels: 4.1 us -> 1.16 us  [the longest x1 0.71 us: on_device(): pl.pallas_call(functools.partial(down_kernel, by_slot), out_shape=[down_s...]
    reduce_sum x0 -> x3, other arithmetic: none -> 1.71 us  [the longest x1 0.85 us: token_facts(): groups = jnp.sum(jnp.where(hits, owner[None, :], 0), axis=1)]
    ppermute x12, starting transfers between devices: 13.5 us -> 12.3 us  [partnered(): return lax.ppermute(x, 'seq', [(i, i ^ bits) for i in range(n_seq)])]
    pallas_call x2, Pallas kernels: 8.5 us -> 7.38 us  [attention(): pl.pallas_call(functools.partial(attention_kernel, len(halos), by_slot, h...]
  transfers between devices with their start and end apart: 25 -> 25, of which waited for: 5 -> 7; matrix products, arithmetic and copies ran while one was open for 3% -> 9% of each run, Pallas kernels for 14% -> 11%
where the time goes in v5:
time: 71.5 us; the launch traced here: 71.1 us
  starting transfers between devices  40.5 us (57%)
  waiting for transfers between devices  12.6 us (18%)
  Pallas kernels  8.54 us (12%)
  other arithmetic  5.49 us (8%)
  local copies, waits for them, and re-layouts  2.97 us (4%)
  between operations  0.99 us (1%)
    ppermute x9, starting transfers between devices, shifted(): lax.ppermute(x, 'head', [(i, (i + j) % n_head) for i in range(n_head)])  20.6 us
    ppermute x12, starting transfers between devices, partnered(): return lax.ppermute(x, 'seq', [(i, i ^ bits) for i in range(n_seq)])  12.3 us
    ppermute x9, waiting for transfers between devices, shifted(): lax.ppermute(x, 'head', [(i, (i + j) % n_head) for i in range(n_head)])  9.09 us
    ppermute x4, starting transfers between devices, halo_of(): lax.ppermute(packed[h * len(tails) + tails.index(rows)], 'head', shift)  7.6 us
    pallas_call x2, Pallas kernels, attention(): pl.pallas_call(functools.partial(attention_kernel, len(halos), by_slot, h...  7.38 us
    ppermute x12, waiting for transfers between devices, partnered(): return lax.ppermute(x, 'seq', [(i, i ^ bits) for i in range(n_seq)])  3.5 us
  transfers between devices with their start and end apart: 25, of which 7 were waited for; matrix products, arithmetic and copies ran while one was open for 9% of the time, Pallas kernels for 11%

profile of v5, /device:TPU:0, one launch (start us, length us, event | category | flops | bytes accessed | tf_op | source)
XLA Modules:
  0.0 71.1 jit_solution(6675565905245971729)
XLA Ops:
  0.6 4.1 %collective-permute-start.5 = (bf16[1,16,1024]{2,1,0:T(8,128)(2,1)}, bf16[1,16,1024]{2,1,0:T(8,128)(2,1)S(1)}, u32[]{:S(2)}, u32[]{:S(2)}) collective-permute-start(bf16[1,16,1024]{2,1,0:T(8,128)(2,1)} %param.16), channel_id=1, source_target_pairs={{0,2},{1,3},{2,0},{3,1},{4,6},{5,7},{6,4},{7,5},{8,10},{9,11},{10,... | collective-permute-start | bytes 98312 | tf_op jit(solution)/shard_map/ppermute | solution.py:196
  4.7 1.6 %collective-permute-start.4 = (bf16[1,16,1024]{2,1,0:T(8,128)(2,1)}, bf16[1,16,1024]{2,1,0:T(8,128)(2,1)S(1)}, u32[]{:S(2)}, u32[]{:S(2)}) collective-permute-start(bf16[1,16,1024]{2,1,0:T(8,128)(2,1)} %param.16), channel_id=1, source_target_pairs={{0,1},{1,2},{2,3},{3,0},{4,5},{5,6},{6,7},{7,4},{8,9},{9,10},{10,1... | collective-permute-start | bytes 98312 | tf_op jit(solution)/shard_map/ppermute | solution.py:196
  6.3 2.2 %collective-permute-start.6 = (bf16[1,16,1024]{2,1,0:T(8,128)(2,1)}, bf16[1,16,1024]{2,1,0:T(8,128)(2,1)S(1)}, u32[]{:S(2)}, u32[]{:S(2)}) collective-permute-start(bf16[1,16,1024]{2,1,0:T(8,128)(2,1)} %param.16), channel_id=1, source_target_pairs={{0,3},{1,0},{2,1},{3,2},{4,7},{5,4},{6,5},{7,6},{8,11},{9,8},{10,9... | collective-permute-start | bytes 98312 | tf_op jit(solution)/shard_map/ppermute | solution.py:196
  8.6 1.0 %fusion.16 = (bf16[128,256]{1,0:T(8,128)(2,1)S(1)}, bf16[128,256]{1,0:T(8,128)(2,1)S(1)}, bf16[128,256]{1,0:T(8,128)(2,1)S(1)}, bf16[128,256]{1,0:T(8,128)(2,1)S(1)}) fusion(bf16[128,512]{1,0:T(8,128)(2,1)} %param.11, bf16[128,512]{1,0:T(8,128)(2,1)} %param.12), kind=kLoop, calls=%fused_computation.53 | loop fusion | bytes 524288 | tf_op jit(solution)/shard_map/slice | solution.py:227
  9.5 1.3 %collective-permute-start = (bf16[64,512]{1,0:T(8,128)(2,1)S(1)}, bf16[64,512]{1,0:T(8,128)(2,1)S(1)}, u32[]{:S(2)}, u32[]{:S(2)}) collective-permute-start(bf16[64,512]{1,0:T(8,128)(2,1)S(1)} %fusion.11), channel_id=1, source_target_pairs={{0,2},{1,3},{4,6},{5,7},{8,10},{9,11},{12,14},{13,15},{16,18},{17,... | collective-permute-start | bytes 196616 | tf_op jit(solution)/shard_map/ppermute | solution.py:236
  10.9 3.1 %collective-permute-start.3 = (bf16[128,512]{1,0:T(8,128)(2,1)S(1)}, bf16[128,512]{1,0:T(8,128)(2,1)S(1)}, u32[]{:S(2)}, u32[]{:S(2)}) collective-permute-start(bf16[128,512]{1,0:T(8,128)(2,1)S(1)} %pad_maximum_fusion.2.own_ref), channel_id=1, source_target_pairs={{0,1},{1,2},{2,3},{4,5},{5,6},{6,7},{8,9},{9,10},{10,11},{12,13},{... | collective-permute-start | bytes 393224 | tf_op jit(solution)/shard_map/ppermute | solution.py:236
  14.0 0.8 %select_reduce_fusion.2 = s32[8]{0:T(128)S(1)} fusion(s32[8]{0:T(128)} %bitcast.60), kind=kLoop, calls=%fused_computation.48 | loop fusion | flops 184 | bytes 64 | tf_op jit(solution)/shard_map/reduce_sum | solution.py:183
  14.8 0.7 bitcast_add_fusion
  15.4 0.1 compare_and_fusion
  15.5 0.9 %select_reduce_fusion.1 = s32[8]{0:T(128)S(1)} fusion(s32[8]{0:T(128)} %param.19, s32[8]{0:T(128)} %bitcast.58), kind=kLoop, calls=%fused_computation.46 | loop fusion | flops 184 | bytes 96 | tf_op jit(solution)/shard_map/reduce_sum | solution.py:186
  16.4 0.7 stack.15
  17.1 1.3 %collective-permute-start.2 = (bf16[64,512]{1,0:T(8,128)(2,1)S(1)}, bf16[64,512]{1,0:T(8,128)(2,1)S(1)}, u32[]{:S(2)}, u32[]{:S(2)}) collective-permute-start(bf16[64,512]{1,0:T(8,128)(2,1)S(1)} %fusion.10), channel_id=1, source_target_pairs={{0,2},{1,3},{4,6},{5,7},{8,10},{9,11},{12,14},{13,15},{16,18},{17,... | collective-permute-start | bytes 196616 | tf_op jit(solution)/shard_map/ppermute | solution.py:236
  18.4 1.9 %collective-permute-start.1 = (bf16[128,512]{1,0:T(8,128)(2,1)S(1)}, bf16[128,512]{1,0:T(8,128)(2,1)S(1)}, u32[]{:S(2)}, u32[]{:S(2)}) collective-permute-start(bf16[128,512]{1,0:T(8,128)(2,1)S(1)} %pad_maximum_fusion.1.own_ref), channel_id=1, source_target_pairs={{0,1},{1,2},{2,3},{4,5},{5,6},{6,7},{8,9},{9,10},{10,11},{12,13},{... | collective-permute-start | bytes 393224 | tf_op jit(solution)/shard_map/ppermute | solution.py:236
  20.3 0.8 %maximum_bitcast_fusion = bf16[1,4,16,1024]{3,2,1,0:T(8,128)(2,1)S(1)} fusion(bf16[1,16,1024]{2,1,0:T(8,128)(2,1)S(1)} %collective-permute-done.6, bf16[1,16,1024]{2,1,0:T(8,128)(2,1)S(1)} %collective-permute-done.5, bf16[1,16,1024]{2,1,0:T(8,128)(2,1)S(1)} %collective-permute-done.4, bf16[1,16,1024]{2,1,0:T(8,128)(2,1)} %param.16), kind=kLoop, calls=%fused_computation.21 | loop fusion | flops 196608 | bytes 262144 | tf_op jit(solution)/shard_map/broadcast_in_dim | solution.py:242
  21.1 2.5 %collective-permute-start.9 = (bf16[1,4,16,1024]{3,2,1,0:T(8,128)(2,1)S(1)}, bf16[1,4,16,1024]{3,2,1,0:T(8,128)(2,1)S(1)}, u32[]{:S(2)}, u32[]{:S(2)}) collective-permute-start(bf16[1,4,16,1024]{3,2,1,0:T(8,128)(2,1)S(1)} %maximum_bitcast_fusion), channel_id=1, source_target_pairs={{0,24},{4,28},{8,16},{12,20},{16,8},{20,12},{24,0},{28,4},{1,25},{... | collective-permute-start | bytes 393224 | tf_op jit(solution)/shard_map/ppermute | solution.py:200
  23.6 0.5 collective-permute-start.8
  24.2 0.5 collective-permute-start.7
  24.7 0.1 select_reduce_fusion.facts_ref
  24.8 1.2 %copy-done.1 = bf16[128,4096]{1,0:T(8,128)(2,1)S(1)} copy-done((bf16[128,4096]{1,0:T(8,128)(2,1)S(1)}, bf16[128,4096]{1,0:T(8,128)(2,1)}, u32[]{:S(2)}) %copy-start.1) | copy-done | bytes 1048600
  26.0 3.5 %attention_0.1.refs_3_.refs_2_ = bf16[2048,128]{1,0:T(8,128)(2,1)S(1)} custom-call(s32[8,128]{1,0:T(8,128)S(1)} %select_reduce_fusion.facts_ref, bf16[128,4096]{1,0:T(8,128)(2,1)S(1)} %copy-done, bf16[128,4096]{1,0:T(8,128)(2,1)S(1)} %copy-done.1, bf16[128,512]{1,0:T(8,128)(2,1)S(1)} %pad_maximum_fusion.2.own_ref, ...), custom_call_target="tpu_custom_call" | custom-call | flops 503316480 | bytes 2097152 | tf_op jit(solution)/shard_map/attention_0/pallas_call | solution.py:258
  29.7 3.9 %attention_1.1 = (bf16[2048,128]{1,0:T(8,128)(2,1)S(1)}, bf16[4,4,16,1024]{3,2,1,0:T(8,128)(2,1)S(1)}, bf16[4,4,16,1024]{3,2,1,0:T(8,128)(2,1)S(1)}) custom-call(s32[8,128]{1,0:T(8,128)S(1)} %select_reduce_fusion.facts_ref, bf16[128,4096]{1,0:T(8,128)(2,1)S(1)} %copy-done, bf16[128,4096]{1,0:T(8,128)(2,1)S(1)} %copy-done.1, ...), custom_call_target="tpu_custom_call" | custom-call | flops 503316480 | bytes 2097152 | tf_op jit(solution)/shard_map/attention_1/pallas_call | solution.py:258
  33.6 0.5 collective-permute-start.11
  34.2 0.5 rank_gradient.1.rank_ref
  34.6 1.1 %collective-permute-done.11 = bf16[4,4,16,1024]{3,2,1,0:T(8,128)(2,1)S(1)} collective-permute-done((bf16[4,4,16,1024]{3,2,1,0:T(8,128)(2,1)S(1)}, bf16[4,4,16,1024]{3,2,1,0:T(8,128)(2,1)S(1)}, u32[]{:S(2)}, u32[]{:S(2)}) %collective-permute-start.11) | collective-permute-done | bytes 524320 | tf_op jit(solution)/shard_map/ppermute | solution.py:200
  35.7 0.2 add_convert_fusion.1
  35.9 0.7 down_parts.1
  36.6 0.4 collective-permute-start.12
  37.2 3.8 %collective-permute-start.21 = (bf16[4,16,1024]{2,1,0:T(8,128)(2,1)S(1)}, bf16[4,16,1024]{2,1,0:T(8,128)(2,1)S(1)}, u32[]{:S(2)}, u32[]{:S(2)}) collective-permute-start(bf16[4,16,1024]{2,1,0:T(8,128)(2,1)S(1)} %get-tuple-element.42), channel_id=1, source_target_pairs={{0,3},{1,0},{2,1},{3,2},{4,7},{5,4},{6,5},{7,6},{8,11},{9,8},{10,9... | collective-permute-start | bytes 393224 | tf_op jit(solution)/shard_map/ppermute | solution.py:196
  41.0 1.2 %collective-permute-start.20 = (bf16[4,16,1024]{2,1,0:T(8,128)(2,1)S(1)}, bf16[4,16,1024]{2,1,0:T(8,128)(2,1)S(1)}, u32[]{:S(2)}, u32[]{:S(2)}) collective-permute-start(bf16[4,16,1024]{2,1,0:T(8,128)(2,1)S(1)} %get-tuple-element.43), channel_id=1, source_target_pairs={{0,2},{1,3},{2,0},{3,1},{4,6},{5,7},{6,4},{7,5},{8,10},{9,11},{10,... | collective-permute-start | bytes 393224 | tf_op jit(solution)/shard_map/ppermute | solution.py:196
  42.2 0.4 add_convert_fusion
  42.7 1.6 %collective-permute-start.13 = (bf16[4,16,2048]{2,1,0:T(8,128)(2,1)S(1)}, bf16[4,16,2048]{2,1,0:T(8,128)(2,1)S(1)}, u32[]{:S(2)}, u32[]{:S(2)}) collective-permute-start(bf16[4,16,2048]{2,1,0:T(8,128)(2,1)S(1)} %get-tuple-element.38), channel_id=1, source_target_pairs={{0,8},{4,12},{8,0},{12,4},{16,24},{20,28},{24,16},{28,20},{1,9},{5... | collective-permute-start | bytes 786440 | tf_op jit(solution)/shard_map/ppermute | solution.py:200
  44.3 1.5 %collective-permute-start.15 = (bf16[4,16,2048]{2,1,0:T(8,128)(2,1)S(1)}, bf16[4,16,2048]{2,1,0:T(8,128)(2,1)S(1)}, u32[]{:S(2)}, u32[]{:S(2)}) collective-permute-start(bf16[4,16,2048]{2,1,0:T(8,128)(2,1)S(1)} %get-tuple-element.39), channel_id=1, source_target_pairs={{0,24},{4,28},{8,16},{12,20},{16,8},{20,12},{24,0},{28,4},{1,25},{... | collective-permute-start | bytes 786440 | tf_op jit(solution)/shard_map/ppermute | solution.py:200
  45.8 1.1 %collective-permute-start.14 = (bf16[4,16,2048]{2,1,0:T(8,128)(2,1)S(1)}, bf16[4,16,2048]{2,1,0:T(8,128)(2,1)S(1)}, u32[]{:S(2)}, u32[]{:S(2)}) collective-permute-start(bf16[4,16,2048]{2,1,0:T(8,128)(2,1)S(1)} %get-tuple-element.40), channel_id=1, source_target_pairs={{0,16},{4,20},{8,24},{12,28},{16,0},{20,4},{24,8},{28,12},{1,17},{... | collective-permute-start | bytes 786440 | tf_op jit(solution)/shard_map/ppermute | solution.py:200
  46.8 0.3 collective-permute-done.21
  47.1 5.8 %collective-permute-done.20 = bf16[4,16,1024]{2,1,0:T(8,128)(2,1)S(1)} collective-permute-done((bf16[4,16,1024]{2,1,0:T(8,128)(2,1)S(1)}, bf16[4,16,1024]{2,1,0:T(8,128)(2,1)S(1)}, u32[]{:S(2)}, u32[]{:S(2)}) %collective-permute-start.20) | collective-permute-done | bytes 131104 | tf_op jit(solution)/shard_map/ppermute | solution.py:196
  52.9 0.1 fusion.5
  53.0 1.6 %collective-permute-start.22 = (bf16[16,1024]{1,0:T(8,128)(2,1)S(1)}, bf16[16,1024]{1,0:T(8,128)(2,1)S(1)}, u32[]{:S(2)}, u32[]{:S(2)}) collective-permute-start(bf16[16,1024]{1,0:T(8,128)(2,1)S(1)} %get-tuple-element.47), channel_id=1, source_target_pairs={{0,8},{4,12},{8,0},{12,4},{16,24},{20,28},{24,16},{28,20},{1,9},{5... | collective-permute-start | bytes 98312 | tf_op jit(solution)/shard_map/ppermute | solution.py:200
  54.6 1.5 %collective-permute-start.24 = (bf16[16,1024]{1,0:T(8,128)(2,1)S(1)}, bf16[16,1024]{1,0:T(8,128)(2,1)S(1)}, u32[]{:S(2)}, u32[]{:S(2)}) collective-permute-start(bf16[16,1024]{1,0:T(8,128)(2,1)S(1)} %get-tuple-element.48), channel_id=1, source_target_pairs={{0,24},{4,28},{8,16},{12,20},{16,8},{20,12},{24,0},{28,4},{1,25},{... | collective-permute-start | bytes 98312 | tf_op jit(solution)/shard_map/ppermute | solution.py:200
  56.1 0.5 collective-permute-start.23
  56.6 0.5 collective-permute-done.15
  57.1 1.9 %collective-permute-done.14 = bf16[4,16,2048]{2,1,0:T(8,128)(2,1)S(1)} collective-permute-done((bf16[4,16,2048]{2,1,0:T(8,128)(2,1)S(1)}, bf16[4,16,2048]{2,1,0:T(8,128)(2,1)S(1)}, u32[]{:S(2)}, u32[]{:S(2)}) %collective-permute-start.14) | collective-permute-done | bytes 262176 | tf_op jit(solution)/shard_map/ppermute | solution.py:200
  59.0 0.1 fusion.2
  59.1 4.0 %collective-permute-start.16 = (bf16[16,2048]{1,0:T(8,128)(2,1)S(1)}, bf16[16,2048]{1,0:T(8,128)(2,1)S(1)}, u32[]{:S(2)}, u32[]{:S(2)}) collective-permute-start(bf16[16,2048]{1,0:T(8,128)(2,1)S(1)} %get-tuple-element.44), channel_id=1, source_target_pairs={{0,1},{1,2},{2,3},{3,0},{4,5},{5,6},{6,7},{7,4},{8,9},{9,10},{10,1... | collective-permute-start | bytes 196616 | tf_op jit(solution)/shard_map/ppermute | solution.py:196
  63.1 3.6 %collective-permute-start.17 = (bf16[16,2048]{1,0:T(8,128)(2,1)S(1)}, bf16[16,2048]{1,0:T(8,128)(2,1)S(1)}, u32[]{:S(2)}, u32[]{:S(2)}) collective-permute-start(bf16[16,2048]{1,0:T(8,128)(2,1)S(1)} %get-tuple-element.46), channel_id=1, source_target_pairs={{0,2},{1,3},{2,0},{3,1},{4,6},{5,7},{6,4},{7,5},{8,10},{9,11},{10,... | collective-permute-start | bytes 196616 | tf_op jit(solution)/shard_map/ppermute | solution.py:196
  66.8 0.7 fusion.15
  67.4 0.2 collective-permute-done.18
  67.7 2.7 %collective-permute-done.17 = bf16[16,2048]{1,0:T(8,128)(2,1)S(1)} collective-permute-done((bf16[16,2048]{1,0:T(8,128)(2,1)S(1)}, bf16[16,2048]{1,0:T(8,128)(2,1)S(1)}, u32[]{:S(2)}, u32[]{:S(2)}) %collective-permute-start.17) | collective-permute-done | bytes 65568 | tf_op jit(solution)/shard_map/ppermute | solution.py:196
  70.4 0.7 fusion.9
  (40 shorter events, 0.4 us)
Async XLA Ops:
  0.6 24.1 %copy-start = (bf16[128,4096]{1,0:T(8,128)(2,1)S(1)}, bf16[128,4096]{1,0:T(8,128)(2,1)}, u32[]{:S(2)}) copy-start(bf16[128,4096]{1,0:T(8,128)(2,1)} %q_hbm.3) | copy-start | bytes 3145732
  0.6 16.4 %collective-permute-start.5 = (bf16[1,16,1024]{2,1,0:T(8,128)(2,1)}, bf16[1,16,1024]{2,1,0:T(8,128)(2,1)S(1)}, u32[]{:S(2)}, u32[]{:S(2)}) collective-permute-start(bf16[1,16,1024]{2,1,0:T(8,128)(2,1)} %param.16), channel_id=1, source_target_pairs={{0,2},{1,3},{2,0},{3,1},{4,6},{5,7},{6,4},{7,5},{8,10},{9,11},{10,... | collective-permute-start | bytes 98312 | tf_op jit(solution)/shard_map/ppermute | solution.py:196
  4.7 13.6 %collective-permute-start.4 = (bf16[1,16,1024]{2,1,0:T(8,128)(2,1)}, bf16[1,16,1024]{2,1,0:T(8,128)(2,1)S(1)}, u32[]{:S(2)}, u32[]{:S(2)}) collective-permute-start(bf16[1,16,1024]{2,1,0:T(8,128)(2,1)} %param.16), channel_id=1, source_target_pairs={{0,1},{1,2},{2,3},{3,0},{4,5},{5,6},{6,7},{7,4},{8,9},{9,10},{10,1... | collective-permute-start | bytes 98312 | tf_op jit(solution)/shard_map/ppermute | solution.py:196
  6.3 14.0 %collective-permute-start.6 = (bf16[1,16,1024]{2,1,0:T(8,128)(2,1)}, bf16[1,16,1024]{2,1,0:T(8,128)(2,1)S(1)}, u32[]{:S(2)}, u32[]{:S(2)}) collective-permute-start(bf16[1,16,1024]{2,1,0:T(8,128)(2,1)} %param.16), channel_id=1, source_target_pairs={{0,3},{1,0},{2,1},{3,2},{4,7},{5,4},{6,5},{7,6},{8,11},{9,8},{10,9... | collective-permute-start | bytes 98312 | tf_op jit(solution)/shard_map/ppermute | solution.py:196
  9.5 20.1 %collective-permute-start = (bf16[64,512]{1,0:T(8,128)(2,1)S(1)}, bf16[64,512]{1,0:T(8,128)(2,1)S(1)}, u32[]{:S(2)}, u32[]{:S(2)}) collective-permute-start(bf16[64,512]{1,0:T(8,128)(2,1)S(1)} %fusion.11), channel_id=1, source_target_pairs={{0,2},{1,3},{4,6},{5,7},{8,10},{9,11},{12,14},{13,15},{16,18},{17,... | collective-permute-start | bytes 196616 | tf_op jit(solution)/shard_map/ppermute | solution.py:236
  10.9 10.3 %collective-permute-start.3 = (bf16[128,512]{1,0:T(8,128)(2,1)S(1)}, bf16[128,512]{1,0:T(8,128)(2,1)S(1)}, u32[]{:S(2)}, u32[]{:S(2)}) collective-permute-start(bf16[128,512]{1,0:T(8,128)(2,1)S(1)} %pad_maximum_fusion.2.own_ref), channel_id=1, source_target_pairs={{0,1},{1,2},{2,3},{4,5},{5,6},{6,7},{8,9},{9,10},{10,11},{12,13},{... | collective-permute-start | bytes 393224 | tf_op jit(solution)/shard_map/ppermute | solution.py:236
  17.1 12.6 %copy-start.3 = (bf16[128,16]{0,1:T(8,128)(2,1)S(1)}, bf16[128,16]{0,1:T(8,128)(2,1)}, u32[]{:S(2)}) copy-start(bf16[128,16]{0,1:T(8,128)(2,1)} %param.15) | copy-start | bytes 12292
  17.1 4.0 %collective-permute-start.2 = (bf16[64,512]{1,0:T(8,128)(2,1)S(1)}, bf16[64,512]{1,0:T(8,128)(2,1)S(1)}, u32[]{:S(2)}, u32[]{:S(2)}) collective-permute-start(bf16[64,512]{1,0:T(8,128)(2,1)S(1)} %fusion.10), channel_id=1, source_target_pairs={{0,2},{1,3},{4,6},{5,7},{8,10},{9,11},{12,14},{13,15},{16,18},{17,... | collective-permute-start | bytes 196616 | tf_op jit(solution)/shard_map/ppermute | solution.py:236
  18.4 11.2 %collective-permute-start.1 = (bf16[128,512]{1,0:T(8,128)(2,1)S(1)}, bf16[128,512]{1,0:T(8,128)(2,1)S(1)}, u32[]{:S(2)}, u32[]{:S(2)}) collective-permute-start(bf16[128,512]{1,0:T(8,128)(2,1)S(1)} %pad_maximum_fusion.1.own_ref), channel_id=1, source_target_pairs={{0,1},{1,2},{2,3},{4,5},{5,6},{6,7},{8,9},{9,10},{10,11},{12,13},{... | collective-permute-start | bytes 393224 | tf_op jit(solution)/shard_map/ppermute | solution.py:236
  21.1 8.4 %collective-permute-start.9 = (bf16[1,4,16,1024]{3,2,1,0:T(8,128)(2,1)S(1)}, bf16[1,4,16,1024]{3,2,1,0:T(8,128)(2,1)S(1)}, u32[]{:S(2)}, u32[]{:S(2)}) collective-permute-start(bf16[1,4,16,1024]{3,2,1,0:T(8,128)(2,1)S(1)} %maximum_bitcast_fusion), channel_id=1, source_target_pairs={{0,24},{4,28},{8,16},{12,20},{16,8},{20,12},{24,0},{28,4},{1,25},{... | collective-permute-start | bytes 393224 | tf_op jit(solution)/shard_map/ppermute | solution.py:200
  23.6 5.9 %collective-permute-start.8 = (bf16[1,4,16,1024]{3,2,1,0:T(8,128)(2,1)S(1)}, bf16[1,4,16,1024]{3,2,1,0:T(8,128)(2,1)S(1)}, u32[]{:S(2)}, u32[]{:S(2)}) collective-permute-start(bf16[1,4,16,1024]{3,2,1,0:T(8,128)(2,1)S(1)} %maximum_bitcast_fusion), channel_id=1, source_target_pairs={{0,16},{4,20},{8,24},{12,28},{16,0},{20,4},{24,8},{28,12},{1,17},{... | collective-permute-start | bytes 393224 | tf_op jit(solution)/shard_map/ppermute | solution.py:200
  24.2 5.4 %collective-permute-start.7 = (bf16[1,4,16,1024]{3,2,1,0:T(8,128)(2,1)S(1)}, bf16[1,4,16,1024]{3,2,1,0:T(8,128)(2,1)S(1)}, u32[]{:S(2)}, u32[]{:S(2)}) collective-permute-start(bf16[1,4,16,1024]{3,2,1,0:T(8,128)(2,1)S(1)} %maximum_bitcast_fusion), channel_id=1, source_target_pairs={{0,8},{4,12},{8,0},{12,4},{16,24},{20,28},{24,16},{28,20},{1,9},{5... | collective-permute-start | bytes 393224 | tf_op jit(solution)/shard_map/ppermute | solution.py:200
  24.8 1.2 %copy-start.1 = (bf16[128,4096]{1,0:T(8,128)(2,1)S(1)}, bf16[128,4096]{1,0:T(8,128)(2,1)}, u32[]{:S(2)}) copy-start(bf16[128,4096]{1,0:T(8,128)(2,1)} %g_hbm.3) | copy-start | bytes 3145732
  29.6 4.0 %collective-permute-start.10 = (bf16[4,4,16,1024]{3,2,1,0:T(8,128)(2,1)S(1)}, bf16[4,4,16,1024]{3,2,1,0:T(8,128)(2,1)S(1)}, u32[]{:S(2)}, u32[]{:S(2)}) collective-permute-start(bf16[4,4,16,1024]{3,2,1,0:T(8,128)(2,1)S(1)} %pad_maximum_fusion.refs_0_), channel_id=1, source_target_pairs={{0,4},{4,0},{8,12},{12,8},{16,20},{20,16},{24,28},{28,24},{1,5},{5... | collective-permute-start | bytes 1572872 | tf_op jit(solution)/shard_map/ppermute | solution.py:200
  33.6 2.3 %copy-start.2 = (bf16[128,8192]{1,0:T(8,128)(2,1)S(1)}, bf16[128,8192]{1,0:T(8,128)(2,1)}, u32[]{:S(2)}) copy-start(bf16[128,8192]{1,0:T(8,128)(2,1)} %x_ref.1) | copy-start | bytes 6291460
  33.6 2.1 %collective-permute-start.11 = (bf16[4,4,16,1024]{3,2,1,0:T(8,128)(2,1)S(1)}, bf16[4,4,16,1024]{3,2,1,0:T(8,128)(2,1)S(1)}, u32[]{:S(2)}, u32[]{:S(2)}) collective-permute-start(bf16[4,4,16,1024]{3,2,1,0:T(8,128)(2,1)S(1)} %get-tuple-element.33), channel_id=1, source_target_pairs={{0,4},{4,0},{8,12},{12,8},{16,20},{20,16},{24,28},{28,24},{1,5},{5... | collective-permute-start | bytes 1572872 | tf_op jit(solution)/shard_map/ppermute | solution.py:200
  36.6 5.6 %collective-permute-start.12 = (bf16[4,4,16,2048]{3,2,1,0:T(8,128)(2,1)S(1)}, bf16[4,4,16,2048]{3,2,1,0:T(8,128)(2,1)S(1)}, u32[]{:S(2)}, u32[]{:S(2)}) collective-permute-start(bf16[4,4,16,2048]{3,2,1,0:T(8,128)(2,1)S(1)} %get-tuple-element.36), channel_id=1, source_target_pairs={{0,4},{4,0},{8,12},{12,8},{16,20},{20,16},{24,28},{28,24},{1,5},{5... | collective-permute-start | bytes 3145736 | tf_op jit(solution)/shard_map/ppermute | solution.py:200
  37.1 8.6 %collective-permute-start.19 = (bf16[4,16,1024]{2,1,0:T(8,128)(2,1)S(1)}, bf16[4,16,1024]{2,1,0:T(8,128)(2,1)S(1)}, u32[]{:S(2)}, u32[]{:S(2)}) collective-permute-start(bf16[4,16,1024]{2,1,0:T(8,128)(2,1)S(1)} %get-tuple-element.41), channel_id=1, source_target_pairs={{0,1},{1,2},{2,3},{3,0},{4,5},{5,6},{6,7},{7,4},{8,9},{9,10},{10,1... | collective-permute-start | bytes 393224 | tf_op jit(solution)/shard_map/ppermute | solution.py:196
  37.2 9.9 %collective-permute-start.21 = (bf16[4,16,1024]{2,1,0:T(8,128)(2,1)S(1)}, bf16[4,16,1024]{2,1,0:T(8,128)(2,1)S(1)}, u32[]{:S(2)}, u32[]{:S(2)}) collective-permute-start(bf16[4,16,1024]{2,1,0:T(8,128)(2,1)S(1)} %get-tuple-element.42), channel_id=1, source_target_pairs={{0,3},{1,0},{2,1},{3,2},{4,7},{5,4},{6,5},{7,6},{8,11},{9,8},{10,9... | collective-permute-start | bytes 393224 | tf_op jit(solution)/shard_map/ppermute | solution.py:196
  41.0 11.9 %collective-permute-start.20 = (bf16[4,16,1024]{2,1,0:T(8,128)(2,1)S(1)}, bf16[4,16,1024]{2,1,0:T(8,128)(2,1)S(1)}, u32[]{:S(2)}, u32[]{:S(2)}) collective-permute-start(bf16[4,16,1024]{2,1,0:T(8,128)(2,1)S(1)} %get-tuple-element.43), channel_id=1, source_target_pairs={{0,2},{1,3},{2,0},{3,1},{4,6},{5,7},{6,4},{7,5},{8,10},{9,11},{10,... | collective-permute-start | bytes 393224 | tf_op jit(solution)/shard_map/ppermute | solution.py:196
  42.7 13.4 %collective-permute-start.13 = (bf16[4,16,2048]{2,1,0:T(8,128)(2,1)S(1)}, bf16[4,16,2048]{2,1,0:T(8,128)(2,1)S(1)}, u32[]{:S(2)}, u32[]{:S(2)}) collective-permute-start(bf16[4,16,2048]{2,1,0:T(8,128)(2,1)S(1)} %get-tuple-element.38), channel_id=1, source_target_pairs={{0,8},{4,12},{8,0},{12,4},{16,24},{20,28},{24,16},{28,20},{1,9},{5... | collective-permute-start | bytes 786440 | tf_op jit(solution)/shard_map/ppermute | solution.py:200
  44.3 12.8 %collective-permute-start.15 = (bf16[4,16,2048]{2,1,0:T(8,128)(2,1)S(1)}, bf16[4,16,2048]{2,1,0:T(8,128)(2,1)S(1)}, u32[]{:S(2)}, u32[]{:S(2)}) collective-permute-start(bf16[4,16,2048]{2,1,0:T(8,128)(2,1)S(1)} %get-tuple-element.39), channel_id=1, source_target_pairs={{0,24},{4,28},{8,16},{12,20},{16,8},{20,12},{24,0},{28,4},{1,25},{... | collective-permute-start | bytes 786440 | tf_op jit(solution)/shard_map/ppermute | solution.py:200
  45.8 13.2 %collective-permute-start.14 = (bf16[4,16,2048]{2,1,0:T(8,128)(2,1)S(1)}, bf16[4,16,2048]{2,1,0:T(8,128)(2,1)S(1)}, u32[]{:S(2)}, u32[]{:S(2)}) collective-permute-start(bf16[4,16,2048]{2,1,0:T(8,128)(2,1)S(1)} %get-tuple-element.40), channel_id=1, source_target_pairs={{0,16},{4,20},{8,24},{12,28},{16,0},{20,4},{24,8},{28,12},{1,17},{... | collective-permute-start | bytes 786440 | tf_op jit(solution)/shard_map/ppermute | solution.py:200
  53.0 10.1 %collective-permute-start.22 = (bf16[16,1024]{1,0:T(8,128)(2,1)S(1)}, bf16[16,1024]{1,0:T(8,128)(2,1)S(1)}, u32[]{:S(2)}, u32[]{:S(2)}) collective-permute-start(bf16[16,1024]{1,0:T(8,128)(2,1)S(1)} %get-tuple-element.47), channel_id=1, source_target_pairs={{0,8},{4,12},{8,0},{12,4},{16,24},{20,28},{24,16},{28,20},{1,9},{5... | collective-permute-start | bytes 98312 | tf_op jit(solution)/shard_map/ppermute | solution.py:200
  54.6 12.2 %collective-permute-start.24 = (bf16[16,1024]{1,0:T(8,128)(2,1)S(1)}, bf16[16,1024]{1,0:T(8,128)(2,1)S(1)}, u32[]{:S(2)}, u32[]{:S(2)}) collective-permute-start(bf16[16,1024]{1,0:T(8,128)(2,1)S(1)} %get-tuple-element.48), channel_id=1, source_target_pairs={{0,24},{4,28},{8,16},{12,20},{16,8},{20,12},{24,0},{28,4},{1,25},{... | collective-permute-start | bytes 98312 | tf_op jit(solution)/shard_map/ppermute | solution.py:200
  56.1 10.7 %collective-permute-start.23 = (bf16[16,1024]{1,0:T(8,128)(2,1)S(1)}, bf16[16,1024]{1,0:T(8,128)(2,1)S(1)}, u32[]{:S(2)}, u32[]{:S(2)}) collective-permute-start(bf16[16,1024]{1,0:T(8,128)(2,1)S(1)} %get-tuple-element.49), channel_id=1, source_target_pairs={{0,16},{4,20},{8,24},{12,28},{16,0},{20,4},{24,8},{28,12},{1,17},{... | collective-permute-start | bytes 98312 | tf_op jit(solution)/shard_map/ppermute | solution.py:200
  59.1 8.3 %collective-permute-start.16 = (bf16[16,2048]{1,0:T(8,128)(2,1)S(1)}, bf16[16,2048]{1,0:T(8,128)(2,1)S(1)}, u32[]{:S(2)}, u32[]{:S(2)}) collective-permute-start(bf16[16,2048]{1,0:T(8,128)(2,1)S(1)} %get-tuple-element.44), channel_id=1, source_target_pairs={{0,1},{1,2},{2,3},{3,0},{4,5},{5,6},{6,7},{7,4},{8,9},{9,10},{10,1... | collective-permute-start | bytes 196616 | tf_op jit(solution)/shard_map/ppermute | solution.py:196
  63.1 4.5 %collective-permute-start.18 = (bf16[16,2048]{1,0:T(8,128)(2,1)S(1)}, bf16[16,2048]{1,0:T(8,128)(2,1)S(1)}, u32[]{:S(2)}, u32[]{:S(2)}) collective-permute-start(bf16[16,2048]{1,0:T(8,128)(2,1)S(1)} %get-tuple-element.45), channel_id=1, source_target_pairs={{0,3},{1,0},{2,1},{3,2},{4,7},{5,4},{6,5},{7,6},{8,11},{9,8},{10,9... | collective-permute-start | bytes 196616 | tf_op jit(solution)/shard_map/ppermute | solution.py:196
  63.1 7.3 %collective-permute-start.17 = (bf16[16,2048]{1,0:T(8,128)(2,1)S(1)}, bf16[16,2048]{1,0:T(8,128)(2,1)S(1)}, u32[]{:S(2)}, u32[]{:S(2)}) collective-permute-start(bf16[16,2048]{1,0:T(8,128)(2,1)S(1)} %get-tuple-element.46), channel_id=1, source_target_pairs={{0,2},{1,3},{2,0},{3,1},{4,6},{5,7},{6,4},{7,5},{8,10},{9,11},{10,... | collective-permute-start | bytes 196616 | tf_op jit(solution)/shard_map/ppermute | solution.py:196

commit v6 on v5

v6 whole, which is shorter than its diff:
```python
import functools
import math

import jax
import jax.numpy as jnp
from jax import lax
from jax.experimental import pallas as pl
from jax.experimental.pallas import tpu as pltpu
from jax.sharding import PartitionSpec as P

QUERY_HEADS = 32
KEY_VALUE_HEADS = 4
HEAD_SIZE = 128
GROUP = QUERY_HEADS // KEY_VALUE_HEADS
ADAPTER_SCALE = 2.0
NEVER = -1e30
LAYOUT_BYTES = 16 * 2**20
BF16 = jnp.bfloat16
F32 = jnp.float32
I32 = jnp.int32
SEQ = ("plane", "core")
VMEM = pl.BlockSpec(memory_space=pltpu.VMEM)
ANY = pl.BlockSpec(memory_space=pl.ANY)


def dot(a, b, a_dim, b_dim):
    return lax.dot_general(a, b, (((a_dim,), (b_dim,)), ((), ())), preferred_element_type=F32)


def seq_index():
    return lax.axis_index("plane") * lax.axis_size("core") + lax.axis_index("core")


def group_rows(rows_of_group, n_groups, width, by_slot):
    row = lax.broadcasted_iota(I32, (n_groups * rows_of_group, width), 0) // rows_of_group
    if by_slot:
        half = n_groups // 2
        core = lax.axis_index("core")
        row = jnp.where(row < half, row * 2 + core, (row - half) * 2 + 1 - core)
    return row


def layout_kernel(n_parts, facts_ref, *refs):
    parts, (k_all, v_all, k_turned) = refs[:n_parts], refs[n_parts:]
    tok = facts_ref.shape[1]
    kv_width = v_all.shape[1]
    key_rows = v_all.shape[0]
    head = lax.axis_index("head")
    position = head * tok + lax.broadcasted_iota(I32, (1, tok), 1)
    key_position = (
        head * tok - (key_rows - tok) + lax.broadcasted_iota(I32, (key_rows, tok), 0)
    )
    allowed = (key_position >= facts_ref[0:1, :]) & (key_position <= position)
    bias = jnp.where(allowed, 0.0, NEVER).astype(BF16)
    for kv in range(KEY_VALUE_HEADS):
        start = 0
        at = slice(kv * HEAD_SIZE, (kv + 1) * HEAD_SIZE)
        for part in parts:
            rows = part.shape[0]
            k_all[kv, start : start + rows, :HEAD_SIZE] = part[:, at]
            v_all[start : start + rows, at] = part[:, kv_width + at.start : kv_width + at.stop]
            start += rows
        k_all[kv, :, HEAD_SIZE:] = bias
        k_turned[at, :] = k_all[kv, :, :HEAD_SIZE].T


def attention_kernel(
    by_slot, facts_ref, act_ref, k_all, v_all, k_turned, q_hbm, g_hbm, dq_turned, *refs
):
    *up_refs, q_ref, g_ref, q_sem, g_sem = refs
    tok = q_ref.shape[0]
    per_kv = GROUP * HEAD_SIZE

    def fetch(kv):
        at = pl.ds(kv * per_kv, per_kv)
        return (
            pltpu.make_async_copy(q_hbm.at[:, at], q_ref.at[:, at], q_sem.at[kv]),
            pltpu.make_async_copy(g_hbm.at[:, at], g_ref.at[:, at], g_sem.at[kv]),
        )

    for kv in range(KEY_VALUE_HEADS):
        for copy in fetch(kv):
            copy.start()

    one = lax.broadcasted_iota(I32, (2 * tok, tok), 0) % tok
    pick = (one == lax.broadcasted_iota(I32, (2 * tok, tok), 1)).astype(F32).astype(BF16)
    scale = 1.0 / HEAD_SIZE**0.5
    to_log2 = scale * math.log2(math.e)

    def one_group(kv, carry):
        for copy in fetch(kv):
            copy.wait()
        at_kv = pl.ds(pl.multiple_of(kv * HEAD_SIZE, HEAD_SIZE), HEAD_SIZE)
        k_g = k_all[kv]
        v_g = v_all[:, at_kv]
        kt_g = k_turned[at_kv, :]
        for i in range(0, GROUP, 2):
            first = (kv * GROUP + i) * HEAD_SIZE
            at = [
                pl.ds(pl.multiple_of(first + n * HEAD_SIZE, HEAD_SIZE), HEAD_SIZE) for n in range(2)
            ]
            q_two = jnp.concatenate([q_ref[:, at[0]], q_ref[:, at[1]]], axis=0)
            g_two = jnp.concatenate([g_ref[:, at[0]], g_ref[:, at[1]]], axis=0)
            s = dot(k_g, jnp.concatenate([q_two, pick], axis=1), 1, 1)
            d_prob = dot(v_g, g_two, 1, 1)
            weights = jnp.exp2((s - jnp.max(s, axis=0, keepdims=True)) * to_log2)
            inverse = 1.0 / jnp.sum(weights, axis=0, keepdims=True)
            delta = jnp.sum(weights * d_prob, axis=0, keepdims=True) * inverse
            dscore = (weights * (d_prob - delta)).astype(BF16)
            dq = dot(kt_g, dscore, 1, 0) * (inverse * scale)
            dq_turned[at[0], :] = dq[:, :tok].astype(BF16)
            dq_turned[at[1], :] = dq[:, tok:].astype(BF16)
        return carry

    lax.fori_loop(0, KEY_VALUE_HEADS, one_group, 0)

    rank = act_ref.shape[0]
    per, n_quarters, _, part = up_refs[0].shape
    n_groups = per * len(up_refs)
    own = group_rows(rank, n_groups, tok, by_slot) == facts_ref[2:3, :]
    act = jnp.concatenate([act_ref[...].astype(F32)] * n_groups, axis=0)
    act_cols = jnp.where(own, act, 0.0).astype(BF16)
    for quarter in range(n_quarters):
        at = slice(quarter * part, (quarter + 1) * part)
        up = dot(act_cols, dq_turned[at, :], 1, 1).astype(BF16)
        for n in range(n_groups):
            up_refs[n // per][n % per, quarter] = up[n * rank : (n + 1) * rank, :]


def rank_kernel(by_slot, n_w, facts_ref, *refs):
    w_refs, (dq_ref, out_ref) = refs[:n_w], refs[n_w:]
    tok = dq_ref.shape[1]
    seq, head = seq_index(), lax.axis_index("head")
    n_adapters, n_quarters, rank, part = w_refs[0].shape
    adapter = facts_ref[1:2, :]
    total = jnp.zeros((rank, tok), F32)
    for c, w_ref in enumerate(w_refs):
        rows = None
        for quarter in range(n_quarters):
            j = lax.rem(head + n_quarters - quarter, n_quarters) if by_slot else quarter
            dq = dq_ref[quarter * part : (quarter + 1) * part, :]
            new = dot(w_ref[:, j].reshape(n_adapters * rank, part), dq, 1, 0)
            rows = new if rows is None else rows + new
        for m in range(n_adapters):
            a = (2 * m + c) ^ seq if by_slot else m
            total = total + jnp.where(adapter == a, rows[m * rank : (m + 1) * rank, :], 0.0)
    out_ref[...] = total.astype(BF16)


def down_kernel(by_slot, facts_ref, x_ref, rank_ref, *out_refs):
    rank, tok = rank_ref.shape
    per, n_quarters, _, x_part = out_refs[0].shape
    n_groups = per * len(out_refs)
    own = group_rows(rank, n_groups, tok, by_slot) == facts_ref[2:3, :]
    low = jnp.concatenate([rank_ref[...].astype(F32)] * n_groups, axis=0)
    cols = jnp.where(own, low, 0.0).astype(BF16)
    step = min(512, x_part)
    for j in range(n_quarters):
        for start in range(0, x_part, step):
            at = slice(j * x_part + start, j * x_part + start + step)
            down = dot(cols, x_ref[:, at], 1, 0).astype(BF16)
            for n in range(n_groups):
                piece = down[n * rank : (n + 1) * rank, :]
                out_refs[n // per][n % per, j, :, start : start + step] = piece


def token_facts(tok, lengths, adapters, owner, by_slot):
    n_seg = lengths.shape[0]
    order = jnp.arange(n_seg, dtype=I32)
    starts = jnp.sum(jnp.where(order[None, :] < order[:, None], lengths[None, :], 0), axis=1)
    if by_slot:
        hits = adapters[:, None] == jnp.arange(owner.shape[0], dtype=I32)[None, :]
        groups = jnp.sum(jnp.where(hits, owner[None, :], 0), axis=1)
    else:
        groups = order
    position = lax.axis_index("head") * tok + jnp.arange(tok, dtype=I32)
    inside = (position >= starts[:, None]) & (position < (starts + lengths)[:, None])
    told = jnp.stack([starts, adapters, groups] + [jnp.zeros_like(starts)] * 5)
    return jnp.sum(jnp.where(inside[None], told[:, :, None], 0), axis=1)


def shifted(x, n_head, j):
    return lax.ppermute(x, "head", [(i, (i + j) % n_head) for i in range(n_head)])


def partnered(x, n_seq, bits):
    return lax.ppermute(x, SEQ, [(i, i ^ bits) for i in range(n_seq)])


def on_device(
    queries, keys, values, output_gradient, inputs, adapter_activation,
    adapter_up_weight, segment_length, segment_adapter, owner,
):
    n_head = lax.axis_size("head")
    n_seq = lax.axis_size(SEQ)
    tok, width = queries.shape
    pack = tok * n_head
    rank = adapter_up_weight.shape[1]
    n_adapters = owner.shape[0]
    n_seg = segment_length.shape[1]
    by_slot = n_adapters == n_seq == 8
    facts = token_facts(tok, segment_length[0], segment_adapter[0], owner, by_slot)

    reach = []
    while sum(reach) < pack * 3 // 8:
        reach.append(min(pack * 3 // 8 - sum(reach), tok))
    key_rows = tok + sum(reach)
    own = jnp.concatenate([keys, values], axis=1)
    parts = [own]
    for hop, rows in enumerate(reach, 1):
        shift = [(i, i + hop) for i in range(n_head - hop)]
        parts.insert(0, lax.ppermute(own[tok - rows :], "head", shift))

    if by_slot:
        w = [adapter_up_weight] + [shifted(adapter_up_weight, n_head, j) for j in range(1, n_head)]
        w = jnp.concatenate(w, axis=0)[None]
        w = [w] + [partnered(w, n_seq, 2 * m) for m in range(1, n_seq // 2)]
        w = jnp.concatenate(w, axis=0)
        up_weight = [w, partnered(w, n_seq, 1)]
    else:
        w = lax.all_gather(adapter_up_weight, SEQ, axis=0, tiled=True)
        up_weight = [lax.all_gather(w, "head", axis=1, tiled=False)]

    n_out = 2 if by_slot else 1
    n_groups = n_seq if by_slot else n_seg
    part = width // n_head
    x_part = inputs.shape[1] // n_head
    params = pltpu.CompilerParams(vmem_limit_bytes=32 * 2**20)

    laid_out = pl.pallas_call(
        functools.partial(layout_kernel, len(parts)),
        out_shape=[
            jax.ShapeDtypeStruct((KEY_VALUE_HEADS, key_rows, 2 * HEAD_SIZE), BF16),
            jax.ShapeDtypeStruct((key_rows, keys.shape[1]), BF16),
            jax.ShapeDtypeStruct((keys.shape[1], key_rows), BF16),
        ],
        in_specs=[VMEM] * (1 + len(parts)),
        out_specs=[VMEM] * 3,
        compiler_params=params,
        cost_estimate=pl.CostEstimate(
            flops=0, bytes_accessed=LAYOUT_BYTES, transcendentals=0
        ),
        name="layout",
    )(facts, *parts)
    if by_slot:
        laid_out, up_weight = lax.optimization_barrier((laid_out, up_weight))

    up_shape = jax.ShapeDtypeStruct((n_groups // n_out, n_head, rank, part), BF16)
    dq, *up = pl.pallas_call(
        functools.partial(attention_kernel, by_slot),
        out_shape=[jax.ShapeDtypeStruct((width, tok), BF16)] + [up_shape] * n_out,
        in_specs=[VMEM] * 5 + [ANY] * 2,
        out_specs=[VMEM] * (1 + n_out),
        scratch_shapes=[
            pltpu.VMEM((tok, width), BF16),
            pltpu.VMEM((tok, width), BF16),
            pltpu.SemaphoreType.DMA((KEY_VALUE_HEADS,)),
            pltpu.SemaphoreType.DMA((KEY_VALUE_HEADS,)),
        ],
        compiler_params=params,
        cost_estimate=pl.CostEstimate(
            flops=2 * tok * width * key_rows * 3,
            bytes_accessed=4 * tok * width * 2,
            transcendentals=tok * key_rows * QUERY_HEADS,
        ),
        name="attention",
    )(facts, adapter_activation.T, *laid_out, queries, output_gradient)

    rank_low = pl.pallas_call(
        functools.partial(rank_kernel, by_slot, len(up_weight)),
        out_shape=jax.ShapeDtypeStruct((rank, tok), BF16),
        in_specs=[VMEM] * (2 + len(up_weight)),
        out_specs=VMEM,
        compiler_params=params,
        name="rank_gradient",
    )(facts, *up_weight, dq)
    if by_slot:
        rank_low, up = lax.optimization_barrier((rank_low, over_cores(up, n_seq)))

    down_shape = jax.ShapeDtypeStruct((n_groups // n_out, n_head, rank, x_part), BF16)
    down = pl.pallas_call(
        functools.partial(down_kernel, by_slot),
        out_shape=[down_shape] * n_out,
        in_specs=[VMEM] * 3,
        out_specs=[VMEM] * n_out,
        compiler_params=params,
        cost_estimate=pl.CostEstimate(
            flops=2 * n_groups * rank * tok * inputs.shape[1],
            bytes_accessed=4 * tok * inputs.shape[1] * 2,
            transcendentals=0,
        ),
        name="down_parts",
    )(facts, inputs, rank_low)

    if by_slot:
        up = added(up.reshape(-1, rank, part), ("plane", "head"))
        down = added(over_cores(down, n_seq), "plane").astype(BF16)
        down = added(down, "head")
    else:
        up = spread(added(up[0].swapaxes(0, 1), "head"), segment_adapter, owner, n_seq)
        down = spread(added(down[0].swapaxes(0, 1), "head"), segment_adapter, owner, n_seq)
    return down.T[None] * ADAPTER_SCALE, up[None] * ADAPTER_SCALE


def over_cores(parts, n_seq):
    keep, send = parts
    return (keep.astype(F32) + partnered(send, n_seq, 1).astype(F32)).astype(BF16)


def added(parts, axes):
    got = lax.all_to_all(parts, axes, split_axis=0, concat_axis=0, tiled=True)
    return jnp.sum(got.astype(F32), axis=0)


def spread(part, segment_adapter, owner, n_seq):
    goes_to = owner[segment_adapter[0]]
    slots = (goes_to[:, None] == jnp.arange(n_seq, dtype=I32)[None, :]).astype(F32)
    slotted = jnp.einsum("srw,so->orw", part, slots, precision=lax.Precision.HIGHEST)
    return added(slotted.astype(BF16), SEQ)


def solution(mesh):
    n_seq, n_head = mesh.devices.shape
    devices = mesh.devices.reshape(n_seq // 2, 2, n_head)
    return jax.shard_map(
        on_device,
        mesh=jax.sharding.Mesh(devices, ("plane", "core", "head")),
        in_specs=(
            P((*SEQ, "head"), None),
            P((*SEQ, "head"), None),
            P((*SEQ, "head"), None),
            P((*SEQ, "head"), None),
            P((*SEQ, "head"), None),
            P((*SEQ, "head"), None),
            P(SEQ, None, "head"),
            P(SEQ, None),
            P(SEQ, None),
            P(),
        ),
        out_specs=(P(SEQ, "head", None), P(SEQ, None, "head")),
        check_vma=False,
    )
```

time: 71.5 us -> 90.3 us (1.26)
  waiting for transfers between devices: 12.6 us -> 30.4 us
  blocking collectives: 0 us -> 17.2 us
  starting transfers between devices: 40.5 us -> 23.3 us
  other arithmetic: 5.49 us -> 6.41 us
    all_to_all x0 -> x2, waiting for transfers between devices: none -> 21.5 us  [added(): got = lax.all_to_all(parts, axes, split_axis=0, concat_axis=0, tiled=True)]
    all_to_all x0 -> x1, blocking collectives: none -> 17.2 us  [added(): got = lax.all_to_all(parts, axes, split_axis=0, concat_axis=0, tiled=True)]
    ppermute x9 -> x3, starting transfers between devices: 20.6 us -> 7.93 us  [shifted(): lax.ppermute(x, 'head', [(i, (i + j) % n_head) for i in range(n_head)])]
    ppermute x16 -> x8, starting transfers between devices: 19.9 us -> 8.43 us  [the longest x2 4.39 us: on_device(): parts.insert(0, lax.ppermute(own[tok - rows:], 'head', shift))]
    ppermute x9 -> x3, waiting for transfers between devices: 9.09 us -> 0.01 us  [shifted(): lax.ppermute(x, 'head', [(i, (i + j) % n_head) for i in range(n_head)])]
    all_to_all x0 -> x2, starting transfers between devices: none -> 6.98 us  [added(): got = lax.all_to_all(parts, axes, split_axis=0, concat_axis=0, tiled=True)]
    ppermute x16 -> x8, waiting for transfers between devices: 3.51 us -> 8.87 us  [the longest x6 8.87 us: partnered(): return lax.ppermute(x, SEQ, [(i, i ^ bits) for i in range(n_seq)])]
    reduce_sum x0 -> x3, other arithmetic: none -> 1.03 us  [added(): return jnp.sum(got.astype(F32), axis=0)]
  transfers between devices with their start and end apart: 25 -> 13, of which waited for: 7 -> 7; matrix products, arithmetic and copies ran while one was open for 9% -> 7% of each run, Pallas kernels for 11% -> 1%
where the time goes in v6:
time: 90.3 us; the launch traced here: 89.7 us
  waiting for transfers between devices  30.4 us (34%)
  starting transfers between devices  23.3 us (26%)
  blocking collectives  17.2 us (19%)
  Pallas kernels  8.5 us (9%)
  other arithmetic  6.41 us (7%)
  local copies, waits for them, and re-layouts  3.12 us (3%)
    all_to_all x2, waiting for transfers between devices, added(): got = lax.all_to_all(parts, axes, split_axis=0, concat_axis=0, tiled=True)  21.5 us
    all_to_all x1, blocking collectives, added(): got = lax.all_to_all(parts, axes, split_axis=0, concat_axis=0, tiled=True)  17.2 us
    ppermute x6, waiting for transfers between devices, partnered(): return lax.ppermute(x, SEQ, [(i, i ^ bits) for i in range(n_seq)])  8.87 us
    ppermute x3, starting transfers between devices, shifted(): lax.ppermute(x, 'head', [(i, (i + j) % n_head) for i in range(n_head)])  7.93 us
    pallas_call x1, Pallas kernels, on_device(): pl.pallas_call(functools.partial(attention_kernel, by_slot), out_shape=[j...  7.13 us
    all_to_all x2, starting transfers between devices, added(): got = lax.all_to_all(parts, axes, split_axis=0, concat_axis=0, tiled=True)  6.98 us
    ppermute x2, starting transfers between devices, on_device(): parts.insert(0, lax.ppermute(own[tok - rows:], 'head', shift))  4.39 us
    ppermute x6, starting transfers between devices, partnered(): return lax.ppermute(x, SEQ, [(i, i ^ bits) for i in range(n_seq)])  4.04 us
  transfers between devices with their start and end apart: 13, of which 7 were waited for; matrix products, arithmetic and copies ran while one was open for 7% of the time, Pallas kernels for 1%

profile of v6, /device:TPU:0, one launch (start us, length us, event | category | flops | bytes accessed | tf_op | source)
XLA Modules:
  0.0 89.7 jit_solution(6130305678078013361)
XLA Ops:
  0.7 4.1 %collective-permute-start.3 = (bf16[1,16,1024]{2,1,0:T(8,128)(2,1)}, bf16[1,16,1024]{2,1,0:T(8,128)(2,1)S(1)}, u32[]{:S(2)}, u32[]{:S(2)}) collective-permute-start(bf16[1,16,1024]{2,1,0:T(8,128)(2,1)} %param.16), channel_id=1, source_target_pairs={{0,2},{1,3},{2,0},{3,1},{4,6},{5,7},{6,4},{7,5},{8,10},{9,11},{10,... | collective-permute-start | bytes 98312 | tf_op jit(solution)/shard_map/ppermute | solution.py:183
  4.8 1.6 %collective-permute-start.2 = (bf16[1,16,1024]{2,1,0:T(8,128)(2,1)}, bf16[1,16,1024]{2,1,0:T(8,128)(2,1)S(1)}, u32[]{:S(2)}, u32[]{:S(2)}) collective-permute-start(bf16[1,16,1024]{2,1,0:T(8,128)(2,1)} %param.16), channel_id=1, source_target_pairs={{0,1},{1,2},{2,3},{3,0},{4,5},{5,6},{6,7},{7,4},{8,9},{9,10},{10,1... | collective-permute-start | bytes 98312 | tf_op jit(solution)/shard_map/ppermute | solution.py:183
  6.3 2.2 %collective-permute-start.4 = (bf16[1,16,1024]{2,1,0:T(8,128)(2,1)}, bf16[1,16,1024]{2,1,0:T(8,128)(2,1)S(1)}, u32[]{:S(2)}, u32[]{:S(2)}) collective-permute-start(bf16[1,16,1024]{2,1,0:T(8,128)(2,1)} %param.16), channel_id=1, source_target_pairs={{0,3},{1,0},{2,1},{3,2},{4,7},{5,4},{6,5},{7,6},{8,11},{9,8},{10,9... | collective-permute-start | bytes 98312 | tf_op jit(solution)/shard_map/ppermute | solution.py:183
  8.6 0.9 %constant_dynamic-update-slice_fusion.1 = bf16[128,1024]{1,0:T(8,128)(2,1)S(1)} fusion(bf16[128,512]{1,0:T(8,128)(2,1)} %param.11), kind=kLoop, calls=%fused_computation.10 | loop fusion | bytes 262144
  9.5 0.9 %constant_dynamic-update-slice_fusion.refs_2_ = bf16[128,1024]{1,0:T(8,128)(2,1)S(1)} fusion(bf16[128,1024]{1,0:T(8,128)(2,1)S(1)} %constant_dynamic-update-slice_fusion.1, bf16[128,512]{1,0:T(8,128)(2,1)} %param.12), kind=kLoop, calls=%fused_computation.9 | loop fusion | bytes 262144 | tf_op jit(solution)/shard_map/concatenate | solution.py:208
  10.4 1.7 %collective-permute-start.1 = (bf16[128,1024]{1,0:T(8,128)(2,1)S(1)}, bf16[128,1024]{1,0:T(8,128)(2,1)S(1)}, u32[]{:S(2)}, u32[]{:S(2)}) collective-permute-start(bf16[128,1024]{1,0:T(8,128)(2,1)S(1)} %constant_dynamic-update-slice_fusion.refs_2_), channel_id=1, source_target_pairs={{0,1},{1,2},{2,3},{4,5},{5,6},{6,7},{8,9},{9,10},{10,11},{12,13},{... | collective-permute-start | bytes 786440 | tf_op jit(solution)/shard_map/ppermute | solution.py:212
  12.2 2.7 %collective-permute-start = (bf16[64,1024]{1,0:T(8,128)(2,1)S(1)}, bf16[64,1024]{1,0:T(8,128)(2,1)S(1)}, u32[]{:S(2)}, u32[]{:S(2)}) collective-permute-start(bf16[64,1024]{1,0:T(8,128)(2,1)S(1)} %slice.4), channel_id=1, source_target_pairs={{0,2},{1,3},{4,6},{5,7},{8,10},{9,11},{12,14},{13,15},{16,18},{17,... | collective-permute-start | bytes 393224 | tf_op jit(solution)/shard_map/ppermute | solution.py:212
  14.9 0.8 select_reduce_fusion.2
  15.6 0.0 collective-permute-done.3
  15.6 0.0 collective-permute-done.2
  15.6 0.0 collective-permute-done.4
  15.7 0.8 maximum_bitcast_fusion
  16.4 2.5 %collective-permute-start.7 = (bf16[1,4,16,1024]{3,2,1,0:T(8,128)(2,1)S(1)}, bf16[1,4,16,1024]{3,2,1,0:T(8,128)(2,1)S(1)}, u32[]{:S(2)}, u32[]{:S(2)}) collective-permute-start(bf16[1,4,16,1024]{3,2,1,0:T(8,128)(2,1)S(1)} %maximum_bitcast_fusion), channel_id=1, source_target_pairs={{0,24},{4,28},{8,16},{12,20},{16,8},{20,12},{24,0},{28,4},{1,25},{... | collective-permute-start | bytes 393224 | tf_op jit(solution)/shard_map/ppermute | solution.py:187
  18.9 0.5 collective-permute-start.6
  19.5 0.5 collective-permute-start.5
  20.0 0.7 bitcast_add_fusion
  20.6 2.9 %collective-permute-done.7 = bf16[1,4,16,1024]{3,2,1,0:T(8,128)(2,1)S(1)} collective-permute-done((bf16[1,4,16,1024]{3,2,1,0:T(8,128)(2,1)S(1)}, bf16[1,4,16,1024]{3,2,1,0:T(8,128)(2,1)S(1)}, u32[]{:S(2)}, u32[]{:S(2)}) %collective-permute-start.7) | collective-permute-done | bytes 131104 | tf_op jit(solution)/shard_map/ppermute | solution.py:187
  23.6 0.9 collective-permute-done.6
  24.4 0.0 collective-permute-done.5
  24.5 0.1 pad_maximum_fusion.refs_0_
  24.5 0.1 collective-permute-start.8
  24.6 0.1 compare_and_fusion
  24.7 0.2 select_reduce_fusion.1
  24.9 0.1 select_reduce_fusion.facts_ref
  25.0 0.0 collective-permute-done.refs_0_
  25.0 0.0 collective-permute-done.1.refs_1_
  25.0 0.2 layout.1
  25.3 1.2 %collective-permute-done.8.refs_1_ = bf16[4,4,16,1024]{3,2,1,0:T(8,128)(2,1)S(1)} collective-permute-done((bf16[4,4,16,1024]{3,2,1,0:T(8,128)(2,1)S(1)}, bf16[4,4,16,1024]{3,2,1,0:T(8,128)(2,1)S(1)}, u32[]{:S(2)}, u32[]{:S(2)}) %collective-permute-start.8) | collective-permute-done | bytes 524320 | tf_op jit(solution)/shard_map/ppermute | solution.py:187
  26.5 1.2 %copy-done.2 = bf16[128,4096]{1,0:T(8,128)(2,1)S(1)} copy-done((bf16[128,4096]{1,0:T(8,128)(2,1)S(1)}, bf16[128,4096]{1,0:T(8,128)(2,1)}, u32[]{:S(2)}) %copy-start.2) | copy-done | bytes 1048600
  27.7 7.1 %attention.1 = (bf16[4096,128]{1,0:T(8,128)(2,1)S(1)}, bf16[4,4,16,1024]{3,2,1,0:T(8,128)(2,1)S(1)}, bf16[4,4,16,1024]{3,2,1,0:T(8,128)(2,1)S(1)}) custom-call(s32[8,128]{1,0:T(8,128)S(1)} %select_reduce_fusion.facts_ref, bf16[16,128]{1,0:T(8,128)(2,1)S(1)} %bitcast.15, bf16[4,320,256]{2,1,0:T(8,128)(2,1)S(1)} %get-tuple-element.22.k_all, ...), custom_call_target="tpu_custom_call" | custom-call | flops 1006632960 | bytes 4194304 | tf_op jit(solution)/shard_map/attention/pallas_call | solution.py:249
  34.9 0.0 copy-start
  34.9 0.2 collective-permute-start.9
  35.1 0.5 rank_gradient.1.rank_ref
  35.6 1.3 %collective-permute-done.9 = bf16[4,4,16,1024]{3,2,1,0:T(8,128)(2,1)S(1)} collective-permute-done((bf16[4,4,16,1024]{3,2,1,0:T(8,128)(2,1)S(1)}, bf16[4,4,16,1024]{3,2,1,0:T(8,128)(2,1)S(1)}, u32[]{:S(2)}, u32[]{:S(2)}) %collective-permute-start.9) | collective-permute-done | bytes 524320 | tf_op jit(solution)/shard_map/ppermute | solution.py:187
  36.9 1.0 %add_convert_fusion.1 = bf16[4,4,16,1024]{3,2,1,0:T(8,128)(2,1)} fusion(bf16[4,4,16,1024]{3,2,1,0:T(8,128)(2,1)S(1)} %collective-permute-done.9, bf16[4,4,16,1024]{3,2,1,0:T(8,128)(2,1)S(1)} %get-tuple-element.26), kind=kLoop, calls=%fused_computation.2 | loop fusion | flops 1048576 | bytes 1572864 | tf_op jit(solution)/shard_map/convert_element_type | solution.py:307
  37.9 0.7 down_parts.1
  38.6 0.2 collective-permute-start.10
  38.8 2.5 %collective-permute-done.10 = bf16[4,4,16,2048]{3,2,1,0:T(8,128)(2,1)S(1)} collective-permute-done((bf16[4,4,16,2048]{3,2,1,0:T(8,128)(2,1)S(1)}, bf16[4,4,16,2048]{3,2,1,0:T(8,128)(2,1)S(1)}, u32[]{:S(2)}, u32[]{:S(2)}) %collective-permute-start.10) | collective-permute-done | bytes 1048608 | tf_op jit(solution)/shard_map/ppermute | solution.py:187
  41.3 0.5 add_convert_fusion
  41.7 17.2 %all_to_all.15 = bf16[4,4,16,2048]{3,2,1,0:T(8,128)(2,1)S(1)} all-to-all(bf16[4,4,16,2048]{3,2,1,0:T(8,128)(2,1)S(1)} %add_convert_fusion), channel_id=1, replica_groups=mesh['plane'=4,'core'=2,'head'=4] {'plane'}, dimensions={0} | all-to-all | bytes 2097152 | tf_op jit(solution)/shard_map/all_to_all | solution.py:311
  58.9 3.6 %all-to-all-start.2 = ((bf16[16,16,1024]{2,1,0:T(8,128)(2,1)}), bf16[16,16,1024]{2,1,0:T(8,128)(2,1)S(1)}, u32[]{:S(2)}, u32[]{:S(2)}) async-start(bf16[16,16,1024]{2,1,0:T(8,128)(2,1)} %bitcast.8), calls=%async_computation.2 | async-start | bytes 1048576 | tf_op jit(solution)/shard_map/all_to_all | solution.py:311
  62.5 0.9 %reduce_sum.60 = bf16[4,16,2048]{2,1,0:T(8,128)(2,1)} reduce(bf16[4,4,16,2048]{3,2,1,0:T(8,128)(2,1)S(1)} %all_to_all.15, bf16[]{:T(256)} %constant.2.clone.1), dimensions={0}, to_apply=%region_3.4 | reduce | flops 393216 | bytes 1310722 | tf_op jit(solution)/shard_map/reduce_sum | solution.py:312
  63.4 14.1 %all-to-all-done.2 = bf16[16,16,1024]{2,1,0:T(8,128)(2,1)S(1)} async-done(((bf16[16,16,1024]{2,1,0:T(8,128)(2,1)}), bf16[16,16,1024]{2,1,0:T(8,128)(2,1)S(1)}, u32[]{:S(2)}, u32[]{:S(2)}) %all-to-all-start.2) | async-done | bytes 524320 | tf_op jit(solution)/shard_map/all_to_all | solution.py:311
  77.5 3.4 %all-to-all-start.1 = ((bf16[4,16,2048]{2,1,0:T(8,128)(2,1)}), bf16[4,16,2048]{2,1,0:T(8,128)(2,1)S(1)}, u32[]{:S(2)}, u32[]{:S(2)}) async-start(bf16[4,16,2048]{2,1,0:T(8,128)(2,1)} %reduce_sum.60), calls=%async_computation.1 | async-start | bytes 524288 | tf_op jit(solution)/shard_map/all_to_all | solution.py:311
  80.9 0.1 convert_reduce_fusion
  81.0 0.6 multiply_bitcast_fusion.1
  81.7 7.4 %all-to-all-done.1 = bf16[4,16,2048]{2,1,0:T(8,128)(2,1)S(1)} async-done(((bf16[4,16,2048]{2,1,0:T(8,128)(2,1)}), bf16[4,16,2048]{2,1,0:T(8,128)(2,1)S(1)}, u32[]{:S(2)}, u32[]{:S(2)}) %all-to-all-start.1) | async-done | bytes 262176 | tf_op jit(solution)/shard_map/all_to_all | solution.py:311
  89.1 0.7 multiply_bitcast_fusion
  (16 shorter events, 0.1 us)
Async XLA Ops:
  0.6 24.1 %copy-start.4 = (s32[1,8]{1,0:T(1,128)S(1)}, s32[1,8]{1,0:T(1,128)}, u32[]{:S(2)}) copy-start(s32[1,8]{1,0:T(1,128)} %param.18) | copy-start | bytes 100
  0.6 24.1 %copy-start.5 = (s32[8]{0:T(128)S(1)}, s32[8]{0:T(128)}, u32[]{:S(2)}) copy-start(s32[8]{0:T(128)} %param.19) | copy-start | bytes 100
  0.7 25.9 %copy-start.3 = (bf16[128,16]{0,1:T(8,128)(2,1)S(1)}, bf16[128,16]{0,1:T(8,128)(2,1)}, u32[]{:S(2)}) copy-start(bf16[128,16]{0,1:T(8,128)(2,1)} %param.15) | copy-start | bytes 12292
  0.7 25.8 %copy-start.1 = (bf16[128,4096]{1,0:T(8,128)(2,1)S(1)}, bf16[128,4096]{1,0:T(8,128)(2,1)}, u32[]{:S(2)}) copy-start(bf16[128,4096]{1,0:T(8,128)(2,1)} %q_hbm.1) | copy-start | bytes 3145732
  0.7 15.0 %collective-permute-start.3 = (bf16[1,16,1024]{2,1,0:T(8,128)(2,1)}, bf16[1,16,1024]{2,1,0:T(8,128)(2,1)S(1)}, u32[]{:S(2)}, u32[]{:S(2)}) collective-permute-start(bf16[1,16,1024]{2,1,0:T(8,128)(2,1)} %param.16), channel_id=1, source_target_pairs={{0,2},{1,3},{2,0},{3,1},{4,6},{5,7},{6,4},{7,5},{8,10},{9,11},{10,... | collective-permute-start | bytes 98312 | tf_op jit(solution)/shard_map/ppermute | solution.py:183
  4.8 10.9 %collective-permute-start.2 = (bf16[1,16,1024]{2,1,0:T(8,128)(2,1)}, bf16[1,16,1024]{2,1,0:T(8,128)(2,1)S(1)}, u32[]{:S(2)}, u32[]{:S(2)}) collective-permute-start(bf16[1,16,1024]{2,1,0:T(8,128)(2,1)} %param.16), channel_id=1, source_target_pairs={{0,1},{1,2},{2,3},{3,0},{4,5},{5,6},{6,7},{7,4},{8,9},{9,10},{10,1... | collective-permute-start | bytes 98312 | tf_op jit(solution)/shard_map/ppermute | solution.py:183
  6.3 9.3 %collective-permute-start.4 = (bf16[1,16,1024]{2,1,0:T(8,128)(2,1)}, bf16[1,16,1024]{2,1,0:T(8,128)(2,1)S(1)}, u32[]{:S(2)}, u32[]{:S(2)}) collective-permute-start(bf16[1,16,1024]{2,1,0:T(8,128)(2,1)} %param.16), channel_id=1, source_target_pairs={{0,3},{1,0},{2,1},{3,2},{4,7},{5,4},{6,5},{7,6},{8,11},{9,8},{10,9... | collective-permute-start | bytes 98312 | tf_op jit(solution)/shard_map/ppermute | solution.py:183
  10.4 14.6 %collective-permute-start.1 = (bf16[128,1024]{1,0:T(8,128)(2,1)S(1)}, bf16[128,1024]{1,0:T(8,128)(2,1)S(1)}, u32[]{:S(2)}, u32[]{:S(2)}) collective-permute-start(bf16[128,1024]{1,0:T(8,128)(2,1)S(1)} %constant_dynamic-update-slice_fusion.refs_2_), channel_id=1, source_target_pairs={{0,1},{1,2},{2,3},{4,5},{5,6},{6,7},{8,9},{9,10},{10,11},{12,13},{... | collective-permute-start | bytes 786440 | tf_op jit(solution)/shard_map/ppermute | solution.py:212
  12.2 12.9 %collective-permute-start = (bf16[64,1024]{1,0:T(8,128)(2,1)S(1)}, bf16[64,1024]{1,0:T(8,128)(2,1)S(1)}, u32[]{:S(2)}, u32[]{:S(2)}) collective-permute-start(bf16[64,1024]{1,0:T(8,128)(2,1)S(1)} %slice.4), channel_id=1, source_target_pairs={{0,2},{1,3},{4,6},{5,7},{8,10},{9,11},{12,14},{13,15},{16,18},{17,... | collective-permute-start | bytes 393224 | tf_op jit(solution)/shard_map/ppermute | solution.py:212
  16.4 7.1 %collective-permute-start.7 = (bf16[1,4,16,1024]{3,2,1,0:T(8,128)(2,1)S(1)}, bf16[1,4,16,1024]{3,2,1,0:T(8,128)(2,1)S(1)}, u32[]{:S(2)}, u32[]{:S(2)}) collective-permute-start(bf16[1,4,16,1024]{3,2,1,0:T(8,128)(2,1)S(1)} %maximum_bitcast_fusion), channel_id=1, source_target_pairs={{0,24},{4,28},{8,16},{12,20},{16,8},{20,12},{24,0},{28,4},{1,25},{... | collective-permute-start | bytes 393224 | tf_op jit(solution)/shard_map/ppermute | solution.py:187
  18.9 5.5 %collective-permute-start.6 = (bf16[1,4,16,1024]{3,2,1,0:T(8,128)(2,1)S(1)}, bf16[1,4,16,1024]{3,2,1,0:T(8,128)(2,1)S(1)}, u32[]{:S(2)}, u32[]{:S(2)}) collective-permute-start(bf16[1,4,16,1024]{3,2,1,0:T(8,128)(2,1)S(1)} %maximum_bitcast_fusion), channel_id=1, source_target_pairs={{0,16},{4,20},{8,24},{12,28},{16,0},{20,4},{24,8},{28,12},{1,17},{... | collective-permute-start | bytes 393224 | tf_op jit(solution)/shard_map/ppermute | solution.py:187
  19.5 5.0 %collective-permute-start.5 = (bf16[1,4,16,1024]{3,2,1,0:T(8,128)(2,1)S(1)}, bf16[1,4,16,1024]{3,2,1,0:T(8,128)(2,1)S(1)}, u32[]{:S(2)}, u32[]{:S(2)}) collective-permute-start(bf16[1,4,16,1024]{3,2,1,0:T(8,128)(2,1)S(1)} %maximum_bitcast_fusion), channel_id=1, source_target_pairs={{0,8},{4,12},{8,0},{12,4},{16,24},{20,28},{24,16},{28,20},{1,9},{5... | collective-permute-start | bytes 393224 | tf_op jit(solution)/shard_map/ppermute | solution.py:187
  24.5 2.0 %collective-permute-start.8 = (bf16[4,4,16,1024]{3,2,1,0:T(8,128)(2,1)S(1)}, bf16[4,4,16,1024]{3,2,1,0:T(8,128)(2,1)S(1)}, u32[]{:S(2)}, u32[]{:S(2)}) collective-permute-start(bf16[4,4,16,1024]{3,2,1,0:T(8,128)(2,1)S(1)} %pad_maximum_fusion.refs_0_), channel_id=1, source_target_pairs={{0,4},{4,0},{8,12},{12,8},{16,20},{20,16},{24,28},{28,24},{1,5},{5... | collective-permute-start | bytes 1572872 | tf_op jit(solution)/shard_map/ppermute | solution.py:187
  26.5 1.2 %copy-start.2 = (bf16[128,4096]{1,0:T(8,128)(2,1)S(1)}, bf16[128,4096]{1,0:T(8,128)(2,1)}, u32[]{:S(2)}) copy-start(bf16[128,4096]{1,0:T(8,128)(2,1)} %g_hbm.1) | copy-start | bytes 3145732
  34.9 3.0 %copy-start = (bf16[128,8192]{1,0:T(8,128)(2,1)S(1)}, bf16[128,8192]{1,0:T(8,128)(2,1)}, u32[]{:S(2)}) copy-start(bf16[128,8192]{1,0:T(8,128)(2,1)} %x_ref.1) | copy-start | bytes 6291460
  34.9 2.0 %collective-permute-start.9 = (bf16[4,4,16,1024]{3,2,1,0:T(8,128)(2,1)S(1)}, bf16[4,4,16,1024]{3,2,1,0:T(8,128)(2,1)S(1)}, u32[]{:S(2)}, u32[]{:S(2)}) collective-permute-start(bf16[4,4,16,1024]{3,2,1,0:T(8,128)(2,1)S(1)} %get-tuple-element.27), channel_id=1, source_target_pairs={{0,4},{4,0},{8,12},{12,8},{16,20},{20,16},{24,28},{28,24},{1,5},{5... | collective-permute-start | bytes 1572872 | tf_op jit(solution)/shard_map/ppermute | solution.py:187
  38.6 2.7 %collective-permute-start.10 = (bf16[4,4,16,2048]{3,2,1,0:T(8,128)(2,1)S(1)}, bf16[4,4,16,2048]{3,2,1,0:T(8,128)(2,1)S(1)}, u32[]{:S(2)}, u32[]{:S(2)}) collective-permute-start(bf16[4,4,16,2048]{3,2,1,0:T(8,128)(2,1)S(1)} %get-tuple-element.30), channel_id=1, source_target_pairs={{0,4},{4,0},{8,12},{12,8},{16,20},{20,16},{24,28},{28,24},{1,5},{5... | collective-permute-start | bytes 3145736 | tf_op jit(solution)/shard_map/ppermute | solution.py:187
  58.9 18.6 %all-to-all-start.2 = ((bf16[16,16,1024]{2,1,0:T(8,128)(2,1)}), bf16[16,16,1024]{2,1,0:T(8,128)(2,1)S(1)}, u32[]{:S(2)}, u32[]{:S(2)}) async-start(bf16[16,16,1024]{2,1,0:T(8,128)(2,1)} %bitcast.8), calls=%async_computation.2 | async-start | bytes 1048576 | tf_op jit(solution)/shard_map/all_to_all | solution.py:311
  77.5 11.5 %all-to-all-start.1 = ((bf16[4,16,2048]{2,1,0:T(8,128)(2,1)}), bf16[4,16,2048]{2,1,0:T(8,128)(2,1)S(1)}, u32[]{:S(2)}, u32[]{:S(2)}) async-start(bf16[4,16,2048]{2,1,0:T(8,128)(2,1)} %reduce_sum.60), calls=%async_computation.1 | async-start | bytes 524288 | tf_op jit(solution)/shard_map/all_to_all | solution.py:311

commit v7 on v5

--- a/solution.py
+++ b/solution.py
@@ -14,6 +14,8 @@
 GROUP = QUERY_HEADS // KEY_VALUE_HEADS
 ADAPTER_SCALE = 2.0
 NEVER = -1e30
+LAYOUT_BYTES = 16 * 2**20
+SUM_BYTES = 16 * 2**20
 BF16 = jnp.bfloat16
 F32 = jnp.float32
 I32 = jnp.int32
@@ -33,18 +35,34 @@
     return row
 
 
-def attention_kernel(
-    n_halo, by_slot, first_kv, n_kv,
-    facts_ref, q_hbm, g_hbm, own_ref, *refs,
-):
-    halo_refs = refs[:n_halo]
-    n_before = 2 if first_kv else 0
-    before = refs[n_halo : n_halo + n_before]
-    dq_turned, *up_refs = refs[n_halo + n_before : -7]
-    q_ref, g_ref, q_sem, g_sem, k_all, v_all, k_turned = refs[-7:]
+def layout_kernel(n_parts, facts_ref, *refs):
+    parts, (k_all, v_all, k_turned) = refs[:n_parts], refs[n_parts:]
+    tok = facts_ref.shape[1]
+    kv_width = v_all.shape[1]
+    key_rows = v_all.shape[0]
+    head = lax.axis_index("head")
+    position = head * tok + lax.broadcasted_iota(I32, (1, tok), 1)
+    key_position = (
+        head * tok - (key_rows - tok) + lax.broadcasted_iota(I32, (key_rows, tok), 0)
+    )
+    allowed = (key_position >= facts_ref[0:1, :]) & (key_position <= position)
+    bias = jnp.where(allowed, 0.0, NEVER).astype(BF16)
+    for kv in range(KEY_VALUE_HEADS):
+        start = 0
+        at = slice(kv * HEAD_SIZE, (kv + 1) * HEAD_SIZE)
+        for part in parts:
+            rows = part.shape[0]
+            k_all[kv, start : start + rows, :HEAD_SIZE] = part[:, at]
+            v_all[start : start + rows, at] = part[:, kv_width + at.start : kv_width + at.stop]
+            start += rows
+        k_all[kv, :, HEAD_SIZE:] = bias
+        k_turned[at, :] = k_all[kv, :, :HEAD_SIZE].T
+
+
+def attention_kernel(by_slot, first_kv, n_kv, k_all, v_all, k_turned, q_hbm, g_hbm, *refs):
+    before, refs = (refs[:3], refs[3:]) if first_kv else ((), refs)
+    dq_turned, *up_refs, q_ref, g_ref, q_sem, g_sem = refs
     tok = q_ref.shape[0]
-    kv_width = n_kv * HEAD_SIZE
-    key_rows = v_all.shape[0]
     seq, head = lax.axis_index("seq"), lax.axis_index("head")
     per_kv = GROUP * HEAD_SIZE
 
@@ -60,25 +78,6 @@
         for copy in fetch(kv):
             copy.start()
 
-    position = head * tok + lax.broadcasted_iota(I32, (1, tok), 1)
-    seg_start = facts_ref[0:1, :]
-    key_position = (
-        head * tok - (key_rows - tok) + lax.broadcasted_iota(I32, (key_rows, tok), 0)
-    )
-    allowed = (key_position >= seg_start) & (key_position <= position)
-    bias = jnp.where(allowed, 0.0, NEVER).astype(BF16)
-
-    for kv in range(n_kv):
-        start = 0
-        at = slice(kv * HEAD_SIZE, (kv + 1) * HEAD_SIZE)
-        for halo_ref in (*halo_refs, own_ref):
-            rows = halo_ref.shape[0]
-            k_all[kv, start : start + rows, :HEAD_SIZE] = halo_ref[:, at]
-            v_all[start : start + rows, at] = halo_ref[:, kv_width + at.start : kv_width + at.stop]
-            start += rows
-        k_all[kv, :, HEAD_SIZE:] = bias
-        k_turned[at, :] = k_all[kv, :, :HEAD_SIZE].T
-
     one = lax.broadcasted_iota(I32, (2 * tok, tok), 0) % tok
     pick = (one == lax.broadcasted_iota(I32, (2 * tok, tok), 1)).astype(F32).astype(BF16)
     scale = 1.0 / HEAD_SIZE**0.5
@@ -87,8 +86,8 @@
     def one_group(kv, carry):
         for copy in fetch(kv):
             copy.wait()
-        at_kv = pl.ds(pl.multiple_of(kv * HEAD_SIZE, HEAD_SIZE), HEAD_SIZE)
-        k_g = k_all[kv]
+        at_kv = pl.ds(pl.multiple_of((first_kv + kv) * HEAD_SIZE, HEAD_SIZE), HEAD_SIZE)
+        k_g = k_all[first_kv + kv]
         v_g = v_all[:, at_kv]
         kt_g = k_turned[at_kv, :]
         for i in range(0, GROUP, 2):
@@ -113,7 +112,7 @@
     if not up_refs:
         return
 
-    act_ref, dq_before = before
+    facts_ref, act_ref, dq_before = before
     rank = act_ref.shape[0]
     n_quarters, per, _, part = up_refs[0].shape
     n_groups = per * len(up_refs)
@@ -121,19 +120,12 @@
     act = jnp.concatenate([act_ref[...].astype(F32)] * n_groups, axis=0)
     act_cols = jnp.where(own, act, 0.0).astype(BF16)
     n_before = dq_before.shape[0] // part
-
-    def write(i, dq_ref, quarter):
-        at = pl.ds(pl.multiple_of(i * part, part), part)
-        up = dot(act_cols, dq_ref[at, :], 1, 1).astype(BF16)
+    for quarter in range(n_quarters):
+        i, dq_ref = (quarter, dq_before) if quarter < n_before else (quarter - n_before, dq_turned)
+        up = dot(act_cols, dq_ref[i * part : (i + 1) * part, :], 1, 1).astype(BF16)
         j = lax.rem(quarter + n_quarters - head, n_quarters) if by_slot else quarter
         for n in range(n_groups):
             up_refs[n // per][j, n % per] = up[n * rank : (n + 1) * rank, :]
-
-    for i in range(n_quarters):
-        if i < n_before:
-            write(i, dq_before, i)
-        else:
-            write(i - n_before, dq_turned, i)
 
 
 def rank_kernel(by_slot, n_w, facts_ref, *refs):
@@ -177,6 +169,11 @@
                 out_refs[n // per][n % per, j, :, start : start + step] = piece
 
 
+def sum_kernel(a_ref, b_ref, *out_refs):
+    for i, out_ref in enumerate(out_refs):
+        out_ref[...] = (a_ref[i].astype(F32) + b_ref[i].astype(F32)).astype(BF16)
+
+
 def token_facts(tok, lengths, adapters, owner, by_slot):
     n_seg = lengths.shape[0]
     order = jnp.arange(n_seg, dtype=I32)
@@ -217,32 +214,17 @@
     reach = []
     while sum(reach) < pack * 3 // 8:
         reach.append(min(pack * 3 // 8 - sum(reach), tok))
-    tails = sorted(set(reach))
     key_rows = tok + sum(reach)
-    halves = 2
-    n_kv = KEY_VALUE_HEADS // halves
-    kv_width = n_kv * HEAD_SIZE
-    def pack_of(h):
-        at = slice(h * kv_width, (h + 1) * kv_width)
-        return jnp.concatenate([keys[:, at], values[:, at]], axis=1)
-
-    own = [pack_of(h) for h in range(halves)]
-    packed = [own[h][tok - rows :] for h in range(halves) for rows in tails]
-
-    def halo_of(h):
-        got = []
-        for hop, rows in enumerate(reach, 1):
-            shift = [(i, i + hop) for i in range(n_head - hop)]
-            got.insert(0, lax.ppermute(packed[h * len(tails) + tails.index(rows)], "head", shift))
-        return got
-
-    halo_a, halo_b = halo_of(0), halo_of(1)
+    own = jnp.concatenate([keys, values], axis=1)
+    parts = [own]
+    for hop, rows in enumerate(reach, 1):
+        shift = [(i, i + hop) for i in range(n_head - hop)]
+        parts.insert(0, lax.ppermute(own[tok - rows :], "head", shift))
+
     if by_slot:
         w = [adapter_up_weight] + [shifted(adapter_up_weight, n_head, j) for j in range(1, n_head)]
         w = jnp.concatenate(w, axis=0)[None]
-        halo_a, w = lax.optimization_barrier((halo_a, w))
         w = [w] + [partnered(w, n_seq, 2 * m) for m in range(1, n_seq // 2)]
-        w = jnp.concatenate(w, axis=0)
     else:
         w = lax.all_gather(adapter_up_weight, "seq", axis=0, tiled=True)
         up_weight = [lax.all_gather(w, "head", axis=1, tiled=False)]
@@ -253,21 +235,36 @@
     x_part = inputs.shape[1] // n_head
     params = pltpu.CompilerParams(vmem_limit_bytes=32 * 2**20)
 
-    def attention(h, halos, before, up_shapes):
-        half = width // halves
+    laid_out = pl.pallas_call(
+        functools.partial(layout_kernel, len(parts)),
+        out_shape=[
+            jax.ShapeDtypeStruct((KEY_VALUE_HEADS, key_rows, 2 * HEAD_SIZE), BF16),
+            jax.ShapeDtypeStruct((key_rows, keys.shape[1]), BF16),
+            jax.ShapeDtypeStruct((keys.shape[1], key_rows), BF16),
+        ],
+        in_specs=[VMEM] * (1 + len(parts)),
+        out_specs=[VMEM] * 3,
+        compiler_params=params,
+        cost_estimate=pl.CostEstimate(
+            flops=0, bytes_accessed=LAYOUT_BYTES, transcendentals=0
+        ),
+        name="layout",
+    )(facts, *parts)
+    halves = 2
+    n_kv = KEY_VALUE_HEADS // halves
+    half = width // halves
+
+    def attention(h, before, up_shapes):
         return pl.pallas_call(
-            functools.partial(attention_kernel, len(halos), by_slot, h * n_kv, n_kv),
+            functools.partial(attention_kernel, by_slot, h * n_kv, n_kv),
             out_shape=[jax.ShapeDtypeStruct((half, tok), BF16)] + up_shapes,
-            in_specs=[VMEM] + [ANY] * 2 + [VMEM] * (1 + len(halos) + len(before)),
+            in_specs=[VMEM] * 3 + [ANY] * 2 + [VMEM] * len(before),
             out_specs=[VMEM] * (1 + len(up_shapes)),
             scratch_shapes=[
                 pltpu.VMEM((tok, half), BF16),
                 pltpu.VMEM((tok, half), BF16),
                 pltpu.SemaphoreType.DMA((n_kv,)),
                 pltpu.SemaphoreType.DMA((n_kv,)),
-                pltpu.VMEM((n_kv, key_rows, 2 * HEAD_SIZE), BF16),
-                pltpu.VMEM((key_rows, kv_width), BF16),
-                pltpu.VMEM((kv_width, key_rows), BF16),
             ],
             compiler_params=params,
             cost_estimate=pl.CostEstimate(
@@ -276,14 +273,15 @@
                 transcendentals=tok * key_rows * QUERY_HEADS // halves,
             ),
             name="attention_%d" % h,
-        )(facts, queries, output_gradient, own[h], *halos, *before)
-
-    (dq_a,) = attention(0, halo_a, [], [])
-    if by_slot:
-        halo_b, dq_a, w = lax.optimization_barrier((halo_b, dq_a, w))
+        )(*laid_out, queries, output_gradient, *before)
+
+    (dq_a,) = attention(0, [], [])
+    if by_slot:
+        dq_a, w = lax.optimization_barrier((dq_a, w))
+        w = jnp.concatenate(w, axis=0)
         up_weight = [w, partnered(w, n_seq, 1)]
     up_shape = jax.ShapeDtypeStruct((n_head, n_groups // n_out, rank, part), BF16)
-    dq_b, *up = attention(1, halo_b, [adapter_activation.T, dq_a], [up_shape] * n_out)
+    dq_b, *up = attention(1, [facts, adapter_activation.T, dq_a], [up_shape] * n_out)
 
     if by_slot:
         up, up_weight = lax.optimization_barrier((up, up_weight))
@@ -314,8 +312,20 @@
     )(facts, inputs, rank_low)
 
     if by_slot:
-        up = over_chips(over_z(up, n_head).astype(BF16), n_seq)
-        down = over_z(over_chips(over_cores(down, n_seq), n_seq).astype(BF16), n_head)
+        down = pl.pallas_call(
+            sum_kernel,
+            out_shape=[jax.ShapeDtypeStruct(down[0].shape[1:], BF16)] * down[0].shape[0],
+            in_specs=[VMEM] * 2,
+            out_specs=[VMEM] * down[0].shape[0],
+            compiler_params=params,
+            cost_estimate=pl.CostEstimate(flops=0, bytes_accessed=SUM_BYTES, transcendentals=0),
+            name="core_sum",
+        )(down[0], partnered(down[1], n_seq, 1))
+        down_got = [partnered(down[m], n_seq, 2 * m) for m in range(1, n_seq // 2)]
+        up_got = [shifted(up[j], n_head, j) for j in range(1, n_head)]
+        down_got, up_got = lax.optimization_barrier((down_got, up_got))
+        up = over_chips(added(up[0], up_got).astype(BF16), n_seq)
+        down = over_z(added(down[0], down_got).astype(BF16), n_head)
     else:
         up = lax.all_to_all(up[0], "head", split_axis=0, concat_axis=0, tiled=True)
         up = spread(jnp.sum(up.astype(F32), axis=0), segment_adapter, owner, n_seq)
@@ -329,18 +339,19 @@
     return (keep.astype(F32) + partnered(send, n_seq, 1).astype(F32)).astype(BF16)
 
 
+def added(own, got):
+    total = own.astype(F32)
+    for piece in got:
+        total = total + piece.astype(F32)
+    return total
+
+
 def over_chips(both, n_seq):
-    total = both[0].astype(F32)
-    for m in range(1, n_seq // 2):
-        total = total + partnered(both[m], n_seq, 2 * m).astype(F32)
-    return total
+    return added(both[0], [partnered(both[m], n_seq, 2 * m) for m in range(1, n_seq // 2)])
 
 
 def over_z(both, n_head):
-    total = both[0].astype(F32)
-    for j in range(1, n_head):
-        total = total + shifted(both[j], n_head, j).astype(F32)
-    return total
+    return added(both[0], [shifted(both[j], n_head, j) for j in range(1, n_head)])
 
 
 def spread(part, segment_adapter, owner, n_seq):

time: 71.5 us -> 67.7 us (0.947)
  starting transfers between devices: 40.5 us -> 30.8 us
  waiting for transfers between devices: 12.6 us -> 18 us
  local copies, waits for them, and re-layouts: 2.97 us -> 3.85 us
    ppermute x9, starting transfers between devices: 20.6 us -> 11.9 us  [shifted(): lax.ppermute(x, 'head', [(i, (i + j) % n_head) for i in range(n_head)])]
    ppermute x12, waiting for transfers between devices: 3.5 us -> 6.34 us  [partnered(): return lax.ppermute(x, 'seq', [(i, i ^ bits) for i in range(n_seq)])]
    ppermute x9, waiting for transfers between devices: 9.09 us -> 11.7 us  [shifted(): lax.ppermute(x, 'head', [(i, (i + j) % n_head) for i in range(n_head)])]
    unnamed x8 -> x14, local copies, waits for them, and re-layouts: 1.23 us -> 2.18 us
    slice x1, local copies, waits for them, and re-layouts: 0.95 us -> 0.01 us  [on_device(): parts.insert(0, lax.ppermute(own[tok - rows:], 'head', shift))]
    concatenate x0 -> x2, local copies, waits for them, and re-layouts: none -> 0.93 us  [the longest x1 0.92 us: on_device(): own = jnp.concatenate([keys, values], axis=1)]
    ppermute x4 -> x2, starting transfers between devices: 7.6 us -> 7.2 us  [on_device(): parts.insert(0, lax.ppermute(own[tok - rows:], 'head', shift))]
    pallas_call x2 -> x4, Pallas kernels: 7.38 us -> 7.62 us  [the longest x2 7.16 us: attention(): pl.pallas_call(functools.partial(attention_kernel, by_slot, h * n_kv, n_k...]
  transfers between devices with their start and end apart: 25 -> 23, of which waited for: 7 -> 10; matrix products, arithmetic and copies ran while one was open for 9% -> 10% of each run, Pallas kernels for 11% -> 12%
where the time goes in v7:
time: 67.7 us; the launch traced here: 67.4 us
  starting transfers between devices  30.8 us (45%)
  waiting for transfers between devices  18 us (27%)
  Pallas kernels  8.78 us (13%)
  other arithmetic  4.97 us (7%)
  local copies, waits for them, and re-layouts  3.85 us (6%)
  between operations  0.92 us (1%)
    ppermute x9, starting transfers between devices, shifted(): lax.ppermute(x, 'head', [(i, (i + j) % n_head) for i in range(n_head)])  11.9 us
    ppermute x12, starting transfers between devices, partnered(): return lax.ppermute(x, 'seq', [(i, i ^ bits) for i in range(n_seq)])  11.7 us
    ppermute x9, waiting for transfers between devices, shifted(): lax.ppermute(x, 'head', [(i, (i + j) % n_head) for i in range(n_head)])  11.7 us
    ppermute x2, starting transfers between devices, on_device(): parts.insert(0, lax.ppermute(own[tok - rows:], 'head', shift))  7.2 us
    pallas_call x2, Pallas kernels, attention(): pl.pallas_call(functools.partial(attention_kernel, by_slot, h * n_kv, n_k...  7.16 us
    ppermute x12, waiting for transfers between devices, partnered(): return lax.ppermute(x, 'seq', [(i, i ^ bits) for i in range(n_seq)])  6.34 us
    unnamed x14, local copies, waits for them, and re-layouts  2.18 us
  transfers between devices with their start and end apart: 23, of which 10 were waited for; matrix products, arithmetic and copies ran while one was open for 10% of the time, Pallas kernels for 12%

profile of v7, /device:TPU:0, one launch (start us, length us, event | category | flops | bytes accessed | tf_op | source)
XLA Modules:
  0.0 67.4 jit_solution(10990174847859509886)
XLA Ops:
  0.6 5.1 %collective-permute-start.4 = (bf16[1,16,1024]{2,1,0:T(8,128)(2,1)}, bf16[1,16,1024]{2,1,0:T(8,128)(2,1)S(1)}, u32[]{:S(2)}, u32[]{:S(2)}) collective-permute-start(bf16[1,16,1024]{2,1,0:T(8,128)(2,1)} %param.16), channel_id=1, source_target_pairs={{0,3},{1,0},{2,1},{3,2},{4,7},{5,4},{6,5},{7,6},{8,11},{9,8},{10,9... | collective-permute-start | bytes 98312 | tf_op jit(solution)/shard_map/ppermute | solution.py:193
  5.7 1.0 %collective-permute-start.2 = (bf16[1,16,1024]{2,1,0:T(8,128)(2,1)}, bf16[1,16,1024]{2,1,0:T(8,128)(2,1)S(1)}, u32[]{:S(2)}, u32[]{:S(2)}) collective-permute-start(bf16[1,16,1024]{2,1,0:T(8,128)(2,1)} %param.16), channel_id=1, source_target_pairs={{0,1},{1,2},{2,3},{3,0},{4,5},{5,6},{6,7},{7,4},{8,9},{9,10},{10,1... | collective-permute-start | bytes 98312 | tf_op jit(solution)/shard_map/ppermute | solution.py:193
  6.8 0.9 %constant_dynamic-update-slice_fusion.1 = bf16[128,1024]{1,0:T(8,128)(2,1)S(1)} fusion(bf16[128,512]{1,0:T(8,128)(2,1)} %param.11), kind=kLoop, calls=%fused_computation.30 | loop fusion | bytes 262144
  7.7 0.9 %constant_dynamic-update-slice_fusion.refs_2_ = bf16[128,1024]{1,0:T(8,128)(2,1)S(1)} fusion(bf16[128,1024]{1,0:T(8,128)(2,1)S(1)} %constant_dynamic-update-slice_fusion.1, bf16[128,512]{1,0:T(8,128)(2,1)} %param.12), kind=kLoop, calls=%fused_computation.29 | loop fusion | bytes 262144 | tf_op jit(solution)/shard_map/concatenate | solution.py:218
  8.6 4.4 %collective-permute-start.1 = (bf16[128,1024]{1,0:T(8,128)(2,1)S(1)}, bf16[128,1024]{1,0:T(8,128)(2,1)S(1)}, u32[]{:S(2)}, u32[]{:S(2)}) collective-permute-start(bf16[128,1024]{1,0:T(8,128)(2,1)S(1)} %constant_dynamic-update-slice_fusion.refs_2_), channel_id=1, source_target_pairs={{0,1},{1,2},{2,3},{4,5},{5,6},{6,7},{8,9},{9,10},{10,11},{12,13},{... | collective-permute-start | bytes 786440 | tf_op jit(solution)/shard_map/ppermute | solution.py:222
  13.0 2.8 %collective-permute-start = (bf16[64,1024]{1,0:T(8,128)(2,1)S(1)}, bf16[64,1024]{1,0:T(8,128)(2,1)S(1)}, u32[]{:S(2)}, u32[]{:S(2)}) collective-permute-start(bf16[64,1024]{1,0:T(8,128)(2,1)S(1)} %slice.52), channel_id=1, source_target_pairs={{0,2},{1,3},{4,6},{5,7},{8,10},{9,11},{12,14},{13,15},{16,18},{17,... | collective-permute-start | bytes 393224 | tf_op jit(solution)/shard_map/ppermute | solution.py:222
  15.8 0.8 %select_reduce_fusion.2 = s32[8]{0:T(128)S(1)} fusion(s32[8]{0:T(128)} %bitcast.49), kind=kLoop, calls=%fused_computation.37 | loop fusion | flops 184 | bytes 64 | tf_op jit(solution)/shard_map/reduce_sum | solution.py:180
  16.6 0.7 bitcast_add_fusion
  17.3 0.9 %select_reduce_fusion.1 = s32[8]{0:T(128)S(1)} fusion(s32[8]{0:T(128)} %param.19, s32[8]{0:T(128)} %bitcast.47), kind=kLoop, calls=%fused_computation.35 | loop fusion | flops 184 | bytes 96 | tf_op jit(solution)/shard_map/reduce_sum | solution.py:183
  18.2 0.7 %stack.15 = s32[8,8]{1,0:T(8,128)S(1)} concatenate(s32[1,8]{1,0:T(1,128)S(1)} %bitcast.46, s32[1,8]{1,0:T(1,128)} %param.18, s32[1,8]{1,0:T(1,128)S(1)} %bitcast.48, s32[1,8]{1,0:T(1,128)S(1)} %broadcast.49, s32[4,8]{1,0:T(4,128)S(1)} %stack.14), dimensions={0} | concatenate | bytes 512 | tf_op jit(solution)/shard_map/stack | solution.py:188
  18.9 0.8 %maximum_bitcast_fusion = bf16[1,4,16,1024]{3,2,1,0:T(8,128)(2,1)S(1)} fusion(bf16[1,16,1024]{2,1,0:T(8,128)(2,1)S(1)} %collective-permute-done.4, bf16[1,16,1024]{2,1,0:T(8,128)(2,1)S(1)} %collective-permute-done.3, bf16[1,16,1024]{2,1,0:T(8,128)(2,1)S(1)} %collective-permute-done.2, bf16[1,16,1024]{2,1,0:T(8,128)(2,1)} %param.16), kind=kLoop, calls=%fused_computation.6 | loop fusion | flops 196608 | bytes 262144 | tf_op jit(solution)/shard_map/broadcast_in_dim | solution.py:226
  19.7 1.6 %collective-permute-start.5 = (bf16[1,4,16,1024]{3,2,1,0:T(8,128)(2,1)S(1)}, bf16[1,4,16,1024]{3,2,1,0:T(8,128)(2,1)S(1)}, u32[]{:S(2)}, u32[]{:S(2)}) collective-permute-start(bf16[1,4,16,1024]{3,2,1,0:T(8,128)(2,1)S(1)} %maximum_bitcast_fusion), channel_id=1, source_target_pairs={{0,8},{4,12},{8,0},{12,4},{16,24},{20,28},{24,16},{28,20},{1,9},{5... | collective-permute-start | bytes 393224 | tf_op jit(solution)/shard_map/ppermute | solution.py:197
  21.3 1.5 %collective-permute-start.6 = (bf16[1,4,16,1024]{3,2,1,0:T(8,128)(2,1)S(1)}, bf16[1,4,16,1024]{3,2,1,0:T(8,128)(2,1)S(1)}, u32[]{:S(2)}, u32[]{:S(2)}) collective-permute-start(bf16[1,4,16,1024]{3,2,1,0:T(8,128)(2,1)S(1)} %maximum_bitcast_fusion), channel_id=1, source_target_pairs={{0,16},{4,20},{8,24},{12,28},{16,0},{20,4},{24,8},{28,12},{1,17},{... | collective-permute-start | bytes 393224 | tf_op jit(solution)/shard_map/ppermute | solution.py:197
  22.8 0.5 collective-permute-start.7
  23.2 0.1 select_reduce_fusion.facts_ref.refs_0_
  23.4 0.2 layout.1
  23.6 1.2 %copy-done.1 = bf16[128,4096]{1,0:T(8,128)(2,1)S(1)} copy-done((bf16[128,4096]{1,0:T(8,128)(2,1)S(1)}, bf16[128,4096]{1,0:T(8,128)(2,1)}, u32[]{:S(2)}) %copy-start.1) | copy-done | bytes 1048600
  24.8 3.4 %attention_0.1.refs_2_ = bf16[2048,128]{1,0:T(8,128)(2,1)S(1)} custom-call(bf16[4,320,256]{2,1,0:T(8,128)(2,1)S(1)} %get-tuple-element.31.k_all, bf16[320,512]{1,0:T(8,128)(2,1)S(1)} %get-tuple-element.32.v_all, bf16[512,320]{1,0:T(8,128)(2,1)S(1)} %get-tuple-element.33.k_turned, bf16[128,4096]{1,0:T(8,128)(2,1)S(1)} %copy-done, bf16[128,4096]{1,0:T(8,128)(2,1)S(1)} %copy-done.1), custom_call_target="tpu_custom_call" | custom-call | flops 503316480 | bytes 2097152 | tf_op jit(solution)/shard_map/attention_0/pallas_call | solution.py:258
  28.2 0.6 collective-permute-done.6
  29.0 3.8 %attention_1.1 = (bf16[2048,128]{1,0:T(8,128)(2,1)S(1)}, bf16[4,4,16,1024]{3,2,1,0:T(8,128)(2,1)S(1)}, bf16[4,4,16,1024]{3,2,1,0:T(8,128)(2,1)S(1)}) custom-call(bf16[4,320,256]{2,1,0:T(8,128)(2,1)S(1)} %get-tuple-element.31.k_all, bf16[320,512]{1,0:T(8,128)(2,1)S(1)} %get-tuple-element.32.v_all, bf16[512,320]{1,0:T(8,128)(2,1)S(1)} %get-tuple-element.33.k_turned, ...), custom_call_target="tpu_custom_call" | custom-call | flops 503316480 | bytes 2097152 | tf_op jit(solution)/shard_map/attention_1/pallas_call | solution.py:258
  32.8 0.5 collective-permute-start.9
  33.4 0.5 rank_gradient.1.rank_ref
  33.8 1.1 %collective-permute-done.9 = bf16[4,4,16,1024]{3,2,1,0:T(8,128)(2,1)S(1)} collective-permute-done((bf16[4,4,16,1024]{3,2,1,0:T(8,128)(2,1)S(1)}, bf16[4,4,16,1024]{3,2,1,0:T(8,128)(2,1)S(1)}, u32[]{:S(2)}, u32[]{:S(2)}) %collective-permute-start.9) | collective-permute-done | bytes 524320 | tf_op jit(solution)/shard_map/ppermute | solution.py:197
  34.9 0.2 add_convert_fusion
  35.1 0.7 %down_parts.1 = (bf16[4,4,16,2048]{3,2,1,0:T(8,128)(2,1)S(1)}, bf16[4,4,16,2048]{3,2,1,0:T(8,128)(2,1)S(1)}) custom-call(s32[8,128]{1,0:T(8,128)S(1)} %select_reduce_fusion.facts_ref.refs_0_, bf16[128,8192]{1,0:T(8,128)(2,1)S(1)} %copy-done.3, bf16[16,128]{1,0:T(8,128)(2,1)S(1)} %rank_gradient.1.rank_ref), custom_call_target="tpu_custom_call" | custom-call | flops 268435456 | bytes 8388608 | tf_op jit(solution)/shard_map/down_parts/pallas_call | solution.py:300
  35.8 0.4 collective-permute-start.10
  36.4 2.2 %collective-permute-done.10.b_ref = bf16[4,4,16,2048]{3,2,1,0:T(8,128)(2,1)S(1)} collective-permute-done((bf16[4,4,16,2048]{3,2,1,0:T(8,128)(2,1)S(1)}, bf16[4,4,16,2048]{3,2,1,0:T(8,128)(2,1)S(1)}, u32[]{:S(2)}, u32[]{:S(2)}) %collective-permute-start.10) | collective-permute-done | bytes 1048608 | tf_op jit(solution)/shard_map/ppermute | solution.py:197
  38.5 0.2 core_sum.1
  38.8 1.0 %collective-permute-start.11 = (bf16[4,16,2048]{2,1,0:T(8,128)(2,1)S(1)}, bf16[4,16,2048]{2,1,0:T(8,128)(2,1)S(1)}, u32[]{:S(2)}, u32[]{:S(2)}) collective-permute-start(bf16[4,16,2048]{2,1,0:T(8,128)(2,1)S(1)} %get-tuple-element.50), channel_id=1, source_target_pairs={{0,8},{4,12},{8,0},{12,4},{16,24},{20,28},{24,16},{28,20},{1,9},{5... | collective-permute-start | bytes 786440 | tf_op jit(solution)/shard_map/ppermute | solution.py:197
  39.8 1.5 %collective-permute-start.12 = (bf16[4,16,2048]{2,1,0:T(8,128)(2,1)S(1)}, bf16[4,16,2048]{2,1,0:T(8,128)(2,1)S(1)}, u32[]{:S(2)}, u32[]{:S(2)}) collective-permute-start(bf16[4,16,2048]{2,1,0:T(8,128)(2,1)S(1)} %get-tuple-element.51), channel_id=1, source_target_pairs={{0,16},{4,20},{8,24},{12,28},{16,0},{20,4},{24,8},{28,12},{1,17},{... | collective-permute-start | bytes 786440 | tf_op jit(solution)/shard_map/ppermute | solution.py:197
  41.3 1.1 %collective-permute-start.13 = (bf16[4,16,2048]{2,1,0:T(8,128)(2,1)S(1)}, bf16[4,16,2048]{2,1,0:T(8,128)(2,1)S(1)}, u32[]{:S(2)}, u32[]{:S(2)}) collective-permute-start(bf16[4,16,2048]{2,1,0:T(8,128)(2,1)S(1)} %get-tuple-element.52), channel_id=1, source_target_pairs={{0,24},{4,28},{8,16},{12,20},{16,8},{20,12},{24,0},{28,4},{1,25},{... | collective-permute-start | bytes 786440 | tf_op jit(solution)/shard_map/ppermute | solution.py:197
  42.4 0.8 %collective-permute-start.15 = (bf16[4,16,1024]{2,1,0:T(8,128)(2,1)S(1)}, bf16[4,16,1024]{2,1,0:T(8,128)(2,1)S(1)}, u32[]{:S(2)}, u32[]{:S(2)}) collective-permute-start(bf16[4,16,1024]{2,1,0:T(8,128)(2,1)S(1)} %get-tuple-element.61), channel_id=1, source_target_pairs={{0,2},{1,3},{2,0},{3,1},{4,6},{5,7},{6,4},{7,5},{8,10},{9,11},{10,... | collective-permute-start | bytes 393224 | tf_op jit(solution)/shard_map/ppermute | solution.py:193
  43.2 0.5 collective-permute-done.14
  43.7 1.1 %collective-permute-start.16 = (bf16[4,16,1024]{2,1,0:T(8,128)(2,1)S(1)}, bf16[4,16,1024]{2,1,0:T(8,128)(2,1)S(1)}, u32[]{:S(2)}, u32[]{:S(2)}) collective-permute-start(bf16[4,16,1024]{2,1,0:T(8,128)(2,1)S(1)} %get-tuple-element.60), channel_id=1, source_target_pairs={{0,3},{1,0},{2,1},{3,2},{4,7},{5,4},{6,5},{7,6},{8,11},{9,8},{10,9... | collective-permute-start | bytes 393224 | tf_op jit(solution)/shard_map/ppermute | solution.py:193
  44.8 6.1 %collective-permute-done.15 = bf16[4,16,1024]{2,1,0:T(8,128)(2,1)S(1)} collective-permute-done((bf16[4,16,1024]{2,1,0:T(8,128)(2,1)S(1)}, bf16[4,16,1024]{2,1,0:T(8,128)(2,1)S(1)}, u32[]{:S(2)}, u32[]{:S(2)}) %collective-permute-start.15) | collective-permute-done | bytes 131104 | tf_op jit(solution)/shard_map/ppermute | solution.py:193
  50.9 0.3 collective-permute-done.16
  51.2 2.4 %collective-permute-done.12 = bf16[4,16,2048]{2,1,0:T(8,128)(2,1)S(1)} collective-permute-done((bf16[4,16,2048]{2,1,0:T(8,128)(2,1)S(1)}, bf16[4,16,2048]{2,1,0:T(8,128)(2,1)S(1)}, u32[]{:S(2)}, u32[]{:S(2)}) %collective-permute-start.12) | collective-permute-done | bytes 262176 | tf_op jit(solution)/shard_map/ppermute | solution.py:197
  53.8 1.7 %collective-permute-start.22 = (bf16[16,1024]{1,0:T(8,128)(2,1)S(1)}, bf16[16,1024]{1,0:T(8,128)(2,1)S(1)}, u32[]{:S(2)}, u32[]{:S(2)}) collective-permute-start(bf16[16,1024]{1,0:T(8,128)(2,1)S(1)} %get-tuple-element.67), channel_id=1, source_target_pairs={{0,24},{4,28},{8,16},{12,20},{16,8},{20,12},{24,0},{28,4},{1,25},{... | collective-permute-start | bytes 98312 | tf_op jit(solution)/shard_map/ppermute | solution.py:197
  55.4 1.1 %collective-permute-start.21 = (bf16[16,1024]{1,0:T(8,128)(2,1)S(1)}, bf16[16,1024]{1,0:T(8,128)(2,1)S(1)}, u32[]{:S(2)}, u32[]{:S(2)}) collective-permute-start(bf16[16,1024]{1,0:T(8,128)(2,1)S(1)} %get-tuple-element.68), channel_id=1, source_target_pairs={{0,16},{4,20},{8,24},{12,28},{16,0},{20,4},{24,8},{28,12},{1,17},{... | collective-permute-start | bytes 98312 | tf_op jit(solution)/shard_map/ppermute | solution.py:197
  56.5 0.8 %collective-permute-start.20 = (bf16[16,1024]{1,0:T(8,128)(2,1)S(1)}, bf16[16,1024]{1,0:T(8,128)(2,1)S(1)}, u32[]{:S(2)}, u32[]{:S(2)}) collective-permute-start(bf16[16,1024]{1,0:T(8,128)(2,1)S(1)} %get-tuple-element.66), channel_id=1, source_target_pairs={{0,8},{4,12},{8,0},{12,4},{16,24},{20,28},{24,16},{28,20},{1,9},{5... | collective-permute-start | bytes 98312 | tf_op jit(solution)/shard_map/ppermute | solution.py:197
  57.3 0.1 add_convert_fusion.1
  57.5 3.1 %collective-permute-start.19 = (bf16[16,2048]{1,0:T(8,128)(2,1)S(1)}, bf16[16,2048]{1,0:T(8,128)(2,1)S(1)}, u32[]{:S(2)}, u32[]{:S(2)}) collective-permute-start(bf16[16,2048]{1,0:T(8,128)(2,1)S(1)} %get-tuple-element.64), channel_id=1, source_target_pairs={{0,3},{1,0},{2,1},{3,2},{4,7},{5,4},{6,5},{7,6},{8,11},{9,8},{10,9... | collective-permute-start | bytes 196616 | tf_op jit(solution)/shard_map/ppermute | solution.py:193
  60.6 0.6 collective-permute-start.17
  61.2 0.7 fusion.10
  61.9 0.6 collective-permute-done.19
  62.5 3.3 %collective-permute-done.18 = bf16[16,2048]{1,0:T(8,128)(2,1)S(1)} collective-permute-done((bf16[16,2048]{1,0:T(8,128)(2,1)S(1)}, bf16[16,2048]{1,0:T(8,128)(2,1)S(1)}, u32[]{:S(2)}, u32[]{:S(2)}) %collective-permute-start.18) | collective-permute-done | bytes 65568 | tf_op jit(solution)/shard_map/ppermute | solution.py:193
  65.8 0.9 %collective-permute-done.17 = bf16[16,2048]{1,0:T(8,128)(2,1)S(1)} collective-permute-done((bf16[16,2048]{1,0:T(8,128)(2,1)S(1)}, bf16[16,2048]{1,0:T(8,128)(2,1)S(1)}, u32[]{:S(2)}, u32[]{:S(2)}) %collective-permute-start.17) | collective-permute-done | bytes 65568 | tf_op jit(solution)/shard_map/ppermute | solution.py:193
  66.7 0.7 %fusion.6 = f32[1,2048,16]{1,2,0:T(8,128)} fusion(bf16[16,2048]{1,0:T(8,128)(2,1)S(1)} %collective-permute-done.19, bf16[16,2048]{1,0:T(8,128)(2,1)S(1)} %collective-permute-done.18, bf16[16,2048]{1,0:T(8,128)(2,1)S(1)} %collective-permute-done.17, bf16[4,16,2048]{2,1,0:T(8,128)(2,1)S(1)} %add_convert_fusion.1), kind=kLoop, calls=%fused_computation.11 | loop fusion | flops 262144 | bytes 393216 | tf_op jit(solution)/shard_map/mul | solution.py:334
  (39 shorter events, 0.5 us)
Async XLA Ops:
  0.6 23.0 %copy-start = (bf16[128,4096]{1,0:T(8,128)(2,1)S(1)}, bf16[128,4096]{1,0:T(8,128)(2,1)}, u32[]{:S(2)}) copy-start(bf16[128,4096]{1,0:T(8,128)(2,1)} %q_hbm.3) | copy-start | bytes 3145732
  0.6 18.2 %collective-permute-start.4 = (bf16[1,16,1024]{2,1,0:T(8,128)(2,1)}, bf16[1,16,1024]{2,1,0:T(8,128)(2,1)S(1)}, u32[]{:S(2)}, u32[]{:S(2)}) collective-permute-start(bf16[1,16,1024]{2,1,0:T(8,128)(2,1)} %param.16), channel_id=1, source_target_pairs={{0,3},{1,0},{2,1},{3,2},{4,7},{5,4},{6,5},{7,6},{8,11},{9,8},{10,9... | collective-permute-start | bytes 98312 | tf_op jit(solution)/shard_map/ppermute | solution.py:193
  5.7 13.2 %collective-permute-start.3 = (bf16[1,16,1024]{2,1,0:T(8,128)(2,1)}, bf16[1,16,1024]{2,1,0:T(8,128)(2,1)S(1)}, u32[]{:S(2)}, u32[]{:S(2)}) collective-permute-start(bf16[1,16,1024]{2,1,0:T(8,128)(2,1)} %param.16), channel_id=1, source_target_pairs={{0,2},{1,3},{2,0},{3,1},{4,6},{5,7},{6,4},{7,5},{8,10},{9,11},{10,... | collective-permute-start | bytes 98312 | tf_op jit(solution)/shard_map/ppermute | solution.py:193
  5.7 13.2 %collective-permute-start.2 = (bf16[1,16,1024]{2,1,0:T(8,128)(2,1)}, bf16[1,16,1024]{2,1,0:T(8,128)(2,1)S(1)}, u32[]{:S(2)}, u32[]{:S(2)}) collective-permute-start(bf16[1,16,1024]{2,1,0:T(8,128)(2,1)} %param.16), channel_id=1, source_target_pairs={{0,1},{1,2},{2,3},{3,0},{4,5},{5,6},{6,7},{7,4},{8,9},{9,10},{10,1... | collective-permute-start | bytes 98312 | tf_op jit(solution)/shard_map/ppermute | solution.py:193
  8.6 14.8 %collective-permute-start.1 = (bf16[128,1024]{1,0:T(8,128)(2,1)S(1)}, bf16[128,1024]{1,0:T(8,128)(2,1)S(1)}, u32[]{:S(2)}, u32[]{:S(2)}) collective-permute-start(bf16[128,1024]{1,0:T(8,128)(2,1)S(1)} %constant_dynamic-update-slice_fusion.refs_2_), channel_id=1, source_target_pairs={{0,1},{1,2},{2,3},{4,5},{5,6},{6,7},{8,9},{9,10},{10,11},{12,13},{... | collective-permute-start | bytes 786440 | tf_op jit(solution)/shard_map/ppermute | solution.py:222
  13.0 10.3 %collective-permute-start = (bf16[64,1024]{1,0:T(8,128)(2,1)S(1)}, bf16[64,1024]{1,0:T(8,128)(2,1)S(1)}, u32[]{:S(2)}, u32[]{:S(2)}) collective-permute-start(bf16[64,1024]{1,0:T(8,128)(2,1)S(1)} %slice.52), channel_id=1, source_target_pairs={{0,2},{1,3},{4,6},{5,7},{8,10},{9,11},{12,14},{13,15},{16,18},{17,... | collective-permute-start | bytes 393224 | tf_op jit(solution)/shard_map/ppermute | solution.py:222
  19.7 8.5 %collective-permute-start.5 = (bf16[1,4,16,1024]{3,2,1,0:T(8,128)(2,1)S(1)}, bf16[1,4,16,1024]{3,2,1,0:T(8,128)(2,1)S(1)}, u32[]{:S(2)}, u32[]{:S(2)}) collective-permute-start(bf16[1,4,16,1024]{3,2,1,0:T(8,128)(2,1)S(1)} %maximum_bitcast_fusion), channel_id=1, source_target_pairs={{0,8},{4,12},{8,0},{12,4},{16,24},{20,28},{24,16},{28,20},{1,9},{5... | collective-permute-start | bytes 393224 | tf_op jit(solution)/shard_map/ppermute | solution.py:197
  21.3 7.6 %collective-permute-start.6 = (bf16[1,4,16,1024]{3,2,1,0:T(8,128)(2,1)S(1)}, bf16[1,4,16,1024]{3,2,1,0:T(8,128)(2,1)S(1)}, u32[]{:S(2)}, u32[]{:S(2)}) collective-permute-start(bf16[1,4,16,1024]{3,2,1,0:T(8,128)(2,1)S(1)} %maximum_bitcast_fusion), channel_id=1, source_target_pairs={{0,16},{4,20},{8,24},{12,28},{16,0},{20,4},{24,8},{28,12},{1,17},{... | collective-permute-start | bytes 393224 | tf_op jit(solution)/shard_map/ppermute | solution.py:197
  22.8 6.1 %collective-permute-start.7 = (bf16[1,4,16,1024]{3,2,1,0:T(8,128)(2,1)S(1)}, bf16[1,4,16,1024]{3,2,1,0:T(8,128)(2,1)S(1)}, u32[]{:S(2)}, u32[]{:S(2)}) collective-permute-start(bf16[1,4,16,1024]{3,2,1,0:T(8,128)(2,1)S(1)} %maximum_bitcast_fusion), channel_id=1, source_target_pairs={{0,24},{4,28},{8,16},{12,20},{16,8},{20,12},{24,0},{28,4},{1,25},{... | collective-permute-start | bytes 393224 | tf_op jit(solution)/shard_map/ppermute | solution.py:197
  23.6 1.2 %copy-start.1 = (bf16[128,4096]{1,0:T(8,128)(2,1)S(1)}, bf16[128,4096]{1,0:T(8,128)(2,1)}, u32[]{:S(2)}) copy-start(bf16[128,4096]{1,0:T(8,128)(2,1)} %g_hbm.3) | copy-start | bytes 3145732
  24.8 4.2 %copy-start.2 = (bf16[128,4096]{1,0:T(8,128)(2,1)S(1)}, bf16[128,4096]{1,0:T(8,128)(2,1)}, u32[]{:S(2)}) copy-start(bf16[128,4096]{1,0:T(8,128)(2,1)} %g_hbm.3) | copy-start | bytes 3145732
  24.8 4.2 %copy-start.4 = (bf16[128,16]{0,1:T(8,128)(2,1)S(1)}, bf16[128,16]{0,1:T(8,128)(2,1)}, u32[]{:S(2)}) copy-start(bf16[128,16]{0,1:T(8,128)(2,1)} %param.15) | copy-start | bytes 12292
  28.9 3.9 %collective-permute-start.8 = (bf16[4,4,16,1024]{3,2,1,0:T(8,128)(2,1)S(1)}, bf16[4,4,16,1024]{3,2,1,0:T(8,128)(2,1)S(1)}, u32[]{:S(2)}, u32[]{:S(2)}) collective-permute-start(bf16[4,4,16,1024]{3,2,1,0:T(8,128)(2,1)S(1)} %constant_dynamic-update-slice_fusion.2.refs_0_), channel_id=1, source_target_pairs={{0,4},{4,0},{8,12},{12,8},{16,20},{20,16},{24,28},{28,24},{1,5},{5... | collective-permute-start | bytes 1572872 | tf_op jit(solution)/shard_map/ppermute | solution.py:197
  32.8 2.3 %copy-start.3 = (bf16[128,8192]{1,0:T(8,128)(2,1)S(1)}, bf16[128,8192]{1,0:T(8,128)(2,1)}, u32[]{:S(2)}) copy-start(bf16[128,8192]{1,0:T(8,128)(2,1)} %x_ref.1) | copy-start | bytes 6291460
  32.8 2.1 %collective-permute-start.9 = (bf16[4,4,16,1024]{3,2,1,0:T(8,128)(2,1)S(1)}, bf16[4,4,16,1024]{3,2,1,0:T(8,128)(2,1)S(1)}, u32[]{:S(2)}, u32[]{:S(2)}) collective-permute-start(bf16[4,4,16,1024]{3,2,1,0:T(8,128)(2,1)S(1)} %get-tuple-element.45), channel_id=1, source_target_pairs={{0,4},{4,0},{8,12},{12,8},{16,20},{20,16},{24,28},{28,24},{1,5},{5... | collective-permute-start | bytes 1572872 | tf_op jit(solution)/shard_map/ppermute | solution.py:197
  35.8 2.7 %collective-permute-start.10 = (bf16[4,4,16,2048]{3,2,1,0:T(8,128)(2,1)S(1)}, bf16[4,4,16,2048]{3,2,1,0:T(8,128)(2,1)S(1)}, u32[]{:S(2)}, u32[]{:S(2)}) collective-permute-start(bf16[4,4,16,2048]{3,2,1,0:T(8,128)(2,1)S(1)} %get-tuple-element.48), channel_id=1, source_target_pairs={{0,4},{4,0},{8,12},{12,8},{16,20},{20,16},{24,28},{28,24},{1,5},{5... | collective-permute-start | bytes 3145736 | tf_op jit(solution)/shard_map/ppermute | solution.py:197
  36.3 7.4 %collective-permute-start.14 = (bf16[4,16,1024]{2,1,0:T(8,128)(2,1)S(1)}, bf16[4,16,1024]{2,1,0:T(8,128)(2,1)S(1)}, u32[]{:S(2)}, u32[]{:S(2)}) collective-permute-start(bf16[4,16,1024]{2,1,0:T(8,128)(2,1)S(1)} %get-tuple-element.62), channel_id=1, source_target_pairs={{0,1},{1,2},{2,3},{3,0},{4,5},{5,6},{6,7},{7,4},{8,9},{9,10},{10,1... | collective-permute-start | bytes 393224 | tf_op jit(solution)/shard_map/ppermute | solution.py:193
  38.8 12.4 %collective-permute-start.11 = (bf16[4,16,2048]{2,1,0:T(8,128)(2,1)S(1)}, bf16[4,16,2048]{2,1,0:T(8,128)(2,1)S(1)}, u32[]{:S(2)}, u32[]{:S(2)}) collective-permute-start(bf16[4,16,2048]{2,1,0:T(8,128)(2,1)S(1)} %get-tuple-element.50), channel_id=1, source_target_pairs={{0,8},{4,12},{8,0},{12,4},{16,24},{20,28},{24,16},{28,20},{1,9},{5... | collective-permute-start | bytes 786440 | tf_op jit(solution)/shard_map/ppermute | solution.py:197
  39.8 13.9 %collective-permute-start.12 = (bf16[4,16,2048]{2,1,0:T(8,128)(2,1)S(1)}, bf16[4,16,2048]{2,1,0:T(8,128)(2,1)S(1)}, u32[]{:S(2)}, u32[]{:S(2)}) collective-permute-start(bf16[4,16,2048]{2,1,0:T(8,128)(2,1)S(1)} %get-tuple-element.51), channel_id=1, source_target_pairs={{0,16},{4,20},{8,24},{12,28},{16,0},{20,4},{24,8},{28,12},{1,17},{... | collective-permute-start | bytes 786440 | tf_op jit(solution)/shard_map/ppermute | solution.py:197
  41.3 12.4 %collective-permute-start.13 = (bf16[4,16,2048]{2,1,0:T(8,128)(2,1)S(1)}, bf16[4,16,2048]{2,1,0:T(8,128)(2,1)S(1)}, u32[]{:S(2)}, u32[]{:S(2)}) collective-permute-start(bf16[4,16,2048]{2,1,0:T(8,128)(2,1)S(1)} %get-tuple-element.52), channel_id=1, source_target_pairs={{0,24},{4,28},{8,16},{12,20},{16,8},{20,12},{24,0},{28,4},{1,25},{... | collective-permute-start | bytes 786440 | tf_op jit(solution)/shard_map/ppermute | solution.py:197
  42.4 8.6 %collective-permute-start.15 = (bf16[4,16,1024]{2,1,0:T(8,128)(2,1)S(1)}, bf16[4,16,1024]{2,1,0:T(8,128)(2,1)S(1)}, u32[]{:S(2)}, u32[]{:S(2)}) collective-permute-start(bf16[4,16,1024]{2,1,0:T(8,128)(2,1)S(1)} %get-tuple-element.61), channel_id=1, source_target_pairs={{0,2},{1,3},{2,0},{3,1},{4,6},{5,7},{6,4},{7,5},{8,10},{9,11},{10,... | collective-permute-start | bytes 393224 | tf_op jit(solution)/shard_map/ppermute | solution.py:193
  43.7 7.6 %collective-permute-start.16 = (bf16[4,16,1024]{2,1,0:T(8,128)(2,1)S(1)}, bf16[4,16,1024]{2,1,0:T(8,128)(2,1)S(1)}, u32[]{:S(2)}, u32[]{:S(2)}) collective-permute-start(bf16[4,16,1024]{2,1,0:T(8,128)(2,1)S(1)} %get-tuple-element.60), channel_id=1, source_target_pairs={{0,3},{1,0},{2,1},{3,2},{4,7},{5,4},{6,5},{7,6},{8,11},{9,8},{10,9... | collective-permute-start | bytes 393224 | tf_op jit(solution)/shard_map/ppermute | solution.py:193
  53.8 6.8 %collective-permute-start.22 = (bf16[16,1024]{1,0:T(8,128)(2,1)S(1)}, bf16[16,1024]{1,0:T(8,128)(2,1)S(1)}, u32[]{:S(2)}, u32[]{:S(2)}) collective-permute-start(bf16[16,1024]{1,0:T(8,128)(2,1)S(1)} %get-tuple-element.67), channel_id=1, source_target_pairs={{0,24},{4,28},{8,16},{12,20},{16,8},{20,12},{24,0},{28,4},{1,25},{... | collective-permute-start | bytes 98312 | tf_op jit(solution)/shard_map/ppermute | solution.py:197
  55.4 5.8 %collective-permute-start.21 = (bf16[16,1024]{1,0:T(8,128)(2,1)S(1)}, bf16[16,1024]{1,0:T(8,128)(2,1)S(1)}, u32[]{:S(2)}, u32[]{:S(2)}) collective-permute-start(bf16[16,1024]{1,0:T(8,128)(2,1)S(1)} %get-tuple-element.68), channel_id=1, source_target_pairs={{0,16},{4,20},{8,24},{12,28},{16,0},{20,4},{24,8},{28,12},{1,17},{... | collective-permute-start | bytes 98312 | tf_op jit(solution)/shard_map/ppermute | solution.py:197
  56.5 4.7 %collective-permute-start.20 = (bf16[16,1024]{1,0:T(8,128)(2,1)S(1)}, bf16[16,1024]{1,0:T(8,128)(2,1)S(1)}, u32[]{:S(2)}, u32[]{:S(2)}) collective-permute-start(bf16[16,1024]{1,0:T(8,128)(2,1)S(1)} %get-tuple-element.66), channel_id=1, source_target_pairs={{0,8},{4,12},{8,0},{12,4},{16,24},{20,28},{24,16},{28,20},{1,9},{5... | collective-permute-start | bytes 98312 | tf_op jit(solution)/shard_map/ppermute | solution.py:197
  57.5 5.0 %collective-permute-start.19 = (bf16[16,2048]{1,0:T(8,128)(2,1)S(1)}, bf16[16,2048]{1,0:T(8,128)(2,1)S(1)}, u32[]{:S(2)}, u32[]{:S(2)}) collective-permute-start(bf16[16,2048]{1,0:T(8,128)(2,1)S(1)} %get-tuple-element.64), channel_id=1, source_target_pairs={{0,3},{1,0},{2,1},{3,2},{4,7},{5,4},{6,5},{7,6},{8,11},{9,8},{10,9... | collective-permute-start | bytes 196616 | tf_op jit(solution)/shard_map/ppermute | solution.py:193
  60.6 5.2 %collective-permute-start.18 = (bf16[16,2048]{1,0:T(8,128)(2,1)S(1)}, bf16[16,2048]{1,0:T(8,128)(2,1)S(1)}, u32[]{:S(2)}, u32[]{:S(2)}) collective-permute-start(bf16[16,2048]{1,0:T(8,128)(2,1)S(1)} %get-tuple-element.65), channel_id=1, source_target_pairs={{0,2},{1,3},{2,0},{3,1},{4,6},{5,7},{6,4},{7,5},{8,10},{9,11},{10,... | collective-permute-start | bytes 196616 | tf_op jit(solution)/shard_map/ppermute | solution.py:193
  60.6 6.1 %collective-permute-start.17 = (bf16[16,2048]{1,0:T(8,128)(2,1)S(1)}, bf16[16,2048]{1,0:T(8,128)(2,1)S(1)}, u32[]{:S(2)}, u32[]{:S(2)}) collective-permute-start(bf16[16,2048]{1,0:T(8,128)(2,1)S(1)} %get-tuple-element.63), channel_id=1, source_target_pairs={{0,1},{1,2},{2,3},{3,0},{4,5},{5,6},{6,7},{7,4},{8,9},{9,10},{10,1... | collective-permute-start | bytes 196616 | tf_op jit(solution)/shard_map/ppermute | solution.py:193

commit v8 on v7

--- a/solution.py
+++ b/solution.py
@@ -36,7 +36,8 @@
 
 
 def layout_kernel(n_parts, facts_ref, *refs):
-    parts, (k_all, v_all, k_turned) = refs[:n_parts], refs[n_parts:]
+    own_turned, *parts = refs[: n_parts + 1]
+    k_all, v_all, k_turned, bias = refs[n_parts + 1 :]
     tok = facts_ref.shape[1]
     kv_width = v_all.shape[1]
     key_rows = v_all.shape[0]
@@ -46,20 +47,20 @@
         head * tok - (key_rows - tok) + lax.broadcasted_iota(I32, (key_rows, tok), 0)
     )
     allowed = (key_position >= facts_ref[0:1, :]) & (key_position <= position)
-    bias = jnp.where(allowed, 0.0, NEVER).astype(BF16)
+    bias[...] = jnp.where(allowed, 0.0, NEVER)
     for kv in range(KEY_VALUE_HEADS):
         start = 0
         at = slice(kv * HEAD_SIZE, (kv + 1) * HEAD_SIZE)
         for part in parts:
             rows = part.shape[0]
-            k_all[kv, start : start + rows, :HEAD_SIZE] = part[:, at]
+            k_all[start : start + rows, at] = part[:, at]
             v_all[start : start + rows, at] = part[:, kv_width + at.start : kv_width + at.stop]
             start += rows
-        k_all[kv, :, HEAD_SIZE:] = bias
-        k_turned[at, :] = k_all[kv, :, :HEAD_SIZE].T
-
-
-def attention_kernel(by_slot, first_kv, n_kv, k_all, v_all, k_turned, q_hbm, g_hbm, *refs):
+        k_turned[at, : start - tok] = k_all[: start - tok, at].T
+        k_turned[at, start - tok :] = own_turned[at, :]
+
+
+def attention_kernel(by_slot, first_kv, n_kv, k_all, v_all, k_turned, bias, q_hbm, g_hbm, *refs):
     before, refs = (refs[:3], refs[3:]) if first_kv else ((), refs)
     dq_turned, *up_refs, q_ref, g_ref, q_sem, g_sem = refs
     tok = q_ref.shape[0]
@@ -78,8 +79,6 @@
         for copy in fetch(kv):
             copy.start()
 
-    one = lax.broadcasted_iota(I32, (2 * tok, tok), 0) % tok
-    pick = (one == lax.broadcasted_iota(I32, (2 * tok, tok), 1)).astype(F32).astype(BF16)
     scale = 1.0 / HEAD_SIZE**0.5
     to_log2 = scale * math.log2(math.e)
 
@@ -87,7 +86,7 @@
         for copy in fetch(kv):
             copy.wait()
         at_kv = pl.ds(pl.multiple_of((first_kv + kv) * HEAD_SIZE, HEAD_SIZE), HEAD_SIZE)
-        k_g = k_all[first_kv + kv]
+        k_g = k_all[:, at_kv]
         v_g = v_all[:, at_kv]
         kt_g = k_turned[at_kv, :]
         for i in range(0, GROUP, 2):
@@ -97,7 +96,7 @@
             ]
             q_two = jnp.concatenate([q_ref[:, at[0]], q_ref[:, at[1]]], axis=0)
             g_two = jnp.concatenate([g_ref[:, at[0]], g_ref[:, at[1]]], axis=0)
-            s = dot(k_g, jnp.concatenate([q_two, pick], axis=1), 1, 1)
+            s = dot(k_g, q_two, 1, 1) + jnp.concatenate([bias[...]] * 2, axis=1)
             d_prob = dot(v_g, g_two, 1, 1)
             weights = jnp.exp2((s - jnp.max(s, axis=0, keepdims=True)) * to_log2)
             inverse = 1.0 / jnp.sum(weights, axis=0, keepdims=True)
@@ -238,18 +237,19 @@
     laid_out = pl.pallas_call(
         functools.partial(layout_kernel, len(parts)),
         out_shape=[
-            jax.ShapeDtypeStruct((KEY_VALUE_HEADS, key_rows, 2 * HEAD_SIZE), BF16),
+            jax.ShapeDtypeStruct((key_rows, keys.shape[1]), BF16),
             jax.ShapeDtypeStruct((key_rows, keys.shape[1]), BF16),
             jax.ShapeDtypeStruct((keys.shape[1], key_rows), BF16),
+            jax.ShapeDtypeStruct((key_rows, tok), F32),
         ],
-        in_specs=[VMEM] * (1 + len(parts)),
-        out_specs=[VMEM] * 3,
+        in_specs=[VMEM] * (2 + len(parts)),
+        out_specs=[VMEM] * 4,
         compiler_params=params,
         cost_estimate=pl.CostEstimate(
             flops=0, bytes_accessed=LAYOUT_BYTES, transcendentals=0
         ),
         name="layout",
-    )(facts, *parts)
+    )(facts, keys.T, *parts)
     halves = 2
     n_kv = KEY_VALUE_HEADS // halves
     half = width // halves
@@ -258,7 +258,7 @@
         return pl.pallas_call(
             functools.partial(attention_kernel, by_slot, h * n_kv, n_kv),
             out_shape=[jax.ShapeDtypeStruct((half, tok), BF16)] + up_shapes,
-            in_specs=[VMEM] * 3 + [ANY] * 2 + [VMEM] * len(before),
+            in_specs=[VMEM] * 4 + [ANY] * 2 + [VMEM] * len(before),
             out_specs=[VMEM] * (1 + len(up_shapes)),
             scratch_shapes=[
                 pltpu.VMEM((tok, half), BF16),
@@ -293,8 +293,6 @@
         compiler_params=params,
         name="rank_gradient",
     )(facts, *up_weight, dq_a, dq_b)
-    if by_slot:
-        rank_low, up = lax.optimization_barrier((rank_low, over_cores(up, n_seq)))
 
     down_shape = jax.ShapeDtypeStruct((n_groups // n_out, n_head, rank, x_part), BF16)
     down = pl.pallas_call(
@@ -322,10 +320,15 @@
             name="core_sum",
         )(down[0], partnered(down[1], n_seq, 1))
         down_got = [partnered(down[m], n_seq, 2 * m) for m in range(1, n_seq // 2)]
+        up = over_cores(up, n_seq)
         up_got = [shifted(up[j], n_head, j) for j in range(1, n_head)]
         down_got, up_got = lax.optimization_barrier((down_got, up_got))
-        up = over_chips(added(up[0], up_got).astype(BF16), n_seq)
-        down = over_z(added(down[0], down_got).astype(BF16), n_head)
+        up = added(up[0], up_got).astype(BF16)
+        down = added(down[0], down_got).astype(BF16)
+        up_got = [partnered(up[m], n_seq, 2 * m) for m in range(1, n_seq // 2)]
+        down_got = [shifted(down[j], n_head, j) for j in range(1, n_head)]
+        down_got, up_got = lax.optimization_barrier((down_got, up_got))
+        up, down = added(up[0], up_got), added(down[0], down_got)
     else:
         up = lax.all_to_all(up[0], "head", split_axis=0, concat_axis=0, tiled=True)
         up = spread(jnp.sum(up.astype(F32), axis=0), segment_adapter, owner, n_seq)

time: 67.7 us -> 65.3 us (0.965)
  starting transfers between devices: 30.8 us -> 28.1 us
    ppermute x2, starting transfers between devices: 7.2 us -> 4.39 us  [on_device(): parts.insert(0, lax.ppermute(own[tok - rows:], 'head', shift))]
    ppermute x9, starting transfers between devices: 11.9 us -> 12.7 us  [shifted(): lax.ppermute(x, 'head', [(i, (i + j) % n_head) for i in range(n_head)])]
    ppermute x12, waiting for transfers between devices: 6.34 us -> 7.15 us  [partnered(): return lax.ppermute(x, 'seq', [(i, i ^ bits) for i in range(n_seq)])]
    ppermute x12, starting transfers between devices: 11.7 us -> 11 us  [partnered(): return lax.ppermute(x, 'seq', [(i, i ^ bits) for i in range(n_seq)])]
    unnamed x14 -> x13, local copies, waits for them, and re-layouts: 2.18 us -> 1.99 us
  transfers between devices with their start and end apart: 23 -> 23, of which waited for: 10 -> 8; matrix products, arithmetic and copies ran while one was open for 10% -> 11% of each run, Pallas kernels for 12% -> 12%
where the time goes in v8:
time: 65.3 us; the launch traced here: 64.9 us
  starting transfers between devices  28.1 us (43%)
  waiting for transfers between devices  18.5 us (28%)
  Pallas kernels  8.8 us (13%)
  other arithmetic  4.97 us (8%)
  local copies, waits for them, and re-layouts  3.66 us (6%)
  between operations  0.95 us (1%)
    ppermute x9, starting transfers between devices, shifted(): lax.ppermute(x, 'head', [(i, (i + j) % n_head) for i in range(n_head)])  12.7 us
    ppermute x9, waiting for transfers between devices, shifted(): lax.ppermute(x, 'head', [(i, (i + j) % n_head) for i in range(n_head)])  11.3 us
    ppermute x12, starting transfers between devices, partnered(): return lax.ppermute(x, 'seq', [(i, i ^ bits) for i in range(n_seq)])  11 us
    ppermute x12, waiting for transfers between devices, partnered(): return lax.ppermute(x, 'seq', [(i, i ^ bits) for i in range(n_seq)])  7.15 us
    pallas_call x2, Pallas kernels, attention(): pl.pallas_call(functools.partial(attention_kernel, by_slot, h * n_kv, n_k...  7.14 us
    ppermute x2, starting transfers between devices, on_device(): parts.insert(0, lax.ppermute(own[tok - rows:], 'head', shift))  4.39 us
    unnamed x13, local copies, waits for them, and re-layouts  1.99 us
    mul x2, other arithmetic, on_device(): return (down.T[None] * ADAPTER_SCALE, up[None] * ADAPTER_SCALE)  1.34 us
  transfers between devices with their start and end apart: 23, of which 8 were waited for; matrix products, arithmetic and copies ran while one was open for 11% of the time, Pallas kernels for 12%

profile of v8, /device:TPU:0, one launch (start us, length us, event | category | flops | bytes accessed | tf_op | source)
XLA Modules:
  0.0 64.9 jit_solution(6127985334604375138)
XLA Ops:
  0.6 4.1 %collective-permute-start.3 = (bf16[1,16,1024]{2,1,0:T(8,128)(2,1)}, bf16[1,16,1024]{2,1,0:T(8,128)(2,1)S(1)}, u32[]{:S(2)}, u32[]{:S(2)}) collective-permute-start(bf16[1,16,1024]{2,1,0:T(8,128)(2,1)} %param.16), channel_id=1, source_target_pairs={{0,2},{1,3},{2,0},{3,1},{4,6},{5,7},{6,4},{7,5},{8,10},{9,11},{10,... | collective-permute-start | bytes 98312 | tf_op jit(solution)/shard_map/ppermute | solution.py:192
  4.8 1.6 %collective-permute-start.2 = (bf16[1,16,1024]{2,1,0:T(8,128)(2,1)}, bf16[1,16,1024]{2,1,0:T(8,128)(2,1)S(1)}, u32[]{:S(2)}, u32[]{:S(2)}) collective-permute-start(bf16[1,16,1024]{2,1,0:T(8,128)(2,1)} %param.16), channel_id=1, source_target_pairs={{0,1},{1,2},{2,3},{3,0},{4,5},{5,6},{6,7},{7,4},{8,9},{9,10},{10,1... | collective-permute-start | bytes 98312 | tf_op jit(solution)/shard_map/ppermute | solution.py:192
  6.3 2.2 %collective-permute-start.4 = (bf16[1,16,1024]{2,1,0:T(8,128)(2,1)}, bf16[1,16,1024]{2,1,0:T(8,128)(2,1)S(1)}, u32[]{:S(2)}, u32[]{:S(2)}) collective-permute-start(bf16[1,16,1024]{2,1,0:T(8,128)(2,1)} %param.16), channel_id=1, source_target_pairs={{0,3},{1,0},{2,1},{3,2},{4,7},{5,4},{6,5},{7,6},{8,11},{9,8},{10,9... | collective-permute-start | bytes 98312 | tf_op jit(solution)/shard_map/ppermute | solution.py:192
  8.6 0.9 %constant_dynamic-update-slice_fusion.1 = bf16[128,1024]{1,0:T(8,128)(2,1)S(1)} fusion(bf16[128,512]{1,0:T(8,128)(2,1)} %param.11), kind=kLoop, calls=%fused_computation.31 | loop fusion | bytes 262144
  9.5 0.9 %constant_dynamic-update-slice_fusion.refs_3_ = bf16[128,1024]{1,0:T(8,128)(2,1)S(1)} fusion(bf16[128,1024]{1,0:T(8,128)(2,1)S(1)} %constant_dynamic-update-slice_fusion.1, bf16[128,512]{1,0:T(8,128)(2,1)} %param.12), kind=kLoop, calls=%fused_computation.30 | loop fusion | bytes 262144 | tf_op jit(solution)/shard_map/concatenate | solution.py:217
  10.4 1.7 %collective-permute-start.1 = (bf16[128,1024]{1,0:T(8,128)(2,1)S(1)}, bf16[128,1024]{1,0:T(8,128)(2,1)S(1)}, u32[]{:S(2)}, u32[]{:S(2)}) collective-permute-start(bf16[128,1024]{1,0:T(8,128)(2,1)S(1)} %constant_dynamic-update-slice_fusion.refs_3_), channel_id=1, source_target_pairs={{0,1},{1,2},{2,3},{4,5},{5,6},{6,7},{8,9},{9,10},{10,11},{12,13},{... | collective-permute-start | bytes 786440 | tf_op jit(solution)/shard_map/ppermute | solution.py:221
  12.1 2.7 %collective-permute-start = (bf16[64,1024]{1,0:T(8,128)(2,1)S(1)}, bf16[64,1024]{1,0:T(8,128)(2,1)S(1)}, u32[]{:S(2)}, u32[]{:S(2)}) collective-permute-start(bf16[64,1024]{1,0:T(8,128)(2,1)S(1)} %slice.52), channel_id=1, source_target_pairs={{0,2},{1,3},{4,6},{5,7},{8,10},{9,11},{12,14},{13,15},{16,18},{17,... | collective-permute-start | bytes 393224 | tf_op jit(solution)/shard_map/ppermute | solution.py:221
  14.8 0.8 %select_reduce_fusion.2 = s32[8]{0:T(128)S(1)} fusion(s32[8]{0:T(128)} %bitcast.53), kind=kLoop, calls=%fused_computation.38 | loop fusion | flops 184 | bytes 64 | tf_op jit(solution)/shard_map/reduce_sum | solution.py:179
  15.6 0.7 %bitcast_add_fusion = s32[8]{0:T(128)S(1)} fusion(s32[8]{0:T(128)S(1)} %select_reduce_fusion.2, s32[1,8]{1,0:T(1,128)} %param.17), kind=kLoop, calls=%fused_computation.42 | loop fusion | flops 8 | bytes 96 | tf_op jit(solution)/shard_map/add | solution.py:186
  16.4 0.9 %select_reduce_fusion.1 = s32[8]{0:T(128)S(1)} fusion(s32[8]{0:T(128)} %param.19, s32[8]{0:T(128)} %bitcast.51), kind=kLoop, calls=%fused_computation.36 | loop fusion | flops 184 | bytes 96 | tf_op jit(solution)/shard_map/reduce_sum | solution.py:182
  17.2 1.0 %copy.13 = bf16[128,512]{0,1:T(8,128)(2,1)S(1)} copy(bf16[128,512]{1,0:T(8,128)(2,1)} %param.11) | data formatting | bytes 262144 | tf_op args[1]
  18.3 0.7 %stack.15 = s32[8,8]{1,0:T(8,128)S(1)} concatenate(s32[1,8]{1,0:T(1,128)S(1)} %bitcast.50, s32[1,8]{1,0:T(1,128)} %param.18, s32[1,8]{1,0:T(1,128)S(1)} %bitcast.52, s32[1,8]{1,0:T(1,128)S(1)} %broadcast.49, s32[4,8]{1,0:T(4,128)S(1)} %stack.14), dimensions={0} | concatenate | bytes 512 | tf_op jit(solution)/shard_map/stack | solution.py:187
  19.0 0.8 %maximum_bitcast_fusion = bf16[1,4,16,1024]{3,2,1,0:T(8,128)(2,1)S(1)} fusion(bf16[1,16,1024]{2,1,0:T(8,128)(2,1)S(1)} %collective-permute-done.4, bf16[1,16,1024]{2,1,0:T(8,128)(2,1)S(1)} %collective-permute-done.3, bf16[1,16,1024]{2,1,0:T(8,128)(2,1)S(1)} %collective-permute-done.2, bf16[1,16,1024]{2,1,0:T(8,128)(2,1)} %param.16), kind=kLoop, calls=%fused_computation.10 | loop fusion | flops 196608 | bytes 262144 | tf_op jit(solution)/shard_map/broadcast_in_dim | solution.py:225
  19.7 2.5 %collective-permute-start.7 = (bf16[1,4,16,1024]{3,2,1,0:T(8,128)(2,1)S(1)}, bf16[1,4,16,1024]{3,2,1,0:T(8,128)(2,1)S(1)}, u32[]{:S(2)}, u32[]{:S(2)}) collective-permute-start(bf16[1,4,16,1024]{3,2,1,0:T(8,128)(2,1)S(1)} %maximum_bitcast_fusion), channel_id=1, source_target_pairs={{0,24},{4,28},{8,16},{12,20},{16,8},{20,12},{24,0},{28,4},{1,25},{... | collective-permute-start | bytes 393224 | tf_op jit(solution)/shard_map/ppermute | solution.py:196
  22.3 0.5 collective-permute-start.6
  22.8 0.5 collective-permute-start.5
  23.3 0.1 select_reduce_fusion.facts_ref.refs_0_
  23.4 0.3 layout.1
  23.7 3.4 %attention_0.1.refs_2_ = bf16[2048,128]{1,0:T(8,128)(2,1)S(1)} custom-call(bf16[320,512]{1,0:T(8,128)(2,1)S(1)} %get-tuple-element.36.k_all, bf16[320,512]{1,0:T(8,128)(2,1)S(1)} %get-tuple-element.37.v_all, bf16[512,320]{1,0:T(8,128)(2,1)S(1)} %get-tuple-element.38.k_turned, f32[320,128]{1,0:T(8,128)S(1)} %get-tuple-element.39.bias, ...), custom_call_target="tpu_custom_call" | custom-call | flops 503316480 | bytes 2097152 | tf_op jit(solution)/shard_map/attention_0/pallas_call | solution.py:258
  27.1 0.7 %collective-permute-done.6 = bf16[1,4,16,1024]{3,2,1,0:T(8,128)(2,1)S(1)} collective-permute-done((bf16[1,4,16,1024]{3,2,1,0:T(8,128)(2,1)S(1)}, bf16[1,4,16,1024]{3,2,1,0:T(8,128)(2,1)S(1)}, u32[]{:S(2)}, u32[]{:S(2)}) %collective-permute-start.6) | collective-permute-done | bytes 131104 | tf_op jit(solution)/shard_map/ppermute | solution.py:196
  27.9 3.8 %attention_1.1 = (bf16[2048,128]{1,0:T(8,128)(2,1)S(1)}, bf16[4,4,16,1024]{3,2,1,0:T(8,128)(2,1)S(1)}, bf16[4,4,16,1024]{3,2,1,0:T(8,128)(2,1)S(1)}) custom-call(bf16[320,512]{1,0:T(8,128)(2,1)S(1)} %get-tuple-element.36.k_all, bf16[320,512]{1,0:T(8,128)(2,1)S(1)} %get-tuple-element.37.v_all, bf16[512,320]{1,0:T(8,128)(2,1)S(1)} %get-tuple-element.38.k_turned, ...), custom_call_target="tpu_custom_call" | custom-call | flops 503316480 | bytes 2097152 | tf_op jit(solution)/shard_map/attention_1/pallas_call | solution.py:258
  31.7 0.5 rank_gradient.1.rank_ref
  32.2 0.7 %down_parts.1 = (bf16[4,4,16,2048]{3,2,1,0:T(8,128)(2,1)S(1)}, bf16[4,4,16,2048]{3,2,1,0:T(8,128)(2,1)S(1)}) custom-call(s32[8,128]{1,0:T(8,128)S(1)} %select_reduce_fusion.facts_ref.refs_0_, bf16[128,8192]{1,0:T(8,128)(2,1)S(1)} %copy-done.2, bf16[16,128]{1,0:T(8,128)(2,1)S(1)} %rank_gradient.1.rank_ref), custom_call_target="tpu_custom_call" | custom-call | flops 268435456 | bytes 8388608 | tf_op jit(solution)/shard_map/down_parts/pallas_call | solution.py:298
  32.9 0.5 collective-permute-start.9
  33.4 0.1 collective-permute-start.13
  33.5 3.0 %collective-permute-done.13 = bf16[4,4,16,1024]{3,2,1,0:T(8,128)(2,1)S(1)} collective-permute-done((bf16[4,4,16,1024]{3,2,1,0:T(8,128)(2,1)S(1)}, bf16[4,4,16,1024]{3,2,1,0:T(8,128)(2,1)S(1)}, u32[]{:S(2)}, u32[]{:S(2)}) %collective-permute-start.13) | collective-permute-done | bytes 524320 | tf_op jit(solution)/shard_map/ppermute | solution.py:196
  36.5 0.2 add_convert_fusion
  36.7 1.8 %collective-permute-start.16 = (bf16[4,16,1024]{2,1,0:T(8,128)(2,1)S(1)}, bf16[4,16,1024]{2,1,0:T(8,128)(2,1)S(1)}, u32[]{:S(2)}, u32[]{:S(2)}) collective-permute-start(bf16[4,16,1024]{2,1,0:T(8,128)(2,1)S(1)} %get-tuple-element.70), channel_id=1, source_target_pairs={{0,3},{1,0},{2,1},{3,2},{4,7},{5,4},{6,5},{7,6},{8,11},{9,8},{10,9... | collective-permute-start | bytes 393224 | tf_op jit(solution)/shard_map/ppermute | solution.py:192
  38.5 0.2 core_sum.1
  38.7 1.6 %collective-permute-start.10 = (bf16[4,16,2048]{2,1,0:T(8,128)(2,1)S(1)}, bf16[4,16,2048]{2,1,0:T(8,128)(2,1)S(1)}, u32[]{:S(2)}, u32[]{:S(2)}) collective-permute-start(bf16[4,16,2048]{2,1,0:T(8,128)(2,1)S(1)} %get-tuple-element.53), channel_id=1, source_target_pairs={{0,8},{4,12},{8,0},{12,4},{16,24},{20,28},{24,16},{28,20},{1,9},{5... | collective-permute-start | bytes 786440 | tf_op jit(solution)/shard_map/ppermute | solution.py:196
  40.3 1.5 %collective-permute-start.11 = (bf16[4,16,2048]{2,1,0:T(8,128)(2,1)S(1)}, bf16[4,16,2048]{2,1,0:T(8,128)(2,1)S(1)}, u32[]{:S(2)}, u32[]{:S(2)}) collective-permute-start(bf16[4,16,2048]{2,1,0:T(8,128)(2,1)S(1)} %get-tuple-element.54), channel_id=1, source_target_pairs={{0,16},{4,20},{8,24},{12,28},{16,0},{20,4},{24,8},{28,12},{1,17},{... | collective-permute-start | bytes 786440 | tf_op jit(solution)/shard_map/ppermute | solution.py:196
  41.8 0.5 collective-permute-start.12
  42.3 0.3 collective-permute-done.16
  42.5 0.3 collective-permute-start.14
  42.9 10.3 %collective-permute-done.15 = bf16[4,16,1024]{2,1,0:T(8,128)(2,1)S(1)} collective-permute-done((bf16[4,16,1024]{2,1,0:T(8,128)(2,1)S(1)}, bf16[4,16,1024]{2,1,0:T(8,128)(2,1)S(1)}, u32[]{:S(2)}, u32[]{:S(2)}) %collective-permute-start.15) | collective-permute-done | bytes 131104 | tf_op jit(solution)/shard_map/ppermute | solution.py:192
  53.2 0.7 %collective-permute-done.11 = bf16[4,16,2048]{2,1,0:T(8,128)(2,1)S(1)} collective-permute-done((bf16[4,16,2048]{2,1,0:T(8,128)(2,1)S(1)}, bf16[4,16,2048]{2,1,0:T(8,128)(2,1)S(1)}, u32[]{:S(2)}, u32[]{:S(2)}) %collective-permute-start.11) | collective-permute-done | bytes 262176 | tf_op jit(solution)/shard_map/ppermute | solution.py:196
  54.0 1.6 %collective-permute-start.22 = (bf16[16,1024]{1,0:T(8,128)(2,1)S(1)}, bf16[16,1024]{1,0:T(8,128)(2,1)S(1)}, u32[]{:S(2)}, u32[]{:S(2)}) collective-permute-start(bf16[16,1024]{1,0:T(8,128)(2,1)S(1)} %get-tuple-element.76), channel_id=1, source_target_pairs={{0,24},{4,28},{8,16},{12,20},{16,8},{20,12},{24,0},{28,4},{1,25},{... | collective-permute-start | bytes 98312 | tf_op jit(solution)/shard_map/ppermute | solution.py:196
  55.5 0.1 add_convert_fusion.1
  55.7 0.4 collective-permute-start.19
  56.1 1.4 %collective-permute-start.18 = (bf16[16,2048]{1,0:T(8,128)(2,1)S(1)}, bf16[16,2048]{1,0:T(8,128)(2,1)S(1)}, u32[]{:S(2)}, u32[]{:S(2)}) collective-permute-start(bf16[16,2048]{1,0:T(8,128)(2,1)S(1)} %get-tuple-element.74), channel_id=1, source_target_pairs={{0,2},{1,3},{2,0},{3,1},{4,6},{5,7},{6,4},{7,5},{8,10},{9,11},{10,... | collective-permute-start | bytes 196616 | tf_op jit(solution)/shard_map/ppermute | solution.py:192
  57.5 0.9 %collective-permute-start.17 = (bf16[16,2048]{1,0:T(8,128)(2,1)S(1)}, bf16[16,2048]{1,0:T(8,128)(2,1)S(1)}, u32[]{:S(2)}, u32[]{:S(2)}) collective-permute-start(bf16[16,2048]{1,0:T(8,128)(2,1)S(1)} %get-tuple-element.75), channel_id=1, source_target_pairs={{0,1},{1,2},{2,3},{3,0},{4,5},{5,6},{6,7},{7,4},{8,9},{9,10},{10,1... | collective-permute-start | bytes 196616 | tf_op jit(solution)/shard_map/ppermute | solution.py:192
  58.5 0.5 collective-permute-start.21
  59.0 1.1 %collective-permute-start.20 = (bf16[16,1024]{1,0:T(8,128)(2,1)S(1)}, bf16[16,1024]{1,0:T(8,128)(2,1)S(1)}, u32[]{:S(2)}, u32[]{:S(2)}) collective-permute-start(bf16[16,1024]{1,0:T(8,128)(2,1)S(1)} %get-tuple-element.78), channel_id=1, source_target_pairs={{0,8},{4,12},{8,0},{12,4},{16,24},{20,28},{24,16},{28,20},{1,9},{5... | collective-permute-start | bytes 98312 | tf_op jit(solution)/shard_map/ppermute | solution.py:196
  60.1 2.3 %collective-permute-done.21 = bf16[16,1024]{1,0:T(8,128)(2,1)S(1)} collective-permute-done((bf16[16,1024]{1,0:T(8,128)(2,1)S(1)}, bf16[16,1024]{1,0:T(8,128)(2,1)S(1)}, u32[]{:S(2)}, u32[]{:S(2)}) %collective-permute-start.21) | collective-permute-done | bytes 32800 | tf_op jit(solution)/shard_map/ppermute | solution.py:196
  62.4 0.5 collective-permute-done.20
  62.9 0.7 %collective-permute-done.17 = bf16[16,2048]{1,0:T(8,128)(2,1)S(1)} collective-permute-done((bf16[16,2048]{1,0:T(8,128)(2,1)S(1)}, bf16[16,2048]{1,0:T(8,128)(2,1)S(1)}, u32[]{:S(2)}, u32[]{:S(2)}) %collective-permute-start.17) | collective-permute-done | bytes 65568 | tf_op jit(solution)/shard_map/ppermute | solution.py:192
  63.6 0.7 %fusion.10 = f32[1,16,1024]{2,1,0:T(8,128)} fusion(bf16[16,1024]{1,0:T(8,128)(2,1)S(1)} %collective-permute-done.22, bf16[16,1024]{1,0:T(8,128)(2,1)S(1)} %collective-permute-done.21, bf16[16,1024]{1,0:T(8,128)(2,1)S(1)} %collective-permute-done.20, bf16[4,16,1024]{2,1,0:T(8,128)(2,1)S(1)} %fusion.2), kind=kLoop, calls=%fused_computation.24 | loop fusion | flops 131072 | bytes 196608 | tf_op jit(solution)/shard_map/mul | solution.py:337
  64.3 0.7 %fusion.6 = f32[1,2048,16]{1,2,0:T(8,128)} fusion(bf16[16,2048]{1,0:T(8,128)(2,1)S(1)} %collective-permute-done.19, bf16[16,2048]{1,0:T(8,128)(2,1)S(1)} %collective-permute-done.18, bf16[16,2048]{1,0:T(8,128)(2,1)S(1)} %collective-permute-done.17, bf16[4,16,2048]{2,1,0:T(8,128)(2,1)S(1)} %add_convert_fusion.1), kind=kLoop, calls=%fused_computation.15 | loop fusion | flops 262144 | bytes 393216 | tf_op jit(solution)/shard_map/mul | solution.py:337
  (38 shorter events, 0.4 us)
Async XLA Ops:
  0.6 23.0 %copy-start.1 = (bf16[128,4096]{1,0:T(8,128)(2,1)S(1)}, bf16[128,4096]{1,0:T(8,128)(2,1)}, u32[]{:S(2)}) copy-start(bf16[128,4096]{1,0:T(8,128)(2,1)} %g_hbm.3) | copy-start | bytes 3145732
  0.6 23.0 %copy-start = (bf16[128,4096]{1,0:T(8,128)(2,1)S(1)}, bf16[128,4096]{1,0:T(8,128)(2,1)}, u32[]{:S(2)}) copy-start(bf16[128,4096]{1,0:T(8,128)(2,1)} %q_hbm.3) | copy-start | bytes 3145732
  0.6 18.3 %collective-permute-start.3 = (bf16[1,16,1024]{2,1,0:T(8,128)(2,1)}, bf16[1,16,1024]{2,1,0:T(8,128)(2,1)S(1)}, u32[]{:S(2)}, u32[]{:S(2)}) collective-permute-start(bf16[1,16,1024]{2,1,0:T(8,128)(2,1)} %param.16), channel_id=1, source_target_pairs={{0,2},{1,3},{2,0},{3,1},{4,6},{5,7},{6,4},{7,5},{8,10},{9,11},{10,... | collective-permute-start | bytes 98312 | tf_op jit(solution)/shard_map/ppermute | solution.py:192
  4.8 14.2 %collective-permute-start.2 = (bf16[1,16,1024]{2,1,0:T(8,128)(2,1)}, bf16[1,16,1024]{2,1,0:T(8,128)(2,1)S(1)}, u32[]{:S(2)}, u32[]{:S(2)}) collective-permute-start(bf16[1,16,1024]{2,1,0:T(8,128)(2,1)} %param.16), channel_id=1, source_target_pairs={{0,1},{1,2},{2,3},{3,0},{4,5},{5,6},{6,7},{7,4},{8,9},{9,10},{10,1... | collective-permute-start | bytes 98312 | tf_op jit(solution)/shard_map/ppermute | solution.py:192
  6.3 12.6 %collective-permute-start.4 = (bf16[1,16,1024]{2,1,0:T(8,128)(2,1)}, bf16[1,16,1024]{2,1,0:T(8,128)(2,1)S(1)}, u32[]{:S(2)}, u32[]{:S(2)}) collective-permute-start(bf16[1,16,1024]{2,1,0:T(8,128)(2,1)} %param.16), channel_id=1, source_target_pairs={{0,3},{1,0},{2,1},{3,2},{4,7},{5,4},{6,5},{7,6},{8,11},{9,8},{10,9... | collective-permute-start | bytes 98312 | tf_op jit(solution)/shard_map/ppermute | solution.py:192
  10.4 13.0 %collective-permute-start.1 = (bf16[128,1024]{1,0:T(8,128)(2,1)S(1)}, bf16[128,1024]{1,0:T(8,128)(2,1)S(1)}, u32[]{:S(2)}, u32[]{:S(2)}) collective-permute-start(bf16[128,1024]{1,0:T(8,128)(2,1)S(1)} %constant_dynamic-update-slice_fusion.refs_3_), channel_id=1, source_target_pairs={{0,1},{1,2},{2,3},{4,5},{5,6},{6,7},{8,9},{9,10},{10,11},{12,13},{... | collective-permute-start | bytes 786440 | tf_op jit(solution)/shard_map/ppermute | solution.py:221
  12.1 11.3 %collective-permute-start = (bf16[64,1024]{1,0:T(8,128)(2,1)S(1)}, bf16[64,1024]{1,0:T(8,128)(2,1)S(1)}, u32[]{:S(2)}, u32[]{:S(2)}) collective-permute-start(bf16[64,1024]{1,0:T(8,128)(2,1)S(1)} %slice.52), channel_id=1, source_target_pairs={{0,2},{1,3},{4,6},{5,7},{8,10},{9,11},{12,14},{13,15},{16,18},{17,... | collective-permute-start | bytes 393224 | tf_op jit(solution)/shard_map/ppermute | solution.py:221
  19.7 7.3 %collective-permute-start.7 = (bf16[1,4,16,1024]{3,2,1,0:T(8,128)(2,1)S(1)}, bf16[1,4,16,1024]{3,2,1,0:T(8,128)(2,1)S(1)}, u32[]{:S(2)}, u32[]{:S(2)}) collective-permute-start(bf16[1,4,16,1024]{3,2,1,0:T(8,128)(2,1)S(1)} %maximum_bitcast_fusion), channel_id=1, source_target_pairs={{0,24},{4,28},{8,16},{12,20},{16,8},{20,12},{24,0},{28,4},{1,25},{... | collective-permute-start | bytes 393224 | tf_op jit(solution)/shard_map/ppermute | solution.py:196
  22.3 5.5 %collective-permute-start.6 = (bf16[1,4,16,1024]{3,2,1,0:T(8,128)(2,1)S(1)}, bf16[1,4,16,1024]{3,2,1,0:T(8,128)(2,1)S(1)}, u32[]{:S(2)}, u32[]{:S(2)}) collective-permute-start(bf16[1,4,16,1024]{3,2,1,0:T(8,128)(2,1)S(1)} %maximum_bitcast_fusion), channel_id=1, source_target_pairs={{0,16},{4,20},{8,24},{12,28},{16,0},{20,4},{24,8},{28,12},{1,17},{... | collective-permute-start | bytes 393224 | tf_op jit(solution)/shard_map/ppermute | solution.py:196
  22.8 5.0 %collective-permute-start.5 = (bf16[1,4,16,1024]{3,2,1,0:T(8,128)(2,1)S(1)}, bf16[1,4,16,1024]{3,2,1,0:T(8,128)(2,1)S(1)}, u32[]{:S(2)}, u32[]{:S(2)}) collective-permute-start(bf16[1,4,16,1024]{3,2,1,0:T(8,128)(2,1)S(1)} %maximum_bitcast_fusion), channel_id=1, source_target_pairs={{0,8},{4,12},{8,0},{12,4},{16,24},{20,28},{24,16},{28,20},{1,9},{5... | collective-permute-start | bytes 393224 | tf_op jit(solution)/shard_map/ppermute | solution.py:196
  23.7 4.2 %copy-start.3 = (bf16[128,16]{0,1:T(8,128)(2,1)S(1)}, bf16[128,16]{0,1:T(8,128)(2,1)}, u32[]{:S(2)}) copy-start(bf16[128,16]{0,1:T(8,128)(2,1)} %param.15) | copy-start | bytes 12292
  27.8 3.9 %collective-permute-start.8 = (bf16[4,4,16,1024]{3,2,1,0:T(8,128)(2,1)S(1)}, bf16[4,4,16,1024]{3,2,1,0:T(8,128)(2,1)S(1)}, u32[]{:S(2)}, u32[]{:S(2)}) collective-permute-start(bf16[4,4,16,1024]{3,2,1,0:T(8,128)(2,1)S(1)} %constant_dynamic-update-slice_fusion.2.refs_0_), channel_id=1, source_target_pairs={{0,4},{4,0},{8,12},{12,8},{16,20},{20,16},{24,28},{28,24},{1,5},{5... | collective-permute-start | bytes 1572872 | tf_op jit(solution)/shard_map/ppermute | solution.py:196
  27.9 4.3 %copy-start.2 = (bf16[128,8192]{1,0:T(8,128)(2,1)S(1)}, bf16[128,8192]{1,0:T(8,128)(2,1)}, u32[]{:S(2)}) copy-start(bf16[128,8192]{1,0:T(8,128)(2,1)} %x_ref.1) | copy-start | bytes 6291460
  32.9 5.5 %collective-permute-start.9 = (bf16[4,4,16,2048]{3,2,1,0:T(8,128)(2,1)S(1)}, bf16[4,4,16,2048]{3,2,1,0:T(8,128)(2,1)S(1)}, u32[]{:S(2)}, u32[]{:S(2)}) collective-permute-start(bf16[4,4,16,2048]{3,2,1,0:T(8,128)(2,1)S(1)} %get-tuple-element.51), channel_id=1, source_target_pairs={{0,4},{4,0},{8,12},{12,8},{16,20},{20,16},{24,28},{28,24},{1,5},{5... | collective-permute-start | bytes 3145736 | tf_op jit(solution)/shard_map/ppermute | solution.py:196
  33.4 3.0 %collective-permute-start.13 = (bf16[4,4,16,1024]{3,2,1,0:T(8,128)(2,1)S(1)}, bf16[4,4,16,1024]{3,2,1,0:T(8,128)(2,1)S(1)}, u32[]{:S(2)}, u32[]{:S(2)}) collective-permute-start(bf16[4,4,16,1024]{3,2,1,0:T(8,128)(2,1)S(1)} %get-tuple-element.57), channel_id=1, source_target_pairs={{0,4},{4,0},{8,12},{12,8},{16,20},{20,16},{24,28},{28,24},{1,5},{5... | collective-permute-start | bytes 1572872 | tf_op jit(solution)/shard_map/ppermute | solution.py:196
  36.7 5.8 %collective-permute-start.16 = (bf16[4,16,1024]{2,1,0:T(8,128)(2,1)S(1)}, bf16[4,16,1024]{2,1,0:T(8,128)(2,1)S(1)}, u32[]{:S(2)}, u32[]{:S(2)}) collective-permute-start(bf16[4,16,1024]{2,1,0:T(8,128)(2,1)S(1)} %get-tuple-element.70), channel_id=1, source_target_pairs={{0,3},{1,0},{2,1},{3,2},{4,7},{5,4},{6,5},{7,6},{8,11},{9,8},{10,9... | collective-permute-start | bytes 393224 | tf_op jit(solution)/shard_map/ppermute | solution.py:192
  38.7 14.5 %collective-permute-start.10 = (bf16[4,16,2048]{2,1,0:T(8,128)(2,1)S(1)}, bf16[4,16,2048]{2,1,0:T(8,128)(2,1)S(1)}, u32[]{:S(2)}, u32[]{:S(2)}) collective-permute-start(bf16[4,16,2048]{2,1,0:T(8,128)(2,1)S(1)} %get-tuple-element.53), channel_id=1, source_target_pairs={{0,8},{4,12},{8,0},{12,4},{16,24},{20,28},{24,16},{28,20},{1,9},{5... | collective-permute-start | bytes 786440 | tf_op jit(solution)/shard_map/ppermute | solution.py:196
  40.3 13.6 %collective-permute-start.11 = (bf16[4,16,2048]{2,1,0:T(8,128)(2,1)S(1)}, bf16[4,16,2048]{2,1,0:T(8,128)(2,1)S(1)}, u32[]{:S(2)}, u32[]{:S(2)}) collective-permute-start(bf16[4,16,2048]{2,1,0:T(8,128)(2,1)S(1)} %get-tuple-element.54), channel_id=1, source_target_pairs={{0,16},{4,20},{8,24},{12,28},{16,0},{20,4},{24,8},{28,12},{1,17},{... | collective-permute-start | bytes 786440 | tf_op jit(solution)/shard_map/ppermute | solution.py:196
  41.8 12.1 %collective-permute-start.12 = (bf16[4,16,2048]{2,1,0:T(8,128)(2,1)S(1)}, bf16[4,16,2048]{2,1,0:T(8,128)(2,1)S(1)}, u32[]{:S(2)}, u32[]{:S(2)}) collective-permute-start(bf16[4,16,2048]{2,1,0:T(8,128)(2,1)S(1)} %get-tuple-element.55), channel_id=1, source_target_pairs={{0,24},{4,28},{8,16},{12,20},{16,8},{20,12},{24,0},{28,4},{1,25},{... | collective-permute-start | bytes 786440 | tf_op jit(solution)/shard_map/ppermute | solution.py:196
  42.3 10.9 %collective-permute-start.15 = (bf16[4,16,1024]{2,1,0:T(8,128)(2,1)S(1)}, bf16[4,16,1024]{2,1,0:T(8,128)(2,1)S(1)}, u32[]{:S(2)}, u32[]{:S(2)}) collective-permute-start(bf16[4,16,1024]{2,1,0:T(8,128)(2,1)S(1)} %get-tuple-element.71), channel_id=1, source_target_pairs={{0,2},{1,3},{2,0},{3,1},{4,6},{5,7},{6,4},{7,5},{8,10},{9,11},{10,... | collective-permute-start | bytes 393224 | tf_op jit(solution)/shard_map/ppermute | solution.py:192
  42.5 10.7 %collective-permute-start.14 = (bf16[4,16,1024]{2,1,0:T(8,128)(2,1)S(1)}, bf16[4,16,1024]{2,1,0:T(8,128)(2,1)S(1)}, u32[]{:S(2)}, u32[]{:S(2)}) collective-permute-start(bf16[4,16,1024]{2,1,0:T(8,128)(2,1)S(1)} %get-tuple-element.72), channel_id=1, source_target_pairs={{0,1},{1,2},{2,3},{3,0},{4,5},{5,6},{6,7},{7,4},{8,9},{9,10},{10,1... | collective-permute-start | bytes 393224 | tf_op jit(solution)/shard_map/ppermute | solution.py:192
  54.0 5.0 %collective-permute-start.22 = (bf16[16,1024]{1,0:T(8,128)(2,1)S(1)}, bf16[16,1024]{1,0:T(8,128)(2,1)S(1)}, u32[]{:S(2)}, u32[]{:S(2)}) collective-permute-start(bf16[16,1024]{1,0:T(8,128)(2,1)S(1)} %get-tuple-element.76), channel_id=1, source_target_pairs={{0,24},{4,28},{8,16},{12,20},{16,8},{20,12},{24,0},{28,4},{1,25},{... | collective-permute-start | bytes 98312 | tf_op jit(solution)/shard_map/ppermute | solution.py:196
  55.7 7.2 %collective-permute-start.19 = (bf16[16,2048]{1,0:T(8,128)(2,1)S(1)}, bf16[16,2048]{1,0:T(8,128)(2,1)S(1)}, u32[]{:S(2)}, u32[]{:S(2)}) collective-permute-start(bf16[16,2048]{1,0:T(8,128)(2,1)S(1)} %get-tuple-element.73), channel_id=1, source_target_pairs={{0,3},{1,0},{2,1},{3,2},{4,7},{5,4},{6,5},{7,6},{8,11},{9,8},{10,9... | collective-permute-start | bytes 196616 | tf_op jit(solution)/shard_map/ppermute | solution.py:192
  56.1 6.8 %collective-permute-start.18 = (bf16[16,2048]{1,0:T(8,128)(2,1)S(1)}, bf16[16,2048]{1,0:T(8,128)(2,1)S(1)}, u32[]{:S(2)}, u32[]{:S(2)}) collective-permute-start(bf16[16,2048]{1,0:T(8,128)(2,1)S(1)} %get-tuple-element.74), channel_id=1, source_target_pairs={{0,2},{1,3},{2,0},{3,1},{4,6},{5,7},{6,4},{7,5},{8,10},{9,11},{10,... | collective-permute-start | bytes 196616 | tf_op jit(solution)/shard_map/ppermute | solution.py:192
  57.5 6.1 %collective-permute-start.17 = (bf16[16,2048]{1,0:T(8,128)(2,1)S(1)}, bf16[16,2048]{1,0:T(8,128)(2,1)S(1)}, u32[]{:S(2)}, u32[]{:S(2)}) collective-permute-start(bf16[16,2048]{1,0:T(8,128)(2,1)S(1)} %get-tuple-element.75), channel_id=1, source_target_pairs={{0,1},{1,2},{2,3},{3,0},{4,5},{5,6},{6,7},{7,4},{8,9},{9,10},{10,1... | collective-permute-start | bytes 196616 | tf_op jit(solution)/shard_map/ppermute | solution.py:192
  58.5 3.9 %collective-permute-start.21 = (bf16[16,1024]{1,0:T(8,128)(2,1)S(1)}, bf16[16,1024]{1,0:T(8,128)(2,1)S(1)}, u32[]{:S(2)}, u32[]{:S(2)}) collective-permute-start(bf16[16,1024]{1,0:T(8,128)(2,1)S(1)} %get-tuple-element.77), channel_id=1, source_target_pairs={{0,16},{4,20},{8,24},{12,28},{16,0},{20,4},{24,8},{28,12},{1,17},{... | collective-permute-start | bytes 98312 | tf_op jit(solution)/shard_map/ppermute | solution.py:196
  59.0 3.9 %collective-permute-start.20 = (bf16[16,1024]{1,0:T(8,128)(2,1)S(1)}, bf16[16,1024]{1,0:T(8,128)(2,1)S(1)}, u32[]{:S(2)}, u32[]{:S(2)}) collective-permute-start(bf16[16,1024]{1,0:T(8,128)(2,1)S(1)} %get-tuple-element.78), channel_id=1, source_target_pairs={{0,8},{4,12},{8,0},{12,4},{16,24},{20,28},{24,16},{28,20},{1,9},{5... | collective-permute-start | bytes 98312 | tf_op jit(solution)/shard_map/ppermute | solution.py:196

commit v9 on v8

--- a/solution.py
+++ b/solution.py
@@ -122,9 +122,8 @@
     for quarter in range(n_quarters):
         i, dq_ref = (quarter, dq_before) if quarter < n_before else (quarter - n_before, dq_turned)
         up = dot(act_cols, dq_ref[i * part : (i + 1) * part, :], 1, 1).astype(BF16)
-        j = lax.rem(quarter + n_quarters - head, n_quarters) if by_slot else quarter
         for n in range(n_groups):
-            up_refs[n // per][j, n % per] = up[n * rank : (n + 1) * rank, :]
+            up_refs[n // per][quarter, n % per] = up[n * rank : (n + 1) * rank, :]
 
 
 def rank_kernel(by_slot, n_w, facts_ref, *refs):
@@ -319,16 +318,9 @@
             cost_estimate=pl.CostEstimate(flops=0, bytes_accessed=SUM_BYTES, transcendentals=0),
             name="core_sum",
         )(down[0], partnered(down[1], n_seq, 1))
-        down_got = [partnered(down[m], n_seq, 2 * m) for m in range(1, n_seq // 2)]
-        up = over_cores(up, n_seq)
-        up_got = [shifted(up[j], n_head, j) for j in range(1, n_head)]
-        down_got, up_got = lax.optimization_barrier((down_got, up_got))
-        up = added(up[0], up_got).astype(BF16)
-        down = added(down[0], down_got).astype(BF16)
-        up_got = [partnered(up[m], n_seq, 2 * m) for m in range(1, n_seq // 2)]
-        down_got = [shifted(down[j], n_head, j) for j in range(1, n_head)]
-        down_got, up_got = lax.optimization_barrier((down_got, up_got))
-        up, down = added(up[0], up_got), added(down[0], down_got)
+        up = lax.all_to_all(over_cores(up, n_seq), "head", split_axis=0, concat_axis=0, tiled=True)
+        up = over_chips(jnp.sum(up.astype(F32), axis=0).astype(BF16), n_seq)
+        down = over_z(over_chips(down, n_seq).astype(BF16), n_head)
     else:
         up = lax.all_to_all(up[0], "head", split_axis=0, concat_axis=0, tiled=True)
         up = spread(jnp.sum(up.astype(F32), axis=0), segment_adapter, owner, n_seq)

time: 65.3 us -> 69.3 us (1.061)
  starting transfers between devices: 28.1 us -> 31.7 us
  other arithmetic: 4.97 us -> 6.83 us
  waiting for transfers between devices: 18.5 us -> 17 us
    all_to_all x0 -> x1, waiting for transfers between devices: none -> 11.5 us  [on_device(): lax.all_to_all(over_cores(up, n_seq), 'head', split_axis=0, concat_axis=0...]
    ppermute x9 -> x6, waiting for transfers between devices: 11.3 us -> 4.5 us  [shifted(): lax.ppermute(x, 'head', [(i, (i + j) % n_head) for i in range(n_head)])]
    ppermute x12, waiting for transfers between devices: 7.15 us -> 0.95 us  [partnered(): return lax.ppermute(x, 'seq', [(i, i ^ bits) for i in range(n_seq)])]
    all_to_all x0 -> x1, starting transfers between devices: none -> 4.14 us  [on_device(): lax.all_to_all(over_cores(up, n_seq), 'head', split_axis=0, concat_axis=0...]
    reduce_sum x0 -> x1, other arithmetic: none -> 1.13 us  [on_device(): up = over_chips(jnp.sum(up.astype(F32), axis=0).astype(BF16), n_seq)]
    ppermute x9 -> x6, starting transfers between devices: 12.7 us -> 11.8 us  [shifted(): lax.ppermute(x, 'head', [(i, (i + j) % n_head) for i in range(n_head)])]
    convert_element_type x1, other arithmetic: 0.19 us -> 1 us  [over_cores(): (keep.astype(F32) + partnered(send, n_seq, 1).astype(F32)).astype(BF16)]
  transfers between devices with their start and end apart: 23 -> 21, of which waited for: 8 -> 5; matrix products, arithmetic and copies ran while one was open for 11% -> 14% of each run, Pallas kernels for 12% -> 13%
where the time goes in v9:
time: 69.3 us; the launch traced here: 68.9 us
  starting transfers between devices  31.7 us (46%)
  waiting for transfers between devices  17 us (25%)
  Pallas kernels  8.79 us (13%)
  other arithmetic  6.83 us (10%)
  local copies, waits for them, and re-layouts  3.63 us (5%)
  between operations  0.97 us (1%)
    ppermute x6, starting transfers between devices, shifted(): lax.ppermute(x, 'head', [(i, (i + j) % n_head) for i in range(n_head)])  11.8 us
    all_to_all x1, waiting for transfers between devices, on_device(): lax.all_to_all(over_cores(up, n_seq), 'head', split_axis=0, concat_axis=0...  11.5 us
    ppermute x12, starting transfers between devices, partnered(): return lax.ppermute(x, 'seq', [(i, i ^ bits) for i in range(n_seq)])  11.4 us
    pallas_call x2, Pallas kernels, attention(): pl.pallas_call(functools.partial(attention_kernel, by_slot, h * n_kv, n_k...  7.14 us
    ppermute x6, waiting for transfers between devices, shifted(): lax.ppermute(x, 'head', [(i, (i + j) % n_head) for i in range(n_head)])  4.5 us
    ppermute x2, starting transfers between devices, on_device(): parts.insert(0, lax.ppermute(own[tok - rows:], 'head', shift))  4.39 us
    all_to_all x1, starting transfers between devices, on_device(): lax.all_to_all(over_cores(up, n_seq), 'head', split_axis=0, concat_axis=0...  4.14 us
    unnamed x13, local copies, waits for them, and re-layouts  1.99 us
  transfers between devices with their start and end apart: 21, of which 5 were waited for; matrix products, arithmetic and copies ran while one was open for 14% of the time, Pallas kernels for 13%

profile of v9, /device:TPU:0, one launch (start us, length us, event | category | flops | bytes accessed | tf_op | source)
XLA Modules:
  0.0 68.9 jit_solution(6744263531482004268)
XLA Ops:
  0.6 4.1 %collective-permute-start.3 = (bf16[1,16,1024]{2,1,0:T(8,128)(2,1)}, bf16[1,16,1024]{2,1,0:T(8,128)(2,1)S(1)}, u32[]{:S(2)}, u32[]{:S(2)}) collective-permute-start(bf16[1,16,1024]{2,1,0:T(8,128)(2,1)} %param.16), channel_id=1, source_target_pairs={{0,2},{1,3},{2,0},{3,1},{4,6},{5,7},{6,4},{7,5},{8,10},{9,11},{10,... | collective-permute-start | bytes 98312 | tf_op jit(solution)/shard_map/ppermute | solution.py:191
  4.8 1.6 %collective-permute-start.2 = (bf16[1,16,1024]{2,1,0:T(8,128)(2,1)}, bf16[1,16,1024]{2,1,0:T(8,128)(2,1)S(1)}, u32[]{:S(2)}, u32[]{:S(2)}) collective-permute-start(bf16[1,16,1024]{2,1,0:T(8,128)(2,1)} %param.16), channel_id=1, source_target_pairs={{0,1},{1,2},{2,3},{3,0},{4,5},{5,6},{6,7},{7,4},{8,9},{9,10},{10,1... | collective-permute-start | bytes 98312 | tf_op jit(solution)/shard_map/ppermute | solution.py:191
  6.3 2.2 %collective-permute-start.4 = (bf16[1,16,1024]{2,1,0:T(8,128)(2,1)}, bf16[1,16,1024]{2,1,0:T(8,128)(2,1)S(1)}, u32[]{:S(2)}, u32[]{:S(2)}) collective-permute-start(bf16[1,16,1024]{2,1,0:T(8,128)(2,1)} %param.16), channel_id=1, source_target_pairs={{0,3},{1,0},{2,1},{3,2},{4,7},{5,4},{6,5},{7,6},{8,11},{9,8},{10,9... | collective-permute-start | bytes 98312 | tf_op jit(solution)/shard_map/ppermute | solution.py:191
  8.6 0.9 %constant_dynamic-update-slice_fusion.1 = bf16[128,1024]{1,0:T(8,128)(2,1)S(1)} fusion(bf16[128,512]{1,0:T(8,128)(2,1)} %param.11), kind=kLoop, calls=%fused_computation.23 | loop fusion | bytes 262144
  9.5 0.9 %constant_dynamic-update-slice_fusion.refs_3_ = bf16[128,1024]{1,0:T(8,128)(2,1)S(1)} fusion(bf16[128,1024]{1,0:T(8,128)(2,1)S(1)} %constant_dynamic-update-slice_fusion.1, bf16[128,512]{1,0:T(8,128)(2,1)} %param.12), kind=kLoop, calls=%fused_computation.22 | loop fusion | bytes 262144 | tf_op jit(solution)/shard_map/concatenate | solution.py:216
  10.4 1.7 %collective-permute-start.1 = (bf16[128,1024]{1,0:T(8,128)(2,1)S(1)}, bf16[128,1024]{1,0:T(8,128)(2,1)S(1)}, u32[]{:S(2)}, u32[]{:S(2)}) collective-permute-start(bf16[128,1024]{1,0:T(8,128)(2,1)S(1)} %constant_dynamic-update-slice_fusion.refs_3_), channel_id=1, source_target_pairs={{0,1},{1,2},{2,3},{4,5},{5,6},{6,7},{8,9},{9,10},{10,11},{12,13},{... | collective-permute-start | bytes 786440 | tf_op jit(solution)/shard_map/ppermute | solution.py:220
  12.1 2.7 %collective-permute-start = (bf16[64,1024]{1,0:T(8,128)(2,1)S(1)}, bf16[64,1024]{1,0:T(8,128)(2,1)S(1)}, u32[]{:S(2)}, u32[]{:S(2)}) collective-permute-start(bf16[64,1024]{1,0:T(8,128)(2,1)S(1)} %slice.36), channel_id=1, source_target_pairs={{0,2},{1,3},{4,6},{5,7},{8,10},{9,11},{12,14},{13,15},{16,18},{17,... | collective-permute-start | bytes 393224 | tf_op jit(solution)/shard_map/ppermute | solution.py:220
  14.8 0.8 %select_reduce_fusion.2 = s32[8]{0:T(128)S(1)} fusion(s32[8]{0:T(128)} %bitcast.42), kind=kLoop, calls=%fused_computation.30 | loop fusion | flops 184 | bytes 64 | tf_op jit(solution)/shard_map/reduce_sum | solution.py:178
  15.6 0.7 bitcast_add_fusion
  16.3 0.1 compare_and_fusion
  16.4 0.9 %select_reduce_fusion.1 = s32[8]{0:T(128)S(1)} fusion(s32[8]{0:T(128)} %param.19, s32[8]{0:T(128)} %bitcast.40), kind=kLoop, calls=%fused_computation.28 | loop fusion | flops 184 | bytes 96 | tf_op jit(solution)/shard_map/reduce_sum | solution.py:181
  17.2 1.0 %copy.13 = bf16[128,512]{0,1:T(8,128)(2,1)S(1)} copy(bf16[128,512]{1,0:T(8,128)(2,1)} %param.11) | data formatting | bytes 262144 | tf_op args[1]
  18.3 0.7 stack.15
  19.0 0.8 %maximum_bitcast_fusion = bf16[1,4,16,1024]{3,2,1,0:T(8,128)(2,1)S(1)} fusion(bf16[1,16,1024]{2,1,0:T(8,128)(2,1)S(1)} %collective-permute-done.4, bf16[1,16,1024]{2,1,0:T(8,128)(2,1)S(1)} %collective-permute-done.3, bf16[1,16,1024]{2,1,0:T(8,128)(2,1)S(1)} %collective-permute-done.2, bf16[1,16,1024]{2,1,0:T(8,128)(2,1)} %param.16), kind=kLoop, calls=%fused_computation.2 | loop fusion | flops 196608 | bytes 262144 | tf_op jit(solution)/shard_map/broadcast_in_dim | solution.py:224
  19.7 2.5 %collective-permute-start.7 = (bf16[1,4,16,1024]{3,2,1,0:T(8,128)(2,1)S(1)}, bf16[1,4,16,1024]{3,2,1,0:T(8,128)(2,1)S(1)}, u32[]{:S(2)}, u32[]{:S(2)}) collective-permute-start(bf16[1,4,16,1024]{3,2,1,0:T(8,128)(2,1)S(1)} %maximum_bitcast_fusion), channel_id=1, source_target_pairs={{0,24},{4,28},{8,16},{12,20},{16,8},{20,12},{24,0},{28,4},{1,25},{... | collective-permute-start | bytes 393224 | tf_op jit(solution)/shard_map/ppermute | solution.py:195
  22.3 0.5 collective-permute-start.6
  22.8 0.5 collective-permute-start.5
  23.3 0.1 select_reduce_fusion.facts_ref.refs_0_
  23.4 0.3 layout.1
  23.7 0.0 copy-start.3
  23.7 3.4 %attention_0.1.refs_2_ = bf16[2048,128]{1,0:T(8,128)(2,1)S(1)} custom-call(bf16[320,512]{1,0:T(8,128)(2,1)S(1)} %get-tuple-element.24.k_all, bf16[320,512]{1,0:T(8,128)(2,1)S(1)} %get-tuple-element.25.v_all, bf16[512,320]{1,0:T(8,128)(2,1)S(1)} %get-tuple-element.26.k_turned, f32[320,128]{1,0:T(8,128)S(1)} %get-tuple-element.27.bias, ...), custom_call_target="tpu_custom_call" | custom-call | flops 503316480 | bytes 2097152 | tf_op jit(solution)/shard_map/attention_0/pallas_call | solution.py:257
  27.1 0.7 collective-permute-done.6
  27.8 0.1 collective-permute-start.8
  27.9 0.0 copy-start.2
  27.9 3.8 %attention_1.1 = (bf16[2048,128]{1,0:T(8,128)(2,1)S(1)}, bf16[4,4,16,1024]{3,2,1,0:T(8,128)(2,1)S(1)}, bf16[4,4,16,1024]{3,2,1,0:T(8,128)(2,1)S(1)}) custom-call(bf16[320,512]{1,0:T(8,128)(2,1)S(1)} %get-tuple-element.24.k_all, bf16[320,512]{1,0:T(8,128)(2,1)S(1)} %get-tuple-element.25.v_all, bf16[512,320]{1,0:T(8,128)(2,1)S(1)} %get-tuple-element.26.k_turned, ...), custom_call_target="tpu_custom_call" | custom-call | flops 503316480 | bytes 2097152 | tf_op jit(solution)/shard_map/attention_1/pallas_call | solution.py:257
  31.7 0.5 collective-permute-start.16
  32.3 0.4 rank_gradient.1.rank_ref
  32.7 0.7 %down_parts.1 = (bf16[4,4,16,2048]{3,2,1,0:T(8,128)(2,1)S(1)}, bf16[4,4,16,2048]{3,2,1,0:T(8,128)(2,1)S(1)}) custom-call(s32[8,128]{1,0:T(8,128)S(1)} %select_reduce_fusion.facts_ref.refs_0_, bf16[128,8192]{1,0:T(8,128)(2,1)S(1)} %copy-done.2, bf16[16,128]{1,0:T(8,128)(2,1)S(1)} %rank_gradient.1.rank_ref), custom_call_target="tpu_custom_call" | custom-call | flops 268435456 | bytes 8388608 | tf_op jit(solution)/shard_map/down_parts/pallas_call | solution.py:297
  33.4 0.1 collective-permute-start.9
  33.5 0.3 collective-permute-done.16
  33.8 1.0 %add_convert_fusion = bf16[4,4,16,1024]{3,2,1,0:T(8,128)(2,1)} fusion(bf16[4,4,16,1024]{3,2,1,0:T(8,128)(2,1)S(1)} %collective-permute-done.16, bf16[4,4,16,1024]{3,2,1,0:T(8,128)(2,1)S(1)} %get-tuple-element.44), kind=kLoop, calls=%fused_computation | loop fusion | flops 1048576 | bytes 1572864 | tf_op jit(solution)/shard_map/convert_element_type | solution.py:334
  34.8 4.1 %all-to-all-start = ((bf16[4,4,16,1024]{3,2,1,0:T(8,128)(2,1)}), bf16[4,4,16,1024]{3,2,1,0:T(8,128)(2,1)}, u32[]{:S(2)}, u32[]{:S(2)}) async-start(bf16[4,4,16,1024]{3,2,1,0:T(8,128)(2,1)} %add_convert_fusion), calls=%async_computation | async-start | bytes 1048576 | tf_op jit(solution)/shard_map/all_to_all | solution.py:321
  39.0 0.2 core_sum.1
  39.2 1.5 %collective-permute-start.10 = (bf16[4,16,2048]{2,1,0:T(8,128)(2,1)S(1)}, bf16[4,16,2048]{2,1,0:T(8,128)(2,1)S(1)}, u32[]{:S(2)}, u32[]{:S(2)}) collective-permute-start(bf16[4,16,2048]{2,1,0:T(8,128)(2,1)S(1)} %get-tuple-element.41), channel_id=1, source_target_pairs={{0,8},{4,12},{8,0},{12,4},{16,24},{20,28},{24,16},{28,20},{1,9},{5... | collective-permute-start | bytes 786440 | tf_op jit(solution)/shard_map/ppermute | solution.py:195
  40.7 0.9 %collective-permute-start.11 = (bf16[4,16,2048]{2,1,0:T(8,128)(2,1)S(1)}, bf16[4,16,2048]{2,1,0:T(8,128)(2,1)S(1)}, u32[]{:S(2)}, u32[]{:S(2)}) collective-permute-start(bf16[4,16,2048]{2,1,0:T(8,128)(2,1)S(1)} %get-tuple-element.42), channel_id=1, source_target_pairs={{0,16},{4,20},{8,24},{12,28},{16,0},{20,4},{24,8},{28,12},{1,17},{... | collective-permute-start | bytes 786440 | tf_op jit(solution)/shard_map/ppermute | solution.py:195
  41.6 1.1 %collective-permute-start.12 = (bf16[4,16,2048]{2,1,0:T(8,128)(2,1)S(1)}, bf16[4,16,2048]{2,1,0:T(8,128)(2,1)S(1)}, u32[]{:S(2)}, u32[]{:S(2)}) collective-permute-start(bf16[4,16,2048]{2,1,0:T(8,128)(2,1)S(1)} %get-tuple-element.43), channel_id=1, source_target_pairs={{0,24},{4,28},{8,16},{12,20},{16,8},{20,12},{24,0},{28,4},{1,25},{... | collective-permute-start | bytes 786440 | tf_op jit(solution)/shard_map/ppermute | solution.py:195
  42.8 11.5 %all-to-all-done = bf16[4,4,16,1024]{3,2,1,0:T(8,128)(2,1)} async-done(((bf16[4,4,16,1024]{3,2,1,0:T(8,128)(2,1)}), bf16[4,4,16,1024]{3,2,1,0:T(8,128)(2,1)}, u32[]{:S(2)}, u32[]{:S(2)}) %all-to-all-start) | async-done | bytes 524320 | tf_op jit(solution)/shard_map/all_to_all | solution.py:321
  54.3 1.1 %reduce_sum.42 = bf16[4,16,1024]{2,1,0:T(8,128)(2,1)S(1)} reduce(bf16[4,4,16,1024]{3,2,1,0:T(8,128)(2,1)} %all-to-all-done, bf16[]{:T(256)} %constant.2.clone.1), dimensions={0}, to_apply=%region_3.4 | reduce | flops 196608 | bytes 655362 | tf_op jit(solution)/shard_map/reduce_sum | solution.py:322
  55.5 1.5 %collective-permute-start.17 = (bf16[16,1024]{1,0:T(8,128)(2,1)S(1)}, bf16[16,1024]{1,0:T(8,128)(2,1)S(1)}, u32[]{:S(2)}, u32[]{:S(2)}) collective-permute-start(bf16[16,1024]{1,0:T(8,128)(2,1)S(1)} %get-tuple-element.49), channel_id=1, source_target_pairs={{0,8},{4,12},{8,0},{12,4},{16,24},{20,28},{24,16},{28,20},{1,9},{5... | collective-permute-start | bytes 98312 | tf_op jit(solution)/shard_map/ppermute | solution.py:195
  57.0 1.5 %collective-permute-start.19 = (bf16[16,1024]{1,0:T(8,128)(2,1)S(1)}, bf16[16,1024]{1,0:T(8,128)(2,1)S(1)}, u32[]{:S(2)}, u32[]{:S(2)}) collective-permute-start(bf16[16,1024]{1,0:T(8,128)(2,1)S(1)} %get-tuple-element.50), channel_id=1, source_target_pairs={{0,24},{4,28},{8,16},{12,20},{16,8},{20,12},{24,0},{28,4},{1,25},{... | collective-permute-start | bytes 98312 | tf_op jit(solution)/shard_map/ppermute | solution.py:195
  58.5 0.5 collective-permute-start.18
  59.0 0.1 add_convert_fusion.1
  59.2 0.1 collective-permute-start.13
  59.3 3.8 %collective-permute-start.15 = (bf16[16,2048]{1,0:T(8,128)(2,1)S(1)}, bf16[16,2048]{1,0:T(8,128)(2,1)S(1)}, u32[]{:S(2)}, u32[]{:S(2)}) collective-permute-start(bf16[16,2048]{1,0:T(8,128)(2,1)S(1)} %get-tuple-element.47), channel_id=1, source_target_pairs={{0,3},{1,0},{2,1},{3,2},{4,7},{5,4},{6,5},{7,6},{8,11},{9,8},{10,9... | collective-permute-start | bytes 196616 | tf_op jit(solution)/shard_map/ppermute | solution.py:191
  63.1 0.7 fusion.7
  63.7 1.6 %collective-permute-done.13 = bf16[16,2048]{1,0:T(8,128)(2,1)S(1)} collective-permute-done((bf16[16,2048]{1,0:T(8,128)(2,1)S(1)}, bf16[16,2048]{1,0:T(8,128)(2,1)S(1)}, u32[]{:S(2)}, u32[]{:S(2)}) %collective-permute-start.13) | collective-permute-done | bytes 65568 | tf_op jit(solution)/shard_map/ppermute | solution.py:191
  65.4 2.9 %collective-permute-done.14 = bf16[16,2048]{1,0:T(8,128)(2,1)S(1)} collective-permute-done((bf16[16,2048]{1,0:T(8,128)(2,1)S(1)}, bf16[16,2048]{1,0:T(8,128)(2,1)S(1)}, u32[]{:S(2)}, u32[]{:S(2)}) %collective-permute-start.14) | collective-permute-done | bytes 65568 | tf_op jit(solution)/shard_map/ppermute | solution.py:191
  68.2 0.7 %fusion.3 = f32[1,2048,16]{1,2,0:T(8,128)} fusion(bf16[16,2048]{1,0:T(8,128)(2,1)S(1)} %collective-permute-done.15, bf16[16,2048]{1,0:T(8,128)(2,1)S(1)} %collective-permute-done.14, bf16[16,2048]{1,0:T(8,128)(2,1)S(1)} %collective-permute-done.13, bf16[4,16,2048]{2,1,0:T(8,128)(2,1)S(1)} %add_convert_fusion.1), kind=kLoop, calls=%fused_computation.7 | loop fusion | flops 262144 | bytes 393216 | tf_op jit(solution)/shard_map/mul | solution.py:329
  (33 shorter events, 0.1 us)
Async XLA Ops:
  0.6 23.0 %copy-start.1 = (bf16[128,4096]{1,0:T(8,128)(2,1)S(1)}, bf16[128,4096]{1,0:T(8,128)(2,1)}, u32[]{:S(2)}) copy-start(bf16[128,4096]{1,0:T(8,128)(2,1)} %g_hbm.3) | copy-start | bytes 3145732
  0.6 23.0 %copy-start = (bf16[128,4096]{1,0:T(8,128)(2,1)S(1)}, bf16[128,4096]{1,0:T(8,128)(2,1)}, u32[]{:S(2)}) copy-start(bf16[128,4096]{1,0:T(8,128)(2,1)} %q_hbm.3) | copy-start | bytes 3145732
  0.6 18.3 %collective-permute-start.3 = (bf16[1,16,1024]{2,1,0:T(8,128)(2,1)}, bf16[1,16,1024]{2,1,0:T(8,128)(2,1)S(1)}, u32[]{:S(2)}, u32[]{:S(2)}) collective-permute-start(bf16[1,16,1024]{2,1,0:T(8,128)(2,1)} %param.16), channel_id=1, source_target_pairs={{0,2},{1,3},{2,0},{3,1},{4,6},{5,7},{6,4},{7,5},{8,10},{9,11},{10,... | collective-permute-start | bytes 98312 | tf_op jit(solution)/shard_map/ppermute | solution.py:191
  4.8 14.2 %collective-permute-start.2 = (bf16[1,16,1024]{2,1,0:T(8,128)(2,1)}, bf16[1,16,1024]{2,1,0:T(8,128)(2,1)S(1)}, u32[]{:S(2)}, u32[]{:S(2)}) collective-permute-start(bf16[1,16,1024]{2,1,0:T(8,128)(2,1)} %param.16), channel_id=1, source_target_pairs={{0,1},{1,2},{2,3},{3,0},{4,5},{5,6},{6,7},{7,4},{8,9},{9,10},{10,1... | collective-permute-start | bytes 98312 | tf_op jit(solution)/shard_map/ppermute | solution.py:191
  6.3 12.6 %collective-permute-start.4 = (bf16[1,16,1024]{2,1,0:T(8,128)(2,1)}, bf16[1,16,1024]{2,1,0:T(8,128)(2,1)S(1)}, u32[]{:S(2)}, u32[]{:S(2)}) collective-permute-start(bf16[1,16,1024]{2,1,0:T(8,128)(2,1)} %param.16), channel_id=1, source_target_pairs={{0,3},{1,0},{2,1},{3,2},{4,7},{5,4},{6,5},{7,6},{8,11},{9,8},{10,9... | collective-permute-start | bytes 98312 | tf_op jit(solution)/shard_map/ppermute | solution.py:191
  10.4 13.0 %collective-permute-start.1 = (bf16[128,1024]{1,0:T(8,128)(2,1)S(1)}, bf16[128,1024]{1,0:T(8,128)(2,1)S(1)}, u32[]{:S(2)}, u32[]{:S(2)}) collective-permute-start(bf16[128,1024]{1,0:T(8,128)(2,1)S(1)} %constant_dynamic-update-slice_fusion.refs_3_), channel_id=1, source_target_pairs={{0,1},{1,2},{2,3},{4,5},{5,6},{6,7},{8,9},{9,10},{10,11},{12,13},{... | collective-permute-start | bytes 786440 | tf_op jit(solution)/shard_map/ppermute | solution.py:220
  12.1 11.3 %collective-permute-start = (bf16[64,1024]{1,0:T(8,128)(2,1)S(1)}, bf16[64,1024]{1,0:T(8,128)(2,1)S(1)}, u32[]{:S(2)}, u32[]{:S(2)}) collective-permute-start(bf16[64,1024]{1,0:T(8,128)(2,1)S(1)} %slice.36), channel_id=1, source_target_pairs={{0,2},{1,3},{4,6},{5,7},{8,10},{9,11},{12,14},{13,15},{16,18},{17,... | collective-permute-start | bytes 393224 | tf_op jit(solution)/shard_map/ppermute | solution.py:220
  19.7 7.3 %collective-permute-start.7 = (bf16[1,4,16,1024]{3,2,1,0:T(8,128)(2,1)S(1)}, bf16[1,4,16,1024]{3,2,1,0:T(8,128)(2,1)S(1)}, u32[]{:S(2)}, u32[]{:S(2)}) collective-permute-start(bf16[1,4,16,1024]{3,2,1,0:T(8,128)(2,1)S(1)} %maximum_bitcast_fusion), channel_id=1, source_target_pairs={{0,24},{4,28},{8,16},{12,20},{16,8},{20,12},{24,0},{28,4},{1,25},{... | collective-permute-start | bytes 393224 | tf_op jit(solution)/shard_map/ppermute | solution.py:195
  22.3 5.5 %collective-permute-start.6 = (bf16[1,4,16,1024]{3,2,1,0:T(8,128)(2,1)S(1)}, bf16[1,4,16,1024]{3,2,1,0:T(8,128)(2,1)S(1)}, u32[]{:S(2)}, u32[]{:S(2)}) collective-permute-start(bf16[1,4,16,1024]{3,2,1,0:T(8,128)(2,1)S(1)} %maximum_bitcast_fusion), channel_id=1, source_target_pairs={{0,16},{4,20},{8,24},{12,28},{16,0},{20,4},{24,8},{28,12},{1,17},{... | collective-permute-start | bytes 393224 | tf_op jit(solution)/shard_map/ppermute | solution.py:195
  22.8 5.0 %collective-permute-start.5 = (bf16[1,4,16,1024]{3,2,1,0:T(8,128)(2,1)S(1)}, bf16[1,4,16,1024]{3,2,1,0:T(8,128)(2,1)S(1)}, u32[]{:S(2)}, u32[]{:S(2)}) collective-permute-start(bf16[1,4,16,1024]{3,2,1,0:T(8,128)(2,1)S(1)} %maximum_bitcast_fusion), channel_id=1, source_target_pairs={{0,8},{4,12},{8,0},{12,4},{16,24},{20,28},{24,16},{28,20},{1,9},{5... | collective-permute-start | bytes 393224 | tf_op jit(solution)/shard_map/ppermute | solution.py:195
  23.7 4.2 %copy-start.3 = (bf16[128,16]{0,1:T(8,128)(2,1)S(1)}, bf16[128,16]{0,1:T(8,128)(2,1)}, u32[]{:S(2)}) copy-start(bf16[128,16]{0,1:T(8,128)(2,1)} %param.15) | copy-start | bytes 12292
  27.8 3.9 %collective-permute-start.8 = (bf16[4,4,16,1024]{3,2,1,0:T(8,128)(2,1)S(1)}, bf16[4,4,16,1024]{3,2,1,0:T(8,128)(2,1)S(1)}, u32[]{:S(2)}, u32[]{:S(2)}) collective-permute-start(bf16[4,4,16,1024]{3,2,1,0:T(8,128)(2,1)S(1)} %constant_dynamic-update-slice_fusion.2.refs_0_), channel_id=1, source_target_pairs={{0,4},{4,0},{8,12},{12,8},{16,20},{20,16},{24,28},{28,24},{1,5},{5... | collective-permute-start | bytes 1572872 | tf_op jit(solution)/shard_map/ppermute | solution.py:195
  27.9 4.8 %copy-start.2 = (bf16[128,8192]{1,0:T(8,128)(2,1)S(1)}, bf16[128,8192]{1,0:T(8,128)(2,1)}, u32[]{:S(2)}) copy-start(bf16[128,8192]{1,0:T(8,128)(2,1)} %x_ref.1) | copy-start | bytes 6291460
  31.7 2.1 %collective-permute-start.16 = (bf16[4,4,16,1024]{3,2,1,0:T(8,128)(2,1)S(1)}, bf16[4,4,16,1024]{3,2,1,0:T(8,128)(2,1)S(1)}, u32[]{:S(2)}, u32[]{:S(2)}) collective-permute-start(bf16[4,4,16,1024]{3,2,1,0:T(8,128)(2,1)S(1)} %get-tuple-element.45), channel_id=1, source_target_pairs={{0,4},{4,0},{8,12},{12,8},{16,20},{20,16},{24,28},{28,24},{1,5},{5... | collective-permute-start | bytes 1572872 | tf_op jit(solution)/shard_map/ppermute | solution.py:195
  33.4 5.5 %collective-permute-start.9 = (bf16[4,4,16,2048]{3,2,1,0:T(8,128)(2,1)S(1)}, bf16[4,4,16,2048]{3,2,1,0:T(8,128)(2,1)S(1)}, u32[]{:S(2)}, u32[]{:S(2)}) collective-permute-start(bf16[4,4,16,2048]{3,2,1,0:T(8,128)(2,1)S(1)} %get-tuple-element.39), channel_id=1, source_target_pairs={{0,4},{4,0},{8,12},{12,8},{16,20},{20,16},{24,28},{28,24},{1,5},{5... | collective-permute-start | bytes 3145736 | tf_op jit(solution)/shard_map/ppermute | solution.py:195
  34.8 19.5 %all-to-all-start = ((bf16[4,4,16,1024]{3,2,1,0:T(8,128)(2,1)}), bf16[4,4,16,1024]{3,2,1,0:T(8,128)(2,1)}, u32[]{:S(2)}, u32[]{:S(2)}) async-start(bf16[4,4,16,1024]{3,2,1,0:T(8,128)(2,1)} %add_convert_fusion), calls=%async_computation | async-start | bytes 1048576 | tf_op jit(solution)/shard_map/all_to_all | solution.py:321
  39.2 19.3 %collective-permute-start.10 = (bf16[4,16,2048]{2,1,0:T(8,128)(2,1)S(1)}, bf16[4,16,2048]{2,1,0:T(8,128)(2,1)S(1)}, u32[]{:S(2)}, u32[]{:S(2)}) collective-permute-start(bf16[4,16,2048]{2,1,0:T(8,128)(2,1)S(1)} %get-tuple-element.41), channel_id=1, source_target_pairs={{0,8},{4,12},{8,0},{12,4},{16,24},{20,28},{24,16},{28,20},{1,9},{5... | collective-permute-start | bytes 786440 | tf_op jit(solution)/shard_map/ppermute | solution.py:195
  40.7 18.3 %collective-permute-start.11 = (bf16[4,16,2048]{2,1,0:T(8,128)(2,1)S(1)}, bf16[4,16,2048]{2,1,0:T(8,128)(2,1)S(1)}, u32[]{:S(2)}, u32[]{:S(2)}) collective-permute-start(bf16[4,16,2048]{2,1,0:T(8,128)(2,1)S(1)} %get-tuple-element.42), channel_id=1, source_target_pairs={{0,16},{4,20},{8,24},{12,28},{16,0},{20,4},{24,8},{28,12},{1,17},{... | collective-permute-start | bytes 786440 | tf_op jit(solution)/shard_map/ppermute | solution.py:195
  41.6 17.4 %collective-permute-start.12 = (bf16[4,16,2048]{2,1,0:T(8,128)(2,1)S(1)}, bf16[4,16,2048]{2,1,0:T(8,128)(2,1)S(1)}, u32[]{:S(2)}, u32[]{:S(2)}) collective-permute-start(bf16[4,16,2048]{2,1,0:T(8,128)(2,1)S(1)} %get-tuple-element.43), channel_id=1, source_target_pairs={{0,24},{4,28},{8,16},{12,20},{16,8},{20,12},{24,0},{28,4},{1,25},{... | collective-permute-start | bytes 786440 | tf_op jit(solution)/shard_map/ppermute | solution.py:195
  55.5 7.6 %collective-permute-start.17 = (bf16[16,1024]{1,0:T(8,128)(2,1)S(1)}, bf16[16,1024]{1,0:T(8,128)(2,1)S(1)}, u32[]{:S(2)}, u32[]{:S(2)}) collective-permute-start(bf16[16,1024]{1,0:T(8,128)(2,1)S(1)} %get-tuple-element.49), channel_id=1, source_target_pairs={{0,8},{4,12},{8,0},{12,4},{16,24},{20,28},{24,16},{28,20},{1,9},{5... | collective-permute-start | bytes 98312 | tf_op jit(solution)/shard_map/ppermute | solution.py:195
  57.0 6.1 %collective-permute-start.19 = (bf16[16,1024]{1,0:T(8,128)(2,1)S(1)}, bf16[16,1024]{1,0:T(8,128)(2,1)S(1)}, u32[]{:S(2)}, u32[]{:S(2)}) collective-permute-start(bf16[16,1024]{1,0:T(8,128)(2,1)S(1)} %get-tuple-element.50), channel_id=1, source_target_pairs={{0,24},{4,28},{8,16},{12,20},{16,8},{20,12},{24,0},{28,4},{1,25},{... | collective-permute-start | bytes 98312 | tf_op jit(solution)/shard_map/ppermute | solution.py:195
  58.5 4.6 %collective-permute-start.18 = (bf16[16,1024]{1,0:T(8,128)(2,1)S(1)}, bf16[16,1024]{1,0:T(8,128)(2,1)S(1)}, u32[]{:S(2)}, u32[]{:S(2)}) collective-permute-start(bf16[16,1024]{1,0:T(8,128)(2,1)S(1)} %get-tuple-element.51), channel_id=1, source_target_pairs={{0,16},{4,20},{8,24},{12,28},{16,0},{20,4},{24,8},{28,12},{1,17},{... | collective-permute-start | bytes 98312 | tf_op jit(solution)/shard_map/ppermute | solution.py:195
  59.2 6.2 %collective-permute-start.13 = (bf16[16,2048]{1,0:T(8,128)(2,1)S(1)}, bf16[16,2048]{1,0:T(8,128)(2,1)S(1)}, u32[]{:S(2)}, u32[]{:S(2)}) collective-permute-start(bf16[16,2048]{1,0:T(8,128)(2,1)S(1)} %get-tuple-element.46), channel_id=1, source_target_pairs={{0,1},{1,2},{2,3},{3,0},{4,5},{5,6},{6,7},{7,4},{8,9},{9,10},{10,1... | collective-permute-start | bytes 196616 | tf_op jit(solution)/shard_map/ppermute | solution.py:191
  59.3 6.1 %collective-permute-start.15 = (bf16[16,2048]{1,0:T(8,128)(2,1)S(1)}, bf16[16,2048]{1,0:T(8,128)(2,1)S(1)}, u32[]{:S(2)}, u32[]{:S(2)}) collective-permute-start(bf16[16,2048]{1,0:T(8,128)(2,1)S(1)} %get-tuple-element.47), channel_id=1, source_target_pairs={{0,3},{1,0},{2,1},{3,2},{4,7},{5,4},{6,5},{7,6},{8,11},{9,8},{10,9... | collective-permute-start | bytes 196616 | tf_op jit(solution)/shard_map/ppermute | solution.py:191
  63.1 5.2 %collective-permute-start.14 = (bf16[16,2048]{1,0:T(8,128)(2,1)S(1)}, bf16[16,2048]{1,0:T(8,128)(2,1)S(1)}, u32[]{:S(2)}, u32[]{:S(2)}) collective-permute-start(bf16[16,2048]{1,0:T(8,128)(2,1)S(1)} %get-tuple-element.48), channel_id=1, source_target_pairs={{0,2},{1,3},{2,0},{3,1},{4,6},{5,7},{6,4},{7,5},{8,10},{9,11},{10,... | collective-permute-start | bytes 196616 | tf_op jit(solution)/shard_map/ppermute | solution.py:191

commit v10 on v9

--- a/solution.py
+++ b/solution.py
@@ -113,7 +113,7 @@
 
     facts_ref, act_ref, dq_before = before
     rank = act_ref.shape[0]
-    n_quarters, per, _, part = up_refs[0].shape
+    per, n_quarters, _, part = up_refs[0].shape
     n_groups = per * len(up_refs)
     own = group_rows(rank, n_groups, tok, seq, by_slot) == facts_ref[2:3, :]
     act = jnp.concatenate([act_ref[...].astype(F32)] * n_groups, axis=0)
@@ -122,8 +122,9 @@
     for quarter in range(n_quarters):
         i, dq_ref = (quarter, dq_before) if quarter < n_before else (quarter - n_before, dq_turned)
         up = dot(act_cols, dq_ref[i * part : (i + 1) * part, :], 1, 1).astype(BF16)
+        j = lax.rem(quarter + n_quarters - head, n_quarters) if by_slot else quarter
         for n in range(n_groups):
-            up_refs[n // per][quarter, n % per] = up[n * rank : (n + 1) * rank, :]
+            up_refs[n // per][n % per, j] = up[n * rank : (n + 1) * rank, :]
 
 
 def rank_kernel(by_slot, n_w, facts_ref, *refs):
@@ -279,7 +280,7 @@
         dq_a, w = lax.optimization_barrier((dq_a, w))
         w = jnp.concatenate(w, axis=0)
         up_weight = [w, partnered(w, n_seq, 1)]
-    up_shape = jax.ShapeDtypeStruct((n_head, n_groups // n_out, rank, part), BF16)
+    up_shape = jax.ShapeDtypeStruct((n_groups // n_out, n_head, rank, part), BF16)
     dq_b, *up = attention(1, [facts, adapter_activation.T, dq_a], [up_shape] * n_out)
 
     if by_slot:
@@ -318,12 +319,11 @@
             cost_estimate=pl.CostEstimate(flops=0, bytes_accessed=SUM_BYTES, transcendentals=0),
             name="core_sum",
         )(down[0], partnered(down[1], n_seq, 1))
-        up = lax.all_to_all(over_cores(up, n_seq), "head", split_axis=0, concat_axis=0, tiled=True)
-        up = over_chips(jnp.sum(up.astype(F32), axis=0).astype(BF16), n_seq)
+        up = over_z(over_chips(over_cores(up, n_seq), n_seq).astype(BF16), n_head)
         down = over_z(over_chips(down, n_seq).astype(BF16), n_head)
     else:
-        up = lax.all_to_all(up[0], "head", split_axis=0, concat_axis=0, tiled=True)
-        up = spread(jnp.sum(up.astype(F32), axis=0), segment_adapter, owner, n_seq)
+        up = lax.all_to_all(up[0], "head", split_axis=1, concat_axis=1, tiled=True)
+        up = spread(jnp.sum(up.astype(F32), axis=1), segment_adapter, owner, n_seq)
         down = lax.all_to_all(down[0], "head", split_axis=1, concat_axis=1, tiled=True)
         down = spread(jnp.sum(down.astype(F32), axis=1), segment_adapter, owner, n_seq)
     return down.T[None] * ADAPTER_SCALE, up[None] * ADAPTER_SCALE

time: 69.3 us -> 66.5 us (0.960)
  other arithmetic: 6.83 us -> 4.97 us
  waiting for transfers between devices: 17 us -> 15.7 us
    all_to_all x1 -> x0, waiting for transfers between devices: 11.5 us -> none  [on_device(): lax.all_to_all(over_cores(up, n_seq), 'head', split_axis=0, concat_axis=0...]
    ppermute x12, waiting for transfers between devices: 0.95 us -> 11.2 us  [partnered(): return lax.ppermute(x, 'seq', [(i, i ^ bits) for i in range(n_seq)])]
    all_to_all x1 -> x0, starting transfers between devices: 4.14 us -> none  [on_device(): lax.all_to_all(over_cores(up, n_seq), 'head', split_axis=0, concat_axis=0...]
    ppermute x6 -> x9, starting transfers between devices: 11.8 us -> 15.7 us  [shifted(): lax.ppermute(x, 'head', [(i, (i + j) % n_head) for i in range(n_head)])]
    reduce_sum x1 -> x0, other arithmetic: 1.13 us -> none  [on_device(): up = over_chips(jnp.sum(up.astype(F32), axis=0).astype(BF16), n_seq)]
    convert_element_type x1, other arithmetic: 1 us -> 0.19 us  [over_cores(): (keep.astype(F32) + partnered(send, n_seq, 1).astype(F32)).astype(BF16)]
    ppermute x6 -> x9, waiting for transfers between devices: 4.5 us -> 4.51 us  [shifted(): lax.ppermute(x, 'head', [(i, (i + j) % n_head) for i in range(n_head)])]
  transfers between devices with their start and end apart: 21 -> 23, of which waited for: 5 -> 8; matrix products, arithmetic and copies ran while one was open for 14% -> 12% of each run, Pallas kernels for 13% -> 13%
where the time goes in v10:
time: 66.5 us; the launch traced here: 66.2 us
  starting transfers between devices  32.1 us (48%)
  waiting for transfers between devices  15.7 us (24%)
  Pallas kernels  8.79 us (13%)
  other arithmetic  4.97 us (7%)
  local copies, waits for them, and re-layouts  3.66 us (6%)
  between operations  0.97 us (1%)
    ppermute x9, starting transfers between devices, shifted(): lax.ppermute(x, 'head', [(i, (i + j) % n_head) for i in range(n_head)])  15.7 us
    ppermute x12, starting transfers between devices, partnered(): return lax.ppermute(x, 'seq', [(i, i ^ bits) for i in range(n_seq)])  12.1 us
    ppermute x12, waiting for transfers between devices, partnered(): return lax.ppermute(x, 'seq', [(i, i ^ bits) for i in range(n_seq)])  11.2 us
    pallas_call x2, Pallas kernels, attention(): pl.pallas_call(functools.partial(attention_kernel, by_slot, h * n_kv, n_k...  7.14 us
    ppermute x9, waiting for transfers between devices, shifted(): lax.ppermute(x, 'head', [(i, (i + j) % n_head) for i in range(n_head)])  4.51 us
    ppermute x2, starting transfers between devices, on_device(): parts.insert(0, lax.ppermute(own[tok - rows:], 'head', shift))  4.39 us
    unnamed x13, local copies, waits for them, and re-layouts  1.99 us
    mul x2, other arithmetic, on_device(): return (down.T[None] * ADAPTER_SCALE, up[None] * ADAPTER_SCALE)  1.35 us
  transfers between devices with their start and end apart: 23, of which 8 were waited for; matrix products, arithmetic and copies ran while one was open for 12% of the time, Pallas kernels for 13%

profile of v10, /device:TPU:0, one launch (start us, length us, event | category | flops | bytes accessed | tf_op | source)
XLA Modules:
  0.0 66.2 jit_solution(3540771311480954924)
XLA Ops:
  0.6 4.1 %collective-permute-start.3 = (bf16[1,16,1024]{2,1,0:T(8,128)(2,1)}, bf16[1,16,1024]{2,1,0:T(8,128)(2,1)S(1)}, u32[]{:S(2)}, u32[]{:S(2)}) collective-permute-start(bf16[1,16,1024]{2,1,0:T(8,128)(2,1)} %param.16), channel_id=1, source_target_pairs={{0,2},{1,3},{2,0},{3,1},{4,6},{5,7},{6,4},{7,5},{8,10},{9,11},{10,... | collective-permute-start | bytes 98312 | tf_op jit(solution)/shard_map/ppermute | solution.py:192
  4.8 1.6 %collective-permute-start.2 = (bf16[1,16,1024]{2,1,0:T(8,128)(2,1)}, bf16[1,16,1024]{2,1,0:T(8,128)(2,1)S(1)}, u32[]{:S(2)}, u32[]{:S(2)}) collective-permute-start(bf16[1,16,1024]{2,1,0:T(8,128)(2,1)} %param.16), channel_id=1, source_target_pairs={{0,1},{1,2},{2,3},{3,0},{4,5},{5,6},{6,7},{7,4},{8,9},{9,10},{10,1... | collective-permute-start | bytes 98312 | tf_op jit(solution)/shard_map/ppermute | solution.py:192
  6.3 2.2 %collective-permute-start.4 = (bf16[1,16,1024]{2,1,0:T(8,128)(2,1)}, bf16[1,16,1024]{2,1,0:T(8,128)(2,1)S(1)}, u32[]{:S(2)}, u32[]{:S(2)}) collective-permute-start(bf16[1,16,1024]{2,1,0:T(8,128)(2,1)} %param.16), channel_id=1, source_target_pairs={{0,3},{1,0},{2,1},{3,2},{4,7},{5,4},{6,5},{7,6},{8,11},{9,8},{10,9... | collective-permute-start | bytes 98312 | tf_op jit(solution)/shard_map/ppermute | solution.py:192
  8.6 0.9 %constant_dynamic-update-slice_fusion.1 = bf16[128,1024]{1,0:T(8,128)(2,1)S(1)} fusion(bf16[128,512]{1,0:T(8,128)(2,1)} %param.11), kind=kLoop, calls=%fused_computation.31 | loop fusion | bytes 262144
  9.5 0.9 %constant_dynamic-update-slice_fusion.refs_3_ = bf16[128,1024]{1,0:T(8,128)(2,1)S(1)} fusion(bf16[128,1024]{1,0:T(8,128)(2,1)S(1)} %constant_dynamic-update-slice_fusion.1, bf16[128,512]{1,0:T(8,128)(2,1)} %param.12), kind=kLoop, calls=%fused_computation.30 | loop fusion | bytes 262144 | tf_op jit(solution)/shard_map/concatenate | solution.py:217
  10.4 1.7 %collective-permute-start.1 = (bf16[128,1024]{1,0:T(8,128)(2,1)S(1)}, bf16[128,1024]{1,0:T(8,128)(2,1)S(1)}, u32[]{:S(2)}, u32[]{:S(2)}) collective-permute-start(bf16[128,1024]{1,0:T(8,128)(2,1)S(1)} %constant_dynamic-update-slice_fusion.refs_3_), channel_id=1, source_target_pairs={{0,1},{1,2},{2,3},{4,5},{5,6},{6,7},{8,9},{9,10},{10,11},{12,13},{... | collective-permute-start | bytes 786440 | tf_op jit(solution)/shard_map/ppermute | solution.py:221
  12.1 2.7 %collective-permute-start = (bf16[64,1024]{1,0:T(8,128)(2,1)S(1)}, bf16[64,1024]{1,0:T(8,128)(2,1)S(1)}, u32[]{:S(2)}, u32[]{:S(2)}) collective-permute-start(bf16[64,1024]{1,0:T(8,128)(2,1)S(1)} %slice.52), channel_id=1, source_target_pairs={{0,2},{1,3},{4,6},{5,7},{8,10},{9,11},{12,14},{13,15},{16,18},{17,... | collective-permute-start | bytes 393224 | tf_op jit(solution)/shard_map/ppermute | solution.py:221
  14.8 0.8 %select_reduce_fusion.2 = s32[8]{0:T(128)S(1)} fusion(s32[8]{0:T(128)} %bitcast.53), kind=kLoop, calls=%fused_computation.38 | loop fusion | flops 184 | bytes 64 | tf_op jit(solution)/shard_map/reduce_sum | solution.py:179
  15.6 0.7 bitcast_add_fusion
  16.3 0.1 compare_and_fusion
  16.4 0.9 %select_reduce_fusion.1 = s32[8]{0:T(128)S(1)} fusion(s32[8]{0:T(128)} %param.19, s32[8]{0:T(128)} %bitcast.51), kind=kLoop, calls=%fused_computation.36 | loop fusion | flops 184 | bytes 96 | tf_op jit(solution)/shard_map/reduce_sum | solution.py:182
  17.2 1.0 %copy.13 = bf16[128,512]{0,1:T(8,128)(2,1)S(1)} copy(bf16[128,512]{1,0:T(8,128)(2,1)} %param.11) | data formatting | bytes 262144 | tf_op args[1]
  18.3 0.7 %stack.15 = s32[8,8]{1,0:T(8,128)S(1)} concatenate(s32[1,8]{1,0:T(1,128)S(1)} %bitcast.50, s32[1,8]{1,0:T(1,128)} %param.18, s32[1,8]{1,0:T(1,128)S(1)} %bitcast.52, s32[1,8]{1,0:T(1,128)S(1)} %broadcast.49, s32[4,8]{1,0:T(4,128)S(1)} %stack.14), dimensions={0} | concatenate | bytes 512 | tf_op jit(solution)/shard_map/stack | solution.py:187
  19.0 0.8 %maximum_bitcast_fusion = bf16[1,4,16,1024]{3,2,1,0:T(8,128)(2,1)S(1)} fusion(bf16[1,16,1024]{2,1,0:T(8,128)(2,1)S(1)} %collective-permute-done.4, bf16[1,16,1024]{2,1,0:T(8,128)(2,1)S(1)} %collective-permute-done.3, bf16[1,16,1024]{2,1,0:T(8,128)(2,1)S(1)} %collective-permute-done.2, bf16[1,16,1024]{2,1,0:T(8,128)(2,1)} %param.16), kind=kLoop, calls=%fused_computation.10 | loop fusion | flops 196608 | bytes 262144 | tf_op jit(solution)/shard_map/broadcast_in_dim | solution.py:225
  19.7 2.5 %collective-permute-start.7 = (bf16[1,4,16,1024]{3,2,1,0:T(8,128)(2,1)S(1)}, bf16[1,4,16,1024]{3,2,1,0:T(8,128)(2,1)S(1)}, u32[]{:S(2)}, u32[]{:S(2)}) collective-permute-start(bf16[1,4,16,1024]{3,2,1,0:T(8,128)(2,1)S(1)} %maximum_bitcast_fusion), channel_id=1, source_target_pairs={{0,24},{4,28},{8,16},{12,20},{16,8},{20,12},{24,0},{28,4},{1,25},{... | collective-permute-start | bytes 393224 | tf_op jit(solution)/shard_map/ppermute | solution.py:196
  22.3 0.5 collective-permute-start.6
  22.8 0.5 collective-permute-start.5
  23.3 0.1 select_reduce_fusion.facts_ref.refs_0_
  23.4 0.3 layout.1
  23.7 3.4 %attention_0.1.refs_2_ = bf16[2048,128]{1,0:T(8,128)(2,1)S(1)} custom-call(bf16[320,512]{1,0:T(8,128)(2,1)S(1)} %get-tuple-element.24.k_all, bf16[320,512]{1,0:T(8,128)(2,1)S(1)} %get-tuple-element.25.v_all, bf16[512,320]{1,0:T(8,128)(2,1)S(1)} %get-tuple-element.26.k_turned, f32[320,128]{1,0:T(8,128)S(1)} %get-tuple-element.27.bias, ...), custom_call_target="tpu_custom_call" | custom-call | flops 503316480 | bytes 2097152 | tf_op jit(solution)/shard_map/attention_0/pallas_call | solution.py:258
  27.1 0.7 %collective-permute-done.6 = bf16[1,4,16,1024]{3,2,1,0:T(8,128)(2,1)S(1)} collective-permute-done((bf16[1,4,16,1024]{3,2,1,0:T(8,128)(2,1)S(1)}, bf16[1,4,16,1024]{3,2,1,0:T(8,128)(2,1)S(1)}, u32[]{:S(2)}, u32[]{:S(2)}) %collective-permute-start.6) | collective-permute-done | bytes 131104 | tf_op jit(solution)/shard_map/ppermute | solution.py:196
  27.8 0.1 collective-permute-start.8
  27.9 3.8 %attention_1.1 = (bf16[2048,128]{1,0:T(8,128)(2,1)S(1)}, bf16[4,4,16,1024]{3,2,1,0:T(8,128)(2,1)S(1)}, bf16[4,4,16,1024]{3,2,1,0:T(8,128)(2,1)S(1)}) custom-call(bf16[320,512]{1,0:T(8,128)(2,1)S(1)} %get-tuple-element.24.k_all, bf16[320,512]{1,0:T(8,128)(2,1)S(1)} %get-tuple-element.25.v_all, bf16[512,320]{1,0:T(8,128)(2,1)S(1)} %get-tuple-element.26.k_turned, ...), custom_call_target="tpu_custom_call" | custom-call | flops 503316480 | bytes 2097152 | tf_op jit(solution)/shard_map/attention_1/pallas_call | solution.py:258
  31.7 0.5 collective-permute-start.16
  32.3 0.4 rank_gradient.1.rank_ref
  32.7 0.7 %down_parts.1 = (bf16[4,4,16,2048]{3,2,1,0:T(8,128)(2,1)S(1)}, bf16[4,4,16,2048]{3,2,1,0:T(8,128)(2,1)S(1)}) custom-call(s32[8,128]{1,0:T(8,128)S(1)} %select_reduce_fusion.facts_ref.refs_0_, bf16[128,8192]{1,0:T(8,128)(2,1)S(1)} %copy-done.2, bf16[16,128]{1,0:T(8,128)(2,1)S(1)} %rank_gradient.1.rank_ref), custom_call_target="tpu_custom_call" | custom-call | flops 268435456 | bytes 8388608 | tf_op jit(solution)/shard_map/down_parts/pallas_call | solution.py:298
  33.4 0.1 collective-permute-start.9
  33.5 0.3 collective-permute-done.16
  33.8 0.2 add_convert_fusion
  34.0 1.5 %collective-permute-start.17 = (bf16[4,16,1024]{2,1,0:T(8,128)(2,1)S(1)}, bf16[4,16,1024]{2,1,0:T(8,128)(2,1)S(1)}, u32[]{:S(2)}, u32[]{:S(2)}) collective-permute-start(bf16[4,16,1024]{2,1,0:T(8,128)(2,1)S(1)} %get-tuple-element.46), channel_id=1, source_target_pairs={{0,8},{4,12},{8,0},{12,4},{16,24},{20,28},{24,16},{28,20},{1,9},{5... | collective-permute-start | bytes 393224 | tf_op jit(solution)/shard_map/ppermute | solution.py:196
  35.6 1.5 %collective-permute-start.19 = (bf16[4,16,1024]{2,1,0:T(8,128)(2,1)S(1)}, bf16[4,16,1024]{2,1,0:T(8,128)(2,1)S(1)}, u32[]{:S(2)}, u32[]{:S(2)}) collective-permute-start(bf16[4,16,1024]{2,1,0:T(8,128)(2,1)S(1)} %get-tuple-element.47), channel_id=1, source_target_pairs={{0,24},{4,28},{8,16},{12,20},{16,8},{20,12},{24,0},{28,4},{1,25},{... | collective-permute-start | bytes 393224 | tf_op jit(solution)/shard_map/ppermute | solution.py:196
  37.1 0.5 collective-permute-start.18
  37.6 0.2 core_sum.1
  37.8 1.5 %collective-permute-start.10 = (bf16[4,16,2048]{2,1,0:T(8,128)(2,1)S(1)}, bf16[4,16,2048]{2,1,0:T(8,128)(2,1)S(1)}, u32[]{:S(2)}, u32[]{:S(2)}) collective-permute-start(bf16[4,16,2048]{2,1,0:T(8,128)(2,1)S(1)} %get-tuple-element.41), channel_id=1, source_target_pairs={{0,8},{4,12},{8,0},{12,4},{16,24},{20,28},{24,16},{28,20},{1,9},{5... | collective-permute-start | bytes 786440 | tf_op jit(solution)/shard_map/ppermute | solution.py:196
  39.4 0.9 %collective-permute-start.11 = (bf16[4,16,2048]{2,1,0:T(8,128)(2,1)S(1)}, bf16[4,16,2048]{2,1,0:T(8,128)(2,1)S(1)}, u32[]{:S(2)}, u32[]{:S(2)}) collective-permute-start(bf16[4,16,2048]{2,1,0:T(8,128)(2,1)S(1)} %get-tuple-element.42), channel_id=1, source_target_pairs={{0,16},{4,20},{8,24},{12,28},{16,0},{20,4},{24,8},{28,12},{1,17},{... | collective-permute-start | bytes 786440 | tf_op jit(solution)/shard_map/ppermute | solution.py:196
  40.3 0.2 collective-permute-done.17
  40.4 1.8 %collective-permute-start.12 = (bf16[4,16,2048]{2,1,0:T(8,128)(2,1)S(1)}, bf16[4,16,2048]{2,1,0:T(8,128)(2,1)S(1)}, u32[]{:S(2)}, u32[]{:S(2)}) collective-permute-start(bf16[4,16,2048]{2,1,0:T(8,128)(2,1)S(1)} %get-tuple-element.43), channel_id=1, source_target_pairs={{0,24},{4,28},{8,16},{12,20},{16,8},{20,12},{24,0},{28,4},{1,25},{... | collective-permute-start | bytes 786440 | tf_op jit(solution)/shard_map/ppermute | solution.py:196
  42.2 2.0 %collective-permute-done.19 = bf16[4,16,1024]{2,1,0:T(8,128)(2,1)S(1)} collective-permute-done((bf16[4,16,1024]{2,1,0:T(8,128)(2,1)S(1)}, bf16[4,16,1024]{2,1,0:T(8,128)(2,1)S(1)}, u32[]{:S(2)}, u32[]{:S(2)}) %collective-permute-start.19) | collective-permute-done | bytes 131104 | tf_op jit(solution)/shard_map/ppermute | solution.py:196
  44.2 1.9 %collective-permute-done.18 = bf16[4,16,1024]{2,1,0:T(8,128)(2,1)S(1)} collective-permute-done((bf16[4,16,1024]{2,1,0:T(8,128)(2,1)S(1)}, bf16[4,16,1024]{2,1,0:T(8,128)(2,1)S(1)}, u32[]{:S(2)}, u32[]{:S(2)}) %collective-permute-start.18) | collective-permute-done | bytes 131104 | tf_op jit(solution)/shard_map/ppermute | solution.py:196
  46.1 0.1 fusion.2
  46.2 3.8 %collective-permute-start.22 = (bf16[16,1024]{1,0:T(8,128)(2,1)S(1)}, bf16[16,1024]{1,0:T(8,128)(2,1)S(1)}, u32[]{:S(2)}, u32[]{:S(2)}) collective-permute-start(bf16[16,1024]{1,0:T(8,128)(2,1)S(1)} %get-tuple-element.53), channel_id=1, source_target_pairs={{0,3},{1,0},{2,1},{3,2},{4,7},{5,4},{6,5},{7,6},{8,11},{9,8},{10,9... | collective-permute-start | bytes 98312 | tf_op jit(solution)/shard_map/ppermute | solution.py:192
  50.1 6.3 %collective-permute-done.11 = bf16[4,16,2048]{2,1,0:T(8,128)(2,1)S(1)} collective-permute-done((bf16[4,16,2048]{2,1,0:T(8,128)(2,1)S(1)}, bf16[4,16,2048]{2,1,0:T(8,128)(2,1)S(1)}, u32[]{:S(2)}, u32[]{:S(2)}) %collective-permute-start.11) | collective-permute-done | bytes 262176 | tf_op jit(solution)/shard_map/ppermute | solution.py:196
  56.3 0.1 add_convert_fusion.1
  56.5 3.8 %collective-permute-start.15 = (bf16[16,2048]{1,0:T(8,128)(2,1)S(1)}, bf16[16,2048]{1,0:T(8,128)(2,1)S(1)}, u32[]{:S(2)}, u32[]{:S(2)}) collective-permute-start(bf16[16,2048]{1,0:T(8,128)(2,1)S(1)} %get-tuple-element.50), channel_id=1, source_target_pairs={{0,3},{1,0},{2,1},{3,2},{4,7},{5,4},{6,5},{7,6},{8,11},{9,8},{10,9... | collective-permute-start | bytes 196616 | tf_op jit(solution)/shard_map/ppermute | solution.py:192
  60.4 0.7 fusion.10
  61.0 1.9 %collective-permute-done.13 = bf16[16,2048]{1,0:T(8,128)(2,1)S(1)} collective-permute-done((bf16[16,2048]{1,0:T(8,128)(2,1)S(1)}, bf16[16,2048]{1,0:T(8,128)(2,1)S(1)}, u32[]{:S(2)}, u32[]{:S(2)}) %collective-permute-start.13) | collective-permute-done | bytes 65568 | tf_op jit(solution)/shard_map/ppermute | solution.py:192
  62.9 2.6 %collective-permute-done.14 = bf16[16,2048]{1,0:T(8,128)(2,1)S(1)} collective-permute-done((bf16[16,2048]{1,0:T(8,128)(2,1)S(1)}, bf16[16,2048]{1,0:T(8,128)(2,1)S(1)}, u32[]{:S(2)}, u32[]{:S(2)}) %collective-permute-start.14) | collective-permute-done | bytes 65568 | tf_op jit(solution)/shard_map/ppermute | solution.py:192
  65.5 0.7 %fusion.6 = f32[1,2048,16]{1,2,0:T(8,128)} fusion(bf16[16,2048]{1,0:T(8,128)(2,1)S(1)} %collective-permute-done.15, bf16[16,2048]{1,0:T(8,128)(2,1)S(1)} %collective-permute-done.14, bf16[16,2048]{1,0:T(8,128)(2,1)S(1)} %collective-permute-done.13, bf16[4,16,2048]{2,1,0:T(8,128)(2,1)S(1)} %add_convert_fusion.1), kind=kLoop, calls=%fused_computation.15 | loop fusion | flops 262144 | bytes 393216 | tf_op jit(solution)/shard_map/mul | solution.py:329
  (38 shorter events, 0.3 us)
Async XLA Ops:
  0.6 23.0 %copy-start.1 = (bf16[128,4096]{1,0:T(8,128)(2,1)S(1)}, bf16[128,4096]{1,0:T(8,128)(2,1)}, u32[]{:S(2)}) copy-start(bf16[128,4096]{1,0:T(8,128)(2,1)} %g_hbm.3) | copy-start | bytes 3145732
  0.6 23.0 %copy-start = (bf16[128,4096]{1,0:T(8,128)(2,1)S(1)}, bf16[128,4096]{1,0:T(8,128)(2,1)}, u32[]{:S(2)}) copy-start(bf16[128,4096]{1,0:T(8,128)(2,1)} %q_hbm.3) | copy-start | bytes 3145732
  0.6 18.3 %collective-permute-start.3 = (bf16[1,16,1024]{2,1,0:T(8,128)(2,1)}, bf16[1,16,1024]{2,1,0:T(8,128)(2,1)S(1)}, u32[]{:S(2)}, u32[]{:S(2)}) collective-permute-start(bf16[1,16,1024]{2,1,0:T(8,128)(2,1)} %param.16), channel_id=1, source_target_pairs={{0,2},{1,3},{2,0},{3,1},{4,6},{5,7},{6,4},{7,5},{8,10},{9,11},{10,... | collective-permute-start | bytes 98312 | tf_op jit(solution)/shard_map/ppermute | solution.py:192
  4.8 14.2 %collective-permute-start.2 = (bf16[1,16,1024]{2,1,0:T(8,128)(2,1)}, bf16[1,16,1024]{2,1,0:T(8,128)(2,1)S(1)}, u32[]{:S(2)}, u32[]{:S(2)}) collective-permute-start(bf16[1,16,1024]{2,1,0:T(8,128)(2,1)} %param.16), channel_id=1, source_target_pairs={{0,1},{1,2},{2,3},{3,0},{4,5},{5,6},{6,7},{7,4},{8,9},{9,10},{10,1... | collective-permute-start | bytes 98312 | tf_op jit(solution)/shard_map/ppermute | solution.py:192
  6.3 12.6 %collective-permute-start.4 = (bf16[1,16,1024]{2,1,0:T(8,128)(2,1)}, bf16[1,16,1024]{2,1,0:T(8,128)(2,1)S(1)}, u32[]{:S(2)}, u32[]{:S(2)}) collective-permute-start(bf16[1,16,1024]{2,1,0:T(8,128)(2,1)} %param.16), channel_id=1, source_target_pairs={{0,3},{1,0},{2,1},{3,2},{4,7},{5,4},{6,5},{7,6},{8,11},{9,8},{10,9... | collective-permute-start | bytes 98312 | tf_op jit(solution)/shard_map/ppermute | solution.py:192
  10.4 13.0 %collective-permute-start.1 = (bf16[128,1024]{1,0:T(8,128)(2,1)S(1)}, bf16[128,1024]{1,0:T(8,128)(2,1)S(1)}, u32[]{:S(2)}, u32[]{:S(2)}) collective-permute-start(bf16[128,1024]{1,0:T(8,128)(2,1)S(1)} %constant_dynamic-update-slice_fusion.refs_3_), channel_id=1, source_target_pairs={{0,1},{1,2},{2,3},{4,5},{5,6},{6,7},{8,9},{9,10},{10,11},{12,13},{... | collective-permute-start | bytes 786440 | tf_op jit(solution)/shard_map/ppermute | solution.py:221
  12.1 11.3 %collective-permute-start = (bf16[64,1024]{1,0:T(8,128)(2,1)S(1)}, bf16[64,1024]{1,0:T(8,128)(2,1)S(1)}, u32[]{:S(2)}, u32[]{:S(2)}) collective-permute-start(bf16[64,1024]{1,0:T(8,128)(2,1)S(1)} %slice.52), channel_id=1, source_target_pairs={{0,2},{1,3},{4,6},{5,7},{8,10},{9,11},{12,14},{13,15},{16,18},{17,... | collective-permute-start | bytes 393224 | tf_op jit(solution)/shard_map/ppermute | solution.py:221
  19.7 7.3 %collective-permute-start.7 = (bf16[1,4,16,1024]{3,2,1,0:T(8,128)(2,1)S(1)}, bf16[1,4,16,1024]{3,2,1,0:T(8,128)(2,1)S(1)}, u32[]{:S(2)}, u32[]{:S(2)}) collective-permute-start(bf16[1,4,16,1024]{3,2,1,0:T(8,128)(2,1)S(1)} %maximum_bitcast_fusion), channel_id=1, source_target_pairs={{0,24},{4,28},{8,16},{12,20},{16,8},{20,12},{24,0},{28,4},{1,25},{... | collective-permute-start | bytes 393224 | tf_op jit(solution)/shard_map/ppermute | solution.py:196
  22.3 5.5 %collective-permute-start.6 = (bf16[1,4,16,1024]{3,2,1,0:T(8,128)(2,1)S(1)}, bf16[1,4,16,1024]{3,2,1,0:T(8,128)(2,1)S(1)}, u32[]{:S(2)}, u32[]{:S(2)}) collective-permute-start(bf16[1,4,16,1024]{3,2,1,0:T(8,128)(2,1)S(1)} %maximum_bitcast_fusion), channel_id=1, source_target_pairs={{0,16},{4,20},{8,24},{12,28},{16,0},{20,4},{24,8},{28,12},{1,17},{... | collective-permute-start | bytes 393224 | tf_op jit(solution)/shard_map/ppermute | solution.py:196
  22.8 5.0 %collective-permute-start.5 = (bf16[1,4,16,1024]{3,2,1,0:T(8,128)(2,1)S(1)}, bf16[1,4,16,1024]{3,2,1,0:T(8,128)(2,1)S(1)}, u32[]{:S(2)}, u32[]{:S(2)}) collective-permute-start(bf16[1,4,16,1024]{3,2,1,0:T(8,128)(2,1)S(1)} %maximum_bitcast_fusion), channel_id=1, source_target_pairs={{0,8},{4,12},{8,0},{12,4},{16,24},{20,28},{24,16},{28,20},{1,9},{5... | collective-permute-start | bytes 393224 | tf_op jit(solution)/shard_map/ppermute | solution.py:196
  23.7 4.2 %copy-start.3 = (bf16[128,16]{0,1:T(8,128)(2,1)S(1)}, bf16[128,16]{0,1:T(8,128)(2,1)}, u32[]{:S(2)}) copy-start(bf16[128,16]{0,1:T(8,128)(2,1)} %param.15) | copy-start | bytes 12292
  27.8 3.9 %collective-permute-start.8 = (bf16[4,4,16,1024]{3,2,1,0:T(8,128)(2,1)S(1)}, bf16[4,4,16,1024]{3,2,1,0:T(8,128)(2,1)S(1)}, u32[]{:S(2)}, u32[]{:S(2)}) collective-permute-start(bf16[4,4,16,1024]{3,2,1,0:T(8,128)(2,1)S(1)} %constant_dynamic-update-slice_fusion.2.refs_0_), channel_id=1, source_target_pairs={{0,4},{4,0},{8,12},{12,8},{16,20},{20,16},{24,28},{28,24},{1,5},{5... | collective-permute-start | bytes 1572872 | tf_op jit(solution)/shard_map/ppermute | solution.py:196
  27.9 4.8 %copy-start.2 = (bf16[128,8192]{1,0:T(8,128)(2,1)S(1)}, bf16[128,8192]{1,0:T(8,128)(2,1)}, u32[]{:S(2)}) copy-start(bf16[128,8192]{1,0:T(8,128)(2,1)} %x_ref.1) | copy-start | bytes 6291460
  31.7 2.1 %collective-permute-start.16 = (bf16[4,4,16,1024]{3,2,1,0:T(8,128)(2,1)S(1)}, bf16[4,4,16,1024]{3,2,1,0:T(8,128)(2,1)S(1)}, u32[]{:S(2)}, u32[]{:S(2)}) collective-permute-start(bf16[4,4,16,1024]{3,2,1,0:T(8,128)(2,1)S(1)} %get-tuple-element.45), channel_id=1, source_target_pairs={{0,4},{4,0},{8,12},{12,8},{16,20},{20,16},{24,28},{28,24},{1,5},{5... | collective-permute-start | bytes 1572872 | tf_op jit(solution)/shard_map/ppermute | solution.py:196
  33.4 4.2 %collective-permute-start.9 = (bf16[4,4,16,2048]{3,2,1,0:T(8,128)(2,1)S(1)}, bf16[4,4,16,2048]{3,2,1,0:T(8,128)(2,1)S(1)}, u32[]{:S(2)}, u32[]{:S(2)}) collective-permute-start(bf16[4,4,16,2048]{3,2,1,0:T(8,128)(2,1)S(1)} %get-tuple-element.39), channel_id=1, source_target_pairs={{0,4},{4,0},{8,12},{12,8},{16,20},{20,16},{24,28},{28,24},{1,5},{5... | collective-permute-start | bytes 3145736 | tf_op jit(solution)/shard_map/ppermute | solution.py:196
  34.0 6.4 %collective-permute-start.17 = (bf16[4,16,1024]{2,1,0:T(8,128)(2,1)S(1)}, bf16[4,16,1024]{2,1,0:T(8,128)(2,1)S(1)}, u32[]{:S(2)}, u32[]{:S(2)}) collective-permute-start(bf16[4,16,1024]{2,1,0:T(8,128)(2,1)S(1)} %get-tuple-element.46), channel_id=1, source_target_pairs={{0,8},{4,12},{8,0},{12,4},{16,24},{20,28},{24,16},{28,20},{1,9},{5... | collective-permute-start | bytes 393224 | tf_op jit(solution)/shard_map/ppermute | solution.py:196
  35.6 8.6 %collective-permute-start.19 = (bf16[4,16,1024]{2,1,0:T(8,128)(2,1)S(1)}, bf16[4,16,1024]{2,1,0:T(8,128)(2,1)S(1)}, u32[]{:S(2)}, u32[]{:S(2)}) collective-permute-start(bf16[4,16,1024]{2,1,0:T(8,128)(2,1)S(1)} %get-tuple-element.47), channel_id=1, source_target_pairs={{0,24},{4,28},{8,16},{12,20},{16,8},{20,12},{24,0},{28,4},{1,25},{... | collective-permute-start | bytes 393224 | tf_op jit(solution)/shard_map/ppermute | solution.py:196
  37.1 9.0 %collective-permute-start.18 = (bf16[4,16,1024]{2,1,0:T(8,128)(2,1)S(1)}, bf16[4,16,1024]{2,1,0:T(8,128)(2,1)S(1)}, u32[]{:S(2)}, u32[]{:S(2)}) collective-permute-start(bf16[4,16,1024]{2,1,0:T(8,128)(2,1)S(1)} %get-tuple-element.48), channel_id=1, source_target_pairs={{0,16},{4,20},{8,24},{12,28},{16,0},{20,4},{24,8},{28,12},{1,17},{... | collective-permute-start | bytes 393224 | tf_op jit(solution)/shard_map/ppermute | solution.py:196
  37.8 12.2 %collective-permute-start.10 = (bf16[4,16,2048]{2,1,0:T(8,128)(2,1)S(1)}, bf16[4,16,2048]{2,1,0:T(8,128)(2,1)S(1)}, u32[]{:S(2)}, u32[]{:S(2)}) collective-permute-start(bf16[4,16,2048]{2,1,0:T(8,128)(2,1)S(1)} %get-tuple-element.41), channel_id=1, source_target_pairs={{0,8},{4,12},{8,0},{12,4},{16,24},{20,28},{24,16},{28,20},{1,9},{5... | collective-permute-start | bytes 786440 | tf_op jit(solution)/shard_map/ppermute | solution.py:196
  39.4 16.9 %collective-permute-start.11 = (bf16[4,16,2048]{2,1,0:T(8,128)(2,1)S(1)}, bf16[4,16,2048]{2,1,0:T(8,128)(2,1)S(1)}, u32[]{:S(2)}, u32[]{:S(2)}) collective-permute-start(bf16[4,16,2048]{2,1,0:T(8,128)(2,1)S(1)} %get-tuple-element.42), channel_id=1, source_target_pairs={{0,16},{4,20},{8,24},{12,28},{16,0},{20,4},{24,8},{28,12},{1,17},{... | collective-permute-start | bytes 786440 | tf_op jit(solution)/shard_map/ppermute | solution.py:196
  40.4 15.9 %collective-permute-start.12 = (bf16[4,16,2048]{2,1,0:T(8,128)(2,1)S(1)}, bf16[4,16,2048]{2,1,0:T(8,128)(2,1)S(1)}, u32[]{:S(2)}, u32[]{:S(2)}) collective-permute-start(bf16[4,16,2048]{2,1,0:T(8,128)(2,1)S(1)} %get-tuple-element.43), channel_id=1, source_target_pairs={{0,24},{4,28},{8,16},{12,20},{16,8},{20,12},{24,0},{28,4},{1,25},{... | collective-permute-start | bytes 786440 | tf_op jit(solution)/shard_map/ppermute | solution.py:196
  46.2 14.2 %collective-permute-start.20 = (bf16[16,1024]{1,0:T(8,128)(2,1)S(1)}, bf16[16,1024]{1,0:T(8,128)(2,1)S(1)}, u32[]{:S(2)}, u32[]{:S(2)}) collective-permute-start(bf16[16,1024]{1,0:T(8,128)(2,1)S(1)} %get-tuple-element.52), channel_id=1, source_target_pairs={{0,1},{1,2},{2,3},{3,0},{4,5},{5,6},{6,7},{7,4},{8,9},{9,10},{10,1... | collective-permute-start | bytes 98312 | tf_op jit(solution)/shard_map/ppermute | solution.py:192
  46.2 14.1 %collective-permute-start.22 = (bf16[16,1024]{1,0:T(8,128)(2,1)S(1)}, bf16[16,1024]{1,0:T(8,128)(2,1)S(1)}, u32[]{:S(2)}, u32[]{:S(2)}) collective-permute-start(bf16[16,1024]{1,0:T(8,128)(2,1)S(1)} %get-tuple-element.53), channel_id=1, source_target_pairs={{0,3},{1,0},{2,1},{3,2},{4,7},{5,4},{6,5},{7,6},{8,11},{9,8},{10,9... | collective-permute-start | bytes 98312 | tf_op jit(solution)/shard_map/ppermute | solution.py:192
  50.0 10.3 %collective-permute-start.21 = (bf16[16,1024]{1,0:T(8,128)(2,1)S(1)}, bf16[16,1024]{1,0:T(8,128)(2,1)S(1)}, u32[]{:S(2)}, u32[]{:S(2)}) collective-permute-start(bf16[16,1024]{1,0:T(8,128)(2,1)S(1)} %get-tuple-element.54), channel_id=1, source_target_pairs={{0,2},{1,3},{2,0},{3,1},{4,6},{5,7},{6,4},{7,5},{8,10},{9,11},{10,... | collective-permute-start | bytes 98312 | tf_op jit(solution)/shard_map/ppermute | solution.py:192
  56.5 6.4 %collective-permute-start.13 = (bf16[16,2048]{1,0:T(8,128)(2,1)S(1)}, bf16[16,2048]{1,0:T(8,128)(2,1)S(1)}, u32[]{:S(2)}, u32[]{:S(2)}) collective-permute-start(bf16[16,2048]{1,0:T(8,128)(2,1)S(1)} %get-tuple-element.49), channel_id=1, source_target_pairs={{0,1},{1,2},{2,3},{3,0},{4,5},{5,6},{6,7},{7,4},{8,9},{9,10},{10,1... | collective-permute-start | bytes 196616 | tf_op jit(solution)/shard_map/ppermute | solution.py:192
  56.5 6.3 %collective-permute-start.15 = (bf16[16,2048]{1,0:T(8,128)(2,1)S(1)}, bf16[16,2048]{1,0:T(8,128)(2,1)S(1)}, u32[]{:S(2)}, u32[]{:S(2)}) collective-permute-start(bf16[16,2048]{1,0:T(8,128)(2,1)S(1)} %get-tuple-element.50), channel_id=1, source_target_pairs={{0,3},{1,0},{2,1},{3,2},{4,7},{5,4},{6,5},{7,6},{8,11},{9,8},{10,9... | collective-permute-start | bytes 196616 | tf_op jit(solution)/shard_map/ppermute | solution.py:192
  60.4 5.2 %collective-permute-start.14 = (bf16[16,2048]{1,0:T(8,128)(2,1)S(1)}, bf16[16,2048]{1,0:T(8,128)(2,1)S(1)}, u32[]{:S(2)}, u32[]{:S(2)}) collective-permute-start(bf16[16,2048]{1,0:T(8,128)(2,1)S(1)} %get-tuple-element.51), channel_id=1, source_target_pairs={{0,2},{1,3},{2,0},{3,1},{4,6},{5,7},{6,4},{7,5},{8,10},{9,11},{10,... | collective-permute-start | bytes 196616 | tf_op jit(solution)/shard_map/ppermute | solution.py:192

commit v11 on v9

--- a/solution.py
+++ b/solution.py
@@ -122,8 +122,9 @@
     for quarter in range(n_quarters):
         i, dq_ref = (quarter, dq_before) if quarter < n_before else (quarter - n_before, dq_turned)
         up = dot(act_cols, dq_ref[i * part : (i + 1) * part, :], 1, 1).astype(BF16)
+        j = head ^ quarter if by_slot else quarter
         for n in range(n_groups):
-            up_refs[n // per][quarter, n % per] = up[n * rank : (n + 1) * rank, :]
+            up_refs[n // per][j, n % per] = up[n * rank : (n + 1) * rank, :]
 
 
 def rank_kernel(by_slot, n_w, facts_ref, *refs):
@@ -137,7 +138,7 @@
     for c, w_ref in enumerate(w_refs):
         rows = None
         for quarter in range(n_quarters):
-            j = lax.rem(head + n_quarters - quarter, n_quarters) if by_slot else quarter
+            j = head ^ quarter if by_slot else quarter
             i, dq_ref = (quarter, dq_a) if quarter < n_a else (quarter - n_a, dq_b)
             dq = dq_ref[i * part : (i + 1) * part, :]
             new = dot(w_ref[:, j].reshape(n_adapters * rank, part), dq, 1, 0)
@@ -158,7 +159,7 @@
     cols = jnp.where(own, low, 0.0).astype(BF16)
     step = min(512, x_part)
     for j in range(n_quarters):
-        quarter = lax.rem(head + j, n_quarters) if by_slot else j
+        quarter = head ^ j if by_slot else j
         for start in range(0, x_part, step):
             at = pl.ds(pl.multiple_of(quarter * x_part + start, step), step)
             down = dot(cols, x_ref[:, at], 1, 0).astype(BF16)
@@ -187,8 +188,8 @@
     return jnp.sum(jnp.where(inside[None], told[:, :, None], 0), axis=1)
 
 
-def shifted(x, n_head, j):
-    return lax.ppermute(x, "head", [(i, (i + j) % n_head) for i in range(n_head)])
+def across(x, n_head, j):
+    return lax.ppermute(x, "head", [(i, i ^ j) for i in range(n_head)])
 
 
 def partnered(x, n_seq, bits):
@@ -206,7 +207,7 @@
     rank = adapter_up_weight.shape[1]
     n_adapters = owner.shape[0]
     n_seg = segment_length.shape[1]
-    by_slot = n_adapters == n_seq == 8
+    by_slot = n_adapters == n_seq == 8 and n_head == 4
     facts = token_facts(tok, segment_length[0], segment_adapter[0], owner, by_slot)
 
     reach = []
@@ -220,7 +221,7 @@
         parts.insert(0, lax.ppermute(own[tok - rows :], "head", shift))
 
     if by_slot:
-        w = [adapter_up_weight] + [shifted(adapter_up_weight, n_head, j) for j in range(1, n_head)]
+        w = [adapter_up_weight] + [across(adapter_up_weight, n_head, j) for j in range(1, n_head)]
         w = jnp.concatenate(w, axis=0)[None]
         w = [w] + [partnered(w, n_seq, 2 * m) for m in range(1, n_seq // 2)]
     else:
@@ -318,8 +319,7 @@
             cost_estimate=pl.CostEstimate(flops=0, bytes_accessed=SUM_BYTES, transcendentals=0),
             name="core_sum",
         )(down[0], partnered(down[1], n_seq, 1))
-        up = lax.all_to_all(over_cores(up, n_seq), "head", split_axis=0, concat_axis=0, tiled=True)
-        up = over_chips(jnp.sum(up.astype(F32), axis=0).astype(BF16), n_seq)
+        up = over_chips(over_z(over_cores(up, n_seq), n_head).astype(BF16), n_seq)
         down = over_z(over_chips(down, n_seq).astype(BF16), n_head)
     else:
         up = lax.all_to_all(up[0], "head", split_axis=0, concat_axis=0, tiled=True)
@@ -346,7 +346,7 @@
 
 
 def over_z(both, n_head):
-    return added(both[0], [shifted(both[j], n_head, j) for j in range(1, n_head)])
+    return added(both[0], [across(both[j], n_head, j) for j in range(1, n_head)])
 
 
 def spread(part, segment_adapter, owner, n_seq):

time: 69.3 us -> 64.2 us (0.926)
  waiting for transfers between devices: 17 us -> 12.6 us
  other arithmetic: 6.83 us -> 4.97 us
  starting transfers between devices: 31.7 us -> 32.8 us
    all_to_all x1 -> x0, waiting for transfers between devices: 11.5 us -> none  [on_device(): lax.all_to_all(over_cores(up, n_seq), 'head', split_axis=0, concat_axis=0...]
    ppermute x6 -> x9, waiting for transfers between devices: 4.5 us -> 11.6 us  [across(): return lax.ppermute(x, 'head', [(i, i ^ j) for i in range(n_head)])]
    all_to_all x1 -> x0, starting transfers between devices: 4.14 us -> none  [on_device(): lax.all_to_all(over_cores(up, n_seq), 'head', split_axis=0, concat_axis=0...]
    ppermute x2, starting transfers between devices: 4.39 us -> 8.2 us  [on_device(): parts.insert(0, lax.ppermute(own[tok - rows:], 'head', shift))]
    reduce_sum x1 -> x0, other arithmetic: 1.13 us -> none  [on_device(): up = over_chips(jnp.sum(up.astype(F32), axis=0).astype(BF16), n_seq)]
    ppermute x6 -> x9, starting transfers between devices: 11.8 us -> 12.8 us  [across(): return lax.ppermute(x, 'head', [(i, i ^ j) for i in range(n_head)])]
    convert_element_type x1, other arithmetic: 1 us -> 0.19 us  [over_cores(): (keep.astype(F32) + partnered(send, n_seq, 1).astype(F32)).astype(BF16)]
  transfers between devices with their start and end apart: 21 -> 23, of which waited for: 5 -> 7; matrix products, arithmetic and copies ran while one was open for 14% -> 12% of each run, Pallas kernels for 13% -> 14%
where the time goes in v11:
time: 64.2 us; the launch traced here: 63.8 us
  starting transfers between devices  32.8 us (51%)
  waiting for transfers between devices  12.6 us (20%)
  Pallas kernels  8.79 us (14%)
  other arithmetic  4.97 us (8%)
  local copies, waits for them, and re-layouts  3.66 us (6%)
  between operations  0.95 us (1%)
    ppermute x9, starting transfers between devices, across(): return lax.ppermute(x, 'head', [(i, i ^ j) for i in range(n_head)])  12.8 us
    ppermute x12, starting transfers between devices, partnered(): return lax.ppermute(x, 'seq', [(i, i ^ bits) for i in range(n_seq)])  11.8 us
    ppermute x9, waiting for transfers between devices, across(): return lax.ppermute(x, 'head', [(i, i ^ j) for i in range(n_head)])  11.6 us
    ppermute x2, starting transfers between devices, on_device(): parts.insert(0, lax.ppermute(own[tok - rows:], 'head', shift))  8.2 us
    pallas_call x2, Pallas kernels, attention(): pl.pallas_call(functools.partial(attention_kernel, by_slot, h * n_kv, n_k...  7.14 us
    unnamed x13, local copies, waits for them, and re-layouts  1.99 us
    mul x2, other arithmetic, on_device(): return (down.T[None] * ADAPTER_SCALE, up[None] * ADAPTER_SCALE)  1.35 us
  transfers between devices with their start and end apart: 23, of which 7 were waited for; matrix products, arithmetic and copies ran while one was open for 12% of the time, Pallas kernels for 14%

profile of v11, /device:TPU:0, one launch (start us, length us, event | category | flops | bytes accessed | tf_op | source)
XLA Modules:
  0.0 63.8 jit_solution(12338035535318995122)
XLA Ops:
  0.6 4.1 %collective-permute-start.3 = (bf16[1,16,1024]{2,1,0:T(8,128)(2,1)}, bf16[1,16,1024]{2,1,0:T(8,128)(2,1)S(1)}, u32[]{:S(2)}, u32[]{:S(2)}) collective-permute-start(bf16[1,16,1024]{2,1,0:T(8,128)(2,1)} %param.16), channel_id=1, source_target_pairs={{0,2},{1,3},{2,0},{3,1},{4,6},{5,7},{6,4},{7,5},{8,10},{9,11},{10,... | collective-permute-start | bytes 98312 | tf_op jit(solution)/shard_map/ppermute | solution.py:192
  4.8 1.6 %collective-permute-start.2 = (bf16[1,16,1024]{2,1,0:T(8,128)(2,1)}, bf16[1,16,1024]{2,1,0:T(8,128)(2,1)S(1)}, u32[]{:S(2)}, u32[]{:S(2)}) collective-permute-start(bf16[1,16,1024]{2,1,0:T(8,128)(2,1)} %param.16), channel_id=1, source_target_pairs={{0,1},{1,0},{2,3},{3,2},{4,5},{5,4},{6,7},{7,6},{8,9},{9,8},{10,11... | collective-permute-start | bytes 98312 | tf_op jit(solution)/shard_map/ppermute | solution.py:192
  6.3 0.9 %constant_dynamic-update-slice_fusion.1 = bf16[128,1024]{1,0:T(8,128)(2,1)S(1)} fusion(bf16[128,512]{1,0:T(8,128)(2,1)} %param.11), kind=kLoop, calls=%fused_computation.31 | loop fusion | bytes 262144
  7.2 0.9 %constant_dynamic-update-slice_fusion.refs_3_ = bf16[128,1024]{1,0:T(8,128)(2,1)S(1)} fusion(bf16[128,1024]{1,0:T(8,128)(2,1)S(1)} %constant_dynamic-update-slice_fusion.1, bf16[128,512]{1,0:T(8,128)(2,1)} %param.12), kind=kLoop, calls=%fused_computation.30 | loop fusion | bytes 262144 | tf_op jit(solution)/shard_map/concatenate | solution.py:217
  8.2 2.8 %collective-permute-start.1 = (bf16[128,1024]{1,0:T(8,128)(2,1)S(1)}, bf16[128,1024]{1,0:T(8,128)(2,1)S(1)}, u32[]{:S(2)}, u32[]{:S(2)}) collective-permute-start(bf16[128,1024]{1,0:T(8,128)(2,1)S(1)} %constant_dynamic-update-slice_fusion.refs_3_), channel_id=1, source_target_pairs={{0,1},{1,2},{2,3},{4,5},{5,6},{6,7},{8,9},{9,10},{10,11},{12,13},{... | collective-permute-start | bytes 786440 | tf_op jit(solution)/shard_map/ppermute | solution.py:221
  11.0 5.4 %collective-permute-start = (bf16[64,1024]{1,0:T(8,128)(2,1)S(1)}, bf16[64,1024]{1,0:T(8,128)(2,1)S(1)}, u32[]{:S(2)}, u32[]{:S(2)}) collective-permute-start(bf16[64,1024]{1,0:T(8,128)(2,1)S(1)} %slice.52), channel_id=1, source_target_pairs={{0,2},{1,3},{4,6},{5,7},{8,10},{9,11},{12,14},{13,15},{16,18},{17,... | collective-permute-start | bytes 393224 | tf_op jit(solution)/shard_map/ppermute | solution.py:221
  16.4 0.8 %select_reduce_fusion.2 = s32[8]{0:T(128)S(1)} fusion(s32[8]{0:T(128)} %bitcast.53), kind=kLoop, calls=%fused_computation.38 | loop fusion | flops 184 | bytes 64 | tf_op jit(solution)/shard_map/reduce_sum | solution.py:179
  17.2 0.7 %bitcast_add_fusion = s32[8]{0:T(128)S(1)} fusion(s32[8]{0:T(128)S(1)} %select_reduce_fusion.2, s32[1,8]{1,0:T(1,128)} %param.17), kind=kLoop, calls=%fused_computation.42 | loop fusion | flops 8 | bytes 96 | tf_op jit(solution)/shard_map/add | solution.py:186
  17.9 0.1 compare_and_fusion
  17.9 0.9 %select_reduce_fusion.1 = s32[8]{0:T(128)S(1)} fusion(s32[8]{0:T(128)} %param.19, s32[8]{0:T(128)} %bitcast.51), kind=kLoop, calls=%fused_computation.36 | loop fusion | flops 184 | bytes 96 | tf_op jit(solution)/shard_map/reduce_sum | solution.py:182
  18.8 1.0 %copy.13 = bf16[128,512]{0,1:T(8,128)(2,1)S(1)} copy(bf16[128,512]{1,0:T(8,128)(2,1)} %param.11) | data formatting | bytes 262144 | tf_op args[1]
  19.8 0.7 %stack.15 = s32[8,8]{1,0:T(8,128)S(1)} concatenate(s32[1,8]{1,0:T(1,128)S(1)} %bitcast.50, s32[1,8]{1,0:T(1,128)} %param.18, s32[1,8]{1,0:T(1,128)S(1)} %bitcast.52, s32[1,8]{1,0:T(1,128)S(1)} %broadcast.49, s32[4,8]{1,0:T(4,128)S(1)} %stack.14), dimensions={0} | concatenate | bytes 512 | tf_op jit(solution)/shard_map/stack | solution.py:187
  20.5 0.8 %maximum_bitcast_fusion = bf16[1,4,16,1024]{3,2,1,0:T(8,128)(2,1)S(1)} fusion(bf16[1,16,1024]{2,1,0:T(8,128)(2,1)S(1)} %collective-permute-done.4, bf16[1,16,1024]{2,1,0:T(8,128)(2,1)S(1)} %collective-permute-done.3, bf16[1,16,1024]{2,1,0:T(8,128)(2,1)S(1)} %collective-permute-done.2, bf16[1,16,1024]{2,1,0:T(8,128)(2,1)} %param.16), kind=kLoop, calls=%fused_computation.10 | loop fusion | flops 196608 | bytes 262144 | tf_op jit(solution)/shard_map/broadcast_in_dim | solution.py:225
  21.3 2.5 %collective-permute-start.7 = (bf16[1,4,16,1024]{3,2,1,0:T(8,128)(2,1)S(1)}, bf16[1,4,16,1024]{3,2,1,0:T(8,128)(2,1)S(1)}, u32[]{:S(2)}, u32[]{:S(2)}) collective-permute-start(bf16[1,4,16,1024]{3,2,1,0:T(8,128)(2,1)S(1)} %maximum_bitcast_fusion), channel_id=1, source_target_pairs={{0,24},{4,28},{8,16},{12,20},{16,8},{20,12},{24,0},{28,4},{1,25},{... | collective-permute-start | bytes 393224 | tf_op jit(solution)/shard_map/ppermute | solution.py:196
  23.8 0.5 collective-permute-start.6
  24.3 0.5 collective-permute-start.5
  24.9 0.1 select_reduce_fusion.facts_ref.refs_0_
  25.0 0.3 layout.1
  25.3 3.4 %attention_0.1.refs_2_ = bf16[2048,128]{1,0:T(8,128)(2,1)S(1)} custom-call(bf16[320,512]{1,0:T(8,128)(2,1)S(1)} %get-tuple-element.24.k_all, bf16[320,512]{1,0:T(8,128)(2,1)S(1)} %get-tuple-element.25.v_all, bf16[512,320]{1,0:T(8,128)(2,1)S(1)} %get-tuple-element.26.k_turned, f32[320,128]{1,0:T(8,128)S(1)} %get-tuple-element.27.bias, ...), custom_call_target="tpu_custom_call" | custom-call | flops 503316480 | bytes 2097152 | tf_op jit(solution)/shard_map/attention_0/pallas_call | solution.py:258
  28.7 0.8 %collective-permute-done.6 = bf16[1,4,16,1024]{3,2,1,0:T(8,128)(2,1)S(1)} collective-permute-done((bf16[1,4,16,1024]{3,2,1,0:T(8,128)(2,1)S(1)}, bf16[1,4,16,1024]{3,2,1,0:T(8,128)(2,1)S(1)}, u32[]{:S(2)}, u32[]{:S(2)}) %collective-permute-start.6) | collective-permute-done | bytes 131104 | tf_op jit(solution)/shard_map/ppermute | solution.py:196
  29.6 3.8 %attention_1.1 = (bf16[2048,128]{1,0:T(8,128)(2,1)S(1)}, bf16[4,4,16,1024]{3,2,1,0:T(8,128)(2,1)S(1)}, bf16[4,4,16,1024]{3,2,1,0:T(8,128)(2,1)S(1)}) custom-call(bf16[320,512]{1,0:T(8,128)(2,1)S(1)} %get-tuple-element.24.k_all, bf16[320,512]{1,0:T(8,128)(2,1)S(1)} %get-tuple-element.25.v_all, bf16[512,320]{1,0:T(8,128)(2,1)S(1)} %get-tuple-element.26.k_turned, ...), custom_call_target="tpu_custom_call" | custom-call | flops 503316480 | bytes 2097152 | tf_op jit(solution)/shard_map/attention_1/pallas_call | solution.py:258
  33.4 0.5 collective-permute-start.16
  33.9 0.4 rank_gradient.1.rank_ref
  34.4 0.7 %down_parts.1 = (bf16[4,4,16,2048]{3,2,1,0:T(8,128)(2,1)S(1)}, bf16[4,4,16,2048]{3,2,1,0:T(8,128)(2,1)S(1)}) custom-call(s32[8,128]{1,0:T(8,128)S(1)} %select_reduce_fusion.facts_ref.refs_0_, bf16[128,8192]{1,0:T(8,128)(2,1)S(1)} %copy-done.2, bf16[16,128]{1,0:T(8,128)(2,1)S(1)} %rank_gradient.1.rank_ref), custom_call_target="tpu_custom_call" | custom-call | flops 268435456 | bytes 8388608 | tf_op jit(solution)/shard_map/down_parts/pallas_call | solution.py:298
  35.1 0.1 collective-permute-start.9
  35.2 0.3 collective-permute-done.16
  35.5 0.2 add_convert_fusion
  35.8 0.7 %collective-permute-start.19 = (bf16[4,16,1024]{2,1,0:T(8,128)(2,1)S(1)}, bf16[4,16,1024]{2,1,0:T(8,128)(2,1)S(1)}, u32[]{:S(2)}, u32[]{:S(2)}) collective-permute-start(bf16[4,16,1024]{2,1,0:T(8,128)(2,1)S(1)} %get-tuple-element.47), channel_id=1, source_target_pairs={{0,3},{1,2},{2,1},{3,0},{4,7},{5,6},{6,5},{7,4},{8,11},{9,10},{10,... | collective-permute-start | bytes 393224 | tf_op jit(solution)/shard_map/ppermute | solution.py:192
  36.5 2.7 %collective-permute-start.18 = (bf16[4,16,1024]{2,1,0:T(8,128)(2,1)S(1)}, bf16[4,16,1024]{2,1,0:T(8,128)(2,1)S(1)}, u32[]{:S(2)}, u32[]{:S(2)}) collective-permute-start(bf16[4,16,1024]{2,1,0:T(8,128)(2,1)S(1)} %get-tuple-element.48), channel_id=1, source_target_pairs={{0,2},{1,3},{2,0},{3,1},{4,6},{5,7},{6,4},{7,5},{8,10},{9,11},{10,... | collective-permute-start | bytes 393224 | tf_op jit(solution)/shard_map/ppermute | solution.py:192
  39.3 0.2 core_sum.1
  39.5 1.2 %collective-permute-start.10 = (bf16[4,16,2048]{2,1,0:T(8,128)(2,1)S(1)}, bf16[4,16,2048]{2,1,0:T(8,128)(2,1)S(1)}, u32[]{:S(2)}, u32[]{:S(2)}) collective-permute-start(bf16[4,16,2048]{2,1,0:T(8,128)(2,1)S(1)} %get-tuple-element.41), channel_id=1, source_target_pairs={{0,8},{4,12},{8,0},{12,4},{16,24},{20,28},{24,16},{28,20},{1,9},{5... | collective-permute-start | bytes 786440 | tf_op jit(solution)/shard_map/ppermute | solution.py:196
  40.7 1.1 %collective-permute-start.11 = (bf16[4,16,2048]{2,1,0:T(8,128)(2,1)S(1)}, bf16[4,16,2048]{2,1,0:T(8,128)(2,1)S(1)}, u32[]{:S(2)}, u32[]{:S(2)}) collective-permute-start(bf16[4,16,2048]{2,1,0:T(8,128)(2,1)S(1)} %get-tuple-element.42), channel_id=1, source_target_pairs={{0,16},{4,20},{8,24},{12,28},{16,0},{20,4},{24,8},{28,12},{1,17},{... | collective-permute-start | bytes 786440 | tf_op jit(solution)/shard_map/ppermute | solution.py:196
  41.8 2.5 %collective-permute-done.17 = bf16[4,16,1024]{2,1,0:T(8,128)(2,1)S(1)} collective-permute-done((bf16[4,16,1024]{2,1,0:T(8,128)(2,1)S(1)}, bf16[4,16,1024]{2,1,0:T(8,128)(2,1)S(1)}, u32[]{:S(2)}, u32[]{:S(2)}) %collective-permute-start.17) | collective-permute-done | bytes 131104 | tf_op jit(solution)/shard_map/ppermute | solution.py:192
  44.4 1.7 %collective-permute-start.12 = (bf16[4,16,2048]{2,1,0:T(8,128)(2,1)S(1)}, bf16[4,16,2048]{2,1,0:T(8,128)(2,1)S(1)}, u32[]{:S(2)}, u32[]{:S(2)}) collective-permute-start(bf16[4,16,2048]{2,1,0:T(8,128)(2,1)S(1)} %get-tuple-element.43), channel_id=1, source_target_pairs={{0,24},{4,28},{8,16},{12,20},{16,8},{20,12},{24,0},{28,4},{1,25},{... | collective-permute-start | bytes 786440 | tf_op jit(solution)/shard_map/ppermute | solution.py:196
  46.1 5.1 %collective-permute-done.18 = bf16[4,16,1024]{2,1,0:T(8,128)(2,1)S(1)} collective-permute-done((bf16[4,16,1024]{2,1,0:T(8,128)(2,1)S(1)}, bf16[4,16,1024]{2,1,0:T(8,128)(2,1)S(1)}, u32[]{:S(2)}, u32[]{:S(2)}) %collective-permute-start.18) | collective-permute-done | bytes 131104 | tf_op jit(solution)/shard_map/ppermute | solution.py:192
  51.2 0.1 fusion.2
  51.2 1.2 %collective-permute-start.20 = (bf16[16,1024]{1,0:T(8,128)(2,1)S(1)}, bf16[16,1024]{1,0:T(8,128)(2,1)S(1)}, u32[]{:S(2)}, u32[]{:S(2)}) collective-permute-start(bf16[16,1024]{1,0:T(8,128)(2,1)S(1)} %get-tuple-element.52), channel_id=1, source_target_pairs={{0,8},{4,12},{8,0},{12,4},{16,24},{20,28},{24,16},{28,20},{1,9},{5... | collective-permute-start | bytes 98312 | tf_op jit(solution)/shard_map/ppermute | solution.py:196
  52.4 1.7 %collective-permute-start.22 = (bf16[16,1024]{1,0:T(8,128)(2,1)S(1)}, bf16[16,1024]{1,0:T(8,128)(2,1)S(1)}, u32[]{:S(2)}, u32[]{:S(2)}) collective-permute-start(bf16[16,1024]{1,0:T(8,128)(2,1)S(1)} %get-tuple-element.53), channel_id=1, source_target_pairs={{0,24},{4,28},{8,16},{12,20},{16,8},{20,12},{24,0},{28,4},{1,25},{... | collective-permute-start | bytes 98312 | tf_op jit(solution)/shard_map/ppermute | solution.py:196
  54.2 0.6 collective-permute-start.21
  54.8 0.1 add_convert_fusion.1
  55.0 1.0 %collective-permute-start.13 = (bf16[16,2048]{1,0:T(8,128)(2,1)S(1)}, bf16[16,2048]{1,0:T(8,128)(2,1)S(1)}, u32[]{:S(2)}, u32[]{:S(2)}) collective-permute-start(bf16[16,2048]{1,0:T(8,128)(2,1)S(1)} %get-tuple-element.49), channel_id=1, source_target_pairs={{0,1},{1,0},{2,3},{3,2},{4,5},{5,4},{6,7},{7,6},{8,9},{9,8},{10,11... | collective-permute-start | bytes 196616 | tf_op jit(solution)/shard_map/ppermute | solution.py:192
  56.0 0.3 collective-permute-start.15
  56.3 2.2 %collective-permute-start.14 = (bf16[16,2048]{1,0:T(8,128)(2,1)S(1)}, bf16[16,2048]{1,0:T(8,128)(2,1)S(1)}, u32[]{:S(2)}, u32[]{:S(2)}) collective-permute-start(bf16[16,2048]{1,0:T(8,128)(2,1)S(1)} %get-tuple-element.51), channel_id=1, source_target_pairs={{0,2},{1,3},{2,0},{3,1},{4,6},{5,7},{6,4},{7,5},{8,10},{9,11},{10,... | collective-permute-start | bytes 196616 | tf_op jit(solution)/shard_map/ppermute | solution.py:192
  58.5 0.7 %fusion.10 = f32[1,16,1024]{2,1,0:T(8,128)} fusion(bf16[16,1024]{1,0:T(8,128)(2,1)S(1)} %collective-permute-done.22, bf16[16,1024]{1,0:T(8,128)(2,1)S(1)} %collective-permute-done.21, bf16[16,1024]{1,0:T(8,128)(2,1)S(1)} %collective-permute-done.20, bf16[4,16,1024]{2,1,0:T(8,128)(2,1)S(1)} %fusion.2), kind=kLoop, calls=%fused_computation.24 | loop fusion | flops 131072 | bytes 196608 | tf_op jit(solution)/shard_map/mul | solution.py:329
  59.2 0.7 %collective-permute-done.13 = bf16[16,2048]{1,0:T(8,128)(2,1)S(1)} collective-permute-done((bf16[16,2048]{1,0:T(8,128)(2,1)S(1)}, bf16[16,2048]{1,0:T(8,128)(2,1)S(1)}, u32[]{:S(2)}, u32[]{:S(2)}) %collective-permute-start.13) | collective-permute-done | bytes 65568 | tf_op jit(solution)/shard_map/ppermute | solution.py:192
  59.9 2.3 %collective-permute-done.15 = bf16[16,2048]{1,0:T(8,128)(2,1)S(1)} collective-permute-done((bf16[16,2048]{1,0:T(8,128)(2,1)S(1)}, bf16[16,2048]{1,0:T(8,128)(2,1)S(1)}, u32[]{:S(2)}, u32[]{:S(2)}) %collective-permute-start.15) | collective-permute-done | bytes 65568 | tf_op jit(solution)/shard_map/ppermute | solution.py:192
  62.2 1.0 %collective-permute-done.14 = bf16[16,2048]{1,0:T(8,128)(2,1)S(1)} collective-permute-done((bf16[16,2048]{1,0:T(8,128)(2,1)S(1)}, bf16[16,2048]{1,0:T(8,128)(2,1)S(1)}, u32[]{:S(2)}, u32[]{:S(2)}) %collective-permute-start.14) | collective-permute-done | bytes 65568 | tf_op jit(solution)/shard_map/ppermute | solution.py:192
  63.1 0.7 %fusion.6 = f32[1,2048,16]{1,2,0:T(8,128)} fusion(bf16[16,2048]{1,0:T(8,128)(2,1)S(1)} %collective-permute-done.15, bf16[16,2048]{1,0:T(8,128)(2,1)S(1)} %collective-permute-done.14, bf16[16,2048]{1,0:T(8,128)(2,1)S(1)} %collective-permute-done.13, bf16[4,16,2048]{2,1,0:T(8,128)(2,1)S(1)} %add_convert_fusion.1), kind=kLoop, calls=%fused_computation.15 | loop fusion | flops 262144 | bytes 393216 | tf_op jit(solution)/shard_map/mul | solution.py:329
  (38 shorter events, 0.4 us)
Async XLA Ops:
  0.6 24.6 %copy-start.1 = (bf16[128,4096]{1,0:T(8,128)(2,1)S(1)}, bf16[128,4096]{1,0:T(8,128)(2,1)}, u32[]{:S(2)}) copy-start(bf16[128,4096]{1,0:T(8,128)(2,1)} %g_hbm.3) | copy-start | bytes 3145732
  0.6 24.6 %copy-start = (bf16[128,4096]{1,0:T(8,128)(2,1)S(1)}, bf16[128,4096]{1,0:T(8,128)(2,1)}, u32[]{:S(2)}) copy-start(bf16[128,4096]{1,0:T(8,128)(2,1)} %q_hbm.3) | copy-start | bytes 3145732
  0.6 19.9 %collective-permute-start.3 = (bf16[1,16,1024]{2,1,0:T(8,128)(2,1)}, bf16[1,16,1024]{2,1,0:T(8,128)(2,1)S(1)}, u32[]{:S(2)}, u32[]{:S(2)}) collective-permute-start(bf16[1,16,1024]{2,1,0:T(8,128)(2,1)} %param.16), channel_id=1, source_target_pairs={{0,2},{1,3},{2,0},{3,1},{4,6},{5,7},{6,4},{7,5},{8,10},{9,11},{10,... | collective-permute-start | bytes 98312 | tf_op jit(solution)/shard_map/ppermute | solution.py:192
  4.8 15.8 %collective-permute-start.2 = (bf16[1,16,1024]{2,1,0:T(8,128)(2,1)}, bf16[1,16,1024]{2,1,0:T(8,128)(2,1)S(1)}, u32[]{:S(2)}, u32[]{:S(2)}) collective-permute-start(bf16[1,16,1024]{2,1,0:T(8,128)(2,1)} %param.16), channel_id=1, source_target_pairs={{0,1},{1,0},{2,3},{3,2},{4,5},{5,4},{6,7},{7,6},{8,9},{9,8},{10,11... | collective-permute-start | bytes 98312 | tf_op jit(solution)/shard_map/ppermute | solution.py:192
  6.3 14.2 %collective-permute-start.4 = (bf16[1,16,1024]{2,1,0:T(8,128)(2,1)}, bf16[1,16,1024]{2,1,0:T(8,128)(2,1)S(1)}, u32[]{:S(2)}, u32[]{:S(2)}) collective-permute-start(bf16[1,16,1024]{2,1,0:T(8,128)(2,1)} %param.16), channel_id=1, source_target_pairs={{0,3},{1,2},{2,1},{3,0},{4,7},{5,6},{6,5},{7,4},{8,11},{9,10},{10,... | collective-permute-start | bytes 98312 | tf_op jit(solution)/shard_map/ppermute | solution.py:192
  8.2 16.8 %collective-permute-start.1 = (bf16[128,1024]{1,0:T(8,128)(2,1)S(1)}, bf16[128,1024]{1,0:T(8,128)(2,1)S(1)}, u32[]{:S(2)}, u32[]{:S(2)}) collective-permute-start(bf16[128,1024]{1,0:T(8,128)(2,1)S(1)} %constant_dynamic-update-slice_fusion.refs_3_), channel_id=1, source_target_pairs={{0,1},{1,2},{2,3},{4,5},{5,6},{6,7},{8,9},{9,10},{10,11},{12,13},{... | collective-permute-start | bytes 786440 | tf_op jit(solution)/shard_map/ppermute | solution.py:221
  11.0 14.0 %collective-permute-start = (bf16[64,1024]{1,0:T(8,128)(2,1)S(1)}, bf16[64,1024]{1,0:T(8,128)(2,1)S(1)}, u32[]{:S(2)}, u32[]{:S(2)}) collective-permute-start(bf16[64,1024]{1,0:T(8,128)(2,1)S(1)} %slice.52), channel_id=1, source_target_pairs={{0,2},{1,3},{4,6},{5,7},{8,10},{9,11},{12,14},{13,15},{16,18},{17,... | collective-permute-start | bytes 393224 | tf_op jit(solution)/shard_map/ppermute | solution.py:221
  21.3 7.4 %collective-permute-start.7 = (bf16[1,4,16,1024]{3,2,1,0:T(8,128)(2,1)S(1)}, bf16[1,4,16,1024]{3,2,1,0:T(8,128)(2,1)S(1)}, u32[]{:S(2)}, u32[]{:S(2)}) collective-permute-start(bf16[1,4,16,1024]{3,2,1,0:T(8,128)(2,1)S(1)} %maximum_bitcast_fusion), channel_id=1, source_target_pairs={{0,24},{4,28},{8,16},{12,20},{16,8},{20,12},{24,0},{28,4},{1,25},{... | collective-permute-start | bytes 393224 | tf_op jit(solution)/shard_map/ppermute | solution.py:196
  23.8 5.6 %collective-permute-start.6 = (bf16[1,4,16,1024]{3,2,1,0:T(8,128)(2,1)S(1)}, bf16[1,4,16,1024]{3,2,1,0:T(8,128)(2,1)S(1)}, u32[]{:S(2)}, u32[]{:S(2)}) collective-permute-start(bf16[1,4,16,1024]{3,2,1,0:T(8,128)(2,1)S(1)} %maximum_bitcast_fusion), channel_id=1, source_target_pairs={{0,16},{4,20},{8,24},{12,28},{16,0},{20,4},{24,8},{28,12},{1,17},{... | collective-permute-start | bytes 393224 | tf_op jit(solution)/shard_map/ppermute | solution.py:196
  24.3 5.1 %collective-permute-start.5 = (bf16[1,4,16,1024]{3,2,1,0:T(8,128)(2,1)S(1)}, bf16[1,4,16,1024]{3,2,1,0:T(8,128)(2,1)S(1)}, u32[]{:S(2)}, u32[]{:S(2)}) collective-permute-start(bf16[1,4,16,1024]{3,2,1,0:T(8,128)(2,1)S(1)} %maximum_bitcast_fusion), channel_id=1, source_target_pairs={{0,8},{4,12},{8,0},{12,4},{16,24},{20,28},{24,16},{28,20},{1,9},{5... | collective-permute-start | bytes 393224 | tf_op jit(solution)/shard_map/ppermute | solution.py:196
  25.3 4.3 %copy-start.3 = (bf16[128,16]{0,1:T(8,128)(2,1)S(1)}, bf16[128,16]{0,1:T(8,128)(2,1)}, u32[]{:S(2)}) copy-start(bf16[128,16]{0,1:T(8,128)(2,1)} %param.15) | copy-start | bytes 12292
  29.5 3.9 %collective-permute-start.8 = (bf16[4,4,16,1024]{3,2,1,0:T(8,128)(2,1)S(1)}, bf16[4,4,16,1024]{3,2,1,0:T(8,128)(2,1)S(1)}, u32[]{:S(2)}, u32[]{:S(2)}) collective-permute-start(bf16[4,4,16,1024]{3,2,1,0:T(8,128)(2,1)S(1)} %constant_dynamic-update-slice_fusion.2.refs_0_), channel_id=1, source_target_pairs={{0,4},{4,0},{8,12},{12,8},{16,20},{20,16},{24,28},{28,24},{1,5},{5... | collective-permute-start | bytes 1572872 | tf_op jit(solution)/shard_map/ppermute | solution.py:196
  29.6 4.8 %copy-start.2 = (bf16[128,8192]{1,0:T(8,128)(2,1)S(1)}, bf16[128,8192]{1,0:T(8,128)(2,1)}, u32[]{:S(2)}) copy-start(bf16[128,8192]{1,0:T(8,128)(2,1)} %x_ref.1) | copy-start | bytes 6291460
  33.4 2.1 %collective-permute-start.16 = (bf16[4,4,16,1024]{3,2,1,0:T(8,128)(2,1)S(1)}, bf16[4,4,16,1024]{3,2,1,0:T(8,128)(2,1)S(1)}, u32[]{:S(2)}, u32[]{:S(2)}) collective-permute-start(bf16[4,4,16,1024]{3,2,1,0:T(8,128)(2,1)S(1)} %get-tuple-element.45), channel_id=1, source_target_pairs={{0,4},{4,0},{8,12},{12,8},{16,20},{20,16},{24,28},{28,24},{1,5},{5... | collective-permute-start | bytes 1572872 | tf_op jit(solution)/shard_map/ppermute | solution.py:196
  35.1 4.2 %collective-permute-start.9 = (bf16[4,4,16,2048]{3,2,1,0:T(8,128)(2,1)S(1)}, bf16[4,4,16,2048]{3,2,1,0:T(8,128)(2,1)S(1)}, u32[]{:S(2)}, u32[]{:S(2)}) collective-permute-start(bf16[4,4,16,2048]{3,2,1,0:T(8,128)(2,1)S(1)} %get-tuple-element.39), channel_id=1, source_target_pairs={{0,4},{4,0},{8,12},{12,8},{16,20},{20,16},{24,28},{28,24},{1,5},{5... | collective-permute-start | bytes 3145736 | tf_op jit(solution)/shard_map/ppermute | solution.py:196
  35.7 8.7 %collective-permute-start.17 = (bf16[4,16,1024]{2,1,0:T(8,128)(2,1)S(1)}, bf16[4,16,1024]{2,1,0:T(8,128)(2,1)S(1)}, u32[]{:S(2)}, u32[]{:S(2)}) collective-permute-start(bf16[4,16,1024]{2,1,0:T(8,128)(2,1)S(1)} %get-tuple-element.46), channel_id=1, source_target_pairs={{0,1},{1,0},{2,3},{3,2},{4,5},{5,4},{6,7},{7,6},{8,9},{9,8},{10,11... | collective-permute-start | bytes 393224 | tf_op jit(solution)/shard_map/ppermute | solution.py:192
  35.8 10.3 %collective-permute-start.19 = (bf16[4,16,1024]{2,1,0:T(8,128)(2,1)S(1)}, bf16[4,16,1024]{2,1,0:T(8,128)(2,1)S(1)}, u32[]{:S(2)}, u32[]{:S(2)}) collective-permute-start(bf16[4,16,1024]{2,1,0:T(8,128)(2,1)S(1)} %get-tuple-element.47), channel_id=1, source_target_pairs={{0,3},{1,2},{2,1},{3,0},{4,7},{5,6},{6,5},{7,4},{8,11},{9,10},{10,... | collective-permute-start | bytes 393224 | tf_op jit(solution)/shard_map/ppermute | solution.py:192
  36.5 14.6 %collective-permute-start.18 = (bf16[4,16,1024]{2,1,0:T(8,128)(2,1)S(1)}, bf16[4,16,1024]{2,1,0:T(8,128)(2,1)S(1)}, u32[]{:S(2)}, u32[]{:S(2)}) collective-permute-start(bf16[4,16,1024]{2,1,0:T(8,128)(2,1)S(1)} %get-tuple-element.48), channel_id=1, source_target_pairs={{0,2},{1,3},{2,0},{3,1},{4,6},{5,7},{6,4},{7,5},{8,10},{9,11},{10,... | collective-permute-start | bytes 393224 | tf_op jit(solution)/shard_map/ppermute | solution.py:192
  39.5 14.7 %collective-permute-start.10 = (bf16[4,16,2048]{2,1,0:T(8,128)(2,1)S(1)}, bf16[4,16,2048]{2,1,0:T(8,128)(2,1)S(1)}, u32[]{:S(2)}, u32[]{:S(2)}) collective-permute-start(bf16[4,16,2048]{2,1,0:T(8,128)(2,1)S(1)} %get-tuple-element.41), channel_id=1, source_target_pairs={{0,8},{4,12},{8,0},{12,4},{16,24},{20,28},{24,16},{28,20},{1,9},{5... | collective-permute-start | bytes 786440 | tf_op jit(solution)/shard_map/ppermute | solution.py:196
  40.7 14.1 %collective-permute-start.11 = (bf16[4,16,2048]{2,1,0:T(8,128)(2,1)S(1)}, bf16[4,16,2048]{2,1,0:T(8,128)(2,1)S(1)}, u32[]{:S(2)}, u32[]{:S(2)}) collective-permute-start(bf16[4,16,2048]{2,1,0:T(8,128)(2,1)S(1)} %get-tuple-element.42), channel_id=1, source_target_pairs={{0,16},{4,20},{8,24},{12,28},{16,0},{20,4},{24,8},{28,12},{1,17},{... | collective-permute-start | bytes 786440 | tf_op jit(solution)/shard_map/ppermute | solution.py:196
  44.4 10.5 %collective-permute-start.12 = (bf16[4,16,2048]{2,1,0:T(8,128)(2,1)S(1)}, bf16[4,16,2048]{2,1,0:T(8,128)(2,1)S(1)}, u32[]{:S(2)}, u32[]{:S(2)}) collective-permute-start(bf16[4,16,2048]{2,1,0:T(8,128)(2,1)S(1)} %get-tuple-element.43), channel_id=1, source_target_pairs={{0,24},{4,28},{8,16},{12,20},{16,8},{20,12},{24,0},{28,4},{1,25},{... | collective-permute-start | bytes 786440 | tf_op jit(solution)/shard_map/ppermute | solution.py:196
  51.2 5.1 %collective-permute-start.20 = (bf16[16,1024]{1,0:T(8,128)(2,1)S(1)}, bf16[16,1024]{1,0:T(8,128)(2,1)S(1)}, u32[]{:S(2)}, u32[]{:S(2)}) collective-permute-start(bf16[16,1024]{1,0:T(8,128)(2,1)S(1)} %get-tuple-element.52), channel_id=1, source_target_pairs={{0,8},{4,12},{8,0},{12,4},{16,24},{20,28},{24,16},{28,20},{1,9},{5... | collective-permute-start | bytes 98312 | tf_op jit(solution)/shard_map/ppermute | solution.py:196
  52.4 6.1 %collective-permute-start.22 = (bf16[16,1024]{1,0:T(8,128)(2,1)S(1)}, bf16[16,1024]{1,0:T(8,128)(2,1)S(1)}, u32[]{:S(2)}, u32[]{:S(2)}) collective-permute-start(bf16[16,1024]{1,0:T(8,128)(2,1)S(1)} %get-tuple-element.53), channel_id=1, source_target_pairs={{0,24},{4,28},{8,16},{12,20},{16,8},{20,12},{24,0},{28,4},{1,25},{... | collective-permute-start | bytes 98312 | tf_op jit(solution)/shard_map/ppermute | solution.py:196
  54.2 4.4 %collective-permute-start.21 = (bf16[16,1024]{1,0:T(8,128)(2,1)S(1)}, bf16[16,1024]{1,0:T(8,128)(2,1)S(1)}, u32[]{:S(2)}, u32[]{:S(2)}) collective-permute-start(bf16[16,1024]{1,0:T(8,128)(2,1)S(1)} %get-tuple-element.54), channel_id=1, source_target_pairs={{0,16},{4,20},{8,24},{12,28},{16,0},{20,4},{24,8},{28,12},{1,17},{... | collective-permute-start | bytes 98312 | tf_op jit(solution)/shard_map/ppermute | solution.py:196
  55.0 4.9 %collective-permute-start.13 = (bf16[16,2048]{1,0:T(8,128)(2,1)S(1)}, bf16[16,2048]{1,0:T(8,128)(2,1)S(1)}, u32[]{:S(2)}, u32[]{:S(2)}) collective-permute-start(bf16[16,2048]{1,0:T(8,128)(2,1)S(1)} %get-tuple-element.49), channel_id=1, source_target_pairs={{0,1},{1,0},{2,3},{3,2},{4,5},{5,4},{6,7},{7,6},{8,9},{9,8},{10,11... | collective-permute-start | bytes 196616 | tf_op jit(solution)/shard_map/ppermute | solution.py:192
  56.0 6.2 %collective-permute-start.15 = (bf16[16,2048]{1,0:T(8,128)(2,1)S(1)}, bf16[16,2048]{1,0:T(8,128)(2,1)S(1)}, u32[]{:S(2)}, u32[]{:S(2)}) collective-permute-start(bf16[16,2048]{1,0:T(8,128)(2,1)S(1)} %get-tuple-element.50), channel_id=1, source_target_pairs={{0,3},{1,2},{2,1},{3,0},{4,7},{5,6},{6,5},{7,4},{8,11},{9,10},{10,... | collective-permute-start | bytes 196616 | tf_op jit(solution)/shard_map/ppermute | solution.py:192
  56.3 6.8 %collective-permute-start.14 = (bf16[16,2048]{1,0:T(8,128)(2,1)S(1)}, bf16[16,2048]{1,0:T(8,128)(2,1)S(1)}, u32[]{:S(2)}, u32[]{:S(2)}) collective-permute-start(bf16[16,2048]{1,0:T(8,128)(2,1)S(1)} %get-tuple-element.51), channel_id=1, source_target_pairs={{0,2},{1,3},{2,0},{3,1},{4,6},{5,7},{6,4},{7,5},{8,10},{9,11},{10,... | collective-permute-start | bytes 196616 | tf_op jit(solution)/shard_map/ppermute | solution.py:192

commit v12 on v11

--- a/solution.py
+++ b/solution.py
@@ -138,7 +138,7 @@
     for c, w_ref in enumerate(w_refs):
         rows = None
         for quarter in range(n_quarters):
-            j = head ^ quarter if by_slot else quarter
+            j = lax.rem(head + n_quarters - quarter, n_quarters) if by_slot else quarter
             i, dq_ref = (quarter, dq_a) if quarter < n_a else (quarter - n_a, dq_b)
             dq = dq_ref[i * part : (i + 1) * part, :]
             new = dot(w_ref[:, j].reshape(n_adapters * rank, part), dq, 1, 0)
@@ -188,6 +188,10 @@
     return jnp.sum(jnp.where(inside[None], told[:, :, None], 0), axis=1)
 
 
+def shifted(x, n_head, j):
+    return lax.ppermute(x, "head", [(i, (i + j) % n_head) for i in range(n_head)])
+
+
 def across(x, n_head, j):
     return lax.ppermute(x, "head", [(i, i ^ j) for i in range(n_head)])
 
@@ -221,7 +225,7 @@
         parts.insert(0, lax.ppermute(own[tok - rows :], "head", shift))
 
     if by_slot:
-        w = [adapter_up_weight] + [across(adapter_up_weight, n_head, j) for j in range(1, n_head)]
+        w = [adapter_up_weight] + [shifted(adapter_up_weight, n_head, j) for j in range(1, n_head)]
         w = jnp.concatenate(w, axis=0)[None]
         w = [w] + [partnered(w, n_seq, 2 * m) for m in range(1, n_seq // 2)]
     else:
@@ -319,8 +323,8 @@
             cost_estimate=pl.CostEstimate(flops=0, bytes_accessed=SUM_BYTES, transcendentals=0),
             name="core_sum",
         )(down[0], partnered(down[1], n_seq, 1))
-        up = over_chips(over_z(over_cores(up, n_seq), n_head).astype(BF16), n_seq)
-        down = over_z(over_chips(down, n_seq).astype(BF16), n_head)
+        up = over_chips(over_z(over_cores(up, n_seq), n_head, (1, 2, 3)).astype(BF16), n_seq)
+        down = over_z(over_chips(down, n_seq).astype(BF16), n_head, (3, 1, 2))
     else:
         up = lax.all_to_all(up[0], "head", split_axis=0, concat_axis=0, tiled=True)
         up = spread(jnp.sum(up.astype(F32), axis=0), segment_adapter, owner, n_seq)
@@ -345,8 +349,8 @@
     return added(both[0], [partnered(both[m], n_seq, 2 * m) for m in range(1, n_seq // 2)])
 
 
-def over_z(both, n_head):
-    return added(both[0], [across(both[j], n_head, j) for j in range(1, n_head)])
+def over_z(both, n_head, order):
+    return added(both[0], [across(both[j], n_head, j) for j in order])
 
 
 def spread(part, segment_adapter, owner, n_seq):

time: 64.2 us -> 62.1 us (0.967)
  waiting for transfers between devices: 12.6 us -> 11.4 us
  starting transfers between devices: 32.8 us -> 32 us
    ppermute x0 -> x3, starting transfers between devices: none -> 7.93 us  [shifted(): lax.ppermute(x, 'head', [(i, (i + j) % n_head) for i in range(n_head)])]
    ppermute x9 -> x6, starting transfers between devices: 12.8 us -> 8.01 us  [across(): return lax.ppermute(x, 'head', [(i, i ^ j) for i in range(n_head)])]
    ppermute x2, starting transfers between devices: 8.2 us -> 4.39 us  [on_device(): parts.insert(0, lax.ppermute(own[tok - rows:], 'head', shift))]
    ppermute x9 -> x6, waiting for transfers between devices: 11.6 us -> 10.5 us  [across(): return lax.ppermute(x, 'head', [(i, i ^ j) for i in range(n_head)])]
  transfers between devices with their start and end apart: 23 -> 23, of which waited for: 7 -> 6; matrix products, arithmetic and copies ran while one was open for 12% -> 13% of each run, Pallas kernels for 14% -> 14%
where the time goes in v12:
time: 62.1 us; the launch traced here: 61.8 us
  starting transfers between devices  32 us (52%)
  waiting for transfers between devices  11.4 us (18%)
  Pallas kernels  8.8 us (14%)
  other arithmetic  4.97 us (8%)
  local copies, waits for them, and re-layouts  3.66 us (6%)
  between operations  0.95 us (2%)
    ppermute x12, starting transfers between devices, partnered(): return lax.ppermute(x, 'seq', [(i, i ^ bits) for i in range(n_seq)])  11.6 us
    ppermute x6, waiting for transfers between devices, across(): return lax.ppermute(x, 'head', [(i, i ^ j) for i in range(n_head)])  10.5 us
    ppermute x6, starting transfers between devices, across(): return lax.ppermute(x, 'head', [(i, i ^ j) for i in range(n_head)])  8.01 us
    ppermute x3, starting transfers between devices, shifted(): lax.ppermute(x, 'head', [(i, (i + j) % n_head) for i in range(n_head)])  7.93 us
    pallas_call x2, Pallas kernels, attention(): pl.pallas_call(functools.partial(attention_kernel, by_slot, h * n_kv, n_k...  7.14 us
    ppermute x2, starting transfers between devices, on_device(): parts.insert(0, lax.ppermute(own[tok - rows:], 'head', shift))  4.39 us
    unnamed x13, local copies, waits for them, and re-layouts  1.99 us
    mul x2, other arithmetic, on_device(): return (down.T[None] * ADAPTER_SCALE, up[None] * ADAPTER_SCALE)  1.35 us
  transfers between devices with their start and end apart: 23, of which 6 were waited for; matrix products, arithmetic and copies ran while one was open for 13% of the time, Pallas kernels for 14%

profile of v12, /device:TPU:0, one launch (start us, length us, event | category | flops | bytes accessed | tf_op | source)
XLA Modules:
  0.0 61.8 jit_solution(14858275453414642799)
XLA Ops:
  0.6 4.1 %collective-permute-start.3 = (bf16[1,16,1024]{2,1,0:T(8,128)(2,1)}, bf16[1,16,1024]{2,1,0:T(8,128)(2,1)S(1)}, u32[]{:S(2)}, u32[]{:S(2)}) collective-permute-start(bf16[1,16,1024]{2,1,0:T(8,128)(2,1)} %param.16), channel_id=1, source_target_pairs={{0,2},{1,3},{2,0},{3,1},{4,6},{5,7},{6,4},{7,5},{8,10},{9,11},{10,... | collective-permute-start | bytes 98312 | tf_op jit(solution)/shard_map/ppermute | solution.py:192
  4.8 1.6 %collective-permute-start.2 = (bf16[1,16,1024]{2,1,0:T(8,128)(2,1)}, bf16[1,16,1024]{2,1,0:T(8,128)(2,1)S(1)}, u32[]{:S(2)}, u32[]{:S(2)}) collective-permute-start(bf16[1,16,1024]{2,1,0:T(8,128)(2,1)} %param.16), channel_id=1, source_target_pairs={{0,1},{1,2},{2,3},{3,0},{4,5},{5,6},{6,7},{7,4},{8,9},{9,10},{10,1... | collective-permute-start | bytes 98312 | tf_op jit(solution)/shard_map/ppermute | solution.py:192
  6.3 2.2 %collective-permute-start.4 = (bf16[1,16,1024]{2,1,0:T(8,128)(2,1)}, bf16[1,16,1024]{2,1,0:T(8,128)(2,1)S(1)}, u32[]{:S(2)}, u32[]{:S(2)}) collective-permute-start(bf16[1,16,1024]{2,1,0:T(8,128)(2,1)} %param.16), channel_id=1, source_target_pairs={{0,3},{1,0},{2,1},{3,2},{4,7},{5,4},{6,5},{7,6},{8,11},{9,8},{10,9... | collective-permute-start | bytes 98312 | tf_op jit(solution)/shard_map/ppermute | solution.py:192
  8.6 0.9 %constant_dynamic-update-slice_fusion.1 = bf16[128,1024]{1,0:T(8,128)(2,1)S(1)} fusion(bf16[128,512]{1,0:T(8,128)(2,1)} %param.11), kind=kLoop, calls=%fused_computation.31 | loop fusion | bytes 262144
  9.5 0.9 %constant_dynamic-update-slice_fusion.refs_3_ = bf16[128,1024]{1,0:T(8,128)(2,1)S(1)} fusion(bf16[128,1024]{1,0:T(8,128)(2,1)S(1)} %constant_dynamic-update-slice_fusion.1, bf16[128,512]{1,0:T(8,128)(2,1)} %param.12), kind=kLoop, calls=%fused_computation.30 | loop fusion | bytes 262144 | tf_op jit(solution)/shard_map/concatenate | solution.py:221
  10.4 1.7 %collective-permute-start.1 = (bf16[128,1024]{1,0:T(8,128)(2,1)S(1)}, bf16[128,1024]{1,0:T(8,128)(2,1)S(1)}, u32[]{:S(2)}, u32[]{:S(2)}) collective-permute-start(bf16[128,1024]{1,0:T(8,128)(2,1)S(1)} %constant_dynamic-update-slice_fusion.refs_3_), channel_id=1, source_target_pairs={{0,1},{1,2},{2,3},{4,5},{5,6},{6,7},{8,9},{9,10},{10,11},{12,13},{... | collective-permute-start | bytes 786440 | tf_op jit(solution)/shard_map/ppermute | solution.py:225
  12.1 2.7 %collective-permute-start = (bf16[64,1024]{1,0:T(8,128)(2,1)S(1)}, bf16[64,1024]{1,0:T(8,128)(2,1)S(1)}, u32[]{:S(2)}, u32[]{:S(2)}) collective-permute-start(bf16[64,1024]{1,0:T(8,128)(2,1)S(1)} %slice.52), channel_id=1, source_target_pairs={{0,2},{1,3},{4,6},{5,7},{8,10},{9,11},{12,14},{13,15},{16,18},{17,... | collective-permute-start | bytes 393224 | tf_op jit(solution)/shard_map/ppermute | solution.py:225
  14.8 0.8 %select_reduce_fusion.2 = s32[8]{0:T(128)S(1)} fusion(s32[8]{0:T(128)} %bitcast.53), kind=kLoop, calls=%fused_computation.38 | loop fusion | flops 184 | bytes 64 | tf_op jit(solution)/shard_map/reduce_sum | solution.py:179
  15.6 0.7 %bitcast_add_fusion = s32[8]{0:T(128)S(1)} fusion(s32[8]{0:T(128)S(1)} %select_reduce_fusion.2, s32[1,8]{1,0:T(1,128)} %param.17), kind=kLoop, calls=%fused_computation.42 | loop fusion | flops 8 | bytes 96 | tf_op jit(solution)/shard_map/add | solution.py:186
  16.3 0.1 compare_and_fusion
  16.4 0.9 %select_reduce_fusion.1 = s32[8]{0:T(128)S(1)} fusion(s32[8]{0:T(128)} %param.19, s32[8]{0:T(128)} %bitcast.51), kind=kLoop, calls=%fused_computation.36 | loop fusion | flops 184 | bytes 96 | tf_op jit(solution)/shard_map/reduce_sum | solution.py:182
  17.2 1.0 %copy.13 = bf16[128,512]{0,1:T(8,128)(2,1)S(1)} copy(bf16[128,512]{1,0:T(8,128)(2,1)} %param.11) | data formatting | bytes 262144 | tf_op args[1]
  18.3 0.7 %stack.15 = s32[8,8]{1,0:T(8,128)S(1)} concatenate(s32[1,8]{1,0:T(1,128)S(1)} %bitcast.50, s32[1,8]{1,0:T(1,128)} %param.18, s32[1,8]{1,0:T(1,128)S(1)} %bitcast.52, s32[1,8]{1,0:T(1,128)S(1)} %broadcast.49, s32[4,8]{1,0:T(4,128)S(1)} %stack.14), dimensions={0} | concatenate | bytes 512 | tf_op jit(solution)/shard_map/stack | solution.py:187
  19.0 0.8 %maximum_bitcast_fusion = bf16[1,4,16,1024]{3,2,1,0:T(8,128)(2,1)S(1)} fusion(bf16[1,16,1024]{2,1,0:T(8,128)(2,1)S(1)} %collective-permute-done.4, bf16[1,16,1024]{2,1,0:T(8,128)(2,1)S(1)} %collective-permute-done.3, bf16[1,16,1024]{2,1,0:T(8,128)(2,1)S(1)} %collective-permute-done.2, bf16[1,16,1024]{2,1,0:T(8,128)(2,1)} %param.16), kind=kLoop, calls=%fused_computation.10 | loop fusion | flops 196608 | bytes 262144 | tf_op jit(solution)/shard_map/broadcast_in_dim | solution.py:229
  19.7 2.5 %collective-permute-start.7 = (bf16[1,4,16,1024]{3,2,1,0:T(8,128)(2,1)S(1)}, bf16[1,4,16,1024]{3,2,1,0:T(8,128)(2,1)S(1)}, u32[]{:S(2)}, u32[]{:S(2)}) collective-permute-start(bf16[1,4,16,1024]{3,2,1,0:T(8,128)(2,1)S(1)} %maximum_bitcast_fusion), channel_id=1, source_target_pairs={{0,24},{4,28},{8,16},{12,20},{16,8},{20,12},{24,0},{28,4},{1,25},{... | collective-permute-start | bytes 393224 | tf_op jit(solution)/shard_map/ppermute | solution.py:200
  22.3 0.5 collective-permute-start.6
  22.8 0.5 collective-permute-start.5
  23.3 0.1 select_reduce_fusion.facts_ref.refs_0_
  23.4 0.3 layout.1
  23.7 3.4 %attention_0.1.refs_2_ = bf16[2048,128]{1,0:T(8,128)(2,1)S(1)} custom-call(bf16[320,512]{1,0:T(8,128)(2,1)S(1)} %get-tuple-element.24.k_all, bf16[320,512]{1,0:T(8,128)(2,1)S(1)} %get-tuple-element.25.v_all, bf16[512,320]{1,0:T(8,128)(2,1)S(1)} %get-tuple-element.26.k_turned, f32[320,128]{1,0:T(8,128)S(1)} %get-tuple-element.27.bias, ...), custom_call_target="tpu_custom_call" | custom-call | flops 503316480 | bytes 2097152 | tf_op jit(solution)/shard_map/attention_0/pallas_call | solution.py:262
  27.1 0.7 %collective-permute-done.6 = bf16[1,4,16,1024]{3,2,1,0:T(8,128)(2,1)S(1)} collective-permute-done((bf16[1,4,16,1024]{3,2,1,0:T(8,128)(2,1)S(1)}, bf16[1,4,16,1024]{3,2,1,0:T(8,128)(2,1)S(1)}, u32[]{:S(2)}, u32[]{:S(2)}) %collective-permute-start.6) | collective-permute-done | bytes 131104 | tf_op jit(solution)/shard_map/ppermute | solution.py:200
  27.9 3.8 %attention_1.1 = (bf16[2048,128]{1,0:T(8,128)(2,1)S(1)}, bf16[4,4,16,1024]{3,2,1,0:T(8,128)(2,1)S(1)}, bf16[4,4,16,1024]{3,2,1,0:T(8,128)(2,1)S(1)}) custom-call(bf16[320,512]{1,0:T(8,128)(2,1)S(1)} %get-tuple-element.24.k_all, bf16[320,512]{1,0:T(8,128)(2,1)S(1)} %get-tuple-element.25.v_all, bf16[512,320]{1,0:T(8,128)(2,1)S(1)} %get-tuple-element.26.k_turned, ...), custom_call_target="tpu_custom_call" | custom-call | flops 503316480 | bytes 2097152 | tf_op jit(solution)/shard_map/attention_1/pallas_call | solution.py:262
  31.7 0.5 collective-permute-start.16
  32.3 0.4 rank_gradient.1.rank_ref
  32.7 0.7 %down_parts.1 = (bf16[4,4,16,2048]{3,2,1,0:T(8,128)(2,1)S(1)}, bf16[4,4,16,2048]{3,2,1,0:T(8,128)(2,1)S(1)}) custom-call(s32[8,128]{1,0:T(8,128)S(1)} %select_reduce_fusion.facts_ref.refs_0_, bf16[128,8192]{1,0:T(8,128)(2,1)S(1)} %copy-done.2, bf16[16,128]{1,0:T(8,128)(2,1)S(1)} %rank_gradient.1.rank_ref), custom_call_target="tpu_custom_call" | custom-call | flops 268435456 | bytes 8388608 | tf_op jit(solution)/shard_map/down_parts/pallas_call | solution.py:302
  33.4 0.1 collective-permute-start.9
  33.6 0.2 collective-permute-done.16
  33.8 0.2 add_convert_fusion
  34.1 1.8 %collective-permute-start.19 = (bf16[4,16,1024]{2,1,0:T(8,128)(2,1)S(1)}, bf16[4,16,1024]{2,1,0:T(8,128)(2,1)S(1)}, u32[]{:S(2)}, u32[]{:S(2)}) collective-permute-start(bf16[4,16,1024]{2,1,0:T(8,128)(2,1)S(1)} %get-tuple-element.47), channel_id=1, source_target_pairs={{0,3},{1,2},{2,1},{3,0},{4,7},{5,6},{6,5},{7,4},{8,11},{9,10},{10,... | collective-permute-start | bytes 393224 | tf_op jit(solution)/shard_map/ppermute | solution.py:196
  35.9 1.7 %collective-permute-start.18 = (bf16[4,16,1024]{2,1,0:T(8,128)(2,1)S(1)}, bf16[4,16,1024]{2,1,0:T(8,128)(2,1)S(1)}, u32[]{:S(2)}, u32[]{:S(2)}) collective-permute-start(bf16[4,16,1024]{2,1,0:T(8,128)(2,1)S(1)} %get-tuple-element.48), channel_id=1, source_target_pairs={{0,2},{1,3},{2,0},{3,1},{4,6},{5,7},{6,4},{7,5},{8,10},{9,11},{10,... | collective-permute-start | bytes 393224 | tf_op jit(solution)/shard_map/ppermute | solution.py:196
  37.6 0.2 core_sum.1
  37.8 1.5 %collective-permute-start.10 = (bf16[4,16,2048]{2,1,0:T(8,128)(2,1)S(1)}, bf16[4,16,2048]{2,1,0:T(8,128)(2,1)S(1)}, u32[]{:S(2)}, u32[]{:S(2)}) collective-permute-start(bf16[4,16,2048]{2,1,0:T(8,128)(2,1)S(1)} %get-tuple-element.41), channel_id=1, source_target_pairs={{0,8},{4,12},{8,0},{12,4},{16,24},{20,28},{24,16},{28,20},{1,9},{5... | collective-permute-start | bytes 786440 | tf_op jit(solution)/shard_map/ppermute | solution.py:200
  39.4 0.9 %collective-permute-start.11 = (bf16[4,16,2048]{2,1,0:T(8,128)(2,1)S(1)}, bf16[4,16,2048]{2,1,0:T(8,128)(2,1)S(1)}, u32[]{:S(2)}, u32[]{:S(2)}) collective-permute-start(bf16[4,16,2048]{2,1,0:T(8,128)(2,1)S(1)} %get-tuple-element.42), channel_id=1, source_target_pairs={{0,16},{4,20},{8,24},{12,28},{16,0},{20,4},{24,8},{28,12},{1,17},{... | collective-permute-start | bytes 786440 | tf_op jit(solution)/shard_map/ppermute | solution.py:200
  40.3 1.4 %collective-permute-start.12 = (bf16[4,16,2048]{2,1,0:T(8,128)(2,1)S(1)}, bf16[4,16,2048]{2,1,0:T(8,128)(2,1)S(1)}, u32[]{:S(2)}, u32[]{:S(2)}) collective-permute-start(bf16[4,16,2048]{2,1,0:T(8,128)(2,1)S(1)} %get-tuple-element.43), channel_id=1, source_target_pairs={{0,24},{4,28},{8,16},{12,20},{16,8},{20,12},{24,0},{28,4},{1,25},{... | collective-permute-start | bytes 786440 | tf_op jit(solution)/shard_map/ppermute | solution.py:200
  41.7 1.4 %collective-permute-done.19 = bf16[4,16,1024]{2,1,0:T(8,128)(2,1)S(1)} collective-permute-done((bf16[4,16,1024]{2,1,0:T(8,128)(2,1)S(1)}, bf16[4,16,1024]{2,1,0:T(8,128)(2,1)S(1)}, u32[]{:S(2)}, u32[]{:S(2)}) %collective-permute-start.19) | collective-permute-done | bytes 131104 | tf_op jit(solution)/shard_map/ppermute | solution.py:196
  43.0 6.4 %collective-permute-done.18 = bf16[4,16,1024]{2,1,0:T(8,128)(2,1)S(1)} collective-permute-done((bf16[4,16,1024]{2,1,0:T(8,128)(2,1)S(1)}, bf16[4,16,1024]{2,1,0:T(8,128)(2,1)S(1)}, u32[]{:S(2)}, u32[]{:S(2)}) %collective-permute-start.18) | collective-permute-done | bytes 131104 | tf_op jit(solution)/shard_map/ppermute | solution.py:196
  49.5 0.1 fusion.2
  49.6 1.5 %collective-permute-start.20 = (bf16[16,1024]{1,0:T(8,128)(2,1)S(1)}, bf16[16,1024]{1,0:T(8,128)(2,1)S(1)}, u32[]{:S(2)}, u32[]{:S(2)}) collective-permute-start(bf16[16,1024]{1,0:T(8,128)(2,1)S(1)} %get-tuple-element.52), channel_id=1, source_target_pairs={{0,8},{4,12},{8,0},{12,4},{16,24},{20,28},{24,16},{28,20},{1,9},{5... | collective-permute-start | bytes 98312 | tf_op jit(solution)/shard_map/ppermute | solution.py:200
  51.1 1.5 %collective-permute-start.22 = (bf16[16,1024]{1,0:T(8,128)(2,1)S(1)}, bf16[16,1024]{1,0:T(8,128)(2,1)S(1)}, u32[]{:S(2)}, u32[]{:S(2)}) collective-permute-start(bf16[16,1024]{1,0:T(8,128)(2,1)S(1)} %get-tuple-element.53), channel_id=1, source_target_pairs={{0,24},{4,28},{8,16},{12,20},{16,8},{20,12},{24,0},{28,4},{1,25},{... | collective-permute-start | bytes 98312 | tf_op jit(solution)/shard_map/ppermute | solution.py:200
  52.6 0.5 collective-permute-start.21
  53.1 0.1 add_convert_fusion.1
  53.3 1.7 %collective-permute-start.13 = (bf16[16,2048]{1,0:T(8,128)(2,1)S(1)}, bf16[16,2048]{1,0:T(8,128)(2,1)S(1)}, u32[]{:S(2)}, u32[]{:S(2)}) collective-permute-start(bf16[16,2048]{1,0:T(8,128)(2,1)S(1)} %get-tuple-element.49), channel_id=1, source_target_pairs={{0,3},{1,2},{2,1},{3,0},{4,7},{5,6},{6,5},{7,4},{8,11},{9,10},{10,... | collective-permute-start | bytes 196616 | tf_op jit(solution)/shard_map/ppermute | solution.py:196
  55.0 0.9 %collective-permute-start.15 = (bf16[16,2048]{1,0:T(8,128)(2,1)S(1)}, bf16[16,2048]{1,0:T(8,128)(2,1)S(1)}, u32[]{:S(2)}, u32[]{:S(2)}) collective-permute-start(bf16[16,2048]{1,0:T(8,128)(2,1)S(1)} %get-tuple-element.50), channel_id=1, source_target_pairs={{0,2},{1,3},{2,0},{3,1},{4,6},{5,7},{6,4},{7,5},{8,10},{9,11},{10,... | collective-permute-start | bytes 196616 | tf_op jit(solution)/shard_map/ppermute | solution.py:196
  55.9 1.8 %collective-permute-start.14 = (bf16[16,2048]{1,0:T(8,128)(2,1)S(1)}, bf16[16,2048]{1,0:T(8,128)(2,1)S(1)}, u32[]{:S(2)}, u32[]{:S(2)}) collective-permute-start(bf16[16,2048]{1,0:T(8,128)(2,1)S(1)} %get-tuple-element.51), channel_id=1, source_target_pairs={{0,1},{1,0},{2,3},{3,2},{4,5},{5,4},{6,7},{7,6},{8,9},{9,8},{10,11... | collective-permute-start | bytes 196616 | tf_op jit(solution)/shard_map/ppermute | solution.py:196
  57.8 0.7 %fusion.10 = f32[1,16,1024]{2,1,0:T(8,128)} fusion(bf16[16,1024]{1,0:T(8,128)(2,1)S(1)} %collective-permute-done.22, bf16[16,1024]{1,0:T(8,128)(2,1)S(1)} %collective-permute-done.21, bf16[16,1024]{1,0:T(8,128)(2,1)S(1)} %collective-permute-done.20, bf16[4,16,1024]{2,1,0:T(8,128)(2,1)S(1)} %fusion.2), kind=kLoop, calls=%fused_computation.24 | loop fusion | flops 131072 | bytes 196608 | tf_op jit(solution)/shard_map/mul | solution.py:333
  58.4 1.1 %collective-permute-done.13 = bf16[16,2048]{1,0:T(8,128)(2,1)S(1)} collective-permute-done((bf16[16,2048]{1,0:T(8,128)(2,1)S(1)}, bf16[16,2048]{1,0:T(8,128)(2,1)S(1)}, u32[]{:S(2)}, u32[]{:S(2)}) %collective-permute-start.13) | collective-permute-done | bytes 65568 | tf_op jit(solution)/shard_map/ppermute | solution.py:196
  59.5 1.5 %collective-permute-done.15 = bf16[16,2048]{1,0:T(8,128)(2,1)S(1)} collective-permute-done((bf16[16,2048]{1,0:T(8,128)(2,1)S(1)}, bf16[16,2048]{1,0:T(8,128)(2,1)S(1)}, u32[]{:S(2)}, u32[]{:S(2)}) %collective-permute-start.15) | collective-permute-done | bytes 65568 | tf_op jit(solution)/shard_map/ppermute | solution.py:196
  61.1 0.7 %fusion.6 = f32[1,2048,16]{1,2,0:T(8,128)} fusion(bf16[16,2048]{1,0:T(8,128)(2,1)S(1)} %collective-permute-done.15, bf16[16,2048]{1,0:T(8,128)(2,1)S(1)} %collective-permute-done.14, bf16[16,2048]{1,0:T(8,128)(2,1)S(1)} %collective-permute-done.13, bf16[4,16,2048]{2,1,0:T(8,128)(2,1)S(1)} %add_convert_fusion.1), kind=kLoop, calls=%fused_computation.15 | loop fusion | flops 262144 | bytes 393216 | tf_op jit(solution)/shard_map/mul | solution.py:333
  (38 shorter events, 0.3 us)
Async XLA Ops:
  0.6 23.0 %copy-start.1 = (bf16[128,4096]{1,0:T(8,128)(2,1)S(1)}, bf16[128,4096]{1,0:T(8,128)(2,1)}, u32[]{:S(2)}) copy-start(bf16[128,4096]{1,0:T(8,128)(2,1)} %g_hbm.3) | copy-start | bytes 3145732
  0.6 23.0 %copy-start = (bf16[128,4096]{1,0:T(8,128)(2,1)S(1)}, bf16[128,4096]{1,0:T(8,128)(2,1)}, u32[]{:S(2)}) copy-start(bf16[128,4096]{1,0:T(8,128)(2,1)} %q_hbm.3) | copy-start | bytes 3145732
  0.6 18.3 %collective-permute-start.3 = (bf16[1,16,1024]{2,1,0:T(8,128)(2,1)}, bf16[1,16,1024]{2,1,0:T(8,128)(2,1)S(1)}, u32[]{:S(2)}, u32[]{:S(2)}) collective-permute-start(bf16[1,16,1024]{2,1,0:T(8,128)(2,1)} %param.16), channel_id=1, source_target_pairs={{0,2},{1,3},{2,0},{3,1},{4,6},{5,7},{6,4},{7,5},{8,10},{9,11},{10,... | collective-permute-start | bytes 98312 | tf_op jit(solution)/shard_map/ppermute | solution.py:192
  4.8 14.2 %collective-permute-start.2 = (bf16[1,16,1024]{2,1,0:T(8,128)(2,1)}, bf16[1,16,1024]{2,1,0:T(8,128)(2,1)S(1)}, u32[]{:S(2)}, u32[]{:S(2)}) collective-permute-start(bf16[1,16,1024]{2,1,0:T(8,128)(2,1)} %param.16), channel_id=1, source_target_pairs={{0,1},{1,2},{2,3},{3,0},{4,5},{5,6},{6,7},{7,4},{8,9},{9,10},{10,1... | collective-permute-start | bytes 98312 | tf_op jit(solution)/shard_map/ppermute | solution.py:192
  6.3 12.6 %collective-permute-start.4 = (bf16[1,16,1024]{2,1,0:T(8,128)(2,1)}, bf16[1,16,1024]{2,1,0:T(8,128)(2,1)S(1)}, u32[]{:S(2)}, u32[]{:S(2)}) collective-permute-start(bf16[1,16,1024]{2,1,0:T(8,128)(2,1)} %param.16), channel_id=1, source_target_pairs={{0,3},{1,0},{2,1},{3,2},{4,7},{5,4},{6,5},{7,6},{8,11},{9,8},{10,9... | collective-permute-start | bytes 98312 | tf_op jit(solution)/shard_map/ppermute | solution.py:192
  10.4 13.0 %collective-permute-start.1 = (bf16[128,1024]{1,0:T(8,128)(2,1)S(1)}, bf16[128,1024]{1,0:T(8,128)(2,1)S(1)}, u32[]{:S(2)}, u32[]{:S(2)}) collective-permute-start(bf16[128,1024]{1,0:T(8,128)(2,1)S(1)} %constant_dynamic-update-slice_fusion.refs_3_), channel_id=1, source_target_pairs={{0,1},{1,2},{2,3},{4,5},{5,6},{6,7},{8,9},{9,10},{10,11},{12,13},{... | collective-permute-start | bytes 786440 | tf_op jit(solution)/shard_map/ppermute | solution.py:225
  12.1 11.3 %collective-permute-start = (bf16[64,1024]{1,0:T(8,128)(2,1)S(1)}, bf16[64,1024]{1,0:T(8,128)(2,1)S(1)}, u32[]{:S(2)}, u32[]{:S(2)}) collective-permute-start(bf16[64,1024]{1,0:T(8,128)(2,1)S(1)} %slice.52), channel_id=1, source_target_pairs={{0,2},{1,3},{4,6},{5,7},{8,10},{9,11},{12,14},{13,15},{16,18},{17,... | collective-permute-start | bytes 393224 | tf_op jit(solution)/shard_map/ppermute | solution.py:225
  19.7 7.3 %collective-permute-start.7 = (bf16[1,4,16,1024]{3,2,1,0:T(8,128)(2,1)S(1)}, bf16[1,4,16,1024]{3,2,1,0:T(8,128)(2,1)S(1)}, u32[]{:S(2)}, u32[]{:S(2)}) collective-permute-start(bf16[1,4,16,1024]{3,2,1,0:T(8,128)(2,1)S(1)} %maximum_bitcast_fusion), channel_id=1, source_target_pairs={{0,24},{4,28},{8,16},{12,20},{16,8},{20,12},{24,0},{28,4},{1,25},{... | collective-permute-start | bytes 393224 | tf_op jit(solution)/shard_map/ppermute | solution.py:200
  22.3 5.5 %collective-permute-start.6 = (bf16[1,4,16,1024]{3,2,1,0:T(8,128)(2,1)S(1)}, bf16[1,4,16,1024]{3,2,1,0:T(8,128)(2,1)S(1)}, u32[]{:S(2)}, u32[]{:S(2)}) collective-permute-start(bf16[1,4,16,1024]{3,2,1,0:T(8,128)(2,1)S(1)} %maximum_bitcast_fusion), channel_id=1, source_target_pairs={{0,16},{4,20},{8,24},{12,28},{16,0},{20,4},{24,8},{28,12},{1,17},{... | collective-permute-start | bytes 393224 | tf_op jit(solution)/shard_map/ppermute | solution.py:200
  22.8 5.0 %collective-permute-start.5 = (bf16[1,4,16,1024]{3,2,1,0:T(8,128)(2,1)S(1)}, bf16[1,4,16,1024]{3,2,1,0:T(8,128)(2,1)S(1)}, u32[]{:S(2)}, u32[]{:S(2)}) collective-permute-start(bf16[1,4,16,1024]{3,2,1,0:T(8,128)(2,1)S(1)} %maximum_bitcast_fusion), channel_id=1, source_target_pairs={{0,8},{4,12},{8,0},{12,4},{16,24},{20,28},{24,16},{28,20},{1,9},{5... | collective-permute-start | bytes 393224 | tf_op jit(solution)/shard_map/ppermute | solution.py:200
  23.7 4.2 %copy-start.3 = (bf16[128,16]{0,1:T(8,128)(2,1)S(1)}, bf16[128,16]{0,1:T(8,128)(2,1)}, u32[]{:S(2)}) copy-start(bf16[128,16]{0,1:T(8,128)(2,1)} %param.15) | copy-start | bytes 12292
  27.8 3.9 %collective-permute-start.8 = (bf16[4,4,16,1024]{3,2,1,0:T(8,128)(2,1)S(1)}, bf16[4,4,16,1024]{3,2,1,0:T(8,128)(2,1)S(1)}, u32[]{:S(2)}, u32[]{:S(2)}) collective-permute-start(bf16[4,4,16,1024]{3,2,1,0:T(8,128)(2,1)S(1)} %constant_dynamic-update-slice_fusion.2.refs_0_), channel_id=1, source_target_pairs={{0,4},{4,0},{8,12},{12,8},{16,20},{20,16},{24,28},{28,24},{1,5},{5... | collective-permute-start | bytes 1572872 | tf_op jit(solution)/shard_map/ppermute | solution.py:200
  27.9 4.8 %copy-start.2 = (bf16[128,8192]{1,0:T(8,128)(2,1)S(1)}, bf16[128,8192]{1,0:T(8,128)(2,1)}, u32[]{:S(2)}) copy-start(bf16[128,8192]{1,0:T(8,128)(2,1)} %x_ref.1) | copy-start | bytes 6291460
  31.7 2.1 %collective-permute-start.16 = (bf16[4,4,16,1024]{3,2,1,0:T(8,128)(2,1)S(1)}, bf16[4,4,16,1024]{3,2,1,0:T(8,128)(2,1)S(1)}, u32[]{:S(2)}, u32[]{:S(2)}) collective-permute-start(bf16[4,4,16,1024]{3,2,1,0:T(8,128)(2,1)S(1)} %get-tuple-element.45), channel_id=1, source_target_pairs={{0,4},{4,0},{8,12},{12,8},{16,20},{20,16},{24,28},{28,24},{1,5},{5... | collective-permute-start | bytes 1572872 | tf_op jit(solution)/shard_map/ppermute | solution.py:200
  33.4 4.2 %collective-permute-start.9 = (bf16[4,4,16,2048]{3,2,1,0:T(8,128)(2,1)S(1)}, bf16[4,4,16,2048]{3,2,1,0:T(8,128)(2,1)S(1)}, u32[]{:S(2)}, u32[]{:S(2)}) collective-permute-start(bf16[4,4,16,2048]{3,2,1,0:T(8,128)(2,1)S(1)} %get-tuple-element.39), channel_id=1, source_target_pairs={{0,4},{4,0},{8,12},{12,8},{16,20},{20,16},{24,28},{28,24},{1,5},{5... | collective-permute-start | bytes 3145736 | tf_op jit(solution)/shard_map/ppermute | solution.py:200
  34.0 6.2 %collective-permute-start.17 = (bf16[4,16,1024]{2,1,0:T(8,128)(2,1)S(1)}, bf16[4,16,1024]{2,1,0:T(8,128)(2,1)S(1)}, u32[]{:S(2)}, u32[]{:S(2)}) collective-permute-start(bf16[4,16,1024]{2,1,0:T(8,128)(2,1)S(1)} %get-tuple-element.46), channel_id=1, source_target_pairs={{0,1},{1,0},{2,3},{3,2},{4,5},{5,4},{6,7},{7,6},{8,9},{9,8},{10,11... | collective-permute-start | bytes 393224 | tf_op jit(solution)/shard_map/ppermute | solution.py:196
  34.1 8.9 %collective-permute-start.19 = (bf16[4,16,1024]{2,1,0:T(8,128)(2,1)S(1)}, bf16[4,16,1024]{2,1,0:T(8,128)(2,1)S(1)}, u32[]{:S(2)}, u32[]{:S(2)}) collective-permute-start(bf16[4,16,1024]{2,1,0:T(8,128)(2,1)S(1)} %get-tuple-element.47), channel_id=1, source_target_pairs={{0,3},{1,2},{2,1},{3,0},{4,7},{5,6},{6,5},{7,4},{8,11},{9,10},{10,... | collective-permute-start | bytes 393224 | tf_op jit(solution)/shard_map/ppermute | solution.py:196
  35.9 13.6 %collective-permute-start.18 = (bf16[4,16,1024]{2,1,0:T(8,128)(2,1)S(1)}, bf16[4,16,1024]{2,1,0:T(8,128)(2,1)S(1)}, u32[]{:S(2)}, u32[]{:S(2)}) collective-permute-start(bf16[4,16,1024]{2,1,0:T(8,128)(2,1)S(1)} %get-tuple-element.48), channel_id=1, source_target_pairs={{0,2},{1,3},{2,0},{3,1},{4,6},{5,7},{6,4},{7,5},{8,10},{9,11},{10,... | collective-permute-start | bytes 393224 | tf_op jit(solution)/shard_map/ppermute | solution.py:196
  37.8 14.8 %collective-permute-start.10 = (bf16[4,16,2048]{2,1,0:T(8,128)(2,1)S(1)}, bf16[4,16,2048]{2,1,0:T(8,128)(2,1)S(1)}, u32[]{:S(2)}, u32[]{:S(2)}) collective-permute-start(bf16[4,16,2048]{2,1,0:T(8,128)(2,1)S(1)} %get-tuple-element.41), channel_id=1, source_target_pairs={{0,8},{4,12},{8,0},{12,4},{16,24},{20,28},{24,16},{28,20},{1,9},{5... | collective-permute-start | bytes 786440 | tf_op jit(solution)/shard_map/ppermute | solution.py:200
  39.4 13.8 %collective-permute-start.11 = (bf16[4,16,2048]{2,1,0:T(8,128)(2,1)S(1)}, bf16[4,16,2048]{2,1,0:T(8,128)(2,1)S(1)}, u32[]{:S(2)}, u32[]{:S(2)}) collective-permute-start(bf16[4,16,2048]{2,1,0:T(8,128)(2,1)S(1)} %get-tuple-element.42), channel_id=1, source_target_pairs={{0,16},{4,20},{8,24},{12,28},{16,0},{20,4},{24,8},{28,12},{1,17},{... | collective-permute-start | bytes 786440 | tf_op jit(solution)/shard_map/ppermute | solution.py:200
  40.3 12.9 %collective-permute-start.12 = (bf16[4,16,2048]{2,1,0:T(8,128)(2,1)S(1)}, bf16[4,16,2048]{2,1,0:T(8,128)(2,1)S(1)}, u32[]{:S(2)}, u32[]{:S(2)}) collective-permute-start(bf16[4,16,2048]{2,1,0:T(8,128)(2,1)S(1)} %get-tuple-element.43), channel_id=1, source_target_pairs={{0,24},{4,28},{8,16},{12,20},{16,8},{20,12},{24,0},{28,4},{1,25},{... | collective-permute-start | bytes 786440 | tf_op jit(solution)/shard_map/ppermute | solution.py:200
  49.6 6.4 %collective-permute-start.20 = (bf16[16,1024]{1,0:T(8,128)(2,1)S(1)}, bf16[16,1024]{1,0:T(8,128)(2,1)S(1)}, u32[]{:S(2)}, u32[]{:S(2)}) collective-permute-start(bf16[16,1024]{1,0:T(8,128)(2,1)S(1)} %get-tuple-element.52), channel_id=1, source_target_pairs={{0,8},{4,12},{8,0},{12,4},{16,24},{20,28},{24,16},{28,20},{1,9},{5... | collective-permute-start | bytes 98312 | tf_op jit(solution)/shard_map/ppermute | solution.py:200
  51.1 6.7 %collective-permute-start.22 = (bf16[16,1024]{1,0:T(8,128)(2,1)S(1)}, bf16[16,1024]{1,0:T(8,128)(2,1)S(1)}, u32[]{:S(2)}, u32[]{:S(2)}) collective-permute-start(bf16[16,1024]{1,0:T(8,128)(2,1)S(1)} %get-tuple-element.53), channel_id=1, source_target_pairs={{0,24},{4,28},{8,16},{12,20},{16,8},{20,12},{24,0},{28,4},{1,25},{... | collective-permute-start | bytes 98312 | tf_op jit(solution)/shard_map/ppermute | solution.py:200
  52.6 5.2 %collective-permute-start.21 = (bf16[16,1024]{1,0:T(8,128)(2,1)S(1)}, bf16[16,1024]{1,0:T(8,128)(2,1)S(1)}, u32[]{:S(2)}, u32[]{:S(2)}) collective-permute-start(bf16[16,1024]{1,0:T(8,128)(2,1)S(1)} %get-tuple-element.54), channel_id=1, source_target_pairs={{0,16},{4,20},{8,24},{12,28},{16,0},{20,4},{24,8},{28,12},{1,17},{... | collective-permute-start | bytes 98312 | tf_op jit(solution)/shard_map/ppermute | solution.py:200
  53.3 6.2 %collective-permute-start.13 = (bf16[16,2048]{1,0:T(8,128)(2,1)S(1)}, bf16[16,2048]{1,0:T(8,128)(2,1)S(1)}, u32[]{:S(2)}, u32[]{:S(2)}) collective-permute-start(bf16[16,2048]{1,0:T(8,128)(2,1)S(1)} %get-tuple-element.49), channel_id=1, source_target_pairs={{0,3},{1,2},{2,1},{3,0},{4,7},{5,6},{6,5},{7,4},{8,11},{9,10},{10,... | collective-permute-start | bytes 196616 | tf_op jit(solution)/shard_map/ppermute | solution.py:196
  55.0 6.0 %collective-permute-start.15 = (bf16[16,2048]{1,0:T(8,128)(2,1)S(1)}, bf16[16,2048]{1,0:T(8,128)(2,1)S(1)}, u32[]{:S(2)}, u32[]{:S(2)}) collective-permute-start(bf16[16,2048]{1,0:T(8,128)(2,1)S(1)} %get-tuple-element.50), channel_id=1, source_target_pairs={{0,2},{1,3},{2,0},{3,1},{4,6},{5,7},{6,4},{7,5},{8,10},{9,11},{10,... | collective-permute-start | bytes 196616 | tf_op jit(solution)/shard_map/ppermute | solution.py:196
  55.9 5.1 %collective-permute-start.14 = (bf16[16,2048]{1,0:T(8,128)(2,1)S(1)}, bf16[16,2048]{1,0:T(8,128)(2,1)S(1)}, u32[]{:S(2)}, u32[]{:S(2)}) collective-permute-start(bf16[16,2048]{1,0:T(8,128)(2,1)S(1)} %get-tuple-element.51), channel_id=1, source_target_pairs={{0,1},{1,0},{2,3},{3,2},{4,5},{5,4},{6,7},{7,6},{8,9},{9,8},{10,11... | collective-permute-start | bytes 196616 | tf_op jit(solution)/shard_map/ppermute | solution.py:196

commit v13 on v12

--- a/solution.py
+++ b/solution.py
@@ -323,8 +323,16 @@
             cost_estimate=pl.CostEstimate(flops=0, bytes_accessed=SUM_BYTES, transcendentals=0),
             name="core_sum",
         )(down[0], partnered(down[1], n_seq, 1))
-        up = over_chips(over_z(over_cores(up, n_seq), n_head, (1, 2, 3)).astype(BF16), n_seq)
-        down = over_z(over_chips(down, n_seq).astype(BF16), n_head, (3, 1, 2))
+        up = over_cores(up, n_seq)
+        up = added(up[:2], [across(up[2:], n_head, 2)])
+        up_got = across(up[1].astype(BF16), n_head, 1)
+        down = over_chips(down, n_seq).astype(BF16)
+        up_got, _ = lax.optimization_barrier((up_got, down))
+        up = added(up[0], [up_got]).astype(BF16)
+        down = over_z(down, n_head, (3, 1, 2))
+        up_got = [partnered(up[m], n_seq, 2 * m) for m in range(1, n_seq // 2)]
+        up_got, _ = lax.optimization_barrier((up_got, down))
+        up = added(up[0], up_got)
     else:
         up = lax.all_to_all(up[0], "head", split_axis=0, concat_axis=0, tiled=True)
         up = spread(jnp.sum(up.astype(F32), axis=0), segment_adapter, owner, n_seq)

time: 62.1 us -> 66.3 us (1.068)
  waiting for transfers between devices: 11.4 us -> 19.2 us
  starting transfers between devices: 32 us -> 28.3 us
    ppermute x12, waiting for transfers between devices: 0.95 us -> 8.62 us  [partnered(): return lax.ppermute(x, 'seq', [(i, i ^ bits) for i in range(n_seq)])]
    ppermute x6 -> x5, starting transfers between devices: 8.01 us -> 4.59 us  [across(): return lax.ppermute(x, 'head', [(i, i ^ j) for i in range(n_head)])]
    ppermute x6 -> x5, waiting for transfers between devices: 10.5 us -> 10.6 us  [across(): return lax.ppermute(x, 'head', [(i, i ^ j) for i in range(n_head)])]
  transfers between devices with their start and end apart: 23 -> 22, of which waited for: 6 -> 10; matrix products, arithmetic and copies ran while one was open for 13% -> 12% of each run, Pallas kernels for 14% -> 13%
where the time goes in v13:
time: 66.3 us; the launch traced here: 66 us
  starting transfers between devices  28.3 us (43%)
  waiting for transfers between devices  19.2 us (29%)
  Pallas kernels  8.8 us (13%)
  other arithmetic  5 us (8%)
  local copies, waits for them, and re-layouts  3.66 us (6%)
  between operations  0.98 us (1%)
    ppermute x12, starting transfers between devices, partnered(): return lax.ppermute(x, 'seq', [(i, i ^ bits) for i in range(n_seq)])  11.4 us
    ppermute x5, waiting for transfers between devices, across(): return lax.ppermute(x, 'head', [(i, i ^ j) for i in range(n_head)])  10.6 us
    ppermute x12, waiting for transfers between devices, partnered(): return lax.ppermute(x, 'seq', [(i, i ^ bits) for i in range(n_seq)])  8.62 us
    ppermute x3, starting transfers between devices, shifted(): lax.ppermute(x, 'head', [(i, (i + j) % n_head) for i in range(n_head)])  7.93 us
    pallas_call x2, Pallas kernels, attention(): pl.pallas_call(functools.partial(attention_kernel, by_slot, h * n_kv, n_k...  7.14 us
    ppermute x5, starting transfers between devices, across(): return lax.ppermute(x, 'head', [(i, i ^ j) for i in range(n_head)])  4.59 us
    ppermute x2, starting transfers between devices, on_device(): parts.insert(0, lax.ppermute(own[tok - rows:], 'head', shift))  4.39 us
    unnamed x13, local copies, waits for them, and re-layouts  1.99 us
  transfers between devices with their start and end apart: 22, of which 10 were waited for; matrix products, arithmetic and copies ran while one was open for 12% of the time, Pallas kernels for 13%

profile of v13, /device:TPU:0, one launch (start us, length us, event | category | flops | bytes accessed | tf_op | source)
XLA Modules:
  0.0 66.0 jit_solution(12548042378301304111)
XLA Ops:
  0.6 4.1 %collective-permute-start.3 = (bf16[1,16,1024]{2,1,0:T(8,128)(2,1)}, bf16[1,16,1024]{2,1,0:T(8,128)(2,1)S(1)}, u32[]{:S(2)}, u32[]{:S(2)}) collective-permute-start(bf16[1,16,1024]{2,1,0:T(8,128)(2,1)} %param.16), channel_id=1, source_target_pairs={{0,2},{1,3},{2,0},{3,1},{4,6},{5,7},{6,4},{7,5},{8,10},{9,11},{10,... | collective-permute-start | bytes 98312 | tf_op jit(solution)/shard_map/ppermute | solution.py:192
  4.8 1.6 %collective-permute-start.2 = (bf16[1,16,1024]{2,1,0:T(8,128)(2,1)}, bf16[1,16,1024]{2,1,0:T(8,128)(2,1)S(1)}, u32[]{:S(2)}, u32[]{:S(2)}) collective-permute-start(bf16[1,16,1024]{2,1,0:T(8,128)(2,1)} %param.16), channel_id=1, source_target_pairs={{0,1},{1,2},{2,3},{3,0},{4,5},{5,6},{6,7},{7,4},{8,9},{9,10},{10,1... | collective-permute-start | bytes 98312 | tf_op jit(solution)/shard_map/ppermute | solution.py:192
  6.3 2.2 %collective-permute-start.4 = (bf16[1,16,1024]{2,1,0:T(8,128)(2,1)}, bf16[1,16,1024]{2,1,0:T(8,128)(2,1)S(1)}, u32[]{:S(2)}, u32[]{:S(2)}) collective-permute-start(bf16[1,16,1024]{2,1,0:T(8,128)(2,1)} %param.16), channel_id=1, source_target_pairs={{0,3},{1,0},{2,1},{3,2},{4,7},{5,4},{6,5},{7,6},{8,11},{9,8},{10,9... | collective-permute-start | bytes 98312 | tf_op jit(solution)/shard_map/ppermute | solution.py:192
  8.6 0.9 %constant_dynamic-update-slice_fusion.1 = bf16[128,1024]{1,0:T(8,128)(2,1)S(1)} fusion(bf16[128,512]{1,0:T(8,128)(2,1)} %param.11), kind=kLoop, calls=%fused_computation.28 | loop fusion | bytes 262144
  9.5 0.9 %constant_dynamic-update-slice_fusion.refs_3_ = bf16[128,1024]{1,0:T(8,128)(2,1)S(1)} fusion(bf16[128,1024]{1,0:T(8,128)(2,1)S(1)} %constant_dynamic-update-slice_fusion.1, bf16[128,512]{1,0:T(8,128)(2,1)} %param.12), kind=kLoop, calls=%fused_computation.27 | loop fusion | bytes 262144 | tf_op jit(solution)/shard_map/concatenate | solution.py:221
  10.4 1.7 %collective-permute-start.1 = (bf16[128,1024]{1,0:T(8,128)(2,1)S(1)}, bf16[128,1024]{1,0:T(8,128)(2,1)S(1)}, u32[]{:S(2)}, u32[]{:S(2)}) collective-permute-start(bf16[128,1024]{1,0:T(8,128)(2,1)S(1)} %constant_dynamic-update-slice_fusion.refs_3_), channel_id=1, source_target_pairs={{0,1},{1,2},{2,3},{4,5},{5,6},{6,7},{8,9},{9,10},{10,11},{12,13},{... | collective-permute-start | bytes 786440 | tf_op jit(solution)/shard_map/ppermute | solution.py:225
  12.1 2.7 %collective-permute-start = (bf16[64,1024]{1,0:T(8,128)(2,1)S(1)}, bf16[64,1024]{1,0:T(8,128)(2,1)S(1)}, u32[]{:S(2)}, u32[]{:S(2)}) collective-permute-start(bf16[64,1024]{1,0:T(8,128)(2,1)S(1)} %slice.53), channel_id=1, source_target_pairs={{0,2},{1,3},{4,6},{5,7},{8,10},{9,11},{12,14},{13,15},{16,18},{17,... | collective-permute-start | bytes 393224 | tf_op jit(solution)/shard_map/ppermute | solution.py:225
  14.8 0.8 %select_reduce_fusion.2 = s32[8]{0:T(128)S(1)} fusion(s32[8]{0:T(128)} %bitcast.51), kind=kLoop, calls=%fused_computation.35 | loop fusion | flops 184 | bytes 64 | tf_op jit(solution)/shard_map/reduce_sum | solution.py:179
  15.6 0.7 bitcast_add_fusion
  16.3 0.1 compare_and_fusion
  16.4 0.9 %select_reduce_fusion.1 = s32[8]{0:T(128)S(1)} fusion(s32[8]{0:T(128)} %param.19, s32[8]{0:T(128)} %bitcast.49), kind=kLoop, calls=%fused_computation.33 | loop fusion | flops 184 | bytes 96 | tf_op jit(solution)/shard_map/reduce_sum | solution.py:182
  17.2 1.0 %copy.13 = bf16[128,512]{0,1:T(8,128)(2,1)S(1)} copy(bf16[128,512]{1,0:T(8,128)(2,1)} %param.11) | data formatting | bytes 262144 | tf_op args[1]
  18.3 0.7 %stack.15 = s32[8,8]{1,0:T(8,128)S(1)} concatenate(s32[1,8]{1,0:T(1,128)S(1)} %bitcast.48, s32[1,8]{1,0:T(1,128)} %param.18, s32[1,8]{1,0:T(1,128)S(1)} %bitcast.50, s32[1,8]{1,0:T(1,128)S(1)} %broadcast.49, s32[4,8]{1,0:T(4,128)S(1)} %stack.14), dimensions={0} | concatenate | bytes 512 | tf_op jit(solution)/shard_map/stack | solution.py:187
  19.0 0.8 %maximum_bitcast_fusion = bf16[1,4,16,1024]{3,2,1,0:T(8,128)(2,1)S(1)} fusion(bf16[1,16,1024]{2,1,0:T(8,128)(2,1)S(1)} %collective-permute-done.4, bf16[1,16,1024]{2,1,0:T(8,128)(2,1)S(1)} %collective-permute-done.3, bf16[1,16,1024]{2,1,0:T(8,128)(2,1)S(1)} %collective-permute-done.2, bf16[1,16,1024]{2,1,0:T(8,128)(2,1)} %param.16), kind=kLoop, calls=%fused_computation.8 | loop fusion | flops 196608 | bytes 262144 | tf_op jit(solution)/shard_map/broadcast_in_dim | solution.py:229
  19.7 2.5 %collective-permute-start.7 = (bf16[1,4,16,1024]{3,2,1,0:T(8,128)(2,1)S(1)}, bf16[1,4,16,1024]{3,2,1,0:T(8,128)(2,1)S(1)}, u32[]{:S(2)}, u32[]{:S(2)}) collective-permute-start(bf16[1,4,16,1024]{3,2,1,0:T(8,128)(2,1)S(1)} %maximum_bitcast_fusion), channel_id=1, source_target_pairs={{0,24},{4,28},{8,16},{12,20},{16,8},{20,12},{24,0},{28,4},{1,25},{... | collective-permute-start | bytes 393224 | tf_op jit(solution)/shard_map/ppermute | solution.py:200
  22.3 0.5 collective-permute-start.6
  22.8 0.5 collective-permute-start.5
  23.3 0.1 select_reduce_fusion.facts_ref.refs_0_
  23.4 0.3 layout.1
  23.7 3.4 %attention_0.1.refs_2_ = bf16[2048,128]{1,0:T(8,128)(2,1)S(1)} custom-call(bf16[320,512]{1,0:T(8,128)(2,1)S(1)} %get-tuple-element.28.k_all, bf16[320,512]{1,0:T(8,128)(2,1)S(1)} %get-tuple-element.29.v_all, bf16[512,320]{1,0:T(8,128)(2,1)S(1)} %get-tuple-element.30.k_turned, f32[320,128]{1,0:T(8,128)S(1)} %get-tuple-element.31.bias, ...), custom_call_target="tpu_custom_call" | custom-call | flops 503316480 | bytes 2097152 | tf_op jit(solution)/shard_map/attention_0/pallas_call | solution.py:262
  27.1 0.7 %collective-permute-done.6 = bf16[1,4,16,1024]{3,2,1,0:T(8,128)(2,1)S(1)} collective-permute-done((bf16[1,4,16,1024]{3,2,1,0:T(8,128)(2,1)S(1)}, bf16[1,4,16,1024]{3,2,1,0:T(8,128)(2,1)S(1)}, u32[]{:S(2)}, u32[]{:S(2)}) %collective-permute-start.6) | collective-permute-done | bytes 131104 | tf_op jit(solution)/shard_map/ppermute | solution.py:200
  27.9 3.8 %attention_1.1 = (bf16[2048,128]{1,0:T(8,128)(2,1)S(1)}, bf16[4,4,16,1024]{3,2,1,0:T(8,128)(2,1)S(1)}, bf16[4,4,16,1024]{3,2,1,0:T(8,128)(2,1)S(1)}) custom-call(bf16[320,512]{1,0:T(8,128)(2,1)S(1)} %get-tuple-element.28.k_all, bf16[320,512]{1,0:T(8,128)(2,1)S(1)} %get-tuple-element.29.v_all, bf16[512,320]{1,0:T(8,128)(2,1)S(1)} %get-tuple-element.30.k_turned, ...), custom_call_target="tpu_custom_call" | custom-call | flops 503316480 | bytes 2097152 | tf_op jit(solution)/shard_map/attention_1/pallas_call | solution.py:262
  31.7 0.5 collective-permute-start.16
  32.3 0.4 rank_gradient.1.rank_ref
  32.7 0.7 %down_parts.1 = (bf16[4,4,16,2048]{3,2,1,0:T(8,128)(2,1)S(1)}, bf16[4,4,16,2048]{3,2,1,0:T(8,128)(2,1)S(1)}) custom-call(s32[8,128]{1,0:T(8,128)S(1)} %select_reduce_fusion.facts_ref.refs_0_, bf16[128,8192]{1,0:T(8,128)(2,1)S(1)} %copy-done.2, bf16[16,128]{1,0:T(8,128)(2,1)S(1)} %rank_gradient.1.rank_ref), custom_call_target="tpu_custom_call" | custom-call | flops 268435456 | bytes 8388608 | tf_op jit(solution)/shard_map/down_parts/pallas_call | solution.py:302
  33.4 0.1 collective-permute-start.9
  33.6 0.2 collective-permute-done.16
  33.8 0.2 add_convert_fusion
  34.1 2.1 %collective-permute-done.9.b_ref = bf16[4,4,16,2048]{3,2,1,0:T(8,128)(2,1)S(1)} collective-permute-done((bf16[4,4,16,2048]{3,2,1,0:T(8,128)(2,1)S(1)}, bf16[4,4,16,2048]{3,2,1,0:T(8,128)(2,1)S(1)}, u32[]{:S(2)}, u32[]{:S(2)}) %collective-permute-start.9) | collective-permute-done | bytes 1048608 | tf_op jit(solution)/shard_map/ppermute | solution.py:200
  36.2 0.2 core_sum.1
  36.4 1.5 %collective-permute-start.10 = (bf16[4,16,2048]{2,1,0:T(8,128)(2,1)S(1)}, bf16[4,16,2048]{2,1,0:T(8,128)(2,1)S(1)}, u32[]{:S(2)}, u32[]{:S(2)}) collective-permute-start(bf16[4,16,2048]{2,1,0:T(8,128)(2,1)S(1)} %get-tuple-element.45), channel_id=1, source_target_pairs={{0,8},{4,12},{8,0},{12,4},{16,24},{20,28},{24,16},{28,20},{1,9},{5... | collective-permute-start | bytes 786440 | tf_op jit(solution)/shard_map/ppermute | solution.py:200
  37.9 0.9 %collective-permute-start.11 = (bf16[4,16,2048]{2,1,0:T(8,128)(2,1)S(1)}, bf16[4,16,2048]{2,1,0:T(8,128)(2,1)S(1)}, u32[]{:S(2)}, u32[]{:S(2)}) collective-permute-start(bf16[4,16,2048]{2,1,0:T(8,128)(2,1)S(1)} %get-tuple-element.46), channel_id=1, source_target_pairs={{0,16},{4,20},{8,24},{12,28},{16,0},{20,4},{24,8},{28,12},{1,17},{... | collective-permute-start | bytes 786440 | tf_op jit(solution)/shard_map/ppermute | solution.py:200
  38.8 1.1 %collective-permute-start.12 = (bf16[4,16,2048]{2,1,0:T(8,128)(2,1)S(1)}, bf16[4,16,2048]{2,1,0:T(8,128)(2,1)S(1)}, u32[]{:S(2)}, u32[]{:S(2)}) collective-permute-start(bf16[4,16,2048]{2,1,0:T(8,128)(2,1)S(1)} %get-tuple-element.47), channel_id=1, source_target_pairs={{0,24},{4,28},{8,16},{12,20},{16,8},{20,12},{24,0},{28,4},{1,25},{... | collective-permute-start | bytes 786440 | tf_op jit(solution)/shard_map/ppermute | solution.py:200
  40.0 8.3 %collective-permute-done.17 = bf16[2,4,16,1024]{3,2,1,0:T(8,128)(2,1)S(1)} collective-permute-done((bf16[2,4,16,1024]{3,2,1,0:T(8,128)(2,1)S(1)}, bf16[2,4,16,1024]{3,2,1,0:T(8,128)(2,1)S(1)}, u32[]{:S(2)}, u32[]{:S(2)}) %collective-permute-start.17) | collective-permute-done | bytes 262176 | tf_op jit(solution)/shard_map/ppermute | solution.py:196
  48.4 3.2 %collective-permute-done.11 = bf16[4,16,2048]{2,1,0:T(8,128)(2,1)S(1)} collective-permute-done((bf16[4,16,2048]{2,1,0:T(8,128)(2,1)S(1)}, bf16[4,16,2048]{2,1,0:T(8,128)(2,1)S(1)}, u32[]{:S(2)}, u32[]{:S(2)}) %collective-permute-start.11) | collective-permute-done | bytes 262176 | tf_op jit(solution)/shard_map/ppermute | solution.py:200
  51.6 0.1 add_convert_fusion.1
  51.8 2.1 %collective-permute-done.18 = bf16[4,16,1024]{2,1,0:T(8,128)(2,1)S(1)} collective-permute-done((bf16[4,16,1024]{2,1,0:T(8,128)(2,1)S(1)}, bf16[4,16,1024]{2,1,0:T(8,128)(2,1)S(1)}, u32[]{:S(2)}, u32[]{:S(2)}) %collective-permute-start.18) | collective-permute-done | bytes 131104 | tf_op jit(solution)/shard_map/ppermute | solution.py:196
  53.9 2.2 %collective-permute-start.13 = (bf16[16,2048]{1,0:T(8,128)(2,1)S(1)}, bf16[16,2048]{1,0:T(8,128)(2,1)S(1)}, u32[]{:S(2)}, u32[]{:S(2)}) collective-permute-start(bf16[16,2048]{1,0:T(8,128)(2,1)S(1)} %get-tuple-element.56), channel_id=1, source_target_pairs={{0,3},{1,2},{2,1},{3,0},{4,7},{5,6},{6,5},{7,4},{8,11},{9,10},{10,... | collective-permute-start | bytes 196616 | tf_op jit(solution)/shard_map/ppermute | solution.py:196
  56.1 2.3 %collective-permute-start.14 = (bf16[16,2048]{1,0:T(8,128)(2,1)S(1)}, bf16[16,2048]{1,0:T(8,128)(2,1)S(1)}, u32[]{:S(2)}, u32[]{:S(2)}) collective-permute-start(bf16[16,2048]{1,0:T(8,128)(2,1)S(1)} %get-tuple-element.58), channel_id=1, source_target_pairs={{0,1},{1,0},{2,3},{3,2},{4,5},{5,4},{6,7},{7,6},{8,9},{9,8},{10,11... | collective-permute-start | bytes 196616 | tf_op jit(solution)/shard_map/ppermute | solution.py:196
  58.4 2.5 %collective-permute-start.21 = (bf16[16,1024]{1,0:T(8,128)(2,1)S(1)}, bf16[16,1024]{1,0:T(8,128)(2,1)S(1)}, u32[]{:S(2)}, u32[]{:S(2)}) collective-permute-start(bf16[16,1024]{1,0:T(8,128)(2,1)S(1)} %get-tuple-element.59), channel_id=1, source_target_pairs={{0,24},{4,28},{8,16},{12,20},{16,8},{20,12},{24,0},{28,4},{1,25},{... | collective-permute-start | bytes 98312 | tf_op jit(solution)/shard_map/ppermute | solution.py:200
  60.9 0.5 collective-permute-start.20
  61.4 0.6 collective-permute-start.19
  62.0 0.2 collective-permute-done.15
  62.2 0.7 %multiply_bitcast_fusion = f32[1,2048,16]{1,2,0:T(8,128)} fusion(bf16[16,2048]{1,0:T(8,128)(2,1)S(1)} %collective-permute-done.15, bf16[16,2048]{1,0:T(8,128)(2,1)S(1)} %collective-permute-done.14, bf16[16,2048]{1,0:T(8,128)(2,1)S(1)} %collective-permute-done.13, bf16[4,16,2048]{2,1,0:T(8,128)(2,1)S(1)} %add_convert_fusion.1), kind=kLoop, calls=%fused_computation.12 | loop fusion | flops 262144 | bytes 393216 | tf_op jit(solution)/shard_map/mul | solution.py:341
  62.9 0.6 collective-permute-done.21
  63.4 1.3 %collective-permute-done.20 = bf16[16,1024]{1,0:T(8,128)(2,1)S(1)} collective-permute-done((bf16[16,1024]{1,0:T(8,128)(2,1)S(1)}, bf16[16,1024]{1,0:T(8,128)(2,1)S(1)}, u32[]{:S(2)}, u32[]{:S(2)}) %collective-permute-start.20) | collective-permute-done | bytes 32800 | tf_op jit(solution)/shard_map/ppermute | solution.py:200
  64.8 0.5 collective-permute-done.19
  65.3 0.7 fusion.8
  (38 shorter events, 0.5 us)
Async XLA Ops:
  0.6 23.0 %copy-start.1 = (bf16[128,4096]{1,0:T(8,128)(2,1)S(1)}, bf16[128,4096]{1,0:T(8,128)(2,1)}, u32[]{:S(2)}) copy-start(bf16[128,4096]{1,0:T(8,128)(2,1)} %g_hbm.3) | copy-start | bytes 3145732
  0.6 23.0 %copy-start = (bf16[128,4096]{1,0:T(8,128)(2,1)S(1)}, bf16[128,4096]{1,0:T(8,128)(2,1)}, u32[]{:S(2)}) copy-start(bf16[128,4096]{1,0:T(8,128)(2,1)} %q_hbm.3) | copy-start | bytes 3145732
  0.6 18.3 %collective-permute-start.3 = (bf16[1,16,1024]{2,1,0:T(8,128)(2,1)}, bf16[1,16,1024]{2,1,0:T(8,128)(2,1)S(1)}, u32[]{:S(2)}, u32[]{:S(2)}) collective-permute-start(bf16[1,16,1024]{2,1,0:T(8,128)(2,1)} %param.16), channel_id=1, source_target_pairs={{0,2},{1,3},{2,0},{3,1},{4,6},{5,7},{6,4},{7,5},{8,10},{9,11},{10,... | collective-permute-start | bytes 98312 | tf_op jit(solution)/shard_map/ppermute | solution.py:192
  4.8 14.2 %collective-permute-start.2 = (bf16[1,16,1024]{2,1,0:T(8,128)(2,1)}, bf16[1,16,1024]{2,1,0:T(8,128)(2,1)S(1)}, u32[]{:S(2)}, u32[]{:S(2)}) collective-permute-start(bf16[1,16,1024]{2,1,0:T(8,128)(2,1)} %param.16), channel_id=1, source_target_pairs={{0,1},{1,2},{2,3},{3,0},{4,5},{5,6},{6,7},{7,4},{8,9},{9,10},{10,1... | collective-permute-start | bytes 98312 | tf_op jit(solution)/shard_map/ppermute | solution.py:192
  6.3 12.6 %collective-permute-start.4 = (bf16[1,16,1024]{2,1,0:T(8,128)(2,1)}, bf16[1,16,1024]{2,1,0:T(8,128)(2,1)S(1)}, u32[]{:S(2)}, u32[]{:S(2)}) collective-permute-start(bf16[1,16,1024]{2,1,0:T(8,128)(2,1)} %param.16), channel_id=1, source_target_pairs={{0,3},{1,0},{2,1},{3,2},{4,7},{5,4},{6,5},{7,6},{8,11},{9,8},{10,9... | collective-permute-start | bytes 98312 | tf_op jit(solution)/shard_map/ppermute | solution.py:192
  10.4 13.0 %collective-permute-start.1 = (bf16[128,1024]{1,0:T(8,128)(2,1)S(1)}, bf16[128,1024]{1,0:T(8,128)(2,1)S(1)}, u32[]{:S(2)}, u32[]{:S(2)}) collective-permute-start(bf16[128,1024]{1,0:T(8,128)(2,1)S(1)} %constant_dynamic-update-slice_fusion.refs_3_), channel_id=1, source_target_pairs={{0,1},{1,2},{2,3},{4,5},{5,6},{6,7},{8,9},{9,10},{10,11},{12,13},{... | collective-permute-start | bytes 786440 | tf_op jit(solution)/shard_map/ppermute | solution.py:225
  12.1 11.3 %collective-permute-start = (bf16[64,1024]{1,0:T(8,128)(2,1)S(1)}, bf16[64,1024]{1,0:T(8,128)(2,1)S(1)}, u32[]{:S(2)}, u32[]{:S(2)}) collective-permute-start(bf16[64,1024]{1,0:T(8,128)(2,1)S(1)} %slice.53), channel_id=1, source_target_pairs={{0,2},{1,3},{4,6},{5,7},{8,10},{9,11},{12,14},{13,15},{16,18},{17,... | collective-permute-start | bytes 393224 | tf_op jit(solution)/shard_map/ppermute | solution.py:225
  19.7 7.3 %collective-permute-start.7 = (bf16[1,4,16,1024]{3,2,1,0:T(8,128)(2,1)S(1)}, bf16[1,4,16,1024]{3,2,1,0:T(8,128)(2,1)S(1)}, u32[]{:S(2)}, u32[]{:S(2)}) collective-permute-start(bf16[1,4,16,1024]{3,2,1,0:T(8,128)(2,1)S(1)} %maximum_bitcast_fusion), channel_id=1, source_target_pairs={{0,24},{4,28},{8,16},{12,20},{16,8},{20,12},{24,0},{28,4},{1,25},{... | collective-permute-start | bytes 393224 | tf_op jit(solution)/shard_map/ppermute | solution.py:200
  22.3 5.5 %collective-permute-start.6 = (bf16[1,4,16,1024]{3,2,1,0:T(8,128)(2,1)S(1)}, bf16[1,4,16,1024]{3,2,1,0:T(8,128)(2,1)S(1)}, u32[]{:S(2)}, u32[]{:S(2)}) collective-permute-start(bf16[1,4,16,1024]{3,2,1,0:T(8,128)(2,1)S(1)} %maximum_bitcast_fusion), channel_id=1, source_target_pairs={{0,16},{4,20},{8,24},{12,28},{16,0},{20,4},{24,8},{28,12},{1,17},{... | collective-permute-start | bytes 393224 | tf_op jit(solution)/shard_map/ppermute | solution.py:200
  22.8 5.0 %collective-permute-start.5 = (bf16[1,4,16,1024]{3,2,1,0:T(8,128)(2,1)S(1)}, bf16[1,4,16,1024]{3,2,1,0:T(8,128)(2,1)S(1)}, u32[]{:S(2)}, u32[]{:S(2)}) collective-permute-start(bf16[1,4,16,1024]{3,2,1,0:T(8,128)(2,1)S(1)} %maximum_bitcast_fusion), channel_id=1, source_target_pairs={{0,8},{4,12},{8,0},{12,4},{16,24},{20,28},{24,16},{28,20},{1,9},{5... | collective-permute-start | bytes 393224 | tf_op jit(solution)/shard_map/ppermute | solution.py:200
  23.7 4.2 %copy-start.3 = (bf16[128,16]{0,1:T(8,128)(2,1)S(1)}, bf16[128,16]{0,1:T(8,128)(2,1)}, u32[]{:S(2)}) copy-start(bf16[128,16]{0,1:T(8,128)(2,1)} %param.15) | copy-start | bytes 12292
  27.8 3.9 %collective-permute-start.8 = (bf16[4,4,16,1024]{3,2,1,0:T(8,128)(2,1)S(1)}, bf16[4,4,16,1024]{3,2,1,0:T(8,128)(2,1)S(1)}, u32[]{:S(2)}, u32[]{:S(2)}) collective-permute-start(bf16[4,4,16,1024]{3,2,1,0:T(8,128)(2,1)S(1)} %constant_dynamic-update-slice_fusion.2.refs_0_), channel_id=1, source_target_pairs={{0,4},{4,0},{8,12},{12,8},{16,20},{20,16},{24,28},{28,24},{1,5},{5... | collective-permute-start | bytes 1572872 | tf_op jit(solution)/shard_map/ppermute | solution.py:200
  27.9 4.8 %copy-start.2 = (bf16[128,8192]{1,0:T(8,128)(2,1)S(1)}, bf16[128,8192]{1,0:T(8,128)(2,1)}, u32[]{:S(2)}) copy-start(bf16[128,8192]{1,0:T(8,128)(2,1)} %x_ref.1) | copy-start | bytes 6291460
  31.7 2.1 %collective-permute-start.16 = (bf16[4,4,16,1024]{3,2,1,0:T(8,128)(2,1)S(1)}, bf16[4,4,16,1024]{3,2,1,0:T(8,128)(2,1)S(1)}, u32[]{:S(2)}, u32[]{:S(2)}) collective-permute-start(bf16[4,4,16,1024]{3,2,1,0:T(8,128)(2,1)S(1)} %get-tuple-element.49), channel_id=1, source_target_pairs={{0,4},{4,0},{8,12},{12,8},{16,20},{20,16},{24,28},{28,24},{1,5},{5... | collective-permute-start | bytes 1572872 | tf_op jit(solution)/shard_map/ppermute | solution.py:200
  33.4 2.7 %collective-permute-start.9 = (bf16[4,4,16,2048]{3,2,1,0:T(8,128)(2,1)S(1)}, bf16[4,4,16,2048]{3,2,1,0:T(8,128)(2,1)S(1)}, u32[]{:S(2)}, u32[]{:S(2)}) collective-permute-start(bf16[4,4,16,2048]{3,2,1,0:T(8,128)(2,1)S(1)} %get-tuple-element.43), channel_id=1, source_target_pairs={{0,4},{4,0},{8,12},{12,8},{16,20},{20,16},{24,28},{28,24},{1,5},{5... | collective-permute-start | bytes 3145736 | tf_op jit(solution)/shard_map/ppermute | solution.py:200
  34.0 14.2 %collective-permute-start.17 = (bf16[2,4,16,1024]{3,2,1,0:T(8,128)(2,1)S(1)}, bf16[2,4,16,1024]{3,2,1,0:T(8,128)(2,1)S(1)}, u32[]{:S(2)}, u32[]{:S(2)}) collective-permute-start(bf16[2,4,16,1024]{3,2,1,0:T(8,128)(2,1)S(1)} %slice.59), channel_id=1, source_target_pairs={{0,2},{1,3},{2,0},{3,1},{4,6},{5,7},{6,4},{7,5},{8,10},{9,11},{10,... | collective-permute-start | bytes 786440 | tf_op jit(solution)/shard_map/ppermute | solution.py:196
  36.4 12.0 %collective-permute-start.10 = (bf16[4,16,2048]{2,1,0:T(8,128)(2,1)S(1)}, bf16[4,16,2048]{2,1,0:T(8,128)(2,1)S(1)}, u32[]{:S(2)}, u32[]{:S(2)}) collective-permute-start(bf16[4,16,2048]{2,1,0:T(8,128)(2,1)S(1)} %get-tuple-element.45), channel_id=1, source_target_pairs={{0,8},{4,12},{8,0},{12,4},{16,24},{20,28},{24,16},{28,20},{1,9},{5... | collective-permute-start | bytes 786440 | tf_op jit(solution)/shard_map/ppermute | solution.py:200
  37.9 13.7 %collective-permute-start.11 = (bf16[4,16,2048]{2,1,0:T(8,128)(2,1)S(1)}, bf16[4,16,2048]{2,1,0:T(8,128)(2,1)S(1)}, u32[]{:S(2)}, u32[]{:S(2)}) collective-permute-start(bf16[4,16,2048]{2,1,0:T(8,128)(2,1)S(1)} %get-tuple-element.46), channel_id=1, source_target_pairs={{0,16},{4,20},{8,24},{12,28},{16,0},{20,4},{24,8},{28,12},{1,17},{... | collective-permute-start | bytes 786440 | tf_op jit(solution)/shard_map/ppermute | solution.py:200
  38.8 12.8 %collective-permute-start.12 = (bf16[4,16,2048]{2,1,0:T(8,128)(2,1)S(1)}, bf16[4,16,2048]{2,1,0:T(8,128)(2,1)S(1)}, u32[]{:S(2)}, u32[]{:S(2)}) collective-permute-start(bf16[4,16,2048]{2,1,0:T(8,128)(2,1)S(1)} %get-tuple-element.47), channel_id=1, source_target_pairs={{0,24},{4,28},{8,16},{12,20},{16,8},{20,12},{24,0},{28,4},{1,25},{... | collective-permute-start | bytes 786440 | tf_op jit(solution)/shard_map/ppermute | solution.py:200
  48.4 5.5 %collective-permute-start.18 = (bf16[4,16,1024]{2,1,0:T(8,128)(2,1)S(1)}, bf16[4,16,1024]{2,1,0:T(8,128)(2,1)S(1)}, u32[]{:S(2)}, u32[]{:S(2)}) collective-permute-start(bf16[4,16,1024]{2,1,0:T(8,128)(2,1)S(1)} %fusion.2), channel_id=1, source_target_pairs={{0,1},{1,0},{2,3},{3,2},{4,5},{5,4},{6,7},{7,6},{8,9},{9,8},{10,11... | collective-permute-start | bytes 393224 | tf_op jit(solution)/shard_map/ppermute | solution.py:196
  53.9 7.5 %collective-permute-start.13 = (bf16[16,2048]{1,0:T(8,128)(2,1)S(1)}, bf16[16,2048]{1,0:T(8,128)(2,1)S(1)}, u32[]{:S(2)}, u32[]{:S(2)}) collective-permute-start(bf16[16,2048]{1,0:T(8,128)(2,1)S(1)} %get-tuple-element.56), channel_id=1, source_target_pairs={{0,3},{1,2},{2,1},{3,0},{4,7},{5,6},{6,5},{7,4},{8,11},{9,10},{10,... | collective-permute-start | bytes 196616 | tf_op jit(solution)/shard_map/ppermute | solution.py:196
  56.1 6.1 %collective-permute-start.15 = (bf16[16,2048]{1,0:T(8,128)(2,1)S(1)}, bf16[16,2048]{1,0:T(8,128)(2,1)S(1)}, u32[]{:S(2)}, u32[]{:S(2)}) collective-permute-start(bf16[16,2048]{1,0:T(8,128)(2,1)S(1)} %get-tuple-element.57), channel_id=1, source_target_pairs={{0,2},{1,3},{2,0},{3,1},{4,6},{5,7},{6,4},{7,5},{8,10},{9,11},{10,... | collective-permute-start | bytes 196616 | tf_op jit(solution)/shard_map/ppermute | solution.py:196
  56.1 6.1 %collective-permute-start.14 = (bf16[16,2048]{1,0:T(8,128)(2,1)S(1)}, bf16[16,2048]{1,0:T(8,128)(2,1)S(1)}, u32[]{:S(2)}, u32[]{:S(2)}) collective-permute-start(bf16[16,2048]{1,0:T(8,128)(2,1)S(1)} %get-tuple-element.58), channel_id=1, source_target_pairs={{0,1},{1,0},{2,3},{3,2},{4,5},{5,4},{6,7},{7,6},{8,9},{9,8},{10,11... | collective-permute-start | bytes 196616 | tf_op jit(solution)/shard_map/ppermute | solution.py:196
  58.4 5.1 %collective-permute-start.21 = (bf16[16,1024]{1,0:T(8,128)(2,1)S(1)}, bf16[16,1024]{1,0:T(8,128)(2,1)S(1)}, u32[]{:S(2)}, u32[]{:S(2)}) collective-permute-start(bf16[16,1024]{1,0:T(8,128)(2,1)S(1)} %get-tuple-element.59), channel_id=1, source_target_pairs={{0,24},{4,28},{8,16},{12,20},{16,8},{20,12},{24,0},{28,4},{1,25},{... | collective-permute-start | bytes 98312 | tf_op jit(solution)/shard_map/ppermute | solution.py:200
  60.9 3.9 %collective-permute-start.20 = (bf16[16,1024]{1,0:T(8,128)(2,1)S(1)}, bf16[16,1024]{1,0:T(8,128)(2,1)S(1)}, u32[]{:S(2)}, u32[]{:S(2)}) collective-permute-start(bf16[16,1024]{1,0:T(8,128)(2,1)S(1)} %get-tuple-element.60), channel_id=1, source_target_pairs={{0,16},{4,20},{8,24},{12,28},{16,0},{20,4},{24,8},{28,12},{1,17},{... | collective-permute-start | bytes 98312 | tf_op jit(solution)/shard_map/ppermute | solution.py:200
  61.4 3.9 %collective-permute-start.19 = (bf16[16,1024]{1,0:T(8,128)(2,1)S(1)}, bf16[16,1024]{1,0:T(8,128)(2,1)S(1)}, u32[]{:S(2)}, u32[]{:S(2)}) collective-permute-start(bf16[16,1024]{1,0:T(8,128)(2,1)S(1)} %get-tuple-element.61), channel_id=1, source_target_pairs={{0,8},{4,12},{8,0},{12,4},{16,24},{20,28},{24,16},{28,20},{1,9},{5... | collective-permute-start | bytes 98312 | tf_op jit(solution)/shard_map/ppermute | solution.py:200

commit v14 on v12

--- a/solution.py
+++ b/solution.py
@@ -89,7 +89,7 @@
         k_g = k_all[:, at_kv]
         v_g = v_all[:, at_kv]
         kt_g = k_turned[at_kv, :]
-        for i in range(0, GROUP, 2):
+        def products(i):
             first = (kv * GROUP + i) * HEAD_SIZE
             at = [
                 pl.ds(pl.multiple_of(first + n * HEAD_SIZE, HEAD_SIZE), HEAD_SIZE) for n in range(2)
@@ -97,7 +97,13 @@
             q_two = jnp.concatenate([q_ref[:, at[0]], q_ref[:, at[1]]], axis=0)
             g_two = jnp.concatenate([g_ref[:, at[0]], g_ref[:, at[1]]], axis=0)
             s = dot(k_g, q_two, 1, 1) + jnp.concatenate([bias[...]] * 2, axis=1)
-            d_prob = dot(v_g, g_two, 1, 1)
+            return at, s, dot(v_g, g_two, 1, 1)
+
+        ahead = products(0)
+        for i in range(0, GROUP, 2):
+            at, s, d_prob = ahead
+            if i + 2 < GROUP:
+                ahead = products(i + 2)
             weights = jnp.exp2((s - jnp.max(s, axis=0, keepdims=True)) * to_log2)
             inverse = 1.0 / jnp.sum(weights, axis=0, keepdims=True)
             delta = jnp.sum(weights * d_prob, axis=0, keepdims=True) * inverse
@@ -175,16 +181,22 @@
 
 def token_facts(tok, lengths, adapters, owner, by_slot):
     n_seg = lengths.shape[0]
-    order = jnp.arange(n_seg, dtype=I32)
-    starts = jnp.sum(jnp.where(order[None, :] < order[:, None], lengths[None, :], 0), axis=1)
-    if by_slot:
-        hits = adapters[:, None] == jnp.arange(owner.shape[0], dtype=I32)[None, :]
-        groups = jnp.sum(jnp.where(hits, owner[None, :], 0), axis=1)
+    cube = (8, n_seg, n_seg)
+    row, at, k = (lax.broadcasted_iota(I32, cube, d) for d in range(3))
+    length = jnp.broadcast_to(lengths[None, None, :], cube)
+    adapter = jnp.broadcast_to(adapters[None, None, :], cube)
+    if by_slot:
+        hit = jnp.broadcast_to(adapters[None, :, None], cube) == k
+        group = jnp.where(hit, jnp.broadcast_to(owner[None, None, :], cube), 0)
     else:
-        groups = order
+        group = jnp.where(k == at, k, 0)
+    terms = jnp.where(row == 2, group, 0)
+    terms = jnp.where((row == 0) & (k < at), length, terms)
+    terms = jnp.where((row == 1) & (k == at), adapter, terms)
+    terms = jnp.where((row == 3) & (k <= at), length, terms)
+    told = jnp.sum(terms, axis=2)
     position = lax.axis_index("head") * tok + jnp.arange(tok, dtype=I32)
-    inside = (position >= starts[:, None]) & (position < (starts + lengths)[:, None])
-    told = jnp.stack([starts, adapters, groups] + [jnp.zeros_like(starts)] * 5)
+    inside = (position >= told[0][:, None]) & (position < told[3][:, None])
     return jnp.sum(jnp.where(inside[None], told[:, :, None], 0), axis=1)
 
 
@@ -211,7 +223,7 @@
     rank = adapter_up_weight.shape[1]
     n_adapters = owner.shape[0]
     n_seg = segment_length.shape[1]
-    by_slot = n_adapters == n_seq == 8 and n_head == 4
+    by_slot = n_adapters == n_seq == n_seg == 8 and n_head == 4
     facts = token_facts(tok, segment_length[0], segment_adapter[0], owner, by_slot)
 
     reach = []

time: 62.1 us -> 60 us (0.966)
  waiting for transfers between devices: 11.4 us -> 13 us
  Pallas kernels: 8.8 us -> 7.21 us
  other arithmetic: 4.97 us -> 3.72 us
  local copies, waits for them, and re-layouts: 3.66 us -> 2.98 us
    pallas_call x2, Pallas kernels: 7.14 us -> 5.56 us  [attention(): pl.pallas_call(functools.partial(attention_kernel, by_slot, h * n_kv, n_k...]
    ppermute x6, waiting for transfers between devices: 10.5 us -> 11.3 us  [across(): return lax.ppermute(x, 'head', [(i, i ^ j) for i in range(n_head)])]
    ppermute x12, waiting for transfers between devices: 0.95 us -> 1.73 us  [partnered(): return lax.ppermute(x, 'seq', [(i, i ^ bits) for i in range(n_seq)])]
    another operation x3 -> x0, local copies, waits for them, and re-layouts: 0.68 us -> none  [the longest x2 0.68 us: token_facts(): told = jnp.stack([starts, adapters, groups] + [jnp.zeros_like(starts)] * 5)]
    add x1 -> x0, other arithmetic: 0.66 us -> none  [token_facts(): starts + lengths]
    reduce_sum x2 -> x1, other arithmetic: 1.62 us -> 1.02 us  [token_facts(): told = jnp.sum(terms, axis=2)]
  transfers between devices with their start and end apart: 23 -> 23, of which waited for: 6 -> 7; matrix products, arithmetic and copies ran while one was open for 13% -> 10% of each run, Pallas kernels for 14% -> 12%
where the time goes in v14:
time: 60 us; the launch traced here: 59.7 us
  starting transfers between devices  31.8 us (53%)
  waiting for transfers between devices  13 us (22%)
  Pallas kernels  7.21 us (12%)
  other arithmetic  3.72 us (6%)
  local copies, waits for them, and re-layouts  2.98 us (5%)
  between operations  0.96 us (2%)
    ppermute x12, starting transfers between devices, partnered(): return lax.ppermute(x, 'seq', [(i, i ^ bits) for i in range(n_seq)])  11.5 us
    ppermute x6, waiting for transfers between devices, across(): return lax.ppermute(x, 'head', [(i, i ^ j) for i in range(n_head)])  11.3 us
    ppermute x6, starting transfers between devices, across(): return lax.ppermute(x, 'head', [(i, i ^ j) for i in range(n_head)])  8.02 us
    ppermute x3, starting transfers between devices, shifted(): lax.ppermute(x, 'head', [(i, (i + j) % n_head) for i in range(n_head)])  7.93 us
    pallas_call x2, Pallas kernels, attention(): pl.pallas_call(functools.partial(attention_kernel, by_slot, h * n_kv, n_k...  5.56 us
    ppermute x2, starting transfers between devices, on_device(): parts.insert(0, lax.ppermute(own[tok - rows:], 'head', shift))  4.39 us
    unnamed x13, local copies, waits for them, and re-layouts  1.99 us
    ppermute x12, waiting for transfers between devices, partnered(): return lax.ppermute(x, 'seq', [(i, i ^ bits) for i in range(n_seq)])  1.73 us
  transfers between devices with their start and end apart: 23, of which 7 were waited for; matrix products, arithmetic and copies ran while one was open for 10% of the time, Pallas kernels for 12%

profile of v14, /device:TPU:0, one launch (start us, length us, event | category | flops | bytes accessed | tf_op | source)
XLA Modules:
  0.0 59.7 jit_solution(10383595641062089540)
XLA Ops:
  0.6 4.1 %collective-permute-start.3 = (bf16[1,16,1024]{2,1,0:T(8,128)(2,1)}, bf16[1,16,1024]{2,1,0:T(8,128)(2,1)S(1)}, u32[]{:S(2)}, u32[]{:S(2)}) collective-permute-start(bf16[1,16,1024]{2,1,0:T(8,128)(2,1)} %param.16), channel_id=1, source_target_pairs={{0,2},{1,3},{2,0},{3,1},{4,6},{5,7},{6,4},{7,5},{8,10},{9,11},{10,... | collective-permute-start | bytes 98312 | tf_op jit(solution)/shard_map/ppermute | solution.py:204
  4.8 1.6 %collective-permute-start.2 = (bf16[1,16,1024]{2,1,0:T(8,128)(2,1)}, bf16[1,16,1024]{2,1,0:T(8,128)(2,1)S(1)}, u32[]{:S(2)}, u32[]{:S(2)}) collective-permute-start(bf16[1,16,1024]{2,1,0:T(8,128)(2,1)} %param.16), channel_id=1, source_target_pairs={{0,1},{1,2},{2,3},{3,0},{4,5},{5,6},{6,7},{7,4},{8,9},{9,10},{10,1... | collective-permute-start | bytes 98312 | tf_op jit(solution)/shard_map/ppermute | solution.py:204
  6.3 2.2 %collective-permute-start.4 = (bf16[1,16,1024]{2,1,0:T(8,128)(2,1)}, bf16[1,16,1024]{2,1,0:T(8,128)(2,1)S(1)}, u32[]{:S(2)}, u32[]{:S(2)}) collective-permute-start(bf16[1,16,1024]{2,1,0:T(8,128)(2,1)} %param.16), channel_id=1, source_target_pairs={{0,3},{1,0},{2,1},{3,2},{4,7},{5,4},{6,5},{7,6},{8,11},{9,8},{10,9... | collective-permute-start | bytes 98312 | tf_op jit(solution)/shard_map/ppermute | solution.py:204
  8.6 0.9 %constant_dynamic-update-slice_fusion.1 = bf16[128,1024]{1,0:T(8,128)(2,1)S(1)} fusion(bf16[128,512]{1,0:T(8,128)(2,1)} %param.11), kind=kLoop, calls=%fused_computation.39 | loop fusion | bytes 262144
  9.5 0.9 %constant_dynamic-update-slice_fusion.refs_3_ = bf16[128,1024]{1,0:T(8,128)(2,1)S(1)} fusion(bf16[128,1024]{1,0:T(8,128)(2,1)S(1)} %constant_dynamic-update-slice_fusion.1, bf16[128,512]{1,0:T(8,128)(2,1)} %param.12), kind=kLoop, calls=%fused_computation.38 | loop fusion | bytes 262144 | tf_op jit(solution)/shard_map/concatenate | solution.py:233
  10.4 1.7 %collective-permute-start.1 = (bf16[128,1024]{1,0:T(8,128)(2,1)S(1)}, bf16[128,1024]{1,0:T(8,128)(2,1)S(1)}, u32[]{:S(2)}, u32[]{:S(2)}) collective-permute-start(bf16[128,1024]{1,0:T(8,128)(2,1)S(1)} %constant_dynamic-update-slice_fusion.refs_3_), channel_id=1, source_target_pairs={{0,1},{1,2},{2,3},{4,5},{5,6},{6,7},{8,9},{9,10},{10,11},{12,13},{... | collective-permute-start | bytes 786440 | tf_op jit(solution)/shard_map/ppermute | solution.py:237
  12.1 2.7 %collective-permute-start = (bf16[64,1024]{1,0:T(8,128)(2,1)S(1)}, bf16[64,1024]{1,0:T(8,128)(2,1)S(1)}, u32[]{:S(2)}, u32[]{:S(2)}) collective-permute-start(bf16[64,1024]{1,0:T(8,128)(2,1)S(1)} %slice.60), channel_id=1, source_target_pairs={{0,2},{1,3},{4,6},{5,7},{8,10},{9,11},{12,14},{13,15},{16,18},{17,... | collective-permute-start | bytes 393224 | tf_op jit(solution)/shard_map/ppermute | solution.py:237
  14.9 1.0 %select_reduce_fusion.1 = s32[8,8]{1,0:T(8,128)S(1)} fusion(s32[8]{0:T(128)} %param.19, s32[8]{0:T(128)} %bitcast.51, s32[8]{0:T(128)} %bitcast.52, pred[8]{0:T(512)(128)(4,1)S(1)} %get-tuple-element.57, pred[8]{0:T(512)(128)(4,1)S(1)} %get-tuple-element.58, pred[8]{0:T(512)(128)(4,1)S(1)} %get-tuple-element.59, pred[8]{0:T(512)(128)(4,1)S(1)} %get-tuple-element.60), kind=kLoop, calls=%fused_computation.30 | loop fusion | flops 6592 | bytes 384 | tf_op jit(solution)/shard_map/reduce_sum | solution.py:197
  15.9 0.1 compare_and_fusion
  16.0 1.0 %copy.13 = bf16[128,512]{0,1:T(8,128)(2,1)S(1)} copy(bf16[128,512]{1,0:T(8,128)(2,1)} %param.11) | data formatting | bytes 262144 | tf_op args[1]
  17.0 0.8 %maximum_bitcast_fusion = bf16[1,4,16,1024]{3,2,1,0:T(8,128)(2,1)S(1)} fusion(bf16[1,16,1024]{2,1,0:T(8,128)(2,1)S(1)} %collective-permute-done.4, bf16[1,16,1024]{2,1,0:T(8,128)(2,1)S(1)} %collective-permute-done.3, bf16[1,16,1024]{2,1,0:T(8,128)(2,1)S(1)} %collective-permute-done.2, bf16[1,16,1024]{2,1,0:T(8,128)(2,1)} %param.16), kind=kLoop, calls=%fused_computation.10 | loop fusion | flops 196608 | bytes 262144 | tf_op jit(solution)/shard_map/broadcast_in_dim | solution.py:241
  17.8 2.5 %collective-permute-start.7 = (bf16[1,4,16,1024]{3,2,1,0:T(8,128)(2,1)S(1)}, bf16[1,4,16,1024]{3,2,1,0:T(8,128)(2,1)S(1)}, u32[]{:S(2)}, u32[]{:S(2)}) collective-permute-start(bf16[1,4,16,1024]{3,2,1,0:T(8,128)(2,1)S(1)} %maximum_bitcast_fusion), channel_id=1, source_target_pairs={{0,24},{4,28},{8,16},{12,20},{16,8},{20,12},{24,0},{28,4},{1,25},{... | collective-permute-start | bytes 393224 | tf_op jit(solution)/shard_map/ppermute | solution.py:212
  20.3 0.5 collective-permute-start.6
  20.9 0.5 collective-permute-start.5
  21.4 0.1 select_reduce_fusion.facts_ref.refs_0_
  21.5 0.3 layout.1
  21.8 2.6 %attention_0.1.refs_2_ = bf16[2048,128]{1,0:T(8,128)(2,1)S(1)} custom-call(bf16[320,512]{1,0:T(8,128)(2,1)S(1)} %get-tuple-element.24.k_all, bf16[320,512]{1,0:T(8,128)(2,1)S(1)} %get-tuple-element.25.v_all, bf16[512,320]{1,0:T(8,128)(2,1)S(1)} %get-tuple-element.26.k_turned, f32[320,128]{1,0:T(8,128)S(1)} %get-tuple-element.27.bias, ...), custom_call_target="tpu_custom_call" | custom-call | flops 503316480 | bytes 2097152 | tf_op jit(solution)/shard_map/attention_0/pallas_call | solution.py:274
  24.4 0.6 collective-permute-done.7
  25.0 0.9 %collective-permute-done.6 = bf16[1,4,16,1024]{3,2,1,0:T(8,128)(2,1)S(1)} collective-permute-done((bf16[1,4,16,1024]{3,2,1,0:T(8,128)(2,1)S(1)}, bf16[1,4,16,1024]{3,2,1,0:T(8,128)(2,1)S(1)}, u32[]{:S(2)}, u32[]{:S(2)}) %collective-permute-start.6) | collective-permute-done | bytes 131104 | tf_op jit(solution)/shard_map/ppermute | solution.py:212
  25.9 0.1 collective-permute-start.8
  26.0 0.0 copy-start.2
  26.0 3.0 %attention_1.1 = (bf16[2048,128]{1,0:T(8,128)(2,1)S(1)}, bf16[4,4,16,1024]{3,2,1,0:T(8,128)(2,1)S(1)}, bf16[4,4,16,1024]{3,2,1,0:T(8,128)(2,1)S(1)}) custom-call(bf16[320,512]{1,0:T(8,128)(2,1)S(1)} %get-tuple-element.24.k_all, bf16[320,512]{1,0:T(8,128)(2,1)S(1)} %get-tuple-element.25.v_all, bf16[512,320]{1,0:T(8,128)(2,1)S(1)} %get-tuple-element.26.k_turned, ...), custom_call_target="tpu_custom_call" | custom-call | flops 503316480 | bytes 2097152 | tf_op jit(solution)/shard_map/attention_1/pallas_call | solution.py:274
  29.0 0.5 collective-permute-start.16
  29.5 0.4 rank_gradient.1.rank_ref
  30.0 0.7 %down_parts.1 = (bf16[4,4,16,2048]{3,2,1,0:T(8,128)(2,1)S(1)}, bf16[4,4,16,2048]{3,2,1,0:T(8,128)(2,1)S(1)}) custom-call(s32[8,128]{1,0:T(8,128)S(1)} %select_reduce_fusion.facts_ref.refs_0_, bf16[128,8192]{1,0:T(8,128)(2,1)S(1)} %copy-done.2, bf16[16,128]{1,0:T(8,128)(2,1)S(1)} %rank_gradient.1.rank_ref), custom_call_target="tpu_custom_call" | custom-call | flops 268435456 | bytes 8388608 | tf_op jit(solution)/shard_map/down_parts/pallas_call | solution.py:314
  30.7 0.1 collective-permute-start.9
  30.8 0.2 collective-permute-done.16
  31.1 0.2 add_convert_fusion
  31.3 0.1 collective-permute-start.17
  31.4 2.9 %collective-permute-start.19 = (bf16[4,16,1024]{2,1,0:T(8,128)(2,1)S(1)}, bf16[4,16,1024]{2,1,0:T(8,128)(2,1)S(1)}, u32[]{:S(2)}, u32[]{:S(2)}) collective-permute-start(bf16[4,16,1024]{2,1,0:T(8,128)(2,1)S(1)} %get-tuple-element.47), channel_id=1, source_target_pairs={{0,3},{1,2},{2,1},{3,0},{4,7},{5,6},{6,5},{7,4},{8,11},{9,10},{10,... | collective-permute-start | bytes 393224 | tf_op jit(solution)/shard_map/ppermute | solution.py:208
  34.3 0.6 collective-permute-start.18
  34.9 0.2 core_sum.1
  35.1 1.5 %collective-permute-start.10 = (bf16[4,16,2048]{2,1,0:T(8,128)(2,1)S(1)}, bf16[4,16,2048]{2,1,0:T(8,128)(2,1)S(1)}, u32[]{:S(2)}, u32[]{:S(2)}) collective-permute-start(bf16[4,16,2048]{2,1,0:T(8,128)(2,1)S(1)} %get-tuple-element.41), channel_id=1, source_target_pairs={{0,8},{4,12},{8,0},{12,4},{16,24},{20,28},{24,16},{28,20},{1,9},{5... | collective-permute-start | bytes 786440 | tf_op jit(solution)/shard_map/ppermute | solution.py:212
  36.7 1.5 %collective-permute-start.11 = (bf16[4,16,2048]{2,1,0:T(8,128)(2,1)S(1)}, bf16[4,16,2048]{2,1,0:T(8,128)(2,1)S(1)}, u32[]{:S(2)}, u32[]{:S(2)}) collective-permute-start(bf16[4,16,2048]{2,1,0:T(8,128)(2,1)S(1)} %get-tuple-element.42), channel_id=1, source_target_pairs={{0,16},{4,20},{8,24},{12,28},{16,0},{20,4},{24,8},{28,12},{1,17},{... | collective-permute-start | bytes 786440 | tf_op jit(solution)/shard_map/ppermute | solution.py:212
  38.1 0.7 %collective-permute-start.12 = (bf16[4,16,2048]{2,1,0:T(8,128)(2,1)S(1)}, bf16[4,16,2048]{2,1,0:T(8,128)(2,1)S(1)}, u32[]{:S(2)}, u32[]{:S(2)}) collective-permute-start(bf16[4,16,2048]{2,1,0:T(8,128)(2,1)S(1)} %get-tuple-element.43), channel_id=1, source_target_pairs={{0,24},{4,28},{8,16},{12,20},{16,8},{20,12},{24,0},{28,4},{1,25},{... | collective-permute-start | bytes 786440 | tf_op jit(solution)/shard_map/ppermute | solution.py:212
  38.8 2.7 %collective-permute-done.19 = bf16[4,16,1024]{2,1,0:T(8,128)(2,1)S(1)} collective-permute-done((bf16[4,16,1024]{2,1,0:T(8,128)(2,1)S(1)}, bf16[4,16,1024]{2,1,0:T(8,128)(2,1)S(1)}, u32[]{:S(2)}, u32[]{:S(2)}) %collective-permute-start.19) | collective-permute-done | bytes 131104 | tf_op jit(solution)/shard_map/ppermute | solution.py:208
  41.5 5.5 %collective-permute-done.18 = bf16[4,16,1024]{2,1,0:T(8,128)(2,1)S(1)} collective-permute-done((bf16[4,16,1024]{2,1,0:T(8,128)(2,1)S(1)}, bf16[4,16,1024]{2,1,0:T(8,128)(2,1)S(1)}, u32[]{:S(2)}, u32[]{:S(2)}) %collective-permute-start.18) | collective-permute-done | bytes 131104 | tf_op jit(solution)/shard_map/ppermute | solution.py:208
  47.0 0.1 fusion.2
  47.0 1.6 %collective-permute-start.20 = (bf16[16,1024]{1,0:T(8,128)(2,1)S(1)}, bf16[16,1024]{1,0:T(8,128)(2,1)S(1)}, u32[]{:S(2)}, u32[]{:S(2)}) collective-permute-start(bf16[16,1024]{1,0:T(8,128)(2,1)S(1)} %get-tuple-element.52), channel_id=1, source_target_pairs={{0,8},{4,12},{8,0},{12,4},{16,24},{20,28},{24,16},{28,20},{1,9},{5... | collective-permute-start | bytes 98312 | tf_op jit(solution)/shard_map/ppermute | solution.py:212
  48.6 1.5 %collective-permute-start.22 = (bf16[16,1024]{1,0:T(8,128)(2,1)S(1)}, bf16[16,1024]{1,0:T(8,128)(2,1)S(1)}, u32[]{:S(2)}, u32[]{:S(2)}) collective-permute-start(bf16[16,1024]{1,0:T(8,128)(2,1)S(1)} %get-tuple-element.53), channel_id=1, source_target_pairs={{0,24},{4,28},{8,16},{12,20},{16,8},{20,12},{24,0},{28,4},{1,25},{... | collective-permute-start | bytes 98312 | tf_op jit(solution)/shard_map/ppermute | solution.py:212
  50.1 0.5 collective-permute-start.21
  50.6 0.1 add_convert_fusion.1
  50.8 2.7 %collective-permute-start.13 = (bf16[16,2048]{1,0:T(8,128)(2,1)S(1)}, bf16[16,2048]{1,0:T(8,128)(2,1)S(1)}, u32[]{:S(2)}, u32[]{:S(2)}) collective-permute-start(bf16[16,2048]{1,0:T(8,128)(2,1)S(1)} %get-tuple-element.49), channel_id=1, source_target_pairs={{0,3},{1,2},{2,1},{3,0},{4,7},{5,6},{6,5},{7,4},{8,11},{9,10},{10,... | collective-permute-start | bytes 196616 | tf_op jit(solution)/shard_map/ppermute | solution.py:208
  53.5 1.7 %collective-permute-start.14 = (bf16[16,2048]{1,0:T(8,128)(2,1)S(1)}, bf16[16,2048]{1,0:T(8,128)(2,1)S(1)}, u32[]{:S(2)}, u32[]{:S(2)}) collective-permute-start(bf16[16,2048]{1,0:T(8,128)(2,1)S(1)} %get-tuple-element.51), channel_id=1, source_target_pairs={{0,1},{1,0},{2,3},{3,2},{4,5},{5,4},{6,7},{7,6},{8,9},{9,8},{10,11... | collective-permute-start | bytes 196616 | tf_op jit(solution)/shard_map/ppermute | solution.py:208
  55.2 0.7 %fusion.10 = f32[1,16,1024]{2,1,0:T(8,128)} fusion(bf16[16,1024]{1,0:T(8,128)(2,1)S(1)} %collective-permute-done.22, bf16[16,1024]{1,0:T(8,128)(2,1)S(1)} %collective-permute-done.21, bf16[16,1024]{1,0:T(8,128)(2,1)S(1)} %collective-permute-done.20, bf16[4,16,1024]{2,1,0:T(8,128)(2,1)S(1)} %fusion.2), kind=kLoop, calls=%fused_computation.24 | loop fusion | flops 131072 | bytes 196608 | tf_op jit(solution)/shard_map/mul | solution.py:345
  55.9 1.6 %collective-permute-done.13 = bf16[16,2048]{1,0:T(8,128)(2,1)S(1)} collective-permute-done((bf16[16,2048]{1,0:T(8,128)(2,1)S(1)}, bf16[16,2048]{1,0:T(8,128)(2,1)S(1)}, u32[]{:S(2)}, u32[]{:S(2)}) %collective-permute-start.13) | collective-permute-done | bytes 65568 | tf_op jit(solution)/shard_map/ppermute | solution.py:208
  57.5 1.5 %collective-permute-done.15 = bf16[16,2048]{1,0:T(8,128)(2,1)S(1)} collective-permute-done((bf16[16,2048]{1,0:T(8,128)(2,1)S(1)}, bf16[16,2048]{1,0:T(8,128)(2,1)S(1)}, u32[]{:S(2)}, u32[]{:S(2)}) %collective-permute-start.15) | collective-permute-done | bytes 65568 | tf_op jit(solution)/shard_map/ppermute | solution.py:208
  59.0 0.7 %fusion.6 = f32[1,2048,16]{1,2,0:T(8,128)} fusion(bf16[16,2048]{1,0:T(8,128)(2,1)S(1)} %collective-permute-done.15, bf16[16,2048]{1,0:T(8,128)(2,1)S(1)} %collective-permute-done.14, bf16[16,2048]{1,0:T(8,128)(2,1)S(1)} %collective-permute-done.13, bf16[4,16,2048]{2,1,0:T(8,128)(2,1)S(1)} %add_convert_fusion.1), kind=kLoop, calls=%fused_computation.15 | loop fusion | flops 262144 | bytes 393216 | tf_op jit(solution)/shard_map/mul | solution.py:345
  (36 shorter events, 0.2 us)
Async XLA Ops:
  0.6 21.1 %copy-start.1 = (bf16[128,4096]{1,0:T(8,128)(2,1)S(1)}, bf16[128,4096]{1,0:T(8,128)(2,1)}, u32[]{:S(2)}) copy-start(bf16[128,4096]{1,0:T(8,128)(2,1)} %g_hbm.3) | copy-start | bytes 3145732
  0.6 21.1 %copy-start = (bf16[128,4096]{1,0:T(8,128)(2,1)S(1)}, bf16[128,4096]{1,0:T(8,128)(2,1)}, u32[]{:S(2)}) copy-start(bf16[128,4096]{1,0:T(8,128)(2,1)} %q_hbm.3) | copy-start | bytes 3145732
  0.6 16.4 %collective-permute-start.3 = (bf16[1,16,1024]{2,1,0:T(8,128)(2,1)}, bf16[1,16,1024]{2,1,0:T(8,128)(2,1)S(1)}, u32[]{:S(2)}, u32[]{:S(2)}) collective-permute-start(bf16[1,16,1024]{2,1,0:T(8,128)(2,1)} %param.16), channel_id=1, source_target_pairs={{0,2},{1,3},{2,0},{3,1},{4,6},{5,7},{6,4},{7,5},{8,10},{9,11},{10,... | collective-permute-start | bytes 98312 | tf_op jit(solution)/shard_map/ppermute | solution.py:204
  4.8 12.3 %collective-permute-start.2 = (bf16[1,16,1024]{2,1,0:T(8,128)(2,1)}, bf16[1,16,1024]{2,1,0:T(8,128)(2,1)S(1)}, u32[]{:S(2)}, u32[]{:S(2)}) collective-permute-start(bf16[1,16,1024]{2,1,0:T(8,128)(2,1)} %param.16), channel_id=1, source_target_pairs={{0,1},{1,2},{2,3},{3,0},{4,5},{5,6},{6,7},{7,4},{8,9},{9,10},{10,1... | collective-permute-start | bytes 98312 | tf_op jit(solution)/shard_map/ppermute | solution.py:204
  6.3 10.7 %collective-permute-start.4 = (bf16[1,16,1024]{2,1,0:T(8,128)(2,1)}, bf16[1,16,1024]{2,1,0:T(8,128)(2,1)S(1)}, u32[]{:S(2)}, u32[]{:S(2)}) collective-permute-start(bf16[1,16,1024]{2,1,0:T(8,128)(2,1)} %param.16), channel_id=1, source_target_pairs={{0,3},{1,0},{2,1},{3,2},{4,7},{5,4},{6,5},{7,6},{8,11},{9,8},{10,9... | collective-permute-start | bytes 98312 | tf_op jit(solution)/shard_map/ppermute | solution.py:204
  10.4 11.1 %collective-permute-start.1 = (bf16[128,1024]{1,0:T(8,128)(2,1)S(1)}, bf16[128,1024]{1,0:T(8,128)(2,1)S(1)}, u32[]{:S(2)}, u32[]{:S(2)}) collective-permute-start(bf16[128,1024]{1,0:T(8,128)(2,1)S(1)} %constant_dynamic-update-slice_fusion.refs_3_), channel_id=1, source_target_pairs={{0,1},{1,2},{2,3},{4,5},{5,6},{6,7},{8,9},{9,10},{10,11},{12,13},{... | collective-permute-start | bytes 786440 | tf_op jit(solution)/shard_map/ppermute | solution.py:237
  12.1 9.3 %collective-permute-start = (bf16[64,1024]{1,0:T(8,128)(2,1)S(1)}, bf16[64,1024]{1,0:T(8,128)(2,1)S(1)}, u32[]{:S(2)}, u32[]{:S(2)}) collective-permute-start(bf16[64,1024]{1,0:T(8,128)(2,1)S(1)} %slice.60), channel_id=1, source_target_pairs={{0,2},{1,3},{4,6},{5,7},{8,10},{9,11},{12,14},{13,15},{16,18},{17,... | collective-permute-start | bytes 393224 | tf_op jit(solution)/shard_map/ppermute | solution.py:237
  17.8 7.1 %collective-permute-start.7 = (bf16[1,4,16,1024]{3,2,1,0:T(8,128)(2,1)S(1)}, bf16[1,4,16,1024]{3,2,1,0:T(8,128)(2,1)S(1)}, u32[]{:S(2)}, u32[]{:S(2)}) collective-permute-start(bf16[1,4,16,1024]{3,2,1,0:T(8,128)(2,1)S(1)} %maximum_bitcast_fusion), channel_id=1, source_target_pairs={{0,24},{4,28},{8,16},{12,20},{16,8},{20,12},{24,0},{28,4},{1,25},{... | collective-permute-start | bytes 393224 | tf_op jit(solution)/shard_map/ppermute | solution.py:212
  20.3 5.5 %collective-permute-start.6 = (bf16[1,4,16,1024]{3,2,1,0:T(8,128)(2,1)S(1)}, bf16[1,4,16,1024]{3,2,1,0:T(8,128)(2,1)S(1)}, u32[]{:S(2)}, u32[]{:S(2)}) collective-permute-start(bf16[1,4,16,1024]{3,2,1,0:T(8,128)(2,1)S(1)} %maximum_bitcast_fusion), channel_id=1, source_target_pairs={{0,16},{4,20},{8,24},{12,28},{16,0},{20,4},{24,8},{28,12},{1,17},{... | collective-permute-start | bytes 393224 | tf_op jit(solution)/shard_map/ppermute | solution.py:212
  20.9 5.0 %collective-permute-start.5 = (bf16[1,4,16,1024]{3,2,1,0:T(8,128)(2,1)S(1)}, bf16[1,4,16,1024]{3,2,1,0:T(8,128)(2,1)S(1)}, u32[]{:S(2)}, u32[]{:S(2)}) collective-permute-start(bf16[1,4,16,1024]{3,2,1,0:T(8,128)(2,1)S(1)} %maximum_bitcast_fusion), channel_id=1, source_target_pairs={{0,8},{4,12},{8,0},{12,4},{16,24},{20,28},{24,16},{28,20},{1,9},{5... | collective-permute-start | bytes 393224 | tf_op jit(solution)/shard_map/ppermute | solution.py:212
  21.8 4.2 %copy-start.3 = (bf16[128,16]{0,1:T(8,128)(2,1)S(1)}, bf16[128,16]{0,1:T(8,128)(2,1)}, u32[]{:S(2)}) copy-start(bf16[128,16]{0,1:T(8,128)(2,1)} %param.15) | copy-start | bytes 12292
  25.9 3.1 %collective-permute-start.8 = (bf16[4,4,16,1024]{3,2,1,0:T(8,128)(2,1)S(1)}, bf16[4,4,16,1024]{3,2,1,0:T(8,128)(2,1)S(1)}, u32[]{:S(2)}, u32[]{:S(2)}) collective-permute-start(bf16[4,4,16,1024]{3,2,1,0:T(8,128)(2,1)S(1)} %constant_dynamic-update-slice_fusion.2.refs_0_), channel_id=1, source_target_pairs={{0,4},{4,0},{8,12},{12,8},{16,20},{20,16},{24,28},{28,24},{1,5},{5... | collective-permute-start | bytes 1572872 | tf_op jit(solution)/shard_map/ppermute | solution.py:212
  26.0 4.0 %copy-start.2 = (bf16[128,8192]{1,0:T(8,128)(2,1)S(1)}, bf16[128,8192]{1,0:T(8,128)(2,1)}, u32[]{:S(2)}) copy-start(bf16[128,8192]{1,0:T(8,128)(2,1)} %x_ref.1) | copy-start | bytes 6291460
  29.0 2.1 %collective-permute-start.16 = (bf16[4,4,16,1024]{3,2,1,0:T(8,128)(2,1)S(1)}, bf16[4,4,16,1024]{3,2,1,0:T(8,128)(2,1)S(1)}, u32[]{:S(2)}, u32[]{:S(2)}) collective-permute-start(bf16[4,4,16,1024]{3,2,1,0:T(8,128)(2,1)S(1)} %get-tuple-element.45), channel_id=1, source_target_pairs={{0,4},{4,0},{8,12},{12,8},{16,20},{20,16},{24,28},{28,24},{1,5},{5... | collective-permute-start | bytes 1572872 | tf_op jit(solution)/shard_map/ppermute | solution.py:212
  30.7 4.2 %collective-permute-start.9 = (bf16[4,4,16,2048]{3,2,1,0:T(8,128)(2,1)S(1)}, bf16[4,4,16,2048]{3,2,1,0:T(8,128)(2,1)S(1)}, u32[]{:S(2)}, u32[]{:S(2)}) collective-permute-start(bf16[4,4,16,2048]{3,2,1,0:T(8,128)(2,1)S(1)} %get-tuple-element.39), channel_id=1, source_target_pairs={{0,4},{4,0},{8,12},{12,8},{16,20},{20,16},{24,28},{28,24},{1,5},{5... | collective-permute-start | bytes 3145736 | tf_op jit(solution)/shard_map/ppermute | solution.py:212
  31.3 6.8 %collective-permute-start.17 = (bf16[4,16,1024]{2,1,0:T(8,128)(2,1)S(1)}, bf16[4,16,1024]{2,1,0:T(8,128)(2,1)S(1)}, u32[]{:S(2)}, u32[]{:S(2)}) collective-permute-start(bf16[4,16,1024]{2,1,0:T(8,128)(2,1)S(1)} %get-tuple-element.46), channel_id=1, source_target_pairs={{0,1},{1,0},{2,3},{3,2},{4,5},{5,4},{6,7},{7,6},{8,9},{9,8},{10,11... | collective-permute-start | bytes 393224 | tf_op jit(solution)/shard_map/ppermute | solution.py:208
  31.4 10.1 %collective-permute-start.19 = (bf16[4,16,1024]{2,1,0:T(8,128)(2,1)S(1)}, bf16[4,16,1024]{2,1,0:T(8,128)(2,1)S(1)}, u32[]{:S(2)}, u32[]{:S(2)}) collective-permute-start(bf16[4,16,1024]{2,1,0:T(8,128)(2,1)S(1)} %get-tuple-element.47), channel_id=1, source_target_pairs={{0,3},{1,2},{2,1},{3,0},{4,7},{5,6},{6,5},{7,4},{8,11},{9,10},{10,... | collective-permute-start | bytes 393224 | tf_op jit(solution)/shard_map/ppermute | solution.py:208
  34.3 12.7 %collective-permute-start.18 = (bf16[4,16,1024]{2,1,0:T(8,128)(2,1)S(1)}, bf16[4,16,1024]{2,1,0:T(8,128)(2,1)S(1)}, u32[]{:S(2)}, u32[]{:S(2)}) collective-permute-start(bf16[4,16,1024]{2,1,0:T(8,128)(2,1)S(1)} %get-tuple-element.48), channel_id=1, source_target_pairs={{0,2},{1,3},{2,0},{3,1},{4,6},{5,7},{6,4},{7,5},{8,10},{9,11},{10,... | collective-permute-start | bytes 393224 | tf_op jit(solution)/shard_map/ppermute | solution.py:208
  35.1 15.0 %collective-permute-start.10 = (bf16[4,16,2048]{2,1,0:T(8,128)(2,1)S(1)}, bf16[4,16,2048]{2,1,0:T(8,128)(2,1)S(1)}, u32[]{:S(2)}, u32[]{:S(2)}) collective-permute-start(bf16[4,16,2048]{2,1,0:T(8,128)(2,1)S(1)} %get-tuple-element.41), channel_id=1, source_target_pairs={{0,8},{4,12},{8,0},{12,4},{16,24},{20,28},{24,16},{28,20},{1,9},{5... | collective-permute-start | bytes 786440 | tf_op jit(solution)/shard_map/ppermute | solution.py:212
  36.7 13.9 %collective-permute-start.11 = (bf16[4,16,2048]{2,1,0:T(8,128)(2,1)S(1)}, bf16[4,16,2048]{2,1,0:T(8,128)(2,1)S(1)}, u32[]{:S(2)}, u32[]{:S(2)}) collective-permute-start(bf16[4,16,2048]{2,1,0:T(8,128)(2,1)S(1)} %get-tuple-element.42), channel_id=1, source_target_pairs={{0,16},{4,20},{8,24},{12,28},{16,0},{20,4},{24,8},{28,12},{1,17},{... | collective-permute-start | bytes 786440 | tf_op jit(solution)/shard_map/ppermute | solution.py:212
  38.1 12.5 %collective-permute-start.12 = (bf16[4,16,2048]{2,1,0:T(8,128)(2,1)S(1)}, bf16[4,16,2048]{2,1,0:T(8,128)(2,1)S(1)}, u32[]{:S(2)}, u32[]{:S(2)}) collective-permute-start(bf16[4,16,2048]{2,1,0:T(8,128)(2,1)S(1)} %get-tuple-element.43), channel_id=1, source_target_pairs={{0,24},{4,28},{8,16},{12,20},{16,8},{20,12},{24,0},{28,4},{1,25},{... | collective-permute-start | bytes 786440 | tf_op jit(solution)/shard_map/ppermute | solution.py:212
  47.0 6.4 %collective-permute-start.20 = (bf16[16,1024]{1,0:T(8,128)(2,1)S(1)}, bf16[16,1024]{1,0:T(8,128)(2,1)S(1)}, u32[]{:S(2)}, u32[]{:S(2)}) collective-permute-start(bf16[16,1024]{1,0:T(8,128)(2,1)S(1)} %get-tuple-element.52), channel_id=1, source_target_pairs={{0,8},{4,12},{8,0},{12,4},{16,24},{20,28},{24,16},{28,20},{1,9},{5... | collective-permute-start | bytes 98312 | tf_op jit(solution)/shard_map/ppermute | solution.py:212
  48.6 6.6 %collective-permute-start.22 = (bf16[16,1024]{1,0:T(8,128)(2,1)S(1)}, bf16[16,1024]{1,0:T(8,128)(2,1)S(1)}, u32[]{:S(2)}, u32[]{:S(2)}) collective-permute-start(bf16[16,1024]{1,0:T(8,128)(2,1)S(1)} %get-tuple-element.53), channel_id=1, source_target_pairs={{0,24},{4,28},{8,16},{12,20},{16,8},{20,12},{24,0},{28,4},{1,25},{... | collective-permute-start | bytes 98312 | tf_op jit(solution)/shard_map/ppermute | solution.py:212
  50.1 5.2 %collective-permute-start.21 = (bf16[16,1024]{1,0:T(8,128)(2,1)S(1)}, bf16[16,1024]{1,0:T(8,128)(2,1)S(1)}, u32[]{:S(2)}, u32[]{:S(2)}) collective-permute-start(bf16[16,1024]{1,0:T(8,128)(2,1)S(1)} %get-tuple-element.54), channel_id=1, source_target_pairs={{0,16},{4,20},{8,24},{12,28},{16,0},{20,4},{24,8},{28,12},{1,17},{... | collective-permute-start | bytes 98312 | tf_op jit(solution)/shard_map/ppermute | solution.py:212
  50.8 6.7 %collective-permute-start.13 = (bf16[16,2048]{1,0:T(8,128)(2,1)S(1)}, bf16[16,2048]{1,0:T(8,128)(2,1)S(1)}, u32[]{:S(2)}, u32[]{:S(2)}) collective-permute-start(bf16[16,2048]{1,0:T(8,128)(2,1)S(1)} %get-tuple-element.49), channel_id=1, source_target_pairs={{0,3},{1,2},{2,1},{3,0},{4,7},{5,6},{6,5},{7,4},{8,11},{9,10},{10,... | collective-permute-start | bytes 196616 | tf_op jit(solution)/shard_map/ppermute | solution.py:208
  53.5 5.5 %collective-permute-start.15 = (bf16[16,2048]{1,0:T(8,128)(2,1)S(1)}, bf16[16,2048]{1,0:T(8,128)(2,1)S(1)}, u32[]{:S(2)}, u32[]{:S(2)}) collective-permute-start(bf16[16,2048]{1,0:T(8,128)(2,1)S(1)} %get-tuple-element.50), channel_id=1, source_target_pairs={{0,2},{1,3},{2,0},{3,1},{4,6},{5,7},{6,4},{7,5},{8,10},{9,11},{10,... | collective-permute-start | bytes 196616 | tf_op jit(solution)/shard_map/ppermute | solution.py:208
  53.5 5.5 %collective-permute-start.14 = (bf16[16,2048]{1,0:T(8,128)(2,1)S(1)}, bf16[16,2048]{1,0:T(8,128)(2,1)S(1)}, u32[]{:S(2)}, u32[]{:S(2)}) collective-permute-start(bf16[16,2048]{1,0:T(8,128)(2,1)S(1)} %get-tuple-element.51), channel_id=1, source_target_pairs={{0,1},{1,0},{2,3},{3,2},{4,5},{5,4},{6,7},{7,6},{8,9},{9,8},{10,11... | collective-permute-start | bytes 196616 | tf_op jit(solution)/shard_map/ppermute | solution.py:208

commit v15 on v14

--- a/solution.py
+++ b/solution.py
@@ -82,38 +82,39 @@
     scale = 1.0 / HEAD_SIZE**0.5
     to_log2 = scale * math.log2(math.e)
 
-    def one_group(kv, carry):
-        for copy in fetch(kv):
-            copy.wait()
-        at_kv = pl.ds(pl.multiple_of((first_kv + kv) * HEAD_SIZE, HEAD_SIZE), HEAD_SIZE)
-        k_g = k_all[:, at_kv]
-        v_g = v_all[:, at_kv]
-        kt_g = k_turned[at_kv, :]
-        def products(i):
-            first = (kv * GROUP + i) * HEAD_SIZE
-            at = [
-                pl.ds(pl.multiple_of(first + n * HEAD_SIZE, HEAD_SIZE), HEAD_SIZE) for n in range(2)
-            ]
-            q_two = jnp.concatenate([q_ref[:, at[0]], q_ref[:, at[1]]], axis=0)
-            g_two = jnp.concatenate([g_ref[:, at[0]], g_ref[:, at[1]]], axis=0)
-            s = dot(k_g, q_two, 1, 1) + jnp.concatenate([bias[...]] * 2, axis=1)
-            return at, s, dot(v_g, g_two, 1, 1)
-
-        ahead = products(0)
-        for i in range(0, GROUP, 2):
-            at, s, d_prob = ahead
-            if i + 2 < GROUP:
-                ahead = products(i + 2)
-            weights = jnp.exp2((s - jnp.max(s, axis=0, keepdims=True)) * to_log2)
-            inverse = 1.0 / jnp.sum(weights, axis=0, keepdims=True)
-            delta = jnp.sum(weights * d_prob, axis=0, keepdims=True) * inverse
-            dscore = (weights * (d_prob - delta)).astype(BF16)
-            dq = dot(kt_g, dscore, 1, 0) * (inverse * scale)
-            dq_turned[at[0], :] = dq[:, :tok].astype(BF16)
-            dq_turned[at[1], :] = dq[:, tok:].astype(BF16)
-        return carry
-
-    lax.fori_loop(0, n_kv, one_group, 0)
+    def products(kv, i):
+        if i == 0:
+            for copy in fetch(kv):
+                copy.wait()
+        at_kv = slice((first_kv + kv) * HEAD_SIZE, (first_kv + kv + 1) * HEAD_SIZE)
+        first = (kv * GROUP + i) * HEAD_SIZE
+        at = [slice(first + n * HEAD_SIZE, first + (n + 1) * HEAD_SIZE) for n in range(2)]
+        q_two = jnp.concatenate([q_ref[:, at[0]], q_ref[:, at[1]]], axis=0)
+        g_two = jnp.concatenate([g_ref[:, at[0]], g_ref[:, at[1]]], axis=0)
+        s = dot(k_all[:, at_kv], q_two, 1, 1) + jnp.concatenate([bias[...]] * 2, axis=1)
+        return at, at_kv, s, dot(v_all[:, at_kv], g_two, 1, 1)
+
+    def softmax(at, at_kv, s, d_prob):
+        weights = jnp.exp2((s - jnp.max(s, axis=0, keepdims=True)) * to_log2)
+        inverse = 1.0 / jnp.sum(weights, axis=0, keepdims=True)
+        delta = jnp.sum(weights * d_prob, axis=0, keepdims=True) * inverse
+        return at, at_kv, (weights * (d_prob - delta)).astype(BF16), inverse * scale
+
+    def finish(at, at_kv, dscore, factor):
+        dq = dot(k_turned[at_kv, :], dscore, 1, 0) * factor
+        dq_turned[at[0], :] = dq[:, :tok].astype(BF16)
+        dq_turned[at[1], :] = dq[:, tok:].astype(BF16)
+
+    pairs = [(kv, i) for kv in range(n_kv) for i in range(0, GROUP, 2)]
+    ahead, behind = products(*pairs[0]), None
+    for n in range(len(pairs)):
+        now = ahead
+        if n + 1 < len(pairs):
+            ahead = products(*pairs[n + 1])
+        if behind is not None:
+            finish(*behind)
+        behind = softmax(*now)
+    finish(*behind)
     if not up_refs:
         return
 

time: 60 us -> 59.2 us (0.987)
  Pallas kernels: 7.21 us -> 6.36 us
    pallas_call x2, Pallas kernels: 5.56 us -> 4.7 us  [attention(): pl.pallas_call(functools.partial(attention_kernel, by_slot, h * n_kv, n_k...]
  transfers between devices with their start and end apart: 23 -> 23, of which waited for: 7 -> 7; matrix products, arithmetic and copies ran while one was open for 10% -> 10% of each run, Pallas kernels for 12% -> 11%
where the time goes in v15:
time: 59.2 us; the launch traced here: 58.9 us
  starting transfers between devices  31.8 us (54%)
  waiting for transfers between devices  13.1 us (22%)
  Pallas kernels  6.36 us (11%)
  other arithmetic  3.72 us (6%)
  local copies, waits for them, and re-layouts  2.98 us (5%)
  between operations  0.96 us (2%)
    ppermute x12, starting transfers between devices, partnered(): return lax.ppermute(x, 'seq', [(i, i ^ bits) for i in range(n_seq)])  11.5 us
    ppermute x6, waiting for transfers between devices, across(): return lax.ppermute(x, 'head', [(i, i ^ j) for i in range(n_head)])  11 us
    ppermute x6, starting transfers between devices, across(): return lax.ppermute(x, 'head', [(i, i ^ j) for i in range(n_head)])  8.01 us
    ppermute x3, starting transfers between devices, shifted(): lax.ppermute(x, 'head', [(i, (i + j) % n_head) for i in range(n_head)])  7.93 us
    pallas_call x2, Pallas kernels, attention(): pl.pallas_call(functools.partial(attention_kernel, by_slot, h * n_kv, n_k...  4.7 us
    ppermute x2, starting transfers between devices, on_device(): parts.insert(0, lax.ppermute(own[tok - rows:], 'head', shift))  4.39 us
    ppermute x12, waiting for transfers between devices, partnered(): return lax.ppermute(x, 'seq', [(i, i ^ bits) for i in range(n_seq)])  2.1 us
    unnamed x13, local copies, waits for them, and re-layouts  1.99 us
  transfers between devices with their start and end apart: 23, of which 7 were waited for; matrix products, arithmetic and copies ran while one was open for 10% of the time, Pallas kernels for 11%

profile of v15, /device:TPU:0, one launch (start us, length us, event | category | flops | bytes accessed | tf_op | source)
XLA Modules:
  0.0 58.9 jit_solution(3251261882451384022)
XLA Ops:
  0.6 4.1 %collective-permute-start.3 = (bf16[1,16,1024]{2,1,0:T(8,128)(2,1)}, bf16[1,16,1024]{2,1,0:T(8,128)(2,1)S(1)}, u32[]{:S(2)}, u32[]{:S(2)}) collective-permute-start(bf16[1,16,1024]{2,1,0:T(8,128)(2,1)} %param.16), channel_id=1, source_target_pairs={{0,2},{1,3},{2,0},{3,1},{4,6},{5,7},{6,4},{7,5},{8,10},{9,11},{10,... | collective-permute-start | bytes 98312 | tf_op jit(solution)/shard_map/ppermute | solution.py:205
  4.8 1.6 %collective-permute-start.2 = (bf16[1,16,1024]{2,1,0:T(8,128)(2,1)}, bf16[1,16,1024]{2,1,0:T(8,128)(2,1)S(1)}, u32[]{:S(2)}, u32[]{:S(2)}) collective-permute-start(bf16[1,16,1024]{2,1,0:T(8,128)(2,1)} %param.16), channel_id=1, source_target_pairs={{0,1},{1,2},{2,3},{3,0},{4,5},{5,6},{6,7},{7,4},{8,9},{9,10},{10,1... | collective-permute-start | bytes 98312 | tf_op jit(solution)/shard_map/ppermute | solution.py:205
  6.3 2.2 %collective-permute-start.4 = (bf16[1,16,1024]{2,1,0:T(8,128)(2,1)}, bf16[1,16,1024]{2,1,0:T(8,128)(2,1)S(1)}, u32[]{:S(2)}, u32[]{:S(2)}) collective-permute-start(bf16[1,16,1024]{2,1,0:T(8,128)(2,1)} %param.16), channel_id=1, source_target_pairs={{0,3},{1,0},{2,1},{3,2},{4,7},{5,4},{6,5},{7,6},{8,11},{9,8},{10,9... | collective-permute-start | bytes 98312 | tf_op jit(solution)/shard_map/ppermute | solution.py:205
  8.6 0.9 %constant_dynamic-update-slice_fusion.1 = bf16[128,1024]{1,0:T(8,128)(2,1)S(1)} fusion(bf16[128,512]{1,0:T(8,128)(2,1)} %param.11), kind=kLoop, calls=%fused_computation.39 | loop fusion | bytes 262144
  9.5 0.9 %constant_dynamic-update-slice_fusion.refs_3_ = bf16[128,1024]{1,0:T(8,128)(2,1)S(1)} fusion(bf16[128,1024]{1,0:T(8,128)(2,1)S(1)} %constant_dynamic-update-slice_fusion.1, bf16[128,512]{1,0:T(8,128)(2,1)} %param.12), kind=kLoop, calls=%fused_computation.38 | loop fusion | bytes 262144 | tf_op jit(solution)/shard_map/concatenate | solution.py:234
  10.4 1.7 %collective-permute-start.1 = (bf16[128,1024]{1,0:T(8,128)(2,1)S(1)}, bf16[128,1024]{1,0:T(8,128)(2,1)S(1)}, u32[]{:S(2)}, u32[]{:S(2)}) collective-permute-start(bf16[128,1024]{1,0:T(8,128)(2,1)S(1)} %constant_dynamic-update-slice_fusion.refs_3_), channel_id=1, source_target_pairs={{0,1},{1,2},{2,3},{4,5},{5,6},{6,7},{8,9},{9,10},{10,11},{12,13},{... | collective-permute-start | bytes 786440 | tf_op jit(solution)/shard_map/ppermute | solution.py:238
  12.1 2.7 %collective-permute-start = (bf16[64,1024]{1,0:T(8,128)(2,1)S(1)}, bf16[64,1024]{1,0:T(8,128)(2,1)S(1)}, u32[]{:S(2)}, u32[]{:S(2)}) collective-permute-start(bf16[64,1024]{1,0:T(8,128)(2,1)S(1)} %slice.60), channel_id=1, source_target_pairs={{0,2},{1,3},{4,6},{5,7},{8,10},{9,11},{12,14},{13,15},{16,18},{17,... | collective-permute-start | bytes 393224 | tf_op jit(solution)/shard_map/ppermute | solution.py:238
  14.9 1.0 %select_reduce_fusion.1 = s32[8,8]{1,0:T(8,128)S(1)} fusion(s32[8]{0:T(128)} %param.19, s32[8]{0:T(128)} %bitcast.51, s32[8]{0:T(128)} %bitcast.52, pred[8]{0:T(512)(128)(4,1)S(1)} %get-tuple-element.57, pred[8]{0:T(512)(128)(4,1)S(1)} %get-tuple-element.58, pred[8]{0:T(512)(128)(4,1)S(1)} %get-tuple-element.59, pred[8]{0:T(512)(128)(4,1)S(1)} %get-tuple-element.60), kind=kLoop, calls=%fused_computation.30 | loop fusion | flops 6592 | bytes 384 | tf_op jit(solution)/shard_map/reduce_sum | solution.py:198
  15.9 0.1 compare_and_fusion
  16.0 1.0 %copy.13 = bf16[128,512]{0,1:T(8,128)(2,1)S(1)} copy(bf16[128,512]{1,0:T(8,128)(2,1)} %param.11) | data formatting | bytes 262144 | tf_op args[1]
  17.0 0.8 %maximum_bitcast_fusion = bf16[1,4,16,1024]{3,2,1,0:T(8,128)(2,1)S(1)} fusion(bf16[1,16,1024]{2,1,0:T(8,128)(2,1)S(1)} %collective-permute-done.4, bf16[1,16,1024]{2,1,0:T(8,128)(2,1)S(1)} %collective-permute-done.3, bf16[1,16,1024]{2,1,0:T(8,128)(2,1)S(1)} %collective-permute-done.2, bf16[1,16,1024]{2,1,0:T(8,128)(2,1)} %param.16), kind=kLoop, calls=%fused_computation.10 | loop fusion | flops 196608 | bytes 262144 | tf_op jit(solution)/shard_map/broadcast_in_dim | solution.py:242
  17.8 2.5 %collective-permute-start.7 = (bf16[1,4,16,1024]{3,2,1,0:T(8,128)(2,1)S(1)}, bf16[1,4,16,1024]{3,2,1,0:T(8,128)(2,1)S(1)}, u32[]{:S(2)}, u32[]{:S(2)}) collective-permute-start(bf16[1,4,16,1024]{3,2,1,0:T(8,128)(2,1)S(1)} %maximum_bitcast_fusion), channel_id=1, source_target_pairs={{0,24},{4,28},{8,16},{12,20},{16,8},{20,12},{24,0},{28,4},{1,25},{... | collective-permute-start | bytes 393224 | tf_op jit(solution)/shard_map/ppermute | solution.py:213
  20.3 0.5 collective-permute-start.6
  20.9 0.5 collective-permute-start.5
  21.4 0.1 select_reduce_fusion.facts_ref.refs_0_
  21.5 0.3 layout.1
  21.8 2.2 %attention_0.1.refs_2_ = bf16[2048,128]{1,0:T(8,128)(2,1)S(1)} custom-call(bf16[320,512]{1,0:T(8,128)(2,1)S(1)} %get-tuple-element.24.k_all, bf16[320,512]{1,0:T(8,128)(2,1)S(1)} %get-tuple-element.25.v_all, bf16[512,320]{1,0:T(8,128)(2,1)S(1)} %get-tuple-element.26.k_turned, f32[320,128]{1,0:T(8,128)S(1)} %get-tuple-element.27.bias, ...), custom_call_target="tpu_custom_call" | custom-call | flops 503316480 | bytes 2097152 | tf_op jit(solution)/shard_map/attention_0/pallas_call | solution.py:275
  24.0 1.0 %collective-permute-done.7 = bf16[1,4,16,1024]{3,2,1,0:T(8,128)(2,1)S(1)} collective-permute-done((bf16[1,4,16,1024]{3,2,1,0:T(8,128)(2,1)S(1)}, bf16[1,4,16,1024]{3,2,1,0:T(8,128)(2,1)S(1)}, u32[]{:S(2)}, u32[]{:S(2)}) %collective-permute-start.7) | collective-permute-done | bytes 131104 | tf_op jit(solution)/shard_map/ppermute | solution.py:213
  25.0 0.9 %collective-permute-done.6 = bf16[1,4,16,1024]{3,2,1,0:T(8,128)(2,1)S(1)} collective-permute-done((bf16[1,4,16,1024]{3,2,1,0:T(8,128)(2,1)S(1)}, bf16[1,4,16,1024]{3,2,1,0:T(8,128)(2,1)S(1)}, u32[]{:S(2)}, u32[]{:S(2)}) %collective-permute-start.6) | collective-permute-done | bytes 131104 | tf_op jit(solution)/shard_map/ppermute | solution.py:213
  25.9 0.1 collective-permute-start.8
  26.0 2.5 %attention_1.1 = (bf16[2048,128]{1,0:T(8,128)(2,1)S(1)}, bf16[4,4,16,1024]{3,2,1,0:T(8,128)(2,1)S(1)}, bf16[4,4,16,1024]{3,2,1,0:T(8,128)(2,1)S(1)}) custom-call(bf16[320,512]{1,0:T(8,128)(2,1)S(1)} %get-tuple-element.24.k_all, bf16[320,512]{1,0:T(8,128)(2,1)S(1)} %get-tuple-element.25.v_all, bf16[512,320]{1,0:T(8,128)(2,1)S(1)} %get-tuple-element.26.k_turned, ...), custom_call_target="tpu_custom_call" | custom-call | flops 503316480 | bytes 2097152 | tf_op jit(solution)/shard_map/attention_1/pallas_call | solution.py:275
  28.5 0.5 collective-permute-start.16
  29.1 0.4 rank_gradient.1.rank_ref
  29.5 0.7 %down_parts.1 = (bf16[4,4,16,2048]{3,2,1,0:T(8,128)(2,1)S(1)}, bf16[4,4,16,2048]{3,2,1,0:T(8,128)(2,1)S(1)}) custom-call(s32[8,128]{1,0:T(8,128)S(1)} %select_reduce_fusion.facts_ref.refs_0_, bf16[128,8192]{1,0:T(8,128)(2,1)S(1)} %copy-done.2, bf16[16,128]{1,0:T(8,128)(2,1)S(1)} %rank_gradient.1.rank_ref), custom_call_target="tpu_custom_call" | custom-call | flops 268435456 | bytes 8388608 | tf_op jit(solution)/shard_map/down_parts/pallas_call | solution.py:315
  30.2 0.1 collective-permute-start.9
  30.3 0.2 collective-permute-done.16
  30.6 0.2 add_convert_fusion
  30.8 0.1 collective-permute-start.17
  30.9 2.5 %collective-permute-start.19 = (bf16[4,16,1024]{2,1,0:T(8,128)(2,1)S(1)}, bf16[4,16,1024]{2,1,0:T(8,128)(2,1)S(1)}, u32[]{:S(2)}, u32[]{:S(2)}) collective-permute-start(bf16[4,16,1024]{2,1,0:T(8,128)(2,1)S(1)} %get-tuple-element.47), channel_id=1, source_target_pairs={{0,3},{1,2},{2,1},{3,0},{4,7},{5,6},{6,5},{7,4},{8,11},{9,10},{10,... | collective-permute-start | bytes 393224 | tf_op jit(solution)/shard_map/ppermute | solution.py:209
  33.4 1.0 %collective-permute-start.18 = (bf16[4,16,1024]{2,1,0:T(8,128)(2,1)S(1)}, bf16[4,16,1024]{2,1,0:T(8,128)(2,1)S(1)}, u32[]{:S(2)}, u32[]{:S(2)}) collective-permute-start(bf16[4,16,1024]{2,1,0:T(8,128)(2,1)S(1)} %get-tuple-element.48), channel_id=1, source_target_pairs={{0,2},{1,3},{2,0},{3,1},{4,6},{5,7},{6,4},{7,5},{8,10},{9,11},{10,... | collective-permute-start | bytes 393224 | tf_op jit(solution)/shard_map/ppermute | solution.py:209
  34.4 0.2 core_sum.1
  34.6 1.5 %collective-permute-start.10 = (bf16[4,16,2048]{2,1,0:T(8,128)(2,1)S(1)}, bf16[4,16,2048]{2,1,0:T(8,128)(2,1)S(1)}, u32[]{:S(2)}, u32[]{:S(2)}) collective-permute-start(bf16[4,16,2048]{2,1,0:T(8,128)(2,1)S(1)} %get-tuple-element.41), channel_id=1, source_target_pairs={{0,8},{4,12},{8,0},{12,4},{16,24},{20,28},{24,16},{28,20},{1,9},{5... | collective-permute-start | bytes 786440 | tf_op jit(solution)/shard_map/ppermute | solution.py:213
  36.2 1.1 %collective-permute-start.11 = (bf16[4,16,2048]{2,1,0:T(8,128)(2,1)S(1)}, bf16[4,16,2048]{2,1,0:T(8,128)(2,1)S(1)}, u32[]{:S(2)}, u32[]{:S(2)}) collective-permute-start(bf16[4,16,2048]{2,1,0:T(8,128)(2,1)S(1)} %get-tuple-element.42), channel_id=1, source_target_pairs={{0,16},{4,20},{8,24},{12,28},{16,0},{20,4},{24,8},{28,12},{1,17},{... | collective-permute-start | bytes 786440 | tf_op jit(solution)/shard_map/ppermute | solution.py:213
  37.3 1.0 %collective-permute-start.12 = (bf16[4,16,2048]{2,1,0:T(8,128)(2,1)S(1)}, bf16[4,16,2048]{2,1,0:T(8,128)(2,1)S(1)}, u32[]{:S(2)}, u32[]{:S(2)}) collective-permute-start(bf16[4,16,2048]{2,1,0:T(8,128)(2,1)S(1)} %get-tuple-element.43), channel_id=1, source_target_pairs={{0,24},{4,28},{8,16},{12,20},{16,8},{20,12},{24,0},{28,4},{1,25},{... | collective-permute-start | bytes 786440 | tf_op jit(solution)/shard_map/ppermute | solution.py:213
  38.3 2.3 %collective-permute-done.19 = bf16[4,16,1024]{2,1,0:T(8,128)(2,1)S(1)} collective-permute-done((bf16[4,16,1024]{2,1,0:T(8,128)(2,1)S(1)}, bf16[4,16,1024]{2,1,0:T(8,128)(2,1)S(1)}, u32[]{:S(2)}, u32[]{:S(2)}) %collective-permute-start.19) | collective-permute-done | bytes 131104 | tf_op jit(solution)/shard_map/ppermute | solution.py:209
  40.6 5.7 %collective-permute-done.18 = bf16[4,16,1024]{2,1,0:T(8,128)(2,1)S(1)} collective-permute-done((bf16[4,16,1024]{2,1,0:T(8,128)(2,1)S(1)}, bf16[4,16,1024]{2,1,0:T(8,128)(2,1)S(1)}, u32[]{:S(2)}, u32[]{:S(2)}) %collective-permute-start.18) | collective-permute-done | bytes 131104 | tf_op jit(solution)/shard_map/ppermute | solution.py:209
  46.3 0.1 fusion.2
  46.4 1.5 %collective-permute-start.20 = (bf16[16,1024]{1,0:T(8,128)(2,1)S(1)}, bf16[16,1024]{1,0:T(8,128)(2,1)S(1)}, u32[]{:S(2)}, u32[]{:S(2)}) collective-permute-start(bf16[16,1024]{1,0:T(8,128)(2,1)S(1)} %get-tuple-element.52), channel_id=1, source_target_pairs={{0,8},{4,12},{8,0},{12,4},{16,24},{20,28},{24,16},{28,20},{1,9},{5... | collective-permute-start | bytes 98312 | tf_op jit(solution)/shard_map/ppermute | solution.py:213
  47.9 1.5 %collective-permute-start.22 = (bf16[16,1024]{1,0:T(8,128)(2,1)S(1)}, bf16[16,1024]{1,0:T(8,128)(2,1)S(1)}, u32[]{:S(2)}, u32[]{:S(2)}) collective-permute-start(bf16[16,1024]{1,0:T(8,128)(2,1)S(1)} %get-tuple-element.53), channel_id=1, source_target_pairs={{0,24},{4,28},{8,16},{12,20},{16,8},{20,12},{24,0},{28,4},{1,25},{... | collective-permute-start | bytes 98312 | tf_op jit(solution)/shard_map/ppermute | solution.py:213
  49.4 0.5 collective-permute-start.21
  49.9 0.1 add_convert_fusion.1
  50.1 2.5 %collective-permute-start.13 = (bf16[16,2048]{1,0:T(8,128)(2,1)S(1)}, bf16[16,2048]{1,0:T(8,128)(2,1)S(1)}, u32[]{:S(2)}, u32[]{:S(2)}) collective-permute-start(bf16[16,2048]{1,0:T(8,128)(2,1)S(1)} %get-tuple-element.49), channel_id=1, source_target_pairs={{0,3},{1,2},{2,1},{3,0},{4,7},{5,6},{6,5},{7,4},{8,11},{9,10},{10,... | collective-permute-start | bytes 196616 | tf_op jit(solution)/shard_map/ppermute | solution.py:209
  52.6 0.1 collective-permute-start.15
  52.7 1.8 %collective-permute-start.14 = (bf16[16,2048]{1,0:T(8,128)(2,1)S(1)}, bf16[16,2048]{1,0:T(8,128)(2,1)S(1)}, u32[]{:S(2)}, u32[]{:S(2)}) collective-permute-start(bf16[16,2048]{1,0:T(8,128)(2,1)S(1)} %get-tuple-element.51), channel_id=1, source_target_pairs={{0,1},{1,0},{2,3},{3,2},{4,5},{5,4},{6,7},{7,6},{8,9},{9,8},{10,11... | collective-permute-start | bytes 196616 | tf_op jit(solution)/shard_map/ppermute | solution.py:209
  54.6 0.7 %fusion.10 = f32[1,16,1024]{2,1,0:T(8,128)} fusion(bf16[16,1024]{1,0:T(8,128)(2,1)S(1)} %collective-permute-done.22, bf16[16,1024]{1,0:T(8,128)(2,1)S(1)} %collective-permute-done.21, bf16[16,1024]{1,0:T(8,128)(2,1)S(1)} %collective-permute-done.20, bf16[4,16,1024]{2,1,0:T(8,128)(2,1)S(1)} %fusion.2), kind=kLoop, calls=%fused_computation.24 | loop fusion | flops 131072 | bytes 196608 | tf_op jit(solution)/shard_map/mul | solution.py:346
  55.2 1.7 %collective-permute-done.13 = bf16[16,2048]{1,0:T(8,128)(2,1)S(1)} collective-permute-done((bf16[16,2048]{1,0:T(8,128)(2,1)S(1)}, bf16[16,2048]{1,0:T(8,128)(2,1)S(1)}, u32[]{:S(2)}, u32[]{:S(2)}) %collective-permute-start.13) | collective-permute-done | bytes 65568 | tf_op jit(solution)/shard_map/ppermute | solution.py:209
  56.9 1.3 %collective-permute-done.15 = bf16[16,2048]{1,0:T(8,128)(2,1)S(1)} collective-permute-done((bf16[16,2048]{1,0:T(8,128)(2,1)S(1)}, bf16[16,2048]{1,0:T(8,128)(2,1)S(1)}, u32[]{:S(2)}, u32[]{:S(2)}) %collective-permute-start.15) | collective-permute-done | bytes 65568 | tf_op jit(solution)/shard_map/ppermute | solution.py:209
  58.2 0.7 %fusion.6 = f32[1,2048,16]{1,2,0:T(8,128)} fusion(bf16[16,2048]{1,0:T(8,128)(2,1)S(1)} %collective-permute-done.15, bf16[16,2048]{1,0:T(8,128)(2,1)S(1)} %collective-permute-done.14, bf16[16,2048]{1,0:T(8,128)(2,1)S(1)} %collective-permute-done.13, bf16[4,16,2048]{2,1,0:T(8,128)(2,1)S(1)} %add_convert_fusion.1), kind=kLoop, calls=%fused_computation.15 | loop fusion | flops 262144 | bytes 393216 | tf_op jit(solution)/shard_map/mul | solution.py:346
  (36 shorter events, 0.2 us)
Async XLA Ops:
  0.6 21.1 %copy-start.1 = (bf16[128,4096]{1,0:T(8,128)(2,1)S(1)}, bf16[128,4096]{1,0:T(8,128)(2,1)}, u32[]{:S(2)}) copy-start(bf16[128,4096]{1,0:T(8,128)(2,1)} %g_hbm.3) | copy-start | bytes 3145732
  0.6 21.1 %copy-start = (bf16[128,4096]{1,0:T(8,128)(2,1)S(1)}, bf16[128,4096]{1,0:T(8,128)(2,1)}, u32[]{:S(2)}) copy-start(bf16[128,4096]{1,0:T(8,128)(2,1)} %q_hbm.3) | copy-start | bytes 3145732
  0.6 16.4 %collective-permute-start.3 = (bf16[1,16,1024]{2,1,0:T(8,128)(2,1)}, bf16[1,16,1024]{2,1,0:T(8,128)(2,1)S(1)}, u32[]{:S(2)}, u32[]{:S(2)}) collective-permute-start(bf16[1,16,1024]{2,1,0:T(8,128)(2,1)} %param.16), channel_id=1, source_target_pairs={{0,2},{1,3},{2,0},{3,1},{4,6},{5,7},{6,4},{7,5},{8,10},{9,11},{10,... | collective-permute-start | bytes 98312 | tf_op jit(solution)/shard_map/ppermute | solution.py:205
  4.8 12.3 %collective-permute-start.2 = (bf16[1,16,1024]{2,1,0:T(8,128)(2,1)}, bf16[1,16,1024]{2,1,0:T(8,128)(2,1)S(1)}, u32[]{:S(2)}, u32[]{:S(2)}) collective-permute-start(bf16[1,16,1024]{2,1,0:T(8,128)(2,1)} %param.16), channel_id=1, source_target_pairs={{0,1},{1,2},{2,3},{3,0},{4,5},{5,6},{6,7},{7,4},{8,9},{9,10},{10,1... | collective-permute-start | bytes 98312 | tf_op jit(solution)/shard_map/ppermute | solution.py:205
  6.3 10.7 %collective-permute-start.4 = (bf16[1,16,1024]{2,1,0:T(8,128)(2,1)}, bf16[1,16,1024]{2,1,0:T(8,128)(2,1)S(1)}, u32[]{:S(2)}, u32[]{:S(2)}) collective-permute-start(bf16[1,16,1024]{2,1,0:T(8,128)(2,1)} %param.16), channel_id=1, source_target_pairs={{0,3},{1,0},{2,1},{3,2},{4,7},{5,4},{6,5},{7,6},{8,11},{9,8},{10,9... | collective-permute-start | bytes 98312 | tf_op jit(solution)/shard_map/ppermute | solution.py:205
  10.4 11.1 %collective-permute-start.1 = (bf16[128,1024]{1,0:T(8,128)(2,1)S(1)}, bf16[128,1024]{1,0:T(8,128)(2,1)S(1)}, u32[]{:S(2)}, u32[]{:S(2)}) collective-permute-start(bf16[128,1024]{1,0:T(8,128)(2,1)S(1)} %constant_dynamic-update-slice_fusion.refs_3_), channel_id=1, source_target_pairs={{0,1},{1,2},{2,3},{4,5},{5,6},{6,7},{8,9},{9,10},{10,11},{12,13},{... | collective-permute-start | bytes 786440 | tf_op jit(solution)/shard_map/ppermute | solution.py:238
  12.1 9.3 %collective-permute-start = (bf16[64,1024]{1,0:T(8,128)(2,1)S(1)}, bf16[64,1024]{1,0:T(8,128)(2,1)S(1)}, u32[]{:S(2)}, u32[]{:S(2)}) collective-permute-start(bf16[64,1024]{1,0:T(8,128)(2,1)S(1)} %slice.60), channel_id=1, source_target_pairs={{0,2},{1,3},{4,6},{5,7},{8,10},{9,11},{12,14},{13,15},{16,18},{17,... | collective-permute-start | bytes 393224 | tf_op jit(solution)/shard_map/ppermute | solution.py:238
  17.8 7.1 %collective-permute-start.7 = (bf16[1,4,16,1024]{3,2,1,0:T(8,128)(2,1)S(1)}, bf16[1,4,16,1024]{3,2,1,0:T(8,128)(2,1)S(1)}, u32[]{:S(2)}, u32[]{:S(2)}) collective-permute-start(bf16[1,4,16,1024]{3,2,1,0:T(8,128)(2,1)S(1)} %maximum_bitcast_fusion), channel_id=1, source_target_pairs={{0,24},{4,28},{8,16},{12,20},{16,8},{20,12},{24,0},{28,4},{1,25},{... | collective-permute-start | bytes 393224 | tf_op jit(solution)/shard_map/ppermute | solution.py:213
  20.3 5.5 %collective-permute-start.6 = (bf16[1,4,16,1024]{3,2,1,0:T(8,128)(2,1)S(1)}, bf16[1,4,16,1024]{3,2,1,0:T(8,128)(2,1)S(1)}, u32[]{:S(2)}, u32[]{:S(2)}) collective-permute-start(bf16[1,4,16,1024]{3,2,1,0:T(8,128)(2,1)S(1)} %maximum_bitcast_fusion), channel_id=1, source_target_pairs={{0,16},{4,20},{8,24},{12,28},{16,0},{20,4},{24,8},{28,12},{1,17},{... | collective-permute-start | bytes 393224 | tf_op jit(solution)/shard_map/ppermute | solution.py:213
  20.9 5.0 %collective-permute-start.5 = (bf16[1,4,16,1024]{3,2,1,0:T(8,128)(2,1)S(1)}, bf16[1,4,16,1024]{3,2,1,0:T(8,128)(2,1)S(1)}, u32[]{:S(2)}, u32[]{:S(2)}) collective-permute-start(bf16[1,4,16,1024]{3,2,1,0:T(8,128)(2,1)S(1)} %maximum_bitcast_fusion), channel_id=1, source_target_pairs={{0,8},{4,12},{8,0},{12,4},{16,24},{20,28},{24,16},{28,20},{1,9},{5... | collective-permute-start | bytes 393224 | tf_op jit(solution)/shard_map/ppermute | solution.py:213
  21.8 4.2 %copy-start.3 = (bf16[128,16]{0,1:T(8,128)(2,1)S(1)}, bf16[128,16]{0,1:T(8,128)(2,1)}, u32[]{:S(2)}) copy-start(bf16[128,16]{0,1:T(8,128)(2,1)} %param.15) | copy-start | bytes 12292
  25.9 2.6 %collective-permute-start.8 = (bf16[4,4,16,1024]{3,2,1,0:T(8,128)(2,1)S(1)}, bf16[4,4,16,1024]{3,2,1,0:T(8,128)(2,1)S(1)}, u32[]{:S(2)}, u32[]{:S(2)}) collective-permute-start(bf16[4,4,16,1024]{3,2,1,0:T(8,128)(2,1)S(1)} %constant_dynamic-update-slice_fusion.2.refs_0_), channel_id=1, source_target_pairs={{0,4},{4,0},{8,12},{12,8},{16,20},{20,16},{24,28},{28,24},{1,5},{5... | collective-permute-start | bytes 1572872 | tf_op jit(solution)/shard_map/ppermute | solution.py:213
  26.0 3.5 %copy-start.2 = (bf16[128,8192]{1,0:T(8,128)(2,1)S(1)}, bf16[128,8192]{1,0:T(8,128)(2,1)}, u32[]{:S(2)}) copy-start(bf16[128,8192]{1,0:T(8,128)(2,1)} %x_ref.1) | copy-start | bytes 6291460
  28.5 2.1 %collective-permute-start.16 = (bf16[4,4,16,1024]{3,2,1,0:T(8,128)(2,1)S(1)}, bf16[4,4,16,1024]{3,2,1,0:T(8,128)(2,1)S(1)}, u32[]{:S(2)}, u32[]{:S(2)}) collective-permute-start(bf16[4,4,16,1024]{3,2,1,0:T(8,128)(2,1)S(1)} %get-tuple-element.45), channel_id=1, source_target_pairs={{0,4},{4,0},{8,12},{12,8},{16,20},{20,16},{24,28},{28,24},{1,5},{5... | collective-permute-start | bytes 1572872 | tf_op jit(solution)/shard_map/ppermute | solution.py:213
  30.2 4.2 %collective-permute-start.9 = (bf16[4,4,16,2048]{3,2,1,0:T(8,128)(2,1)S(1)}, bf16[4,4,16,2048]{3,2,1,0:T(8,128)(2,1)S(1)}, u32[]{:S(2)}, u32[]{:S(2)}) collective-permute-start(bf16[4,4,16,2048]{3,2,1,0:T(8,128)(2,1)S(1)} %get-tuple-element.39), channel_id=1, source_target_pairs={{0,4},{4,0},{8,12},{12,8},{16,20},{20,16},{24,28},{28,24},{1,5},{5... | collective-permute-start | bytes 3145736 | tf_op jit(solution)/shard_map/ppermute | solution.py:213
  30.8 6.4 %collective-permute-start.17 = (bf16[4,16,1024]{2,1,0:T(8,128)(2,1)S(1)}, bf16[4,16,1024]{2,1,0:T(8,128)(2,1)S(1)}, u32[]{:S(2)}, u32[]{:S(2)}) collective-permute-start(bf16[4,16,1024]{2,1,0:T(8,128)(2,1)S(1)} %get-tuple-element.46), channel_id=1, source_target_pairs={{0,1},{1,0},{2,3},{3,2},{4,5},{5,4},{6,7},{7,6},{8,9},{9,8},{10,11... | collective-permute-start | bytes 393224 | tf_op jit(solution)/shard_map/ppermute | solution.py:209
  30.9 9.7 %collective-permute-start.19 = (bf16[4,16,1024]{2,1,0:T(8,128)(2,1)S(1)}, bf16[4,16,1024]{2,1,0:T(8,128)(2,1)S(1)}, u32[]{:S(2)}, u32[]{:S(2)}) collective-permute-start(bf16[4,16,1024]{2,1,0:T(8,128)(2,1)S(1)} %get-tuple-element.47), channel_id=1, source_target_pairs={{0,3},{1,2},{2,1},{3,0},{4,7},{5,6},{6,5},{7,4},{8,11},{9,10},{10,... | collective-permute-start | bytes 393224 | tf_op jit(solution)/shard_map/ppermute | solution.py:209
  33.4 12.8 %collective-permute-start.18 = (bf16[4,16,1024]{2,1,0:T(8,128)(2,1)S(1)}, bf16[4,16,1024]{2,1,0:T(8,128)(2,1)S(1)}, u32[]{:S(2)}, u32[]{:S(2)}) collective-permute-start(bf16[4,16,1024]{2,1,0:T(8,128)(2,1)S(1)} %get-tuple-element.48), channel_id=1, source_target_pairs={{0,2},{1,3},{2,0},{3,1},{4,6},{5,7},{6,4},{7,5},{8,10},{9,11},{10,... | collective-permute-start | bytes 393224 | tf_op jit(solution)/shard_map/ppermute | solution.py:209
  34.6 14.7 %collective-permute-start.10 = (bf16[4,16,2048]{2,1,0:T(8,128)(2,1)S(1)}, bf16[4,16,2048]{2,1,0:T(8,128)(2,1)S(1)}, u32[]{:S(2)}, u32[]{:S(2)}) collective-permute-start(bf16[4,16,2048]{2,1,0:T(8,128)(2,1)S(1)} %get-tuple-element.41), channel_id=1, source_target_pairs={{0,8},{4,12},{8,0},{12,4},{16,24},{20,28},{24,16},{28,20},{1,9},{5... | collective-permute-start | bytes 786440 | tf_op jit(solution)/shard_map/ppermute | solution.py:213
  36.2 13.8 %collective-permute-start.11 = (bf16[4,16,2048]{2,1,0:T(8,128)(2,1)S(1)}, bf16[4,16,2048]{2,1,0:T(8,128)(2,1)S(1)}, u32[]{:S(2)}, u32[]{:S(2)}) collective-permute-start(bf16[4,16,2048]{2,1,0:T(8,128)(2,1)S(1)} %get-tuple-element.42), channel_id=1, source_target_pairs={{0,16},{4,20},{8,24},{12,28},{16,0},{20,4},{24,8},{28,12},{1,17},{... | collective-permute-start | bytes 786440 | tf_op jit(solution)/shard_map/ppermute | solution.py:213
  37.3 12.7 %collective-permute-start.12 = (bf16[4,16,2048]{2,1,0:T(8,128)(2,1)S(1)}, bf16[4,16,2048]{2,1,0:T(8,128)(2,1)S(1)}, u32[]{:S(2)}, u32[]{:S(2)}) collective-permute-start(bf16[4,16,2048]{2,1,0:T(8,128)(2,1)S(1)} %get-tuple-element.43), channel_id=1, source_target_pairs={{0,24},{4,28},{8,16},{12,20},{16,8},{20,12},{24,0},{28,4},{1,25},{... | collective-permute-start | bytes 786440 | tf_op jit(solution)/shard_map/ppermute | solution.py:213
  46.4 6.4 %collective-permute-start.20 = (bf16[16,1024]{1,0:T(8,128)(2,1)S(1)}, bf16[16,1024]{1,0:T(8,128)(2,1)S(1)}, u32[]{:S(2)}, u32[]{:S(2)}) collective-permute-start(bf16[16,1024]{1,0:T(8,128)(2,1)S(1)} %get-tuple-element.52), channel_id=1, source_target_pairs={{0,8},{4,12},{8,0},{12,4},{16,24},{20,28},{24,16},{28,20},{1,9},{5... | collective-permute-start | bytes 98312 | tf_op jit(solution)/shard_map/ppermute | solution.py:213
  47.9 6.7 %collective-permute-start.22 = (bf16[16,1024]{1,0:T(8,128)(2,1)S(1)}, bf16[16,1024]{1,0:T(8,128)(2,1)S(1)}, u32[]{:S(2)}, u32[]{:S(2)}) collective-permute-start(bf16[16,1024]{1,0:T(8,128)(2,1)S(1)} %get-tuple-element.53), channel_id=1, source_target_pairs={{0,24},{4,28},{8,16},{12,20},{16,8},{20,12},{24,0},{28,4},{1,25},{... | collective-permute-start | bytes 98312 | tf_op jit(solution)/shard_map/ppermute | solution.py:213
  49.4 5.2 %collective-permute-start.21 = (bf16[16,1024]{1,0:T(8,128)(2,1)S(1)}, bf16[16,1024]{1,0:T(8,128)(2,1)S(1)}, u32[]{:S(2)}, u32[]{:S(2)}) collective-permute-start(bf16[16,1024]{1,0:T(8,128)(2,1)S(1)} %get-tuple-element.54), channel_id=1, source_target_pairs={{0,16},{4,20},{8,24},{12,28},{16,0},{20,4},{24,8},{28,12},{1,17},{... | collective-permute-start | bytes 98312 | tf_op jit(solution)/shard_map/ppermute | solution.py:213
  50.1 6.8 %collective-permute-start.13 = (bf16[16,2048]{1,0:T(8,128)(2,1)S(1)}, bf16[16,2048]{1,0:T(8,128)(2,1)S(1)}, u32[]{:S(2)}, u32[]{:S(2)}) collective-permute-start(bf16[16,2048]{1,0:T(8,128)(2,1)S(1)} %get-tuple-element.49), channel_id=1, source_target_pairs={{0,3},{1,2},{2,1},{3,0},{4,7},{5,6},{6,5},{7,4},{8,11},{9,10},{10,... | collective-permute-start | bytes 196616 | tf_op jit(solution)/shard_map/ppermute | solution.py:209
  52.6 5.6 %collective-permute-start.15 = (bf16[16,2048]{1,0:T(8,128)(2,1)S(1)}, bf16[16,2048]{1,0:T(8,128)(2,1)S(1)}, u32[]{:S(2)}, u32[]{:S(2)}) collective-permute-start(bf16[16,2048]{1,0:T(8,128)(2,1)S(1)} %get-tuple-element.50), channel_id=1, source_target_pairs={{0,2},{1,3},{2,0},{3,1},{4,6},{5,7},{6,4},{7,5},{8,10},{9,11},{10,... | collective-permute-start | bytes 196616 | tf_op jit(solution)/shard_map/ppermute | solution.py:209
  52.7 5.5 %collective-permute-start.14 = (bf16[16,2048]{1,0:T(8,128)(2,1)S(1)}, bf16[16,2048]{1,0:T(8,128)(2,1)S(1)}, u32[]{:S(2)}, u32[]{:S(2)}) collective-permute-start(bf16[16,2048]{1,0:T(8,128)(2,1)S(1)} %get-tuple-element.51), channel_id=1, source_target_pairs={{0,1},{1,0},{2,3},{3,2},{4,5},{5,4},{6,7},{7,6},{8,9},{9,8},{10,11... | collective-permute-start | bytes 196616 | tf_op jit(solution)/shard_map/ppermute | solution.py:209

commit v16 on v15

--- a/solution.py
+++ b/solution.py
@@ -225,7 +225,6 @@
     n_adapters = owner.shape[0]
     n_seg = segment_length.shape[1]
     by_slot = n_adapters == n_seq == n_seg == 8 and n_head == 4
-    facts = token_facts(tok, segment_length[0], segment_adapter[0], owner, by_slot)
 
     reach = []
     while sum(reach) < pack * 3 // 8:
@@ -240,11 +239,14 @@
     if by_slot:
         w = [adapter_up_weight] + [shifted(adapter_up_weight, n_head, j) for j in range(1, n_head)]
         w = jnp.concatenate(w, axis=0)[None]
+        lengths, own_keys, _ = lax.optimization_barrier((segment_length, keys, w))
         w = [w] + [partnered(w, n_seq, 2 * m) for m in range(1, n_seq // 2)]
     else:
+        lengths, own_keys = segment_length, keys
         w = lax.all_gather(adapter_up_weight, "seq", axis=0, tiled=True)
         up_weight = [lax.all_gather(w, "head", axis=1, tiled=False)]
 
+    facts = token_facts(tok, lengths[0], segment_adapter[0], owner, by_slot)
     n_out = 2 if by_slot else 1
     n_groups = n_seq if by_slot else n_seg
     part = width // n_head
@@ -266,7 +268,7 @@
             flops=0, bytes_accessed=LAYOUT_BYTES, transcendentals=0
         ),
         name="layout",
-    )(facts, keys.T, *parts)
+    )(facts, own_keys.T, *parts)
     halves = 2
     n_kv = KEY_VALUE_HEADS // halves
     half = width // halves

time: 59.2 us -> 59.1 us (level)
  waiting for transfers between devices: 13.1 us -> 11.8 us
  starting transfers between devices: 31.8 us -> 33 us
    ppermute x12, waiting for transfers between devices: 2.1 us -> 0.27 us  [partnered(): return lax.ppermute(x, 'seq', [(i, i ^ bits) for i in range(n_seq)])]
    ppermute x6, starting transfers between devices: 8.01 us -> 9.35 us  [across(): return lax.ppermute(x, 'head', [(i, i ^ j) for i in range(n_head)])]
    optimization_barrier x0 -> x1, local copies, waits for them, and re-layouts: none -> 1.02 us  [on_device(): lengths, own_keys, _ = lax.optimization_barrier((segment_length, keys, w))]
    unnamed x13 -> x12, local copies, waits for them, and re-layouts: 1.99 us -> 0.97 us
  transfers between devices with their start and end apart: 23 -> 23, of which waited for: 7 -> 5; matrix products, arithmetic and copies ran while one was open for 10% -> 10% of each run, Pallas kernels for 11% -> 11%
where the time goes in v16:
time: 59.1 us; the launch traced here: 58.9 us
  starting transfers between devices  33 us (56%)
  waiting for transfers between devices  11.8 us (20%)
  Pallas kernels  6.36 us (11%)
  other arithmetic  3.72 us (6%)
  local copies, waits for them, and re-layouts  2.98 us (5%)
  between operations  0.99 us (2%)
    ppermute x6, waiting for transfers between devices, across(): return lax.ppermute(x, 'head', [(i, i ^ j) for i in range(n_head)])  11.5 us
    ppermute x12, starting transfers between devices, partnered(): return lax.ppermute(x, 'seq', [(i, i ^ bits) for i in range(n_seq)])  11.4 us
    ppermute x6, starting transfers between devices, across(): return lax.ppermute(x, 'head', [(i, i ^ j) for i in range(n_head)])  9.35 us
    ppermute x3, starting transfers between devices, shifted(): lax.ppermute(x, 'head', [(i, (i + j) % n_head) for i in range(n_head)])  7.93 us
    pallas_call x2, Pallas kernels, attention(): pl.pallas_call(functools.partial(attention_kernel, by_slot, h * n_kv, n_k...  4.71 us
    ppermute x2, starting transfers between devices, on_device(): parts.insert(0, lax.ppermute(own[tok - rows:], 'head', shift))  4.39 us
    mul x2, other arithmetic, on_device(): return (down.T[None] * ADAPTER_SCALE, up[None] * ADAPTER_SCALE)  1.35 us
  transfers between devices with their start and end apart: 23, of which 5 were waited for; matrix products, arithmetic and copies ran while one was open for 10% of the time, Pallas kernels for 11%

profile of v16, /device:TPU:0, one launch (start us, length us, event | category | flops | bytes accessed | tf_op | source)
XLA Modules:
  0.0 58.9 jit_solution(3599390722126458371)
XLA Ops:
  0.6 4.1 %collective-permute-start.1 = (bf16[1,16,1024]{2,1,0:T(8,128)(2,1)}, bf16[1,16,1024]{2,1,0:T(8,128)(2,1)S(1)}, u32[]{:S(2)}, u32[]{:S(2)}) collective-permute-start(bf16[1,16,1024]{2,1,0:T(8,128)(2,1)} %param.16), channel_id=1, source_target_pairs={{0,2},{1,3},{2,0},{3,1},{4,6},{5,7},{6,4},{7,5},{8,10},{9,11},{10,... | collective-permute-start | bytes 98312 | tf_op jit(solution)/shard_map/ppermute | solution.py:205
  4.8 1.6 %collective-permute-start = (bf16[1,16,1024]{2,1,0:T(8,128)(2,1)}, bf16[1,16,1024]{2,1,0:T(8,128)(2,1)S(1)}, u32[]{:S(2)}, u32[]{:S(2)}) collective-permute-start(bf16[1,16,1024]{2,1,0:T(8,128)(2,1)} %param.16), channel_id=1, source_target_pairs={{0,1},{1,2},{2,3},{3,0},{4,5},{5,6},{6,7},{7,4},{8,9},{9,10},{10,1... | collective-permute-start | bytes 98312 | tf_op jit(solution)/shard_map/ppermute | solution.py:205
  6.3 2.2 %collective-permute-start.2 = (bf16[1,16,1024]{2,1,0:T(8,128)(2,1)}, bf16[1,16,1024]{2,1,0:T(8,128)(2,1)S(1)}, u32[]{:S(2)}, u32[]{:S(2)}) collective-permute-start(bf16[1,16,1024]{2,1,0:T(8,128)(2,1)} %param.16), channel_id=1, source_target_pairs={{0,3},{1,0},{2,1},{3,2},{4,7},{5,4},{6,5},{7,6},{8,11},{9,8},{10,9... | collective-permute-start | bytes 98312 | tf_op jit(solution)/shard_map/ppermute | solution.py:205
  8.6 0.9 %constant_dynamic-update-slice_fusion.1 = bf16[128,1024]{1,0:T(8,128)(2,1)S(1)} fusion(bf16[128,512]{1,0:T(8,128)(2,1)} %param.11), kind=kLoop, calls=%fused_computation.39 | loop fusion | bytes 262144
  9.5 0.9 %constant_dynamic-update-slice_fusion.refs_3_ = bf16[128,1024]{1,0:T(8,128)(2,1)S(1)} fusion(bf16[128,1024]{1,0:T(8,128)(2,1)S(1)} %constant_dynamic-update-slice_fusion.1, bf16[128,512]{1,0:T(8,128)(2,1)} %param.12), kind=kLoop, calls=%fused_computation.38 | loop fusion | bytes 262144 | tf_op jit(solution)/shard_map/concatenate | solution.py:233
  10.4 1.7 %collective-permute-start.4 = (bf16[128,1024]{1,0:T(8,128)(2,1)S(1)}, bf16[128,1024]{1,0:T(8,128)(2,1)S(1)}, u32[]{:S(2)}, u32[]{:S(2)}) collective-permute-start(bf16[128,1024]{1,0:T(8,128)(2,1)S(1)} %constant_dynamic-update-slice_fusion.refs_3_), channel_id=1, source_target_pairs={{0,1},{1,2},{2,3},{4,5},{5,6},{6,7},{8,9},{9,10},{10,11},{12,13},{... | collective-permute-start | bytes 786440 | tf_op jit(solution)/shard_map/ppermute | solution.py:237
  12.1 2.7 %collective-permute-start.3 = (bf16[64,1024]{1,0:T(8,128)(2,1)S(1)}, bf16[64,1024]{1,0:T(8,128)(2,1)S(1)}, u32[]{:S(2)}, u32[]{:S(2)}) collective-permute-start(bf16[64,1024]{1,0:T(8,128)(2,1)S(1)} %slice.60), channel_id=1, source_target_pairs={{0,2},{1,3},{4,6},{5,7},{8,10},{9,11},{12,14},{13,15},{16,18},{17,... | collective-permute-start | bytes 393224 | tf_op jit(solution)/shard_map/ppermute | solution.py:237
  14.9 0.0 collective-permute-done.1
  14.9 0.8 %maximum_bitcast_fusion = bf16[1,4,16,1024]{3,2,1,0:T(8,128)(2,1)S(1)} fusion(bf16[1,16,1024]{2,1,0:T(8,128)(2,1)S(1)} %collective-permute-done.2, bf16[1,16,1024]{2,1,0:T(8,128)(2,1)S(1)} %collective-permute-done.1, bf16[1,16,1024]{2,1,0:T(8,128)(2,1)S(1)} %collective-permute-done, bf16[1,16,1024]{2,1,0:T(8,128)(2,1)} %param.16), kind=kLoop, calls=%fused_computation.10 | loop fusion | flops 196608 | bytes 262144 | tf_op jit(solution)/shard_map/broadcast_in_dim | solution.py:241
  15.7 2.5 %collective-permute-start.7 = (bf16[1,4,16,1024]{3,2,1,0:T(8,128)(2,1)S(1)}, bf16[1,4,16,1024]{3,2,1,0:T(8,128)(2,1)S(1)}, u32[]{:S(2)}, u32[]{:S(2)}) collective-permute-start(bf16[1,4,16,1024]{3,2,1,0:T(8,128)(2,1)S(1)} %maximum_bitcast_fusion), channel_id=1, source_target_pairs={{0,24},{4,28},{8,16},{12,20},{16,8},{20,12},{24,0},{28,4},{1,25},{... | collective-permute-start | bytes 393224 | tf_op jit(solution)/shard_map/ppermute | solution.py:213
  18.2 0.5 collective-permute-start.6
  18.7 0.5 collective-permute-start.5
  19.2 1.0 %select_reduce_fusion.1 = s32[8,8]{1,0:T(8,128)S(1)} fusion(s32[8]{0:T(128)} %param.19, s32[8]{0:T(128)} %bitcast.51, s32[8]{0:T(128)} %bitcast.52, pred[8]{0:T(512)(128)(4,1)S(1)} %get-tuple-element.61, pred[8]{0:T(512)(128)(4,1)S(1)} %get-tuple-element.62, pred[8]{0:T(512)(128)(4,1)S(1)} %get-tuple-element.63, pred[8]{0:T(512)(128)(4,1)S(1)} %get-tuple-element.64), kind=kLoop, calls=%fused_computation.30 | loop fusion | flops 6592 | bytes 384 | tf_op jit(solution)/shard_map/reduce_sum | solution.py:198
  20.3 0.1 compare_and_fusion
  20.4 1.0 %copy.13 = bf16[128,512]{0,1:T(8,128)(2,1)S(1)} copy(bf16[128,512]{1,0:T(8,128)(2,1)} %param.11) | data formatting | bytes 262144 | tf_op jit(solution)/shard_map/optimization_barrier | solution.py:242
  21.4 0.1 select_reduce_fusion.facts_ref.refs_0_
  21.5 0.3 layout.1
  21.8 0.0 copy-start.3
  21.8 2.2 %attention_0.1.refs_2_ = bf16[2048,128]{1,0:T(8,128)(2,1)S(1)} custom-call(bf16[320,512]{1,0:T(8,128)(2,1)S(1)} %get-tuple-element.28.k_all, bf16[320,512]{1,0:T(8,128)(2,1)S(1)} %get-tuple-element.29.v_all, bf16[512,320]{1,0:T(8,128)(2,1)S(1)} %get-tuple-element.30.k_turned, f32[320,128]{1,0:T(8,128)S(1)} %get-tuple-element.31.bias, ...), custom_call_target="tpu_custom_call" | custom-call | flops 503316480 | bytes 2097152 | tf_op jit(solution)/shard_map/attention_0/pallas_call | solution.py:277
  24.1 0.1 collective-permute-start.8
  24.2 0.0 copy-start.2
  24.2 2.5 %attention_1.1 = (bf16[2048,128]{1,0:T(8,128)(2,1)S(1)}, bf16[4,4,16,1024]{3,2,1,0:T(8,128)(2,1)S(1)}, bf16[4,4,16,1024]{3,2,1,0:T(8,128)(2,1)S(1)}) custom-call(bf16[320,512]{1,0:T(8,128)(2,1)S(1)} %get-tuple-element.28.k_all, bf16[320,512]{1,0:T(8,128)(2,1)S(1)} %get-tuple-element.29.v_all, bf16[512,320]{1,0:T(8,128)(2,1)S(1)} %get-tuple-element.30.k_turned, ...), custom_call_target="tpu_custom_call" | custom-call | flops 503316480 | bytes 2097152 | tf_op jit(solution)/shard_map/attention_1/pallas_call | solution.py:277
  26.7 0.5 collective-permute-start.16
  27.3 0.4 rank_gradient.1.rank_ref
  27.7 0.7 %down_parts.1 = (bf16[4,4,16,2048]{3,2,1,0:T(8,128)(2,1)S(1)}, bf16[4,4,16,2048]{3,2,1,0:T(8,128)(2,1)S(1)}) custom-call(s32[8,128]{1,0:T(8,128)S(1)} %select_reduce_fusion.facts_ref.refs_0_, bf16[128,8192]{1,0:T(8,128)(2,1)S(1)} %copy-done.2, bf16[16,128]{1,0:T(8,128)(2,1)S(1)} %rank_gradient.1.rank_ref), custom_call_target="tpu_custom_call" | custom-call | flops 268435456 | bytes 8388608 | tf_op jit(solution)/shard_map/down_parts/pallas_call | solution.py:317
  28.4 0.1 collective-permute-start.9
  28.6 0.2 collective-permute-done.16
  28.8 0.2 add_convert_fusion
  29.0 1.5 %collective-permute-start.17 = (bf16[4,16,1024]{2,1,0:T(8,128)(2,1)S(1)}, bf16[4,16,1024]{2,1,0:T(8,128)(2,1)S(1)}, u32[]{:S(2)}, u32[]{:S(2)}) collective-permute-start(bf16[4,16,1024]{2,1,0:T(8,128)(2,1)S(1)} %get-tuple-element.50), channel_id=1, source_target_pairs={{0,1},{1,0},{2,3},{3,2},{4,5},{5,4},{6,7},{7,6},{8,9},{9,8},{10,11... | collective-permute-start | bytes 393224 | tf_op jit(solution)/shard_map/ppermute | solution.py:209
  30.5 2.9 %collective-permute-start.19 = (bf16[4,16,1024]{2,1,0:T(8,128)(2,1)S(1)}, bf16[4,16,1024]{2,1,0:T(8,128)(2,1)S(1)}, u32[]{:S(2)}, u32[]{:S(2)}) collective-permute-start(bf16[4,16,1024]{2,1,0:T(8,128)(2,1)S(1)} %get-tuple-element.51), channel_id=1, source_target_pairs={{0,3},{1,2},{2,1},{3,0},{4,7},{5,6},{6,5},{7,4},{8,11},{9,10},{10,... | collective-permute-start | bytes 393224 | tf_op jit(solution)/shard_map/ppermute | solution.py:209
  33.4 0.5 collective-permute-start.18
  33.9 0.2 core_sum.1
  34.2 1.6 %collective-permute-start.10 = (bf16[4,16,2048]{2,1,0:T(8,128)(2,1)S(1)}, bf16[4,16,2048]{2,1,0:T(8,128)(2,1)S(1)}, u32[]{:S(2)}, u32[]{:S(2)}) collective-permute-start(bf16[4,16,2048]{2,1,0:T(8,128)(2,1)S(1)} %get-tuple-element.45), channel_id=1, source_target_pairs={{0,8},{4,12},{8,0},{12,4},{16,24},{20,28},{24,16},{28,20},{1,9},{5... | collective-permute-start | bytes 786440 | tf_op jit(solution)/shard_map/ppermute | solution.py:213
  35.7 1.5 %collective-permute-start.11 = (bf16[4,16,2048]{2,1,0:T(8,128)(2,1)S(1)}, bf16[4,16,2048]{2,1,0:T(8,128)(2,1)S(1)}, u32[]{:S(2)}, u32[]{:S(2)}) collective-permute-start(bf16[4,16,2048]{2,1,0:T(8,128)(2,1)S(1)} %get-tuple-element.46), channel_id=1, source_target_pairs={{0,16},{4,20},{8,24},{12,28},{16,0},{20,4},{24,8},{28,12},{1,17},{... | collective-permute-start | bytes 786440 | tf_op jit(solution)/shard_map/ppermute | solution.py:213
  37.3 0.5 collective-permute-start.12
  37.7 2.9 %collective-permute-done.19 = bf16[4,16,1024]{2,1,0:T(8,128)(2,1)S(1)} collective-permute-done((bf16[4,16,1024]{2,1,0:T(8,128)(2,1)S(1)}, bf16[4,16,1024]{2,1,0:T(8,128)(2,1)S(1)}, u32[]{:S(2)}, u32[]{:S(2)}) %collective-permute-start.19) | collective-permute-done | bytes 131104 | tf_op jit(solution)/shard_map/ppermute | solution.py:209
  40.6 5.5 %collective-permute-done.18 = bf16[4,16,1024]{2,1,0:T(8,128)(2,1)S(1)} collective-permute-done((bf16[4,16,1024]{2,1,0:T(8,128)(2,1)S(1)}, bf16[4,16,1024]{2,1,0:T(8,128)(2,1)S(1)}, u32[]{:S(2)}, u32[]{:S(2)}) %collective-permute-start.18) | collective-permute-done | bytes 131104 | tf_op jit(solution)/shard_map/ppermute | solution.py:209
  46.1 0.1 fusion.2
  46.2 1.6 %collective-permute-start.20 = (bf16[16,1024]{1,0:T(8,128)(2,1)S(1)}, bf16[16,1024]{1,0:T(8,128)(2,1)S(1)}, u32[]{:S(2)}, u32[]{:S(2)}) collective-permute-start(bf16[16,1024]{1,0:T(8,128)(2,1)S(1)} %get-tuple-element.56), channel_id=1, source_target_pairs={{0,8},{4,12},{8,0},{12,4},{16,24},{20,28},{24,16},{28,20},{1,9},{5... | collective-permute-start | bytes 98312 | tf_op jit(solution)/shard_map/ppermute | solution.py:213
  47.7 1.5 %collective-permute-start.22 = (bf16[16,1024]{1,0:T(8,128)(2,1)S(1)}, bf16[16,1024]{1,0:T(8,128)(2,1)S(1)}, u32[]{:S(2)}, u32[]{:S(2)}) collective-permute-start(bf16[16,1024]{1,0:T(8,128)(2,1)S(1)} %get-tuple-element.57), channel_id=1, source_target_pairs={{0,24},{4,28},{8,16},{12,20},{16,8},{20,12},{24,0},{28,4},{1,25},{... | collective-permute-start | bytes 98312 | tf_op jit(solution)/shard_map/ppermute | solution.py:213
  49.2 0.5 collective-permute-start.21
  49.8 0.1 add_convert_fusion.1
  49.9 2.7 %collective-permute-start.13 = (bf16[16,2048]{1,0:T(8,128)(2,1)S(1)}, bf16[16,2048]{1,0:T(8,128)(2,1)S(1)}, u32[]{:S(2)}, u32[]{:S(2)}) collective-permute-start(bf16[16,2048]{1,0:T(8,128)(2,1)S(1)} %get-tuple-element.53), channel_id=1, source_target_pairs={{0,3},{1,2},{2,1},{3,0},{4,7},{5,6},{6,5},{7,4},{8,11},{9,10},{10,... | collective-permute-start | bytes 196616 | tf_op jit(solution)/shard_map/ppermute | solution.py:209
  52.6 1.7 %collective-permute-start.14 = (bf16[16,2048]{1,0:T(8,128)(2,1)S(1)}, bf16[16,2048]{1,0:T(8,128)(2,1)S(1)}, u32[]{:S(2)}, u32[]{:S(2)}) collective-permute-start(bf16[16,2048]{1,0:T(8,128)(2,1)S(1)} %get-tuple-element.55), channel_id=1, source_target_pairs={{0,1},{1,0},{2,3},{3,2},{4,5},{5,4},{6,7},{7,6},{8,9},{9,8},{10,11... | collective-permute-start | bytes 196616 | tf_op jit(solution)/shard_map/ppermute | solution.py:209
  54.4 0.7 %fusion.10 = f32[1,16,1024]{2,1,0:T(8,128)} fusion(bf16[16,1024]{1,0:T(8,128)(2,1)S(1)} %collective-permute-done.22, bf16[16,1024]{1,0:T(8,128)(2,1)S(1)} %collective-permute-done.21, bf16[16,1024]{1,0:T(8,128)(2,1)S(1)} %collective-permute-done.20, bf16[4,16,1024]{2,1,0:T(8,128)(2,1)S(1)} %fusion.2), kind=kLoop, calls=%fused_computation.24 | loop fusion | flops 131072 | bytes 196608 | tf_op jit(solution)/shard_map/mul | solution.py:348
  55.0 1.6 %collective-permute-done.13 = bf16[16,2048]{1,0:T(8,128)(2,1)S(1)} collective-permute-done((bf16[16,2048]{1,0:T(8,128)(2,1)S(1)}, bf16[16,2048]{1,0:T(8,128)(2,1)S(1)}, u32[]{:S(2)}, u32[]{:S(2)}) %collective-permute-start.13) | collective-permute-done | bytes 65568 | tf_op jit(solution)/shard_map/ppermute | solution.py:209
  56.6 1.6 %collective-permute-done.15 = bf16[16,2048]{1,0:T(8,128)(2,1)S(1)} collective-permute-done((bf16[16,2048]{1,0:T(8,128)(2,1)S(1)}, bf16[16,2048]{1,0:T(8,128)(2,1)S(1)}, u32[]{:S(2)}, u32[]{:S(2)}) %collective-permute-start.15) | collective-permute-done | bytes 65568 | tf_op jit(solution)/shard_map/ppermute | solution.py:209
  58.2 0.7 %fusion.6 = f32[1,2048,16]{1,2,0:T(8,128)} fusion(bf16[16,2048]{1,0:T(8,128)(2,1)S(1)} %collective-permute-done.15, bf16[16,2048]{1,0:T(8,128)(2,1)S(1)} %collective-permute-done.14, bf16[16,2048]{1,0:T(8,128)(2,1)S(1)} %collective-permute-done.13, bf16[4,16,2048]{2,1,0:T(8,128)(2,1)S(1)} %add_convert_fusion.1), kind=kLoop, calls=%fused_computation.15 | loop fusion | flops 262144 | bytes 393216 | tf_op jit(solution)/shard_map/mul | solution.py:348
  (36 shorter events, 0.2 us)
Async XLA Ops:
  0.6 21.1 %copy-start.1 = (bf16[128,4096]{1,0:T(8,128)(2,1)S(1)}, bf16[128,4096]{1,0:T(8,128)(2,1)}, u32[]{:S(2)}) copy-start(bf16[128,4096]{1,0:T(8,128)(2,1)} %g_hbm.3) | copy-start | bytes 3145732
  0.6 21.1 %copy-start = (bf16[128,4096]{1,0:T(8,128)(2,1)S(1)}, bf16[128,4096]{1,0:T(8,128)(2,1)}, u32[]{:S(2)}) copy-start(bf16[128,4096]{1,0:T(8,128)(2,1)} %q_hbm.3) | copy-start | bytes 3145732
  0.6 14.2 %collective-permute-start.1 = (bf16[1,16,1024]{2,1,0:T(8,128)(2,1)}, bf16[1,16,1024]{2,1,0:T(8,128)(2,1)S(1)}, u32[]{:S(2)}, u32[]{:S(2)}) collective-permute-start(bf16[1,16,1024]{2,1,0:T(8,128)(2,1)} %param.16), channel_id=1, source_target_pairs={{0,2},{1,3},{2,0},{3,1},{4,6},{5,7},{6,4},{7,5},{8,10},{9,11},{10,... | collective-permute-start | bytes 98312 | tf_op jit(solution)/shard_map/ppermute | solution.py:205
  4.8 10.1 %collective-permute-start = (bf16[1,16,1024]{2,1,0:T(8,128)(2,1)}, bf16[1,16,1024]{2,1,0:T(8,128)(2,1)S(1)}, u32[]{:S(2)}, u32[]{:S(2)}) collective-permute-start(bf16[1,16,1024]{2,1,0:T(8,128)(2,1)} %param.16), channel_id=1, source_target_pairs={{0,1},{1,2},{2,3},{3,0},{4,5},{5,6},{6,7},{7,4},{8,9},{9,10},{10,1... | collective-permute-start | bytes 98312 | tf_op jit(solution)/shard_map/ppermute | solution.py:205
  6.3 8.6 %collective-permute-start.2 = (bf16[1,16,1024]{2,1,0:T(8,128)(2,1)}, bf16[1,16,1024]{2,1,0:T(8,128)(2,1)S(1)}, u32[]{:S(2)}, u32[]{:S(2)}) collective-permute-start(bf16[1,16,1024]{2,1,0:T(8,128)(2,1)} %param.16), channel_id=1, source_target_pairs={{0,3},{1,0},{2,1},{3,2},{4,7},{5,4},{6,5},{7,6},{8,11},{9,8},{10,9... | collective-permute-start | bytes 98312 | tf_op jit(solution)/shard_map/ppermute | solution.py:205
  10.4 11.1 %collective-permute-start.4 = (bf16[128,1024]{1,0:T(8,128)(2,1)S(1)}, bf16[128,1024]{1,0:T(8,128)(2,1)S(1)}, u32[]{:S(2)}, u32[]{:S(2)}) collective-permute-start(bf16[128,1024]{1,0:T(8,128)(2,1)S(1)} %constant_dynamic-update-slice_fusion.refs_3_), channel_id=1, source_target_pairs={{0,1},{1,2},{2,3},{4,5},{5,6},{6,7},{8,9},{9,10},{10,11},{12,13},{... | collective-permute-start | bytes 786440 | tf_op jit(solution)/shard_map/ppermute | solution.py:237
  12.1 9.3 %collective-permute-start.3 = (bf16[64,1024]{1,0:T(8,128)(2,1)S(1)}, bf16[64,1024]{1,0:T(8,128)(2,1)S(1)}, u32[]{:S(2)}, u32[]{:S(2)}) collective-permute-start(bf16[64,1024]{1,0:T(8,128)(2,1)S(1)} %slice.60), channel_id=1, source_target_pairs={{0,2},{1,3},{4,6},{5,7},{8,10},{9,11},{12,14},{13,15},{16,18},{17,... | collective-permute-start | bytes 393224 | tf_op jit(solution)/shard_map/ppermute | solution.py:237
  15.7 8.3 %collective-permute-start.7 = (bf16[1,4,16,1024]{3,2,1,0:T(8,128)(2,1)S(1)}, bf16[1,4,16,1024]{3,2,1,0:T(8,128)(2,1)S(1)}, u32[]{:S(2)}, u32[]{:S(2)}) collective-permute-start(bf16[1,4,16,1024]{3,2,1,0:T(8,128)(2,1)S(1)} %maximum_bitcast_fusion), channel_id=1, source_target_pairs={{0,24},{4,28},{8,16},{12,20},{16,8},{20,12},{24,0},{28,4},{1,25},{... | collective-permute-start | bytes 393224 | tf_op jit(solution)/shard_map/ppermute | solution.py:213
  18.2 5.8 %collective-permute-start.6 = (bf16[1,4,16,1024]{3,2,1,0:T(8,128)(2,1)S(1)}, bf16[1,4,16,1024]{3,2,1,0:T(8,128)(2,1)S(1)}, u32[]{:S(2)}, u32[]{:S(2)}) collective-permute-start(bf16[1,4,16,1024]{3,2,1,0:T(8,128)(2,1)S(1)} %maximum_bitcast_fusion), channel_id=1, source_target_pairs={{0,16},{4,20},{8,24},{12,28},{16,0},{20,4},{24,8},{28,12},{1,17},{... | collective-permute-start | bytes 393224 | tf_op jit(solution)/shard_map/ppermute | solution.py:213
  18.7 5.3 %collective-permute-start.5 = (bf16[1,4,16,1024]{3,2,1,0:T(8,128)(2,1)S(1)}, bf16[1,4,16,1024]{3,2,1,0:T(8,128)(2,1)S(1)}, u32[]{:S(2)}, u32[]{:S(2)}) collective-permute-start(bf16[1,4,16,1024]{3,2,1,0:T(8,128)(2,1)S(1)} %maximum_bitcast_fusion), channel_id=1, source_target_pairs={{0,8},{4,12},{8,0},{12,4},{16,24},{20,28},{24,16},{28,20},{1,9},{5... | collective-permute-start | bytes 393224 | tf_op jit(solution)/shard_map/ppermute | solution.py:213
  21.8 2.4 %copy-start.3 = (bf16[128,16]{0,1:T(8,128)(2,1)S(1)}, bf16[128,16]{0,1:T(8,128)(2,1)}, u32[]{:S(2)}) copy-start(bf16[128,16]{0,1:T(8,128)(2,1)} %param.15) | copy-start | bytes 12292
  24.1 2.6 %collective-permute-start.8 = (bf16[4,4,16,1024]{3,2,1,0:T(8,128)(2,1)S(1)}, bf16[4,4,16,1024]{3,2,1,0:T(8,128)(2,1)S(1)}, u32[]{:S(2)}, u32[]{:S(2)}) collective-permute-start(bf16[4,4,16,1024]{3,2,1,0:T(8,128)(2,1)S(1)} %constant_dynamic-update-slice_fusion.2.refs_0_), channel_id=1, source_target_pairs={{0,4},{4,0},{8,12},{12,8},{16,20},{20,16},{24,28},{28,24},{1,5},{5... | collective-permute-start | bytes 1572872 | tf_op jit(solution)/shard_map/ppermute | solution.py:213
  24.2 3.5 %copy-start.2 = (bf16[128,8192]{1,0:T(8,128)(2,1)S(1)}, bf16[128,8192]{1,0:T(8,128)(2,1)}, u32[]{:S(2)}) copy-start(bf16[128,8192]{1,0:T(8,128)(2,1)} %x_ref.1) | copy-start | bytes 6291460
  26.7 2.1 %collective-permute-start.16 = (bf16[4,4,16,1024]{3,2,1,0:T(8,128)(2,1)S(1)}, bf16[4,4,16,1024]{3,2,1,0:T(8,128)(2,1)S(1)}, u32[]{:S(2)}, u32[]{:S(2)}) collective-permute-start(bf16[4,4,16,1024]{3,2,1,0:T(8,128)(2,1)S(1)} %get-tuple-element.49), channel_id=1, source_target_pairs={{0,4},{4,0},{8,12},{12,8},{16,20},{20,16},{24,28},{28,24},{1,5},{5... | collective-permute-start | bytes 1572872 | tf_op jit(solution)/shard_map/ppermute | solution.py:213
  28.4 5.5 %collective-permute-start.9 = (bf16[4,4,16,2048]{3,2,1,0:T(8,128)(2,1)S(1)}, bf16[4,4,16,2048]{3,2,1,0:T(8,128)(2,1)S(1)}, u32[]{:S(2)}, u32[]{:S(2)}) collective-permute-start(bf16[4,4,16,2048]{3,2,1,0:T(8,128)(2,1)S(1)} %get-tuple-element.43), channel_id=1, source_target_pairs={{0,4},{4,0},{8,12},{12,8},{16,20},{20,16},{24,28},{28,24},{1,5},{5... | collective-permute-start | bytes 3145736 | tf_op jit(solution)/shard_map/ppermute | solution.py:213
  29.0 8.2 %collective-permute-start.17 = (bf16[4,16,1024]{2,1,0:T(8,128)(2,1)S(1)}, bf16[4,16,1024]{2,1,0:T(8,128)(2,1)S(1)}, u32[]{:S(2)}, u32[]{:S(2)}) collective-permute-start(bf16[4,16,1024]{2,1,0:T(8,128)(2,1)S(1)} %get-tuple-element.50), channel_id=1, source_target_pairs={{0,1},{1,0},{2,3},{3,2},{4,5},{5,4},{6,7},{7,6},{8,9},{9,8},{10,11... | collective-permute-start | bytes 393224 | tf_op jit(solution)/shard_map/ppermute | solution.py:209
  30.5 10.1 %collective-permute-start.19 = (bf16[4,16,1024]{2,1,0:T(8,128)(2,1)S(1)}, bf16[4,16,1024]{2,1,0:T(8,128)(2,1)S(1)}, u32[]{:S(2)}, u32[]{:S(2)}) collective-permute-start(bf16[4,16,1024]{2,1,0:T(8,128)(2,1)S(1)} %get-tuple-element.51), channel_id=1, source_target_pairs={{0,3},{1,2},{2,1},{3,0},{4,7},{5,6},{6,5},{7,4},{8,11},{9,10},{10,... | collective-permute-start | bytes 393224 | tf_op jit(solution)/shard_map/ppermute | solution.py:209
  33.4 12.7 %collective-permute-start.18 = (bf16[4,16,1024]{2,1,0:T(8,128)(2,1)S(1)}, bf16[4,16,1024]{2,1,0:T(8,128)(2,1)S(1)}, u32[]{:S(2)}, u32[]{:S(2)}) collective-permute-start(bf16[4,16,1024]{2,1,0:T(8,128)(2,1)S(1)} %get-tuple-element.52), channel_id=1, source_target_pairs={{0,2},{1,3},{2,0},{3,1},{4,6},{5,7},{6,4},{7,5},{8,10},{9,11},{10,... | collective-permute-start | bytes 393224 | tf_op jit(solution)/shard_map/ppermute | solution.py:209
  34.2 15.1 %collective-permute-start.10 = (bf16[4,16,2048]{2,1,0:T(8,128)(2,1)S(1)}, bf16[4,16,2048]{2,1,0:T(8,128)(2,1)S(1)}, u32[]{:S(2)}, u32[]{:S(2)}) collective-permute-start(bf16[4,16,2048]{2,1,0:T(8,128)(2,1)S(1)} %get-tuple-element.45), channel_id=1, source_target_pairs={{0,8},{4,12},{8,0},{12,4},{16,24},{20,28},{24,16},{28,20},{1,9},{5... | collective-permute-start | bytes 786440 | tf_op jit(solution)/shard_map/ppermute | solution.py:213
  35.7 14.0 %collective-permute-start.11 = (bf16[4,16,2048]{2,1,0:T(8,128)(2,1)S(1)}, bf16[4,16,2048]{2,1,0:T(8,128)(2,1)S(1)}, u32[]{:S(2)}, u32[]{:S(2)}) collective-permute-start(bf16[4,16,2048]{2,1,0:T(8,128)(2,1)S(1)} %get-tuple-element.46), channel_id=1, source_target_pairs={{0,16},{4,20},{8,24},{12,28},{16,0},{20,4},{24,8},{28,12},{1,17},{... | collective-permute-start | bytes 786440 | tf_op jit(solution)/shard_map/ppermute | solution.py:213
  37.3 12.5 %collective-permute-start.12 = (bf16[4,16,2048]{2,1,0:T(8,128)(2,1)S(1)}, bf16[4,16,2048]{2,1,0:T(8,128)(2,1)S(1)}, u32[]{:S(2)}, u32[]{:S(2)}) collective-permute-start(bf16[4,16,2048]{2,1,0:T(8,128)(2,1)S(1)} %get-tuple-element.47), channel_id=1, source_target_pairs={{0,24},{4,28},{8,16},{12,20},{16,8},{20,12},{24,0},{28,4},{1,25},{... | collective-permute-start | bytes 786440 | tf_op jit(solution)/shard_map/ppermute | solution.py:213
  46.2 6.4 %collective-permute-start.20 = (bf16[16,1024]{1,0:T(8,128)(2,1)S(1)}, bf16[16,1024]{1,0:T(8,128)(2,1)S(1)}, u32[]{:S(2)}, u32[]{:S(2)}) collective-permute-start(bf16[16,1024]{1,0:T(8,128)(2,1)S(1)} %get-tuple-element.56), channel_id=1, source_target_pairs={{0,8},{4,12},{8,0},{12,4},{16,24},{20,28},{24,16},{28,20},{1,9},{5... | collective-permute-start | bytes 98312 | tf_op jit(solution)/shard_map/ppermute | solution.py:213
  47.7 6.6 %collective-permute-start.22 = (bf16[16,1024]{1,0:T(8,128)(2,1)S(1)}, bf16[16,1024]{1,0:T(8,128)(2,1)S(1)}, u32[]{:S(2)}, u32[]{:S(2)}) collective-permute-start(bf16[16,1024]{1,0:T(8,128)(2,1)S(1)} %get-tuple-element.57), channel_id=1, source_target_pairs={{0,24},{4,28},{8,16},{12,20},{16,8},{20,12},{24,0},{28,4},{1,25},{... | collective-permute-start | bytes 98312 | tf_op jit(solution)/shard_map/ppermute | solution.py:213
  49.2 5.1 %collective-permute-start.21 = (bf16[16,1024]{1,0:T(8,128)(2,1)S(1)}, bf16[16,1024]{1,0:T(8,128)(2,1)S(1)}, u32[]{:S(2)}, u32[]{:S(2)}) collective-permute-start(bf16[16,1024]{1,0:T(8,128)(2,1)S(1)} %get-tuple-element.58), channel_id=1, source_target_pairs={{0,16},{4,20},{8,24},{12,28},{16,0},{20,4},{24,8},{28,12},{1,17},{... | collective-permute-start | bytes 98312 | tf_op jit(solution)/shard_map/ppermute | solution.py:213
  49.9 6.7 %collective-permute-start.13 = (bf16[16,2048]{1,0:T(8,128)(2,1)S(1)}, bf16[16,2048]{1,0:T(8,128)(2,1)S(1)}, u32[]{:S(2)}, u32[]{:S(2)}) collective-permute-start(bf16[16,2048]{1,0:T(8,128)(2,1)S(1)} %get-tuple-element.53), channel_id=1, source_target_pairs={{0,3},{1,2},{2,1},{3,0},{4,7},{5,6},{6,5},{7,4},{8,11},{9,10},{10,... | collective-permute-start | bytes 196616 | tf_op jit(solution)/shard_map/ppermute | solution.py:209
  52.6 5.5 %collective-permute-start.15 = (bf16[16,2048]{1,0:T(8,128)(2,1)S(1)}, bf16[16,2048]{1,0:T(8,128)(2,1)S(1)}, u32[]{:S(2)}, u32[]{:S(2)}) collective-permute-start(bf16[16,2048]{1,0:T(8,128)(2,1)S(1)} %get-tuple-element.54), channel_id=1, source_target_pairs={{0,2},{1,3},{2,0},{3,1},{4,6},{5,7},{6,4},{7,5},{8,10},{9,11},{10,... | collective-permute-start | bytes 196616 | tf_op jit(solution)/shard_map/ppermute | solution.py:209
  52.6 5.5 %collective-permute-start.14 = (bf16[16,2048]{1,0:T(8,128)(2,1)S(1)}, bf16[16,2048]{1,0:T(8,128)(2,1)S(1)}, u32[]{:S(2)}, u32[]{:S(2)}) collective-permute-start(bf16[16,2048]{1,0:T(8,128)(2,1)S(1)} %get-tuple-element.55), channel_id=1, source_target_pairs={{0,1},{1,0},{2,3},{3,2},{4,5},{5,4},{6,7},{7,6},{8,9},{9,8},{10,11... | collective-permute-start | bytes 196616 | tf_op jit(solution)/shard_map/ppermute | solution.py:209

commit v17 on v16

--- a/solution.py
+++ b/solution.py
@@ -338,8 +338,10 @@
             cost_estimate=pl.CostEstimate(flops=0, bytes_accessed=SUM_BYTES, transcendentals=0),
             name="core_sum",
         )(down[0], partnered(down[1], n_seq, 1))
-        up = over_chips(over_z(over_cores(up, n_seq), n_head, (1, 2, 3)).astype(BF16), n_seq)
-        down = over_z(over_chips(down, n_seq).astype(BF16), n_head, (3, 1, 2))
+        up = over_z(over_cores(up, n_seq), n_head, (1, 2, 3)).astype(BF16)
+        up = over_chips(up, n_seq, (1, 2, 3))
+        down = over_chips(down, n_seq, (1, 3, 2)).astype(BF16)
+        down = over_z(down, n_head, (3, 1, 2))
     else:
         up = lax.all_to_all(up[0], "head", split_axis=0, concat_axis=0, tiled=True)
         up = spread(jnp.sum(up.astype(F32), axis=0), segment_adapter, owner, n_seq)
@@ -360,8 +362,8 @@
     return total
 
 
-def over_chips(both, n_seq):
-    return added(both[0], [partnered(both[m], n_seq, 2 * m) for m in range(1, n_seq // 2)])
+def over_chips(both, n_seq, order):
+    return added(both[0], [partnered(both[m], n_seq, 2 * m) for m in order])
 
 
 def over_z(both, n_head, order):

time: 59.1 us -> 62.5 us (1.058)
  starting transfers between devices: 33 us -> 35.1 us
  waiting for transfers between devices: 11.8 us -> 13 us
    ppermute x6, starting transfers between devices: 9.35 us -> 11.4 us  [across(): return lax.ppermute(x, 'head', [(i, i ^ j) for i in range(n_head)])]
    ppermute x6, waiting for transfers between devices: 11.5 us -> 12.2 us  [across(): return lax.ppermute(x, 'head', [(i, i ^ j) for i in range(n_head)])]
  transfers between devices with their start and end apart: 23 -> 23, of which waited for: 5 -> 6; matrix products, arithmetic and copies ran while one was open for 10% -> 10% of each run, Pallas kernels for 11% -> 10%
where the time goes in v17:
time: 62.5 us; the launch traced here: 62.2 us
  starting transfers between devices  35.1 us (56%)
  waiting for transfers between devices  13 us (21%)
  Pallas kernels  6.36 us (10%)
  other arithmetic  3.72 us (6%)
  local copies, waits for them, and re-layouts  2.98 us (5%)
  between operations  0.98 us (2%)
    ppermute x6, waiting for transfers between devices, across(): return lax.ppermute(x, 'head', [(i, i ^ j) for i in range(n_head)])  12.2 us
    ppermute x6, starting transfers between devices, across(): return lax.ppermute(x, 'head', [(i, i ^ j) for i in range(n_head)])  11.4 us
    ppermute x12, starting transfers between devices, partnered(): return lax.ppermute(x, 'seq', [(i, i ^ bits) for i in range(n_seq)])  11.4 us
    ppermute x3, starting transfers between devices, shifted(): lax.ppermute(x, 'head', [(i, (i + j) % n_head) for i in range(n_head)])  7.93 us
    pallas_call x2, Pallas kernels, attention(): pl.pallas_call(functools.partial(attention_kernel, by_slot, h * n_kv, n_k...  4.71 us
    ppermute x2, starting transfers between devices, on_device(): parts.insert(0, lax.ppermute(own[tok - rows:], 'head', shift))  4.39 us
    mul x2, other arithmetic, on_device(): return (down.T[None] * ADAPTER_SCALE, up[None] * ADAPTER_SCALE)  1.35 us
  transfers between devices with their start and end apart: 23, of which 6 were waited for; matrix products, arithmetic and copies ran while one was open for 10% of the time, Pallas kernels for 10%

profile of v17, /device:TPU:0, one launch (start us, length us, event | category | flops | bytes accessed | tf_op | source)
XLA Modules:
  0.0 62.2 jit_solution(12059885575222823810)
XLA Ops:
  0.6 4.1 %collective-permute-start.1 = (bf16[1,16,1024]{2,1,0:T(8,128)(2,1)}, bf16[1,16,1024]{2,1,0:T(8,128)(2,1)S(1)}, u32[]{:S(2)}, u32[]{:S(2)}) collective-permute-start(bf16[1,16,1024]{2,1,0:T(8,128)(2,1)} %param.16), channel_id=1, source_target_pairs={{0,2},{1,3},{2,0},{3,1},{4,6},{5,7},{6,4},{7,5},{8,10},{9,11},{10,... | collective-permute-start | bytes 98312 | tf_op jit(solution)/shard_map/ppermute | solution.py:205
  4.8 1.6 %collective-permute-start = (bf16[1,16,1024]{2,1,0:T(8,128)(2,1)}, bf16[1,16,1024]{2,1,0:T(8,128)(2,1)S(1)}, u32[]{:S(2)}, u32[]{:S(2)}) collective-permute-start(bf16[1,16,1024]{2,1,0:T(8,128)(2,1)} %param.16), channel_id=1, source_target_pairs={{0,1},{1,2},{2,3},{3,0},{4,5},{5,6},{6,7},{7,4},{8,9},{9,10},{10,1... | collective-permute-start | bytes 98312 | tf_op jit(solution)/shard_map/ppermute | solution.py:205
  6.3 2.2 %collective-permute-start.2 = (bf16[1,16,1024]{2,1,0:T(8,128)(2,1)}, bf16[1,16,1024]{2,1,0:T(8,128)(2,1)S(1)}, u32[]{:S(2)}, u32[]{:S(2)}) collective-permute-start(bf16[1,16,1024]{2,1,0:T(8,128)(2,1)} %param.16), channel_id=1, source_target_pairs={{0,3},{1,0},{2,1},{3,2},{4,7},{5,4},{6,5},{7,6},{8,11},{9,8},{10,9... | collective-permute-start | bytes 98312 | tf_op jit(solution)/shard_map/ppermute | solution.py:205
  8.6 0.9 %constant_dynamic-update-slice_fusion.1 = bf16[128,1024]{1,0:T(8,128)(2,1)S(1)} fusion(bf16[128,512]{1,0:T(8,128)(2,1)} %param.11), kind=kLoop, calls=%fused_computation.39 | loop fusion | bytes 262144
  9.5 0.9 %constant_dynamic-update-slice_fusion.refs_3_ = bf16[128,1024]{1,0:T(8,128)(2,1)S(1)} fusion(bf16[128,1024]{1,0:T(8,128)(2,1)S(1)} %constant_dynamic-update-slice_fusion.1, bf16[128,512]{1,0:T(8,128)(2,1)} %param.12), kind=kLoop, calls=%fused_computation.38 | loop fusion | bytes 262144 | tf_op jit(solution)/shard_map/concatenate | solution.py:233
  10.4 1.7 %collective-permute-start.4 = (bf16[128,1024]{1,0:T(8,128)(2,1)S(1)}, bf16[128,1024]{1,0:T(8,128)(2,1)S(1)}, u32[]{:S(2)}, u32[]{:S(2)}) collective-permute-start(bf16[128,1024]{1,0:T(8,128)(2,1)S(1)} %constant_dynamic-update-slice_fusion.refs_3_), channel_id=1, source_target_pairs={{0,1},{1,2},{2,3},{4,5},{5,6},{6,7},{8,9},{9,10},{10,11},{12,13},{... | collective-permute-start | bytes 786440 | tf_op jit(solution)/shard_map/ppermute | solution.py:237
  12.1 2.7 %collective-permute-start.3 = (bf16[64,1024]{1,0:T(8,128)(2,1)S(1)}, bf16[64,1024]{1,0:T(8,128)(2,1)S(1)}, u32[]{:S(2)}, u32[]{:S(2)}) collective-permute-start(bf16[64,1024]{1,0:T(8,128)(2,1)S(1)} %slice.60), channel_id=1, source_target_pairs={{0,2},{1,3},{4,6},{5,7},{8,10},{9,11},{12,14},{13,15},{16,18},{17,... | collective-permute-start | bytes 393224 | tf_op jit(solution)/shard_map/ppermute | solution.py:237
  14.9 0.8 %maximum_bitcast_fusion = bf16[1,4,16,1024]{3,2,1,0:T(8,128)(2,1)S(1)} fusion(bf16[1,16,1024]{2,1,0:T(8,128)(2,1)S(1)} %collective-permute-done.2, bf16[1,16,1024]{2,1,0:T(8,128)(2,1)S(1)} %collective-permute-done.1, bf16[1,16,1024]{2,1,0:T(8,128)(2,1)S(1)} %collective-permute-done, bf16[1,16,1024]{2,1,0:T(8,128)(2,1)} %param.16), kind=kLoop, calls=%fused_computation.10 | loop fusion | flops 196608 | bytes 262144 | tf_op jit(solution)/shard_map/broadcast_in_dim | solution.py:241
  15.7 2.5 %collective-permute-start.7 = (bf16[1,4,16,1024]{3,2,1,0:T(8,128)(2,1)S(1)}, bf16[1,4,16,1024]{3,2,1,0:T(8,128)(2,1)S(1)}, u32[]{:S(2)}, u32[]{:S(2)}) collective-permute-start(bf16[1,4,16,1024]{3,2,1,0:T(8,128)(2,1)S(1)} %maximum_bitcast_fusion), channel_id=1, source_target_pairs={{0,24},{4,28},{8,16},{12,20},{16,8},{20,12},{24,0},{28,4},{1,25},{... | collective-permute-start | bytes 393224 | tf_op jit(solution)/shard_map/ppermute | solution.py:213
  18.2 0.5 collective-permute-start.6
  18.7 0.5 collective-permute-start.5
  19.2 1.0 %select_reduce_fusion.1 = s32[8,8]{1,0:T(8,128)S(1)} fusion(s32[8]{0:T(128)} %param.19, s32[8]{0:T(128)} %bitcast.51, s32[8]{0:T(128)} %bitcast.52, pred[8]{0:T(512)(128)(4,1)S(1)} %get-tuple-element.61, pred[8]{0:T(512)(128)(4,1)S(1)} %get-tuple-element.62, pred[8]{0:T(512)(128)(4,1)S(1)} %get-tuple-element.63, pred[8]{0:T(512)(128)(4,1)S(1)} %get-tuple-element.64), kind=kLoop, calls=%fused_computation.30 | loop fusion | flops 6592 | bytes 384 | tf_op jit(solution)/shard_map/reduce_sum | solution.py:198
  20.3 0.1 compare_and_fusion
  20.4 1.0 %copy.13 = bf16[128,512]{0,1:T(8,128)(2,1)S(1)} copy(bf16[128,512]{1,0:T(8,128)(2,1)} %param.11) | data formatting | bytes 262144 | tf_op jit(solution)/shard_map/optimization_barrier | solution.py:242
  21.4 0.1 select_reduce_fusion.facts_ref.refs_0_
  21.5 0.3 layout.1
  21.8 0.0 copy-start.3
  21.8 2.2 %attention_0.1.refs_2_ = bf16[2048,128]{1,0:T(8,128)(2,1)S(1)} custom-call(bf16[320,512]{1,0:T(8,128)(2,1)S(1)} %get-tuple-element.28.k_all, bf16[320,512]{1,0:T(8,128)(2,1)S(1)} %get-tuple-element.29.v_all, bf16[512,320]{1,0:T(8,128)(2,1)S(1)} %get-tuple-element.30.k_turned, f32[320,128]{1,0:T(8,128)S(1)} %get-tuple-element.31.bias, ...), custom_call_target="tpu_custom_call" | custom-call | flops 503316480 | bytes 2097152 | tf_op jit(solution)/shard_map/attention_0/pallas_call | solution.py:277
  24.1 0.1 collective-permute-start.8
  24.2 0.0 copy-start.2
  24.2 2.5 %attention_1.1 = (bf16[2048,128]{1,0:T(8,128)(2,1)S(1)}, bf16[4,4,16,1024]{3,2,1,0:T(8,128)(2,1)S(1)}, bf16[4,4,16,1024]{3,2,1,0:T(8,128)(2,1)S(1)}) custom-call(bf16[320,512]{1,0:T(8,128)(2,1)S(1)} %get-tuple-element.28.k_all, bf16[320,512]{1,0:T(8,128)(2,1)S(1)} %get-tuple-element.29.v_all, bf16[512,320]{1,0:T(8,128)(2,1)S(1)} %get-tuple-element.30.k_turned, ...), custom_call_target="tpu_custom_call" | custom-call | flops 503316480 | bytes 2097152 | tf_op jit(solution)/shard_map/attention_1/pallas_call | solution.py:277
  26.7 0.5 collective-permute-start.16
  27.3 0.4 rank_gradient.1.rank_ref
  27.7 0.7 %down_parts.1 = (bf16[4,4,16,2048]{3,2,1,0:T(8,128)(2,1)S(1)}, bf16[4,4,16,2048]{3,2,1,0:T(8,128)(2,1)S(1)}) custom-call(s32[8,128]{1,0:T(8,128)S(1)} %select_reduce_fusion.facts_ref.refs_0_, bf16[128,8192]{1,0:T(8,128)(2,1)S(1)} %copy-done.2, bf16[16,128]{1,0:T(8,128)(2,1)S(1)} %rank_gradient.1.rank_ref), custom_call_target="tpu_custom_call" | custom-call | flops 268435456 | bytes 8388608 | tf_op jit(solution)/shard_map/down_parts/pallas_call | solution.py:317
  28.4 0.1 collective-permute-start.9
  28.6 0.2 collective-permute-done.16
  28.8 0.2 add_convert_fusion
  29.0 1.5 %collective-permute-start.17 = (bf16[4,16,1024]{2,1,0:T(8,128)(2,1)S(1)}, bf16[4,16,1024]{2,1,0:T(8,128)(2,1)S(1)}, u32[]{:S(2)}, u32[]{:S(2)}) collective-permute-start(bf16[4,16,1024]{2,1,0:T(8,128)(2,1)S(1)} %get-tuple-element.50), channel_id=1, source_target_pairs={{0,1},{1,0},{2,3},{3,2},{4,5},{5,4},{6,7},{7,6},{8,9},{9,8},{10,11... | collective-permute-start | bytes 393224 | tf_op jit(solution)/shard_map/ppermute | solution.py:209
  30.5 2.9 %collective-permute-start.19 = (bf16[4,16,1024]{2,1,0:T(8,128)(2,1)S(1)}, bf16[4,16,1024]{2,1,0:T(8,128)(2,1)S(1)}, u32[]{:S(2)}, u32[]{:S(2)}) collective-permute-start(bf16[4,16,1024]{2,1,0:T(8,128)(2,1)S(1)} %get-tuple-element.51), channel_id=1, source_target_pairs={{0,3},{1,2},{2,1},{3,0},{4,7},{5,6},{6,5},{7,4},{8,11},{9,10},{10,... | collective-permute-start | bytes 393224 | tf_op jit(solution)/shard_map/ppermute | solution.py:209
  33.4 0.5 collective-permute-start.18
  33.9 0.2 core_sum.1
  34.2 1.6 %collective-permute-start.10 = (bf16[4,16,2048]{2,1,0:T(8,128)(2,1)S(1)}, bf16[4,16,2048]{2,1,0:T(8,128)(2,1)S(1)}, u32[]{:S(2)}, u32[]{:S(2)}) collective-permute-start(bf16[4,16,2048]{2,1,0:T(8,128)(2,1)S(1)} %get-tuple-element.45), channel_id=1, source_target_pairs={{0,8},{4,12},{8,0},{12,4},{16,24},{20,28},{24,16},{28,20},{1,9},{5... | collective-permute-start | bytes 786440 | tf_op jit(solution)/shard_map/ppermute | solution.py:213
  35.7 1.5 %collective-permute-start.11 = (bf16[4,16,2048]{2,1,0:T(8,128)(2,1)S(1)}, bf16[4,16,2048]{2,1,0:T(8,128)(2,1)S(1)}, u32[]{:S(2)}, u32[]{:S(2)}) collective-permute-start(bf16[4,16,2048]{2,1,0:T(8,128)(2,1)S(1)} %get-tuple-element.46), channel_id=1, source_target_pairs={{0,24},{4,28},{8,16},{12,20},{16,8},{20,12},{24,0},{28,4},{1,25},{... | collective-permute-start | bytes 786440 | tf_op jit(solution)/shard_map/ppermute | solution.py:213
  37.2 0.5 collective-permute-start.12
  37.7 2.9 %collective-permute-done.19 = bf16[4,16,1024]{2,1,0:T(8,128)(2,1)S(1)} collective-permute-done((bf16[4,16,1024]{2,1,0:T(8,128)(2,1)S(1)}, bf16[4,16,1024]{2,1,0:T(8,128)(2,1)S(1)}, u32[]{:S(2)}, u32[]{:S(2)}) %collective-permute-start.19) | collective-permute-done | bytes 131104 | tf_op jit(solution)/shard_map/ppermute | solution.py:209
  40.6 5.5 %collective-permute-done.18 = bf16[4,16,1024]{2,1,0:T(8,128)(2,1)S(1)} collective-permute-done((bf16[4,16,1024]{2,1,0:T(8,128)(2,1)S(1)}, bf16[4,16,1024]{2,1,0:T(8,128)(2,1)S(1)}, u32[]{:S(2)}, u32[]{:S(2)}) %collective-permute-start.18) | collective-permute-done | bytes 131104 | tf_op jit(solution)/shard_map/ppermute | solution.py:209
  46.1 0.1 fusion.2
  46.2 1.6 %collective-permute-start.20 = (bf16[16,1024]{1,0:T(8,128)(2,1)S(1)}, bf16[16,1024]{1,0:T(8,128)(2,1)S(1)}, u32[]{:S(2)}, u32[]{:S(2)}) collective-permute-start(bf16[16,1024]{1,0:T(8,128)(2,1)S(1)} %get-tuple-element.56), channel_id=1, source_target_pairs={{0,8},{4,12},{8,0},{12,4},{16,24},{20,28},{24,16},{28,20},{1,9},{5... | collective-permute-start | bytes 98312 | tf_op jit(solution)/shard_map/ppermute | solution.py:213
  47.7 1.5 %collective-permute-start.22 = (bf16[16,1024]{1,0:T(8,128)(2,1)S(1)}, bf16[16,1024]{1,0:T(8,128)(2,1)S(1)}, u32[]{:S(2)}, u32[]{:S(2)}) collective-permute-start(bf16[16,1024]{1,0:T(8,128)(2,1)S(1)} %get-tuple-element.57), channel_id=1, source_target_pairs={{0,24},{4,28},{8,16},{12,20},{16,8},{20,12},{24,0},{28,4},{1,25},{... | collective-permute-start | bytes 98312 | tf_op jit(solution)/shard_map/ppermute | solution.py:213
  49.2 0.5 collective-permute-start.21
  49.7 0.6 collective-permute-done.12
  50.3 0.1 add_convert_fusion.1
  50.5 5.9 %collective-permute-start.13 = (bf16[16,2048]{1,0:T(8,128)(2,1)S(1)}, bf16[16,2048]{1,0:T(8,128)(2,1)S(1)}, u32[]{:S(2)}, u32[]{:S(2)}) collective-permute-start(bf16[16,2048]{1,0:T(8,128)(2,1)S(1)} %get-tuple-element.53), channel_id=1, source_target_pairs={{0,3},{1,2},{2,1},{3,0},{4,7},{5,6},{6,5},{7,4},{8,11},{9,10},{10,... | collective-permute-start | bytes 196616 | tf_op jit(solution)/shard_map/ppermute | solution.py:209
  56.3 0.6 %collective-permute-start.14 = (bf16[16,2048]{1,0:T(8,128)(2,1)S(1)}, bf16[16,2048]{1,0:T(8,128)(2,1)S(1)}, u32[]{:S(2)}, u32[]{:S(2)}) collective-permute-start(bf16[16,2048]{1,0:T(8,128)(2,1)S(1)} %get-tuple-element.55), channel_id=1, source_target_pairs={{0,1},{1,0},{2,3},{3,2},{4,5},{5,4},{6,7},{7,6},{8,9},{9,8},{10,11... | collective-permute-start | bytes 196616 | tf_op jit(solution)/shard_map/ppermute | solution.py:209
  57.0 0.7 %fusion.10 = f32[1,16,1024]{2,1,0:T(8,128)} fusion(bf16[16,1024]{1,0:T(8,128)(2,1)S(1)} %collective-permute-done.22, bf16[16,1024]{1,0:T(8,128)(2,1)S(1)} %collective-permute-done.21, bf16[16,1024]{1,0:T(8,128)(2,1)S(1)} %collective-permute-done.20, bf16[4,16,1024]{2,1,0:T(8,128)(2,1)S(1)} %fusion.2), kind=kLoop, calls=%fused_computation.24 | loop fusion | flops 131072 | bytes 196608 | tf_op jit(solution)/shard_map/mul | solution.py:350
  57.6 1.0 %collective-permute-done.13 = bf16[16,2048]{1,0:T(8,128)(2,1)S(1)} collective-permute-done((bf16[16,2048]{1,0:T(8,128)(2,1)S(1)}, bf16[16,2048]{1,0:T(8,128)(2,1)S(1)}, u32[]{:S(2)}, u32[]{:S(2)}) %collective-permute-start.13) | collective-permute-done | bytes 65568 | tf_op jit(solution)/shard_map/ppermute | solution.py:209
  58.7 2.8 %collective-permute-done.15 = bf16[16,2048]{1,0:T(8,128)(2,1)S(1)} collective-permute-done((bf16[16,2048]{1,0:T(8,128)(2,1)S(1)}, bf16[16,2048]{1,0:T(8,128)(2,1)S(1)}, u32[]{:S(2)}, u32[]{:S(2)}) %collective-permute-start.15) | collective-permute-done | bytes 65568 | tf_op jit(solution)/shard_map/ppermute | solution.py:209
  61.5 0.7 %fusion.6 = f32[1,2048,16]{1,2,0:T(8,128)} fusion(bf16[16,2048]{1,0:T(8,128)(2,1)S(1)} %collective-permute-done.15, bf16[16,2048]{1,0:T(8,128)(2,1)S(1)} %collective-permute-done.14, bf16[16,2048]{1,0:T(8,128)(2,1)S(1)} %collective-permute-done.13, bf16[4,16,2048]{2,1,0:T(8,128)(2,1)S(1)} %add_convert_fusion.1), kind=kLoop, calls=%fused_computation.15 | loop fusion | flops 262144 | bytes 393216 | tf_op jit(solution)/shard_map/mul | solution.py:350
  (36 shorter events, 0.2 us)
Async XLA Ops:
  0.6 21.1 %copy-start.1 = (bf16[128,4096]{1,0:T(8,128)(2,1)S(1)}, bf16[128,4096]{1,0:T(8,128)(2,1)}, u32[]{:S(2)}) copy-start(bf16[128,4096]{1,0:T(8,128)(2,1)} %g_hbm.3) | copy-start | bytes 3145732
  0.6 21.1 %copy-start = (bf16[128,4096]{1,0:T(8,128)(2,1)S(1)}, bf16[128,4096]{1,0:T(8,128)(2,1)}, u32[]{:S(2)}) copy-start(bf16[128,4096]{1,0:T(8,128)(2,1)} %q_hbm.3) | copy-start | bytes 3145732
  0.6 14.2 %collective-permute-start.1 = (bf16[1,16,1024]{2,1,0:T(8,128)(2,1)}, bf16[1,16,1024]{2,1,0:T(8,128)(2,1)S(1)}, u32[]{:S(2)}, u32[]{:S(2)}) collective-permute-start(bf16[1,16,1024]{2,1,0:T(8,128)(2,1)} %param.16), channel_id=1, source_target_pairs={{0,2},{1,3},{2,0},{3,1},{4,6},{5,7},{6,4},{7,5},{8,10},{9,11},{10,... | collective-permute-start | bytes 98312 | tf_op jit(solution)/shard_map/ppermute | solution.py:205
  4.8 10.1 %collective-permute-start = (bf16[1,16,1024]{2,1,0:T(8,128)(2,1)}, bf16[1,16,1024]{2,1,0:T(8,128)(2,1)S(1)}, u32[]{:S(2)}, u32[]{:S(2)}) collective-permute-start(bf16[1,16,1024]{2,1,0:T(8,128)(2,1)} %param.16), channel_id=1, source_target_pairs={{0,1},{1,2},{2,3},{3,0},{4,5},{5,6},{6,7},{7,4},{8,9},{9,10},{10,1... | collective-permute-start | bytes 98312 | tf_op jit(solution)/shard_map/ppermute | solution.py:205
  6.3 8.6 %collective-permute-start.2 = (bf16[1,16,1024]{2,1,0:T(8,128)(2,1)}, bf16[1,16,1024]{2,1,0:T(8,128)(2,1)S(1)}, u32[]{:S(2)}, u32[]{:S(2)}) collective-permute-start(bf16[1,16,1024]{2,1,0:T(8,128)(2,1)} %param.16), channel_id=1, source_target_pairs={{0,3},{1,0},{2,1},{3,2},{4,7},{5,4},{6,5},{7,6},{8,11},{9,8},{10,9... | collective-permute-start | bytes 98312 | tf_op jit(solution)/shard_map/ppermute | solution.py:205
  10.4 11.1 %collective-permute-start.4 = (bf16[128,1024]{1,0:T(8,128)(2,1)S(1)}, bf16[128,1024]{1,0:T(8,128)(2,1)S(1)}, u32[]{:S(2)}, u32[]{:S(2)}) collective-permute-start(bf16[128,1024]{1,0:T(8,128)(2,1)S(1)} %constant_dynamic-update-slice_fusion.refs_3_), channel_id=1, source_target_pairs={{0,1},{1,2},{2,3},{4,5},{5,6},{6,7},{8,9},{9,10},{10,11},{12,13},{... | collective-permute-start | bytes 786440 | tf_op jit(solution)/shard_map/ppermute | solution.py:237
  12.1 9.3 %collective-permute-start.3 = (bf16[64,1024]{1,0:T(8,128)(2,1)S(1)}, bf16[64,1024]{1,0:T(8,128)(2,1)S(1)}, u32[]{:S(2)}, u32[]{:S(2)}) collective-permute-start(bf16[64,1024]{1,0:T(8,128)(2,1)S(1)} %slice.60), channel_id=1, source_target_pairs={{0,2},{1,3},{4,6},{5,7},{8,10},{9,11},{12,14},{13,15},{16,18},{17,... | collective-permute-start | bytes 393224 | tf_op jit(solution)/shard_map/ppermute | solution.py:237
  15.7 8.3 %collective-permute-start.7 = (bf16[1,4,16,1024]{3,2,1,0:T(8,128)(2,1)S(1)}, bf16[1,4,16,1024]{3,2,1,0:T(8,128)(2,1)S(1)}, u32[]{:S(2)}, u32[]{:S(2)}) collective-permute-start(bf16[1,4,16,1024]{3,2,1,0:T(8,128)(2,1)S(1)} %maximum_bitcast_fusion), channel_id=1, source_target_pairs={{0,24},{4,28},{8,16},{12,20},{16,8},{20,12},{24,0},{28,4},{1,25},{... | collective-permute-start | bytes 393224 | tf_op jit(solution)/shard_map/ppermute | solution.py:213
  18.2 5.8 %collective-permute-start.6 = (bf16[1,4,16,1024]{3,2,1,0:T(8,128)(2,1)S(1)}, bf16[1,4,16,1024]{3,2,1,0:T(8,128)(2,1)S(1)}, u32[]{:S(2)}, u32[]{:S(2)}) collective-permute-start(bf16[1,4,16,1024]{3,2,1,0:T(8,128)(2,1)S(1)} %maximum_bitcast_fusion), channel_id=1, source_target_pairs={{0,16},{4,20},{8,24},{12,28},{16,0},{20,4},{24,8},{28,12},{1,17},{... | collective-permute-start | bytes 393224 | tf_op jit(solution)/shard_map/ppermute | solution.py:213
  18.7 5.3 %collective-permute-start.5 = (bf16[1,4,16,1024]{3,2,1,0:T(8,128)(2,1)S(1)}, bf16[1,4,16,1024]{3,2,1,0:T(8,128)(2,1)S(1)}, u32[]{:S(2)}, u32[]{:S(2)}) collective-permute-start(bf16[1,4,16,1024]{3,2,1,0:T(8,128)(2,1)S(1)} %maximum_bitcast_fusion), channel_id=1, source_target_pairs={{0,8},{4,12},{8,0},{12,4},{16,24},{20,28},{24,16},{28,20},{1,9},{5... | collective-permute-start | bytes 393224 | tf_op jit(solution)/shard_map/ppermute | solution.py:213
  21.8 2.4 %copy-start.3 = (bf16[128,16]{0,1:T(8,128)(2,1)S(1)}, bf16[128,16]{0,1:T(8,128)(2,1)}, u32[]{:S(2)}) copy-start(bf16[128,16]{0,1:T(8,128)(2,1)} %param.15) | copy-start | bytes 12292
  24.1 2.6 %collective-permute-start.8 = (bf16[4,4,16,1024]{3,2,1,0:T(8,128)(2,1)S(1)}, bf16[4,4,16,1024]{3,2,1,0:T(8,128)(2,1)S(1)}, u32[]{:S(2)}, u32[]{:S(2)}) collective-permute-start(bf16[4,4,16,1024]{3,2,1,0:T(8,128)(2,1)S(1)} %constant_dynamic-update-slice_fusion.2.refs_0_), channel_id=1, source_target_pairs={{0,4},{4,0},{8,12},{12,8},{16,20},{20,16},{24,28},{28,24},{1,5},{5... | collective-permute-start | bytes 1572872 | tf_op jit(solution)/shard_map/ppermute | solution.py:213
  24.2 3.5 %copy-start.2 = (bf16[128,8192]{1,0:T(8,128)(2,1)S(1)}, bf16[128,8192]{1,0:T(8,128)(2,1)}, u32[]{:S(2)}) copy-start(bf16[128,8192]{1,0:T(8,128)(2,1)} %x_ref.1) | copy-start | bytes 6291460
  26.7 2.1 %collective-permute-start.16 = (bf16[4,4,16,1024]{3,2,1,0:T(8,128)(2,1)S(1)}, bf16[4,4,16,1024]{3,2,1,0:T(8,128)(2,1)S(1)}, u32[]{:S(2)}, u32[]{:S(2)}) collective-permute-start(bf16[4,4,16,1024]{3,2,1,0:T(8,128)(2,1)S(1)} %get-tuple-element.49), channel_id=1, source_target_pairs={{0,4},{4,0},{8,12},{12,8},{16,20},{20,16},{24,28},{28,24},{1,5},{5... | collective-permute-start | bytes 1572872 | tf_op jit(solution)/shard_map/ppermute | solution.py:213
  28.4 5.5 %collective-permute-start.9 = (bf16[4,4,16,2048]{3,2,1,0:T(8,128)(2,1)S(1)}, bf16[4,4,16,2048]{3,2,1,0:T(8,128)(2,1)S(1)}, u32[]{:S(2)}, u32[]{:S(2)}) collective-permute-start(bf16[4,4,16,2048]{3,2,1,0:T(8,128)(2,1)S(1)} %get-tuple-element.43), channel_id=1, source_target_pairs={{0,4},{4,0},{8,12},{12,8},{16,20},{20,16},{24,28},{28,24},{1,5},{5... | collective-permute-start | bytes 3145736 | tf_op jit(solution)/shard_map/ppermute | solution.py:213
  29.0 8.2 %collective-permute-start.17 = (bf16[4,16,1024]{2,1,0:T(8,128)(2,1)S(1)}, bf16[4,16,1024]{2,1,0:T(8,128)(2,1)S(1)}, u32[]{:S(2)}, u32[]{:S(2)}) collective-permute-start(bf16[4,16,1024]{2,1,0:T(8,128)(2,1)S(1)} %get-tuple-element.50), channel_id=1, source_target_pairs={{0,1},{1,0},{2,3},{3,2},{4,5},{5,4},{6,7},{7,6},{8,9},{9,8},{10,11... | collective-permute-start | bytes 393224 | tf_op jit(solution)/shard_map/ppermute | solution.py:209
  30.5 10.1 %collective-permute-start.19 = (bf16[4,16,1024]{2,1,0:T(8,128)(2,1)S(1)}, bf16[4,16,1024]{2,1,0:T(8,128)(2,1)S(1)}, u32[]{:S(2)}, u32[]{:S(2)}) collective-permute-start(bf16[4,16,1024]{2,1,0:T(8,128)(2,1)S(1)} %get-tuple-element.51), channel_id=1, source_target_pairs={{0,3},{1,2},{2,1},{3,0},{4,7},{5,6},{6,5},{7,4},{8,11},{9,10},{10,... | collective-permute-start | bytes 393224 | tf_op jit(solution)/shard_map/ppermute | solution.py:209
  33.4 12.7 %collective-permute-start.18 = (bf16[4,16,1024]{2,1,0:T(8,128)(2,1)S(1)}, bf16[4,16,1024]{2,1,0:T(8,128)(2,1)S(1)}, u32[]{:S(2)}, u32[]{:S(2)}) collective-permute-start(bf16[4,16,1024]{2,1,0:T(8,128)(2,1)S(1)} %get-tuple-element.52), channel_id=1, source_target_pairs={{0,2},{1,3},{2,0},{3,1},{4,6},{5,7},{6,4},{7,5},{8,10},{9,11},{10,... | collective-permute-start | bytes 393224 | tf_op jit(solution)/shard_map/ppermute | solution.py:209
  34.2 15.1 %collective-permute-start.10 = (bf16[4,16,2048]{2,1,0:T(8,128)(2,1)S(1)}, bf16[4,16,2048]{2,1,0:T(8,128)(2,1)S(1)}, u32[]{:S(2)}, u32[]{:S(2)}) collective-permute-start(bf16[4,16,2048]{2,1,0:T(8,128)(2,1)S(1)} %get-tuple-element.45), channel_id=1, source_target_pairs={{0,8},{4,12},{8,0},{12,4},{16,24},{20,28},{24,16},{28,20},{1,9},{5... | collective-permute-start | bytes 786440 | tf_op jit(solution)/shard_map/ppermute | solution.py:213
  35.7 14.0 %collective-permute-start.11 = (bf16[4,16,2048]{2,1,0:T(8,128)(2,1)S(1)}, bf16[4,16,2048]{2,1,0:T(8,128)(2,1)S(1)}, u32[]{:S(2)}, u32[]{:S(2)}) collective-permute-start(bf16[4,16,2048]{2,1,0:T(8,128)(2,1)S(1)} %get-tuple-element.46), channel_id=1, source_target_pairs={{0,24},{4,28},{8,16},{12,20},{16,8},{20,12},{24,0},{28,4},{1,25},{... | collective-permute-start | bytes 786440 | tf_op jit(solution)/shard_map/ppermute | solution.py:213
  37.2 13.1 %collective-permute-start.12 = (bf16[4,16,2048]{2,1,0:T(8,128)(2,1)S(1)}, bf16[4,16,2048]{2,1,0:T(8,128)(2,1)S(1)}, u32[]{:S(2)}, u32[]{:S(2)}) collective-permute-start(bf16[4,16,2048]{2,1,0:T(8,128)(2,1)S(1)} %get-tuple-element.47), channel_id=1, source_target_pairs={{0,16},{4,20},{8,24},{12,28},{16,0},{20,4},{24,8},{28,12},{1,17},{... | collective-permute-start | bytes 786440 | tf_op jit(solution)/shard_map/ppermute | solution.py:213
  46.2 10.1 %collective-permute-start.20 = (bf16[16,1024]{1,0:T(8,128)(2,1)S(1)}, bf16[16,1024]{1,0:T(8,128)(2,1)S(1)}, u32[]{:S(2)}, u32[]{:S(2)}) collective-permute-start(bf16[16,1024]{1,0:T(8,128)(2,1)S(1)} %get-tuple-element.56), channel_id=1, source_target_pairs={{0,8},{4,12},{8,0},{12,4},{16,24},{20,28},{24,16},{28,20},{1,9},{5... | collective-permute-start | bytes 98312 | tf_op jit(solution)/shard_map/ppermute | solution.py:213
  47.7 9.2 %collective-permute-start.22 = (bf16[16,1024]{1,0:T(8,128)(2,1)S(1)}, bf16[16,1024]{1,0:T(8,128)(2,1)S(1)}, u32[]{:S(2)}, u32[]{:S(2)}) collective-permute-start(bf16[16,1024]{1,0:T(8,128)(2,1)S(1)} %get-tuple-element.57), channel_id=1, source_target_pairs={{0,24},{4,28},{8,16},{12,20},{16,8},{20,12},{24,0},{28,4},{1,25},{... | collective-permute-start | bytes 98312 | tf_op jit(solution)/shard_map/ppermute | solution.py:213
  49.2 7.7 %collective-permute-start.21 = (bf16[16,1024]{1,0:T(8,128)(2,1)S(1)}, bf16[16,1024]{1,0:T(8,128)(2,1)S(1)}, u32[]{:S(2)}, u32[]{:S(2)}) collective-permute-start(bf16[16,1024]{1,0:T(8,128)(2,1)S(1)} %get-tuple-element.58), channel_id=1, source_target_pairs={{0,16},{4,20},{8,24},{12,28},{16,0},{20,4},{24,8},{28,12},{1,17},{... | collective-permute-start | bytes 98312 | tf_op jit(solution)/shard_map/ppermute | solution.py:213
  50.5 8.2 %collective-permute-start.13 = (bf16[16,2048]{1,0:T(8,128)(2,1)S(1)}, bf16[16,2048]{1,0:T(8,128)(2,1)S(1)}, u32[]{:S(2)}, u32[]{:S(2)}) collective-permute-start(bf16[16,2048]{1,0:T(8,128)(2,1)S(1)} %get-tuple-element.53), channel_id=1, source_target_pairs={{0,3},{1,2},{2,1},{3,0},{4,7},{5,6},{6,5},{7,4},{8,11},{9,10},{10,... | collective-permute-start | bytes 196616 | tf_op jit(solution)/shard_map/ppermute | solution.py:209
  56.3 5.2 %collective-permute-start.15 = (bf16[16,2048]{1,0:T(8,128)(2,1)S(1)}, bf16[16,2048]{1,0:T(8,128)(2,1)S(1)}, u32[]{:S(2)}, u32[]{:S(2)}) collective-permute-start(bf16[16,2048]{1,0:T(8,128)(2,1)S(1)} %get-tuple-element.54), channel_id=1, source_target_pairs={{0,2},{1,3},{2,0},{3,1},{4,6},{5,7},{6,4},{7,5},{8,10},{9,11},{10,... | collective-permute-start | bytes 196616 | tf_op jit(solution)/shard_map/ppermute | solution.py:209
  56.3 5.2 %collective-permute-start.14 = (bf16[16,2048]{1,0:T(8,128)(2,1)S(1)}, bf16[16,2048]{1,0:T(8,128)(2,1)S(1)}, u32[]{:S(2)}, u32[]{:S(2)}) collective-permute-start(bf16[16,2048]{1,0:T(8,128)(2,1)S(1)} %get-tuple-element.55), channel_id=1, source_target_pairs={{0,1},{1,0},{2,3},{3,2},{4,5},{5,4},{6,7},{7,6},{8,9},{9,8},{10,11... | collective-permute-start | bytes 196616 | tf_op jit(solution)/shard_map/ppermute | solution.py:209

commit v18 on v16

--- a/solution.py
+++ b/solution.py
@@ -338,8 +338,11 @@
             cost_estimate=pl.CostEstimate(flops=0, bytes_accessed=SUM_BYTES, transcendentals=0),
             name="core_sum",
         )(down[0], partnered(down[1], n_seq, 1))
-        up = over_chips(over_z(over_cores(up, n_seq), n_head, (1, 2, 3)).astype(BF16), n_seq)
+        up = over_z(over_cores(up, n_seq), n_head, (1, 2, 3)).astype(BF16)
         down = over_z(over_chips(down, n_seq).astype(BF16), n_head, (3, 1, 2))
+        up_got = [partnered(up[m], n_seq, 2 * m) for m in range(1, n_seq // 2)]
+        up_got, _ = lax.optimization_barrier((up_got, down))
+        up = added(up[0], up_got)
     else:
         up = lax.all_to_all(up[0], "head", split_axis=0, concat_axis=0, tiled=True)
         up = spread(jnp.sum(up.astype(F32), axis=0), segment_adapter, owner, n_seq)

time: 59.1 us -> 61.3 us (1.037)
  waiting for transfers between devices: 11.8 us -> 14 us
    ppermute x12, waiting for transfers between devices: 0.27 us -> 5.23 us  [partnered(): return lax.ppermute(x, 'seq', [(i, i ^ bits) for i in range(n_seq)])]
    ppermute x6, waiting for transfers between devices: 11.5 us -> 8.72 us  [across(): return lax.ppermute(x, 'head', [(i, i ^ j) for i in range(n_head)])]
  transfers between devices with their start and end apart: 23 -> 23, of which waited for: 5 -> 8; matrix products, arithmetic and copies ran while one was open for 10% -> 10% of each run, Pallas kernels for 11% -> 10%
where the time goes in v18:
time: 61.3 us; the launch traced here: 61 us
  starting transfers between devices  33 us (54%)
  waiting for transfers between devices  14 us (23%)
  Pallas kernels  6.36 us (10%)
  other arithmetic  3.71 us (6%)
  local copies, waits for them, and re-layouts  2.98 us (5%)
  between operations  0.98 us (2%)
    ppermute x12, starting transfers between devices, partnered(): return lax.ppermute(x, 'seq', [(i, i ^ bits) for i in range(n_seq)])  11.4 us
    ppermute x6, starting transfers between devices, across(): return lax.ppermute(x, 'head', [(i, i ^ j) for i in range(n_head)])  9.35 us
    ppermute x6, waiting for transfers between devices, across(): return lax.ppermute(x, 'head', [(i, i ^ j) for i in range(n_head)])  8.72 us
    ppermute x3, starting transfers between devices, shifted(): lax.ppermute(x, 'head', [(i, (i + j) % n_head) for i in range(n_head)])  7.93 us
    ppermute x12, waiting for transfers between devices, partnered(): return lax.ppermute(x, 'seq', [(i, i ^ bits) for i in range(n_seq)])  5.23 us
    pallas_call x2, Pallas kernels, attention(): pl.pallas_call(functools.partial(attention_kernel, by_slot, h * n_kv, n_k...  4.71 us
    ppermute x2, starting transfers between devices, on_device(): parts.insert(0, lax.ppermute(own[tok - rows:], 'head', shift))  4.39 us
    mul x2, other arithmetic, on_device(): return (down.T[None] * ADAPTER_SCALE, up[None] * ADAPTER_SCALE)  1.35 us
  transfers between devices with their start and end apart: 23, of which 8 were waited for; matrix products, arithmetic and copies ran while one was open for 10% of the time, Pallas kernels for 10%

profile of v18, /device:TPU:0, one launch (start us, length us, event | category | flops | bytes accessed | tf_op | source)
XLA Modules:
  0.0 61.0 jit_solution(7028895173531396009)
XLA Ops:
  0.6 4.1 %collective-permute-start.1 = (bf16[1,16,1024]{2,1,0:T(8,128)(2,1)}, bf16[1,16,1024]{2,1,0:T(8,128)(2,1)S(1)}, u32[]{:S(2)}, u32[]{:S(2)}) collective-permute-start(bf16[1,16,1024]{2,1,0:T(8,128)(2,1)} %param.16), channel_id=1, source_target_pairs={{0,2},{1,3},{2,0},{3,1},{4,6},{5,7},{6,4},{7,5},{8,10},{9,11},{10,... | collective-permute-start | bytes 98312 | tf_op jit(solution)/shard_map/ppermute | solution.py:205
  4.8 1.6 %collective-permute-start = (bf16[1,16,1024]{2,1,0:T(8,128)(2,1)}, bf16[1,16,1024]{2,1,0:T(8,128)(2,1)S(1)}, u32[]{:S(2)}, u32[]{:S(2)}) collective-permute-start(bf16[1,16,1024]{2,1,0:T(8,128)(2,1)} %param.16), channel_id=1, source_target_pairs={{0,1},{1,2},{2,3},{3,0},{4,5},{5,6},{6,7},{7,4},{8,9},{9,10},{10,1... | collective-permute-start | bytes 98312 | tf_op jit(solution)/shard_map/ppermute | solution.py:205
  6.3 2.2 %collective-permute-start.2 = (bf16[1,16,1024]{2,1,0:T(8,128)(2,1)}, bf16[1,16,1024]{2,1,0:T(8,128)(2,1)S(1)}, u32[]{:S(2)}, u32[]{:S(2)}) collective-permute-start(bf16[1,16,1024]{2,1,0:T(8,128)(2,1)} %param.16), channel_id=1, source_target_pairs={{0,3},{1,0},{2,1},{3,2},{4,7},{5,4},{6,5},{7,6},{8,11},{9,8},{10,9... | collective-permute-start | bytes 98312 | tf_op jit(solution)/shard_map/ppermute | solution.py:205
  8.6 0.9 %constant_dynamic-update-slice_fusion.1 = bf16[128,1024]{1,0:T(8,128)(2,1)S(1)} fusion(bf16[128,512]{1,0:T(8,128)(2,1)} %param.11), kind=kLoop, calls=%fused_computation.38 | loop fusion | bytes 262144
  9.5 0.9 %constant_dynamic-update-slice_fusion.refs_3_ = bf16[128,1024]{1,0:T(8,128)(2,1)S(1)} fusion(bf16[128,1024]{1,0:T(8,128)(2,1)S(1)} %constant_dynamic-update-slice_fusion.1, bf16[128,512]{1,0:T(8,128)(2,1)} %param.12), kind=kLoop, calls=%fused_computation.37 | loop fusion | bytes 262144 | tf_op jit(solution)/shard_map/concatenate | solution.py:233
  10.4 1.7 %collective-permute-start.4 = (bf16[128,1024]{1,0:T(8,128)(2,1)S(1)}, bf16[128,1024]{1,0:T(8,128)(2,1)S(1)}, u32[]{:S(2)}, u32[]{:S(2)}) collective-permute-start(bf16[128,1024]{1,0:T(8,128)(2,1)S(1)} %constant_dynamic-update-slice_fusion.refs_3_), channel_id=1, source_target_pairs={{0,1},{1,2},{2,3},{4,5},{5,6},{6,7},{8,9},{9,10},{10,11},{12,13},{... | collective-permute-start | bytes 786440 | tf_op jit(solution)/shard_map/ppermute | solution.py:237
  12.1 2.7 %collective-permute-start.3 = (bf16[64,1024]{1,0:T(8,128)(2,1)S(1)}, bf16[64,1024]{1,0:T(8,128)(2,1)S(1)}, u32[]{:S(2)}, u32[]{:S(2)}) collective-permute-start(bf16[64,1024]{1,0:T(8,128)(2,1)S(1)} %slice.60), channel_id=1, source_target_pairs={{0,2},{1,3},{4,6},{5,7},{8,10},{9,11},{12,14},{13,15},{16,18},{17,... | collective-permute-start | bytes 393224 | tf_op jit(solution)/shard_map/ppermute | solution.py:237
  14.9 0.8 %maximum_bitcast_fusion = bf16[1,4,16,1024]{3,2,1,0:T(8,128)(2,1)S(1)} fusion(bf16[1,16,1024]{2,1,0:T(8,128)(2,1)S(1)} %collective-permute-done.2, bf16[1,16,1024]{2,1,0:T(8,128)(2,1)S(1)} %collective-permute-done.1, bf16[1,16,1024]{2,1,0:T(8,128)(2,1)S(1)} %collective-permute-done, bf16[1,16,1024]{2,1,0:T(8,128)(2,1)} %param.16), kind=kLoop, calls=%fused_computation.10 | loop fusion | flops 196608 | bytes 262144 | tf_op jit(solution)/shard_map/broadcast_in_dim | solution.py:241
  15.7 2.5 %collective-permute-start.7 = (bf16[1,4,16,1024]{3,2,1,0:T(8,128)(2,1)S(1)}, bf16[1,4,16,1024]{3,2,1,0:T(8,128)(2,1)S(1)}, u32[]{:S(2)}, u32[]{:S(2)}) collective-permute-start(bf16[1,4,16,1024]{3,2,1,0:T(8,128)(2,1)S(1)} %maximum_bitcast_fusion), channel_id=1, source_target_pairs={{0,24},{4,28},{8,16},{12,20},{16,8},{20,12},{24,0},{28,4},{1,25},{... | collective-permute-start | bytes 393224 | tf_op jit(solution)/shard_map/ppermute | solution.py:213
  18.2 0.5 collective-permute-start.6
  18.7 0.5 collective-permute-start.5
  19.2 1.0 %select_reduce_fusion.1 = s32[8,8]{1,0:T(8,128)S(1)} fusion(s32[8]{0:T(128)} %param.19, s32[8]{0:T(128)} %bitcast.52, s32[8]{0:T(128)} %bitcast.53, pred[8]{0:T(512)(128)(4,1)S(1)} %get-tuple-element.69, pred[8]{0:T(512)(128)(4,1)S(1)} %get-tuple-element.70, pred[8]{0:T(512)(128)(4,1)S(1)} %get-tuple-element.71, pred[8]{0:T(512)(128)(4,1)S(1)} %get-tuple-element.72), kind=kLoop, calls=%fused_computation.29 | loop fusion | flops 6592 | bytes 384 | tf_op jit(solution)/shard_map/reduce_sum | solution.py:198
  20.3 0.1 compare_and_fusion
  20.4 1.0 %copy.13 = bf16[128,512]{0,1:T(8,128)(2,1)S(1)} copy(bf16[128,512]{1,0:T(8,128)(2,1)} %param.11) | data formatting | bytes 262144 | tf_op jit(solution)/shard_map/optimization_barrier | solution.py:242
  21.4 0.1 select_reduce_fusion.facts_ref.refs_0_
  21.5 0.3 layout.1
  21.8 2.2 %attention_0.1.refs_2_ = bf16[2048,128]{1,0:T(8,128)(2,1)S(1)} custom-call(bf16[320,512]{1,0:T(8,128)(2,1)S(1)} %get-tuple-element.31.k_all, bf16[320,512]{1,0:T(8,128)(2,1)S(1)} %get-tuple-element.32.v_all, bf16[512,320]{1,0:T(8,128)(2,1)S(1)} %get-tuple-element.33.k_turned, f32[320,128]{1,0:T(8,128)S(1)} %get-tuple-element.34.bias, ...), custom_call_target="tpu_custom_call" | custom-call | flops 503316480 | bytes 2097152 | tf_op jit(solution)/shard_map/attention_0/pallas_call | solution.py:277
  24.1 0.1 collective-permute-start.8
  24.2 2.5 %attention_1.1 = (bf16[2048,128]{1,0:T(8,128)(2,1)S(1)}, bf16[4,4,16,1024]{3,2,1,0:T(8,128)(2,1)S(1)}, bf16[4,4,16,1024]{3,2,1,0:T(8,128)(2,1)S(1)}) custom-call(bf16[320,512]{1,0:T(8,128)(2,1)S(1)} %get-tuple-element.31.k_all, bf16[320,512]{1,0:T(8,128)(2,1)S(1)} %get-tuple-element.32.v_all, bf16[512,320]{1,0:T(8,128)(2,1)S(1)} %get-tuple-element.33.k_turned, ...), custom_call_target="tpu_custom_call" | custom-call | flops 503316480 | bytes 2097152 | tf_op jit(solution)/shard_map/attention_1/pallas_call | solution.py:277
  26.7 0.5 collective-permute-start.16
  27.3 0.4 rank_gradient.1.rank_ref
  27.7 0.7 %down_parts.1 = (bf16[4,4,16,2048]{3,2,1,0:T(8,128)(2,1)S(1)}, bf16[4,4,16,2048]{3,2,1,0:T(8,128)(2,1)S(1)}) custom-call(s32[8,128]{1,0:T(8,128)S(1)} %select_reduce_fusion.facts_ref.refs_0_, bf16[128,8192]{1,0:T(8,128)(2,1)S(1)} %copy-done.2, bf16[16,128]{1,0:T(8,128)(2,1)S(1)} %rank_gradient.1.rank_ref), custom_call_target="tpu_custom_call" | custom-call | flops 268435456 | bytes 8388608 | tf_op jit(solution)/shard_map/down_parts/pallas_call | solution.py:317
  28.4 0.1 collective-permute-start.9
  28.6 0.2 collective-permute-done.16
  28.8 0.2 add_convert_fusion
  29.0 1.5 %collective-permute-start.17 = (bf16[4,16,1024]{2,1,0:T(8,128)(2,1)S(1)}, bf16[4,16,1024]{2,1,0:T(8,128)(2,1)S(1)}, u32[]{:S(2)}, u32[]{:S(2)}) collective-permute-start(bf16[4,16,1024]{2,1,0:T(8,128)(2,1)S(1)} %get-tuple-element.58), channel_id=1, source_target_pairs={{0,1},{1,0},{2,3},{3,2},{4,5},{5,4},{6,7},{7,6},{8,9},{9,8},{10,11... | collective-permute-start | bytes 393224 | tf_op jit(solution)/shard_map/ppermute | solution.py:209
  30.5 2.9 %collective-permute-start.19 = (bf16[4,16,1024]{2,1,0:T(8,128)(2,1)S(1)}, bf16[4,16,1024]{2,1,0:T(8,128)(2,1)S(1)}, u32[]{:S(2)}, u32[]{:S(2)}) collective-permute-start(bf16[4,16,1024]{2,1,0:T(8,128)(2,1)S(1)} %get-tuple-element.59), channel_id=1, source_target_pairs={{0,3},{1,2},{2,1},{3,0},{4,7},{5,6},{6,5},{7,4},{8,11},{9,10},{10,... | collective-permute-start | bytes 393224 | tf_op jit(solution)/shard_map/ppermute | solution.py:209
  33.4 0.5 collective-permute-start.18
  33.9 0.2 core_sum.1
  34.2 1.6 %collective-permute-start.10 = (bf16[4,16,2048]{2,1,0:T(8,128)(2,1)S(1)}, bf16[4,16,2048]{2,1,0:T(8,128)(2,1)S(1)}, u32[]{:S(2)}, u32[]{:S(2)}) collective-permute-start(bf16[4,16,2048]{2,1,0:T(8,128)(2,1)S(1)} %get-tuple-element.48), channel_id=1, source_target_pairs={{0,8},{4,12},{8,0},{12,4},{16,24},{20,28},{24,16},{28,20},{1,9},{5... | collective-permute-start | bytes 786440 | tf_op jit(solution)/shard_map/ppermute | solution.py:213
  35.7 1.5 %collective-permute-start.11 = (bf16[4,16,2048]{2,1,0:T(8,128)(2,1)S(1)}, bf16[4,16,2048]{2,1,0:T(8,128)(2,1)S(1)}, u32[]{:S(2)}, u32[]{:S(2)}) collective-permute-start(bf16[4,16,2048]{2,1,0:T(8,128)(2,1)S(1)} %get-tuple-element.49), channel_id=1, source_target_pairs={{0,16},{4,20},{8,24},{12,28},{16,0},{20,4},{24,8},{28,12},{1,17},{... | collective-permute-start | bytes 786440 | tf_op jit(solution)/shard_map/ppermute | solution.py:213
  37.3 0.5 collective-permute-start.12
  37.7 2.9 %collective-permute-done.19 = bf16[4,16,1024]{2,1,0:T(8,128)(2,1)S(1)} collective-permute-done((bf16[4,16,1024]{2,1,0:T(8,128)(2,1)S(1)}, bf16[4,16,1024]{2,1,0:T(8,128)(2,1)S(1)}, u32[]{:S(2)}, u32[]{:S(2)}) %collective-permute-start.19) | collective-permute-done | bytes 131104 | tf_op jit(solution)/shard_map/ppermute | solution.py:209
  40.6 5.5 %collective-permute-done.18 = bf16[4,16,1024]{2,1,0:T(8,128)(2,1)S(1)} collective-permute-done((bf16[4,16,1024]{2,1,0:T(8,128)(2,1)S(1)}, bf16[4,16,1024]{2,1,0:T(8,128)(2,1)S(1)}, u32[]{:S(2)}, u32[]{:S(2)}) %collective-permute-start.18) | collective-permute-done | bytes 131104 | tf_op jit(solution)/shard_map/ppermute | solution.py:209
  46.1 0.1 fusion.2
  46.2 2.9 %collective-permute-done.11 = bf16[4,16,2048]{2,1,0:T(8,128)(2,1)S(1)} collective-permute-done((bf16[4,16,2048]{2,1,0:T(8,128)(2,1)S(1)}, bf16[4,16,2048]{2,1,0:T(8,128)(2,1)S(1)}, u32[]{:S(2)}, u32[]{:S(2)}) %collective-permute-start.11) | collective-permute-done | bytes 262176 | tf_op jit(solution)/shard_map/ppermute | solution.py:213
  49.1 0.1 add_convert_fusion.1
  49.2 2.7 %collective-permute-start.13 = (bf16[16,2048]{1,0:T(8,128)(2,1)S(1)}, bf16[16,2048]{1,0:T(8,128)(2,1)S(1)}, u32[]{:S(2)}, u32[]{:S(2)}) collective-permute-start(bf16[16,2048]{1,0:T(8,128)(2,1)S(1)} %get-tuple-element.61), channel_id=1, source_target_pairs={{0,3},{1,2},{2,1},{3,0},{4,7},{5,6},{6,5},{7,4},{8,11},{9,10},{10,... | collective-permute-start | bytes 196616 | tf_op jit(solution)/shard_map/ppermute | solution.py:209
  52.0 1.7 %collective-permute-start.14 = (bf16[16,2048]{1,0:T(8,128)(2,1)S(1)}, bf16[16,2048]{1,0:T(8,128)(2,1)S(1)}, u32[]{:S(2)}, u32[]{:S(2)}) collective-permute-start(bf16[16,2048]{1,0:T(8,128)(2,1)S(1)} %get-tuple-element.63), channel_id=1, source_target_pairs={{0,1},{1,0},{2,3},{3,2},{4,5},{5,4},{6,7},{7,6},{8,9},{9,8},{10,11... | collective-permute-start | bytes 196616 | tf_op jit(solution)/shard_map/ppermute | solution.py:209
  53.7 1.6 %collective-permute-start.22 = (bf16[16,1024]{1,0:T(8,128)(2,1)S(1)}, bf16[16,1024]{1,0:T(8,128)(2,1)S(1)}, u32[]{:S(2)}, u32[]{:S(2)}) collective-permute-start(bf16[16,1024]{1,0:T(8,128)(2,1)S(1)} %get-tuple-element.64), channel_id=1, source_target_pairs={{0,24},{4,28},{8,16},{12,20},{16,8},{20,12},{24,0},{28,4},{1,25},{... | collective-permute-start | bytes 98312 | tf_op jit(solution)/shard_map/ppermute | solution.py:213
  55.3 1.2 %collective-permute-start.21 = (bf16[16,1024]{1,0:T(8,128)(2,1)S(1)}, bf16[16,1024]{1,0:T(8,128)(2,1)S(1)}, u32[]{:S(2)}, u32[]{:S(2)}) collective-permute-start(bf16[16,1024]{1,0:T(8,128)(2,1)S(1)} %get-tuple-element.65), channel_id=1, source_target_pairs={{0,16},{4,20},{8,24},{12,28},{16,0},{20,4},{24,8},{28,12},{1,17},{... | collective-permute-start | bytes 98312 | tf_op jit(solution)/shard_map/ppermute | solution.py:213
  56.5 0.8 %collective-permute-start.20 = (bf16[16,1024]{1,0:T(8,128)(2,1)S(1)}, bf16[16,1024]{1,0:T(8,128)(2,1)S(1)}, u32[]{:S(2)}, u32[]{:S(2)}) collective-permute-start(bf16[16,1024]{1,0:T(8,128)(2,1)S(1)} %get-tuple-element.66), channel_id=1, source_target_pairs={{0,8},{4,12},{8,0},{12,4},{16,24},{20,28},{24,16},{28,20},{1,9},{5... | collective-permute-start | bytes 98312 | tf_op jit(solution)/shard_map/ppermute | solution.py:213
  57.3 0.4 collective-permute-done.15
  57.6 0.7 %multiply_bitcast_fusion = f32[1,2048,16]{1,2,0:T(8,128)} fusion(bf16[16,2048]{1,0:T(8,128)(2,1)S(1)} %collective-permute-done.15, bf16[16,2048]{1,0:T(8,128)(2,1)S(1)} %collective-permute-done.14, bf16[16,2048]{1,0:T(8,128)(2,1)S(1)} %collective-permute-done.13, bf16[4,16,2048]{2,1,0:T(8,128)(2,1)S(1)} %add_convert_fusion.1), kind=kLoop, calls=%fused_computation.14 | loop fusion | flops 262144 | bytes 393216 | tf_op jit(solution)/shard_map/mul | solution.py:351
  58.3 0.3 collective-permute-done.22
  58.6 0.6 collective-permute-done.21
  59.2 1.2 %collective-permute-done.20 = bf16[16,1024]{1,0:T(8,128)(2,1)S(1)} collective-permute-done((bf16[16,1024]{1,0:T(8,128)(2,1)S(1)}, bf16[16,1024]{1,0:T(8,128)(2,1)S(1)}, u32[]{:S(2)}, u32[]{:S(2)}) %collective-permute-start.20) | collective-permute-done | bytes 32800 | tf_op jit(solution)/shard_map/ppermute | solution.py:213
  60.4 0.7 %fusion.8 = f32[1,16,1024]{2,1,0:T(8,128)} fusion(bf16[16,1024]{1,0:T(8,128)(2,1)S(1)} %collective-permute-done.22, bf16[16,1024]{1,0:T(8,128)(2,1)S(1)} %collective-permute-done.21, bf16[16,1024]{1,0:T(8,128)(2,1)S(1)} %collective-permute-done.20, bf16[4,16,1024]{2,1,0:T(8,128)(2,1)S(1)} %fusion.2), kind=kLoop, calls=%fused_computation.23 | loop fusion | flops 131072 | bytes 196608 | tf_op jit(solution)/shard_map/mul | solution.py:351
  (36 shorter events, 0.2 us)
Async XLA Ops:
  0.6 21.1 %copy-start.1 = (bf16[128,4096]{1,0:T(8,128)(2,1)S(1)}, bf16[128,4096]{1,0:T(8,128)(2,1)}, u32[]{:S(2)}) copy-start(bf16[128,4096]{1,0:T(8,128)(2,1)} %g_hbm.3) | copy-start | bytes 3145732
  0.6 21.1 %copy-start = (bf16[128,4096]{1,0:T(8,128)(2,1)S(1)}, bf16[128,4096]{1,0:T(8,128)(2,1)}, u32[]{:S(2)}) copy-start(bf16[128,4096]{1,0:T(8,128)(2,1)} %q_hbm.3) | copy-start | bytes 3145732
  0.6 14.2 %collective-permute-start.1 = (bf16[1,16,1024]{2,1,0:T(8,128)(2,1)}, bf16[1,16,1024]{2,1,0:T(8,128)(2,1)S(1)}, u32[]{:S(2)}, u32[]{:S(2)}) collective-permute-start(bf16[1,16,1024]{2,1,0:T(8,128)(2,1)} %param.16), channel_id=1, source_target_pairs={{0,2},{1,3},{2,0},{3,1},{4,6},{5,7},{6,4},{7,5},{8,10},{9,11},{10,... | collective-permute-start | bytes 98312 | tf_op jit(solution)/shard_map/ppermute | solution.py:205
  4.8 10.1 %collective-permute-start = (bf16[1,16,1024]{2,1,0:T(8,128)(2,1)}, bf16[1,16,1024]{2,1,0:T(8,128)(2,1)S(1)}, u32[]{:S(2)}, u32[]{:S(2)}) collective-permute-start(bf16[1,16,1024]{2,1,0:T(8,128)(2,1)} %param.16), channel_id=1, source_target_pairs={{0,1},{1,2},{2,3},{3,0},{4,5},{5,6},{6,7},{7,4},{8,9},{9,10},{10,1... | collective-permute-start | bytes 98312 | tf_op jit(solution)/shard_map/ppermute | solution.py:205
  6.3 8.6 %collective-permute-start.2 = (bf16[1,16,1024]{2,1,0:T(8,128)(2,1)}, bf16[1,16,1024]{2,1,0:T(8,128)(2,1)S(1)}, u32[]{:S(2)}, u32[]{:S(2)}) collective-permute-start(bf16[1,16,1024]{2,1,0:T(8,128)(2,1)} %param.16), channel_id=1, source_target_pairs={{0,3},{1,0},{2,1},{3,2},{4,7},{5,4},{6,5},{7,6},{8,11},{9,8},{10,9... | collective-permute-start | bytes 98312 | tf_op jit(solution)/shard_map/ppermute | solution.py:205
  10.4 11.1 %collective-permute-start.4 = (bf16[128,1024]{1,0:T(8,128)(2,1)S(1)}, bf16[128,1024]{1,0:T(8,128)(2,1)S(1)}, u32[]{:S(2)}, u32[]{:S(2)}) collective-permute-start(bf16[128,1024]{1,0:T(8,128)(2,1)S(1)} %constant_dynamic-update-slice_fusion.refs_3_), channel_id=1, source_target_pairs={{0,1},{1,2},{2,3},{4,5},{5,6},{6,7},{8,9},{9,10},{10,11},{12,13},{... | collective-permute-start | bytes 786440 | tf_op jit(solution)/shard_map/ppermute | solution.py:237
  12.1 9.3 %collective-permute-start.3 = (bf16[64,1024]{1,0:T(8,128)(2,1)S(1)}, bf16[64,1024]{1,0:T(8,128)(2,1)S(1)}, u32[]{:S(2)}, u32[]{:S(2)}) collective-permute-start(bf16[64,1024]{1,0:T(8,128)(2,1)S(1)} %slice.60), channel_id=1, source_target_pairs={{0,2},{1,3},{4,6},{5,7},{8,10},{9,11},{12,14},{13,15},{16,18},{17,... | collective-permute-start | bytes 393224 | tf_op jit(solution)/shard_map/ppermute | solution.py:237
  15.7 8.3 %collective-permute-start.7 = (bf16[1,4,16,1024]{3,2,1,0:T(8,128)(2,1)S(1)}, bf16[1,4,16,1024]{3,2,1,0:T(8,128)(2,1)S(1)}, u32[]{:S(2)}, u32[]{:S(2)}) collective-permute-start(bf16[1,4,16,1024]{3,2,1,0:T(8,128)(2,1)S(1)} %maximum_bitcast_fusion), channel_id=1, source_target_pairs={{0,24},{4,28},{8,16},{12,20},{16,8},{20,12},{24,0},{28,4},{1,25},{... | collective-permute-start | bytes 393224 | tf_op jit(solution)/shard_map/ppermute | solution.py:213
  18.2 5.8 %collective-permute-start.6 = (bf16[1,4,16,1024]{3,2,1,0:T(8,128)(2,1)S(1)}, bf16[1,4,16,1024]{3,2,1,0:T(8,128)(2,1)S(1)}, u32[]{:S(2)}, u32[]{:S(2)}) collective-permute-start(bf16[1,4,16,1024]{3,2,1,0:T(8,128)(2,1)S(1)} %maximum_bitcast_fusion), channel_id=1, source_target_pairs={{0,16},{4,20},{8,24},{12,28},{16,0},{20,4},{24,8},{28,12},{1,17},{... | collective-permute-start | bytes 393224 | tf_op jit(solution)/shard_map/ppermute | solution.py:213
  18.7 5.3 %collective-permute-start.5 = (bf16[1,4,16,1024]{3,2,1,0:T(8,128)(2,1)S(1)}, bf16[1,4,16,1024]{3,2,1,0:T(8,128)(2,1)S(1)}, u32[]{:S(2)}, u32[]{:S(2)}) collective-permute-start(bf16[1,4,16,1024]{3,2,1,0:T(8,128)(2,1)S(1)} %maximum_bitcast_fusion), channel_id=1, source_target_pairs={{0,8},{4,12},{8,0},{12,4},{16,24},{20,28},{24,16},{28,20},{1,9},{5... | collective-permute-start | bytes 393224 | tf_op jit(solution)/shard_map/ppermute | solution.py:213
  21.8 2.4 %copy-start.3 = (bf16[128,16]{0,1:T(8,128)(2,1)S(1)}, bf16[128,16]{0,1:T(8,128)(2,1)}, u32[]{:S(2)}) copy-start(bf16[128,16]{0,1:T(8,128)(2,1)} %param.15) | copy-start | bytes 12292
  24.1 2.6 %collective-permute-start.8 = (bf16[4,4,16,1024]{3,2,1,0:T(8,128)(2,1)S(1)}, bf16[4,4,16,1024]{3,2,1,0:T(8,128)(2,1)S(1)}, u32[]{:S(2)}, u32[]{:S(2)}) collective-permute-start(bf16[4,4,16,1024]{3,2,1,0:T(8,128)(2,1)S(1)} %constant_dynamic-update-slice_fusion.2.refs_0_), channel_id=1, source_target_pairs={{0,4},{4,0},{8,12},{12,8},{16,20},{20,16},{24,28},{28,24},{1,5},{5... | collective-permute-start | bytes 1572872 | tf_op jit(solution)/shard_map/ppermute | solution.py:213
  24.2 3.5 %copy-start.2 = (bf16[128,8192]{1,0:T(8,128)(2,1)S(1)}, bf16[128,8192]{1,0:T(8,128)(2,1)}, u32[]{:S(2)}) copy-start(bf16[128,8192]{1,0:T(8,128)(2,1)} %x_ref.1) | copy-start | bytes 6291460
  26.7 2.1 %collective-permute-start.16 = (bf16[4,4,16,1024]{3,2,1,0:T(8,128)(2,1)S(1)}, bf16[4,4,16,1024]{3,2,1,0:T(8,128)(2,1)S(1)}, u32[]{:S(2)}, u32[]{:S(2)}) collective-permute-start(bf16[4,4,16,1024]{3,2,1,0:T(8,128)(2,1)S(1)} %get-tuple-element.52), channel_id=1, source_target_pairs={{0,4},{4,0},{8,12},{12,8},{16,20},{20,16},{24,28},{28,24},{1,5},{5... | collective-permute-start | bytes 1572872 | tf_op jit(solution)/shard_map/ppermute | solution.py:213
  28.4 5.5 %collective-permute-start.9 = (bf16[4,4,16,2048]{3,2,1,0:T(8,128)(2,1)S(1)}, bf16[4,4,16,2048]{3,2,1,0:T(8,128)(2,1)S(1)}, u32[]{:S(2)}, u32[]{:S(2)}) collective-permute-start(bf16[4,4,16,2048]{3,2,1,0:T(8,128)(2,1)S(1)} %get-tuple-element.46), channel_id=1, source_target_pairs={{0,4},{4,0},{8,12},{12,8},{16,20},{20,16},{24,28},{28,24},{1,5},{5... | collective-permute-start | bytes 3145736 | tf_op jit(solution)/shard_map/ppermute | solution.py:213
  29.0 8.2 %collective-permute-start.17 = (bf16[4,16,1024]{2,1,0:T(8,128)(2,1)S(1)}, bf16[4,16,1024]{2,1,0:T(8,128)(2,1)S(1)}, u32[]{:S(2)}, u32[]{:S(2)}) collective-permute-start(bf16[4,16,1024]{2,1,0:T(8,128)(2,1)S(1)} %get-tuple-element.58), channel_id=1, source_target_pairs={{0,1},{1,0},{2,3},{3,2},{4,5},{5,4},{6,7},{7,6},{8,9},{9,8},{10,11... | collective-permute-start | bytes 393224 | tf_op jit(solution)/shard_map/ppermute | solution.py:209
  30.5 10.1 %collective-permute-start.19 = (bf16[4,16,1024]{2,1,0:T(8,128)(2,1)S(1)}, bf16[4,16,1024]{2,1,0:T(8,128)(2,1)S(1)}, u32[]{:S(2)}, u32[]{:S(2)}) collective-permute-start(bf16[4,16,1024]{2,1,0:T(8,128)(2,1)S(1)} %get-tuple-element.59), channel_id=1, source_target_pairs={{0,3},{1,2},{2,1},{3,0},{4,7},{5,6},{6,5},{7,4},{8,11},{9,10},{10,... | collective-permute-start | bytes 393224 | tf_op jit(solution)/shard_map/ppermute | solution.py:209
  33.4 12.7 %collective-permute-start.18 = (bf16[4,16,1024]{2,1,0:T(8,128)(2,1)S(1)}, bf16[4,16,1024]{2,1,0:T(8,128)(2,1)S(1)}, u32[]{:S(2)}, u32[]{:S(2)}) collective-permute-start(bf16[4,16,1024]{2,1,0:T(8,128)(2,1)S(1)} %get-tuple-element.60), channel_id=1, source_target_pairs={{0,2},{1,3},{2,0},{3,1},{4,6},{5,7},{6,4},{7,5},{8,10},{9,11},{10,... | collective-permute-start | bytes 393224 | tf_op jit(solution)/shard_map/ppermute | solution.py:209
  34.2 12.0 %collective-permute-start.10 = (bf16[4,16,2048]{2,1,0:T(8,128)(2,1)S(1)}, bf16[4,16,2048]{2,1,0:T(8,128)(2,1)S(1)}, u32[]{:S(2)}, u32[]{:S(2)}) collective-permute-start(bf16[4,16,2048]{2,1,0:T(8,128)(2,1)S(1)} %get-tuple-element.48), channel_id=1, source_target_pairs={{0,8},{4,12},{8,0},{12,4},{16,24},{20,28},{24,16},{28,20},{1,9},{5... | collective-permute-start | bytes 786440 | tf_op jit(solution)/shard_map/ppermute | solution.py:213
  35.7 13.3 %collective-permute-start.11 = (bf16[4,16,2048]{2,1,0:T(8,128)(2,1)S(1)}, bf16[4,16,2048]{2,1,0:T(8,128)(2,1)S(1)}, u32[]{:S(2)}, u32[]{:S(2)}) collective-permute-start(bf16[4,16,2048]{2,1,0:T(8,128)(2,1)S(1)} %get-tuple-element.49), channel_id=1, source_target_pairs={{0,16},{4,20},{8,24},{12,28},{16,0},{20,4},{24,8},{28,12},{1,17},{... | collective-permute-start | bytes 786440 | tf_op jit(solution)/shard_map/ppermute | solution.py:213
  37.3 11.8 %collective-permute-start.12 = (bf16[4,16,2048]{2,1,0:T(8,128)(2,1)S(1)}, bf16[4,16,2048]{2,1,0:T(8,128)(2,1)S(1)}, u32[]{:S(2)}, u32[]{:S(2)}) collective-permute-start(bf16[4,16,2048]{2,1,0:T(8,128)(2,1)S(1)} %get-tuple-element.50), channel_id=1, source_target_pairs={{0,24},{4,28},{8,16},{12,20},{16,8},{20,12},{24,0},{28,4},{1,25},{... | collective-permute-start | bytes 786440 | tf_op jit(solution)/shard_map/ppermute | solution.py:213
  49.2 7.2 %collective-permute-start.13 = (bf16[16,2048]{1,0:T(8,128)(2,1)S(1)}, bf16[16,2048]{1,0:T(8,128)(2,1)S(1)}, u32[]{:S(2)}, u32[]{:S(2)}) collective-permute-start(bf16[16,2048]{1,0:T(8,128)(2,1)S(1)} %get-tuple-element.61), channel_id=1, source_target_pairs={{0,3},{1,2},{2,1},{3,0},{4,7},{5,6},{6,5},{7,4},{8,11},{9,10},{10,... | collective-permute-start | bytes 196616 | tf_op jit(solution)/shard_map/ppermute | solution.py:209
  52.0 5.7 %collective-permute-start.15 = (bf16[16,2048]{1,0:T(8,128)(2,1)S(1)}, bf16[16,2048]{1,0:T(8,128)(2,1)S(1)}, u32[]{:S(2)}, u32[]{:S(2)}) collective-permute-start(bf16[16,2048]{1,0:T(8,128)(2,1)S(1)} %get-tuple-element.62), channel_id=1, source_target_pairs={{0,2},{1,3},{2,0},{3,1},{4,6},{5,7},{6,4},{7,5},{8,10},{9,11},{10,... | collective-permute-start | bytes 196616 | tf_op jit(solution)/shard_map/ppermute | solution.py:209
  52.0 5.7 %collective-permute-start.14 = (bf16[16,2048]{1,0:T(8,128)(2,1)S(1)}, bf16[16,2048]{1,0:T(8,128)(2,1)S(1)}, u32[]{:S(2)}, u32[]{:S(2)}) collective-permute-start(bf16[16,2048]{1,0:T(8,128)(2,1)S(1)} %get-tuple-element.63), channel_id=1, source_target_pairs={{0,1},{1,0},{2,3},{3,2},{4,5},{5,4},{6,7},{7,6},{8,9},{9,8},{10,11... | collective-permute-start | bytes 196616 | tf_op jit(solution)/shard_map/ppermute | solution.py:209
  53.7 4.9 %collective-permute-start.22 = (bf16[16,1024]{1,0:T(8,128)(2,1)S(1)}, bf16[16,1024]{1,0:T(8,128)(2,1)S(1)}, u32[]{:S(2)}, u32[]{:S(2)}) collective-permute-start(bf16[16,1024]{1,0:T(8,128)(2,1)S(1)} %get-tuple-element.64), channel_id=1, source_target_pairs={{0,24},{4,28},{8,16},{12,20},{16,8},{20,12},{24,0},{28,4},{1,25},{... | collective-permute-start | bytes 98312 | tf_op jit(solution)/shard_map/ppermute | solution.py:213
  55.3 3.9 %collective-permute-start.21 = (bf16[16,1024]{1,0:T(8,128)(2,1)S(1)}, bf16[16,1024]{1,0:T(8,128)(2,1)S(1)}, u32[]{:S(2)}, u32[]{:S(2)}) collective-permute-start(bf16[16,1024]{1,0:T(8,128)(2,1)S(1)} %get-tuple-element.65), channel_id=1, source_target_pairs={{0,16},{4,20},{8,24},{12,28},{16,0},{20,4},{24,8},{28,12},{1,17},{... | collective-permute-start | bytes 98312 | tf_op jit(solution)/shard_map/ppermute | solution.py:213
  56.5 3.9 %collective-permute-start.20 = (bf16[16,1024]{1,0:T(8,128)(2,1)S(1)}, bf16[16,1024]{1,0:T(8,128)(2,1)S(1)}, u32[]{:S(2)}, u32[]{:S(2)}) collective-permute-start(bf16[16,1024]{1,0:T(8,128)(2,1)S(1)} %get-tuple-element.66), channel_id=1, source_target_pairs={{0,8},{4,12},{8,0},{12,4},{16,24},{20,28},{24,16},{28,20},{1,9},{5... | collective-permute-start | bytes 98312 | tf_op jit(solution)/shard_map/ppermute | solution.py:213

commit v19 on v16

--- a/solution.py
+++ b/solution.py
@@ -20,7 +20,6 @@
 F32 = jnp.float32
 I32 = jnp.int32
 VMEM = pl.BlockSpec(memory_space=pltpu.VMEM)
-ANY = pl.BlockSpec(memory_space=pl.ANY)
 
 
 def dot(a, b, a_dim, b_dim):
@@ -60,37 +59,23 @@
         k_turned[at, start - tok :] = own_turned[at, :]
 
 
-def attention_kernel(by_slot, first_kv, n_kv, k_all, v_all, k_turned, bias, q_hbm, g_hbm, *refs):
+def attention_kernel(by_slot, first_kv, n_kv, k_all, v_all, k_turned, bias, q_ref, g_ref, *refs):
     before, refs = (refs[:3], refs[3:]) if first_kv else ((), refs)
-    dq_turned, *up_refs, q_ref, g_ref, q_sem, g_sem = refs
+    dq_turned, *up_refs = refs
     tok = q_ref.shape[0]
     seq, head = lax.axis_index("seq"), lax.axis_index("head")
-    per_kv = GROUP * HEAD_SIZE
-
-    def fetch(kv):
-        to = pl.ds(kv * per_kv, per_kv)
-        at = pl.ds((first_kv + kv) * per_kv, per_kv)
-        return (
-            pltpu.make_async_copy(q_hbm.at[:, at], q_ref.at[:, to], q_sem.at[kv]),
-            pltpu.make_async_copy(g_hbm.at[:, at], g_ref.at[:, to], g_sem.at[kv]),
-        )
-
-    for kv in range(n_kv):
-        for copy in fetch(kv):
-            copy.start()
 
     scale = 1.0 / HEAD_SIZE**0.5
     to_log2 = scale * math.log2(math.e)
 
     def products(kv, i):
-        if i == 0:
-            for copy in fetch(kv):
-                copy.wait()
         at_kv = slice((first_kv + kv) * HEAD_SIZE, (first_kv + kv + 1) * HEAD_SIZE)
         first = (kv * GROUP + i) * HEAD_SIZE
         at = [slice(first + n * HEAD_SIZE, first + (n + 1) * HEAD_SIZE) for n in range(2)]
-        q_two = jnp.concatenate([q_ref[:, at[0]], q_ref[:, at[1]]], axis=0)
-        g_two = jnp.concatenate([g_ref[:, at[0]], g_ref[:, at[1]]], axis=0)
+        skip = first_kv * GROUP * HEAD_SIZE
+        wide = [slice(skip + a.start, skip + a.stop) for a in at]
+        q_two = jnp.concatenate([q_ref[:, wide[0]], q_ref[:, wide[1]]], axis=0)
+        g_two = jnp.concatenate([g_ref[:, wide[0]], g_ref[:, wide[1]]], axis=0)
         s = dot(k_all[:, at_kv], q_two, 1, 1) + jnp.concatenate([bias[...]] * 2, axis=1)
         return at, at_kv, s, dot(v_all[:, at_kv], g_two, 1, 1)
 
@@ -277,14 +262,8 @@
         return pl.pallas_call(
             functools.partial(attention_kernel, by_slot, h * n_kv, n_kv),
             out_shape=[jax.ShapeDtypeStruct((half, tok), BF16)] + up_shapes,
-            in_specs=[VMEM] * 4 + [ANY] * 2 + [VMEM] * len(before),
+            in_specs=[VMEM] * (6 + len(before)),
             out_specs=[VMEM] * (1 + len(up_shapes)),
-            scratch_shapes=[
-                pltpu.VMEM((tok, half), BF16),
-                pltpu.VMEM((tok, half), BF16),
-                pltpu.SemaphoreType.DMA((n_kv,)),
-                pltpu.SemaphoreType.DMA((n_kv,)),
-            ],
             compiler_params=params,
             cost_estimate=pl.CostEstimate(
                 flops=2 * tok * half * key_rows * 3,

time: 59.1 us -> 58.7 us (level)
  transfers between devices with their start and end apart: 23 -> 23, of which waited for: 5 -> 5; matrix products, arithmetic and copies ran while one was open for 10% -> 10% of each run, Pallas kernels for 11% -> 10%
where the time goes in v19:
time: 58.7 us; the launch traced here: 58.4 us
  starting transfers between devices  33 us (56%)
  waiting for transfers between devices  11.8 us (20%)
  Pallas kernels  5.94 us (10%)
  other arithmetic  3.72 us (6%)
  local copies, waits for them, and re-layouts  2.98 us (5%)
  between operations  0.98 us (2%)
    ppermute x6, waiting for transfers between devices, across(): return lax.ppermute(x, 'head', [(i, i ^ j) for i in range(n_head)])  11.5 us
    ppermute x12, starting transfers between devices, partnered(): return lax.ppermute(x, 'seq', [(i, i ^ bits) for i in range(n_seq)])  11.4 us
    ppermute x6, starting transfers between devices, across(): return lax.ppermute(x, 'head', [(i, i ^ j) for i in range(n_head)])  9.34 us
    ppermute x3, starting transfers between devices, shifted(): lax.ppermute(x, 'head', [(i, (i + j) % n_head) for i in range(n_head)])  7.93 us
    ppermute x2, starting transfers between devices, on_device(): parts.insert(0, lax.ppermute(own[tok - rows:], 'head', shift))  4.39 us
    pallas_call x2, Pallas kernels, attention(): pl.pallas_call(functools.partial(attention_kernel, by_slot, h * n_kv, n_k...  4.29 us
    mul x2, other arithmetic, on_device(): return (down.T[None] * ADAPTER_SCALE, up[None] * ADAPTER_SCALE)  1.35 us
  transfers between devices with their start and end apart: 23, of which 5 were waited for; matrix products, arithmetic and copies ran while one was open for 10% of the time, Pallas kernels for 10%

profile of v19, /device:TPU:0, one launch (start us, length us, event | category | flops | bytes accessed | tf_op | source)
XLA Modules:
  0.0 58.4 jit_solution(6631842486979712751)
XLA Ops:
  0.6 4.1 %collective-permute-start.1 = (bf16[1,16,1024]{2,1,0:T(8,128)(2,1)}, bf16[1,16,1024]{2,1,0:T(8,128)(2,1)S(1)}, u32[]{:S(2)}, u32[]{:S(2)}) collective-permute-start(bf16[1,16,1024]{2,1,0:T(8,128)(2,1)} %param.16), channel_id=1, source_target_pairs={{0,2},{1,3},{2,0},{3,1},{4,6},{5,7},{6,4},{7,5},{8,10},{9,11},{10,... | collective-permute-start | bytes 98312 | tf_op jit(solution)/shard_map/ppermute | solution.py:190
  4.8 1.6 %collective-permute-start = (bf16[1,16,1024]{2,1,0:T(8,128)(2,1)}, bf16[1,16,1024]{2,1,0:T(8,128)(2,1)S(1)}, u32[]{:S(2)}, u32[]{:S(2)}) collective-permute-start(bf16[1,16,1024]{2,1,0:T(8,128)(2,1)} %param.16), channel_id=1, source_target_pairs={{0,1},{1,2},{2,3},{3,0},{4,5},{5,6},{6,7},{7,4},{8,9},{9,10},{10,1... | collective-permute-start | bytes 98312 | tf_op jit(solution)/shard_map/ppermute | solution.py:190
  6.3 2.2 %collective-permute-start.2 = (bf16[1,16,1024]{2,1,0:T(8,128)(2,1)}, bf16[1,16,1024]{2,1,0:T(8,128)(2,1)S(1)}, u32[]{:S(2)}, u32[]{:S(2)}) collective-permute-start(bf16[1,16,1024]{2,1,0:T(8,128)(2,1)} %param.16), channel_id=1, source_target_pairs={{0,3},{1,0},{2,1},{3,2},{4,7},{5,4},{6,5},{7,6},{8,11},{9,8},{10,9... | collective-permute-start | bytes 98312 | tf_op jit(solution)/shard_map/ppermute | solution.py:190
  8.6 0.9 %constant_dynamic-update-slice_fusion.1 = bf16[128,1024]{1,0:T(8,128)(2,1)S(1)} fusion(bf16[128,512]{1,0:T(8,128)(2,1)} %param.11), kind=kLoop, calls=%fused_computation.39 | loop fusion | bytes 262144
  9.5 0.9 %constant_dynamic-update-slice_fusion.refs_3_ = bf16[128,1024]{1,0:T(8,128)(2,1)S(1)} fusion(bf16[128,1024]{1,0:T(8,128)(2,1)S(1)} %constant_dynamic-update-slice_fusion.1, bf16[128,512]{1,0:T(8,128)(2,1)} %param.12), kind=kLoop, calls=%fused_computation.38 | loop fusion | bytes 262144 | tf_op jit(solution)/shard_map/concatenate | solution.py:218
  10.4 1.7 %collective-permute-start.4 = (bf16[128,1024]{1,0:T(8,128)(2,1)S(1)}, bf16[128,1024]{1,0:T(8,128)(2,1)S(1)}, u32[]{:S(2)}, u32[]{:S(2)}) collective-permute-start(bf16[128,1024]{1,0:T(8,128)(2,1)S(1)} %constant_dynamic-update-slice_fusion.refs_3_), channel_id=1, source_target_pairs={{0,1},{1,2},{2,3},{4,5},{5,6},{6,7},{8,9},{9,10},{10,11},{12,13},{... | collective-permute-start | bytes 786440 | tf_op jit(solution)/shard_map/ppermute | solution.py:222
  12.1 2.7 %collective-permute-start.3 = (bf16[64,1024]{1,0:T(8,128)(2,1)S(1)}, bf16[64,1024]{1,0:T(8,128)(2,1)S(1)}, u32[]{:S(2)}, u32[]{:S(2)}) collective-permute-start(bf16[64,1024]{1,0:T(8,128)(2,1)S(1)} %slice.60), channel_id=1, source_target_pairs={{0,2},{1,3},{4,6},{5,7},{8,10},{9,11},{12,14},{13,15},{16,18},{17,... | collective-permute-start | bytes 393224 | tf_op jit(solution)/shard_map/ppermute | solution.py:222
  14.9 0.0 collective-permute-done.2
  14.9 0.8 %maximum_bitcast_fusion = bf16[1,4,16,1024]{3,2,1,0:T(8,128)(2,1)S(1)} fusion(bf16[1,16,1024]{2,1,0:T(8,128)(2,1)S(1)} %collective-permute-done.2, bf16[1,16,1024]{2,1,0:T(8,128)(2,1)S(1)} %collective-permute-done.1, bf16[1,16,1024]{2,1,0:T(8,128)(2,1)S(1)} %collective-permute-done, bf16[1,16,1024]{2,1,0:T(8,128)(2,1)} %param.16), kind=kLoop, calls=%fused_computation.10 | loop fusion | flops 196608 | bytes 262144 | tf_op jit(solution)/shard_map/broadcast_in_dim | solution.py:226
  15.7 2.5 %collective-permute-start.7 = (bf16[1,4,16,1024]{3,2,1,0:T(8,128)(2,1)S(1)}, bf16[1,4,16,1024]{3,2,1,0:T(8,128)(2,1)S(1)}, u32[]{:S(2)}, u32[]{:S(2)}) collective-permute-start(bf16[1,4,16,1024]{3,2,1,0:T(8,128)(2,1)S(1)} %maximum_bitcast_fusion), channel_id=1, source_target_pairs={{0,24},{4,28},{8,16},{12,20},{16,8},{20,12},{24,0},{28,4},{1,25},{... | collective-permute-start | bytes 393224 | tf_op jit(solution)/shard_map/ppermute | solution.py:198
  18.2 0.5 collective-permute-start.6
  18.7 0.5 collective-permute-start.5
  19.2 1.0 %select_reduce_fusion.1 = s32[8,8]{1,0:T(8,128)S(1)} fusion(s32[8]{0:T(128)} %param.19, s32[8]{0:T(128)} %bitcast.51, s32[8]{0:T(128)} %bitcast.52, pred[8]{0:T(512)(128)(4,1)S(1)} %get-tuple-element.61, pred[8]{0:T(512)(128)(4,1)S(1)} %get-tuple-element.62, pred[8]{0:T(512)(128)(4,1)S(1)} %get-tuple-element.63, pred[8]{0:T(512)(128)(4,1)S(1)} %get-tuple-element.64), kind=kLoop, calls=%fused_computation.30 | loop fusion | flops 6592 | bytes 384 | tf_op jit(solution)/shard_map/reduce_sum | solution.py:183
  20.3 0.1 compare_and_fusion
  20.4 1.0 %copy.13 = bf16[128,512]{0,1:T(8,128)(2,1)S(1)} copy(bf16[128,512]{1,0:T(8,128)(2,1)} %param.11) | data formatting | bytes 262144 | tf_op jit(solution)/shard_map/optimization_barrier | solution.py:227
  21.4 0.1 select_reduce_fusion.facts_ref.refs_0_
  21.5 0.3 layout.1
  21.8 0.0 copy-start.3
  21.8 2.0 %attention_0.1.refs_2_ = bf16[2048,128]{1,0:T(8,128)(2,1)S(1)} custom-call(bf16[320,512]{1,0:T(8,128)(2,1)S(1)} %get-tuple-element.28.k_all, bf16[320,512]{1,0:T(8,128)(2,1)S(1)} %get-tuple-element.29.v_all, bf16[512,320]{1,0:T(8,128)(2,1)S(1)} %get-tuple-element.30.k_turned, f32[320,128]{1,0:T(8,128)S(1)} %get-tuple-element.31.bias, ...), custom_call_target="tpu_custom_call" | custom-call | flops 503316480 | bytes 2097152 | tf_op jit(solution)/shard_map/attention_0/pallas_call | solution.py:262
  23.9 0.1 collective-permute-start.8
  24.0 0.0 copy-start.2
  24.0 2.3 %attention_1.1 = (bf16[2048,128]{1,0:T(8,128)(2,1)S(1)}, bf16[4,4,16,1024]{3,2,1,0:T(8,128)(2,1)S(1)}, bf16[4,4,16,1024]{3,2,1,0:T(8,128)(2,1)S(1)}) custom-call(bf16[320,512]{1,0:T(8,128)(2,1)S(1)} %get-tuple-element.28.k_all, bf16[320,512]{1,0:T(8,128)(2,1)S(1)} %get-tuple-element.29.v_all, bf16[512,320]{1,0:T(8,128)(2,1)S(1)} %get-tuple-element.30.k_turned, ...), custom_call_target="tpu_custom_call" | custom-call | flops 503316480 | bytes 2097152 | tf_op jit(solution)/shard_map/attention_1/pallas_call | solution.py:262
  26.3 0.5 collective-permute-start.16
  26.9 0.4 rank_gradient.1.rank_ref
  27.3 0.7 %down_parts.1 = (bf16[4,4,16,2048]{3,2,1,0:T(8,128)(2,1)S(1)}, bf16[4,4,16,2048]{3,2,1,0:T(8,128)(2,1)S(1)}) custom-call(s32[8,128]{1,0:T(8,128)S(1)} %select_reduce_fusion.facts_ref.refs_0_, bf16[128,8192]{1,0:T(8,128)(2,1)S(1)} %copy-done.2, bf16[16,128]{1,0:T(8,128)(2,1)S(1)} %rank_gradient.1.rank_ref), custom_call_target="tpu_custom_call" | custom-call | flops 268435456 | bytes 8388608 | tf_op jit(solution)/shard_map/down_parts/pallas_call | solution.py:296
  28.0 0.1 collective-permute-start.9
  28.1 0.3 collective-permute-done.16
  28.4 0.2 add_convert_fusion
  28.6 1.5 %collective-permute-start.17 = (bf16[4,16,1024]{2,1,0:T(8,128)(2,1)S(1)}, bf16[4,16,1024]{2,1,0:T(8,128)(2,1)S(1)}, u32[]{:S(2)}, u32[]{:S(2)}) collective-permute-start(bf16[4,16,1024]{2,1,0:T(8,128)(2,1)S(1)} %get-tuple-element.50), channel_id=1, source_target_pairs={{0,1},{1,0},{2,3},{3,2},{4,5},{5,4},{6,7},{7,6},{8,9},{9,8},{10,11... | collective-permute-start | bytes 393224 | tf_op jit(solution)/shard_map/ppermute | solution.py:194
  30.1 2.9 %collective-permute-start.19 = (bf16[4,16,1024]{2,1,0:T(8,128)(2,1)S(1)}, bf16[4,16,1024]{2,1,0:T(8,128)(2,1)S(1)}, u32[]{:S(2)}, u32[]{:S(2)}) collective-permute-start(bf16[4,16,1024]{2,1,0:T(8,128)(2,1)S(1)} %get-tuple-element.51), channel_id=1, source_target_pairs={{0,3},{1,2},{2,1},{3,0},{4,7},{5,6},{6,5},{7,4},{8,11},{9,10},{10,... | collective-permute-start | bytes 393224 | tf_op jit(solution)/shard_map/ppermute | solution.py:194
  33.0 0.5 collective-permute-start.18
  33.5 0.2 core_sum.1
  33.8 1.6 %collective-permute-start.10 = (bf16[4,16,2048]{2,1,0:T(8,128)(2,1)S(1)}, bf16[4,16,2048]{2,1,0:T(8,128)(2,1)S(1)}, u32[]{:S(2)}, u32[]{:S(2)}) collective-permute-start(bf16[4,16,2048]{2,1,0:T(8,128)(2,1)S(1)} %get-tuple-element.45), channel_id=1, source_target_pairs={{0,8},{4,12},{8,0},{12,4},{16,24},{20,28},{24,16},{28,20},{1,9},{5... | collective-permute-start | bytes 786440 | tf_op jit(solution)/shard_map/ppermute | solution.py:198
  35.3 1.5 %collective-permute-start.11 = (bf16[4,16,2048]{2,1,0:T(8,128)(2,1)S(1)}, bf16[4,16,2048]{2,1,0:T(8,128)(2,1)S(1)}, u32[]{:S(2)}, u32[]{:S(2)}) collective-permute-start(bf16[4,16,2048]{2,1,0:T(8,128)(2,1)S(1)} %get-tuple-element.46), channel_id=1, source_target_pairs={{0,16},{4,20},{8,24},{12,28},{16,0},{20,4},{24,8},{28,12},{1,17},{... | collective-permute-start | bytes 786440 | tf_op jit(solution)/shard_map/ppermute | solution.py:198
  36.8 0.5 collective-permute-start.12
  37.3 2.9 %collective-permute-done.19 = bf16[4,16,1024]{2,1,0:T(8,128)(2,1)S(1)} collective-permute-done((bf16[4,16,1024]{2,1,0:T(8,128)(2,1)S(1)}, bf16[4,16,1024]{2,1,0:T(8,128)(2,1)S(1)}, u32[]{:S(2)}, u32[]{:S(2)}) %collective-permute-start.19) | collective-permute-done | bytes 131104 | tf_op jit(solution)/shard_map/ppermute | solution.py:194
  40.2 5.5 %collective-permute-done.18 = bf16[4,16,1024]{2,1,0:T(8,128)(2,1)S(1)} collective-permute-done((bf16[4,16,1024]{2,1,0:T(8,128)(2,1)S(1)}, bf16[4,16,1024]{2,1,0:T(8,128)(2,1)S(1)}, u32[]{:S(2)}, u32[]{:S(2)}) %collective-permute-start.18) | collective-permute-done | bytes 131104 | tf_op jit(solution)/shard_map/ppermute | solution.py:194
  45.7 0.1 fusion.2
  45.8 1.6 %collective-permute-start.20 = (bf16[16,1024]{1,0:T(8,128)(2,1)S(1)}, bf16[16,1024]{1,0:T(8,128)(2,1)S(1)}, u32[]{:S(2)}, u32[]{:S(2)}) collective-permute-start(bf16[16,1024]{1,0:T(8,128)(2,1)S(1)} %get-tuple-element.56), channel_id=1, source_target_pairs={{0,8},{4,12},{8,0},{12,4},{16,24},{20,28},{24,16},{28,20},{1,9},{5... | collective-permute-start | bytes 98312 | tf_op jit(solution)/shard_map/ppermute | solution.py:198
  47.3 1.5 %collective-permute-start.22 = (bf16[16,1024]{1,0:T(8,128)(2,1)S(1)}, bf16[16,1024]{1,0:T(8,128)(2,1)S(1)}, u32[]{:S(2)}, u32[]{:S(2)}) collective-permute-start(bf16[16,1024]{1,0:T(8,128)(2,1)S(1)} %get-tuple-element.57), channel_id=1, source_target_pairs={{0,24},{4,28},{8,16},{12,20},{16,8},{20,12},{24,0},{28,4},{1,25},{... | collective-permute-start | bytes 98312 | tf_op jit(solution)/shard_map/ppermute | solution.py:198
  48.8 0.5 collective-permute-start.21
  49.3 0.1 add_convert_fusion.1
  49.5 2.7 %collective-permute-start.13 = (bf16[16,2048]{1,0:T(8,128)(2,1)S(1)}, bf16[16,2048]{1,0:T(8,128)(2,1)S(1)}, u32[]{:S(2)}, u32[]{:S(2)}) collective-permute-start(bf16[16,2048]{1,0:T(8,128)(2,1)S(1)} %get-tuple-element.53), channel_id=1, source_target_pairs={{0,3},{1,2},{2,1},{3,0},{4,7},{5,6},{6,5},{7,4},{8,11},{9,10},{10,... | collective-permute-start | bytes 196616 | tf_op jit(solution)/shard_map/ppermute | solution.py:194
  52.2 1.7 %collective-permute-start.14 = (bf16[16,2048]{1,0:T(8,128)(2,1)S(1)}, bf16[16,2048]{1,0:T(8,128)(2,1)S(1)}, u32[]{:S(2)}, u32[]{:S(2)}) collective-permute-start(bf16[16,2048]{1,0:T(8,128)(2,1)S(1)} %get-tuple-element.55), channel_id=1, source_target_pairs={{0,1},{1,0},{2,3},{3,2},{4,5},{5,4},{6,7},{7,6},{8,9},{9,8},{10,11... | collective-permute-start | bytes 196616 | tf_op jit(solution)/shard_map/ppermute | solution.py:194
  54.0 0.7 %fusion.10 = f32[1,16,1024]{2,1,0:T(8,128)} fusion(bf16[16,1024]{1,0:T(8,128)(2,1)S(1)} %collective-permute-done.22, bf16[16,1024]{1,0:T(8,128)(2,1)S(1)} %collective-permute-done.21, bf16[16,1024]{1,0:T(8,128)(2,1)S(1)} %collective-permute-done.20, bf16[4,16,1024]{2,1,0:T(8,128)(2,1)S(1)} %fusion.2), kind=kLoop, calls=%fused_computation.24 | loop fusion | flops 131072 | bytes 196608 | tf_op jit(solution)/shard_map/mul | solution.py:327
  54.6 1.6 %collective-permute-done.13 = bf16[16,2048]{1,0:T(8,128)(2,1)S(1)} collective-permute-done((bf16[16,2048]{1,0:T(8,128)(2,1)S(1)}, bf16[16,2048]{1,0:T(8,128)(2,1)S(1)}, u32[]{:S(2)}, u32[]{:S(2)}) %collective-permute-start.13) | collective-permute-done | bytes 65568 | tf_op jit(solution)/shard_map/ppermute | solution.py:194
  56.2 1.6 %collective-permute-done.15 = bf16[16,2048]{1,0:T(8,128)(2,1)S(1)} collective-permute-done((bf16[16,2048]{1,0:T(8,128)(2,1)S(1)}, bf16[16,2048]{1,0:T(8,128)(2,1)S(1)}, u32[]{:S(2)}, u32[]{:S(2)}) %collective-permute-start.15) | collective-permute-done | bytes 65568 | tf_op jit(solution)/shard_map/ppermute | solution.py:194
  57.7 0.7 %fusion.6 = f32[1,2048,16]{1,2,0:T(8,128)} fusion(bf16[16,2048]{1,0:T(8,128)(2,1)S(1)} %collective-permute-done.15, bf16[16,2048]{1,0:T(8,128)(2,1)S(1)} %collective-permute-done.14, bf16[16,2048]{1,0:T(8,128)(2,1)S(1)} %collective-permute-done.13, bf16[4,16,2048]{2,1,0:T(8,128)(2,1)S(1)} %add_convert_fusion.1), kind=kLoop, calls=%fused_computation.15 | loop fusion | flops 262144 | bytes 393216 | tf_op jit(solution)/shard_map/mul | solution.py:327
  (36 shorter events, 0.2 us)
Async XLA Ops:
  0.6 21.1 %copy-start.1 = (bf16[128,4096]{1,0:T(8,128)(2,1)S(1)}, bf16[128,4096]{1,0:T(8,128)(2,1)}, u32[]{:S(2)}) copy-start(bf16[128,4096]{1,0:T(8,128)(2,1)} %g_ref.3) | copy-start | bytes 3145732
  0.6 21.1 %copy-start = (bf16[128,4096]{1,0:T(8,128)(2,1)S(1)}, bf16[128,4096]{1,0:T(8,128)(2,1)}, u32[]{:S(2)}) copy-start(bf16[128,4096]{1,0:T(8,128)(2,1)} %q_ref.3) | copy-start | bytes 3145732
  0.6 14.2 %collective-permute-start.1 = (bf16[1,16,1024]{2,1,0:T(8,128)(2,1)}, bf16[1,16,1024]{2,1,0:T(8,128)(2,1)S(1)}, u32[]{:S(2)}, u32[]{:S(2)}) collective-permute-start(bf16[1,16,1024]{2,1,0:T(8,128)(2,1)} %param.16), channel_id=1, source_target_pairs={{0,2},{1,3},{2,0},{3,1},{4,6},{5,7},{6,4},{7,5},{8,10},{9,11},{10,... | collective-permute-start | bytes 98312 | tf_op jit(solution)/shard_map/ppermute | solution.py:190
  4.8 10.1 %collective-permute-start = (bf16[1,16,1024]{2,1,0:T(8,128)(2,1)}, bf16[1,16,1024]{2,1,0:T(8,128)(2,1)S(1)}, u32[]{:S(2)}, u32[]{:S(2)}) collective-permute-start(bf16[1,16,1024]{2,1,0:T(8,128)(2,1)} %param.16), channel_id=1, source_target_pairs={{0,1},{1,2},{2,3},{3,0},{4,5},{5,6},{6,7},{7,4},{8,9},{9,10},{10,1... | collective-permute-start | bytes 98312 | tf_op jit(solution)/shard_map/ppermute | solution.py:190
  6.3 8.6 %collective-permute-start.2 = (bf16[1,16,1024]{2,1,0:T(8,128)(2,1)}, bf16[1,16,1024]{2,1,0:T(8,128)(2,1)S(1)}, u32[]{:S(2)}, u32[]{:S(2)}) collective-permute-start(bf16[1,16,1024]{2,1,0:T(8,128)(2,1)} %param.16), channel_id=1, source_target_pairs={{0,3},{1,0},{2,1},{3,2},{4,7},{5,4},{6,5},{7,6},{8,11},{9,8},{10,9... | collective-permute-start | bytes 98312 | tf_op jit(solution)/shard_map/ppermute | solution.py:190
  10.4 11.1 %collective-permute-start.4 = (bf16[128,1024]{1,0:T(8,128)(2,1)S(1)}, bf16[128,1024]{1,0:T(8,128)(2,1)S(1)}, u32[]{:S(2)}, u32[]{:S(2)}) collective-permute-start(bf16[128,1024]{1,0:T(8,128)(2,1)S(1)} %constant_dynamic-update-slice_fusion.refs_3_), channel_id=1, source_target_pairs={{0,1},{1,2},{2,3},{4,5},{5,6},{6,7},{8,9},{9,10},{10,11},{12,13},{... | collective-permute-start | bytes 786440 | tf_op jit(solution)/shard_map/ppermute | solution.py:222
  12.1 9.3 %collective-permute-start.3 = (bf16[64,1024]{1,0:T(8,128)(2,1)S(1)}, bf16[64,1024]{1,0:T(8,128)(2,1)S(1)}, u32[]{:S(2)}, u32[]{:S(2)}) collective-permute-start(bf16[64,1024]{1,0:T(8,128)(2,1)S(1)} %slice.60), channel_id=1, source_target_pairs={{0,2},{1,3},{4,6},{5,7},{8,10},{9,11},{12,14},{13,15},{16,18},{17,... | collective-permute-start | bytes 393224 | tf_op jit(solution)/shard_map/ppermute | solution.py:222
  15.7 8.1 %collective-permute-start.7 = (bf16[1,4,16,1024]{3,2,1,0:T(8,128)(2,1)S(1)}, bf16[1,4,16,1024]{3,2,1,0:T(8,128)(2,1)S(1)}, u32[]{:S(2)}, u32[]{:S(2)}) collective-permute-start(bf16[1,4,16,1024]{3,2,1,0:T(8,128)(2,1)S(1)} %maximum_bitcast_fusion), channel_id=1, source_target_pairs={{0,24},{4,28},{8,16},{12,20},{16,8},{20,12},{24,0},{28,4},{1,25},{... | collective-permute-start | bytes 393224 | tf_op jit(solution)/shard_map/ppermute | solution.py:198
  18.2 5.6 %collective-permute-start.6 = (bf16[1,4,16,1024]{3,2,1,0:T(8,128)(2,1)S(1)}, bf16[1,4,16,1024]{3,2,1,0:T(8,128)(2,1)S(1)}, u32[]{:S(2)}, u32[]{:S(2)}) collective-permute-start(bf16[1,4,16,1024]{3,2,1,0:T(8,128)(2,1)S(1)} %maximum_bitcast_fusion), channel_id=1, source_target_pairs={{0,16},{4,20},{8,24},{12,28},{16,0},{20,4},{24,8},{28,12},{1,17},{... | collective-permute-start | bytes 393224 | tf_op jit(solution)/shard_map/ppermute | solution.py:198
  18.7 5.1 %collective-permute-start.5 = (bf16[1,4,16,1024]{3,2,1,0:T(8,128)(2,1)S(1)}, bf16[1,4,16,1024]{3,2,1,0:T(8,128)(2,1)S(1)}, u32[]{:S(2)}, u32[]{:S(2)}) collective-permute-start(bf16[1,4,16,1024]{3,2,1,0:T(8,128)(2,1)S(1)} %maximum_bitcast_fusion), channel_id=1, source_target_pairs={{0,8},{4,12},{8,0},{12,4},{16,24},{20,28},{24,16},{28,20},{1,9},{5... | collective-permute-start | bytes 393224 | tf_op jit(solution)/shard_map/ppermute | solution.py:198
  21.8 2.2 %copy-start.3 = (bf16[128,16]{0,1:T(8,128)(2,1)S(1)}, bf16[128,16]{0,1:T(8,128)(2,1)}, u32[]{:S(2)}) copy-start(bf16[128,16]{0,1:T(8,128)(2,1)} %param.15) | copy-start | bytes 12292
  23.9 2.4 %collective-permute-start.8 = (bf16[4,4,16,1024]{3,2,1,0:T(8,128)(2,1)S(1)}, bf16[4,4,16,1024]{3,2,1,0:T(8,128)(2,1)S(1)}, u32[]{:S(2)}, u32[]{:S(2)}) collective-permute-start(bf16[4,4,16,1024]{3,2,1,0:T(8,128)(2,1)S(1)} %constant_dynamic-update-slice_fusion.2.refs_0_), channel_id=1, source_target_pairs={{0,4},{4,0},{8,12},{12,8},{16,20},{20,16},{24,28},{28,24},{1,5},{5... | collective-permute-start | bytes 1572872 | tf_op jit(solution)/shard_map/ppermute | solution.py:198
  24.0 3.3 %copy-start.2 = (bf16[128,8192]{1,0:T(8,128)(2,1)S(1)}, bf16[128,8192]{1,0:T(8,128)(2,1)}, u32[]{:S(2)}) copy-start(bf16[128,8192]{1,0:T(8,128)(2,1)} %x_ref.1) | copy-start | bytes 6291460
  26.3 2.1 %collective-permute-start.16 = (bf16[4,4,16,1024]{3,2,1,0:T(8,128)(2,1)S(1)}, bf16[4,4,16,1024]{3,2,1,0:T(8,128)(2,1)S(1)}, u32[]{:S(2)}, u32[]{:S(2)}) collective-permute-start(bf16[4,4,16,1024]{3,2,1,0:T(8,128)(2,1)S(1)} %get-tuple-element.49), channel_id=1, source_target_pairs={{0,4},{4,0},{8,12},{12,8},{16,20},{20,16},{24,28},{28,24},{1,5},{5... | collective-permute-start | bytes 1572872 | tf_op jit(solution)/shard_map/ppermute | solution.py:198
  28.0 5.5 %collective-permute-start.9 = (bf16[4,4,16,2048]{3,2,1,0:T(8,128)(2,1)S(1)}, bf16[4,4,16,2048]{3,2,1,0:T(8,128)(2,1)S(1)}, u32[]{:S(2)}, u32[]{:S(2)}) collective-permute-start(bf16[4,4,16,2048]{3,2,1,0:T(8,128)(2,1)S(1)} %get-tuple-element.43), channel_id=1, source_target_pairs={{0,4},{4,0},{8,12},{12,8},{16,20},{20,16},{24,28},{28,24},{1,5},{5... | collective-permute-start | bytes 3145736 | tf_op jit(solution)/shard_map/ppermute | solution.py:198
  28.6 8.2 %collective-permute-start.17 = (bf16[4,16,1024]{2,1,0:T(8,128)(2,1)S(1)}, bf16[4,16,1024]{2,1,0:T(8,128)(2,1)S(1)}, u32[]{:S(2)}, u32[]{:S(2)}) collective-permute-start(bf16[4,16,1024]{2,1,0:T(8,128)(2,1)S(1)} %get-tuple-element.50), channel_id=1, source_target_pairs={{0,1},{1,0},{2,3},{3,2},{4,5},{5,4},{6,7},{7,6},{8,9},{9,8},{10,11... | collective-permute-start | bytes 393224 | tf_op jit(solution)/shard_map/ppermute | solution.py:194
  30.1 10.1 %collective-permute-start.19 = (bf16[4,16,1024]{2,1,0:T(8,128)(2,1)S(1)}, bf16[4,16,1024]{2,1,0:T(8,128)(2,1)S(1)}, u32[]{:S(2)}, u32[]{:S(2)}) collective-permute-start(bf16[4,16,1024]{2,1,0:T(8,128)(2,1)S(1)} %get-tuple-element.51), channel_id=1, source_target_pairs={{0,3},{1,2},{2,1},{3,0},{4,7},{5,6},{6,5},{7,4},{8,11},{9,10},{10,... | collective-permute-start | bytes 393224 | tf_op jit(solution)/shard_map/ppermute | solution.py:194
  33.0 12.7 %collective-permute-start.18 = (bf16[4,16,1024]{2,1,0:T(8,128)(2,1)S(1)}, bf16[4,16,1024]{2,1,0:T(8,128)(2,1)S(1)}, u32[]{:S(2)}, u32[]{:S(2)}) collective-permute-start(bf16[4,16,1024]{2,1,0:T(8,128)(2,1)S(1)} %get-tuple-element.52), channel_id=1, source_target_pairs={{0,2},{1,3},{2,0},{3,1},{4,6},{5,7},{6,4},{7,5},{8,10},{9,11},{10,... | collective-permute-start | bytes 393224 | tf_op jit(solution)/shard_map/ppermute | solution.py:194
  33.8 15.1 %collective-permute-start.10 = (bf16[4,16,2048]{2,1,0:T(8,128)(2,1)S(1)}, bf16[4,16,2048]{2,1,0:T(8,128)(2,1)S(1)}, u32[]{:S(2)}, u32[]{:S(2)}) collective-permute-start(bf16[4,16,2048]{2,1,0:T(8,128)(2,1)S(1)} %get-tuple-element.45), channel_id=1, source_target_pairs={{0,8},{4,12},{8,0},{12,4},{16,24},{20,28},{24,16},{28,20},{1,9},{5... | collective-permute-start | bytes 786440 | tf_op jit(solution)/shard_map/ppermute | solution.py:198
  35.3 14.0 %collective-permute-start.11 = (bf16[4,16,2048]{2,1,0:T(8,128)(2,1)S(1)}, bf16[4,16,2048]{2,1,0:T(8,128)(2,1)S(1)}, u32[]{:S(2)}, u32[]{:S(2)}) collective-permute-start(bf16[4,16,2048]{2,1,0:T(8,128)(2,1)S(1)} %get-tuple-element.46), channel_id=1, source_target_pairs={{0,16},{4,20},{8,24},{12,28},{16,0},{20,4},{24,8},{28,12},{1,17},{... | collective-permute-start | bytes 786440 | tf_op jit(solution)/shard_map/ppermute | solution.py:198
  36.8 12.5 %collective-permute-start.12 = (bf16[4,16,2048]{2,1,0:T(8,128)(2,1)S(1)}, bf16[4,16,2048]{2,1,0:T(8,128)(2,1)S(1)}, u32[]{:S(2)}, u32[]{:S(2)}) collective-permute-start(bf16[4,16,2048]{2,1,0:T(8,128)(2,1)S(1)} %get-tuple-element.47), channel_id=1, source_target_pairs={{0,24},{4,28},{8,16},{12,20},{16,8},{20,12},{24,0},{28,4},{1,25},{... | collective-permute-start | bytes 786440 | tf_op jit(solution)/shard_map/ppermute | solution.py:198
  45.8 6.4 %collective-permute-start.20 = (bf16[16,1024]{1,0:T(8,128)(2,1)S(1)}, bf16[16,1024]{1,0:T(8,128)(2,1)S(1)}, u32[]{:S(2)}, u32[]{:S(2)}) collective-permute-start(bf16[16,1024]{1,0:T(8,128)(2,1)S(1)} %get-tuple-element.56), channel_id=1, source_target_pairs={{0,8},{4,12},{8,0},{12,4},{16,24},{20,28},{24,16},{28,20},{1,9},{5... | collective-permute-start | bytes 98312 | tf_op jit(solution)/shard_map/ppermute | solution.py:198
  47.3 6.6 %collective-permute-start.22 = (bf16[16,1024]{1,0:T(8,128)(2,1)S(1)}, bf16[16,1024]{1,0:T(8,128)(2,1)S(1)}, u32[]{:S(2)}, u32[]{:S(2)}) collective-permute-start(bf16[16,1024]{1,0:T(8,128)(2,1)S(1)} %get-tuple-element.57), channel_id=1, source_target_pairs={{0,24},{4,28},{8,16},{12,20},{16,8},{20,12},{24,0},{28,4},{1,25},{... | collective-permute-start | bytes 98312 | tf_op jit(solution)/shard_map/ppermute | solution.py:198
  48.8 5.1 %collective-permute-start.21 = (bf16[16,1024]{1,0:T(8,128)(2,1)S(1)}, bf16[16,1024]{1,0:T(8,128)(2,1)S(1)}, u32[]{:S(2)}, u32[]{:S(2)}) collective-permute-start(bf16[16,1024]{1,0:T(8,128)(2,1)S(1)} %get-tuple-element.58), channel_id=1, source_target_pairs={{0,16},{4,20},{8,24},{12,28},{16,0},{20,4},{24,8},{28,12},{1,17},{... | collective-permute-start | bytes 98312 | tf_op jit(solution)/shard_map/ppermute | solution.py:198
  49.5 6.7 %collective-permute-start.13 = (bf16[16,2048]{1,0:T(8,128)(2,1)S(1)}, bf16[16,2048]{1,0:T(8,128)(2,1)S(1)}, u32[]{:S(2)}, u32[]{:S(2)}) collective-permute-start(bf16[16,2048]{1,0:T(8,128)(2,1)S(1)} %get-tuple-element.53), channel_id=1, source_target_pairs={{0,3},{1,2},{2,1},{3,0},{4,7},{5,6},{6,5},{7,4},{8,11},{9,10},{10,... | collective-permute-start | bytes 196616 | tf_op jit(solution)/shard_map/ppermute | solution.py:194
  52.2 5.5 %collective-permute-start.15 = (bf16[16,2048]{1,0:T(8,128)(2,1)S(1)}, bf16[16,2048]{1,0:T(8,128)(2,1)S(1)}, u32[]{:S(2)}, u32[]{:S(2)}) collective-permute-start(bf16[16,2048]{1,0:T(8,128)(2,1)S(1)} %get-tuple-element.54), channel_id=1, source_target_pairs={{0,2},{1,3},{2,0},{3,1},{4,6},{5,7},{6,4},{7,5},{8,10},{9,11},{10,... | collective-permute-start | bytes 196616 | tf_op jit(solution)/shard_map/ppermute | solution.py:194
  52.2 5.5 %collective-permute-start.14 = (bf16[16,2048]{1,0:T(8,128)(2,1)S(1)}, bf16[16,2048]{1,0:T(8,128)(2,1)S(1)}, u32[]{:S(2)}, u32[]{:S(2)}) collective-permute-start(bf16[16,2048]{1,0:T(8,128)(2,1)S(1)} %get-tuple-element.55), channel_id=1, source_target_pairs={{0,1},{1,0},{2,3},{3,2},{4,5},{5,4},{6,7},{7,6},{8,9},{9,8},{10,11... | collective-permute-start | bytes 196616 | tf_op jit(solution)/shard_map/ppermute | solution.py:194
